TPU v7x, 32 devices: a whole 2x2x4 slice. The times are simulated.
32 devices in a mesh: samp: 8 (over z, y), layer: 4 (over x, core).
Axes of the slice: x: 2, y: 2, z: 4, core: 2. Of those that a mesh axis runs over, the one named last changes fastest.
Arguments:
- spins: int32 [64, 256], P('samp'), may hold values 0 or 1
- activations: bfloat16 [64, 8, 256, 256], P('samp', 'layer'), may hold values from -6 to 6
- cotangents: bfloat16 [64, 8, 256, 256], P('samp', 'layer'), may hold values from -0.023925781 to 0.023925781
- offdiag: float32 [64], P('samp'), may hold values from -24 to 24
Outputs:
- weights: float32 [64], P('samp')
- update: float32 [8, 256, 256], P('layer', 'samp')
All inputs are finite; a program needn't handle non-finite values. No bound on the sum of `spins` on one device may be relied on, other than what follows from the above.
Results may differ from a plain program's by a relative error of at most 0.0029.
Values may be sent and summed in bfloat16 or wider, within the bound.
No kernel may reach another device: no remote copies, remote signals or barrier semaphores. Data moves between devices by JAX's collectives and lax.ppermute only.
A program may use at most 64 MiB of HBM per device.

v0:
```python
import jax
import jax.numpy as jnp
from jax import lax
from jax.sharding import PartitionSpec as P

SIDE = 16


shift_ratio = 0.1
highest = lax.Precision.HIGHEST


def local_energy(spins, offdiag):
    zvals = (2 * spins - 1).astype(jnp.float32).reshape(spins.shape[0], SIDE, SIDE)
    bonds = zvals * jnp.roll(zvals, -1, 2) + zvals * jnp.roll(zvals, -1, 1)
    return offdiag + jnp.sum(bonds, axis=(1, 2))


def small_factor(matrix):
    order = matrix.shape[0]
    positions = lax.iota(jnp.int32, order)

    def one_column(j, carry):
        rest, lower = carry
        column = lax.dynamic_slice_in_dim(rest, j, 1, 1)[:, 0]
        pivot = jnp.sqrt(lax.dynamic_slice_in_dim(column, j, 1)[0])
        scaled = jnp.where(positions >= j, column / pivot, jnp.float32(0.0))
        lower = lax.dynamic_update_slice_in_dim(lower, scaled[:, None], j, 1)
        rest = rest - scaled[:, None] * scaled[None, :]
        return (rest, lower)

    start = (matrix, jnp.zeros_like(matrix))
    return lax.fori_loop(0, order, one_column, start)[1]


def lower_inverse(lower):
    order = lower.shape[0]
    ident = jnp.eye(order, dtype=jnp.float32)

    def one_row(i, inverse):
        lower_row = lax.dynamic_slice_in_dim(lower, i, 1, 0)
        unit_row = lax.dynamic_slice_in_dim(ident, i, 1, 0)
        diag_entry = lax.dynamic_slice_in_dim(lower_row[0], i, 1)[0]
        known = jnp.dot(lower_row, inverse, precision=highest)
        fresh = (unit_row - known) / diag_entry
        return lax.dynamic_update_slice_in_dim(inverse, fresh, i, 0)

    return lax.fori_loop(0, order, one_row, jnp.zeros_like(lower))


def blocked_solve(matrix, rhs):
    block = matrix.shape[0] // 8
    lower_tiles = {}
    inverses = []
    for k in range(8):
        diag_tile = matrix[k * block : (k + 1) * block, k * block : (k + 1) * block]
        for c in range(k):
            diag_tile = diag_tile - jnp.dot(
                lower_tiles[k, c], lower_tiles[k, c].T, precision=highest
            )
        factor = small_factor(diag_tile)
        inverse = lower_inverse(factor)
        inverses.append(inverse)
        for r in range(k + 1, 8):
            tile = matrix[r * block : (r + 1) * block, k * block : (k + 1) * block]
            for c in range(k):
                tile = tile - jnp.dot(lower_tiles[r, c], lower_tiles[k, c].T, precision=highest)
            lower_tiles[r, k] = jnp.dot(tile, inverse.T, precision=highest)
    forward = []
    for k in range(8):
        piece = rhs[k * block : (k + 1) * block]
        for c in range(k):
            piece = piece - jnp.dot(lower_tiles[k, c], forward[c], precision=highest)
        forward.append(jnp.dot(inverses[k], piece, precision=highest))
    backward = [None] * 8
    for k in range(7, -1, -1):
        piece = forward[k]
        for r in range(k + 1, 8):
            piece = piece - jnp.dot(lower_tiles[r, k].T, backward[r], precision=highest)
        backward[k] = jnp.dot(inverses[k].T, piece, precision=highest)
    return jnp.concatenate(backward)


def body(spins, activations, cotangents, offdiag):
    s_local = spins.shape[0]
    energy_local = local_energy(spins, offdiag)
    energy = lax.all_gather(energy_local, "samp", axis=0, tiled=True)
    total = energy.shape[0]
    eps = (energy - jnp.mean(energy)) / jnp.sqrt(jnp.float32(total))
    jac = jnp.einsum(
        "ksad,ksae->ksde", activations, cotangents, preferred_element_type=jnp.float32
    ).astype(jnp.bfloat16)
    regrouped = lax.all_to_all(jac, "samp", split_axis=2, concat_axis=0, tiled=True)
    flat = regrouped.reshape(total, -1)
    col_mean = jnp.mean(flat, axis=0, dtype=jnp.float32)
    raw_gram = jnp.dot(flat, flat.T, preferred_element_type=jnp.float32)
    row_dots = jnp.dot(flat.astype(jnp.float32), col_mean, precision=highest)
    mean_square = jnp.sum(col_mean * col_mean)
    partial_value = (raw_gram - row_dots[:, None] - row_dots[None, :] + mean_square) / total
    gram = lax.psum(partial_value, ("samp", "layer"))
    shift = shift_ratio * jnp.trace(gram) / total
    weights = blocked_solve(gram + shift * jnp.eye(total, dtype=jnp.float32), eps)
    start = lax.axis_index("samp") * s_local
    own_weights = lax.dynamic_slice_in_dim(weights, start, s_local)
    coeffs_all = weights - jnp.mean(weights)
    update = jnp.dot(coeffs_all, flat.astype(jnp.float32), precision=highest).reshape(
        regrouped.shape[1:]
    )
    return (own_weights, update)


def solution(mesh):
    placed = (
        P("samp", None),
        P("samp", "layer", None, None),
        P("samp", "layer", None, None),
        P("samp"),
    )
    return jax.shard_map(
        body,
        mesh=mesh,
        in_specs=placed,
        out_specs=(P("samp"), P("layer", "samp", None)),
        check_vma=False,
    )
```

profile of v0, /device:TPU:0, one launch (start us, length us, event | category | flops | bytes accessed | tf_op | source)
XLA Modules:
  0.0 354.8 jit_solution(12778886980284541014)
XLA Ops:
  0.6 1.6 copy-done
  2.2 2.4 convolution_convert_fusion
  4.6 3.5 copy.85
  8.0 7.4 %all-to-all-start = ((bf16[8,2,256,256]{3,1,0,2:T(2,128)(2,1)}), bf16[8,2,256,256]{3,1,0,2:T(2,128)(2,1)}, u32[]{:S(2)}, u32[]{:S(2)}) async-start(bf16[8,2,256,256]{3,1,0,2:T(2,128)(2,1)} %copy.85), calls=%async_computation | async-start | bytes 4194304 | tf_op jit(solution)/shard_map/all_to_all | solution.py:93
  17.4 48.0 %all-reduce = f32[64]{0:T(128)S(1)} all-reduce(f32[64]{0:T(128)S(1)} %add_dynamic-update-slice_fusion), channel_id=1, replica_groups=mesh['samp'=8,'layer'=4] {'samp'}, use_global_device_ids=true, to_apply=%add | all-reduce | flops 64 | bytes 512
  66.9 2.1 convert_reduce_fusion
  69.0 3.8 %copy.135 = bf16[8,2,8,32,256]{4,3,1,0,2:T(8,128)(2,1)} copy(bf16[8,2,8,32,256]{4,1,0,3,2:T(2,128)(2,1)} %bitcast.32) | data formatting | bytes 4194304 | tf_op jit(solution)/shard_map/all_to_all | solution.py:93
  72.9 4.2 %reshape.473 = bf16[64,16384]{1,0:T(8,128)(2,1)} reshape(bf16[8,8,2,32,256]{4,3,2,1,0:T(8,128)(2,1)} %bitcast.1126) | data formatting | bytes 4194304 | tf_op jit(solution)/shard_map/reshape | solution.py:94
  77.8 3.5 convolution_bitcast_fusion.58
  81.2 1.3 fusion.52
  82.6 46.3 %psum.7 = f32[64,64]{1,0:T(8,128)S(1)} all-reduce(f32[64,64]{1,0:T(8,128)S(1)} %fusion.52), channel_id=1, replica_groups=mesh['samp'=8,'layer'=4] {'samp','layer'}, use_global_device_ids=true, to_apply=%region_2.3 | all-reduce | flops 4096 | bytes 32768 | tf_op jit(solution)/shard_map/psum | solution.py:100
  130.2 11.2 %while.288 = (s32[]{:T(128)}, f32[8,8]{0,1:T(8,128)S(1)}, f32[8,8]{0,1:T(8,128)S(1)}, s32[]{:T(128)}, s32[]{:T(128)}, /*index=5*/s32[]{:T(128)}) while((s32[]{:T(128)}, f32[8,8]{0,1:T(8,128)S(1)}, f32[8,8]{0,1:T(8,128)S(1)}, s32[]{:T(128)}, s32[]{:T(128)}, /*index=5*/s32[]{:T(128)}) %tuple.674), condition=%wide.region_5.6_spmd.clone, body=%wide.region_4.5_spmd.clone.sunk | while | flops 171 | bytes 1949 | solution.py:33
  141.5 11.2 %while.280 = (s32[]{:T(128)}, f32[8,8]{1,0:T(8,128)S(1)}, f32[8,8]{1,0:T(8,128)S(1)}, f32[8,8]{1,0:T(8,128)S(1)}, s32[]{:T(128)}, /*index=5*/s32[]{:T(128)}, s32[]{:T(128)}) while((s32[]{:T(128)}, f32[8,8]{1,0:T(8,128)S(1)}, f32[8,8]{1,0:T(8,128)S(1)}, f32[8,8]{1,0:T(8,128)S(1)}, s32[]{:T(128)}, /*index=5*/s32[]{:T(128)}, s32[]{:T(128)}) %tuple.677), condition=%wide.region_7.8_spmd, body=%wide.region_6.7_spmd.sunk | while | flops 787 | bytes 6361 | solution.py:48
  142.1 0.8 fusion.579
  143.5 0.8 fusion.579
  144.9 0.8 fusion.579
  146.3 0.8 fusion.579
  147.7 0.8 fusion.579
  149.1 0.8 fusion.579
  150.5 0.8 fusion.579
  151.9 0.8 fusion.579
  157.8 11.4 %while.289 = (s32[]{:T(128)}, f32[8,8]{0,1:T(8,128)S(1)}, f32[8,8]{0,1:T(8,128)S(1)}, s32[]{:T(128)}, s32[]{:T(128)}, /*index=5*/s32[]{:T(128)}) while((s32[]{:T(128)}, f32[8,8]{0,1:T(8,128)S(1)}, f32[8,8]{0,1:T(8,128)S(1)}, s32[]{:T(128)}, s32[]{:T(128)}, /*index=5*/s32[]{:T(128)}) %tuple.680), condition=%wide.region_11.12_spmd.clone, body=%wide.region_10.11_spmd.clone.sunk | while | flops 171 | bytes 1949 | solution.py:33
  169.2 11.2 %while.281 = (s32[]{:T(128)}, f32[8,8]{1,0:T(8,128)S(1)}, f32[8,8]{1,0:T(8,128)S(1)}, f32[8,8]{1,0:T(8,128)S(1)}, s32[]{:T(128)}, /*index=5*/s32[]{:T(128)}, s32[]{:T(128)}) while((s32[]{:T(128)}, f32[8,8]{1,0:T(8,128)S(1)}, f32[8,8]{1,0:T(8,128)S(1)}, f32[8,8]{1,0:T(8,128)S(1)}, s32[]{:T(128)}, /*index=5*/s32[]{:T(128)}, s32[]{:T(128)}) %tuple.722), condition=%wide.region_13.14_spmd, body=%wide.region_12.13_spmd.sunk | while | flops 787 | bytes 6361 | solution.py:48
  169.8 0.8 fusion.582
  171.2 0.8 fusion.582
  172.6 0.8 fusion.582
  174.0 0.8 fusion.582
  175.4 0.8 fusion.582
  176.8 0.8 fusion.582
  178.3 0.8 fusion.582
  179.7 0.8 fusion.582
  183.9 11.4 %while.290 = (s32[]{:T(128)}, f32[8,8]{0,1:T(8,128)S(1)}, f32[8,8]{0,1:T(8,128)S(1)}, s32[]{:T(128)}, s32[]{:T(128)}, /*index=5*/s32[]{:T(128)}) while((s32[]{:T(128)}, f32[8,8]{0,1:T(8,128)S(1)}, f32[8,8]{0,1:T(8,128)S(1)}, s32[]{:T(128)}, s32[]{:T(128)}, /*index=5*/s32[]{:T(128)}) %tuple.686), condition=%wide.region_15.16_spmd.clone, body=%wide.region_14.15_spmd.clone.sunk | while | flops 171 | bytes 1949 | solution.py:33
  195.4 11.2 %while.282 = (s32[]{:T(128)}, f32[8,8]{1,0:T(8,128)S(1)}, f32[8,8]{1,0:T(8,128)S(1)}, f32[8,8]{1,0:T(8,128)S(1)}, s32[]{:T(128)}, /*index=5*/s32[]{:T(128)}, s32[]{:T(128)}) while((s32[]{:T(128)}, f32[8,8]{1,0:T(8,128)S(1)}, f32[8,8]{1,0:T(8,128)S(1)}, f32[8,8]{1,0:T(8,128)S(1)}, s32[]{:T(128)}, /*index=5*/s32[]{:T(128)}, s32[]{:T(128)}) %tuple.723), condition=%wide.region_17.18_spmd, body=%wide.region_16.17_spmd.sunk | while | flops 787 | bytes 6361 | solution.py:48
  196.0 0.8 fusion.585
  197.4 0.8 fusion.585
  198.8 0.8 fusion.585
  200.2 0.8 fusion.585
  201.6 0.8 fusion.585
  203.0 0.8 fusion.585
  204.4 0.8 fusion.585
  205.8 0.8 fusion.585
  209.9 11.4 %while.291 = (s32[]{:T(128)}, f32[8,8]{0,1:T(8,128)S(1)}, f32[8,8]{0,1:T(8,128)S(1)}, s32[]{:T(128)}, s32[]{:T(128)}, /*index=5*/s32[]{:T(128)}) while((s32[]{:T(128)}, f32[8,8]{0,1:T(8,128)S(1)}, f32[8,8]{0,1:T(8,128)S(1)}, s32[]{:T(128)}, s32[]{:T(128)}, /*index=5*/s32[]{:T(128)}) %tuple.692), condition=%wide.region_19.20_spmd.clone, body=%wide.region_18.19_spmd.clone.sunk | while | flops 171 | bytes 1949 | solution.py:33
  221.4 11.2 %while.283 = (s32[]{:T(128)}, f32[8,8]{1,0:T(8,128)S(1)}, f32[8,8]{1,0:T(8,128)S(1)}, f32[8,8]{1,0:T(8,128)S(1)}, s32[]{:T(128)}, /*index=5*/s32[]{:T(128)}, s32[]{:T(128)}) while((s32[]{:T(128)}, f32[8,8]{1,0:T(8,128)S(1)}, f32[8,8]{1,0:T(8,128)S(1)}, f32[8,8]{1,0:T(8,128)S(1)}, s32[]{:T(128)}, /*index=5*/s32[]{:T(128)}, s32[]{:T(128)}) %tuple.724), condition=%wide.region_21.22_spmd, body=%wide.region_20.21_spmd.sunk | while | flops 787 | bytes 6361 | solution.py:48
  222.0 0.8 fusion.588
  223.4 0.8 fusion.588
  224.8 0.8 fusion.588
  230.4 0.8 fusion.588
  235.8 11.4 %while.292 = (s32[]{:T(128)}, f32[8,8]{0,1:T(8,128)S(1)}, f32[8,8]{0,1:T(8,128)S(1)}, s32[]{:T(128)}, s32[]{:T(128)}, /*index=5*/s32[]{:T(128)}) while((s32[]{:T(128)}, f32[8,8]{0,1:T(8,128)S(1)}, f32[8,8]{0,1:T(8,128)S(1)}, s32[]{:T(128)}, s32[]{:T(128)}, /*index=5*/s32[]{:T(128)}) %tuple.698), condition=%wide.region_23.24_spmd.clone, body=%wide.region_22.23_spmd.clone.sunk | while | flops 171 | bytes 1949 | solution.py:33
  247.3 11.2 %while.284 = (s32[]{:T(128)}, f32[8,8]{1,0:T(8,128)S(1)}, f32[8,8]{1,0:T(8,128)S(1)}, f32[8,8]{1,0:T(8,128)S(1)}, s32[]{:T(128)}, /*index=5*/s32[]{:T(128)}, s32[]{:T(128)}) while((s32[]{:T(128)}, f32[8,8]{1,0:T(8,128)S(1)}, f32[8,8]{1,0:T(8,128)S(1)}, f32[8,8]{1,0:T(8,128)S(1)}, s32[]{:T(128)}, /*index=5*/s32[]{:T(128)}, s32[]{:T(128)}) %tuple.725), condition=%wide.region_25.26_spmd, body=%wide.region_24.25_spmd.sunk | while | flops 787 | bytes 6361 | solution.py:48
  253.5 0.8 fusion.591
  261.7 11.4 %while.293 = (s32[]{:T(128)}, f32[8,8]{0,1:T(8,128)S(1)}, f32[8,8]{0,1:T(8,128)S(1)}, s32[]{:T(128)}, s32[]{:T(128)}, /*index=5*/s32[]{:T(128)}) while((s32[]{:T(128)}, f32[8,8]{0,1:T(8,128)S(1)}, f32[8,8]{0,1:T(8,128)S(1)}, s32[]{:T(128)}, s32[]{:T(128)}, /*index=5*/s32[]{:T(128)}) %tuple.704), condition=%wide.region_27.28_spmd.clone, body=%wide.region_26.27_spmd.clone.sunk | while | flops 171 | bytes 1949 | solution.py:33
  273.1 11.2 %while.285 = (s32[]{:T(128)}, f32[8,8]{1,0:T(8,128)S(1)}, f32[8,8]{1,0:T(8,128)S(1)}, f32[8,8]{1,0:T(8,128)S(1)}, s32[]{:T(128)}, /*index=5*/s32[]{:T(128)}, s32[]{:T(128)}) while((s32[]{:T(128)}, f32[8,8]{1,0:T(8,128)S(1)}, f32[8,8]{1,0:T(8,128)S(1)}, f32[8,8]{1,0:T(8,128)S(1)}, s32[]{:T(128)}, /*index=5*/s32[]{:T(128)}, s32[]{:T(128)}) %tuple.726), condition=%wide.region_29.30_spmd, body=%wide.region_28.29_spmd.sunk | while | flops 787 | bytes 6361 | solution.py:48
  279.4 0.8 fusion.594
  285.7 11.4 %while.294 = (s32[]{:T(128)}, f32[8,8]{0,1:T(8,128)S(1)}, f32[8,8]{0,1:T(8,128)S(1)}, s32[]{:T(128)}, s32[]{:T(128)}, /*index=5*/s32[]{:T(128)}) while((s32[]{:T(128)}, f32[8,8]{0,1:T(8,128)S(1)}, f32[8,8]{0,1:T(8,128)S(1)}, s32[]{:T(128)}, s32[]{:T(128)}, /*index=5*/s32[]{:T(128)}) %tuple.710), condition=%wide.region_31.32_spmd.clone, body=%wide.region_30.31_spmd.clone.sunk | while | flops 171 | bytes 1949 | solution.py:33
  297.1 11.2 %while.286 = (s32[]{:T(128)}, f32[8,8]{1,0:T(8,128)S(1)}, f32[8,8]{1,0:T(8,128)S(1)}, f32[8,8]{1,0:T(8,128)S(1)}, s32[]{:T(128)}, /*index=5*/s32[]{:T(128)}, s32[]{:T(128)}) while((s32[]{:T(128)}, f32[8,8]{1,0:T(8,128)S(1)}, f32[8,8]{1,0:T(8,128)S(1)}, f32[8,8]{1,0:T(8,128)S(1)}, s32[]{:T(128)}, /*index=5*/s32[]{:T(128)}, s32[]{:T(128)}) %tuple.727), condition=%wide.region_33.34_spmd, body=%wide.region_32.33_spmd.sunk | while | flops 787 | bytes 6361 | solution.py:48
  306.1 0.8 fusion.597
  308.7 11.4 %while.295 = (s32[]{:T(128)}, f32[8,8]{0,1:T(8,128)S(1)}, f32[8,8]{0,1:T(8,128)S(1)}, s32[]{:T(128)}, s32[]{:T(128)}, /*index=5*/s32[]{:T(128)}) while((s32[]{:T(128)}, f32[8,8]{0,1:T(8,128)S(1)}, f32[8,8]{0,1:T(8,128)S(1)}, s32[]{:T(128)}, s32[]{:T(128)}, /*index=5*/s32[]{:T(128)}) %tuple.716), condition=%wide.region_35.36_spmd.clone, body=%wide.region_34.35_spmd.clone.sunk | while | flops 171 | bytes 1949 | solution.py:33
  320.1 11.2 %while.287 = (s32[]{:T(128)}, f32[8,8]{1,0:T(8,128)S(1)}, f32[8,8]{1,0:T(8,128)S(1)}, f32[8,8]{1,0:T(8,128)S(1)}, s32[]{:T(128)}, /*index=5*/s32[]{:T(128)}, s32[]{:T(128)}) while((s32[]{:T(128)}, f32[8,8]{1,0:T(8,128)S(1)}, f32[8,8]{1,0:T(8,128)S(1)}, f32[8,8]{1,0:T(8,128)S(1)}, s32[]{:T(128)}, /*index=5*/s32[]{:T(128)}, s32[]{:T(128)}) %tuple.728), condition=%wide.region_37.38_spmd, body=%wide.region_36.37_spmd.sunk | while | flops 787 | bytes 6361 | solution.py:48
  323.5 0.8 fusion.600
  330.5 0.8 fusion.600
  336.7 0.8 bitcast_reduce_fusion.3
  340.1 0.8 bitcast_reduce_fusion
  346.7 3.4 copy.128
  350.8 3.4 fusion.48
  (725 shorter events, 142.2 us)
Async XLA Ops:
  0.6 1.6 copy-start
  8.0 7.4 %copy-start.2 = (s32[8,256]{1,0:T(8,128)S(1)}, s32[8,256]{1,0:T(8,128)}, u32[]{:S(2)}) copy-start(s32[8,256]{1,0:T(8,128)} %param.36) | copy-start | bytes 24580
  8.0 7.8 %copy-start.4 = (u32[32]{0:T(128)S(1)}, u32[32]{0:T(128)}, u32[]{:S(2)}) copy-start(u32[32]{0:T(128)} %constant.1452) | copy-start | bytes 388
  8.0 9.3 %copy-start.3 = (f32[8]{0:T(128)S(1)}, f32[8]{0:T(128)}, u32[]{:S(2)}) copy-start(f32[8]{0:T(128)} %param.39) | copy-start | bytes 100
  8.0 58.8 %all-to-all-start = ((bf16[8,2,256,256]{3,1,0,2:T(2,128)(2,1)}), bf16[8,2,256,256]{3,1,0,2:T(2,128)(2,1)}, u32[]{:S(2)}, u32[]{:S(2)}) async-start(bf16[8,2,256,256]{3,1,0,2:T(2,128)(2,1)} %copy.85), calls=%async_computation | async-start | bytes 4194304 | tf_op jit(solution)/shard_map/all_to_all | solution.py:93
  77.8 3.5 copy-start.1
where the time goes:
time: 357 us; the launch traced here: 355 us
  local copies, waits for them, and re-layouts  98.7 us (28%)
  blocking collectives  94.4 us (26%)
  matrix products  89.8 us (25%)
  loops' own time  46.6 us (13%)
  other arithmetic  10.1 us (3%)
  between operations  7.88 us (2%)
  starting transfers between devices  7.41 us (2%)
    dot_general x64, matrix products, one_row(): known = jnp.dot(lower_row, inverse, precision=highest)  49.6 us
    unnamed x1, blocking collectives  48 us
    psum x1, blocking collectives, body(): gram = lax.psum(partial_value, ('samp', 'layer'))  46.3 us
    another operation x8, loops' own time, small_factor(): return lax.fori_loop(0, order, one_column, start)[1]  45.6 us
    dynamic_slice x64, local copies, waits for them, and re-layouts, one_column(): pivot = jnp.sqrt(lax.dynamic_slice_in_dim(column, j, 1)[0])  37.8 us
    dynamic_slice x64, local copies, waits for them, and re-layouts, one_row(): diag_entry = lax.dynamic_slice_in_dim(lower_row[0], i, 1)[0]  37.6 us
    dot_general x56, matrix products, blocked_solve(): jnp.dot(lower_tiles[r, c], lower_tiles[k, c].T, precision=highest)  7.64 us
    all_to_all x1, starting transfers between devices, body(): lax.all_to_all(jac, 'samp', split_axis=2, concat_axis=0, tiled=True)  7.41 us
  transfers between devices with their start and end apart: 1, of which 0 were waited for; matrix products, arithmetic and copies ran while one was open for 1% of the time, Pallas kernels for 0%

commit v1 on v0

v1 whole, which is shorter than its diff:
```python
import functools

import jax
import jax.numpy as jnp
from jax import lax
from jax.experimental import pallas as pl
from jax.experimental.pallas import tpu as pltpu
from jax.sharding import PartitionSpec as P

SIDE = 16
LANES = 128
CHUNK = 16
shift_ratio = 0.1
F32 = jnp.float32
BF16 = jnp.bfloat16


def iota(shape, dim):
    return lax.broadcasted_iota(jnp.int32, shape, dim)


def jac_kernel(act_ref, cot_ref, out_ref):
    mats = act_ref.shape[1]
    owners = out_ref.shape[0]
    share = out_ref.shape[2] // mats
    jacs = [
        lax.dot_general(
            act_ref[0, m], cot_ref[0, m], (((0,), (0,)), ((), ())), preferred_element_type=F32
        )
        for m in range(mats)
    ]
    for owner in range(owners):
        rows = [jac[owner * share : (owner + 1) * share] for jac in jacs]
        out_ref[owner, 0] = jnp.concatenate(rows, axis=0).astype(BF16)


def jac_rows(activations, cotangents, owners):
    samples, mats, sites, d = activations.shape
    rows = mats * d // owners
    block = pl.BlockSpec((1, mats, sites, d), lambda s: (s, 0, 0, 0))
    return pl.pallas_call(
        jac_kernel,
        grid=(samples,),
        in_specs=[block, block],
        out_specs=pl.BlockSpec((owners, 1, rows, d), lambda s: (0, s, 0, 0)),
        out_shape=jax.ShapeDtypeStruct((owners, samples, rows, d), BF16),
        cost_estimate=pl.CostEstimate(
            flops=2 * samples * mats * sites * d * d,
            bytes_accessed=6 * samples * mats * sites * d,
            transcendentals=0,
        ),
        name="jac_rows",
    )(activations, cotangents)


def energy_kernel(spins_ref, offdiag_ref, out_ref):
    total, width = out_ref.shape
    local = spins_ref.shape[0]
    sites = SIDE * SIDE
    z = (2 * spins_ref[...] - 1).astype(F32)
    column = iota((local, sites), 1) % SIDE
    right = jnp.where(
        column == SIDE - 1, pltpu.roll(z, SIDE - 1, 1), pltpu.roll(z, sites - 1, 1)
    )
    below = pltpu.roll(z, sites - SIDE, 1)
    energy = offdiag_ref[...] + jnp.sum(z * (right + below), axis=1, keepdims=True)
    first = lax.axis_index("samp") * local
    mine = lax.axis_index("layer") == 0
    spread = jnp.concatenate([energy] * (total // local), axis=0)
    row = iota((total, width), 0)
    here = (row >= first) & (row < first + local) & (iota((total, width), 1) == total) & mine
    out_ref[...] = jnp.where(here, spread, F32(0.0))


def energy_column(spins, offdiag, total, width):
    return pl.pallas_call(
        energy_kernel,
        out_shape=jax.ShapeDtypeStruct((total, width), F32),
        name="energy_column",
    )(spins, offdiag[:, None])


def gram_kernel(rows_ref, start_ref, out_ref):
    total, _, d = rows_ref.shape
    width = out_ref.shape[1]

    @pl.when(pl.program_id(0) == 0)
    def _():
        out_ref[...] = start_ref[...]

    block = CHUNK * CHUNK
    dest = iota((block, block), 0)
    source = (dest % CHUNK) * CHUNK + dest // CHUNK
    swap = (iota((block, block), 1) == source).astype(F32).astype(BF16)
    swapped = []
    for c in range(total // CHUNK):
        piece = rows_ref[c * CHUNK : (c + 1) * CHUNK].reshape(block, d)
        swapped.append(jnp.dot(swap, piece, preferred_element_type=F32).astype(BF16))
    acc = jnp.zeros((total, total), F32)
    for r in range(CHUNK):
        flat = jnp.concatenate([t[r * CHUNK : (r + 1) * CHUNK] for t in swapped], axis=0)
        acc = acc + lax.dot_general(
            flat, flat, (((1,), (1,)), ((), ())), preferred_element_type=F32
        )
    out_ref[:, :total] += acc


def gram_partial(rows, start):
    total, count, d = rows.shape
    width = start.shape[1]
    whole = pl.BlockSpec((total, width), lambda i: (0, 0))
    return pl.pallas_call(
        gram_kernel,
        grid=(count // CHUNK,),
        in_specs=[pl.BlockSpec((total, CHUNK, d), lambda i: (0, i, 0)), whole],
        out_specs=whole,
        out_shape=jax.ShapeDtypeStruct((total, width), F32),
        cost_estimate=pl.CostEstimate(
            flops=2 * total * total * count * d,
            bytes_accessed=2 * total * count * d,
            transcendentals=0,
        ),
        name="gram_partial",
    )(rows, start)


def eliminate(matrix, total):
    row = iota(matrix.shape, 0)
    lane = iota(matrix.shape, 1)
    if total <= 64:
        for k in range(total):
            column = matrix[:, k : k + 1]
            pivot_row = matrix[k : k + 1, :]
            scaled = pivot_row * (F32(1.0) / pivot_row[:, k : k + 1])
            matrix = matrix - jnp.where(row == k, F32(0.0), column) * scaled
    else:

        def one(k, held):
            column = jnp.sum(jnp.where(lane == k, held, F32(0.0)), axis=1, keepdims=True)
            pivot_row = jnp.sum(jnp.where(row == k, held, F32(0.0)), axis=0, keepdims=True)
            here = lane[:1] == k
            pivot = jnp.sum(jnp.where(here, pivot_row, F32(0.0)), axis=1, keepdims=True)
            scaled = pivot_row * (F32(1.0) / pivot)
            return held - jnp.where(row == k, F32(0.0), column) * scaled

        matrix = lax.fori_loop(0, total, one, matrix)
    diag = jnp.sum(jnp.where(row == lane, matrix, F32(0.0)), axis=1, keepdims=True)
    return matrix[:, total : total + 1] / diag


def solve_kernel(gram_ref, rows_ref, weights_ref, update_ref):
    total, width = gram_ref.shape
    mats, share, d = update_ref.shape
    local = weights_ref.shape[1]
    raw = gram_ref[...]
    row = iota((total, width), 0)
    lane = iota((total, width), 1)
    inside = lane < total
    scale = F32(1.0 / total)
    row_mean = jnp.sum(jnp.where(inside, raw, F32(0.0)), axis=1, keepdims=True) * scale
    col_mean = jnp.sum(raw, axis=0, keepdims=True) * scale
    mean = jnp.sum(row_mean, axis=0, keepdims=True) * scale
    gram = (raw - col_mean - row_mean + mean) * scale
    eps = (raw - col_mean) * F32(1.0 / total**0.5)
    on_diag = row == lane
    trace = jnp.sum(
        jnp.sum(jnp.where(on_diag, gram, F32(0.0)), axis=1, keepdims=True), axis=0, keepdims=True
    )
    shift = F32(shift_ratio) * trace * scale
    system = jnp.where(inside, gram + jnp.where(on_diag, shift, F32(0.0)), eps)
    weights = eliminate(system, total)
    first = lax.axis_index("samp") * local
    own = jnp.where(row - first == lane, weights, F32(0.0))
    weights_ref[...] = jnp.sum(own, axis=0, keepdims=True)[:, :local]
    coeffs = weights - jnp.sum(weights, axis=0, keepdims=True) * scale
    coeffs = jnp.broadcast_to(coeffs, (total, d))
    acc = jnp.zeros((mats * share, d), F32)
    for s in range(total):
        acc = acc + coeffs[s : s + 1] * rows_ref[s].astype(F32)
    for m in range(mats):
        update_ref[m] = acc[m * share : (m + 1) * share]


def solve_and_project(gram, rows, local, mats):
    total, count, d = rows.shape
    return pl.pallas_call(
        solve_kernel,
        out_shape=(
            jax.ShapeDtypeStruct((1, local), F32),
            jax.ShapeDtypeStruct((mats, count // mats, d), F32),
        ),
        name="solve_and_project",
    )(gram, rows)


def body(spins, activations, cotangents, offdiag):
    local, mats = activations.shape[:2]
    owners = lax.axis_size("samp")
    total = local * owners
    width = (total // LANES + 1) * LANES
    jac = jac_rows(activations, cotangents, owners)
    rows = lax.all_to_all(jac, "samp", split_axis=0, concat_axis=0, tiled=True)
    rows = rows.reshape(total, rows.shape[2], rows.shape[3])
    partial = gram_partial(rows, energy_column(spins, offdiag, total, width))
    gram = lax.psum(partial, ("samp", "layer"))
    weights, update = solve_and_project(gram, rows, local, mats)
    return weights.reshape(local), update


def solution(mesh):
    placed = (
        P("samp", None),
        P("samp", "layer", None, None),
        P("samp", "layer", None, None),
        P("samp"),
    )
    return jax.shard_map(
        body,
        mesh=mesh,
        in_specs=placed,
        out_specs=(P("samp"), P("layer", "samp", None)),
        check_vma=False,
    )
```

time: 357 us -> 117 us (0.33)
  local copies, waits for them, and re-layouts: 98.7 us -> 2.01 us
  matrix products: 89.8 us -> 0 us
  blocking collectives: 94.4 us -> 38.6 us
  loops' own time: 46.6 us -> 0 us
  waiting for transfers between devices: 0.01 us -> 46 us
  Pallas kernels: 0 us -> 21.4 us
  other arithmetic: 10.1 us -> 0 us
  between operations: 7.88 us -> 0.64 us
    dot_general x252 -> x0, matrix products: 89.8 us -> none  [the longest x64 49.6 us: one_row(): known = jnp.dot(lower_row, inverse, precision=highest)]
    dynamic_slice x129 -> x0, local copies, waits for them, and re-layouts: 76 us -> none  [the longest x64 37.8 us: one_column(): pivot = jnp.sqrt(lax.dynamic_slice_in_dim(column, j, 1)[0])]
    unnamed x1 -> x0, blocking collectives: 48 us -> none
    another operation x16 -> x0, loops' own time: 46.6 us -> none  [the longest x8 45.6 us: small_factor(): return lax.fori_loop(0, order, one_column, start)[1]]
    all_to_all x1, waiting for transfers between devices: 0.01 us -> 46 us  [body(): rows = lax.all_to_all(jac, 'samp', split_axis=0, concat_axis=0, tiled=True)]
    pallas_call x0 -> x4, Pallas kernels: none -> 21.4 us  [the longest x1 8.46 us: solve_and_project(): pl.pallas_call(solve_kernel, out_shape=(jax.ShapeDtypeStruct((1, local),...]
    psum x1, blocking collectives: 46.3 us -> 38.6 us  [body(): gram = lax.psum(partial, ('samp', 'layer'))]
    unnamed x21 -> x4, local copies, waits for them, and re-layouts: 6.27 us -> 1.34 us
  transfers between devices with their start and end apart: 1 -> 1, of which waited for: 0 -> 1; matrix products, arithmetic and copies ran while one was open for 1% -> 1% of each run, Pallas kernels for 0% -> 1%
where the time goes in v1:
time: 117 us; the launch traced here: 116 us
  waiting for transfers between devices  46 us (39%)
  blocking collectives  38.6 us (33%)
  Pallas kernels  21.4 us (18%)
  starting transfers between devices  7.41 us (6%)
  local copies, waits for them, and re-layouts  2.01 us (2%)
    all_to_all x1, waiting for transfers between devices, body(): rows = lax.all_to_all(jac, 'samp', split_axis=0, concat_axis=0, tiled=True)  46 us
    psum x1, blocking collectives, body(): gram = lax.psum(partial, ('samp', 'layer'))  38.6 us
    pallas_call x1, Pallas kernels, solve_and_project(): pl.pallas_call(solve_kernel, out_shape=(jax.ShapeDtypeStruct((1, local),...  8.46 us
    all_to_all x1, starting transfers between devices, body(): rows = lax.all_to_all(jac, 'samp', split_axis=0, concat_axis=0, tiled=True)  7.41 us
    pallas_call x1, Pallas kernels, jac_rows(): pl.pallas_call(jac_kernel, grid=(samples,), in_specs=[block, block], out_...  6.99 us
    pallas_call x1, Pallas kernels, gram_partial(): pl.pallas_call(gram_kernel, grid=(count // CHUNK,), in_specs=[pl.BlockSpe...  4.37 us
  transfers between devices with their start and end apart: 1, of which 1 were waited for; matrix products, arithmetic and copies ran while one was open for 1% of the time, Pallas kernels for 1%

profile of v1, /device:TPU:0, one launch (start us, length us, event | category | flops | bytes accessed | tf_op | source)
XLA Modules:
  0.0 116.0 jit_solution(474885132432813443)
XLA Ops:
  0.6 7.0 %jac_rows.1 = bf16[8,8,64,256]{3,2,1,0:T(8,128)(2,1)} custom-call(bf16[8,2,256,256]{3,2,1,0:T(8,128)(2,1)} %act_ref.1, bf16[8,2,256,256]{3,2,1,0:T(8,128)(2,1)} %cot_ref.1), custom_call_target="tpu_custom_call" | custom-call | flops 536870912 | bytes 6291456 | tf_op jit(solution)/shard_map/jac_rows/pallas_call | solution.py:41
  7.6 0.0 copy-start.1
  7.6 7.4 %all-to-all-start = ((bf16[8,8,64,256]{3,2,1,0:T(8,128)(2,1)}), bf16[8,8,64,256]{3,2,1,0:T(8,128)(2,1)S(1)}, u32[]{:S(2)}, u32[]{:S(2)}) async-start(bf16[8,8,64,256]{3,2,1,0:T(8,128)(2,1)} %jac_rows.1), calls=%async_computation | async-start | bytes 4194304 | tf_op jit(solution)/shard_map/all_to_all | solution.py:202
  15.0 0.0 copy-done.1
  15.0 0.7 copy.6.offdiag_ref
  15.7 1.6 %energy_column.1.start_ref = f32[64,128]{1,0:T(8,128)} custom-call(s32[8,256]{1,0:T(8,128)} %spins_ref.1, f32[8,1]{1,0:T(8,128)} %copy.6.offdiag_ref), custom_call_target="tpu_custom_call" | custom-call | tf_op jit(solution)/shard_map/energy_column/pallas_call | solution.py:76
  17.3 46.0 %all-to-all-done = bf16[8,8,64,256]{3,2,1,0:T(8,128)(2,1)S(1)} async-done(((bf16[8,8,64,256]{3,2,1,0:T(8,128)(2,1)}), bf16[8,8,64,256]{3,2,1,0:T(8,128)(2,1)S(1)}, u32[]{:S(2)}, u32[]{:S(2)}) %all-to-all-start) | async-done | bytes 2097184 | tf_op jit(solution)/shard_map/all_to_all | solution.py:202
  63.3 0.0 copy-start
  63.3 1.3 %copy-done = bf16[8,8,64,256]{3,2,1,0:T(8,128)(2,1)} copy-done((bf16[8,8,64,256]{3,2,1,0:T(8,128)(2,1)}, bf16[8,8,64,256]{3,2,1,0:T(8,128)(2,1)S(1)}, u32[]{:S(2)}) %copy-start) | copy-done | bytes 2097176
  64.6 4.4 %gram_partial.1 = f32[64,128]{1,0:T(8,128)} custom-call(bf16[64,64,256]{2,1,0:T(8,128)(2,1)} %bitcast.3, f32[64,128]{1,0:T(8,128)} %energy_column.1.start_ref), custom_call_target="tpu_custom_call" | custom-call | flops 134217728 | bytes 2097152 | tf_op jit(solution)/shard_map/gram_partial/pallas_call | solution.py:112
  69.0 38.6 %psum.7.gram_ref = f32[64,128]{1,0:T(8,128)} all-reduce(f32[64,128]{1,0:T(8,128)} %gram_partial.1), channel_id=1, replica_groups=mesh['samp'=8,'layer'=4] {'samp','layer'}, use_global_device_ids=true, to_apply=%region_0.0 | all-reduce | flops 8192 | bytes 65536 | tf_op jit(solution)/shard_map/psum | solution.py:205
  107.5 8.5 %solve_and_project.1 = (f32[1,8]{1,0:T(1,128)}, f32[2,32,256]{2,1,0:T(8,128)}) custom-call(f32[64,128]{1,0:T(8,128)} %psum.7.gram_ref, bf16[64,64,256]{2,1,0:T(8,128)(2,1)} %bitcast.4), custom_call_target="tpu_custom_call" | custom-call | tf_op jit(solution)/shard_map/solve_and_project/pallas_call | solution.py:186
Async XLA Ops:
  7.6 7.4 %copy-start.1 = (f32[8]{0:T(128)S(1)}, f32[8]{0:T(128)}, u32[]{:S(2)}) copy-start(f32[8]{0:T(128)} %param.7) | copy-start | bytes 100
  7.6 55.7 %all-to-all-start = ((bf16[8,8,64,256]{3,2,1,0:T(8,128)(2,1)}), bf16[8,8,64,256]{3,2,1,0:T(8,128)(2,1)S(1)}, u32[]{:S(2)}, u32[]{:S(2)}) async-start(bf16[8,8,64,256]{3,2,1,0:T(8,128)(2,1)} %jac_rows.1), calls=%async_computation | async-start | bytes 4194304 | tf_op jit(solution)/shard_map/all_to_all | solution.py:202
  63.3 1.3 %copy-start = (bf16[8,8,64,256]{3,2,1,0:T(8,128)(2,1)}, bf16[8,8,64,256]{3,2,1,0:T(8,128)(2,1)S(1)}, u32[]{:S(2)}) copy-start(bf16[8,8,64,256]{3,2,1,0:T(8,128)(2,1)S(1)} %all-to-all-done) | copy-start | bytes 6291460

commit v2 on v1

--- a/solution.py
+++ b/solution.py
@@ -148,11 +148,27 @@
     return matrix[:, total : total + 1] / diag
 
 
-def solve_kernel(gram_ref, rows_ref, weights_ref, update_ref):
-    total, width = gram_ref.shape
+def tree_sum(parts):
+    while len(parts) > 1:
+        parts = [a + b for a, b in zip(parts[::2], parts[1::2])]
+    return parts[0]
+
+
+def partners(value, axis, first, count):
+    size = lax.axis_size(axis)
+    parts = [value]
+    for k in range(1, count):
+        perm = [(i, i ^ (k * first)) for i in range(size)]
+        parts.append(lax.ppermute(value, axis, perm))
+    return parts
+
+
+def solve_kernel(*refs):
+    *gram_refs, rows_ref, weights_ref, update_ref = refs
+    total, width = gram_refs[0].shape
     mats, share, d = update_ref.shape
     local = weights_ref.shape[1]
-    raw = gram_ref[...]
+    raw = tree_sum([ref[...] for ref in gram_refs])
     row = iota((total, width), 0)
     lane = iota((total, width), 1)
     inside = lane < total
@@ -181,7 +197,7 @@
         update_ref[m] = acc[m * share : (m + 1) * share]
 
 
-def solve_and_project(gram, rows, local, mats):
+def solve_and_project(grams, rows, local, mats):
     total, count, d = rows.shape
     return pl.pallas_call(
         solve_kernel,
@@ -190,7 +206,7 @@
             jax.ShapeDtypeStruct((mats, count // mats, d), F32),
         ),
         name="solve_and_project",
-    )(gram, rows)
+    )(*grams, rows)
 
 
 def body(spins, activations, cotangents, offdiag):
@@ -202,8 +218,12 @@
     rows = lax.all_to_all(jac, "samp", split_axis=0, concat_axis=0, tiled=True)
     rows = rows.reshape(total, rows.shape[2], rows.shape[3])
     partial = gram_partial(rows, energy_column(spins, offdiag, total, width))
-    gram = lax.psum(partial, ("samp", "layer"))
-    weights, update = solve_and_project(gram, rows, local, mats)
+    gram = tree_sum(partners(partial, "layer", 1, lax.axis_size("layer")))
+    reach = min(owners, 8)
+    grams = partners(gram, "samp", 1, reach)
+    if owners > reach:
+        grams = partners(tree_sum(grams), "samp", reach, owners // reach)
+    weights, update = solve_and_project(grams, rows, local, mats)
     return weights.reshape(local), update
 
 

time: 117 us -> 100 us (0.85)
  blocking collectives: 38.6 us -> 0 us
  starting transfers between devices: 7.41 us -> 20.5 us
  waiting for transfers between devices: 46 us -> 53.4 us
    psum x1 -> x0, blocking collectives: 38.6 us -> none  [body(): gram = lax.psum(partial, ('samp', 'layer'))]
    ppermute x0 -> x10, starting transfers between devices: none -> 13.1 us  [partners(): parts.append(lax.ppermute(value, axis, perm))]
    ppermute x0 -> x10, waiting for transfers between devices: none -> 7.41 us  [partners(): parts.append(lax.ppermute(value, axis, perm))]
  transfers between devices with their start and end apart: 1 -> 11, of which waited for: 1 -> 5; matrix products, arithmetic and copies ran while one was open for 1% -> 1% of each run, Pallas kernels for 1% -> 2%
where the time goes in v2:
time: 100 us; the launch traced here: 99.6 us
  waiting for transfers between devices  53.4 us (53%)
  Pallas kernels  21.6 us (22%)
  starting transfers between devices  20.5 us (20%)
  local copies, waits for them, and re-layouts  2.63 us (3%)
    all_to_all x1, waiting for transfers between devices, body(): rows = lax.all_to_all(jac, 'samp', split_axis=0, concat_axis=0, tiled=True)  46 us
    ppermute x10, starting transfers between devices, partners(): parts.append(lax.ppermute(value, axis, perm))  13.1 us
    pallas_call x1, Pallas kernels, solve_and_project(): pl.pallas_call(solve_kernel, out_shape=(jax.ShapeDtypeStruct((1, local),...  8.61 us
    all_to_all x1, starting transfers between devices, body(): rows = lax.all_to_all(jac, 'samp', split_axis=0, concat_axis=0, tiled=True)  7.41 us
    ppermute x10, waiting for transfers between devices, partners(): parts.append(lax.ppermute(value, axis, perm))  7.41 us
    pallas_call x1, Pallas kernels, jac_rows(): pl.pallas_call(jac_kernel, grid=(samples,), in_specs=[block, block], out_...  7.02 us
    pallas_call x1, Pallas kernels, gram_partial(): pl.pallas_call(gram_kernel, grid=(count // CHUNK,), in_specs=[pl.BlockSpe...  4.38 us
  transfers between devices with their start and end apart: 11, of which 5 were waited for; matrix products, arithmetic and copies ran while one was open for 1% of the time, Pallas kernels for 2%

profile of v2, /device:TPU:0, one launch (start us, length us, event | category | flops | bytes accessed | tf_op | source)
XLA Modules:
  0.0 99.6 jit_solution(9017880465512531405)
XLA Ops:
  0.6 7.0 %jac_rows.1 = bf16[8,8,64,256]{3,2,1,0:T(8,128)(2,1)} custom-call(bf16[8,2,256,256]{3,2,1,0:T(8,128)(2,1)} %act_ref.1, bf16[8,2,256,256]{3,2,1,0:T(8,128)(2,1)} %cot_ref.1), custom_call_target="tpu_custom_call" | custom-call | flops 536870912 | bytes 6291456 | tf_op jit(solution)/shard_map/jac_rows/pallas_call | solution.py:41
  7.6 0.0 copy-start.9
  7.7 7.4 %all-to-all-start = ((bf16[8,8,64,256]{3,2,1,0:T(8,128)(2,1)}), bf16[8,8,64,256]{3,2,1,0:T(8,128)(2,1)S(1)}, u32[]{:S(2)}, u32[]{:S(2)}) async-start(bf16[8,8,64,256]{3,2,1,0:T(8,128)(2,1)} %jac_rows.1), calls=%async_computation | async-start | bytes 4194304 | tf_op jit(solution)/shard_map/all_to_all | solution.py:218
  15.1 0.0 copy-done.9
  15.1 0.7 copy.6.offdiag_ref
  15.7 1.6 %energy_column.1.start_ref = f32[64,128]{1,0:T(8,128)} custom-call(s32[8,256]{1,0:T(8,128)} %spins_ref.1, f32[8,1]{1,0:T(8,128)} %copy.6.offdiag_ref), custom_call_target="tpu_custom_call" | custom-call | tf_op jit(solution)/shard_map/energy_column/pallas_call | solution.py:76
  17.3 46.0 %all-to-all-done = bf16[8,8,64,256]{3,2,1,0:T(8,128)(2,1)S(1)} async-done(((bf16[8,8,64,256]{3,2,1,0:T(8,128)(2,1)}), bf16[8,8,64,256]{3,2,1,0:T(8,128)(2,1)S(1)}, u32[]{:S(2)}, u32[]{:S(2)}) %all-to-all-start) | async-done | bytes 2097184 | tf_op jit(solution)/shard_map/all_to_all | solution.py:218
  63.3 0.0 copy-start
  63.3 1.3 %copy-done = bf16[8,8,64,256]{3,2,1,0:T(8,128)(2,1)} copy-done((bf16[8,8,64,256]{3,2,1,0:T(8,128)(2,1)}, bf16[8,8,64,256]{3,2,1,0:T(8,128)(2,1)S(1)}, u32[]{:S(2)}) %copy-start) | copy-done | bytes 2097176
  64.6 4.4 %gram_partial.1 = f32[64,128]{1,0:T(8,128)} custom-call(bf16[64,64,256]{2,1,0:T(8,128)(2,1)} %bitcast.3, f32[64,128]{1,0:T(8,128)} %energy_column.1.start_ref), custom_call_target="tpu_custom_call" | custom-call | flops 134217728 | bytes 2097152 | tf_op jit(solution)/shard_map/gram_partial/pallas_call | solution.py:112
  69.0 0.0 collective-permute-start
  69.0 1.5 %collective-permute-start.1 = (f32[64,128]{1,0:T(8,128)}, f32[64,128]{1,0:T(8,128)S(1)}, u32[]{:S(2)}, u32[]{:S(2)}) collective-permute-start(f32[64,128]{1,0:T(8,128)} %gram_partial.1), channel_id=1, source_target_pairs={{0,2},{1,3},{2,0},{3,1},{4,6},{5,7},{6,4},{7,5},{8,10},{9,11},{10,... | collective-permute-start | bytes 98312 | tf_op jit(solution)/shard_map/ppermute | solution.py:162
  70.5 0.4 collective-permute-start.2
  70.9 0.0 collective-permute-done
  70.9 2.3 %collective-permute-done.1 = f32[64,128]{1,0:T(8,128)S(1)} collective-permute-done((f32[64,128]{1,0:T(8,128)}, f32[64,128]{1,0:T(8,128)S(1)}, u32[]{:S(2)}, u32[]{:S(2)}) %collective-permute-start.1) | collective-permute-done | bytes 32800 | tf_op jit(solution)/shard_map/ppermute | solution.py:162
  73.1 0.9 collective-permute-done.2
  74.0 0.8 add_add_fusion.refs_0_
  74.8 0.0 copy-start.1
  74.8 1.5 %collective-permute-start.3 = (f32[64,128]{1,0:T(8,128)S(1)}, f32[64,128]{1,0:T(8,128)S(1)}, u32[]{:S(2)}, u32[]{:S(2)}) collective-permute-start(f32[64,128]{1,0:T(8,128)S(1)} %add_add_fusion.refs_0_), channel_id=1, source_target_pairs={{0,4},{4,0},{8,12},{12,8},{16,20},{20,16},{24,28},{28,24},{1,5},{5... | collective-permute-start | bytes 98312 | tf_op jit(solution)/shard_map/ppermute | solution.py:162
  76.4 0.0 collective-permute-start.4
  76.4 2.0 %collective-permute-start.5 = (f32[64,128]{1,0:T(8,128)S(1)}, f32[64,128]{1,0:T(8,128)S(1)}, u32[]{:S(2)}, u32[]{:S(2)}) collective-permute-start(f32[64,128]{1,0:T(8,128)S(1)} %add_add_fusion.refs_0_), channel_id=1, source_target_pairs={{0,12},{4,8},{8,4},{12,0},{16,28},{20,24},{24,20},{28,16},{1,13},{... | collective-permute-start | bytes 98312 | tf_op jit(solution)/shard_map/ppermute | solution.py:162
  78.4 0.8 collective-permute-start.6
  79.2 3.0 %collective-permute-start.7 = (f32[64,128]{1,0:T(8,128)S(1)}, f32[64,128]{1,0:T(8,128)S(1)}, u32[]{:S(2)}, u32[]{:S(2)}) collective-permute-start(f32[64,128]{1,0:T(8,128)S(1)} %add_add_fusion.refs_0_), channel_id=1, source_target_pairs={{0,20},{4,16},{8,28},{12,24},{16,4},{20,0},{24,12},{28,8},{1,21},{... | collective-permute-start | bytes 98312 | tf_op jit(solution)/shard_map/ppermute | solution.py:162
  82.2 0.0 collective-permute-done.3.refs_1_
  82.2 0.0 copy-start.2
  82.2 1.5 %collective-permute-start.8 = (f32[64,128]{1,0:T(8,128)S(1)}, f32[64,128]{1,0:T(8,128)S(1)}, u32[]{:S(2)}, u32[]{:S(2)}) collective-permute-start(f32[64,128]{1,0:T(8,128)S(1)} %add_add_fusion.refs_0_), channel_id=1, source_target_pairs={{0,24},{4,28},{8,16},{12,20},{16,8},{20,12},{24,0},{28,4},{1,25},{... | collective-permute-start | bytes 98312 | tf_op jit(solution)/shard_map/ppermute | solution.py:162
  83.7 0.0 collective-permute-done.4.refs_2_
  83.7 0.0 copy-start.3
  83.7 2.3 %collective-permute-start.9 = (f32[64,128]{1,0:T(8,128)S(1)}, f32[64,128]{1,0:T(8,128)S(1)}, u32[]{:S(2)}, u32[]{:S(2)}) collective-permute-start(f32[64,128]{1,0:T(8,128)S(1)} %add_add_fusion.refs_0_), channel_id=1, source_target_pairs={{0,28},{4,24},{8,20},{12,16},{16,12},{20,8},{24,4},{28,0},{1,29},{... | collective-permute-start | bytes 98312 | tf_op jit(solution)/shard_map/ppermute | solution.py:162
  86.0 0.0 collective-permute-done.5.refs_3_
  86.0 0.0 copy-start.4
  86.0 0.0 collective-permute-done.6.refs_4_
  86.1 0.0 copy-start.5
  86.1 0.0 collective-permute-done.7.refs_5_
  86.1 0.0 copy-start.6
  86.1 2.0 %collective-permute-done.8.refs_6_ = f32[64,128]{1,0:T(8,128)S(1)} collective-permute-done((f32[64,128]{1,0:T(8,128)S(1)}, f32[64,128]{1,0:T(8,128)S(1)}, u32[]{:S(2)}, u32[]{:S(2)}) %collective-permute-start.8) | collective-permute-done | bytes 32800 | tf_op jit(solution)/shard_map/ppermute | solution.py:162
  88.1 0.0 copy-start.7
  88.1 2.2 %collective-permute-done.9.refs_7_ = f32[64,128]{1,0:T(8,128)S(1)} collective-permute-done((f32[64,128]{1,0:T(8,128)S(1)}, f32[64,128]{1,0:T(8,128)S(1)}, u32[]{:S(2)}, u32[]{:S(2)}) %collective-permute-start.9) | collective-permute-done | bytes 32800 | tf_op jit(solution)/shard_map/ppermute | solution.py:162
  90.3 0.0 copy-done.1
  90.3 0.0 copy-done.2
  90.3 0.0 copy-done.3
  90.3 0.0 copy-done.4
  90.3 0.0 copy-done.5
  90.3 0.0 copy-done.6
  90.3 0.0 copy-done.7
  90.4 0.0 copy-start.8
  90.4 0.6 copy-done.8
  91.0 8.6 %solve_and_project.1 = (f32[1,8]{1,0:T(1,128)}, f32[2,32,256]{2,1,0:T(8,128)}) custom-call(f32[64,128]{1,0:T(8,128)} %copy-done.1, f32[64,128]{1,0:T(8,128)} %copy-done.2, f32[64,128]{1,0:T(8,128)} %copy-done.3, f32[64,128]{1,0:T(8,128)} %copy-done.4, f32[64,128]{1,0:T(8,128)} %copy-done.5, f32[64,128]{1,0:T(8,128)} %copy-done.6, f32[64,128]{1,0:T(8,128)} %copy-done.7, ...), custom_call_target="tpu_custom_call" | custom-call | tf_op jit(solution)/shard_map/solve_and_project/pallas_call | solution.py:202
Async XLA Ops:
  7.6 7.4 %copy-start.9 = (f32[8]{0:T(128)S(1)}, f32[8]{0:T(128)}, u32[]{:S(2)}) copy-start(f32[8]{0:T(128)} %param.7) | copy-start | bytes 100
  7.7 55.6 %all-to-all-start = ((bf16[8,8,64,256]{3,2,1,0:T(8,128)(2,1)}), bf16[8,8,64,256]{3,2,1,0:T(8,128)(2,1)S(1)}, u32[]{:S(2)}, u32[]{:S(2)}) async-start(bf16[8,8,64,256]{3,2,1,0:T(8,128)(2,1)} %jac_rows.1), calls=%async_computation | async-start | bytes 4194304 | tf_op jit(solution)/shard_map/all_to_all | solution.py:218
  63.3 1.3 %copy-start = (bf16[8,8,64,256]{3,2,1,0:T(8,128)(2,1)}, bf16[8,8,64,256]{3,2,1,0:T(8,128)(2,1)S(1)}, u32[]{:S(2)}) copy-start(bf16[8,8,64,256]{3,2,1,0:T(8,128)(2,1)S(1)} %all-to-all-done) | copy-start | bytes 6291460
  69.0 1.9 %collective-permute-start = (f32[64,128]{1,0:T(8,128)}, f32[64,128]{1,0:T(8,128)S(1)}, u32[]{:S(2)}, u32[]{:S(2)}) collective-permute-start(f32[64,128]{1,0:T(8,128)} %gram_partial.1), channel_id=1, source_target_pairs={{0,1},{1,0},{2,3},{3,2},{4,5},{5,4},{6,7},{7,6},{8,9},{9,8},{10,11... | collective-permute-start | bytes 98312 | tf_op jit(solution)/shard_map/ppermute | solution.py:162
  69.0 4.1 %collective-permute-start.1 = (f32[64,128]{1,0:T(8,128)}, f32[64,128]{1,0:T(8,128)S(1)}, u32[]{:S(2)}, u32[]{:S(2)}) collective-permute-start(f32[64,128]{1,0:T(8,128)} %gram_partial.1), channel_id=1, source_target_pairs={{0,2},{1,3},{2,0},{3,1},{4,6},{5,7},{6,4},{7,5},{8,10},{9,11},{10,... | collective-permute-start | bytes 98312 | tf_op jit(solution)/shard_map/ppermute | solution.py:162
  70.5 3.6 %collective-permute-start.2 = (f32[64,128]{1,0:T(8,128)}, f32[64,128]{1,0:T(8,128)S(1)}, u32[]{:S(2)}, u32[]{:S(2)}) collective-permute-start(f32[64,128]{1,0:T(8,128)} %gram_partial.1), channel_id=1, source_target_pairs={{0,3},{1,2},{2,1},{3,0},{4,7},{5,6},{6,5},{7,4},{8,11},{9,10},{10,... | collective-permute-start | bytes 98312 | tf_op jit(solution)/shard_map/ppermute | solution.py:162
  74.8 15.5 %copy-start.1 = (f32[64,128]{1,0:T(8,128)}, f32[64,128]{1,0:T(8,128)S(1)}, u32[]{:S(2)}) copy-start(f32[64,128]{1,0:T(8,128)S(1)} %add_add_fusion.refs_0_) | copy-start | bytes 98308
  74.8 7.4 %collective-permute-start.3 = (f32[64,128]{1,0:T(8,128)S(1)}, f32[64,128]{1,0:T(8,128)S(1)}, u32[]{:S(2)}, u32[]{:S(2)}) collective-permute-start(f32[64,128]{1,0:T(8,128)S(1)} %add_add_fusion.refs_0_), channel_id=1, source_target_pairs={{0,4},{4,0},{8,12},{12,8},{16,20},{20,16},{24,28},{28,24},{1,5},{5... | collective-permute-start | bytes 98312 | tf_op jit(solution)/shard_map/ppermute | solution.py:162
  76.4 7.3 %collective-permute-start.4 = (f32[64,128]{1,0:T(8,128)S(1)}, f32[64,128]{1,0:T(8,128)S(1)}, u32[]{:S(2)}, u32[]{:S(2)}) collective-permute-start(f32[64,128]{1,0:T(8,128)S(1)} %add_add_fusion.refs_0_), channel_id=1, source_target_pairs={{0,8},{4,12},{8,0},{12,4},{16,24},{20,28},{24,16},{28,20},{1,9},{5... | collective-permute-start | bytes 98312 | tf_op jit(solution)/shard_map/ppermute | solution.py:162
  76.4 9.7 %collective-permute-start.5 = (f32[64,128]{1,0:T(8,128)S(1)}, f32[64,128]{1,0:T(8,128)S(1)}, u32[]{:S(2)}, u32[]{:S(2)}) collective-permute-start(f32[64,128]{1,0:T(8,128)S(1)} %add_add_fusion.refs_0_), channel_id=1, source_target_pairs={{0,12},{4,8},{8,4},{12,0},{16,28},{20,24},{24,20},{28,16},{1,13},{... | collective-permute-start | bytes 98312 | tf_op jit(solution)/shard_map/ppermute | solution.py:162
  78.4 7.7 %collective-permute-start.6 = (f32[64,128]{1,0:T(8,128)S(1)}, f32[64,128]{1,0:T(8,128)S(1)}, u32[]{:S(2)}, u32[]{:S(2)}) collective-permute-start(f32[64,128]{1,0:T(8,128)S(1)} %add_add_fusion.refs_0_), channel_id=1, source_target_pairs={{0,16},{4,20},{8,24},{12,28},{16,0},{20,4},{24,8},{28,12},{1,17},{... | collective-permute-start | bytes 98312 | tf_op jit(solution)/shard_map/ppermute | solution.py:162
  79.2 6.9 %collective-permute-start.7 = (f32[64,128]{1,0:T(8,128)S(1)}, f32[64,128]{1,0:T(8,128)S(1)}, u32[]{:S(2)}, u32[]{:S(2)}) collective-permute-start(f32[64,128]{1,0:T(8,128)S(1)} %add_add_fusion.refs_0_), channel_id=1, source_target_pairs={{0,20},{4,16},{8,28},{12,24},{16,4},{20,0},{24,12},{28,8},{1,21},{... | collective-permute-start | bytes 98312 | tf_op jit(solution)/shard_map/ppermute | solution.py:162
  82.2 8.1 %copy-start.2 = (f32[64,128]{1,0:T(8,128)}, f32[64,128]{1,0:T(8,128)S(1)}, u32[]{:S(2)}) copy-start(f32[64,128]{1,0:T(8,128)S(1)} %collective-permute-done.3.refs_1_) | copy-start | bytes 98308
  82.2 5.9 %collective-permute-start.8 = (f32[64,128]{1,0:T(8,128)S(1)}, f32[64,128]{1,0:T(8,128)S(1)}, u32[]{:S(2)}, u32[]{:S(2)}) collective-permute-start(f32[64,128]{1,0:T(8,128)S(1)} %add_add_fusion.refs_0_), channel_id=1, source_target_pairs={{0,24},{4,28},{8,16},{12,20},{16,8},{20,12},{24,0},{28,4},{1,25},{... | collective-permute-start | bytes 98312 | tf_op jit(solution)/shard_map/ppermute | solution.py:162
  83.7 6.6 %copy-start.3 = (f32[64,128]{1,0:T(8,128)}, f32[64,128]{1,0:T(8,128)S(1)}, u32[]{:S(2)}) copy-start(f32[64,128]{1,0:T(8,128)S(1)} %collective-permute-done.4.refs_2_) | copy-start | bytes 98308
  83.7 6.6 %collective-permute-start.9 = (f32[64,128]{1,0:T(8,128)S(1)}, f32[64,128]{1,0:T(8,128)S(1)}, u32[]{:S(2)}, u32[]{:S(2)}) collective-permute-start(f32[64,128]{1,0:T(8,128)S(1)} %add_add_fusion.refs_0_), channel_id=1, source_target_pairs={{0,28},{4,24},{8,20},{12,16},{16,12},{20,8},{24,4},{28,0},{1,29},{... | collective-permute-start | bytes 98312 | tf_op jit(solution)/shard_map/ppermute | solution.py:162
  86.0 4.3 %copy-start.4 = (f32[64,128]{1,0:T(8,128)}, f32[64,128]{1,0:T(8,128)S(1)}, u32[]{:S(2)}) copy-start(f32[64,128]{1,0:T(8,128)S(1)} %collective-permute-done.5.refs_3_) | copy-start | bytes 98308
  86.1 4.3 %copy-start.5 = (f32[64,128]{1,0:T(8,128)}, f32[64,128]{1,0:T(8,128)S(1)}, u32[]{:S(2)}) copy-start(f32[64,128]{1,0:T(8,128)S(1)} %collective-permute-done.6.refs_4_) | copy-start | bytes 98308
  86.1 4.3 %copy-start.6 = (f32[64,128]{1,0:T(8,128)}, f32[64,128]{1,0:T(8,128)S(1)}, u32[]{:S(2)}) copy-start(f32[64,128]{1,0:T(8,128)S(1)} %collective-permute-done.7.refs_5_) | copy-start | bytes 98308
  88.1 2.2 %copy-start.7 = (f32[64,128]{1,0:T(8,128)}, f32[64,128]{1,0:T(8,128)S(1)}, u32[]{:S(2)}) copy-start(f32[64,128]{1,0:T(8,128)S(1)} %collective-permute-done.8.refs_6_) | copy-start | bytes 98308
  90.4 0.6 copy-start.8

commit v3 on v2

--- a/solution.py
+++ b/solution.py
@@ -218,11 +218,12 @@
     rows = lax.all_to_all(jac, "samp", split_axis=0, concat_axis=0, tiled=True)
     rows = rows.reshape(total, rows.shape[2], rows.shape[3])
     partial = gram_partial(rows, energy_column(spins, offdiag, total, width))
-    gram = tree_sum(partners(partial, "layer", 1, lax.axis_size("layer")))
-    reach = min(owners, 8)
-    grams = partners(gram, "samp", 1, reach)
-    if owners > reach:
-        grams = partners(tree_sum(grams), "samp", reach, owners // reach)
+    grams = partners(partial, "layer", 1, lax.axis_size("layer"))
+    first = 1
+    while first < owners:
+        count = 2 if first == 1 else min(4, owners // first)
+        grams = partners(tree_sum(grams), "samp", first, count)
+        first *= count
     weights, update = solve_and_project(grams, rows, local, mats)
     return weights.reshape(local), update
 

time: 100 us -> 97 us (0.970)
  starting transfers between devices: 20.5 us -> 15.2 us
  waiting for transfers between devices: 53.4 us -> 55.8 us
    ppermute x10 -> x7, starting transfers between devices: 13.1 us -> 7.83 us  [partners(): parts.append(lax.ppermute(value, axis, perm))]
    ppermute x10 -> x7, waiting for transfers between devices: 7.41 us -> 9.81 us  [partners(): parts.append(lax.ppermute(value, axis, perm))]
  transfers between devices with their start and end apart: 11 -> 8, of which waited for: 5 -> 6; matrix products, arithmetic and copies ran while one was open for 1% -> 1% of each run, Pallas kernels for 2% -> 2%
where the time goes in v3:
time: 97 us; the launch traced here: 96.5 us
  waiting for transfers between devices  55.8 us (58%)
  Pallas kernels  21.4 us (22%)
  starting transfers between devices  15.2 us (16%)
  local copies, waits for them, and re-layouts  2.62 us (3%)
    all_to_all x1, waiting for transfers between devices, body(): rows = lax.all_to_all(jac, 'samp', split_axis=0, concat_axis=0, tiled=True)  46 us
    ppermute x7, waiting for transfers between devices, partners(): parts.append(lax.ppermute(value, axis, perm))  9.81 us
    pallas_call x1, Pallas kernels, solve_and_project(): pl.pallas_call(solve_kernel, out_shape=(jax.ShapeDtypeStruct((1, local),...  8.52 us
    ppermute x7, starting transfers between devices, partners(): parts.append(lax.ppermute(value, axis, perm))  7.83 us
    all_to_all x1, starting transfers between devices, body(): rows = lax.all_to_all(jac, 'samp', split_axis=0, concat_axis=0, tiled=True)  7.41 us
    pallas_call x1, Pallas kernels, jac_rows(): pl.pallas_call(jac_kernel, grid=(samples,), in_specs=[block, block], out_...  6.98 us
    pallas_call x1, Pallas kernels, gram_partial(): pl.pallas_call(gram_kernel, grid=(count // CHUNK,), in_specs=[pl.BlockSpe...  4.36 us
    unnamed x12, local copies, waits for them, and re-layouts  1.94 us
  transfers between devices with their start and end apart: 8, of which 6 were waited for; matrix products, arithmetic and copies ran while one was open for 1% of the time, Pallas kernels for 2%

profile of v3, /device:TPU:0, one launch (start us, length us, event | category | flops | bytes accessed | tf_op | source)
XLA Modules:
  0.0 96.5 jit_solution(9955120171413531868)
XLA Ops:
  0.6 7.0 %jac_rows.1 = bf16[8,8,64,256]{3,2,1,0:T(8,128)(2,1)} custom-call(bf16[8,2,256,256]{3,2,1,0:T(8,128)(2,1)} %act_ref.1, bf16[8,2,256,256]{3,2,1,0:T(8,128)(2,1)} %cot_ref.1), custom_call_target="tpu_custom_call" | custom-call | flops 536870912 | bytes 6291456 | tf_op jit(solution)/shard_map/jac_rows/pallas_call | solution.py:41
  7.6 0.0 copy-start.5
  7.6 7.4 %all-to-all-start = ((bf16[8,8,64,256]{3,2,1,0:T(8,128)(2,1)}), bf16[8,8,64,256]{3,2,1,0:T(8,128)(2,1)S(1)}, u32[]{:S(2)}, u32[]{:S(2)}) async-start(bf16[8,8,64,256]{3,2,1,0:T(8,128)(2,1)} %jac_rows.1), calls=%async_computation | async-start | bytes 4194304 | tf_op jit(solution)/shard_map/all_to_all | solution.py:218
  15.0 0.0 copy-done.5
  15.0 0.7 copy.6.offdiag_ref
  15.7 1.5 %energy_column.1.start_ref = f32[64,128]{1,0:T(8,128)} custom-call(s32[8,256]{1,0:T(8,128)} %spins_ref.1, f32[8,1]{1,0:T(8,128)} %copy.6.offdiag_ref), custom_call_target="tpu_custom_call" | custom-call | tf_op jit(solution)/shard_map/energy_column/pallas_call | solution.py:76
  17.2 46.0 %all-to-all-done = bf16[8,8,64,256]{3,2,1,0:T(8,128)(2,1)S(1)} async-done(((bf16[8,8,64,256]{3,2,1,0:T(8,128)(2,1)}), bf16[8,8,64,256]{3,2,1,0:T(8,128)(2,1)S(1)}, u32[]{:S(2)}, u32[]{:S(2)}) %all-to-all-start) | async-done | bytes 2097184 | tf_op jit(solution)/shard_map/all_to_all | solution.py:218
  63.3 0.0 copy-start
  63.3 1.3 %copy-done = bf16[8,8,64,256]{3,2,1,0:T(8,128)(2,1)} copy-done((bf16[8,8,64,256]{3,2,1,0:T(8,128)(2,1)}, bf16[8,8,64,256]{3,2,1,0:T(8,128)(2,1)S(1)}, u32[]{:S(2)}) %copy-start) | copy-done | bytes 2097176
  64.6 4.4 %gram_partial.1 = f32[64,128]{1,0:T(8,128)} custom-call(bf16[64,64,256]{2,1,0:T(8,128)(2,1)} %bitcast.3, f32[64,128]{1,0:T(8,128)} %energy_column.1.start_ref), custom_call_target="tpu_custom_call" | custom-call | flops 134217728 | bytes 2097152 | tf_op jit(solution)/shard_map/gram_partial/pallas_call | solution.py:112
  68.9 0.0 collective-permute-start
  69.0 1.5 %collective-permute-start.1 = (f32[64,128]{1,0:T(8,128)}, f32[64,128]{1,0:T(8,128)S(1)}, u32[]{:S(2)}, u32[]{:S(2)}) collective-permute-start(f32[64,128]{1,0:T(8,128)} %gram_partial.1), channel_id=1, source_target_pairs={{0,2},{1,3},{2,0},{3,1},{4,6},{5,7},{6,4},{7,5},{8,10},{9,11},{10,... | collective-permute-start | bytes 98312 | tf_op jit(solution)/shard_map/ppermute | solution.py:162
  70.4 0.4 collective-permute-start.2
  70.8 0.0 collective-permute-done
  70.8 2.3 %collective-permute-done.1 = f32[64,128]{1,0:T(8,128)S(1)} collective-permute-done((f32[64,128]{1,0:T(8,128)}, f32[64,128]{1,0:T(8,128)S(1)}, u32[]{:S(2)}, u32[]{:S(2)}) %collective-permute-start.1) | collective-permute-done | bytes 32800 | tf_op jit(solution)/shard_map/ppermute | solution.py:162
  73.1 0.9 collective-permute-done.2
  74.0 0.8 add_add_fusion
  74.8 1.5 %collective-permute-start.3 = (f32[64,128]{1,0:T(8,128)S(1)}, f32[64,128]{1,0:T(8,128)S(1)}, u32[]{:S(2)}, u32[]{:S(2)}) collective-permute-start(f32[64,128]{1,0:T(8,128)S(1)} %add_add_fusion), channel_id=1, source_target_pairs={{0,4},{4,0},{8,12},{12,8},{16,20},{20,16},{24,28},{28,24},{1,5},{5... | collective-permute-start | bytes 98312 | tf_op jit(solution)/shard_map/ppermute | solution.py:162
  76.3 2.5 %collective-permute-done.3 = f32[64,128]{1,0:T(8,128)S(1)} collective-permute-done((f32[64,128]{1,0:T(8,128)S(1)}, f32[64,128]{1,0:T(8,128)S(1)}, u32[]{:S(2)}, u32[]{:S(2)}) %collective-permute-start.3) | collective-permute-done | bytes 32800 | tf_op jit(solution)/shard_map/ppermute | solution.py:162
  78.8 0.0 copy-start.1
  78.8 0.1 collective-permute-start.4
  78.8 2.8 %collective-permute-start.5 = (f32[64,128]{1,0:T(8,128)S(1)}, f32[64,128]{1,0:T(8,128)S(1)}, u32[]{:S(2)}, u32[]{:S(2)}) collective-permute-start(f32[64,128]{1,0:T(8,128)S(1)} %add.15.refs_0_), channel_id=1, source_target_pairs={{0,16},{4,20},{8,24},{12,28},{16,0},{20,4},{24,8},{28,12},{1,17},{... | collective-permute-start | bytes 98312 | tf_op jit(solution)/shard_map/ppermute | solution.py:162
  81.7 1.5 %collective-permute-start.6 = (f32[64,128]{1,0:T(8,128)S(1)}, f32[64,128]{1,0:T(8,128)S(1)}, u32[]{:S(2)}, u32[]{:S(2)}) collective-permute-start(f32[64,128]{1,0:T(8,128)S(1)} %add.15.refs_0_), channel_id=1, source_target_pairs={{0,24},{4,28},{8,16},{12,20},{16,8},{20,12},{24,0},{28,4},{1,25},{... | collective-permute-start | bytes 98312 | tf_op jit(solution)/shard_map/ppermute | solution.py:162
  83.2 0.0 collective-permute-done.4.refs_1_
  83.2 0.0 copy-start.2
  83.2 0.5 collective-permute-done.5.refs_2_
  83.7 0.0 copy-start.3
  83.7 3.7 %collective-permute-done.6.refs_3_ = f32[64,128]{1,0:T(8,128)S(1)} collective-permute-done((f32[64,128]{1,0:T(8,128)S(1)}, f32[64,128]{1,0:T(8,128)S(1)}, u32[]{:S(2)}, u32[]{:S(2)}) %collective-permute-start.6) | collective-permute-done | bytes 32800 | tf_op jit(solution)/shard_map/ppermute | solution.py:162
  87.4 0.0 copy-done.1
  87.4 0.0 copy-done.2
  87.4 0.0 copy-done.3
  87.4 0.0 copy-start.4
  87.4 0.6 copy-done.4
  88.0 8.5 %solve_and_project.1 = (f32[1,8]{1,0:T(1,128)}, f32[2,32,256]{2,1,0:T(8,128)}) custom-call(f32[64,128]{1,0:T(8,128)} %copy-done.1, f32[64,128]{1,0:T(8,128)} %copy-done.2, f32[64,128]{1,0:T(8,128)} %copy-done.3, f32[64,128]{1,0:T(8,128)} %copy-done.4, bf16[64,64,256]{2,1,0:T(8,128)(2,1)} %bitcast.4), custom_call_target="tpu_custom_call" | custom-call | tf_op jit(solution)/shard_map/solve_and_project/pallas_call | solution.py:202
  (1 shorter events, 0.0 us)
Async XLA Ops:
  7.6 7.4 %copy-start.5 = (f32[8]{0:T(128)S(1)}, f32[8]{0:T(128)}, u32[]{:S(2)}) copy-start(f32[8]{0:T(128)} %param.7) | copy-start | bytes 100
  7.6 55.6 %all-to-all-start = ((bf16[8,8,64,256]{3,2,1,0:T(8,128)(2,1)}), bf16[8,8,64,256]{3,2,1,0:T(8,128)(2,1)S(1)}, u32[]{:S(2)}, u32[]{:S(2)}) async-start(bf16[8,8,64,256]{3,2,1,0:T(8,128)(2,1)} %jac_rows.1), calls=%async_computation | async-start | bytes 4194304 | tf_op jit(solution)/shard_map/all_to_all | solution.py:218
  63.3 1.3 %copy-start = (bf16[8,8,64,256]{3,2,1,0:T(8,128)(2,1)}, bf16[8,8,64,256]{3,2,1,0:T(8,128)(2,1)S(1)}, u32[]{:S(2)}) copy-start(bf16[8,8,64,256]{3,2,1,0:T(8,128)(2,1)S(1)} %all-to-all-done) | copy-start | bytes 6291460
  68.9 1.9 %collective-permute-start = (f32[64,128]{1,0:T(8,128)}, f32[64,128]{1,0:T(8,128)S(1)}, u32[]{:S(2)}, u32[]{:S(2)}) collective-permute-start(f32[64,128]{1,0:T(8,128)} %gram_partial.1), channel_id=1, source_target_pairs={{0,1},{1,0},{2,3},{3,2},{4,5},{5,4},{6,7},{7,6},{8,9},{9,8},{10,11... | collective-permute-start | bytes 98312 | tf_op jit(solution)/shard_map/ppermute | solution.py:162
  69.0 4.1 %collective-permute-start.1 = (f32[64,128]{1,0:T(8,128)}, f32[64,128]{1,0:T(8,128)S(1)}, u32[]{:S(2)}, u32[]{:S(2)}) collective-permute-start(f32[64,128]{1,0:T(8,128)} %gram_partial.1), channel_id=1, source_target_pairs={{0,2},{1,3},{2,0},{3,1},{4,6},{5,7},{6,4},{7,5},{8,10},{9,11},{10,... | collective-permute-start | bytes 98312 | tf_op jit(solution)/shard_map/ppermute | solution.py:162
  70.4 3.6 %collective-permute-start.2 = (f32[64,128]{1,0:T(8,128)}, f32[64,128]{1,0:T(8,128)S(1)}, u32[]{:S(2)}, u32[]{:S(2)}) collective-permute-start(f32[64,128]{1,0:T(8,128)} %gram_partial.1), channel_id=1, source_target_pairs={{0,3},{1,2},{2,1},{3,0},{4,7},{5,6},{6,5},{7,4},{8,11},{9,10},{10,... | collective-permute-start | bytes 98312 | tf_op jit(solution)/shard_map/ppermute | solution.py:162
  74.8 4.0 %collective-permute-start.3 = (f32[64,128]{1,0:T(8,128)S(1)}, f32[64,128]{1,0:T(8,128)S(1)}, u32[]{:S(2)}, u32[]{:S(2)}) collective-permute-start(f32[64,128]{1,0:T(8,128)S(1)} %add_add_fusion), channel_id=1, source_target_pairs={{0,4},{4,0},{8,12},{12,8},{16,20},{20,16},{24,28},{28,24},{1,5},{5... | collective-permute-start | bytes 98312 | tf_op jit(solution)/shard_map/ppermute | solution.py:162
  78.8 8.6 %copy-start.1 = (f32[64,128]{1,0:T(8,128)}, f32[64,128]{1,0:T(8,128)S(1)}, u32[]{:S(2)}) copy-start(f32[64,128]{1,0:T(8,128)S(1)} %add.15.refs_0_) | copy-start | bytes 98308
  78.8 4.5 %collective-permute-start.4 = (f32[64,128]{1,0:T(8,128)S(1)}, f32[64,128]{1,0:T(8,128)S(1)}, u32[]{:S(2)}, u32[]{:S(2)}) collective-permute-start(f32[64,128]{1,0:T(8,128)S(1)} %add.15.refs_0_), channel_id=1, source_target_pairs={{0,8},{4,12},{8,0},{12,4},{16,24},{20,28},{24,16},{28,20},{1,9},{5... | collective-permute-start | bytes 98312 | tf_op jit(solution)/shard_map/ppermute | solution.py:162
  78.8 4.9 %collective-permute-start.5 = (f32[64,128]{1,0:T(8,128)S(1)}, f32[64,128]{1,0:T(8,128)S(1)}, u32[]{:S(2)}, u32[]{:S(2)}) collective-permute-start(f32[64,128]{1,0:T(8,128)S(1)} %add.15.refs_0_), channel_id=1, source_target_pairs={{0,16},{4,20},{8,24},{12,28},{16,0},{20,4},{24,8},{28,12},{1,17},{... | collective-permute-start | bytes 98312 | tf_op jit(solution)/shard_map/ppermute | solution.py:162
  81.7 5.7 %collective-permute-start.6 = (f32[64,128]{1,0:T(8,128)S(1)}, f32[64,128]{1,0:T(8,128)S(1)}, u32[]{:S(2)}, u32[]{:S(2)}) collective-permute-start(f32[64,128]{1,0:T(8,128)S(1)} %add.15.refs_0_), channel_id=1, source_target_pairs={{0,24},{4,28},{8,16},{12,20},{16,8},{20,12},{24,0},{28,4},{1,25},{... | collective-permute-start | bytes 98312 | tf_op jit(solution)/shard_map/ppermute | solution.py:162
  83.2 4.2 %copy-start.2 = (f32[64,128]{1,0:T(8,128)}, f32[64,128]{1,0:T(8,128)S(1)}, u32[]{:S(2)}) copy-start(f32[64,128]{1,0:T(8,128)S(1)} %collective-permute-done.4.refs_1_) | copy-start | bytes 98308
  83.7 3.7 %copy-start.3 = (f32[64,128]{1,0:T(8,128)}, f32[64,128]{1,0:T(8,128)S(1)}, u32[]{:S(2)}) copy-start(f32[64,128]{1,0:T(8,128)S(1)} %collective-permute-done.5.refs_2_) | copy-start | bytes 98308
  87.4 0.6 copy-start.4

commit v4 on v3

--- a/solution.py
+++ b/solution.py
@@ -34,10 +34,11 @@
         out_ref[owner, 0] = jnp.concatenate(rows, axis=0).astype(BF16)
 
 
-def jac_rows(activations, cotangents, owners):
+def jac_rows(activations, cotangents, owners, part, parts):
     samples, mats, sites, d = activations.shape
+    mats //= parts
     rows = mats * d // owners
-    block = pl.BlockSpec((1, mats, sites, d), lambda s: (s, 0, 0, 0))
+    block = pl.BlockSpec((1, mats, sites, d), lambda s: (s, part, 0, 0))
     return pl.pallas_call(
         jac_kernel,
         grid=(samples,),
@@ -164,10 +165,12 @@
 
 
 def solve_kernel(*refs):
-    *gram_refs, rows_ref, weights_ref, update_ref = refs
-    total, width = gram_refs[0].shape
+    weights_ref, update_ref = refs[-2:]
     mats, share, d = update_ref.shape
     local = weights_ref.shape[1]
+    gram_refs = [ref for ref in refs[:-2] if len(ref.shape) == 2]
+    rows_refs = [ref for ref in refs[:-2] if len(ref.shape) == 3]
+    total, width = gram_refs[0].shape
     raw = tree_sum([ref[...] for ref in gram_refs])
     row = iota((total, width), 0)
     lane = iota((total, width), 1)
@@ -190,23 +193,25 @@
     weights_ref[...] = jnp.sum(own, axis=0, keepdims=True)[:, :local]
     coeffs = weights - jnp.sum(weights, axis=0, keepdims=True) * scale
     coeffs = jnp.broadcast_to(coeffs, (total, d))
-    acc = jnp.zeros((mats * share, d), F32)
-    for s in range(total):
-        acc = acc + coeffs[s : s + 1] * rows_ref[s].astype(F32)
-    for m in range(mats):
-        update_ref[m] = acc[m * share : (m + 1) * share]
+    held = mats // len(rows_refs)
+    for part, rows_ref in enumerate(rows_refs):
+        acc = jnp.zeros((held * share, d), F32)
+        for s in range(total):
+            acc = acc + coeffs[s : s + 1] * rows_ref[s].astype(F32)
+        for m in range(held):
+            update_ref[part * held + m] = acc[m * share : (m + 1) * share]
 
 
 def solve_and_project(grams, rows, local, mats):
-    total, count, d = rows.shape
+    total, count, d = rows[0].shape
     return pl.pallas_call(
         solve_kernel,
         out_shape=(
             jax.ShapeDtypeStruct((1, local), F32),
-            jax.ShapeDtypeStruct((mats, count // mats, d), F32),
+            jax.ShapeDtypeStruct((mats, count * len(rows) // mats, d), F32),
         ),
         name="solve_and_project",
-    )(*grams, rows)
+    )(*grams, *rows)
 
 
 def body(spins, activations, cotangents, offdiag):
@@ -214,10 +219,16 @@
     owners = lax.axis_size("samp")
     total = local * owners
     width = (total // LANES + 1) * LANES
-    jac = jac_rows(activations, cotangents, owners)
-    rows = lax.all_to_all(jac, "samp", split_axis=0, concat_axis=0, tiled=True)
-    rows = rows.reshape(total, rows.shape[2], rows.shape[3])
-    partial = gram_partial(rows, energy_column(spins, offdiag, total, width))
+    share = activations.shape[3] // owners
+    parts = mats if share % CHUNK == 0 else 1
+    partial = energy_column(spins, offdiag, total, width)
+    rows = []
+    for part in range(parts):
+        jac = jac_rows(activations, cotangents, owners, part, parts)
+        held = lax.all_to_all(jac, "samp", split_axis=0, concat_axis=0, tiled=True)
+        rows.append(held.reshape(total, held.shape[2], held.shape[3]))
+    for held in rows:
+        partial = gram_partial(held, partial)
     grams = partners(partial, "layer", 1, lax.axis_size("layer"))
     first = 1
     while first < owners:

time: 97 us -> 101 us (1.041)
  Pallas kernels: 21.4 us -> 28.1 us
  waiting for transfers between devices: 55.8 us -> 49.6 us
  starting transfers between devices: 15.2 us -> 18.9 us
    pallas_call x1 -> x2, Pallas kernels: 6.98 us -> 12.6 us  [jac_rows(): pl.pallas_call(jac_kernel, grid=(samples,), in_specs=[block, block], out_...]
    all_to_all x1 -> x2, waiting for transfers between devices: 46 us -> 40.5 us  [body(): held = lax.all_to_all(jac, 'samp', split_axis=0, concat_axis=0, tiled=True)]
    all_to_all x1 -> x2, starting transfers between devices: 7.41 us -> 10.9 us  [body(): held = lax.all_to_all(jac, 'samp', split_axis=0, concat_axis=0, tiled=True)]
    pallas_call x1 -> x2, Pallas kernels: 4.36 us -> 5.47 us  [gram_partial(): pl.pallas_call(gram_kernel, grid=(count // CHUNK,), in_specs=[pl.BlockSpe...]
  transfers between devices with their start and end apart: 8 -> 9, of which waited for: 6 -> 7; matrix products, arithmetic and copies ran while one was open for 1% -> 1% of each run, Pallas kernels for 2% -> 11%
where the time goes in v4:
time: 101 us; the launch traced here: 100 us
  waiting for transfers between devices  49.6 us (49%)
  Pallas kernels  28.1 us (28%)
  starting transfers between devices  18.9 us (19%)
  local copies, waits for them, and re-layouts  2.27 us (2%)
    all_to_all x2, waiting for transfers between devices, body(): held = lax.all_to_all(jac, 'samp', split_axis=0, concat_axis=0, tiled=True)  40.5 us
    pallas_call x2, Pallas kernels, jac_rows(): pl.pallas_call(jac_kernel, grid=(samples,), in_specs=[block, block], out_...  12.6 us
    all_to_all x2, starting transfers between devices, body(): held = lax.all_to_all(jac, 'samp', split_axis=0, concat_axis=0, tiled=True)  10.9 us
    ppermute x7, waiting for transfers between devices, partners(): parts.append(lax.ppermute(value, axis, perm))  9.08 us
    pallas_call x1, Pallas kernels, solve_and_project(): pl.pallas_call(solve_kernel, out_shape=(jax.ShapeDtypeStruct((1, local),...  8.47 us
    ppermute x7, starting transfers between devices, partners(): parts.append(lax.ppermute(value, axis, perm))  8.07 us
    pallas_call x2, Pallas kernels, gram_partial(): pl.pallas_call(gram_kernel, grid=(count // CHUNK,), in_specs=[pl.BlockSpe...  5.47 us
  transfers between devices with their start and end apart: 9, of which 7 were waited for; matrix products, arithmetic and copies ran while one was open for 1% of the time, Pallas kernels for 11%

profile of v4, /device:TPU:0, one launch (start us, length us, event | category | flops | bytes accessed | tf_op | source)
XLA Modules:
  0.0 100.3 jit_solution(1918112138734122385)
XLA Ops:
  0.6 6.3 %jac_rows.3 = bf16[8,8,32,256]{3,2,1,0:T(8,128)(2,1)} custom-call(bf16[8,2,256,256]{3,2,1,0:T(8,128)(2,1)} %act_ref.3, bf16[8,2,256,256]{3,2,1,0:T(8,128)(2,1)} %cot_ref.3), custom_call_target="tpu_custom_call" | custom-call | flops 268435456 | bytes 3145728 | tf_op jit(solution)/shard_map/jac_rows/pallas_call | solution.py:42
  7.0 7.3 %all-to-all-start.1 = ((bf16[8,8,32,256]{3,2,1,0:T(8,128)(2,1)}), bf16[8,8,32,256]{3,2,1,0:T(8,128)(2,1)S(1)}, u32[]{:S(2)}, u32[]{:S(2)}) async-start(bf16[8,8,32,256]{3,2,1,0:T(8,128)(2,1)} %jac_rows.3), calls=%async_computation.1 | async-start | bytes 2097152 | tf_op jit(solution)/shard_map/all_to_all | solution.py:228
  14.2 6.3 %jac_rows.2 = bf16[8,8,32,256]{3,2,1,0:T(8,128)(2,1)} custom-call(bf16[8,2,256,256]{3,2,1,0:T(8,128)(2,1)} %act_ref.3, bf16[8,2,256,256]{3,2,1,0:T(8,128)(2,1)} %cot_ref.3), custom_call_target="tpu_custom_call" | custom-call | flops 268435456 | bytes 3145728 | tf_op jit(solution)/shard_map/jac_rows/pallas_call | solution.py:42
  20.5 0.0 copy-start.6
  20.6 19.5 %all-to-all-done.1 = bf16[8,8,32,256]{3,2,1,0:T(8,128)(2,1)S(1)} async-done(((bf16[8,8,32,256]{3,2,1,0:T(8,128)(2,1)}), bf16[8,8,32,256]{3,2,1,0:T(8,128)(2,1)S(1)}, u32[]{:S(2)}, u32[]{:S(2)}) %all-to-all-start.1) | async-done | bytes 1048608 | tf_op jit(solution)/shard_map/all_to_all | solution.py:228
  40.0 0.0 copy-start
  40.0 3.6 %all-to-all-start = ((bf16[8,8,32,256]{3,2,1,0:T(8,128)(2,1)}), bf16[8,8,32,256]{3,2,1,0:T(8,128)(2,1)S(1)}, u32[]{:S(2)}, u32[]{:S(2)}) async-start(bf16[8,8,32,256]{3,2,1,0:T(8,128)(2,1)} %jac_rows.2), calls=%async_computation | async-start | bytes 2097152 | tf_op jit(solution)/shard_map/all_to_all | solution.py:228
  43.6 0.0 copy-done.6
  43.6 0.7 copy.6.offdiag_ref
  44.3 1.5 %energy_column.1.start_ref = f32[64,128]{1,0:T(8,128)} custom-call(s32[8,256]{1,0:T(8,128)} %spins_ref.1, f32[8,1]{1,0:T(8,128)} %copy.6.offdiag_ref), custom_call_target="tpu_custom_call" | custom-call | tf_op jit(solution)/shard_map/energy_column/pallas_call | solution.py:77
  45.8 0.0 copy-done
  45.8 2.7 %gram_partial.2.start_ref = f32[64,128]{1,0:T(8,128)} custom-call(bf16[64,32,256]{2,1,0:T(8,128)(2,1)} %bitcast.4, f32[64,128]{1,0:T(8,128)} %energy_column.1.start_ref), custom_call_target="tpu_custom_call" | custom-call | flops 67108864 | bytes 1048576 | tf_op jit(solution)/shard_map/gram_partial/pallas_call | solution.py:113
  48.5 21.0 %all-to-all-done = bf16[8,8,32,256]{3,2,1,0:T(8,128)(2,1)S(1)} async-done(((bf16[8,8,32,256]{3,2,1,0:T(8,128)(2,1)}), bf16[8,8,32,256]{3,2,1,0:T(8,128)(2,1)S(1)}, u32[]{:S(2)}, u32[]{:S(2)}) %all-to-all-start) | async-done | bytes 1048608 | tf_op jit(solution)/shard_map/all_to_all | solution.py:228
  69.6 0.0 copy-start.1
  69.6 1.0 copy-done.1
  70.6 2.7 %gram_partial.3 = f32[64,128]{1,0:T(8,128)} custom-call(bf16[64,32,256]{2,1,0:T(8,128)(2,1)} %bitcast.6, f32[64,128]{1,0:T(8,128)} %gram_partial.2.start_ref), custom_call_target="tpu_custom_call" | custom-call | flops 67108864 | bytes 1048576 | tf_op jit(solution)/shard_map/gram_partial/pallas_call | solution.py:113
  73.3 1.5 %collective-permute-start.1 = (f32[64,128]{1,0:T(8,128)}, f32[64,128]{1,0:T(8,128)S(1)}, u32[]{:S(2)}, u32[]{:S(2)}) collective-permute-start(f32[64,128]{1,0:T(8,128)} %gram_partial.3), channel_id=1, source_target_pairs={{0,2},{1,3},{2,0},{3,1},{4,6},{5,7},{6,4},{7,5},{8,10},{9,11},{10,... | collective-permute-start | bytes 98312 | tf_op jit(solution)/shard_map/ppermute | solution.py:163
  74.8 0.0 collective-permute-start.2
  74.8 0.6 collective-permute-start
  75.4 2.0 %collective-permute-done.1 = f32[64,128]{1,0:T(8,128)S(1)} collective-permute-done((f32[64,128]{1,0:T(8,128)}, f32[64,128]{1,0:T(8,128)S(1)}, u32[]{:S(2)}, u32[]{:S(2)}) %collective-permute-start.1) | collective-permute-done | bytes 32800 | tf_op jit(solution)/shard_map/ppermute | solution.py:163
  77.4 0.9 collective-permute-done.2
  78.3 0.0 collective-permute-done
  78.3 0.8 add_add_fusion
  79.1 1.5 %collective-permute-start.3 = (f32[64,128]{1,0:T(8,128)S(1)}, f32[64,128]{1,0:T(8,128)S(1)}, u32[]{:S(2)}, u32[]{:S(2)}) collective-permute-start(f32[64,128]{1,0:T(8,128)S(1)} %add_add_fusion), channel_id=1, source_target_pairs={{0,4},{4,0},{8,12},{12,8},{16,20},{20,16},{24,28},{28,24},{1,5},{5... | collective-permute-start | bytes 98312 | tf_op jit(solution)/shard_map/ppermute | solution.py:163
  80.6 2.5 %collective-permute-done.3 = f32[64,128]{1,0:T(8,128)S(1)} collective-permute-done((f32[64,128]{1,0:T(8,128)S(1)}, f32[64,128]{1,0:T(8,128)S(1)}, u32[]{:S(2)}, u32[]{:S(2)}) %collective-permute-start.3) | collective-permute-done | bytes 32800 | tf_op jit(solution)/shard_map/ppermute | solution.py:163
  83.1 0.0 copy-start.2
  83.1 0.1 collective-permute-start.4
  83.2 2.4 %collective-permute-start.5 = (f32[64,128]{1,0:T(8,128)S(1)}, f32[64,128]{1,0:T(8,128)S(1)}, u32[]{:S(2)}, u32[]{:S(2)}) collective-permute-start(f32[64,128]{1,0:T(8,128)S(1)} %add.15.refs_0_), channel_id=1, source_target_pairs={{0,16},{4,20},{8,24},{12,28},{16,0},{20,4},{24,8},{28,12},{1,17},{... | collective-permute-start | bytes 98312 | tf_op jit(solution)/shard_map/ppermute | solution.py:163
  85.5 2.0 %collective-permute-start.6 = (f32[64,128]{1,0:T(8,128)S(1)}, f32[64,128]{1,0:T(8,128)S(1)}, u32[]{:S(2)}, u32[]{:S(2)}) collective-permute-start(f32[64,128]{1,0:T(8,128)S(1)} %add.15.refs_0_), channel_id=1, source_target_pairs={{0,24},{4,28},{8,16},{12,20},{16,8},{20,12},{24,0},{28,4},{1,25},{... | collective-permute-start | bytes 98312 | tf_op jit(solution)/shard_map/ppermute | solution.py:163
  87.6 0.0 collective-permute-done.4.refs_1_
  87.6 0.0 copy-start.3
  87.6 0.5 collective-permute-done.5.refs_2_
  88.1 0.0 copy-start.4
  88.1 3.2 %collective-permute-done.6.refs_3_ = f32[64,128]{1,0:T(8,128)S(1)} collective-permute-done((f32[64,128]{1,0:T(8,128)S(1)}, f32[64,128]{1,0:T(8,128)S(1)}, u32[]{:S(2)}, u32[]{:S(2)}) %collective-permute-start.6) | collective-permute-done | bytes 32800 | tf_op jit(solution)/shard_map/ppermute | solution.py:163
  91.2 0.0 copy-done.2
  91.2 0.0 copy-done.3
  91.2 0.0 copy-done.4
  91.3 0.0 copy-start.5
  91.3 0.6 copy-done.5
  91.9 8.5 %solve_and_project.1 = (f32[1,8]{1,0:T(1,128)}, f32[2,32,256]{2,1,0:T(8,128)}) custom-call(f32[64,128]{1,0:T(8,128)} %copy-done.2, f32[64,128]{1,0:T(8,128)} %copy-done.3, f32[64,128]{1,0:T(8,128)} %copy-done.4, f32[64,128]{1,0:T(8,128)} %copy-done.5, bf16[64,32,256]{2,1,0:T(8,128)(2,1)} %bitcast.5, bf16[64,32,256]{2,1,0:T(8,128)(2,1)} %bitcast.7), custom_call_target="tpu_custom_call" | custom-call | tf_op jit(solution)/shard_map/solve_and_project/pallas_call | solution.py:207
  (1 shorter events, 0.0 us)
Async XLA Ops:
  7.0 33.0 %all-to-all-start.1 = ((bf16[8,8,32,256]{3,2,1,0:T(8,128)(2,1)}), bf16[8,8,32,256]{3,2,1,0:T(8,128)(2,1)S(1)}, u32[]{:S(2)}, u32[]{:S(2)}) async-start(bf16[8,8,32,256]{3,2,1,0:T(8,128)(2,1)} %jac_rows.3), calls=%async_computation.1 | async-start | bytes 2097152 | tf_op jit(solution)/shard_map/all_to_all | solution.py:228
  20.5 23.1 %copy-start.6 = (f32[8]{0:T(128)S(1)}, f32[8]{0:T(128)}, u32[]{:S(2)}) copy-start(f32[8]{0:T(128)} %param.7) | copy-start | bytes 100
  40.0 5.8 %copy-start = (bf16[8,8,32,256]{3,2,1,0:T(8,128)(2,1)}, bf16[8,8,32,256]{3,2,1,0:T(8,128)(2,1)S(1)}, u32[]{:S(2)}) copy-start(bf16[8,8,32,256]{3,2,1,0:T(8,128)(2,1)S(1)} %all-to-all-done.1) | copy-start | bytes 3145732
  40.0 29.5 %all-to-all-start = ((bf16[8,8,32,256]{3,2,1,0:T(8,128)(2,1)}), bf16[8,8,32,256]{3,2,1,0:T(8,128)(2,1)S(1)}, u32[]{:S(2)}, u32[]{:S(2)}) async-start(bf16[8,8,32,256]{3,2,1,0:T(8,128)(2,1)} %jac_rows.2), calls=%async_computation | async-start | bytes 2097152 | tf_op jit(solution)/shard_map/all_to_all | solution.py:228
  69.6 1.0 copy-start.1
  73.3 4.1 %collective-permute-start.1 = (f32[64,128]{1,0:T(8,128)}, f32[64,128]{1,0:T(8,128)S(1)}, u32[]{:S(2)}, u32[]{:S(2)}) collective-permute-start(f32[64,128]{1,0:T(8,128)} %gram_partial.3), channel_id=1, source_target_pairs={{0,2},{1,3},{2,0},{3,1},{4,6},{5,7},{6,4},{7,5},{8,10},{9,11},{10,... | collective-permute-start | bytes 98312 | tf_op jit(solution)/shard_map/ppermute | solution.py:163
  74.8 3.6 %collective-permute-start.2 = (f32[64,128]{1,0:T(8,128)}, f32[64,128]{1,0:T(8,128)S(1)}, u32[]{:S(2)}, u32[]{:S(2)}) collective-permute-start(f32[64,128]{1,0:T(8,128)} %gram_partial.3), channel_id=1, source_target_pairs={{0,3},{1,2},{2,1},{3,0},{4,7},{5,6},{6,5},{7,4},{8,11},{9,10},{10,... | collective-permute-start | bytes 98312 | tf_op jit(solution)/shard_map/ppermute | solution.py:163
  74.8 3.6 %collective-permute-start = (f32[64,128]{1,0:T(8,128)}, f32[64,128]{1,0:T(8,128)S(1)}, u32[]{:S(2)}, u32[]{:S(2)}) collective-permute-start(f32[64,128]{1,0:T(8,128)} %gram_partial.3), channel_id=1, source_target_pairs={{0,1},{1,0},{2,3},{3,2},{4,5},{5,4},{6,7},{7,6},{8,9},{9,8},{10,11... | collective-permute-start | bytes 98312 | tf_op jit(solution)/shard_map/ppermute | solution.py:163
  79.1 4.0 %collective-permute-start.3 = (f32[64,128]{1,0:T(8,128)S(1)}, f32[64,128]{1,0:T(8,128)S(1)}, u32[]{:S(2)}, u32[]{:S(2)}) collective-permute-start(f32[64,128]{1,0:T(8,128)S(1)} %add_add_fusion), channel_id=1, source_target_pairs={{0,4},{4,0},{8,12},{12,8},{16,20},{20,16},{24,28},{28,24},{1,5},{5... | collective-permute-start | bytes 98312 | tf_op jit(solution)/shard_map/ppermute | solution.py:163
  83.1 8.2 %copy-start.2 = (f32[64,128]{1,0:T(8,128)}, f32[64,128]{1,0:T(8,128)S(1)}, u32[]{:S(2)}) copy-start(f32[64,128]{1,0:T(8,128)S(1)} %add.15.refs_0_) | copy-start | bytes 98308
  83.1 4.5 %collective-permute-start.4 = (f32[64,128]{1,0:T(8,128)S(1)}, f32[64,128]{1,0:T(8,128)S(1)}, u32[]{:S(2)}, u32[]{:S(2)}) collective-permute-start(f32[64,128]{1,0:T(8,128)S(1)} %add.15.refs_0_), channel_id=1, source_target_pairs={{0,8},{4,12},{8,0},{12,4},{16,24},{20,28},{24,16},{28,20},{1,9},{5... | collective-permute-start | bytes 98312 | tf_op jit(solution)/shard_map/ppermute | solution.py:163
  83.2 4.9 %collective-permute-start.5 = (f32[64,128]{1,0:T(8,128)S(1)}, f32[64,128]{1,0:T(8,128)S(1)}, u32[]{:S(2)}, u32[]{:S(2)}) collective-permute-start(f32[64,128]{1,0:T(8,128)S(1)} %add.15.refs_0_), channel_id=1, source_target_pairs={{0,16},{4,20},{8,24},{12,28},{16,0},{20,4},{24,8},{28,12},{1,17},{... | collective-permute-start | bytes 98312 | tf_op jit(solution)/shard_map/ppermute | solution.py:163
  85.5 5.7 %collective-permute-start.6 = (f32[64,128]{1,0:T(8,128)S(1)}, f32[64,128]{1,0:T(8,128)S(1)}, u32[]{:S(2)}, u32[]{:S(2)}) collective-permute-start(f32[64,128]{1,0:T(8,128)S(1)} %add.15.refs_0_), channel_id=1, source_target_pairs={{0,24},{4,28},{8,16},{12,20},{16,8},{20,12},{24,0},{28,4},{1,25},{... | collective-permute-start | bytes 98312 | tf_op jit(solution)/shard_map/ppermute | solution.py:163
  87.6 3.7 %copy-start.3 = (f32[64,128]{1,0:T(8,128)}, f32[64,128]{1,0:T(8,128)S(1)}, u32[]{:S(2)}) copy-start(f32[64,128]{1,0:T(8,128)S(1)} %collective-permute-done.4.refs_1_) | copy-start | bytes 98308
  88.1 3.2 %copy-start.4 = (f32[64,128]{1,0:T(8,128)}, f32[64,128]{1,0:T(8,128)S(1)}, u32[]{:S(2)}) copy-start(f32[64,128]{1,0:T(8,128)S(1)} %collective-permute-done.5.refs_2_) | copy-start | bytes 98308
  91.3 0.6 copy-start.5

commit v5 on v4

v5 whole, which is shorter than its diff:
```python
import functools

import jax
import jax.numpy as jnp
from jax import lax
from jax.experimental import pallas as pl
from jax.experimental.pallas import tpu as pltpu
from jax.sharding import PartitionSpec as P

SIDE = 16
LANES = 128
CHUNK = 16
VMEM_LIMIT = 24 * 2**20
shift_ratio = 0.1
F32 = jnp.float32
BF16 = jnp.bfloat16


def iota(shape, dim):
    return lax.broadcasted_iota(jnp.int32, shape, dim)


def jac_kernel(first, act_hbm, cot_hbm, *refs):
    *out_refs, act_buf, cot_buf, held, sems = refs
    samples, mats = act_buf.shape[:2]
    share = out_refs[0].shape[1] // mats
    me = lax.axis_index("samp")
    copies = []
    for s in range(samples):
        here = (s, pl.ds(first, mats))
        copies.append(pltpu.make_async_copy(act_hbm.at[here], act_buf.at[s], sems.at[0, s]))
        copies.append(pltpu.make_async_copy(cot_hbm.at[here], cot_buf.at[s], sems.at[1, s]))
    for copy in copies:
        copy.start()
    for s in range(samples):
        copies[2 * s].wait()
        copies[2 * s + 1].wait()
        for m in range(mats):
            held[s, m] = lax.dot_general(
                act_buf[s, m],
                cot_buf[s, m],
                (((0,), (0,)), ((), ())),
                preferred_element_type=F32,
            )
        for k, out_ref in enumerate(out_refs):
            owned = pl.ds(pl.multiple_of((me ^ k) * share, share), share)
            rows = [held[s, m, owned] for m in range(mats)]
            out_ref[s] = jnp.concatenate(rows, axis=0).astype(BF16)


def jac_rows(activations, cotangents, owners, part, parts):
    samples, mats, sites, d = activations.shape
    mats //= parts
    rows = mats * d // owners
    hbm = pl.BlockSpec(memory_space=pltpu.HBM)
    return pl.pallas_call(
        functools.partial(jac_kernel, part * mats),
        in_specs=[hbm, hbm],
        out_shape=[jax.ShapeDtypeStruct((samples, rows, d), BF16)] * owners,
        scratch_shapes=[
            pltpu.VMEM((samples, mats, sites, d), BF16),
            pltpu.VMEM((samples, mats, sites, d), BF16),
            pltpu.VMEM((samples, mats, d, d), F32),
            pltpu.SemaphoreType.DMA((2, samples)),
        ],
        compiler_params=pltpu.CompilerParams(vmem_limit_bytes=VMEM_LIMIT),
        cost_estimate=pl.CostEstimate(
            flops=2 * samples * mats * sites * d * d,
            bytes_accessed=6 * samples * mats * sites * d,
            transcendentals=0,
        ),
        name="jac_rows",
    )(activations, cotangents)


def energy_kernel(spins_ref, offdiag_ref, out_ref):
    total, width = out_ref.shape
    local = spins_ref.shape[0]
    sites = SIDE * SIDE
    z = (2 * spins_ref[...] - 1).astype(F32)
    column = iota((local, sites), 1) % SIDE
    right = jnp.where(
        column == SIDE - 1, pltpu.roll(z, SIDE - 1, 1), pltpu.roll(z, sites - 1, 1)
    )
    below = pltpu.roll(z, sites - SIDE, 1)
    energy = offdiag_ref[...] + jnp.sum(z * (right + below), axis=1, keepdims=True)
    first = lax.axis_index("samp") * local
    mine = lax.axis_index("layer") == 0
    spread = jnp.concatenate([energy] * (total // local), axis=0)
    row = iota((total, width), 0)
    here = (row >= first) & (row < first + local) & (iota((total, width), 1) == total) & mine
    out_ref[...] = jnp.where(here, spread, F32(0.0))


def energy_column(spins, offdiag, total, width):
    return pl.pallas_call(
        energy_kernel,
        out_shape=jax.ShapeDtypeStruct((total, width), F32),
        compiler_params=pltpu.CompilerParams(vmem_limit_bytes=VMEM_LIMIT),
        name="energy_column",
    )(spins, offdiag[:, None])


def gram_kernel(*refs):
    *block_refs, start_ref, out_ref, flat = refs
    local, count, d = block_refs[0].shape
    total = local * len(block_refs)
    joined = CHUNK // local
    me = lax.axis_index("samp")
    block = CHUNK * CHUNK
    dest = iota((block, block), 0)
    sample = dest % CHUNK
    sample = (sample // local ^ me % joined) * local + sample % local
    source = sample * CHUNK + dest // CHUNK
    swap = (iota((block, block), 1) == source).astype(F32).astype(BF16)
    for row in range(0, count, CHUNK):
        for j in range(len(block_refs) // joined):
            pieces = [ref[:, row : row + CHUNK] for ref in block_refs[j * joined : (j + 1) * joined]]
            piece = jnp.concatenate(pieces, axis=0).reshape(block, d)
            turned = jnp.dot(swap, piece, preferred_element_type=F32).astype(BF16)
            place = pl.ds(pl.multiple_of((me // joined ^ j) * CHUNK, CHUNK), CHUNK)
            for r in range(CHUNK):
                flat[row + r, place] = turned[r * CHUNK : (r + 1) * CHUNK]
    lined = jnp.concatenate([flat[r] for r in range(count)], axis=1)
    gram = lax.dot_general(lined, lined, (((1,), (1,)), ((), ())), preferred_element_type=F32)
    out_ref[...] = start_ref[...]
    out_ref[:, :total] += gram


def gram_partial(blocks, start):
    local, count, d = blocks[0].shape
    total, width = start.shape
    return pl.pallas_call(
        gram_kernel,
        out_shape=jax.ShapeDtypeStruct((total, width), F32),
        scratch_shapes=[pltpu.VMEM((count, total, d), BF16)],
        compiler_params=pltpu.CompilerParams(vmem_limit_bytes=VMEM_LIMIT),
        cost_estimate=pl.CostEstimate(
            flops=2 * total * total * count * d,
            bytes_accessed=2 * total * count * d,
            transcendentals=0,
        ),
        name="gram_partial",
    )(*blocks, start)


def eliminate(matrix, total):
    row = iota(matrix.shape, 0)
    lane = iota(matrix.shape, 1)
    if total <= 64:
        for k in range(total):
            column = matrix[:, k : k + 1]
            pivot_row = matrix[k : k + 1, :]
            scaled = pivot_row * (F32(1.0) / pivot_row[:, k : k + 1])
            matrix = matrix - jnp.where(row == k, F32(0.0), column) * scaled
    else:

        def one(k, held):
            column = jnp.sum(jnp.where(lane == k, held, F32(0.0)), axis=1, keepdims=True)
            pivot_row = jnp.sum(jnp.where(row == k, held, F32(0.0)), axis=0, keepdims=True)
            here = lane[:1] == k
            pivot = jnp.sum(jnp.where(here, pivot_row, F32(0.0)), axis=1, keepdims=True)
            scaled = pivot_row * (F32(1.0) / pivot)
            return held - jnp.where(row == k, F32(0.0), column) * scaled

        matrix = lax.fori_loop(0, total, one, matrix)
    diag = jnp.sum(jnp.where(row == lane, matrix, F32(0.0)), axis=1, keepdims=True)
    return matrix[:, total : total + 1] / diag


def tree_sum(parts):
    while len(parts) > 1:
        parts = [a + b for a, b in zip(parts[::2], parts[1::2])]
    return parts[0]


def partners(value, axis, first, count):
    size = lax.axis_size(axis)
    parts = [value]
    for k in range(1, count):
        perm = [(i, i ^ (k * first)) for i in range(size)]
        parts.append(lax.ppermute(value, axis, perm))
    return parts


def solve_kernel(owners, *refs):
    *in_refs, weights_ref, update_ref, held = refs
    mats, share, d = update_ref.shape
    local = weights_ref.shape[1]
    gram_refs = [ref for ref in in_refs if len(ref.shape) == 2]
    block_refs = [ref for ref in in_refs if len(ref.shape) == 3]
    total, width = gram_refs[0].shape
    raw = tree_sum([ref[...] for ref in gram_refs])
    row = iota((total, width), 0)
    lane = iota((total, width), 1)
    inside = lane < total
    scale = F32(1.0 / total)
    row_mean = jnp.sum(jnp.where(inside, raw, F32(0.0)), axis=1, keepdims=True) * scale
    col_mean = jnp.sum(raw, axis=0, keepdims=True) * scale
    mean = jnp.sum(row_mean, axis=0, keepdims=True) * scale
    gram = (raw - col_mean - row_mean + mean) * scale
    eps = (raw - col_mean) * F32(1.0 / total**0.5)
    on_diag = row == lane
    trace = jnp.sum(
        jnp.sum(jnp.where(on_diag, gram, F32(0.0)), axis=1, keepdims=True), axis=0, keepdims=True
    )
    shift = F32(shift_ratio) * trace * scale
    system = jnp.where(inside, gram + jnp.where(on_diag, shift, F32(0.0)), eps)
    weights = eliminate(system, total)
    me = lax.axis_index("samp")
    own = jnp.where(row - me * local == lane, weights, F32(0.0))
    weights_ref[...] = jnp.sum(own, axis=0, keepdims=True)[:, :local]
    coeffs = weights - jnp.sum(weights, axis=0, keepdims=True) * scale
    held[...] = jnp.broadcast_to(coeffs, (total, d))
    parts = len(block_refs) // owners
    each = mats // parts
    for part in range(parts):
        acc = jnp.zeros((each * share, d), F32)
        for k in range(owners):
            mine = held[pl.ds(pl.multiple_of((me ^ k) * local, local), local)]
            for s in range(local):
                acc = acc + mine[s : s + 1] * block_refs[part * owners + k][s].astype(F32)
        for m in range(each):
            update_ref[part * each + m] = acc[m * share : (m + 1) * share]


def solve_and_project(grams, parts, mats):
    total, width = grams[0].shape
    owners = len(parts[0])
    local, count, d = parts[0][0].shape
    share = count * len(parts) // mats
    return pl.pallas_call(
        functools.partial(solve_kernel, owners),
        out_shape=(
            jax.ShapeDtypeStruct((1, local), F32),
            jax.ShapeDtypeStruct((mats, share, d), F32),
        ),
        scratch_shapes=[pltpu.VMEM((total, d), F32)],
        compiler_params=pltpu.CompilerParams(vmem_limit_bytes=VMEM_LIMIT),
        name="solve_and_project",
    )(*grams, *[block for blocks in parts for block in blocks])


def body(spins, activations, cotangents, offdiag):
    local, mats = activations.shape[:2]
    owners = lax.axis_size("samp")
    total = local * owners
    width = (total // LANES + 1) * LANES
    share = activations.shape[3] // owners
    parts = mats if share % CHUNK == 0 else 1
    partial = energy_column(spins, offdiag, total, width)
    held = []
    for part in range(parts):
        blocks = list(jac_rows(activations, cotangents, owners, part, parts))
        for k in range(owners - 1, 0, -1):
            perm = [(i, i ^ k) for i in range(owners)]
            blocks[k] = lax.ppermute(blocks[k], "samp", perm)
        held.append(blocks)
    for blocks in held:
        partial = gram_partial(blocks, partial)
    grams = partners(partial, "layer", 1, lax.axis_size("layer"))
    first = 1
    while first < owners:
        count = 2 if first == 1 else min(4, owners // first)
        grams = partners(tree_sum(grams), "samp", first, count)
        first *= count
    weights, update = solve_and_project(grams, held, mats)
    return weights.reshape(local), update


def solution(mesh):
    placed = (
        P("samp", None),
        P("samp", "layer", None, None),
        P("samp", "layer", None, None),
        P("samp"),
    )
    return jax.shard_map(
        body,
        mesh=mesh,
        in_specs=placed,
        out_specs=(P("samp"), P("layer", "samp", None)),
        check_vma=False,
    )
```

time: 101 us -> 84.9 us (0.84)
  waiting for transfers between devices: 49.6 us -> 20.4 us
  starting transfers between devices: 18.9 us -> 41.8 us
  Pallas kernels: 28.1 us -> 18.6 us
    all_to_all x2 -> x0, waiting for transfers between devices: 40.5 us -> none  [body(): held = lax.all_to_all(jac, 'samp', split_axis=0, concat_axis=0, tiled=True)]
    ppermute x0 -> x14, starting transfers between devices: none -> 31.6 us  [body(): blocks[k] = lax.ppermute(blocks[k], 'samp', perm)]
    ppermute x0 -> x14, waiting for transfers between devices: none -> 12 us  [body(): blocks[k] = lax.ppermute(blocks[k], 'samp', perm)]
    all_to_all x2 -> x0, starting transfers between devices: 10.9 us -> none  [body(): held = lax.all_to_all(jac, 'samp', split_axis=0, concat_axis=0, tiled=True)]
    pallas_call x5, Pallas kernels: 26.6 us -> 18.4 us  [the longest x2 9.67 us: jac_rows(): pl.pallas_call(functools.partial(jac_kernel, part * mats), in_specs=[hbm,...]
    ppermute x7, starting transfers between devices: 8.07 us -> 10.1 us  [partners(): parts.append(lax.ppermute(value, axis, perm))]
    unnamed x14 -> x8, local copies, waits for them, and re-layouts: 1.61 us -> 3.18 us
    pallas_call x1, Pallas kernels: 1.54 us -> 0.22 us  [energy_column(): pl.pallas_call(energy_kernel, out_shape=jax.ShapeDtypeStruct((total, widt...]
  transfers between devices with their start and end apart: 9 -> 21, of which waited for: 7 -> 8; matrix products, arithmetic and copies ran while one was open for 1% -> 0% of each run, Pallas kernels for 11% -> 7%
where the time goes in v5:
time: 84.9 us; the launch traced here: 84.7 us
  starting transfers between devices  41.8 us (49%)
  waiting for transfers between devices  20.4 us (24%)
  Pallas kernels  18.6 us (22%)
  local copies, waits for them, and re-layouts  3.26 us (4%)
    ppermute x14, starting transfers between devices, body(): blocks[k] = lax.ppermute(blocks[k], 'samp', perm)  31.6 us
    ppermute x14, waiting for transfers between devices, body(): blocks[k] = lax.ppermute(blocks[k], 'samp', perm)  12 us
    ppermute x7, starting transfers between devices, partners(): parts.append(lax.ppermute(value, axis, perm))  10.1 us
    pallas_call x2, Pallas kernels, jac_rows(): pl.pallas_call(functools.partial(jac_kernel, part * mats), in_specs=[hbm,...  9.67 us
    ppermute x7, waiting for transfers between devices, partners(): parts.append(lax.ppermute(value, axis, perm))  8.42 us
    pallas_call x1, Pallas kernels, solve_and_project(): pl.pallas_call(functools.partial(solve_kernel, owners), out_shape=(jax.Sh...  6.89 us
    unnamed x8, local copies, waits for them, and re-layouts  3.18 us
    pallas_call x2, Pallas kernels, gram_partial(): pl.pallas_call(gram_kernel, out_shape=jax.ShapeDtypeStruct((total, width)...  1.78 us
  transfers between devices with their start and end apart: 21, of which 8 were waited for; matrix products, arithmetic and copies ran while one was open for 0% of the time, Pallas kernels for 7%

profile of v5, /device:TPU:0, one launch (start us, length us, event | category | flops | bytes accessed | tf_op | source)
XLA Modules:
  0.0 84.7 jit_solution(7653087122911726844)
XLA Ops:
  0.6 0.0 copy-start
  0.6 1.6 %copy-done = bf16[8,2,256,256]{3,2,1,0:T(8,128)(2,1)S(1)} copy-done((bf16[8,2,256,256]{3,2,1,0:T(8,128)(2,1)S(1)}, bf16[8,2,256,256]{3,2,1,0:T(8,128)(2,1)}, u32[]{:S(2)}) %copy-start) | copy-done | bytes 2097176
  2.2 0.0 copy-start.1
  2.2 1.6 %copy-done.1 = bf16[8,2,256,256]{3,2,1,0:T(8,128)(2,1)S(1)} copy-done((bf16[8,2,256,256]{3,2,1,0:T(8,128)(2,1)S(1)}, bf16[8,2,256,256]{3,2,1,0:T(8,128)(2,1)}, u32[]{:S(2)}) %copy-start.1) | copy-done | bytes 2097176
  3.8 4.8 %jac_rows.3 = (bf16[8,32,256]{2,1,0:T(8,128)(2,1)S(1)}, bf16[8,32,256]{2,1,0:T(8,128)(2,1)S(1)}, bf16[8,32,256]{2,1,0:T(8,128)(2,1)S(1)}, bf16[8,32,256]{2,1,0:T...) custom-call(bf16[8,2,256,256]{3,2,1,0:T(8,128)(2,1)S(1)} %copy-done,, ...), custom_call_target="tpu_custom_call" | custom-call | flops 268435456 | bytes 3145728 | tf_op jit(solution)/shard_map/jac_rows/pallas_call | solution.py:56
  8.7 3.0 %collective-permute-start.7 = (bf16[8,32,256]{2,1,0:T(8,128)(2,1)S(1)}, bf16[8,32,256]{2,1,0:T(8,128)(2,1)S(1)}, u32[]{:S(2)}, u32[]{:S(2)}) collective-permute-start(bf16[8,32,256]{2,1,0:T(8,128)(2,1)S(1)} %get-tuple-element.29), channel_id=1, source_target_pairs={{0,4},{4,0},{8,12},{12,8},{16,20},{20,16},{24,28},{28,24},{1,5},{5... | collective-permute-start | bytes 393224 | tf_op jit(solution)/shard_map/ppermute | solution.py:257
  11.7 1.6 %collective-permute-start.8 = (bf16[8,32,256]{2,1,0:T(8,128)(2,1)S(1)}, bf16[8,32,256]{2,1,0:T(8,128)(2,1)S(1)}, u32[]{:S(2)}, u32[]{:S(2)}) collective-permute-start(bf16[8,32,256]{2,1,0:T(8,128)(2,1)S(1)} %get-tuple-element.30), channel_id=1, source_target_pairs={{0,8},{4,12},{8,0},{12,4},{16,24},{20,28},{24,16},{28,20},{1,9},{5... | collective-permute-start | bytes 393224 | tf_op jit(solution)/shard_map/ppermute | solution.py:257
  13.3 0.0 collective-permute-start.9
  13.3 3.0 %collective-permute-start.10 = (bf16[8,32,256]{2,1,0:T(8,128)(2,1)S(1)}, bf16[8,32,256]{2,1,0:T(8,128)(2,1)S(1)}, u32[]{:S(2)}, u32[]{:S(2)}) collective-permute-start(bf16[8,32,256]{2,1,0:T(8,128)(2,1)S(1)} %get-tuple-element.32), channel_id=1, source_target_pairs={{0,16},{4,20},{8,24},{12,28},{16,0},{20,4},{24,8},{28,12},{1,17},{... | collective-permute-start | bytes 393224 | tf_op jit(solution)/shard_map/ppermute | solution.py:257
  16.3 0.0 copy-start.3
  16.3 0.0 copy-start.2
  16.3 1.3 %collective-permute-start.11 = (bf16[8,32,256]{2,1,0:T(8,128)(2,1)S(1)}, bf16[8,32,256]{2,1,0:T(8,128)(2,1)S(1)}, u32[]{:S(2)}, u32[]{:S(2)}) collective-permute-start(bf16[8,32,256]{2,1,0:T(8,128)(2,1)S(1)} %get-tuple-element.33), channel_id=1, source_target_pairs={{0,20},{4,16},{8,28},{12,24},{16,4},{20,0},{24,12},{28,8},{1,21},{... | collective-permute-start | bytes 393224 | tf_op jit(solution)/shard_map/ppermute | solution.py:257
  17.5 4.8 %jac_rows.2 = (bf16[8,32,256]{2,1,0:T(8,128)(2,1)S(1)}, bf16[8,32,256]{2,1,0:T(8,128)(2,1)S(1)}, bf16[8,32,256]{2,1,0:T(8,128)(2,1)S(1)}, bf16[8,32,256]{2,1,0:T...) custom-call(bf16[8,2,256,256]{3,2,1,0:T(8,128)(2,1)S(1)} %copy-done,, ...), custom_call_target="tpu_custom_call" | custom-call | flops 268435456 | bytes 3145728 | tf_op jit(solution)/shard_map/jac_rows/pallas_call | solution.py:56
  22.4 0.0 collective-permute-done.7.refs_1_.refs_5_
  22.4 3.7 %collective-permute-start.12 = (bf16[8,32,256]{2,1,0:T(8,128)(2,1)S(1)}, bf16[8,32,256]{2,1,0:T(8,128)(2,1)S(1)}, u32[]{:S(2)}, u32[]{:S(2)}) collective-permute-start(bf16[8,32,256]{2,1,0:T(8,128)(2,1)S(1)} %get-tuple-element.34), channel_id=1, source_target_pairs={{0,24},{4,28},{8,16},{12,20},{16,8},{20,12},{24,0},{28,4},{1,25},{... | collective-permute-start | bytes 393224 | tf_op jit(solution)/shard_map/ppermute | solution.py:257
  26.1 0.0 collective-permute-done.8.refs_2_.refs_6_
  26.1 0.0 collective-permute-start.13
  26.1 0.0 collective-permute-done.9.refs_3_.refs_7_
  26.2 1.6 %collective-permute-start = (bf16[8,32,256]{2,1,0:T(8,128)(2,1)S(1)}, bf16[8,32,256]{2,1,0:T(8,128)(2,1)S(1)}, u32[]{:S(2)}, u32[]{:S(2)}) collective-permute-start(bf16[8,32,256]{2,1,0:T(8,128)(2,1)S(1)} %get-tuple-element.21), channel_id=1, source_target_pairs={{0,4},{4,0},{8,12},{12,8},{16,20},{20,16},{24,28},{28,24},{1,5},{5... | collective-permute-start | bytes 393224 | tf_op jit(solution)/shard_map/ppermute | solution.py:257
  27.8 0.0 collective-permute-done.10.refs_4_.refs_8_
  27.8 3.1 %collective-permute-start.1 = (bf16[8,32,256]{2,1,0:T(8,128)(2,1)S(1)}, bf16[8,32,256]{2,1,0:T(8,128)(2,1)S(1)}, u32[]{:S(2)}, u32[]{:S(2)}) collective-permute-start(bf16[8,32,256]{2,1,0:T(8,128)(2,1)S(1)} %get-tuple-element.22), channel_id=1, source_target_pairs={{0,8},{4,12},{8,0},{12,4},{16,24},{20,28},{24,16},{28,20},{1,9},{5... | collective-permute-start | bytes 393224 | tf_op jit(solution)/shard_map/ppermute | solution.py:257
  30.8 4.9 %collective-permute-done.11.refs_5_.refs_9_ = bf16[8,32,256]{2,1,0:T(8,128)(2,1)S(1)} collective-permute-done((bf16[8,32,256]{2,1,0:T(8,128)(2,1)S(1)}, bf16[8,32,256]{2,1,0:T(8,128)(2,1)S(1)}, u32[]{:S(2)}, u32[]{:S(2)}) %collective-permute-start.11) | collective-permute-done | bytes 131104 | tf_op jit(solution)/shard_map/ppermute | solution.py:257
  35.7 0.4 collective-permute-start.2
  36.2 0.0 collective-permute-done.12.refs_6_.refs_10_
  36.2 4.2 %collective-permute-start.3 = (bf16[8,32,256]{2,1,0:T(8,128)(2,1)S(1)}, bf16[8,32,256]{2,1,0:T(8,128)(2,1)S(1)}, u32[]{:S(2)}, u32[]{:S(2)}) collective-permute-start(bf16[8,32,256]{2,1,0:T(8,128)(2,1)S(1)} %get-tuple-element.24), channel_id=1, source_target_pairs={{0,16},{4,20},{8,24},{12,28},{16,0},{20,4},{24,8},{28,12},{1,17},{... | collective-permute-start | bytes 393224 | tf_op jit(solution)/shard_map/ppermute | solution.py:257
  40.4 0.0 collective-permute-done.13.refs_7_.refs_11_
  40.4 9.3 %collective-permute-start.4 = (bf16[8,32,256]{2,1,0:T(8,128)(2,1)S(1)}, bf16[8,32,256]{2,1,0:T(8,128)(2,1)S(1)}, u32[]{:S(2)}, u32[]{:S(2)}) collective-permute-start(bf16[8,32,256]{2,1,0:T(8,128)(2,1)S(1)} %get-tuple-element.25), channel_id=1, source_target_pairs={{0,20},{4,16},{8,28},{12,24},{16,4},{20,0},{24,12},{28,8},{1,21},{... | collective-permute-start | bytes 393224 | tf_op jit(solution)/shard_map/ppermute | solution.py:257
  49.7 0.0 collective-permute-done.refs_1_.refs_13_
  49.7 0.0 collective-permute-start.5
  49.7 0.0 collective-permute-done.1.refs_2_.refs_14_
  49.7 0.4 collective-permute-start.6
  50.1 0.0 copy-done.3
  50.1 0.1 copy.6.offdiag_ref
  50.2 0.0 copy-done.2
  50.2 0.2 energy_column.1.refs_8_
  50.4 0.9 %gram_partial.2.refs_8_ = f32[64,128]{1,0:T(8,128)S(1)} custom-call(bf16[8,32,256]{2,1,0:T(8,128)(2,1)S(1)} %get-tuple-element.28.refs_0_.refs_4_, bf16[8,32,256]{2,1,0:T(8,128)(2,1)S(1)} %collective-permute-done.7.refs_1_.refs_5_, bf16[8,32,256]{2,1,0:T(8,128)(2,1)S(1)} %collective-permute-done.8.refs_2_.refs_6_, ...), custom_call_target="tpu_custom_call" | custom-call | flops 67108864 | bytes 1048576 | tf_op jit(solution)/shard_map/gram_partial/pallas_call | solution.py:133
  51.3 0.0 collective-permute-done.2.refs_3_.refs_15_
  51.3 0.5 collective-permute-done.3.refs_4_.refs_16_
  51.8 6.5 %collective-permute-done.4.refs_5_.refs_17_ = bf16[8,32,256]{2,1,0:T(8,128)(2,1)S(1)} collective-permute-done((bf16[8,32,256]{2,1,0:T(8,128)(2,1)S(1)}, bf16[8,32,256]{2,1,0:T(8,128)(2,1)S(1)}, u32[]{:S(2)}, u32[]{:S(2)}) %collective-permute-start.4) | collective-permute-done | bytes 131104 | tf_op jit(solution)/shard_map/ppermute | solution.py:257
  58.3 0.0 collective-permute-done.5.refs_6_.refs_18_
  58.3 0.0 collective-permute-done.6.refs_7_.refs_19_
  58.4 0.9 %gram_partial.3 = f32[64,128]{1,0:T(8,128)S(1)} custom-call(bf16[8,32,256]{2,1,0:T(8,128)(2,1)S(1)} %get-tuple-element.20.refs_0_.refs_12_, bf16[8,32,256]{2,1,0:T(8,128)(2,1)S(1)} %collective-permute-done.refs_1_.refs_13_, bf16[8,32,256]{2,1,0:T(8,128)(2,1)S(1)} %collective-permute-done.1.refs_2_.refs_14_, ...), custom_call_target="tpu_custom_call" | custom-call | flops 67108864 | bytes 1048576 | tf_op jit(solution)/shard_map/gram_partial/pallas_call | solution.py:133
  59.2 0.1 collective-permute-start.16
  59.3 1.6 %collective-permute-start.15 = (f32[64,128]{1,0:T(8,128)S(1)}, f32[64,128]{1,0:T(8,128)S(1)}, u32[]{:S(2)}, u32[]{:S(2)}) collective-permute-start(f32[64,128]{1,0:T(8,128)S(1)} %gram_partial.3), channel_id=1, source_target_pairs={{0,2},{1,3},{2,0},{3,1},{4,6},{5,7},{6,4},{7,5},{8,10},{9,11},{10,... | collective-permute-start | bytes 98312 | tf_op jit(solution)/shard_map/ppermute | solution.py:182
  60.9 0.3 collective-permute-start.14
  61.2 1.8 %collective-permute-done.16 = f32[64,128]{1,0:T(8,128)S(1)} collective-permute-done((f32[64,128]{1,0:T(8,128)S(1)}, f32[64,128]{1,0:T(8,128)S(1)}, u32[]{:S(2)}, u32[]{:S(2)}) %collective-permute-start.16) | collective-permute-done | bytes 32800 | tf_op jit(solution)/shard_map/ppermute | solution.py:182
  63.0 0.4 collective-permute-done.15
  63.4 0.0 collective-permute-done.14
  63.4 1.2 %collective-permute-start.17 = (f32[64,128]{1,0:T(8,128)S(1)}, f32[64,128]{1,0:T(8,128)S(1)}, u32[]{:S(2)}, u32[]{:S(2)}) collective-permute-start(f32[64,128]{1,0:T(8,128)S(1)} %add_add_fusion), channel_id=1, source_target_pairs={{0,4},{4,0},{8,12},{12,8},{16,20},{20,16},{24,28},{28,24},{1,5},{5... | collective-permute-start | bytes 98312 | tf_op jit(solution)/shard_map/ppermute | solution.py:182
  64.5 2.8 %collective-permute-done.17 = f32[64,128]{1,0:T(8,128)S(1)} collective-permute-done((f32[64,128]{1,0:T(8,128)S(1)}, f32[64,128]{1,0:T(8,128)S(1)}, u32[]{:S(2)}, u32[]{:S(2)}) %collective-permute-start.17) | collective-permute-done | bytes 32800 | tf_op jit(solution)/shard_map/ppermute | solution.py:182
  67.4 3.1 %collective-permute-start.20 = (f32[64,128]{1,0:T(8,128)S(1)}, f32[64,128]{1,0:T(8,128)S(1)}, u32[]{:S(2)}, u32[]{:S(2)}) collective-permute-start(f32[64,128]{1,0:T(8,128)S(1)} %add.15.refs_0_), channel_id=1, source_target_pairs={{0,24},{4,28},{8,16},{12,20},{16,8},{20,12},{24,0},{28,4},{1,25},{... | collective-permute-start | bytes 98312 | tf_op jit(solution)/shard_map/ppermute | solution.py:182
  70.5 3.4 %collective-permute-start.19 = (f32[64,128]{1,0:T(8,128)S(1)}, f32[64,128]{1,0:T(8,128)S(1)}, u32[]{:S(2)}, u32[]{:S(2)}) collective-permute-start(f32[64,128]{1,0:T(8,128)S(1)} %add.15.refs_0_), channel_id=1, source_target_pairs={{0,16},{4,20},{8,24},{12,28},{16,0},{20,4},{24,8},{28,12},{1,17},{... | collective-permute-start | bytes 98312 | tf_op jit(solution)/shard_map/ppermute | solution.py:182
  73.9 0.5 collective-permute-start.18
  74.4 0.0 collective-permute-done.20.refs_3_
  74.4 1.7 %collective-permute-done.19.refs_2_ = f32[64,128]{1,0:T(8,128)S(1)} collective-permute-done((f32[64,128]{1,0:T(8,128)S(1)}, f32[64,128]{1,0:T(8,128)S(1)}, u32[]{:S(2)}, u32[]{:S(2)}) %collective-permute-start.19) | collective-permute-done | bytes 32800 | tf_op jit(solution)/shard_map/ppermute | solution.py:182
  76.1 1.7 %collective-permute-done.18.refs_1_ = f32[64,128]{1,0:T(8,128)S(1)} collective-permute-done((f32[64,128]{1,0:T(8,128)S(1)}, f32[64,128]{1,0:T(8,128)S(1)}, u32[]{:S(2)}, u32[]{:S(2)}) %collective-permute-start.18) | collective-permute-done | bytes 32800 | tf_op jit(solution)/shard_map/ppermute | solution.py:182
  77.8 6.9 %solve_and_project.1 = (f32[1,8]{1,0:T(1,128)}, f32[2,32,256]{2,1,0:T(8,128)}) custom-call(f32[64,128]{1,0:T(8,128)S(1)} %add.15.refs_0_, f32[64,128]{1,0:T(8,128)S(1)} %collective-permute-done.18.refs_1_, f32[64,128]{1,0:T(8,128)S(1)} %collective-permute-done.19.refs_2_, f32[64,128]{1,0:T(8,128)S(1)} %collective-permute-done.20.refs_3_, ...), custom_call_target="tpu_custom_call" | custom-call | tf_op jit(solution)/shard_map/solve_and_project/pallas_call | solution.py:232
  (2 shorter events, 0.0 us)
Async XLA Ops:
  0.6 1.6 %copy-start = (bf16[8,2,256,256]{3,2,1,0:T(8,128)(2,1)S(1)}, bf16[8,2,256,256]{3,2,1,0:T(8,128)(2,1)}, u32[]{:S(2)}) copy-start(bf16[8,2,256,256]{3,2,1,0:T(8,128)(2,1)} %act_hbm.3) | copy-start | bytes 6291460
  2.2 1.6 %copy-start.1 = (bf16[8,2,256,256]{3,2,1,0:T(8,128)(2,1)S(1)}, bf16[8,2,256,256]{3,2,1,0:T(8,128)(2,1)}, u32[]{:S(2)}) copy-start(bf16[8,2,256,256]{3,2,1,0:T(8,128)(2,1)} %cot_hbm.3) | copy-start | bytes 6291460
  8.7 13.7 %collective-permute-start.7 = (bf16[8,32,256]{2,1,0:T(8,128)(2,1)S(1)}, bf16[8,32,256]{2,1,0:T(8,128)(2,1)S(1)}, u32[]{:S(2)}, u32[]{:S(2)}) collective-permute-start(bf16[8,32,256]{2,1,0:T(8,128)(2,1)S(1)} %get-tuple-element.29), channel_id=1, source_target_pairs={{0,4},{4,0},{8,12},{12,8},{16,20},{20,16},{24,28},{28,24},{1,5},{5... | collective-permute-start | bytes 393224 | tf_op jit(solution)/shard_map/ppermute | solution.py:257
  11.7 14.4 %collective-permute-start.8 = (bf16[8,32,256]{2,1,0:T(8,128)(2,1)S(1)}, bf16[8,32,256]{2,1,0:T(8,128)(2,1)S(1)}, u32[]{:S(2)}, u32[]{:S(2)}) collective-permute-start(bf16[8,32,256]{2,1,0:T(8,128)(2,1)S(1)} %get-tuple-element.30), channel_id=1, source_target_pairs={{0,8},{4,12},{8,0},{12,4},{16,24},{20,28},{24,16},{28,20},{1,9},{5... | collective-permute-start | bytes 393224 | tf_op jit(solution)/shard_map/ppermute | solution.py:257
  13.3 12.9 %collective-permute-start.9 = (bf16[8,32,256]{2,1,0:T(8,128)(2,1)S(1)}, bf16[8,32,256]{2,1,0:T(8,128)(2,1)S(1)}, u32[]{:S(2)}, u32[]{:S(2)}) collective-permute-start(bf16[8,32,256]{2,1,0:T(8,128)(2,1)S(1)} %get-tuple-element.31), channel_id=1, source_target_pairs={{0,12},{4,8},{8,4},{12,0},{16,28},{20,24},{24,20},{28,16},{1,13},{... | collective-permute-start | bytes 393224 | tf_op jit(solution)/shard_map/ppermute | solution.py:257
  13.3 14.5 %collective-permute-start.10 = (bf16[8,32,256]{2,1,0:T(8,128)(2,1)S(1)}, bf16[8,32,256]{2,1,0:T(8,128)(2,1)S(1)}, u32[]{:S(2)}, u32[]{:S(2)}) collective-permute-start(bf16[8,32,256]{2,1,0:T(8,128)(2,1)S(1)} %get-tuple-element.32), channel_id=1, source_target_pairs={{0,16},{4,20},{8,24},{12,28},{16,0},{20,4},{24,8},{28,12},{1,17},{... | collective-permute-start | bytes 393224 | tf_op jit(solution)/shard_map/ppermute | solution.py:257
  16.3 33.8 %copy-start.3 = (f32[8]{0:T(128)S(1)}, f32[8]{0:T(128)}, u32[]{:S(2)}) copy-start(f32[8]{0:T(128)} %param.7) | copy-start | bytes 100
  16.3 33.9 %copy-start.2 = (s32[8,256]{1,0:T(8,128)S(1)}, s32[8,256]{1,0:T(8,128)}, u32[]{:S(2)}) copy-start(s32[8,256]{1,0:T(8,128)} %spins_ref.1) | copy-start | bytes 24580
  16.3 19.5 %collective-permute-start.11 = (bf16[8,32,256]{2,1,0:T(8,128)(2,1)S(1)}, bf16[8,32,256]{2,1,0:T(8,128)(2,1)S(1)}, u32[]{:S(2)}, u32[]{:S(2)}) collective-permute-start(bf16[8,32,256]{2,1,0:T(8,128)(2,1)S(1)} %get-tuple-element.33), channel_id=1, source_target_pairs={{0,20},{4,16},{8,28},{12,24},{16,4},{20,0},{24,12},{28,8},{1,21},{... | collective-permute-start | bytes 393224 | tf_op jit(solution)/shard_map/ppermute | solution.py:257
  22.4 13.8 %collective-permute-start.12 = (bf16[8,32,256]{2,1,0:T(8,128)(2,1)S(1)}, bf16[8,32,256]{2,1,0:T(8,128)(2,1)S(1)}, u32[]{:S(2)}, u32[]{:S(2)}) collective-permute-start(bf16[8,32,256]{2,1,0:T(8,128)(2,1)S(1)} %get-tuple-element.34), channel_id=1, source_target_pairs={{0,24},{4,28},{8,16},{12,20},{16,8},{20,12},{24,0},{28,4},{1,25},{... | collective-permute-start | bytes 393224 | tf_op jit(solution)/shard_map/ppermute | solution.py:257
  26.1 14.3 %collective-permute-start.13 = (bf16[8,32,256]{2,1,0:T(8,128)(2,1)S(1)}, bf16[8,32,256]{2,1,0:T(8,128)(2,1)S(1)}, u32[]{:S(2)}, u32[]{:S(2)}) collective-permute-start(bf16[8,32,256]{2,1,0:T(8,128)(2,1)S(1)} %get-tuple-element.35), channel_id=1, source_target_pairs={{0,28},{4,24},{8,20},{12,16},{16,12},{20,8},{24,4},{28,0},{1,29},{... | collective-permute-start | bytes 393224 | tf_op jit(solution)/shard_map/ppermute | solution.py:257
  26.2 23.6 %collective-permute-start = (bf16[8,32,256]{2,1,0:T(8,128)(2,1)S(1)}, bf16[8,32,256]{2,1,0:T(8,128)(2,1)S(1)}, u32[]{:S(2)}, u32[]{:S(2)}) collective-permute-start(bf16[8,32,256]{2,1,0:T(8,128)(2,1)S(1)} %get-tuple-element.21), channel_id=1, source_target_pairs={{0,4},{4,0},{8,12},{12,8},{16,20},{20,16},{24,28},{28,24},{1,5},{5... | collective-permute-start | bytes 393224 | tf_op jit(solution)/shard_map/ppermute | solution.py:257
  27.8 22.0 %collective-permute-start.1 = (bf16[8,32,256]{2,1,0:T(8,128)(2,1)S(1)}, bf16[8,32,256]{2,1,0:T(8,128)(2,1)S(1)}, u32[]{:S(2)}, u32[]{:S(2)}) collective-permute-start(bf16[8,32,256]{2,1,0:T(8,128)(2,1)S(1)} %get-tuple-element.22), channel_id=1, source_target_pairs={{0,8},{4,12},{8,0},{12,4},{16,24},{20,28},{24,16},{28,20},{1,9},{5... | collective-permute-start | bytes 393224 | tf_op jit(solution)/shard_map/ppermute | solution.py:257
  35.7 15.6 %collective-permute-start.2 = (bf16[8,32,256]{2,1,0:T(8,128)(2,1)S(1)}, bf16[8,32,256]{2,1,0:T(8,128)(2,1)S(1)}, u32[]{:S(2)}, u32[]{:S(2)}) collective-permute-start(bf16[8,32,256]{2,1,0:T(8,128)(2,1)S(1)} %get-tuple-element.23), channel_id=1, source_target_pairs={{0,12},{4,8},{8,4},{12,0},{16,28},{20,24},{24,20},{28,16},{1,13},{... | collective-permute-start | bytes 393224 | tf_op jit(solution)/shard_map/ppermute | solution.py:257
  36.2 15.7 %collective-permute-start.3 = (bf16[8,32,256]{2,1,0:T(8,128)(2,1)S(1)}, bf16[8,32,256]{2,1,0:T(8,128)(2,1)S(1)}, u32[]{:S(2)}, u32[]{:S(2)}) collective-permute-start(bf16[8,32,256]{2,1,0:T(8,128)(2,1)S(1)} %get-tuple-element.24), channel_id=1, source_target_pairs={{0,16},{4,20},{8,24},{12,28},{16,0},{20,4},{24,8},{28,12},{1,17},{... | collective-permute-start | bytes 393224 | tf_op jit(solution)/shard_map/ppermute | solution.py:257
  40.4 17.9 %collective-permute-start.4 = (bf16[8,32,256]{2,1,0:T(8,128)(2,1)S(1)}, bf16[8,32,256]{2,1,0:T(8,128)(2,1)S(1)}, u32[]{:S(2)}, u32[]{:S(2)}) collective-permute-start(bf16[8,32,256]{2,1,0:T(8,128)(2,1)S(1)} %get-tuple-element.25), channel_id=1, source_target_pairs={{0,20},{4,16},{8,28},{12,24},{16,4},{20,0},{24,12},{28,8},{1,21},{... | collective-permute-start | bytes 393224 | tf_op jit(solution)/shard_map/ppermute | solution.py:257
  49.7 8.6 %collective-permute-start.5 = (bf16[8,32,256]{2,1,0:T(8,128)(2,1)S(1)}, bf16[8,32,256]{2,1,0:T(8,128)(2,1)S(1)}, u32[]{:S(2)}, u32[]{:S(2)}) collective-permute-start(bf16[8,32,256]{2,1,0:T(8,128)(2,1)S(1)} %get-tuple-element.26), channel_id=1, source_target_pairs={{0,24},{4,28},{8,16},{12,20},{16,8},{20,12},{24,0},{28,4},{1,25},{... | collective-permute-start | bytes 393224 | tf_op jit(solution)/shard_map/ppermute | solution.py:257
  49.7 8.6 %collective-permute-start.6 = (bf16[8,32,256]{2,1,0:T(8,128)(2,1)S(1)}, bf16[8,32,256]{2,1,0:T(8,128)(2,1)S(1)}, u32[]{:S(2)}, u32[]{:S(2)}) collective-permute-start(bf16[8,32,256]{2,1,0:T(8,128)(2,1)S(1)} %get-tuple-element.27), channel_id=1, source_target_pairs={{0,28},{4,24},{8,20},{12,16},{16,12},{20,8},{24,4},{28,0},{1,29},{... | collective-permute-start | bytes 393224 | tf_op jit(solution)/shard_map/ppermute | solution.py:257
  59.2 3.7 %collective-permute-start.16 = (f32[64,128]{1,0:T(8,128)S(1)}, f32[64,128]{1,0:T(8,128)S(1)}, u32[]{:S(2)}, u32[]{:S(2)}) collective-permute-start(f32[64,128]{1,0:T(8,128)S(1)} %gram_partial.3), channel_id=1, source_target_pairs={{0,3},{1,2},{2,1},{3,0},{4,7},{5,6},{6,5},{7,4},{8,11},{9,10},{10,... | collective-permute-start | bytes 98312 | tf_op jit(solution)/shard_map/ppermute | solution.py:182
  59.3 4.0 %collective-permute-start.15 = (f32[64,128]{1,0:T(8,128)S(1)}, f32[64,128]{1,0:T(8,128)S(1)}, u32[]{:S(2)}, u32[]{:S(2)}) collective-permute-start(f32[64,128]{1,0:T(8,128)S(1)} %gram_partial.3), channel_id=1, source_target_pairs={{0,2},{1,3},{2,0},{3,1},{4,6},{5,7},{6,4},{7,5},{8,10},{9,11},{10,... | collective-permute-start | bytes 98312 | tf_op jit(solution)/shard_map/ppermute | solution.py:182
  60.9 2.5 %collective-permute-start.14 = (f32[64,128]{1,0:T(8,128)S(1)}, f32[64,128]{1,0:T(8,128)S(1)}, u32[]{:S(2)}, u32[]{:S(2)}) collective-permute-start(f32[64,128]{1,0:T(8,128)S(1)} %gram_partial.3), channel_id=1, source_target_pairs={{0,1},{1,0},{2,3},{3,2},{4,5},{5,4},{6,7},{7,6},{8,9},{9,8},{10,11... | collective-permute-start | bytes 98312 | tf_op jit(solution)/shard_map/ppermute | solution.py:182
  63.4 4.0 %collective-permute-start.17 = (f32[64,128]{1,0:T(8,128)S(1)}, f32[64,128]{1,0:T(8,128)S(1)}, u32[]{:S(2)}, u32[]{:S(2)}) collective-permute-start(f32[64,128]{1,0:T(8,128)S(1)} %add_add_fusion), channel_id=1, source_target_pairs={{0,4},{4,0},{8,12},{12,8},{16,20},{20,16},{24,28},{28,24},{1,5},{5... | collective-permute-start | bytes 98312 | tf_op jit(solution)/shard_map/ppermute | solution.py:182
  67.4 7.0 %collective-permute-start.20 = (f32[64,128]{1,0:T(8,128)S(1)}, f32[64,128]{1,0:T(8,128)S(1)}, u32[]{:S(2)}, u32[]{:S(2)}) collective-permute-start(f32[64,128]{1,0:T(8,128)S(1)} %add.15.refs_0_), channel_id=1, source_target_pairs={{0,24},{4,28},{8,16},{12,20},{16,8},{20,12},{24,0},{28,4},{1,25},{... | collective-permute-start | bytes 98312 | tf_op jit(solution)/shard_map/ppermute | solution.py:182
  70.5 5.6 %collective-permute-start.19 = (f32[64,128]{1,0:T(8,128)S(1)}, f32[64,128]{1,0:T(8,128)S(1)}, u32[]{:S(2)}, u32[]{:S(2)}) collective-permute-start(f32[64,128]{1,0:T(8,128)S(1)} %add.15.refs_0_), channel_id=1, source_target_pairs={{0,16},{4,20},{8,24},{12,28},{16,0},{20,4},{24,8},{28,12},{1,17},{... | collective-permute-start | bytes 98312 | tf_op jit(solution)/shard_map/ppermute | solution.py:182
  73.9 3.9 %collective-permute-start.18 = (f32[64,128]{1,0:T(8,128)S(1)}, f32[64,128]{1,0:T(8,128)S(1)}, u32[]{:S(2)}, u32[]{:S(2)}) collective-permute-start(f32[64,128]{1,0:T(8,128)S(1)} %add.15.refs_0_), channel_id=1, source_target_pairs={{0,8},{4,12},{8,0},{12,4},{16,24},{20,28},{24,16},{28,20},{1,9},{5... | collective-permute-start | bytes 98312 | tf_op jit(solution)/shard_map/ppermute | solution.py:182

commit v6 on v5

v6 whole, which is shorter than its diff:
```python
import functools

import jax
import jax.numpy as jnp
from jax import lax
from jax.experimental import pallas as pl
from jax.experimental.pallas import tpu as pltpu
from jax.sharding import PartitionSpec as P

SIDE = 16
LANES = 128
CHUNK = 16
VMEM_LIMIT = 24 * 2**20
JAC_VMEM_LIMIT = 60 * 2**20
shift_ratio = 0.1
F32 = jnp.float32
BF16 = jnp.bfloat16


def iota(shape, dim):
    return lax.broadcasted_iota(jnp.int32, shape, dim)


def jac_kernel(far, act_hbm, cot_hbm, *refs):
    *out_refs, act_buf, cot_buf, held, sems = refs
    samples, mats = act_buf.shape[:2]
    width = act_buf.shape[3]
    near = lax.axis_size("samp") // 2
    share = width // near
    me = lax.axis_index("samp")
    half = 1 - me // near if far else me // near
    columns = pl.ds(pl.multiple_of(half * width, width), width)
    copies = []
    for s in range(samples):
        copies.append(
            (
                pltpu.make_async_copy(act_hbm.at[s, :, :, columns], act_buf.at[s], sems.at[0, s]),
                pltpu.make_async_copy(cot_hbm.at[s], cot_buf.at[s], sems.at[1, s]),
            )
        )
    for pair in copies:
        for copy in pair:
            copy.start()
    group = 2
    for first in range(0, samples, group):
        for s in range(first, first + group):
            for copy in copies[s]:
                copy.wait()
        for s in range(first, first + group):
            for m in range(mats):
                held[s, m] = lax.dot_general(
                    act_buf[s, m],
                    cot_buf[s, m],
                    (((0,), (0,)), ((), ())),
                    preferred_element_type=F32,
                )
    for k in range(near):
        owner = (me ^ k) % near if far else k
        owned = pl.ds(owner * share, share)
        for s in range(samples):
            rows = jnp.concatenate([held[s, m, owned] for m in range(mats)], axis=0).astype(BF16)
            if far:
                out_refs[k][s] = rows
            else:
                out_refs[0][k, s] = rows


def jac_rows(activations, cotangents, owners, far):
    samples, mats, sites, d = activations.shape
    near = owners // 2
    rows = mats * d // owners
    hbm = pl.BlockSpec(memory_space=pltpu.HBM)
    if far:
        out_shape = [jax.ShapeDtypeStruct((samples, rows, d), BF16)] * near
    else:
        out_shape = [jax.ShapeDtypeStruct((near, samples, rows, d), BF16)]
    return pl.pallas_call(
        functools.partial(jac_kernel, far),
        in_specs=[hbm, hbm],
        out_shape=out_shape,
        scratch_shapes=[
            pltpu.VMEM((samples, mats, sites, d // 2), BF16),
            pltpu.VMEM((samples, mats, sites, d), BF16),
            pltpu.VMEM((samples, mats, d // 2, d), F32),
            pltpu.SemaphoreType.DMA((2, samples)),
        ],
        compiler_params=pltpu.CompilerParams(vmem_limit_bytes=JAC_VMEM_LIMIT),
        cost_estimate=pl.CostEstimate(
            flops=samples * mats * sites * d * d,
            bytes_accessed=4 * samples * mats * sites * d,
            transcendentals=0,
        ),
        name="jac_rows",
    )(activations, cotangents)


def energy_kernel(spins_ref, offdiag_ref, out_ref):
    total, width = out_ref.shape
    local = spins_ref.shape[0]
    sites = SIDE * SIDE
    z = (2 * spins_ref[...] - 1).astype(F32)
    column = iota((local, sites), 1) % SIDE
    right = jnp.where(
        column == SIDE - 1, pltpu.roll(z, SIDE - 1, 1), pltpu.roll(z, sites - 1, 1)
    )
    below = pltpu.roll(z, sites - SIDE, 1)
    energy = offdiag_ref[...] + jnp.sum(z * (right + below), axis=1, keepdims=True)
    first = lax.axis_index("samp") * local
    mine = lax.axis_index("layer") == 0
    spread = jnp.concatenate([energy] * (total // local), axis=0)
    row = iota((total, width), 0)
    here = (row >= first) & (row < first + local) & (iota((total, width), 1) == total) & mine
    out_ref[...] = jnp.where(here, spread, F32(0.0))


def energy_column(spins, offdiag, total, width):
    return pl.pallas_call(
        energy_kernel,
        out_shape=jax.ShapeDtypeStruct((total, width), F32),
        compiler_params=pltpu.CompilerParams(vmem_limit_bytes=VMEM_LIMIT),
        name="energy_column",
    )(spins, offdiag[:, None])


def gram_kernel(*refs):
    near_ref, *far_refs, start_ref, out_ref, flat = refs
    near, local, count, d = near_ref.shape
    total = 2 * near * local
    joined = CHUNK // local
    me = lax.axis_index("samp")
    block = CHUNK * CHUNK
    dest = iota((block, block), 0)
    place = dest % CHUNK
    column = iota((block, block), 1)

    def turn(order):
        sample = (place // local ^ order) * local + place % local
        return (column == sample * CHUNK + dest // CHUNK).astype(F32).astype(BF16)

    turns = (turn(0), turn(me % joined))
    for row in range(0, count, CHUNK):
        here = slice(row, row + CHUNK)
        for j in range(near // joined):
            ks = range(j * joined, (j + 1) * joined)
            spots = ((me // near) * (near // joined) + j, me // joined ^ (near // joined + j))
            pieces = ([near_ref[k, :, here] for k in ks], [far_refs[k][:, here] for k in ks])
            for spot, piece, swap in zip(spots, pieces, turns):
                piece = jnp.concatenate(piece, axis=0).reshape(block, d)
                turned = jnp.dot(swap, piece, preferred_element_type=F32).astype(BF16)
                rows = pl.ds(pl.multiple_of(spot * CHUNK, CHUNK), CHUNK)
                for r in range(CHUNK):
                    flat[row + r, rows] = turned[r * CHUNK : (r + 1) * CHUNK]
    lined = jnp.concatenate([flat[r] for r in range(count)], axis=1)
    gram = lax.dot_general(lined, lined, (((1,), (1,)), ((), ())), preferred_element_type=F32)
    out_ref[...] = start_ref[...]
    out_ref[:, :total] += gram


def gram_partial(near, far, start):
    _, local, count, d = near.shape
    total, width = start.shape
    return pl.pallas_call(
        gram_kernel,
        out_shape=jax.ShapeDtypeStruct((total, width), F32),
        scratch_shapes=[pltpu.VMEM((count, total, d), BF16)],
        compiler_params=pltpu.CompilerParams(vmem_limit_bytes=VMEM_LIMIT),
        cost_estimate=pl.CostEstimate(
            flops=2 * total * total * count * d,
            bytes_accessed=2 * total * count * d,
            transcendentals=0,
        ),
        name="gram_partial",
    )(near, *far, start)


def eliminate(matrix, total):
    row = iota(matrix.shape, 0)
    lane = iota(matrix.shape, 1)
    if total <= 64:
        for k in range(total):
            column = matrix[:, k : k + 1]
            pivot_row = matrix[k : k + 1, :]
            scaled = pivot_row * (F32(1.0) / pivot_row[:, k : k + 1])
            matrix = matrix - jnp.where(row == k, F32(0.0), column) * scaled
    else:

        def one(k, held):
            column = jnp.sum(jnp.where(lane == k, held, F32(0.0)), axis=1, keepdims=True)
            pivot_row = jnp.sum(jnp.where(row == k, held, F32(0.0)), axis=0, keepdims=True)
            here = lane[:1] == k
            pivot = jnp.sum(jnp.where(here, pivot_row, F32(0.0)), axis=1, keepdims=True)
            scaled = pivot_row * (F32(1.0) / pivot)
            return held - jnp.where(row == k, F32(0.0), column) * scaled

        matrix = lax.fori_loop(0, total, one, matrix)
    diag = jnp.sum(jnp.where(row == lane, matrix, F32(0.0)), axis=1, keepdims=True)
    return matrix[:, total : total + 1] / diag


def tree_sum(parts):
    while len(parts) > 1:
        parts = [a + b for a, b in zip(parts[::2], parts[1::2])]
    return parts[0]


def partners(value, axis, first, count):
    size = lax.axis_size(axis)
    parts = [value]
    for k in range(1, count):
        perm = [(i, i ^ (k * first)) for i in range(size)]
        parts.append(lax.ppermute(value, axis, perm))
    return parts


def spread(held, owner, local):
    return held[pl.ds(pl.multiple_of(owner * local, local), local)]


def solve_kernel(grams, *refs):
    gram_refs, refs = refs[:grams], refs[grams:]
    near_ref, *far_refs, weights_ref, update_ref, held = refs
    mats, share, d = update_ref.shape
    near, local = near_ref.shape[:2]
    total, width = gram_refs[0].shape
    raw = tree_sum([ref[...] for ref in gram_refs])
    row = iota((total, width), 0)
    lane = iota((total, width), 1)
    inside = lane < total
    scale = F32(1.0 / total)
    row_mean = jnp.sum(jnp.where(inside, raw, F32(0.0)), axis=1, keepdims=True) * scale
    col_mean = jnp.sum(raw, axis=0, keepdims=True) * scale
    mean = jnp.sum(row_mean, axis=0, keepdims=True) * scale
    gram = (raw - col_mean - row_mean + mean) * scale
    eps = (raw - col_mean) * F32(1.0 / total**0.5)
    on_diag = row == lane
    trace = jnp.sum(
        jnp.sum(jnp.where(on_diag, gram, F32(0.0)), axis=1, keepdims=True), axis=0, keepdims=True
    )
    shift = F32(shift_ratio) * trace * scale
    system = jnp.where(inside, gram + jnp.where(on_diag, shift, F32(0.0)), eps)
    weights = eliminate(system, total)
    me = lax.axis_index("samp")
    own = jnp.where(row - me * local == lane, weights, F32(0.0))
    weights_ref[...] = jnp.sum(own, axis=0, keepdims=True)[:, :local]
    coeffs = weights - jnp.sum(weights, axis=0, keepdims=True) * scale
    held[...] = jnp.broadcast_to(coeffs, (total, d))
    acc = jnp.zeros((mats * share, d), F32)
    for k in range(near):
        mine = spread(held, (me // near) * near + k, local)
        for s in range(local):
            acc = acc + mine[s : s + 1] * near_ref[k, s].astype(F32)
    for k, far_ref in enumerate(far_refs):
        mine = spread(held, me ^ (near + k), local)
        for s in range(local):
            acc = acc + mine[s : s + 1] * far_ref[s].astype(F32)
    for m in range(mats):
        update_ref[m] = acc[m * share : (m + 1) * share]


def solve_and_project(grams, near, far, mats):
    total, width = grams[0].shape
    _, local, count, d = near.shape
    return pl.pallas_call(
        functools.partial(solve_kernel, len(grams)),
        out_shape=(
            jax.ShapeDtypeStruct((1, local), F32),
            jax.ShapeDtypeStruct((mats, count // mats, d), F32),
        ),
        scratch_shapes=[pltpu.VMEM((total, d), F32)],
        compiler_params=pltpu.CompilerParams(vmem_limit_bytes=VMEM_LIMIT),
        name="solve_and_project",
    )(*grams, near, *far)


def body(spins, activations, cotangents, offdiag):
    local, mats = activations.shape[:2]
    owners = lax.axis_size("samp")
    near = owners // 2
    total = local * owners
    width = (total // LANES + 1) * LANES
    far_jac = jac_rows(activations, cotangents, owners, True)
    far = [
        lax.ppermute(block, "samp", [(i, i ^ (near + k)) for i in range(owners)])
        for k, block in enumerate(far_jac)
    ]
    near_jac = jac_rows(activations, cotangents, owners, False)[0]
    halves = [list(range(near)), list(range(near, owners))]
    near_rows = lax.all_to_all(
        near_jac, "samp", split_axis=0, concat_axis=0, tiled=True, axis_index_groups=halves
    )
    start = energy_column(spins, offdiag, total, width)
    partial = gram_partial(near_rows, far, start)
    grams = partners(partial, "layer", 1, lax.axis_size("layer"))
    first = 1
    while first < owners:
        count = 2 if first == 1 else min(4, owners // first)
        grams = partners(tree_sum(grams), "samp", first, count)
        first *= count
    weights, update = solve_and_project(grams, near_rows, far, mats)
    return weights.reshape(local), update


def solution(mesh):
    placed = (
        P("samp", None),
        P("samp", "layer", None, None),
        P("samp", "layer", None, None),
        P("samp"),
    )
    return jax.shard_map(
        body,
        mesh=mesh,
        in_specs=placed,
        out_specs=(P("samp"), P("layer", "samp", None)),
        check_vma=False,
    )
```

time: 84.9 us -> 88 us (1.037)
  waiting for transfers between devices: 20.4 us -> 42.6 us
  starting transfers between devices: 41.8 us -> 29 us
  Pallas kernels: 18.6 us -> 15.4 us
  local copies, waits for them, and re-layouts: 3.26 us -> 0.09 us
    ppermute x14 -> x4, starting transfers between devices: 31.6 us -> 7.93 us  [body(): lax.ppermute(block, 'samp', [(i, i ^ near + k) for i in range(owners)])]
    ppermute x14 -> x4, waiting for transfers between devices: 12 us -> 31.7 us  [body(): lax.ppermute(block, 'samp', [(i, i ^ near + k) for i in range(owners)])]
    ppermute x7, starting transfers between devices: 10.1 us -> 15.8 us  [partners(): parts.append(lax.ppermute(value, axis, perm))]
    all_to_all x0 -> x1, starting transfers between devices: none -> 5.26 us  [body(): lax.all_to_all(near_jac, 'samp', split_axis=0, concat_axis=0, tiled=True,...]
    unnamed x8 -> x4, local copies, waits for them, and re-layouts: 3.18 us -> 0.01 us
    pallas_call x3, Pallas kernels: 16.6 us -> 13.7 us  [the longest x2 6.89 us: jac_rows(): pl.pallas_call(functools.partial(jac_kernel, far), in_specs=[hbm, hbm], o...]
    ppermute x7, waiting for transfers between devices: 8.42 us -> 10.9 us  [partners(): parts.append(lax.ppermute(value, axis, perm))]
    pallas_call x2 -> x1, Pallas kernels: 1.78 us -> 1.46 us  [gram_partial(): pl.pallas_call(gram_kernel, out_shape=jax.ShapeDtypeStruct((total, width)...]
  transfers between devices with their start and end apart: 21 -> 12, of which waited for: 8 -> 7; matrix products, arithmetic and copies ran while one was open for 0% -> 0% of each run, Pallas kernels for 7% -> 4%
where the time goes in v6:
time: 88 us; the launch traced here: 87.8 us
  waiting for transfers between devices  42.6 us (48%)
  starting transfers between devices  29 us (33%)
  Pallas kernels  15.4 us (18%)
    ppermute x4, waiting for transfers between devices, body(): lax.ppermute(block, 'samp', [(i, i ^ near + k) for i in range(owners)])  31.7 us
    ppermute x7, starting transfers between devices, partners(): parts.append(lax.ppermute(value, axis, perm))  15.8 us
    ppermute x7, waiting for transfers between devices, partners(): parts.append(lax.ppermute(value, axis, perm))  10.9 us
    ppermute x4, starting transfers between devices, body(): lax.ppermute(block, 'samp', [(i, i ^ near + k) for i in range(owners)])  7.93 us
    pallas_call x2, Pallas kernels, jac_rows(): pl.pallas_call(functools.partial(jac_kernel, far), in_specs=[hbm, hbm], o...  6.89 us
    pallas_call x1, Pallas kernels, solve_and_project(): pl.pallas_call(functools.partial(solve_kernel, len(grams)), out_shape=(ja...  6.8 us
    all_to_all x1, starting transfers between devices, body(): lax.all_to_all(near_jac, 'samp', split_axis=0, concat_axis=0, tiled=True,...  5.26 us
  transfers between devices with their start and end apart: 12, of which 7 were waited for; matrix products, arithmetic and copies ran while one was open for 0% of the time, Pallas kernels for 4%

profile of v6, /device:TPU:0, one launch (start us, length us, event | category | flops | bytes accessed | tf_op | source)
XLA Modules:
  0.0 87.8 jit_solution(13009636323809411219)
XLA Ops:
  0.6 3.4 %jac_rows.2 = bf16[4,8,64,256]{3,2,1,0:T(8,128)(2,1)} custom-call(bf16[8,2,256,256]{3,2,1,0:T(8,128)(2,1)} %act_hbm.3, bf16[8,2,256,256]{3,2,1,0:T(8,128)(2,1)} %cot_hbm.3), custom_call_target="tpu_custom_call" | custom-call | flops 268435456 | bytes 4194304 | tf_op jit(solution)/shard_map/jac_rows/pallas_call | solution.py:77
  4.0 5.3 %all-to-all-start = ((bf16[4,8,64,256]{3,2,1,0:T(8,128)(2,1)}), bf16[4,8,64,256]{3,2,1,0:T(8,128)(2,1)S(1)}, u32[]{:S(2)}, u32[]{:S(2)}) async-start(bf16[4,8,64,256]{3,2,1,0:T(8,128)(2,1)} %jac_rows.2), calls=%async_computation | async-start | bytes 2097152 | tf_op jit(solution)/shard_map/all_to_all | solution.py:288
  9.3 0.0 copy-start.1
  9.3 0.0 copy-start
  9.3 3.5 %jac_rows.3 = (bf16[8,64,256]{2,1,0:T(8,128)(2,1)}, bf16[8,64,256]{2,1,0:T(8,128)(2,1)}, bf16[8,64,256]{2,1,0:T(8,128)(2,1)}, bf16[8,64,256]{2,1,0:T(8,128)(2,1)}) custom-call(bf16[8,2,256,256]{3,2,1,0:T(8,128)(2,1)} %act_hbm.3, bf16[8,2,256,256]{3,2,1,0:T(8,128)(2,1)} %cot_hbm.3), custom_call_target="tpu_custom_call" | custom-call | flops 268435456 | bytes 4194304 | tf_op jit(solution)/shard_map/jac_rows/pallas_call | solution.py:77
  12.8 2.7 %collective-permute-start = (bf16[8,64,256]{2,1,0:T(8,128)(2,1)}, bf16[8,64,256]{2,1,0:T(8,128)(2,1)S(1)}, u32[]{:S(2)}, u32[]{:S(2)}) collective-permute-start(bf16[8,64,256]{2,1,0:T(8,128)(2,1)} %get-tuple-element.8), channel_id=1, source_target_pairs={{0,16},{4,20},{8,24},{12,28},{16,0},{20,4},{24,8},{28,12},{1,17},{... | collective-permute-start | bytes 786440 | tf_op jit(solution)/shard_map/ppermute | solution.py:283
  15.4 1.8 %collective-permute-start.1 = (bf16[8,64,256]{2,1,0:T(8,128)(2,1)}, bf16[8,64,256]{2,1,0:T(8,128)(2,1)S(1)}, u32[]{:S(2)}, u32[]{:S(2)}) collective-permute-start(bf16[8,64,256]{2,1,0:T(8,128)(2,1)} %get-tuple-element.9), channel_id=1, source_target_pairs={{0,20},{4,16},{8,28},{12,24},{16,4},{20,0},{24,12},{28,8},{1,21},{... | collective-permute-start | bytes 786440 | tf_op jit(solution)/shard_map/ppermute | solution.py:283
  17.2 3.5 %collective-permute-start.2 = (bf16[8,64,256]{2,1,0:T(8,128)(2,1)}, bf16[8,64,256]{2,1,0:T(8,128)(2,1)S(1)}, u32[]{:S(2)}, u32[]{:S(2)}) collective-permute-start(bf16[8,64,256]{2,1,0:T(8,128)(2,1)} %get-tuple-element.10), channel_id=1, source_target_pairs={{0,24},{4,28},{8,16},{12,20},{16,8},{20,12},{24,0},{28,4},{1,25},{... | collective-permute-start | bytes 786440 | tf_op jit(solution)/shard_map/ppermute | solution.py:283
  20.7 0.0 collective-permute-start.3
  20.7 0.0 copy-done.1
  20.7 0.1 copy.6.offdiag_ref
  20.8 0.0 copy-done
  20.8 0.2 energy_column.1.refs_5_
  21.0 6.6 %collective-permute-done.refs_1_.refs_5_ = bf16[8,64,256]{2,1,0:T(8,128)(2,1)S(1)} collective-permute-done((bf16[8,64,256]{2,1,0:T(8,128)(2,1)}, bf16[8,64,256]{2,1,0:T(8,128)(2,1)S(1)}, u32[]{:S(2)}, u32[]{:S(2)}) %collective-permute-start) | collective-permute-done | bytes 262176 | tf_op jit(solution)/shard_map/ppermute | solution.py:283
  27.7 25.1 %collective-permute-done.1.refs_2_.refs_6_ = bf16[8,64,256]{2,1,0:T(8,128)(2,1)S(1)} collective-permute-done((bf16[8,64,256]{2,1,0:T(8,128)(2,1)}, bf16[8,64,256]{2,1,0:T(8,128)(2,1)S(1)}, u32[]{:S(2)}, u32[]{:S(2)}) %collective-permute-start.1) | collective-permute-done | bytes 262176 | tf_op jit(solution)/shard_map/ppermute | solution.py:283
  52.8 0.0 collective-permute-done.2.refs_3_.refs_7_
  52.8 0.0 collective-permute-done.3.refs_4_.refs_8_
  52.8 0.0 all-to-all-done.refs_0_.refs_4_
  52.8 1.5 %gram_partial.1 = f32[64,128]{1,0:T(8,128)S(1)} custom-call(bf16[4,8,64,256]{3,2,1,0:T(8,128)(2,1)S(1)} %all-to-all-done.refs_0_.refs_4_, bf16[8,64,256]{2,1,0:T(8,128)(2,1)S(1)} %collective-permute-done.refs_1_.refs_5_, bf16[8,64,256]{2,1,0:T(8,128)(2,1)S(1)} %collective-permute-done.1.refs_2_.refs_6_, ...), custom_call_target="tpu_custom_call" | custom-call | flops 134217728 | bytes 2097152 | tf_op jit(solution)/shard_map/gram_partial/pallas_call | solution.py:162
  54.2 1.6 %collective-permute-start.5 = (f32[64,128]{1,0:T(8,128)S(1)}, f32[64,128]{1,0:T(8,128)S(1)}, u32[]{:S(2)}, u32[]{:S(2)}) collective-permute-start(f32[64,128]{1,0:T(8,128)S(1)} %gram_partial.1), channel_id=1, source_target_pairs={{0,2},{1,3},{2,0},{3,1},{4,6},{5,7},{6,4},{7,5},{8,10},{9,11},{10,... | collective-permute-start | bytes 98312 | tf_op jit(solution)/shard_map/ppermute | solution.py:211
  55.8 0.0 collective-permute-start.6
  55.8 0.6 collective-permute-start.4
  56.4 1.8 %collective-permute-done.5 = f32[64,128]{1,0:T(8,128)S(1)} collective-permute-done((f32[64,128]{1,0:T(8,128)S(1)}, f32[64,128]{1,0:T(8,128)S(1)}, u32[]{:S(2)}, u32[]{:S(2)}) %collective-permute-start.5) | collective-permute-done | bytes 32800 | tf_op jit(solution)/shard_map/ppermute | solution.py:211
  58.2 0.9 %collective-permute-done.6 = f32[64,128]{1,0:T(8,128)S(1)} collective-permute-done((f32[64,128]{1,0:T(8,128)S(1)}, f32[64,128]{1,0:T(8,128)S(1)}, u32[]{:S(2)}, u32[]{:S(2)}) %collective-permute-start.6) | collective-permute-done | bytes 32800 | tf_op jit(solution)/shard_map/ppermute | solution.py:211
  59.1 0.0 collective-permute-done.4
  59.2 0.1 collective-permute-start.7
  59.2 3.9 %collective-permute-done.7 = f32[64,128]{1,0:T(8,128)S(1)} collective-permute-done((f32[64,128]{1,0:T(8,128)S(1)}, f32[64,128]{1,0:T(8,128)S(1)}, u32[]{:S(2)}, u32[]{:S(2)}) %collective-permute-start.7) | collective-permute-done | bytes 32800 | tf_op jit(solution)/shard_map/ppermute | solution.py:211
  63.1 10.1 %collective-permute-start.8 = (f32[64,128]{1,0:T(8,128)S(1)}, f32[64,128]{1,0:T(8,128)S(1)}, u32[]{:S(2)}, u32[]{:S(2)}) collective-permute-start(f32[64,128]{1,0:T(8,128)S(1)} %add.15.refs_0_), channel_id=1, source_target_pairs={{0,8},{4,12},{8,0},{12,4},{16,24},{20,28},{24,16},{28,20},{1,9},{5... | collective-permute-start | bytes 98312 | tf_op jit(solution)/shard_map/ppermute | solution.py:211
  73.2 2.1 %collective-permute-start.9 = (f32[64,128]{1,0:T(8,128)S(1)}, f32[64,128]{1,0:T(8,128)S(1)}, u32[]{:S(2)}, u32[]{:S(2)}) collective-permute-start(f32[64,128]{1,0:T(8,128)S(1)} %add.15.refs_0_), channel_id=1, source_target_pairs={{0,16},{4,20},{8,24},{12,28},{16,0},{20,4},{24,8},{28,12},{1,17},{... | collective-permute-start | bytes 98312 | tf_op jit(solution)/shard_map/ppermute | solution.py:211
  75.3 1.4 %collective-permute-start.10 = (f32[64,128]{1,0:T(8,128)S(1)}, f32[64,128]{1,0:T(8,128)S(1)}, u32[]{:S(2)}, u32[]{:S(2)}) collective-permute-start(f32[64,128]{1,0:T(8,128)S(1)} %add.15.refs_0_), channel_id=1, source_target_pairs={{0,24},{4,28},{8,16},{12,20},{16,8},{20,12},{24,0},{28,4},{1,25},{... | collective-permute-start | bytes 98312 | tf_op jit(solution)/shard_map/ppermute | solution.py:211
  76.7 0.0 collective-permute-done.8.refs_1_
  76.7 1.5 %collective-permute-done.9.refs_2_ = f32[64,128]{1,0:T(8,128)S(1)} collective-permute-done((f32[64,128]{1,0:T(8,128)S(1)}, f32[64,128]{1,0:T(8,128)S(1)}, u32[]{:S(2)}, u32[]{:S(2)}) %collective-permute-start.9) | collective-permute-done | bytes 32800 | tf_op jit(solution)/shard_map/ppermute | solution.py:211
  78.2 2.8 %collective-permute-done.10.refs_3_ = f32[64,128]{1,0:T(8,128)S(1)} collective-permute-done((f32[64,128]{1,0:T(8,128)S(1)}, f32[64,128]{1,0:T(8,128)S(1)}, u32[]{:S(2)}, u32[]{:S(2)}) %collective-permute-start.10) | collective-permute-done | bytes 32800 | tf_op jit(solution)/shard_map/ppermute | solution.py:211
  81.0 6.8 %solve_and_project.1 = (f32[1,8]{1,0:T(1,128)}, f32[2,32,256]{2,1,0:T(8,128)}) custom-call(f32[64,128]{1,0:T(8,128)S(1)} %add.15.refs_0_, f32[64,128]{1,0:T(8,128)S(1)} %collective-permute-done.8.refs_1_, f32[64,128]{1,0:T(8,128)S(1)} %collective-permute-done.9.refs_2_, f32[64,128]{1,0:T(8,128)S(1)} %collective-permute-done.10.refs_3_, ...), custom_call_target="tpu_custom_call" | custom-call | tf_op jit(solution)/shard_map/solve_and_project/pallas_call | solution.py:263
  (2 shorter events, 0.0 us)
Async XLA Ops:
  4.0 48.7 %all-to-all-start = ((bf16[4,8,64,256]{3,2,1,0:T(8,128)(2,1)}), bf16[4,8,64,256]{3,2,1,0:T(8,128)(2,1)S(1)}, u32[]{:S(2)}, u32[]{:S(2)}) async-start(bf16[4,8,64,256]{3,2,1,0:T(8,128)(2,1)} %jac_rows.2), calls=%async_computation | async-start | bytes 2097152 | tf_op jit(solution)/shard_map/all_to_all | solution.py:288
  9.3 11.4 %copy-start.1 = (f32[8]{0:T(128)S(1)}, f32[8]{0:T(128)}, u32[]{:S(2)}) copy-start(f32[8]{0:T(128)} %param.7) | copy-start | bytes 100
  9.3 11.5 %copy-start = (s32[8,256]{1,0:T(8,128)S(1)}, s32[8,256]{1,0:T(8,128)}, u32[]{:S(2)}) copy-start(s32[8,256]{1,0:T(8,128)} %spins_ref.1) | copy-start | bytes 24580
  12.8 14.9 %collective-permute-start = (bf16[8,64,256]{2,1,0:T(8,128)(2,1)}, bf16[8,64,256]{2,1,0:T(8,128)(2,1)S(1)}, u32[]{:S(2)}, u32[]{:S(2)}) collective-permute-start(bf16[8,64,256]{2,1,0:T(8,128)(2,1)} %get-tuple-element.8), channel_id=1, source_target_pairs={{0,16},{4,20},{8,24},{12,28},{16,0},{20,4},{24,8},{28,12},{1,17},{... | collective-permute-start | bytes 786440 | tf_op jit(solution)/shard_map/ppermute | solution.py:283
  15.4 37.3 %collective-permute-start.1 = (bf16[8,64,256]{2,1,0:T(8,128)(2,1)}, bf16[8,64,256]{2,1,0:T(8,128)(2,1)S(1)}, u32[]{:S(2)}, u32[]{:S(2)}) collective-permute-start(bf16[8,64,256]{2,1,0:T(8,128)(2,1)} %get-tuple-element.9), channel_id=1, source_target_pairs={{0,20},{4,16},{8,28},{12,24},{16,4},{20,0},{24,12},{28,8},{1,21},{... | collective-permute-start | bytes 786440 | tf_op jit(solution)/shard_map/ppermute | solution.py:283
  17.2 35.5 %collective-permute-start.2 = (bf16[8,64,256]{2,1,0:T(8,128)(2,1)}, bf16[8,64,256]{2,1,0:T(8,128)(2,1)S(1)}, u32[]{:S(2)}, u32[]{:S(2)}) collective-permute-start(bf16[8,64,256]{2,1,0:T(8,128)(2,1)} %get-tuple-element.10), channel_id=1, source_target_pairs={{0,24},{4,28},{8,16},{12,20},{16,8},{20,12},{24,0},{28,4},{1,25},{... | collective-permute-start | bytes 786440 | tf_op jit(solution)/shard_map/ppermute | solution.py:283
  20.7 32.0 %collective-permute-start.3 = (bf16[8,64,256]{2,1,0:T(8,128)(2,1)}, bf16[8,64,256]{2,1,0:T(8,128)(2,1)S(1)}, u32[]{:S(2)}, u32[]{:S(2)}) collective-permute-start(bf16[8,64,256]{2,1,0:T(8,128)(2,1)} %get-tuple-element.11), channel_id=1, source_target_pairs={{0,28},{4,24},{8,20},{12,16},{16,12},{20,8},{24,4},{28,0},{1,29},{... | collective-permute-start | bytes 786440 | tf_op jit(solution)/shard_map/ppermute | solution.py:283
  54.2 4.0 %collective-permute-start.5 = (f32[64,128]{1,0:T(8,128)S(1)}, f32[64,128]{1,0:T(8,128)S(1)}, u32[]{:S(2)}, u32[]{:S(2)}) collective-permute-start(f32[64,128]{1,0:T(8,128)S(1)} %gram_partial.1), channel_id=1, source_target_pairs={{0,2},{1,3},{2,0},{3,1},{4,6},{5,7},{6,4},{7,5},{8,10},{9,11},{10,... | collective-permute-start | bytes 98312 | tf_op jit(solution)/shard_map/ppermute | solution.py:211
  55.8 3.3 %collective-permute-start.6 = (f32[64,128]{1,0:T(8,128)S(1)}, f32[64,128]{1,0:T(8,128)S(1)}, u32[]{:S(2)}, u32[]{:S(2)}) collective-permute-start(f32[64,128]{1,0:T(8,128)S(1)} %gram_partial.1), channel_id=1, source_target_pairs={{0,3},{1,2},{2,1},{3,0},{4,7},{5,6},{6,5},{7,4},{8,11},{9,10},{10,... | collective-permute-start | bytes 98312 | tf_op jit(solution)/shard_map/ppermute | solution.py:211
  55.8 3.3 %collective-permute-start.4 = (f32[64,128]{1,0:T(8,128)S(1)}, f32[64,128]{1,0:T(8,128)S(1)}, u32[]{:S(2)}, u32[]{:S(2)}) collective-permute-start(f32[64,128]{1,0:T(8,128)S(1)} %gram_partial.1), channel_id=1, source_target_pairs={{0,1},{1,0},{2,3},{3,2},{4,5},{5,4},{6,7},{7,6},{8,9},{9,8},{10,11... | collective-permute-start | bytes 98312 | tf_op jit(solution)/shard_map/ppermute | solution.py:211
  59.2 4.0 %collective-permute-start.7 = (f32[64,128]{1,0:T(8,128)S(1)}, f32[64,128]{1,0:T(8,128)S(1)}, u32[]{:S(2)}, u32[]{:S(2)}) collective-permute-start(f32[64,128]{1,0:T(8,128)S(1)} %add_add_fusion), channel_id=1, source_target_pairs={{0,4},{4,0},{8,12},{12,8},{16,20},{20,16},{24,28},{28,24},{1,5},{5... | collective-permute-start | bytes 98312 | tf_op jit(solution)/shard_map/ppermute | solution.py:211
  63.1 13.6 %collective-permute-start.8 = (f32[64,128]{1,0:T(8,128)S(1)}, f32[64,128]{1,0:T(8,128)S(1)}, u32[]{:S(2)}, u32[]{:S(2)}) collective-permute-start(f32[64,128]{1,0:T(8,128)S(1)} %add.15.refs_0_), channel_id=1, source_target_pairs={{0,8},{4,12},{8,0},{12,4},{16,24},{20,28},{24,16},{28,20},{1,9},{5... | collective-permute-start | bytes 98312 | tf_op jit(solution)/shard_map/ppermute | solution.py:211
  73.2 5.0 %collective-permute-start.9 = (f32[64,128]{1,0:T(8,128)S(1)}, f32[64,128]{1,0:T(8,128)S(1)}, u32[]{:S(2)}, u32[]{:S(2)}) collective-permute-start(f32[64,128]{1,0:T(8,128)S(1)} %add.15.refs_0_), channel_id=1, source_target_pairs={{0,16},{4,20},{8,24},{12,28},{16,0},{20,4},{24,8},{28,12},{1,17},{... | collective-permute-start | bytes 98312 | tf_op jit(solution)/shard_map/ppermute | solution.py:211
  75.3 5.7 %collective-permute-start.10 = (f32[64,128]{1,0:T(8,128)S(1)}, f32[64,128]{1,0:T(8,128)S(1)}, u32[]{:S(2)}, u32[]{:S(2)}) collective-permute-start(f32[64,128]{1,0:T(8,128)S(1)} %add.15.refs_0_), channel_id=1, source_target_pairs={{0,24},{4,28},{8,16},{12,20},{16,8},{20,12},{24,0},{28,4},{1,25},{... | collective-permute-start | bytes 98312 | tf_op jit(solution)/shard_map/ppermute | solution.py:211

commit v7 on v6

--- a/solution.py
+++ b/solution.py
@@ -21,8 +21,8 @@
     return lax.broadcasted_iota(jnp.int32, shape, dim)
 
 
-def jac_kernel(far, act_hbm, cot_hbm, *refs):
-    *out_refs, act_buf, cot_buf, held, sems = refs
+def jac_kernel(far, after, act_hbm, cot_hbm, *refs):
+    *out_refs, act_buf, cot_buf, held, sems = refs[after:]
     samples, mats = act_buf.shape[:2]
     width = act_buf.shape[3]
     near = lax.axis_size("samp") // 2
@@ -65,7 +65,7 @@
                 out_refs[0][k, s] = rows
 
 
-def jac_rows(activations, cotangents, owners, far):
+def jac_rows(activations, cotangents, owners, far, after=()):
     samples, mats, sites, d = activations.shape
     near = owners // 2
     rows = mats * d // owners
@@ -75,8 +75,8 @@
     else:
         out_shape = [jax.ShapeDtypeStruct((near, samples, rows, d), BF16)]
     return pl.pallas_call(
-        functools.partial(jac_kernel, far),
-        in_specs=[hbm, hbm],
+        functools.partial(jac_kernel, far, len(after)),
+        in_specs=[hbm] * (2 + len(after)),
         out_shape=out_shape,
         scratch_shapes=[
             pltpu.VMEM((samples, mats, sites, d // 2), BF16),
@@ -91,7 +91,7 @@
             transcendentals=0,
         ),
         name="jac_rows",
-    )(activations, cotangents)
+    )(activations, cotangents, *after)
 
 
 def energy_kernel(spins_ref, offdiag_ref, out_ref):
@@ -283,7 +283,7 @@
         lax.ppermute(block, "samp", [(i, i ^ (near + k)) for i in range(owners)])
         for k, block in enumerate(far_jac)
     ]
-    near_jac = jac_rows(activations, cotangents, owners, False)[0]
+    near_jac = jac_rows(activations, cotangents, owners, False, far_jac[:1])[0]
     halves = [list(range(near)), list(range(near, owners))]
     near_rows = lax.all_to_all(
         near_jac, "samp", split_axis=0, concat_axis=0, tiled=True, axis_index_groups=halves

time: 88 us -> 87.7 us (level)
  starting transfers between devices: 29 us -> 28 us
    ppermute x7, starting transfers between devices: 15.8 us -> 14.7 us  [partners(): parts.append(lax.ppermute(value, axis, perm))]
  transfers between devices with their start and end apart: 12 -> 12, of which waited for: 7 -> 7; matrix products, arithmetic and copies ran while one was open for 0% -> 0% of each run, Pallas kernels for 4% -> 0%
where the time goes in v7:
time: 87.7 us; the launch traced here: 87.5 us
  waiting for transfers between devices  43.2 us (49%)
  starting transfers between devices  28 us (32%)
  Pallas kernels  15.4 us (18%)
    ppermute x4, waiting for transfers between devices, body(): lax.ppermute(block, 'samp', [(i, i ^ near + k) for i in range(owners)])  31.4 us
    ppermute x7, starting transfers between devices, partners(): parts.append(lax.ppermute(value, axis, perm))  14.7 us
    ppermute x7, waiting for transfers between devices, partners(): parts.append(lax.ppermute(value, axis, perm))  11.7 us
    ppermute x4, starting transfers between devices, body(): lax.ppermute(block, 'samp', [(i, i ^ near + k) for i in range(owners)])  7.94 us
    pallas_call x2, Pallas kernels, jac_rows(): pl.pallas_call(functools.partial(jac_kernel, far, len(after)), in_specs=[...  6.91 us
    pallas_call x1, Pallas kernels, solve_and_project(): pl.pallas_call(functools.partial(solve_kernel, len(grams)), out_shape=(ja...  6.8 us
    all_to_all x1, starting transfers between devices, body(): lax.all_to_all(near_jac, 'samp', split_axis=0, concat_axis=0, tiled=True,...  5.39 us
  transfers between devices with their start and end apart: 12, of which 7 were waited for; matrix products, arithmetic and copies ran while one was open for 0% of the time, Pallas kernels for 0%

profile of v7, /device:TPU:0, one launch (start us, length us, event | category | flops | bytes accessed | tf_op | source)
XLA Modules:
  0.0 87.5 jit_solution(3213745603555507424)
XLA Ops:
  0.6 3.5 %jac_rows.2 = (bf16[8,64,256]{2,1,0:T(8,128)(2,1)}, bf16[8,64,256]{2,1,0:T(8,128)(2,1)}, bf16[8,64,256]{2,1,0:T(8,128)(2,1)}, bf16[8,64,256]{2,1,0:T(8,128)(2,1)}) custom-call(bf16[8,2,256,256]{3,2,1,0:T(8,128)(2,1)} %act_hbm.3, bf16[8,2,256,256]{3,2,1,0:T(8,128)(2,1)} %cot_hbm.3), custom_call_target="tpu_custom_call" | custom-call | flops 268435456 | bytes 4194304 | tf_op jit(solution)/shard_map/jac_rows/pallas_call | solution.py:77
  4.1 0.0 copy-start.1
  4.1 3.5 %jac_rows.3 = bf16[4,8,64,256]{3,2,1,0:T(8,128)(2,1)} custom-call(bf16[8,2,256,256]{3,2,1,0:T(8,128)(2,1)} %act_hbm.3, bf16[8,2,256,256]{3,2,1,0:T(8,128)(2,1)} %cot_hbm.3, bf16[8,64,256]{2,1,0:T(8,128)(2,1)} %get-tuple-element.8.refs_0_), custom_call_target="tpu_custom_call" | custom-call | flops 268435456 | bytes 4194304 | tf_op jit(solution)/shard_map/jac_rows/pallas_call | solution.py:77
  7.6 0.0 copy-start.5
  7.6 0.0 copy-start.4
  7.6 0.0 copy-start.3
  7.6 0.0 copy-start.2
  7.6 0.0 copy-start
  7.6 5.4 %all-to-all-start = ((bf16[4,8,64,256]{3,2,1,0:T(8,128)(2,1)}), bf16[4,8,64,256]{3,2,1,0:T(8,128)(2,1)S(1)}, u32[]{:S(2)}, u32[]{:S(2)}) async-start(bf16[4,8,64,256]{3,2,1,0:T(8,128)(2,1)} %jac_rows.3), calls=%async_computation | async-start | bytes 2097152 | tf_op jit(solution)/shard_map/all_to_all | solution.py:288
  13.0 0.0 copy-done.1
  13.0 2.6 %collective-permute-start = (bf16[8,64,256]{2,1,0:T(8,128)(2,1)S(1)}, bf16[8,64,256]{2,1,0:T(8,128)(2,1)S(1)}, u32[]{:S(2)}, u32[]{:S(2)}) collective-permute-start(bf16[8,64,256]{2,1,0:T(8,128)(2,1)S(1)} %copy-done.1), channel_id=1, source_target_pairs={{0,16},{4,20},{8,24},{12,28},{16,0},{20,4},{24,8},{28,12},{1,17},{... | collective-permute-start | bytes 786440 | tf_op jit(solution)/shard_map/ppermute | solution.py:283
  15.6 0.0 copy-done.5
  15.6 1.8 %collective-permute-start.1 = (bf16[8,64,256]{2,1,0:T(8,128)(2,1)S(1)}, bf16[8,64,256]{2,1,0:T(8,128)(2,1)S(1)}, u32[]{:S(2)}, u32[]{:S(2)}) collective-permute-start(bf16[8,64,256]{2,1,0:T(8,128)(2,1)S(1)} %copy-done.5), channel_id=1, source_target_pairs={{0,20},{4,16},{8,28},{12,24},{16,4},{20,0},{24,12},{28,8},{1,21},{... | collective-permute-start | bytes 786440 | tf_op jit(solution)/shard_map/ppermute | solution.py:283
  17.4 0.0 copy-done.4
  17.4 3.5 %collective-permute-start.2 = (bf16[8,64,256]{2,1,0:T(8,128)(2,1)S(1)}, bf16[8,64,256]{2,1,0:T(8,128)(2,1)S(1)}, u32[]{:S(2)}, u32[]{:S(2)}) collective-permute-start(bf16[8,64,256]{2,1,0:T(8,128)(2,1)S(1)} %copy-done.4), channel_id=1, source_target_pairs={{0,24},{4,28},{8,16},{12,20},{16,8},{20,12},{24,0},{28,4},{1,25},{... | collective-permute-start | bytes 786440 | tf_op jit(solution)/shard_map/ppermute | solution.py:283
  20.9 0.0 copy-done.3
  20.9 0.1 collective-permute-start.3
  21.0 0.0 copy-done.2
  21.0 0.1 copy.6.offdiag_ref
  21.1 0.0 copy-done
  21.1 0.2 energy_column.1.refs_5_
  21.3 10.0 %collective-permute-done.refs_1_.refs_5_ = bf16[8,64,256]{2,1,0:T(8,128)(2,1)S(1)} collective-permute-done((bf16[8,64,256]{2,1,0:T(8,128)(2,1)S(1)}, bf16[8,64,256]{2,1,0:T(8,128)(2,1)S(1)}, u32[]{:S(2)}, u32[]{:S(2)}) %collective-permute-start) | collective-permute-done | bytes 262176 | tf_op jit(solution)/shard_map/ppermute | solution.py:283
  31.3 21.4 %collective-permute-done.1.refs_2_.refs_6_ = bf16[8,64,256]{2,1,0:T(8,128)(2,1)S(1)} collective-permute-done((bf16[8,64,256]{2,1,0:T(8,128)(2,1)S(1)}, bf16[8,64,256]{2,1,0:T(8,128)(2,1)S(1)}, u32[]{:S(2)}, u32[]{:S(2)}) %collective-permute-start.1) | collective-permute-done | bytes 262176 | tf_op jit(solution)/shard_map/ppermute | solution.py:283
  52.7 0.0 collective-permute-done.2.refs_3_.refs_7_
  52.7 0.0 collective-permute-done.3.refs_4_.refs_8_
  52.7 0.0 all-to-all-done.refs_0_.refs_4_
  52.7 1.5 %gram_partial.1 = f32[64,128]{1,0:T(8,128)S(1)} custom-call(bf16[4,8,64,256]{3,2,1,0:T(8,128)(2,1)S(1)} %all-to-all-done.refs_0_.refs_4_, bf16[8,64,256]{2,1,0:T(8,128)(2,1)S(1)} %collective-permute-done.refs_1_.refs_5_, bf16[8,64,256]{2,1,0:T(8,128)(2,1)S(1)} %collective-permute-done.1.refs_2_.refs_6_, ...), custom_call_target="tpu_custom_call" | custom-call | flops 134217728 | bytes 2097152 | tf_op jit(solution)/shard_map/gram_partial/pallas_call | solution.py:162
  54.2 0.1 collective-permute-start.4
  54.3 1.5 %collective-permute-start.5 = (f32[64,128]{1,0:T(8,128)S(1)}, f32[64,128]{1,0:T(8,128)S(1)}, u32[]{:S(2)}, u32[]{:S(2)}) collective-permute-start(f32[64,128]{1,0:T(8,128)S(1)} %gram_partial.1), channel_id=1, source_target_pairs={{0,2},{1,3},{2,0},{3,1},{4,6},{5,7},{6,4},{7,5},{8,10},{9,11},{10,... | collective-permute-start | bytes 98312 | tf_op jit(solution)/shard_map/ppermute | solution.py:211
  55.8 0.3 collective-permute-start.6
  56.1 0.0 collective-permute-done.4
  56.1 2.1 %collective-permute-done.5 = f32[64,128]{1,0:T(8,128)S(1)} collective-permute-done((f32[64,128]{1,0:T(8,128)S(1)}, f32[64,128]{1,0:T(8,128)S(1)}, u32[]{:S(2)}, u32[]{:S(2)}) %collective-permute-start.5) | collective-permute-done | bytes 32800 | tf_op jit(solution)/shard_map/ppermute | solution.py:211
  58.3 0.9 %collective-permute-done.6 = f32[64,128]{1,0:T(8,128)S(1)} collective-permute-done((f32[64,128]{1,0:T(8,128)S(1)}, f32[64,128]{1,0:T(8,128)S(1)}, u32[]{:S(2)}, u32[]{:S(2)}) %collective-permute-start.6) | collective-permute-done | bytes 32800 | tf_op jit(solution)/shard_map/ppermute | solution.py:211
  59.2 0.1 collective-permute-start.7
  59.3 3.9 %collective-permute-done.7 = f32[64,128]{1,0:T(8,128)S(1)} collective-permute-done((f32[64,128]{1,0:T(8,128)S(1)}, f32[64,128]{1,0:T(8,128)S(1)}, u32[]{:S(2)}, u32[]{:S(2)}) %collective-permute-start.7) | collective-permute-done | bytes 32800 | tf_op jit(solution)/shard_map/ppermute | solution.py:211
  63.2 3.5 %collective-permute-start.10 = (f32[64,128]{1,0:T(8,128)S(1)}, f32[64,128]{1,0:T(8,128)S(1)}, u32[]{:S(2)}, u32[]{:S(2)}) collective-permute-start(f32[64,128]{1,0:T(8,128)S(1)} %add.15.refs_0_), channel_id=1, source_target_pairs={{0,24},{4,28},{8,16},{12,20},{16,8},{20,12},{24,0},{28,4},{1,25},{... | collective-permute-start | bytes 98312 | tf_op jit(solution)/shard_map/ppermute | solution.py:211
  66.7 9.2 %collective-permute-start.8 = (f32[64,128]{1,0:T(8,128)S(1)}, f32[64,128]{1,0:T(8,128)S(1)}, u32[]{:S(2)}, u32[]{:S(2)}) collective-permute-start(f32[64,128]{1,0:T(8,128)S(1)} %add.15.refs_0_), channel_id=1, source_target_pairs={{0,8},{4,12},{8,0},{12,4},{16,24},{20,28},{24,16},{28,20},{1,9},{5... | collective-permute-start | bytes 98312 | tf_op jit(solution)/shard_map/ppermute | solution.py:211
  75.8 0.0 collective-permute-start.9
  75.8 0.0 collective-permute-done.10.refs_3_
  75.8 1.9 %collective-permute-done.8.refs_1_ = f32[64,128]{1,0:T(8,128)S(1)} collective-permute-done((f32[64,128]{1,0:T(8,128)S(1)}, f32[64,128]{1,0:T(8,128)S(1)}, u32[]{:S(2)}, u32[]{:S(2)}) %collective-permute-start.8) | collective-permute-done | bytes 32800 | tf_op jit(solution)/shard_map/ppermute | solution.py:211
  77.7 2.9 %collective-permute-done.9.refs_2_ = f32[64,128]{1,0:T(8,128)S(1)} collective-permute-done((f32[64,128]{1,0:T(8,128)S(1)}, f32[64,128]{1,0:T(8,128)S(1)}, u32[]{:S(2)}, u32[]{:S(2)}) %collective-permute-start.9) | collective-permute-done | bytes 32800 | tf_op jit(solution)/shard_map/ppermute | solution.py:211
  80.7 6.8 %solve_and_project.1 = (f32[1,8]{1,0:T(1,128)}, f32[2,32,256]{2,1,0:T(8,128)}) custom-call(f32[64,128]{1,0:T(8,128)S(1)} %add.15.refs_0_, f32[64,128]{1,0:T(8,128)S(1)} %collective-permute-done.8.refs_1_, f32[64,128]{1,0:T(8,128)S(1)} %collective-permute-done.9.refs_2_, f32[64,128]{1,0:T(8,128)S(1)} %collective-permute-done.10.refs_3_, ...), custom_call_target="tpu_custom_call" | custom-call | tf_op jit(solution)/shard_map/solve_and_project/pallas_call | solution.py:263
  (2 shorter events, 0.0 us)
Async XLA Ops:
  4.1 8.9 %copy-start.1 = (bf16[8,64,256]{2,1,0:T(8,128)(2,1)S(1)}, bf16[8,64,256]{2,1,0:T(8,128)(2,1)}, u32[]{:S(2)}) copy-start(bf16[8,64,256]{2,1,0:T(8,128)(2,1)} %get-tuple-element.8.refs_0_) | copy-start | bytes 786436
  7.6 8.0 %copy-start.5 = (bf16[8,64,256]{2,1,0:T(8,128)(2,1)S(1)}, bf16[8,64,256]{2,1,0:T(8,128)(2,1)}, u32[]{:S(2)}) copy-start(bf16[8,64,256]{2,1,0:T(8,128)(2,1)} %get-tuple-element.9) | copy-start | bytes 786436
  7.6 9.8 %copy-start.4 = (bf16[8,64,256]{2,1,0:T(8,128)(2,1)S(1)}, bf16[8,64,256]{2,1,0:T(8,128)(2,1)}, u32[]{:S(2)}) copy-start(bf16[8,64,256]{2,1,0:T(8,128)(2,1)} %get-tuple-element.10) | copy-start | bytes 786436
  7.6 13.3 %copy-start.3 = (bf16[8,64,256]{2,1,0:T(8,128)(2,1)S(1)}, bf16[8,64,256]{2,1,0:T(8,128)(2,1)}, u32[]{:S(2)}) copy-start(bf16[8,64,256]{2,1,0:T(8,128)(2,1)} %get-tuple-element.11) | copy-start | bytes 786436
  7.6 13.4 %copy-start.2 = (f32[8]{0:T(128)S(1)}, f32[8]{0:T(128)}, u32[]{:S(2)}) copy-start(f32[8]{0:T(128)} %param.7) | copy-start | bytes 100
  7.6 13.4 %copy-start = (s32[8,256]{1,0:T(8,128)S(1)}, s32[8,256]{1,0:T(8,128)}, u32[]{:S(2)}) copy-start(s32[8,256]{1,0:T(8,128)} %spins_ref.1) | copy-start | bytes 24580
  7.6 45.1 %all-to-all-start = ((bf16[4,8,64,256]{3,2,1,0:T(8,128)(2,1)}), bf16[4,8,64,256]{3,2,1,0:T(8,128)(2,1)S(1)}, u32[]{:S(2)}, u32[]{:S(2)}) async-start(bf16[4,8,64,256]{3,2,1,0:T(8,128)(2,1)} %jac_rows.3), calls=%async_computation | async-start | bytes 2097152 | tf_op jit(solution)/shard_map/all_to_all | solution.py:288
  13.0 18.2 %collective-permute-start = (bf16[8,64,256]{2,1,0:T(8,128)(2,1)S(1)}, bf16[8,64,256]{2,1,0:T(8,128)(2,1)S(1)}, u32[]{:S(2)}, u32[]{:S(2)}) collective-permute-start(bf16[8,64,256]{2,1,0:T(8,128)(2,1)S(1)} %copy-done.1), channel_id=1, source_target_pairs={{0,16},{4,20},{8,24},{12,28},{16,0},{20,4},{24,8},{28,12},{1,17},{... | collective-permute-start | bytes 786440 | tf_op jit(solution)/shard_map/ppermute | solution.py:283
  15.6 37.1 %collective-permute-start.1 = (bf16[8,64,256]{2,1,0:T(8,128)(2,1)S(1)}, bf16[8,64,256]{2,1,0:T(8,128)(2,1)S(1)}, u32[]{:S(2)}, u32[]{:S(2)}) collective-permute-start(bf16[8,64,256]{2,1,0:T(8,128)(2,1)S(1)} %copy-done.5), channel_id=1, source_target_pairs={{0,20},{4,16},{8,28},{12,24},{16,4},{20,0},{24,12},{28,8},{1,21},{... | collective-permute-start | bytes 786440 | tf_op jit(solution)/shard_map/ppermute | solution.py:283
  17.4 35.3 %collective-permute-start.2 = (bf16[8,64,256]{2,1,0:T(8,128)(2,1)S(1)}, bf16[8,64,256]{2,1,0:T(8,128)(2,1)S(1)}, u32[]{:S(2)}, u32[]{:S(2)}) collective-permute-start(bf16[8,64,256]{2,1,0:T(8,128)(2,1)S(1)} %copy-done.4), channel_id=1, source_target_pairs={{0,24},{4,28},{8,16},{12,20},{16,8},{20,12},{24,0},{28,4},{1,25},{... | collective-permute-start | bytes 786440 | tf_op jit(solution)/shard_map/ppermute | solution.py:283
  20.9 31.8 %collective-permute-start.3 = (bf16[8,64,256]{2,1,0:T(8,128)(2,1)S(1)}, bf16[8,64,256]{2,1,0:T(8,128)(2,1)S(1)}, u32[]{:S(2)}, u32[]{:S(2)}) collective-permute-start(bf16[8,64,256]{2,1,0:T(8,128)(2,1)S(1)} %copy-done.3), channel_id=1, source_target_pairs={{0,28},{4,24},{8,20},{12,16},{16,12},{20,8},{24,4},{28,0},{1,29},{... | collective-permute-start | bytes 786440 | tf_op jit(solution)/shard_map/ppermute | solution.py:283
  54.2 1.9 %collective-permute-start.4 = (f32[64,128]{1,0:T(8,128)S(1)}, f32[64,128]{1,0:T(8,128)S(1)}, u32[]{:S(2)}, u32[]{:S(2)}) collective-permute-start(f32[64,128]{1,0:T(8,128)S(1)} %gram_partial.1), channel_id=1, source_target_pairs={{0,1},{1,0},{2,3},{3,2},{4,5},{5,4},{6,7},{7,6},{8,9},{9,8},{10,11... | collective-permute-start | bytes 98312 | tf_op jit(solution)/shard_map/ppermute | solution.py:211
  54.3 4.0 %collective-permute-start.5 = (f32[64,128]{1,0:T(8,128)S(1)}, f32[64,128]{1,0:T(8,128)S(1)}, u32[]{:S(2)}, u32[]{:S(2)}) collective-permute-start(f32[64,128]{1,0:T(8,128)S(1)} %gram_partial.1), channel_id=1, source_target_pairs={{0,2},{1,3},{2,0},{3,1},{4,6},{5,7},{6,4},{7,5},{8,10},{9,11},{10,... | collective-permute-start | bytes 98312 | tf_op jit(solution)/shard_map/ppermute | solution.py:211
  55.8 3.3 %collective-permute-start.6 = (f32[64,128]{1,0:T(8,128)S(1)}, f32[64,128]{1,0:T(8,128)S(1)}, u32[]{:S(2)}, u32[]{:S(2)}) collective-permute-start(f32[64,128]{1,0:T(8,128)S(1)} %gram_partial.1), channel_id=1, source_target_pairs={{0,3},{1,2},{2,1},{3,0},{4,7},{5,6},{6,5},{7,4},{8,11},{9,10},{10,... | collective-permute-start | bytes 98312 | tf_op jit(solution)/shard_map/ppermute | solution.py:211
  59.2 4.0 %collective-permute-start.7 = (f32[64,128]{1,0:T(8,128)S(1)}, f32[64,128]{1,0:T(8,128)S(1)}, u32[]{:S(2)}, u32[]{:S(2)}) collective-permute-start(f32[64,128]{1,0:T(8,128)S(1)} %add_add_fusion), channel_id=1, source_target_pairs={{0,4},{4,0},{8,12},{12,8},{16,20},{20,16},{24,28},{28,24},{1,5},{5... | collective-permute-start | bytes 98312 | tf_op jit(solution)/shard_map/ppermute | solution.py:211
  63.2 12.7 %collective-permute-start.10 = (f32[64,128]{1,0:T(8,128)S(1)}, f32[64,128]{1,0:T(8,128)S(1)}, u32[]{:S(2)}, u32[]{:S(2)}) collective-permute-start(f32[64,128]{1,0:T(8,128)S(1)} %add.15.refs_0_), channel_id=1, source_target_pairs={{0,24},{4,28},{8,16},{12,20},{16,8},{20,12},{24,0},{28,4},{1,25},{... | collective-permute-start | bytes 98312 | tf_op jit(solution)/shard_map/ppermute | solution.py:211
  66.7 11.1 %collective-permute-start.8 = (f32[64,128]{1,0:T(8,128)S(1)}, f32[64,128]{1,0:T(8,128)S(1)}, u32[]{:S(2)}, u32[]{:S(2)}) collective-permute-start(f32[64,128]{1,0:T(8,128)S(1)} %add.15.refs_0_), channel_id=1, source_target_pairs={{0,8},{4,12},{8,0},{12,4},{16,24},{20,28},{24,16},{28,20},{1,9},{5... | collective-permute-start | bytes 98312 | tf_op jit(solution)/shard_map/ppermute | solution.py:211
  75.8 4.8 %collective-permute-start.9 = (f32[64,128]{1,0:T(8,128)S(1)}, f32[64,128]{1,0:T(8,128)S(1)}, u32[]{:S(2)}, u32[]{:S(2)}) collective-permute-start(f32[64,128]{1,0:T(8,128)S(1)} %add.15.refs_0_), channel_id=1, source_target_pairs={{0,16},{4,20},{8,24},{12,28},{16,0},{20,4},{24,8},{28,12},{1,17},{... | collective-permute-start | bytes 98312 | tf_op jit(solution)/shard_map/ppermute | solution.py:211

commit v8 on v5

--- a/solution.py
+++ b/solution.py
@@ -11,6 +11,7 @@
 LANES = 128
 CHUNK = 16
 VMEM_LIMIT = 24 * 2**20
+JAC_VMEM_LIMIT = 60 * 2**20
 shift_ratio = 0.1
 F32 = jnp.float32
 BF16 = jnp.bfloat16
@@ -20,57 +21,72 @@
     return lax.broadcasted_iota(jnp.int32, shape, dim)
 
 
-def jac_kernel(first, act_hbm, cot_hbm, *refs):
+def jac_kernel(far, parts, act_hbm, cot_hbm, *refs):
     *out_refs, act_buf, cot_buf, held, sems = refs
     samples, mats = act_buf.shape[:2]
-    share = out_refs[0].shape[1] // mats
+    width = act_buf.shape[3]
+    near = lax.axis_size("samp") // 2
+    share = width // near
     me = lax.axis_index("samp")
+    half = 1 - me // near if far else me // near
+    columns = pl.ds(pl.multiple_of(half * width, width), width)
     copies = []
     for s in range(samples):
-        here = (s, pl.ds(first, mats))
-        copies.append(pltpu.make_async_copy(act_hbm.at[here], act_buf.at[s], sems.at[0, s]))
-        copies.append(pltpu.make_async_copy(cot_hbm.at[here], cot_buf.at[s], sems.at[1, s]))
-    for copy in copies:
-        copy.start()
-    for s in range(samples):
-        copies[2 * s].wait()
-        copies[2 * s + 1].wait()
-        for m in range(mats):
-            held[s, m] = lax.dot_general(
-                act_buf[s, m],
-                cot_buf[s, m],
-                (((0,), (0,)), ((), ())),
-                preferred_element_type=F32,
+        copies.append(
+            (
+                pltpu.make_async_copy(act_hbm.at[s, :, :, columns], act_buf.at[s], sems.at[0, s]),
+                pltpu.make_async_copy(cot_hbm.at[s], cot_buf.at[s], sems.at[1, s]),
             )
-        for k, out_ref in enumerate(out_refs):
-            owned = pl.ds(pl.multiple_of((me ^ k) * share, share), share)
-            rows = [held[s, m, owned] for m in range(mats)]
-            out_ref[s] = jnp.concatenate(rows, axis=0).astype(BF16)
-
-
-def jac_rows(activations, cotangents, owners, part, parts):
+        )
+    for pair in copies:
+        for copy in pair:
+            copy.start()
+    group = 2
+    for first in range(0, samples, group):
+        for s in range(first, first + group):
+            for copy in copies[s]:
+                copy.wait()
+        for s in range(first, first + group):
+            for m in range(mats):
+                held[s, m] = lax.dot_general(
+                    act_buf[s, m],
+                    cot_buf[s, m],
+                    (((0,), (0,)), ((), ())),
+                    preferred_element_type=F32,
+                )
+    each = mats // parts
+    for k in range(near):
+        owned = pl.ds(pl.multiple_of((me ^ k) % near * share, share), share)
+        for part in range(parts):
+            for s in range(samples):
+                rows = [held[s, part * each + m, owned] for m in range(each)]
+                out_refs[part * near + k][s] = jnp.concatenate(rows, axis=0).astype(BF16)
+
+
+def jac_rows(activations, cotangents, owners, parts, far):
     samples, mats, sites, d = activations.shape
-    mats //= parts
-    rows = mats * d // owners
+    near = owners // 2
+    rows = mats // parts * d // owners
     hbm = pl.BlockSpec(memory_space=pltpu.HBM)
-    return pl.pallas_call(
-        functools.partial(jac_kernel, part * mats),
+    blocks = pl.pallas_call(
+        functools.partial(jac_kernel, far, parts),
         in_specs=[hbm, hbm],
-        out_shape=[jax.ShapeDtypeStruct((samples, rows, d), BF16)] * owners,
+        out_shape=[jax.ShapeDtypeStruct((samples, rows, d), BF16)] * (parts * near),
         scratch_shapes=[
+            pltpu.VMEM((samples, mats, sites, d // 2), BF16),
             pltpu.VMEM((samples, mats, sites, d), BF16),
-            pltpu.VMEM((samples, mats, sites, d), BF16),
-            pltpu.VMEM((samples, mats, d, d), F32),
+            pltpu.VMEM((samples, mats, d // 2, d), F32),
             pltpu.SemaphoreType.DMA((2, samples)),
         ],
-        compiler_params=pltpu.CompilerParams(vmem_limit_bytes=VMEM_LIMIT),
+        compiler_params=pltpu.CompilerParams(vmem_limit_bytes=JAC_VMEM_LIMIT),
         cost_estimate=pl.CostEstimate(
-            flops=2 * samples * mats * sites * d * d,
-            bytes_accessed=6 * samples * mats * sites * d,
+            flops=samples * mats * sites * d * d,
+            bytes_accessed=4 * samples * mats * sites * d,
             transcendentals=0,
         ),
-        name="jac_rows",
+        name="far_rows" if far else "near_rows",
     )(activations, cotangents)
+    return [list(blocks[part * near : (part + 1) * near]) for part in range(parts)]
 
 
 def energy_kernel(spins_ref, offdiag_ref, out_ref):
@@ -241,6 +257,24 @@
     )(*grams, *[block for blocks in parts for block in blocks])
 
 
+def exchange(far, near):
+    parts, half = len(far), len(far[0])
+    owners = 2 * half
+    done = {(part, 0): near[part][0] for part in range(parts)}
+    order = []
+    far_left = [(part, k) for part in range(parts) for k in range(owners - 1, half - 1, -1)]
+    near_left = [(part, k) for part in range(parts) for k in range(half - 1, 0, -1)]
+    order += far_left[:half] + near_left[:1]
+    far_left, near_left = far_left[half:], near_left[1:]
+    while far_left or near_left:
+        order += far_left[:2] + near_left[:1]
+        far_left, near_left = far_left[2:], near_left[1:]
+    for part, k in order:
+        block = far[part][k - half] if k >= half else near[part][k]
+        done[part, k] = lax.ppermute(block, "samp", [(i, i ^ k) for i in range(owners)])
+    return [[done[part, k] for k in range(owners)] for part in range(parts)]
+
+
 def body(spins, activations, cotangents, offdiag):
     local, mats = activations.shape[:2]
     owners = lax.axis_size("samp")
@@ -248,14 +282,10 @@
     width = (total // LANES + 1) * LANES
     share = activations.shape[3] // owners
     parts = mats if share % CHUNK == 0 else 1
+    far = jac_rows(activations, cotangents, owners, parts, True)
+    near = jac_rows(activations, cotangents, owners, parts, False)
+    held = exchange(far, near)
     partial = energy_column(spins, offdiag, total, width)
-    held = []
-    for part in range(parts):
-        blocks = list(jac_rows(activations, cotangents, owners, part, parts))
-        for k in range(owners - 1, 0, -1):
-            perm = [(i, i ^ k) for i in range(owners)]
-            blocks[k] = lax.ppermute(blocks[k], "samp", perm)
-        held.append(blocks)
     for blocks in held:
         partial = gram_partial(blocks, partial)
     grams = partners(partial, "layer", 1, lax.axis_size("layer"))

time: 84.9 us -> 85.3 us (level)
  waiting for transfers between devices: 20.4 us -> 27.8 us
  Pallas kernels: 18.6 us -> 15.7 us
  starting transfers between devices: 41.8 us -> 38.9 us
  local copies, waits for them, and re-layouts: 3.26 us -> 1.92 us
    ppermute x14, waiting for transfers between devices: 12 us -> 19.9 us  [exchange(): lax.ppermute(block, 'samp', [(i, i ^ k) for i in range(owners)])]
    pallas_call x2, Pallas kernels: 9.67 us -> 6.83 us  [jac_rows(): pl.pallas_call(functools.partial(jac_kernel, far, parts), in_specs=[hbm,...]
    ppermute x7, starting transfers between devices: 10.1 us -> 7.81 us  [partners(): parts.append(lax.ppermute(value, axis, perm))]
    unnamed x8 -> x16, local copies, waits for them, and re-layouts: 3.18 us -> 1.84 us
  transfers between devices with their start and end apart: 21 -> 21, of which waited for: 8 -> 12; matrix products, arithmetic and copies ran while one was open for 0% -> 0% of each run, Pallas kernels for 7% -> 5%
where the time goes in v8:
time: 85.3 us; the launch traced here: 85.1 us
  starting transfers between devices  38.9 us (46%)
  waiting for transfers between devices  27.8 us (33%)
  Pallas kernels  15.7 us (18%)
  local copies, waits for them, and re-layouts  1.92 us (2%)
    ppermute x14, starting transfers between devices, exchange(): lax.ppermute(block, 'samp', [(i, i ^ k) for i in range(owners)])  31.1 us
    ppermute x14, waiting for transfers between devices, exchange(): lax.ppermute(block, 'samp', [(i, i ^ k) for i in range(owners)])  19.9 us
    ppermute x7, waiting for transfers between devices, partners(): parts.append(lax.ppermute(value, axis, perm))  7.93 us
    ppermute x7, starting transfers between devices, partners(): parts.append(lax.ppermute(value, axis, perm))  7.81 us
    pallas_call x1, Pallas kernels, solve_and_project(): pl.pallas_call(functools.partial(solve_kernel, owners), out_shape=(jax.Sh...  6.89 us
    pallas_call x2, Pallas kernels, jac_rows(): pl.pallas_call(functools.partial(jac_kernel, far, parts), in_specs=[hbm,...  6.83 us
    unnamed x16, local copies, waits for them, and re-layouts  1.84 us
    pallas_call x2, Pallas kernels, gram_partial(): pl.pallas_call(gram_kernel, out_shape=jax.ShapeDtypeStruct((total, width)...  1.75 us
  transfers between devices with their start and end apart: 21, of which 12 were waited for; matrix products, arithmetic and copies ran while one was open for 0% of the time, Pallas kernels for 5%

profile of v8, /device:TPU:0, one launch (start us, length us, event | category | flops | bytes accessed | tf_op | source)
XLA Modules:
  0.0 85.1 jit_solution(15568963949221239710)
XLA Ops:
  0.6 3.4 %far_rows.1 = (bf16[8,32,256]{2,1,0:T(8,128)(2,1)}, bf16[8,32,256]{2,1,0:T(8,128)(2,1)}, bf16[8,32,256]{2,1,0:T(8,128)(2,1)}, bf16[8,32,256]{2,1,0:T(8,128)(2,1)...) custom-call(bf16[8,2,256,256]{3,2,1,0:T(8,128)(2,1)} %act_hbm.3, ...), custom_call_target="tpu_custom_call" | custom-call | flops 268435456 | bytes 4194304 | tf_op jit(solution)/shard_map/far_rows/pallas_call | solution.py:71
  4.0 4.1 %collective-permute-start.3 = (bf16[8,32,256]{2,1,0:T(8,128)(2,1)}, bf16[8,32,256]{2,1,0:T(8,128)(2,1)S(1)}, u32[]{:S(2)}, u32[]{:S(2)}) collective-permute-start(bf16[8,32,256]{2,1,0:T(8,128)(2,1)} %get-tuple-element.24), channel_id=1, source_target_pairs={{0,16},{4,20},{8,24},{12,28},{16,0},{20,4},{24,8},{28,12},{1,17},{... | collective-permute-start | bytes 393224 | tf_op jit(solution)/shard_map/ppermute | solution.py:274
  8.1 1.3 %collective-permute-start.4 = (bf16[8,32,256]{2,1,0:T(8,128)(2,1)}, bf16[8,32,256]{2,1,0:T(8,128)(2,1)S(1)}, u32[]{:S(2)}, u32[]{:S(2)}) collective-permute-start(bf16[8,32,256]{2,1,0:T(8,128)(2,1)} %get-tuple-element.25), channel_id=1, source_target_pairs={{0,20},{4,16},{8,28},{12,24},{16,4},{20,0},{24,12},{28,8},{1,21},{... | collective-permute-start | bytes 393224 | tf_op jit(solution)/shard_map/ppermute | solution.py:274
  9.4 2.6 %collective-permute-start.10 = (bf16[8,32,256]{2,1,0:T(8,128)(2,1)}, bf16[8,32,256]{2,1,0:T(8,128)(2,1)S(1)}, u32[]{:S(2)}, u32[]{:S(2)}) collective-permute-start(bf16[8,32,256]{2,1,0:T(8,128)(2,1)} %get-tuple-element.32), channel_id=1, source_target_pairs={{0,16},{4,20},{8,24},{12,28},{16,0},{20,4},{24,8},{28,12},{1,17},{... | collective-permute-start | bytes 393224 | tf_op jit(solution)/shard_map/ppermute | solution.py:274
  12.0 0.0 collective-permute-start.11
  12.1 0.0 copy-start.7
  12.1 0.0 copy-start.6
  12.1 0.0 copy-start.5
  12.1 0.0 copy-start.4
  12.1 0.0 copy-start.3
  12.1 3.9 %collective-permute-start.12 = (bf16[8,32,256]{2,1,0:T(8,128)(2,1)}, bf16[8,32,256]{2,1,0:T(8,128)(2,1)S(1)}, u32[]{:S(2)}, u32[]{:S(2)}) collective-permute-start(bf16[8,32,256]{2,1,0:T(8,128)(2,1)} %get-tuple-element.34), channel_id=1, source_target_pairs={{0,24},{4,28},{8,16},{12,20},{16,8},{20,12},{24,0},{28,4},{1,25},{... | collective-permute-start | bytes 393224 | tf_op jit(solution)/shard_map/ppermute | solution.py:274
  16.0 3.4 %near_rows.1 = (bf16[8,32,256]{2,1,0:T(8,128)(2,1)}, bf16[8,32,256]{2,1,0:T(8,128)(2,1)}, bf16[8,32,256]{2,1,0:T(8,128)(2,1)}, bf16[8,32,256]{2,1,0:T(8,128)(2,1...) custom-call(bf16[8,2,256,256]{3,2,1,0:T(8,128)(2,1)} %act_hbm.3, ...), custom_call_target="tpu_custom_call" | custom-call | flops 268435456 | bytes 4194304 | tf_op jit(solution)/shard_map/near_rows/pallas_call | solution.py:71
  19.4 7.3 %collective-permute-done.3.refs_4_.refs_16_ = bf16[8,32,256]{2,1,0:T(8,128)(2,1)S(1)} collective-permute-done((bf16[8,32,256]{2,1,0:T(8,128)(2,1)}, bf16[8,32,256]{2,1,0:T(8,128)(2,1)S(1)}, u32[]{:S(2)}, u32[]{:S(2)}) %collective-permute-start.3) | collective-permute-done | bytes 131104 | tf_op jit(solution)/shard_map/ppermute | solution.py:274
  26.7 0.0 copy-done.7
  26.7 3.8 %collective-permute-start.13 = (bf16[8,32,256]{2,1,0:T(8,128)(2,1)S(1)}, bf16[8,32,256]{2,1,0:T(8,128)(2,1)S(1)}, u32[]{:S(2)}, u32[]{:S(2)}) collective-permute-start(bf16[8,32,256]{2,1,0:T(8,128)(2,1)S(1)} %copy-done.7), channel_id=1, source_target_pairs={{0,28},{4,24},{8,20},{12,16},{16,12},{20,8},{24,4},{28,0},{1,29},{... | collective-permute-start | bytes 393224 | tf_op jit(solution)/shard_map/ppermute | solution.py:274
  30.5 0.3 collective-permute-done.4.refs_5_.refs_17_
  30.8 0.2 collective-permute-start.7
  31.0 4.2 %collective-permute-done.10.refs_4_.refs_8_ = bf16[8,32,256]{2,1,0:T(8,128)(2,1)S(1)} collective-permute-done((bf16[8,32,256]{2,1,0:T(8,128)(2,1)}, bf16[8,32,256]{2,1,0:T(8,128)(2,1)S(1)}, u32[]{:S(2)}, u32[]{:S(2)}) %collective-permute-start.10) | collective-permute-done | bytes 131104 | tf_op jit(solution)/shard_map/ppermute | solution.py:274
  35.2 0.0 collective-permute-start.8
  35.2 4.1 %collective-permute-done.11.refs_5_.refs_9_ = bf16[8,32,256]{2,1,0:T(8,128)(2,1)S(1)} collective-permute-done((bf16[8,32,256]{2,1,0:T(8,128)(2,1)}, bf16[8,32,256]{2,1,0:T(8,128)(2,1)S(1)}, u32[]{:S(2)}, u32[]{:S(2)}) %collective-permute-start.11) | collective-permute-done | bytes 131104 | tf_op jit(solution)/shard_map/ppermute | solution.py:274
  39.3 0.0 collective-permute-start.9
  39.3 0.0 collective-permute-done.12.refs_6_.refs_10_
  39.3 0.0 copy-done.6
  39.3 2.5 %collective-permute-start.5 = (bf16[8,32,256]{2,1,0:T(8,128)(2,1)S(1)}, bf16[8,32,256]{2,1,0:T(8,128)(2,1)S(1)}, u32[]{:S(2)}, u32[]{:S(2)}) collective-permute-start(bf16[8,32,256]{2,1,0:T(8,128)(2,1)S(1)} %copy-done.6), channel_id=1, source_target_pairs={{0,24},{4,28},{8,16},{12,20},{16,8},{20,12},{24,0},{28,4},{1,25},{... | collective-permute-start | bytes 393224 | tf_op jit(solution)/shard_map/ppermute | solution.py:274
  41.8 0.0 collective-permute-done.13.refs_7_.refs_11_
  41.8 0.0 copy-done.5
  41.8 1.0 %collective-permute-start.6 = (bf16[8,32,256]{2,1,0:T(8,128)(2,1)S(1)}, bf16[8,32,256]{2,1,0:T(8,128)(2,1)S(1)}, u32[]{:S(2)}, u32[]{:S(2)}) collective-permute-start(bf16[8,32,256]{2,1,0:T(8,128)(2,1)S(1)} %copy-done.5), channel_id=1, source_target_pairs={{0,28},{4,24},{8,20},{12,16},{16,12},{20,8},{24,4},{28,0},{1,29},{... | collective-permute-start | bytes 393224 | tf_op jit(solution)/shard_map/ppermute | solution.py:274
  42.8 0.0 collective-permute-done.7.refs_1_.refs_5_
  42.8 1.8 %collective-permute-start = (bf16[8,32,256]{2,1,0:T(8,128)(2,1)}, bf16[8,32,256]{2,1,0:T(8,128)(2,1)S(1)}, u32[]{:S(2)}, u32[]{:S(2)}) collective-permute-start(bf16[8,32,256]{2,1,0:T(8,128)(2,1)} %get-tuple-element.21), channel_id=1, source_target_pairs={{0,4},{4,0},{8,12},{12,8},{16,20},{20,16},{24,28},{28,24},{1,5},{5... | collective-permute-start | bytes 393224 | tf_op jit(solution)/shard_map/ppermute | solution.py:274
  44.6 0.0 collective-permute-done.8.refs_2_.refs_6_
  44.6 9.9 %collective-permute-start.1 = (bf16[8,32,256]{2,1,0:T(8,128)(2,1)}, bf16[8,32,256]{2,1,0:T(8,128)(2,1)S(1)}, u32[]{:S(2)}, u32[]{:S(2)}) collective-permute-start(bf16[8,32,256]{2,1,0:T(8,128)(2,1)} %get-tuple-element.22), channel_id=1, source_target_pairs={{0,8},{4,12},{8,0},{12,4},{16,24},{20,28},{24,16},{28,20},{1,9},{5... | collective-permute-start | bytes 393224 | tf_op jit(solution)/shard_map/ppermute | solution.py:274
  54.6 0.0 collective-permute-done.9.refs_3_.refs_7_
  54.6 0.0 collective-permute-start.2
  54.6 0.0 copy-done.4
  54.6 0.1 copy.6.offdiag_ref
  54.7 0.0 copy-done.3
  54.7 0.2 energy_column.1.refs_8_
  54.9 0.0 copy-start
  54.9 0.9 %copy-done = bf16[8,32,256]{2,1,0:T(8,128)(2,1)S(1)} copy-done((bf16[8,32,256]{2,1,0:T(8,128)(2,1)S(1)}, bf16[8,32,256]{2,1,0:T(8,128)(2,1)}, u32[]{:S(2)}) %copy-start) | copy-done | bytes 131096
  55.8 0.0 copy-start.1
  55.8 0.9 %gram_partial.2.refs_8_ = f32[64,128]{1,0:T(8,128)S(1)} custom-call(bf16[8,32,256]{2,1,0:T(8,128)(2,1)S(1)} %copy-done, bf16[8,32,256]{2,1,0:T(8,128)(2,1)S(1)} %collective-permute-done.7.refs_1_.refs_5_, bf16[8,32,256]{2,1,0:T(8,128)(2,1)S(1)} %collective-permute-done.8.refs_2_.refs_6_, bf16[8,32,256]{2,1,0:T(8,128)(2,1)S(1)} %collective-permute-done.9.refs_3_.refs_7_, ...), custom_call_target="tpu_custom_call" | custom-call | flops 67108864 | bytes 1048576 | tf_op jit(solution)/shard_map/gram_partial/pallas_call | solution.py:149
  56.7 0.0 collective-permute-done.5.refs_6_.refs_18_
  56.7 0.0 collective-permute-done.6.refs_7_.refs_19_
  56.7 0.0 collective-permute-done.refs_1_.refs_13_
  56.7 2.5 %collective-permute-done.1.refs_2_.refs_14_ = bf16[8,32,256]{2,1,0:T(8,128)(2,1)S(1)} collective-permute-done((bf16[8,32,256]{2,1,0:T(8,128)(2,1)}, bf16[8,32,256]{2,1,0:T(8,128)(2,1)S(1)}, u32[]{:S(2)}, u32[]{:S(2)}) %collective-permute-start.1) | collective-permute-done | bytes 131104 | tf_op jit(solution)/shard_map/ppermute | solution.py:274
  59.2 1.5 %collective-permute-done.2.refs_3_.refs_15_ = bf16[8,32,256]{2,1,0:T(8,128)(2,1)S(1)} collective-permute-done((bf16[8,32,256]{2,1,0:T(8,128)(2,1)}, bf16[8,32,256]{2,1,0:T(8,128)(2,1)S(1)}, u32[]{:S(2)}, u32[]{:S(2)}) %collective-permute-start.2) | collective-permute-done | bytes 131104 | tf_op jit(solution)/shard_map/ppermute | solution.py:274
  60.7 0.9 %copy-done.2 = bf16[8,32,256]{2,1,0:T(8,128)(2,1)S(1)} copy-done((bf16[8,32,256]{2,1,0:T(8,128)(2,1)S(1)}, bf16[8,32,256]{2,1,0:T(8,128)(2,1)}, u32[]{:S(2)}) %copy-start.2) | copy-done | bytes 131096
  61.6 0.9 %gram_partial.3 = f32[64,128]{1,0:T(8,128)S(1)} custom-call(bf16[8,32,256]{2,1,0:T(8,128)(2,1)S(1)} %copy-done.2, bf16[8,32,256]{2,1,0:T(8,128)(2,1)S(1)} %collective-permute-done.refs_1_.refs_13_, bf16[8,32,256]{2,1,0:T(8,128)(2,1)S(1)} %collective-permute-done.1.refs_2_.refs_14_, bf16[8,32,256]{2,1,0:T(8,128)(2,1)S(1)} %collective-permute-done.2.refs_3_.refs_15_, ...), custom_call_target="tpu_custom_call" | custom-call | flops 67108864 | bytes 1048576 | tf_op jit(solution)/shard_map/gram_partial/pallas_call | solution.py:149
  62.4 0.1 collective-permute-start.16
  62.5 1.5 %collective-permute-start.15 = (f32[64,128]{1,0:T(8,128)S(1)}, f32[64,128]{1,0:T(8,128)S(1)}, u32[]{:S(2)}, u32[]{:S(2)}) collective-permute-start(f32[64,128]{1,0:T(8,128)S(1)} %gram_partial.3), channel_id=1, source_target_pairs={{0,2},{1,3},{2,0},{3,1},{4,6},{5,7},{6,4},{7,5},{8,10},{9,11},{10,... | collective-permute-start | bytes 98312 | tf_op jit(solution)/shard_map/ppermute | solution.py:198
  64.1 0.3 collective-permute-start.14
  64.4 1.8 %collective-permute-done.16 = f32[64,128]{1,0:T(8,128)S(1)} collective-permute-done((f32[64,128]{1,0:T(8,128)S(1)}, f32[64,128]{1,0:T(8,128)S(1)}, u32[]{:S(2)}, u32[]{:S(2)}) %collective-permute-start.16) | collective-permute-done | bytes 32800 | tf_op jit(solution)/shard_map/ppermute | solution.py:198
  66.2 0.4 collective-permute-done.15
  66.5 0.0 collective-permute-done.14
  66.6 1.5 %collective-permute-start.17 = (f32[64,128]{1,0:T(8,128)S(1)}, f32[64,128]{1,0:T(8,128)S(1)}, u32[]{:S(2)}, u32[]{:S(2)}) collective-permute-start(f32[64,128]{1,0:T(8,128)S(1)} %add_add_fusion), channel_id=1, source_target_pairs={{0,4},{4,0},{8,12},{12,8},{16,20},{20,16},{24,28},{28,24},{1,5},{5... | collective-permute-start | bytes 98312 | tf_op jit(solution)/shard_map/ppermute | solution.py:198
  68.1 2.5 %collective-permute-done.17 = f32[64,128]{1,0:T(8,128)S(1)} collective-permute-done((f32[64,128]{1,0:T(8,128)S(1)}, f32[64,128]{1,0:T(8,128)S(1)}, u32[]{:S(2)}, u32[]{:S(2)}) %collective-permute-start.17) | collective-permute-done | bytes 32800 | tf_op jit(solution)/shard_map/ppermute | solution.py:198
  70.5 1.2 %collective-permute-start.20 = (f32[64,128]{1,0:T(8,128)S(1)}, f32[64,128]{1,0:T(8,128)S(1)}, u32[]{:S(2)}, u32[]{:S(2)}) collective-permute-start(f32[64,128]{1,0:T(8,128)S(1)} %add.15.refs_0_), channel_id=1, source_target_pairs={{0,24},{4,28},{8,16},{12,20},{16,8},{20,12},{24,0},{28,4},{1,25},{... | collective-permute-start | bytes 98312 | tf_op jit(solution)/shard_map/ppermute | solution.py:198
  71.8 2.5 %collective-permute-start.19 = (f32[64,128]{1,0:T(8,128)S(1)}, f32[64,128]{1,0:T(8,128)S(1)}, u32[]{:S(2)}, u32[]{:S(2)}) collective-permute-start(f32[64,128]{1,0:T(8,128)S(1)} %add.15.refs_0_), channel_id=1, source_target_pairs={{0,16},{4,20},{8,24},{12,28},{16,0},{20,4},{24,8},{28,12},{1,17},{... | collective-permute-start | bytes 98312 | tf_op jit(solution)/shard_map/ppermute | solution.py:198
  74.3 0.6 collective-permute-start.18
  74.9 1.4 %collective-permute-done.20.refs_3_ = f32[64,128]{1,0:T(8,128)S(1)} collective-permute-done((f32[64,128]{1,0:T(8,128)S(1)}, f32[64,128]{1,0:T(8,128)S(1)}, u32[]{:S(2)}, u32[]{:S(2)}) %collective-permute-start.20) | collective-permute-done | bytes 32800 | tf_op jit(solution)/shard_map/ppermute | solution.py:198
  76.4 0.8 collective-permute-done.19.refs_2_
  77.2 1.0 %collective-permute-done.18.refs_1_ = f32[64,128]{1,0:T(8,128)S(1)} collective-permute-done((f32[64,128]{1,0:T(8,128)S(1)}, f32[64,128]{1,0:T(8,128)S(1)}, u32[]{:S(2)}, u32[]{:S(2)}) %collective-permute-start.18) | collective-permute-done | bytes 32800 | tf_op jit(solution)/shard_map/ppermute | solution.py:198
  78.2 0.0 copy-done.1
  78.2 6.9 %solve_and_project.1 = (f32[1,8]{1,0:T(1,128)}, f32[2,32,256]{2,1,0:T(8,128)}) custom-call(f32[64,128]{1,0:T(8,128)S(1)} %add.15.refs_0_, f32[64,128]{1,0:T(8,128)S(1)} %collective-permute-done.18.refs_1_, f32[64,128]{1,0:T(8,128)S(1)} %collective-permute-done.19.refs_2_, f32[64,128]{1,0:T(8,128)S(1)} %collective-permute-done.20.refs_3_, ...), custom_call_target="tpu_custom_call" | custom-call | tf_op jit(solution)/shard_map/solve_and_project/pallas_call | solution.py:248
  (3 shorter events, 0.0 us)
Async XLA Ops:
  4.0 22.7 %collective-permute-start.3 = (bf16[8,32,256]{2,1,0:T(8,128)(2,1)}, bf16[8,32,256]{2,1,0:T(8,128)(2,1)S(1)}, u32[]{:S(2)}, u32[]{:S(2)}) collective-permute-start(bf16[8,32,256]{2,1,0:T(8,128)(2,1)} %get-tuple-element.24), channel_id=1, source_target_pairs={{0,16},{4,20},{8,24},{12,28},{16,0},{20,4},{24,8},{28,12},{1,17},{... | collective-permute-start | bytes 393224 | tf_op jit(solution)/shard_map/ppermute | solution.py:274
  8.1 22.7 %collective-permute-start.4 = (bf16[8,32,256]{2,1,0:T(8,128)(2,1)}, bf16[8,32,256]{2,1,0:T(8,128)(2,1)S(1)}, u32[]{:S(2)}, u32[]{:S(2)}) collective-permute-start(bf16[8,32,256]{2,1,0:T(8,128)(2,1)} %get-tuple-element.25), channel_id=1, source_target_pairs={{0,20},{4,16},{8,28},{12,24},{16,4},{20,0},{24,12},{28,8},{1,21},{... | collective-permute-start | bytes 393224 | tf_op jit(solution)/shard_map/ppermute | solution.py:274
  9.4 25.7 %collective-permute-start.10 = (bf16[8,32,256]{2,1,0:T(8,128)(2,1)}, bf16[8,32,256]{2,1,0:T(8,128)(2,1)S(1)}, u32[]{:S(2)}, u32[]{:S(2)}) collective-permute-start(bf16[8,32,256]{2,1,0:T(8,128)(2,1)} %get-tuple-element.32), channel_id=1, source_target_pairs={{0,16},{4,20},{8,24},{12,28},{16,0},{20,4},{24,8},{28,12},{1,17},{... | collective-permute-start | bytes 393224 | tf_op jit(solution)/shard_map/ppermute | solution.py:274
  12.0 27.2 %collective-permute-start.11 = (bf16[8,32,256]{2,1,0:T(8,128)(2,1)}, bf16[8,32,256]{2,1,0:T(8,128)(2,1)S(1)}, u32[]{:S(2)}, u32[]{:S(2)}) collective-permute-start(bf16[8,32,256]{2,1,0:T(8,128)(2,1)} %get-tuple-element.33), channel_id=1, source_target_pairs={{0,20},{4,16},{8,28},{12,24},{16,4},{20,0},{24,12},{28,8},{1,21},{... | collective-permute-start | bytes 393224 | tf_op jit(solution)/shard_map/ppermute | solution.py:274
  12.1 14.7 %copy-start.7 = (bf16[8,32,256]{2,1,0:T(8,128)(2,1)S(1)}, bf16[8,32,256]{2,1,0:T(8,128)(2,1)}, u32[]{:S(2)}) copy-start(bf16[8,32,256]{2,1,0:T(8,128)(2,1)} %get-tuple-element.35) | copy-start | bytes 393220
  12.1 27.2 %copy-start.6 = (bf16[8,32,256]{2,1,0:T(8,128)(2,1)S(1)}, bf16[8,32,256]{2,1,0:T(8,128)(2,1)}, u32[]{:S(2)}) copy-start(bf16[8,32,256]{2,1,0:T(8,128)(2,1)} %get-tuple-element.26) | copy-start | bytes 393220
  12.1 29.8 %copy-start.5 = (bf16[8,32,256]{2,1,0:T(8,128)(2,1)S(1)}, bf16[8,32,256]{2,1,0:T(8,128)(2,1)}, u32[]{:S(2)}) copy-start(bf16[8,32,256]{2,1,0:T(8,128)(2,1)} %get-tuple-element.27) | copy-start | bytes 393220
  12.1 42.5 %copy-start.4 = (f32[8]{0:T(128)S(1)}, f32[8]{0:T(128)}, u32[]{:S(2)}) copy-start(f32[8]{0:T(128)} %param.7) | copy-start | bytes 100
  12.1 42.6 %copy-start.3 = (s32[8,256]{1,0:T(8,128)S(1)}, s32[8,256]{1,0:T(8,128)}, u32[]{:S(2)}) copy-start(s32[8,256]{1,0:T(8,128)} %spins_ref.1) | copy-start | bytes 24580
  12.1 27.2 %collective-permute-start.12 = (bf16[8,32,256]{2,1,0:T(8,128)(2,1)}, bf16[8,32,256]{2,1,0:T(8,128)(2,1)S(1)}, u32[]{:S(2)}, u32[]{:S(2)}) collective-permute-start(bf16[8,32,256]{2,1,0:T(8,128)(2,1)} %get-tuple-element.34), channel_id=1, source_target_pairs={{0,24},{4,28},{8,16},{12,20},{16,8},{20,12},{24,0},{28,4},{1,25},{... | collective-permute-start | bytes 393224 | tf_op jit(solution)/shard_map/ppermute | solution.py:274
  26.7 15.1 %collective-permute-start.13 = (bf16[8,32,256]{2,1,0:T(8,128)(2,1)S(1)}, bf16[8,32,256]{2,1,0:T(8,128)(2,1)S(1)}, u32[]{:S(2)}, u32[]{:S(2)}) collective-permute-start(bf16[8,32,256]{2,1,0:T(8,128)(2,1)S(1)} %copy-done.7), channel_id=1, source_target_pairs={{0,28},{4,24},{8,20},{12,16},{16,12},{20,8},{24,4},{28,0},{1,29},{... | collective-permute-start | bytes 393224 | tf_op jit(solution)/shard_map/ppermute | solution.py:274
  30.8 12.0 %collective-permute-start.7 = (bf16[8,32,256]{2,1,0:T(8,128)(2,1)}, bf16[8,32,256]{2,1,0:T(8,128)(2,1)S(1)}, u32[]{:S(2)}, u32[]{:S(2)}) collective-permute-start(bf16[8,32,256]{2,1,0:T(8,128)(2,1)} %get-tuple-element.29), channel_id=1, source_target_pairs={{0,4},{4,0},{8,12},{12,8},{16,20},{20,16},{24,28},{28,24},{1,5},{5... | collective-permute-start | bytes 393224 | tf_op jit(solution)/shard_map/ppermute | solution.py:274
  35.2 9.5 %collective-permute-start.8 = (bf16[8,32,256]{2,1,0:T(8,128)(2,1)}, bf16[8,32,256]{2,1,0:T(8,128)(2,1)S(1)}, u32[]{:S(2)}, u32[]{:S(2)}) collective-permute-start(bf16[8,32,256]{2,1,0:T(8,128)(2,1)} %get-tuple-element.30), channel_id=1, source_target_pairs={{0,8},{4,12},{8,0},{12,4},{16,24},{20,28},{24,16},{28,20},{1,9},{5... | collective-permute-start | bytes 393224 | tf_op jit(solution)/shard_map/ppermute | solution.py:274
  39.3 15.3 %collective-permute-start.9 = (bf16[8,32,256]{2,1,0:T(8,128)(2,1)}, bf16[8,32,256]{2,1,0:T(8,128)(2,1)S(1)}, u32[]{:S(2)}, u32[]{:S(2)}) collective-permute-start(bf16[8,32,256]{2,1,0:T(8,128)(2,1)} %get-tuple-element.31), channel_id=1, source_target_pairs={{0,12},{4,8},{8,4},{12,0},{16,28},{20,24},{24,20},{28,16},{1,13},{... | collective-permute-start | bytes 393224 | tf_op jit(solution)/shard_map/ppermute | solution.py:274
  39.3 17.4 %collective-permute-start.5 = (bf16[8,32,256]{2,1,0:T(8,128)(2,1)S(1)}, bf16[8,32,256]{2,1,0:T(8,128)(2,1)S(1)}, u32[]{:S(2)}, u32[]{:S(2)}) collective-permute-start(bf16[8,32,256]{2,1,0:T(8,128)(2,1)S(1)} %copy-done.6), channel_id=1, source_target_pairs={{0,24},{4,28},{8,16},{12,20},{16,8},{20,12},{24,0},{28,4},{1,25},{... | collective-permute-start | bytes 393224 | tf_op jit(solution)/shard_map/ppermute | solution.py:274
  41.8 14.9 %collective-permute-start.6 = (bf16[8,32,256]{2,1,0:T(8,128)(2,1)S(1)}, bf16[8,32,256]{2,1,0:T(8,128)(2,1)S(1)}, u32[]{:S(2)}, u32[]{:S(2)}) collective-permute-start(bf16[8,32,256]{2,1,0:T(8,128)(2,1)S(1)} %copy-done.5), channel_id=1, source_target_pairs={{0,28},{4,24},{8,20},{12,16},{16,12},{20,8},{24,4},{28,0},{1,29},{... | collective-permute-start | bytes 393224 | tf_op jit(solution)/shard_map/ppermute | solution.py:274
  42.8 13.9 %collective-permute-start = (bf16[8,32,256]{2,1,0:T(8,128)(2,1)}, bf16[8,32,256]{2,1,0:T(8,128)(2,1)S(1)}, u32[]{:S(2)}, u32[]{:S(2)}) collective-permute-start(bf16[8,32,256]{2,1,0:T(8,128)(2,1)} %get-tuple-element.21), channel_id=1, source_target_pairs={{0,4},{4,0},{8,12},{12,8},{16,20},{20,16},{24,28},{28,24},{1,5},{5... | collective-permute-start | bytes 393224 | tf_op jit(solution)/shard_map/ppermute | solution.py:274
  44.6 14.5 %collective-permute-start.1 = (bf16[8,32,256]{2,1,0:T(8,128)(2,1)}, bf16[8,32,256]{2,1,0:T(8,128)(2,1)S(1)}, u32[]{:S(2)}, u32[]{:S(2)}) collective-permute-start(bf16[8,32,256]{2,1,0:T(8,128)(2,1)} %get-tuple-element.22), channel_id=1, source_target_pairs={{0,8},{4,12},{8,0},{12,4},{16,24},{20,28},{24,16},{28,20},{1,9},{5... | collective-permute-start | bytes 393224 | tf_op jit(solution)/shard_map/ppermute | solution.py:274
  54.6 6.1 %collective-permute-start.2 = (bf16[8,32,256]{2,1,0:T(8,128)(2,1)}, bf16[8,32,256]{2,1,0:T(8,128)(2,1)S(1)}, u32[]{:S(2)}, u32[]{:S(2)}) collective-permute-start(bf16[8,32,256]{2,1,0:T(8,128)(2,1)} %get-tuple-element.23), channel_id=1, source_target_pairs={{0,12},{4,8},{8,4},{12,0},{16,28},{20,24},{24,20},{28,16},{1,13},{... | collective-permute-start | bytes 393224 | tf_op jit(solution)/shard_map/ppermute | solution.py:274
  54.9 0.9 %copy-start = (bf16[8,32,256]{2,1,0:T(8,128)(2,1)S(1)}, bf16[8,32,256]{2,1,0:T(8,128)(2,1)}, u32[]{:S(2)}) copy-start(bf16[8,32,256]{2,1,0:T(8,128)(2,1)} %get-tuple-element.28.refs_0_.refs_4_) | copy-start | bytes 393220
  55.8 22.4 %copy-start.1 = (bf16[8,32,256]{2,1,0:T(8,128)(2,1)S(1)}, bf16[8,32,256]{2,1,0:T(8,128)(2,1)}, u32[]{:S(2)}) copy-start(bf16[8,32,256]{2,1,0:T(8,128)(2,1)} %get-tuple-element.28.refs_0_.refs_4_) | copy-start | bytes 393220
  60.7 0.9 %copy-start.2 = (bf16[8,32,256]{2,1,0:T(8,128)(2,1)S(1)}, bf16[8,32,256]{2,1,0:T(8,128)(2,1)}, u32[]{:S(2)}) copy-start(bf16[8,32,256]{2,1,0:T(8,128)(2,1)} %get-tuple-element.20.refs_0_.refs_12_) | copy-start | bytes 393220
  62.4 3.7 %collective-permute-start.16 = (f32[64,128]{1,0:T(8,128)S(1)}, f32[64,128]{1,0:T(8,128)S(1)}, u32[]{:S(2)}, u32[]{:S(2)}) collective-permute-start(f32[64,128]{1,0:T(8,128)S(1)} %gram_partial.3), channel_id=1, source_target_pairs={{0,3},{1,2},{2,1},{3,0},{4,7},{5,6},{6,5},{7,4},{8,11},{9,10},{10,... | collective-permute-start | bytes 98312 | tf_op jit(solution)/shard_map/ppermute | solution.py:198
  62.5 4.0 %collective-permute-start.15 = (f32[64,128]{1,0:T(8,128)S(1)}, f32[64,128]{1,0:T(8,128)S(1)}, u32[]{:S(2)}, u32[]{:S(2)}) collective-permute-start(f32[64,128]{1,0:T(8,128)S(1)} %gram_partial.3), channel_id=1, source_target_pairs={{0,2},{1,3},{2,0},{3,1},{4,6},{5,7},{6,4},{7,5},{8,10},{9,11},{10,... | collective-permute-start | bytes 98312 | tf_op jit(solution)/shard_map/ppermute | solution.py:198
  64.1 2.5 %collective-permute-start.14 = (f32[64,128]{1,0:T(8,128)S(1)}, f32[64,128]{1,0:T(8,128)S(1)}, u32[]{:S(2)}, u32[]{:S(2)}) collective-permute-start(f32[64,128]{1,0:T(8,128)S(1)} %gram_partial.3), channel_id=1, source_target_pairs={{0,1},{1,0},{2,3},{3,2},{4,5},{5,4},{6,7},{7,6},{8,9},{9,8},{10,11... | collective-permute-start | bytes 98312 | tf_op jit(solution)/shard_map/ppermute | solution.py:198
  66.6 4.0 %collective-permute-start.17 = (f32[64,128]{1,0:T(8,128)S(1)}, f32[64,128]{1,0:T(8,128)S(1)}, u32[]{:S(2)}, u32[]{:S(2)}) collective-permute-start(f32[64,128]{1,0:T(8,128)S(1)} %add_add_fusion), channel_id=1, source_target_pairs={{0,4},{4,0},{8,12},{12,8},{16,20},{20,16},{24,28},{28,24},{1,5},{5... | collective-permute-start | bytes 98312 | tf_op jit(solution)/shard_map/ppermute | solution.py:198
  70.5 5.8 %collective-permute-start.20 = (f32[64,128]{1,0:T(8,128)S(1)}, f32[64,128]{1,0:T(8,128)S(1)}, u32[]{:S(2)}, u32[]{:S(2)}) collective-permute-start(f32[64,128]{1,0:T(8,128)S(1)} %add.15.refs_0_), channel_id=1, source_target_pairs={{0,24},{4,28},{8,16},{12,20},{16,8},{20,12},{24,0},{28,4},{1,25},{... | collective-permute-start | bytes 98312 | tf_op jit(solution)/shard_map/ppermute | solution.py:198
  71.8 5.4 %collective-permute-start.19 = (f32[64,128]{1,0:T(8,128)S(1)}, f32[64,128]{1,0:T(8,128)S(1)}, u32[]{:S(2)}, u32[]{:S(2)}) collective-permute-start(f32[64,128]{1,0:T(8,128)S(1)} %add.15.refs_0_), channel_id=1, source_target_pairs={{0,16},{4,20},{8,24},{12,28},{16,0},{20,4},{24,8},{28,12},{1,17},{... | collective-permute-start | bytes 98312 | tf_op jit(solution)/shard_map/ppermute | solution.py:198
  74.3 3.9 %collective-permute-start.18 = (f32[64,128]{1,0:T(8,128)S(1)}, f32[64,128]{1,0:T(8,128)S(1)}, u32[]{:S(2)}, u32[]{:S(2)}) collective-permute-start(f32[64,128]{1,0:T(8,128)S(1)} %add.15.refs_0_), channel_id=1, source_target_pairs={{0,8},{4,12},{8,0},{12,4},{16,24},{20,28},{24,16},{28,20},{1,9},{5... | collective-permute-start | bytes 98312 | tf_op jit(solution)/shard_map/ppermute | solution.py:198

commit v9 on v8

--- a/solution.py
+++ b/solution.py
@@ -11,7 +11,7 @@
 LANES = 128
 CHUNK = 16
 VMEM_LIMIT = 24 * 2**20
-JAC_VMEM_LIMIT = 60 * 2**20
+FAR_VMEM_LIMIT = 60 * 2**20
 shift_ratio = 0.1
 F32 = jnp.float32
 BF16 = jnp.bfloat16
@@ -78,7 +78,9 @@
             pltpu.VMEM((samples, mats, d // 2, d), F32),
             pltpu.SemaphoreType.DMA((2, samples)),
         ],
-        compiler_params=pltpu.CompilerParams(vmem_limit_bytes=JAC_VMEM_LIMIT),
+        compiler_params=pltpu.CompilerParams(
+            vmem_limit_bytes=FAR_VMEM_LIMIT if far else VMEM_LIMIT
+        ),
         cost_estimate=pl.CostEstimate(
             flops=samples * mats * sites * d * d,
             bytes_accessed=4 * samples * mats * sites * d,
@@ -280,8 +282,7 @@
     owners = lax.axis_size("samp")
     total = local * owners
     width = (total // LANES + 1) * LANES
-    share = activations.shape[3] // owners
-    parts = mats if share % CHUNK == 0 else 1
+    parts = 1
     far = jac_rows(activations, cotangents, owners, parts, True)
     near = jac_rows(activations, cotangents, owners, parts, False)
     held = exchange(far, near)

time: 85.3 us -> 88.5 us (1.038)
  waiting for transfers between devices: 27.8 us -> 42 us
  starting transfers between devices: 38.9 us -> 28.7 us
  Pallas kernels: 15.7 us -> 13.6 us
  local copies, waits for them, and re-layouts: 1.92 us -> 3.26 us
    ppermute x14 -> x7, starting transfers between devices: 31.1 us -> 12.5 us  [exchange(): lax.ppermute(block, 'samp', [(i, i ^ k) for i in range(owners)])]
    ppermute x14 -> x7, waiting for transfers between devices: 19.9 us -> 31.6 us  [exchange(): lax.ppermute(block, 'samp', [(i, i ^ k) for i in range(owners)])]
    ppermute x7, starting transfers between devices: 7.81 us -> 16.2 us  [partners(): parts.append(lax.ppermute(value, axis, perm))]
    ppermute x7, waiting for transfers between devices: 7.93 us -> 10.4 us  [partners(): parts.append(lax.ppermute(value, axis, perm))]
    pallas_call x2, Pallas kernels: 6.83 us -> 5.14 us  [jac_rows(): pl.pallas_call(functools.partial(jac_kernel, far, parts), in_specs=[hbm,...]
    unnamed x16 -> x8, local copies, waits for them, and re-layouts: 1.84 us -> 3.18 us
  transfers between devices with their start and end apart: 21 -> 14, of which waited for: 12 -> 9; matrix products, arithmetic and copies ran while one was open for 0% -> 0% of each run, Pallas kernels for 5% -> 4%
where the time goes in v9:
time: 88.5 us; the launch traced here: 88.3 us
  waiting for transfers between devices  42 us (47%)
  starting transfers between devices  28.7 us (32%)
  Pallas kernels  13.6 us (15%)
  local copies, waits for them, and re-layouts  3.26 us (4%)
    ppermute x7, waiting for transfers between devices, exchange(): lax.ppermute(block, 'samp', [(i, i ^ k) for i in range(owners)])  31.6 us
    ppermute x7, starting transfers between devices, partners(): parts.append(lax.ppermute(value, axis, perm))  16.2 us
    ppermute x7, starting transfers between devices, exchange(): lax.ppermute(block, 'samp', [(i, i ^ k) for i in range(owners)])  12.5 us
    ppermute x7, waiting for transfers between devices, partners(): parts.append(lax.ppermute(value, axis, perm))  10.4 us
    pallas_call x1, Pallas kernels, solve_and_project(): pl.pallas_call(functools.partial(solve_kernel, owners), out_shape=(jax.Sh...  6.8 us
    pallas_call x2, Pallas kernels, jac_rows(): pl.pallas_call(functools.partial(jac_kernel, far, parts), in_specs=[hbm,...  5.14 us
    unnamed x8, local copies, waits for them, and re-layouts  3.18 us
  transfers between devices with their start and end apart: 14, of which 9 were waited for; matrix products, arithmetic and copies ran while one was open for 0% of the time, Pallas kernels for 4%

profile of v9, /device:TPU:0, one launch (start us, length us, event | category | flops | bytes accessed | tf_op | source)
XLA Modules:
  0.0 88.3 jit_solution(3777838160385702250)
XLA Ops:
  0.6 0.0 copy-start
  0.6 1.6 %copy-done = bf16[8,2,256,256]{3,2,1,0:T(8,128)(2,1)S(1)} copy-done((bf16[8,2,256,256]{3,2,1,0:T(8,128)(2,1)S(1)}, bf16[8,2,256,256]{3,2,1,0:T(8,128)(2,1)}, u32[]{:S(2)}) %copy-start) | copy-done | bytes 2097176
  2.2 0.0 copy-start.1
  2.2 1.6 %copy-done.1 = bf16[8,2,256,256]{3,2,1,0:T(8,128)(2,1)S(1)} copy-done((bf16[8,2,256,256]{3,2,1,0:T(8,128)(2,1)S(1)}, bf16[8,2,256,256]{3,2,1,0:T(8,128)(2,1)}, u32[]{:S(2)}) %copy-start.1) | copy-done | bytes 2097176
  3.8 1.7 %near_rows.1 = (bf16[8,64,256]{2,1,0:T(8,128)(2,1)S(1)}, bf16[8,64,256]{2,1,0:T(8,128)(2,1)S(1)}, bf16[8,64,256]{2,1,0:T(8,128)(2,1)S(1)}, bf16[8,64,256]{2,1,0:T(8,128)(2,1)S(1)}) custom-call(bf16[8,2,256,256]{3,2,1,0:T(8,128)(2,1)S(1)} %copy-done, bf16[8,2,256,256]{3,2,1,0:T(8,128)(2,1)S(1)} %copy-done.1), custom_call_target="tpu_custom_call" | custom-call | flops 268435456 | bytes 4194304 | tf_op jit(solution)/shard_map/near_rows/pallas_call | solution.py:71
  5.5 3.0 %collective-permute-start = (bf16[8,64,256]{2,1,0:T(8,128)(2,1)S(1)}, bf16[8,64,256]{2,1,0:T(8,128)(2,1)S(1)}, u32[]{:S(2)}, u32[]{:S(2)}) collective-permute-start(bf16[8,64,256]{2,1,0:T(8,128)(2,1)S(1)} %get-tuple-element.13), channel_id=1, source_target_pairs={{0,4},{4,0},{8,12},{12,8},{16,20},{20,16},{24,28},{28,24},{1,5},{5... | collective-permute-start | bytes 786440 | tf_op jit(solution)/shard_map/ppermute | solution.py:276
  8.5 1.6 %collective-permute-start.1 = (bf16[8,64,256]{2,1,0:T(8,128)(2,1)S(1)}, bf16[8,64,256]{2,1,0:T(8,128)(2,1)S(1)}, u32[]{:S(2)}, u32[]{:S(2)}) collective-permute-start(bf16[8,64,256]{2,1,0:T(8,128)(2,1)S(1)} %get-tuple-element.14), channel_id=1, source_target_pairs={{0,8},{4,12},{8,0},{12,4},{16,24},{20,28},{24,16},{28,20},{1,9},{5... | collective-permute-start | bytes 786440 | tf_op jit(solution)/shard_map/ppermute | solution.py:276
  10.1 0.0 copy-start.3
  10.1 0.0 copy-start.2
  10.1 0.0 collective-permute-start.2
  10.1 3.4 %far_rows.1 = (bf16[8,64,256]{2,1,0:T(8,128)(2,1)}, bf16[8,64,256]{2,1,0:T(8,128)(2,1)}, bf16[8,64,256]{2,1,0:T(8,128)(2,1)}, bf16[8,64,256]{2,1,0:T(8,128)(2,1)}) custom-call(bf16[8,2,256,256]{3,2,1,0:T(8,128)(2,1)} %act_hbm.3, bf16[8,2,256,256]{3,2,1,0:T(8,128)(2,1)} %cot_hbm.3), custom_call_target="tpu_custom_call" | custom-call | flops 268435456 | bytes 4194304 | tf_op jit(solution)/shard_map/far_rows/pallas_call | solution.py:71
  13.6 3.0 %collective-permute-start.3 = (bf16[8,64,256]{2,1,0:T(8,128)(2,1)}, bf16[8,64,256]{2,1,0:T(8,128)(2,1)S(1)}, u32[]{:S(2)}, u32[]{:S(2)}) collective-permute-start(bf16[8,64,256]{2,1,0:T(8,128)(2,1)} %get-tuple-element.16), channel_id=1, source_target_pairs={{0,16},{4,20},{8,24},{12,28},{16,0},{20,4},{24,8},{28,12},{1,17},{... | collective-permute-start | bytes 786440 | tf_op jit(solution)/shard_map/ppermute | solution.py:276
  16.6 1.3 %collective-permute-start.4 = (bf16[8,64,256]{2,1,0:T(8,128)(2,1)}, bf16[8,64,256]{2,1,0:T(8,128)(2,1)S(1)}, u32[]{:S(2)}, u32[]{:S(2)}) collective-permute-start(bf16[8,64,256]{2,1,0:T(8,128)(2,1)} %get-tuple-element.17), channel_id=1, source_target_pairs={{0,20},{4,16},{8,28},{12,24},{16,4},{20,0},{24,12},{28,8},{1,21},{... | collective-permute-start | bytes 786440 | tf_op jit(solution)/shard_map/ppermute | solution.py:276
  17.9 0.0 collective-permute-done.refs_1_.refs_5_
  17.9 3.6 %collective-permute-start.5 = (bf16[8,64,256]{2,1,0:T(8,128)(2,1)}, bf16[8,64,256]{2,1,0:T(8,128)(2,1)S(1)}, u32[]{:S(2)}, u32[]{:S(2)}) collective-permute-start(bf16[8,64,256]{2,1,0:T(8,128)(2,1)} %get-tuple-element.18), channel_id=1, source_target_pairs={{0,24},{4,28},{8,16},{12,20},{16,8},{20,12},{24,0},{28,4},{1,25},{... | collective-permute-start | bytes 786440 | tf_op jit(solution)/shard_map/ppermute | solution.py:276
  21.5 3.1 %collective-permute-done.1.refs_2_.refs_6_ = bf16[8,64,256]{2,1,0:T(8,128)(2,1)S(1)} collective-permute-done((bf16[8,64,256]{2,1,0:T(8,128)(2,1)S(1)}, bf16[8,64,256]{2,1,0:T(8,128)(2,1)S(1)}, u32[]{:S(2)}, u32[]{:S(2)}) %collective-permute-start.1) | collective-permute-done | bytes 262176 | tf_op jit(solution)/shard_map/ppermute | solution.py:276
  24.6 0.0 collective-permute-start.6
  24.6 0.0 copy-done.3
  24.6 0.1 copy.6.offdiag_ref
  24.7 0.0 copy-done.2
  24.7 0.2 energy_column.1.refs_8_
  24.9 3.1 %collective-permute-done.2.refs_3_.refs_7_ = bf16[8,64,256]{2,1,0:T(8,128)(2,1)S(1)} collective-permute-done((bf16[8,64,256]{2,1,0:T(8,128)(2,1)S(1)}, bf16[8,64,256]{2,1,0:T(8,128)(2,1)S(1)}, u32[]{:S(2)}, u32[]{:S(2)}) %collective-permute-start.2) | collective-permute-done | bytes 262176 | tf_op jit(solution)/shard_map/ppermute | solution.py:276
  28.0 0.3 collective-permute-done.3.refs_4_.refs_8_
  28.3 25.2 %collective-permute-done.4.refs_5_.refs_9_ = bf16[8,64,256]{2,1,0:T(8,128)(2,1)S(1)} collective-permute-done((bf16[8,64,256]{2,1,0:T(8,128)(2,1)}, bf16[8,64,256]{2,1,0:T(8,128)(2,1)S(1)}, u32[]{:S(2)}, u32[]{:S(2)}) %collective-permute-start.4) | collective-permute-done | bytes 262176 | tf_op jit(solution)/shard_map/ppermute | solution.py:276
  53.4 0.0 collective-permute-done.5.refs_6_.refs_10_
  53.4 0.0 collective-permute-done.6.refs_7_.refs_11_
  53.4 1.4 %gram_partial.1 = f32[64,128]{1,0:T(8,128)S(1)} custom-call(bf16[8,64,256]{2,1,0:T(8,128)(2,1)S(1)} %get-tuple-element.12.refs_0_.refs_4_, bf16[8,64,256]{2,1,0:T(8,128)(2,1)S(1)} %collective-permute-done.refs_1_.refs_5_, bf16[8,64,256]{2,1,0:T(8,128)(2,1)S(1)} %collective-permute-done.1.refs_2_.refs_6_, ...), custom_call_target="tpu_custom_call" | custom-call | flops 134217728 | bytes 2097152 | tf_op jit(solution)/shard_map/gram_partial/pallas_call | solution.py:151
  54.9 1.6 %collective-permute-start.8 = (f32[64,128]{1,0:T(8,128)S(1)}, f32[64,128]{1,0:T(8,128)S(1)}, u32[]{:S(2)}, u32[]{:S(2)}) collective-permute-start(f32[64,128]{1,0:T(8,128)S(1)} %gram_partial.1), channel_id=1, source_target_pairs={{0,2},{1,3},{2,0},{3,1},{4,6},{5,7},{6,4},{7,5},{8,10},{9,11},{10,... | collective-permute-start | bytes 98312 | tf_op jit(solution)/shard_map/ppermute | solution.py:200
  56.4 0.0 collective-permute-start.9
  56.4 0.6 collective-permute-start.7
  57.1 1.8 %collective-permute-done.8 = f32[64,128]{1,0:T(8,128)S(1)} collective-permute-done((f32[64,128]{1,0:T(8,128)S(1)}, f32[64,128]{1,0:T(8,128)S(1)}, u32[]{:S(2)}, u32[]{:S(2)}) %collective-permute-start.8) | collective-permute-done | bytes 32800 | tf_op jit(solution)/shard_map/ppermute | solution.py:200
  58.9 0.9 %collective-permute-done.9 = f32[64,128]{1,0:T(8,128)S(1)} collective-permute-done((f32[64,128]{1,0:T(8,128)S(1)}, f32[64,128]{1,0:T(8,128)S(1)}, u32[]{:S(2)}, u32[]{:S(2)}) %collective-permute-start.9) | collective-permute-done | bytes 32800 | tf_op jit(solution)/shard_map/ppermute | solution.py:200
  59.8 0.0 collective-permute-done.7
  59.8 0.6 collective-permute-start.10
  60.4 3.4 %collective-permute-done.10 = f32[64,128]{1,0:T(8,128)S(1)} collective-permute-done((f32[64,128]{1,0:T(8,128)S(1)}, f32[64,128]{1,0:T(8,128)S(1)}, u32[]{:S(2)}, u32[]{:S(2)}) %collective-permute-start.10) | collective-permute-done | bytes 32800 | tf_op jit(solution)/shard_map/ppermute | solution.py:200
  63.8 9.8 %collective-permute-start.11 = (f32[64,128]{1,0:T(8,128)S(1)}, f32[64,128]{1,0:T(8,128)S(1)}, u32[]{:S(2)}, u32[]{:S(2)}) collective-permute-start(f32[64,128]{1,0:T(8,128)S(1)} %add.15.refs_0_), channel_id=1, source_target_pairs={{0,8},{4,12},{8,0},{12,4},{16,24},{20,28},{24,16},{28,20},{1,9},{5... | collective-permute-start | bytes 98312 | tf_op jit(solution)/shard_map/ppermute | solution.py:200
  73.6 2.2 %collective-permute-start.12 = (f32[64,128]{1,0:T(8,128)S(1)}, f32[64,128]{1,0:T(8,128)S(1)}, u32[]{:S(2)}, u32[]{:S(2)}) collective-permute-start(f32[64,128]{1,0:T(8,128)S(1)} %add.15.refs_0_), channel_id=1, source_target_pairs={{0,16},{4,20},{8,24},{12,28},{16,0},{20,4},{24,8},{28,12},{1,17},{... | collective-permute-start | bytes 98312 | tf_op jit(solution)/shard_map/ppermute | solution.py:200
  75.8 1.4 %collective-permute-start.13 = (f32[64,128]{1,0:T(8,128)S(1)}, f32[64,128]{1,0:T(8,128)S(1)}, u32[]{:S(2)}, u32[]{:S(2)}) collective-permute-start(f32[64,128]{1,0:T(8,128)S(1)} %add.15.refs_0_), channel_id=1, source_target_pairs={{0,24},{4,28},{8,16},{12,20},{16,8},{20,12},{24,0},{28,4},{1,25},{... | collective-permute-start | bytes 98312 | tf_op jit(solution)/shard_map/ppermute | solution.py:200
  77.2 0.0 collective-permute-done.11.refs_1_
  77.2 1.5 %collective-permute-done.12.refs_2_ = f32[64,128]{1,0:T(8,128)S(1)} collective-permute-done((f32[64,128]{1,0:T(8,128)S(1)}, f32[64,128]{1,0:T(8,128)S(1)}, u32[]{:S(2)}, u32[]{:S(2)}) %collective-permute-start.12) | collective-permute-done | bytes 32800 | tf_op jit(solution)/shard_map/ppermute | solution.py:200
  78.7 2.8 %collective-permute-done.13.refs_3_ = f32[64,128]{1,0:T(8,128)S(1)} collective-permute-done((f32[64,128]{1,0:T(8,128)S(1)}, f32[64,128]{1,0:T(8,128)S(1)}, u32[]{:S(2)}, u32[]{:S(2)}) %collective-permute-start.13) | collective-permute-done | bytes 32800 | tf_op jit(solution)/shard_map/ppermute | solution.py:200
  81.5 6.8 %solve_and_project.1 = (f32[1,8]{1,0:T(1,128)}, f32[2,32,256]{2,1,0:T(8,128)}) custom-call(f32[64,128]{1,0:T(8,128)S(1)} %add.15.refs_0_, f32[64,128]{1,0:T(8,128)S(1)} %collective-permute-done.11.refs_1_, f32[64,128]{1,0:T(8,128)S(1)} %collective-permute-done.12.refs_2_, f32[64,128]{1,0:T(8,128)S(1)} %collective-permute-done.13.refs_3_, ...), custom_call_target="tpu_custom_call" | custom-call | tf_op jit(solution)/shard_map/solve_and_project/pallas_call | solution.py:250
  (2 shorter events, 0.0 us)
Async XLA Ops:
  0.6 1.6 %copy-start = (bf16[8,2,256,256]{3,2,1,0:T(8,128)(2,1)S(1)}, bf16[8,2,256,256]{3,2,1,0:T(8,128)(2,1)}, u32[]{:S(2)}) copy-start(bf16[8,2,256,256]{3,2,1,0:T(8,128)(2,1)} %act_hbm.3) | copy-start | bytes 6291460
  2.2 1.6 %copy-start.1 = (bf16[8,2,256,256]{3,2,1,0:T(8,128)(2,1)S(1)}, bf16[8,2,256,256]{3,2,1,0:T(8,128)(2,1)}, u32[]{:S(2)}) copy-start(bf16[8,2,256,256]{3,2,1,0:T(8,128)(2,1)} %cot_hbm.3) | copy-start | bytes 6291460
  5.5 12.4 %collective-permute-start = (bf16[8,64,256]{2,1,0:T(8,128)(2,1)S(1)}, bf16[8,64,256]{2,1,0:T(8,128)(2,1)S(1)}, u32[]{:S(2)}, u32[]{:S(2)}) collective-permute-start(bf16[8,64,256]{2,1,0:T(8,128)(2,1)S(1)} %get-tuple-element.13), channel_id=1, source_target_pairs={{0,4},{4,0},{8,12},{12,8},{16,20},{20,16},{24,28},{28,24},{1,5},{5... | collective-permute-start | bytes 786440 | tf_op jit(solution)/shard_map/ppermute | solution.py:276
  8.5 16.1 %collective-permute-start.1 = (bf16[8,64,256]{2,1,0:T(8,128)(2,1)S(1)}, bf16[8,64,256]{2,1,0:T(8,128)(2,1)S(1)}, u32[]{:S(2)}, u32[]{:S(2)}) collective-permute-start(bf16[8,64,256]{2,1,0:T(8,128)(2,1)S(1)} %get-tuple-element.14), channel_id=1, source_target_pairs={{0,8},{4,12},{8,0},{12,4},{16,24},{20,28},{24,16},{28,20},{1,9},{5... | collective-permute-start | bytes 786440 | tf_op jit(solution)/shard_map/ppermute | solution.py:276
  10.1 14.5 %copy-start.3 = (f32[8]{0:T(128)S(1)}, f32[8]{0:T(128)}, u32[]{:S(2)}) copy-start(f32[8]{0:T(128)} %param.7) | copy-start | bytes 100
  10.1 14.6 %copy-start.2 = (s32[8,256]{1,0:T(8,128)S(1)}, s32[8,256]{1,0:T(8,128)}, u32[]{:S(2)}) copy-start(s32[8,256]{1,0:T(8,128)} %spins_ref.1) | copy-start | bytes 24580
  10.1 17.9 %collective-permute-start.2 = (bf16[8,64,256]{2,1,0:T(8,128)(2,1)S(1)}, bf16[8,64,256]{2,1,0:T(8,128)(2,1)S(1)}, u32[]{:S(2)}, u32[]{:S(2)}) collective-permute-start(bf16[8,64,256]{2,1,0:T(8,128)(2,1)S(1)} %get-tuple-element.15), channel_id=1, source_target_pairs={{0,12},{4,8},{8,4},{12,0},{16,28},{20,24},{24,20},{28,16},{1,13},{... | collective-permute-start | bytes 786440 | tf_op jit(solution)/shard_map/ppermute | solution.py:276
  13.6 14.7 %collective-permute-start.3 = (bf16[8,64,256]{2,1,0:T(8,128)(2,1)}, bf16[8,64,256]{2,1,0:T(8,128)(2,1)S(1)}, u32[]{:S(2)}, u32[]{:S(2)}) collective-permute-start(bf16[8,64,256]{2,1,0:T(8,128)(2,1)} %get-tuple-element.16), channel_id=1, source_target_pairs={{0,16},{4,20},{8,24},{12,28},{16,0},{20,4},{24,8},{28,12},{1,17},{... | collective-permute-start | bytes 786440 | tf_op jit(solution)/shard_map/ppermute | solution.py:276
  16.6 36.8 %collective-permute-start.4 = (bf16[8,64,256]{2,1,0:T(8,128)(2,1)}, bf16[8,64,256]{2,1,0:T(8,128)(2,1)S(1)}, u32[]{:S(2)}, u32[]{:S(2)}) collective-permute-start(bf16[8,64,256]{2,1,0:T(8,128)(2,1)} %get-tuple-element.17), channel_id=1, source_target_pairs={{0,20},{4,16},{8,28},{12,24},{16,4},{20,0},{24,12},{28,8},{1,21},{... | collective-permute-start | bytes 786440 | tf_op jit(solution)/shard_map/ppermute | solution.py:276
  17.9 35.5 %collective-permute-start.5 = (bf16[8,64,256]{2,1,0:T(8,128)(2,1)}, bf16[8,64,256]{2,1,0:T(8,128)(2,1)S(1)}, u32[]{:S(2)}, u32[]{:S(2)}) collective-permute-start(bf16[8,64,256]{2,1,0:T(8,128)(2,1)} %get-tuple-element.18), channel_id=1, source_target_pairs={{0,24},{4,28},{8,16},{12,20},{16,8},{20,12},{24,0},{28,4},{1,25},{... | collective-permute-start | bytes 786440 | tf_op jit(solution)/shard_map/ppermute | solution.py:276
  24.6 28.8 %collective-permute-start.6 = (bf16[8,64,256]{2,1,0:T(8,128)(2,1)}, bf16[8,64,256]{2,1,0:T(8,128)(2,1)S(1)}, u32[]{:S(2)}, u32[]{:S(2)}) collective-permute-start(bf16[8,64,256]{2,1,0:T(8,128)(2,1)} %get-tuple-element.19), channel_id=1, source_target_pairs={{0,28},{4,24},{8,20},{12,16},{16,12},{20,8},{24,4},{28,0},{1,29},{... | collective-permute-start | bytes 786440 | tf_op jit(solution)/shard_map/ppermute | solution.py:276
  54.9 4.0 %collective-permute-start.8 = (f32[64,128]{1,0:T(8,128)S(1)}, f32[64,128]{1,0:T(8,128)S(1)}, u32[]{:S(2)}, u32[]{:S(2)}) collective-permute-start(f32[64,128]{1,0:T(8,128)S(1)} %gram_partial.1), channel_id=1, source_target_pairs={{0,2},{1,3},{2,0},{3,1},{4,6},{5,7},{6,4},{7,5},{8,10},{9,11},{10,... | collective-permute-start | bytes 98312 | tf_op jit(solution)/shard_map/ppermute | solution.py:200
  56.4 3.3 %collective-permute-start.9 = (f32[64,128]{1,0:T(8,128)S(1)}, f32[64,128]{1,0:T(8,128)S(1)}, u32[]{:S(2)}, u32[]{:S(2)}) collective-permute-start(f32[64,128]{1,0:T(8,128)S(1)} %gram_partial.1), channel_id=1, source_target_pairs={{0,3},{1,2},{2,1},{3,0},{4,7},{5,6},{6,5},{7,4},{8,11},{9,10},{10,... | collective-permute-start | bytes 98312 | tf_op jit(solution)/shard_map/ppermute | solution.py:200
  56.4 3.3 %collective-permute-start.7 = (f32[64,128]{1,0:T(8,128)S(1)}, f32[64,128]{1,0:T(8,128)S(1)}, u32[]{:S(2)}, u32[]{:S(2)}) collective-permute-start(f32[64,128]{1,0:T(8,128)S(1)} %gram_partial.1), channel_id=1, source_target_pairs={{0,1},{1,0},{2,3},{3,2},{4,5},{5,4},{6,7},{7,6},{8,9},{9,8},{10,11... | collective-permute-start | bytes 98312 | tf_op jit(solution)/shard_map/ppermute | solution.py:200
  59.8 4.0 %collective-permute-start.10 = (f32[64,128]{1,0:T(8,128)S(1)}, f32[64,128]{1,0:T(8,128)S(1)}, u32[]{:S(2)}, u32[]{:S(2)}) collective-permute-start(f32[64,128]{1,0:T(8,128)S(1)} %add_add_fusion), channel_id=1, source_target_pairs={{0,4},{4,0},{8,12},{12,8},{16,20},{20,16},{24,28},{28,24},{1,5},{5... | collective-permute-start | bytes 98312 | tf_op jit(solution)/shard_map/ppermute | solution.py:200
  63.8 13.4 %collective-permute-start.11 = (f32[64,128]{1,0:T(8,128)S(1)}, f32[64,128]{1,0:T(8,128)S(1)}, u32[]{:S(2)}, u32[]{:S(2)}) collective-permute-start(f32[64,128]{1,0:T(8,128)S(1)} %add.15.refs_0_), channel_id=1, source_target_pairs={{0,8},{4,12},{8,0},{12,4},{16,24},{20,28},{24,16},{28,20},{1,9},{5... | collective-permute-start | bytes 98312 | tf_op jit(solution)/shard_map/ppermute | solution.py:200
  73.6 5.1 %collective-permute-start.12 = (f32[64,128]{1,0:T(8,128)S(1)}, f32[64,128]{1,0:T(8,128)S(1)}, u32[]{:S(2)}, u32[]{:S(2)}) collective-permute-start(f32[64,128]{1,0:T(8,128)S(1)} %add.15.refs_0_), channel_id=1, source_target_pairs={{0,16},{4,20},{8,24},{12,28},{16,0},{20,4},{24,8},{28,12},{1,17},{... | collective-permute-start | bytes 98312 | tf_op jit(solution)/shard_map/ppermute | solution.py:200
  75.8 5.7 %collective-permute-start.13 = (f32[64,128]{1,0:T(8,128)S(1)}, f32[64,128]{1,0:T(8,128)S(1)}, u32[]{:S(2)}, u32[]{:S(2)}) collective-permute-start(f32[64,128]{1,0:T(8,128)S(1)} %add.15.refs_0_), channel_id=1, source_target_pairs={{0,24},{4,28},{8,16},{12,20},{16,8},{20,12},{24,0},{28,4},{1,25},{... | collective-permute-start | bytes 98312 | tf_op jit(solution)/shard_map/ppermute | solution.py:200

commit v10 on v5

--- a/solution.py
+++ b/solution.py
@@ -11,6 +11,7 @@
 LANES = 128
 CHUNK = 16
 VMEM_LIMIT = 24 * 2**20
+JAC_VMEM_LIMIT = 52 * 2**20
 shift_ratio = 0.1
 F32 = jnp.float32
 BF16 = jnp.bfloat16
@@ -20,41 +21,48 @@
     return lax.broadcasted_iota(jnp.int32, shape, dim)
 
 
-def jac_kernel(first, act_hbm, cot_hbm, *refs):
+def jac_kernel(act_hbm, cot_hbm, *refs):
     *out_refs, act_buf, cot_buf, held, sems = refs
     samples, mats = act_buf.shape[:2]
     share = out_refs[0].shape[1] // mats
     me = lax.axis_index("samp")
     copies = []
     for s in range(samples):
-        here = (s, pl.ds(first, mats))
-        copies.append(pltpu.make_async_copy(act_hbm.at[here], act_buf.at[s], sems.at[0, s]))
-        copies.append(pltpu.make_async_copy(cot_hbm.at[here], cot_buf.at[s], sems.at[1, s]))
-    for copy in copies:
-        copy.start()
-    for s in range(samples):
-        copies[2 * s].wait()
-        copies[2 * s + 1].wait()
-        for m in range(mats):
-            held[s, m] = lax.dot_general(
-                act_buf[s, m],
-                cot_buf[s, m],
-                (((0,), (0,)), ((), ())),
-                preferred_element_type=F32,
+        copies.append(
+            (
+                pltpu.make_async_copy(act_hbm.at[s], act_buf.at[s], sems.at[0, s]),
+                pltpu.make_async_copy(cot_hbm.at[s], cot_buf.at[s], sems.at[1, s]),
             )
-        for k, out_ref in enumerate(out_refs):
-            owned = pl.ds(pl.multiple_of((me ^ k) * share, share), share)
+        )
+    for pair in copies:
+        for copy in pair:
+            copy.start()
+    group = 2
+    for first in range(0, samples, group):
+        for s in range(first, first + group):
+            for copy in copies[s]:
+                copy.wait()
+        for s in range(first, first + group):
+            for m in range(mats):
+                held[s, m] = lax.dot_general(
+                    act_buf[s, m],
+                    cot_buf[s, m],
+                    (((0,), (0,)), ((), ())),
+                    preferred_element_type=F32,
+                )
+    for k, out_ref in enumerate(out_refs):
+        owned = pl.ds(pl.multiple_of((me ^ k) * share, share), share)
+        for s in range(samples):
             rows = [held[s, m, owned] for m in range(mats)]
             out_ref[s] = jnp.concatenate(rows, axis=0).astype(BF16)
 
 
-def jac_rows(activations, cotangents, owners, part, parts):
+def jac_rows(activations, cotangents, owners):
     samples, mats, sites, d = activations.shape
-    mats //= parts
     rows = mats * d // owners
     hbm = pl.BlockSpec(memory_space=pltpu.HBM)
     return pl.pallas_call(
-        functools.partial(jac_kernel, part * mats),
+        jac_kernel,
         in_specs=[hbm, hbm],
         out_shape=[jax.ShapeDtypeStruct((samples, rows, d), BF16)] * owners,
         scratch_shapes=[
@@ -63,7 +71,7 @@
             pltpu.VMEM((samples, mats, d, d), F32),
             pltpu.SemaphoreType.DMA((2, samples)),
         ],
-        compiler_params=pltpu.CompilerParams(vmem_limit_bytes=VMEM_LIMIT),
+        compiler_params=pltpu.CompilerParams(vmem_limit_bytes=JAC_VMEM_LIMIT),
         cost_estimate=pl.CostEstimate(
             flops=2 * samples * mats * sites * d * d,
             bytes_accessed=6 * samples * mats * sites * d,
@@ -103,6 +111,7 @@
 
 def gram_kernel(*refs):
     *block_refs, start_ref, out_ref, flat = refs
+    block_refs = block_refs[::-1]
     local, count, d = block_refs[0].shape
     total = local * len(block_refs)
     joined = CHUNK // local
@@ -141,7 +150,7 @@
             transcendentals=0,
         ),
         name="gram_partial",
-    )(*blocks, start)
+    )(*blocks[::-1], start)
 
 
 def eliminate(matrix, total):
@@ -183,12 +192,11 @@
     return parts
 
 
-def solve_kernel(owners, *refs):
-    *in_refs, weights_ref, update_ref, held = refs
+def solve_kernel(grams, *refs):
+    gram_refs, (*block_refs, weights_ref, update_ref, held) = refs[:grams], refs[grams:]
+    block_refs = block_refs[::-1]
     mats, share, d = update_ref.shape
     local = weights_ref.shape[1]
-    gram_refs = [ref for ref in in_refs if len(ref.shape) == 2]
-    block_refs = [ref for ref in in_refs if len(ref.shape) == 3]
     total, width = gram_refs[0].shape
     raw = tree_sum([ref[...] for ref in gram_refs])
     row = iota((total, width), 0)
@@ -212,33 +220,28 @@
     weights_ref[...] = jnp.sum(own, axis=0, keepdims=True)[:, :local]
     coeffs = weights - jnp.sum(weights, axis=0, keepdims=True) * scale
     held[...] = jnp.broadcast_to(coeffs, (total, d))
-    parts = len(block_refs) // owners
-    each = mats // parts
-    for part in range(parts):
-        acc = jnp.zeros((each * share, d), F32)
-        for k in range(owners):
-            mine = held[pl.ds(pl.multiple_of((me ^ k) * local, local), local)]
-            for s in range(local):
-                acc = acc + mine[s : s + 1] * block_refs[part * owners + k][s].astype(F32)
-        for m in range(each):
-            update_ref[part * each + m] = acc[m * share : (m + 1) * share]
-
-
-def solve_and_project(grams, parts, mats):
+    acc = jnp.zeros((mats * share, d), F32)
+    for k, block_ref in enumerate(block_refs):
+        mine = held[pl.ds(pl.multiple_of((me ^ k) * local, local), local)]
+        for s in range(local):
+            acc = acc + mine[s : s + 1] * block_ref[s].astype(F32)
+    for m in range(mats):
+        update_ref[m] = acc[m * share : (m + 1) * share]
+
+
+def solve_and_project(grams, blocks, mats):
     total, width = grams[0].shape
-    owners = len(parts[0])
-    local, count, d = parts[0][0].shape
-    share = count * len(parts) // mats
-    return pl.pallas_call(
-        functools.partial(solve_kernel, owners),
+    local, count, d = blocks[0].shape
+    return pl.pallas_call(
+        functools.partial(solve_kernel, len(grams)),
         out_shape=(
             jax.ShapeDtypeStruct((1, local), F32),
-            jax.ShapeDtypeStruct((mats, share, d), F32),
+            jax.ShapeDtypeStruct((mats, count // mats, d), F32),
         ),
         scratch_shapes=[pltpu.VMEM((total, d), F32)],
         compiler_params=pltpu.CompilerParams(vmem_limit_bytes=VMEM_LIMIT),
         name="solve_and_project",
-    )(*grams, *[block for blocks in parts for block in blocks])
+    )(*grams, *blocks[::-1])
 
 
 def body(spins, activations, cotangents, offdiag):
@@ -246,25 +249,17 @@
     owners = lax.axis_size("samp")
     total = local * owners
     width = (total // LANES + 1) * LANES
-    share = activations.shape[3] // owners
-    parts = mats if share % CHUNK == 0 else 1
-    partial = energy_column(spins, offdiag, total, width)
-    held = []
-    for part in range(parts):
-        blocks = list(jac_rows(activations, cotangents, owners, part, parts))
-        for k in range(owners - 1, 0, -1):
-            perm = [(i, i ^ k) for i in range(owners)]
-            blocks[k] = lax.ppermute(blocks[k], "samp", perm)
-        held.append(blocks)
-    for blocks in held:
-        partial = gram_partial(blocks, partial)
+    blocks = list(jac_rows(activations, cotangents, owners))
+    for k in range(owners - 1, 0, -1):
+        blocks[k] = lax.ppermute(blocks[k], "samp", [(i, i ^ k) for i in range(owners)])
+    partial = gram_partial(blocks, energy_column(spins, offdiag, total, width))
     grams = partners(partial, "layer", 1, lax.axis_size("layer"))
     first = 1
     while first < owners:
         count = 2 if first == 1 else min(4, owners // first)
         grams = partners(tree_sum(grams), "samp", first, count)
         first *= count
-    weights, update = solve_and_project(grams, held, mats)
+    weights, update = solve_and_project(grams, blocks, mats)
     return weights.reshape(local), update
 
 

time: 84.9 us -> 83.9 us (0.988)
  Pallas kernels: 18.6 us -> 12.1 us
  waiting for transfers between devices: 20.4 us -> 25.6 us
  starting transfers between devices: 41.8 us -> 45.2 us
  local copies, waits for them, and re-layouts: 3.26 us -> 0.09 us
    pallas_call x3 -> x2, Pallas kernels: 16.6 us -> 10.4 us  [the longest x1 6.8 us: solve_and_project(): pl.pallas_call(functools.partial(solve_kernel, len(grams)), out_shape=(ja...]
    ppermute x14 -> x7, starting transfers between devices: 31.6 us -> 37.2 us  [body(): lax.ppermute(blocks[k], 'samp', [(i, i ^ k) for i in range(owners)])]
    ppermute x14 -> x7, waiting for transfers between devices: 12 us -> 16.1 us  [body(): lax.ppermute(blocks[k], 'samp', [(i, i ^ k) for i in range(owners)])]
    unnamed x8 -> x4, local copies, waits for them, and re-layouts: 3.18 us -> 0.01 us
    ppermute x7, starting transfers between devices: 10.1 us -> 7.97 us  [partners(): parts.append(lax.ppermute(value, axis, perm))]
    ppermute x7, waiting for transfers between devices: 8.42 us -> 9.5 us  [partners(): parts.append(lax.ppermute(value, axis, perm))]
    pallas_call x2 -> x1, Pallas kernels: 1.78 us -> 1.44 us  [gram_partial(): pl.pallas_call(gram_kernel, out_shape=jax.ShapeDtypeStruct((total, width)...]
  transfers between devices with their start and end apart: 21 -> 14, of which waited for: 8 -> 9; matrix products, arithmetic and copies ran while one was open for 0% -> 0% of each run, Pallas kernels for 7% -> 0%
where the time goes in v10:
time: 83.9 us; the launch traced here: 83.7 us
  starting transfers between devices  45.2 us (54%)
  waiting for transfers between devices  25.6 us (31%)
  Pallas kernels  12.1 us (14%)
    ppermute x7, starting transfers between devices, body(): lax.ppermute(blocks[k], 'samp', [(i, i ^ k) for i in range(owners)])  37.2 us
    ppermute x7, waiting for transfers between devices, body(): lax.ppermute(blocks[k], 'samp', [(i, i ^ k) for i in range(owners)])  16.1 us
    ppermute x7, waiting for transfers between devices, partners(): parts.append(lax.ppermute(value, axis, perm))  9.5 us
    ppermute x7, starting transfers between devices, partners(): parts.append(lax.ppermute(value, axis, perm))  7.97 us
    pallas_call x1, Pallas kernels, solve_and_project(): pl.pallas_call(functools.partial(solve_kernel, len(grams)), out_shape=(ja...  6.8 us
    pallas_call x1, Pallas kernels, jac_rows(): pl.pallas_call(jac_kernel, in_specs=[hbm, hbm], out_shape=[jax.ShapeDtype...  3.64 us
  transfers between devices with their start and end apart: 14, of which 9 were waited for; matrix products, arithmetic and copies ran while one was open for 0% of the time, Pallas kernels for 0%

profile of v10, /device:TPU:0, one launch (start us, length us, event | category | flops | bytes accessed | tf_op | source)
XLA Modules:
  0.0 83.7 jit_solution(17474927889744433383)
XLA Ops:
  0.6 0.0 copy-start.1
  0.6 0.0 copy-start
  0.7 3.6 %jac_rows.1 = (bf16[8,64,256]{2,1,0:T(8,128)(2,1)S(1)}, bf16[8,64,256]{2,1,0:T(8,128)(2,1)S(1)}, bf16[8,64,256]{2,1,0:T(8,128)(2,1)S(1)}, bf16[8,64,256]{2,1,0:T...) custom-call(bf16[8,2,256,256]{3,2,1,0:T(8,128)(2,1)} %act_hbm.1, ...), custom_call_target="tpu_custom_call" | custom-call | flops 536870912 | bytes 6291456 | tf_op jit(solution)/shard_map/jac_rows/pallas_call | solution.py:64
  4.3 6.1 %collective-permute-start = (bf16[8,64,256]{2,1,0:T(8,128)(2,1)}, bf16[8,64,256]{2,1,0:T(8,128)(2,1)S(1)}, u32[]{:S(2)}, u32[]{:S(2)}) collective-permute-start(bf16[8,64,256]{2,1,0:T(8,128)(2,1)} %get-tuple-element.12), channel_id=1, source_target_pairs={{0,28},{4,24},{8,20},{12,16},{16,12},{20,8},{24,4},{28,0},{1,29},{... | collective-permute-start | bytes 786440 | tf_op jit(solution)/shard_map/ppermute | solution.py:254
  10.4 0.2 collective-permute-start.1
  10.6 0.7 collective-permute-start.2
  11.3 2.0 %collective-permute-start.3 = (bf16[8,64,256]{2,1,0:T(8,128)(2,1)S(1)}, bf16[8,64,256]{2,1,0:T(8,128)(2,1)S(1)}, u32[]{:S(2)}, u32[]{:S(2)}) collective-permute-start(bf16[8,64,256]{2,1,0:T(8,128)(2,1)S(1)} %get-tuple-element.15), channel_id=1, source_target_pairs={{0,16},{4,20},{8,24},{12,28},{16,0},{20,4},{24,8},{28,12},{1,17},{... | collective-permute-start | bytes 786440 | tf_op jit(solution)/shard_map/ppermute | solution.py:254
  13.4 2.3 %collective-permute-start.4 = (bf16[8,64,256]{2,1,0:T(8,128)(2,1)S(1)}, bf16[8,64,256]{2,1,0:T(8,128)(2,1)S(1)}, u32[]{:S(2)}, u32[]{:S(2)}) collective-permute-start(bf16[8,64,256]{2,1,0:T(8,128)(2,1)S(1)} %get-tuple-element.16), channel_id=1, source_target_pairs={{0,12},{4,8},{8,4},{12,0},{16,28},{20,24},{24,20},{28,16},{1,13},{... | collective-permute-start | bytes 786440 | tf_op jit(solution)/shard_map/ppermute | solution.py:254
  15.7 2.3 %collective-permute-done.refs_0_.refs_4_ = bf16[8,64,256]{2,1,0:T(8,128)(2,1)S(1)} collective-permute-done((bf16[8,64,256]{2,1,0:T(8,128)(2,1)}, bf16[8,64,256]{2,1,0:T(8,128)(2,1)S(1)}, u32[]{:S(2)}, u32[]{:S(2)}) %collective-permute-start) | collective-permute-done | bytes 262176 | tf_op jit(solution)/shard_map/ppermute | solution.py:254
  17.9 24.5 %collective-permute-start.5 = (bf16[8,64,256]{2,1,0:T(8,128)(2,1)S(1)}, bf16[8,64,256]{2,1,0:T(8,128)(2,1)S(1)}, u32[]{:S(2)}, u32[]{:S(2)}) collective-permute-start(bf16[8,64,256]{2,1,0:T(8,128)(2,1)S(1)} %get-tuple-element.17), channel_id=1, source_target_pairs={{0,8},{4,12},{8,0},{12,4},{16,24},{20,28},{24,16},{28,20},{1,9},{5... | collective-permute-start | bytes 786440 | tf_op jit(solution)/shard_map/ppermute | solution.py:254
  42.4 0.0 collective-permute-done.1.refs_1_.refs_5_
  42.4 1.4 %collective-permute-start.6 = (bf16[8,64,256]{2,1,0:T(8,128)(2,1)S(1)}, bf16[8,64,256]{2,1,0:T(8,128)(2,1)S(1)}, u32[]{:S(2)}, u32[]{:S(2)}) collective-permute-start(bf16[8,64,256]{2,1,0:T(8,128)(2,1)S(1)} %get-tuple-element.18), channel_id=1, source_target_pairs={{0,4},{4,0},{8,12},{12,8},{16,20},{20,16},{24,28},{28,24},{1,5},{5... | collective-permute-start | bytes 786440 | tf_op jit(solution)/shard_map/ppermute | solution.py:254
  43.8 0.0 copy-done.1
  43.8 0.1 copy.6.offdiag_ref
  43.9 0.0 copy-done
  43.9 0.2 energy_column.1.refs_8_
  44.1 8.1 %collective-permute-done.2.refs_2_.refs_6_ = bf16[8,64,256]{2,1,0:T(8,128)(2,1)S(1)} collective-permute-done((bf16[8,64,256]{2,1,0:T(8,128)(2,1)S(1)}, bf16[8,64,256]{2,1,0:T(8,128)(2,1)S(1)}, u32[]{:S(2)}, u32[]{:S(2)}) %collective-permute-start.2) | collective-permute-done | bytes 262176 | tf_op jit(solution)/shard_map/ppermute | solution.py:254
  52.2 4.7 %collective-permute-done.3.refs_3_.refs_7_ = bf16[8,64,256]{2,1,0:T(8,128)(2,1)S(1)} collective-permute-done((bf16[8,64,256]{2,1,0:T(8,128)(2,1)S(1)}, bf16[8,64,256]{2,1,0:T(8,128)(2,1)S(1)}, u32[]{:S(2)}, u32[]{:S(2)}) %collective-permute-start.3) | collective-permute-done | bytes 262176 | tf_op jit(solution)/shard_map/ppermute | solution.py:254
  56.9 0.0 collective-permute-done.4.refs_4_.refs_8_
  56.9 1.1 %collective-permute-done.5.refs_5_.refs_9_ = bf16[8,64,256]{2,1,0:T(8,128)(2,1)S(1)} collective-permute-done((bf16[8,64,256]{2,1,0:T(8,128)(2,1)S(1)}, bf16[8,64,256]{2,1,0:T(8,128)(2,1)S(1)}, u32[]{:S(2)}, u32[]{:S(2)}) %collective-permute-start.5) | collective-permute-done | bytes 262176 | tf_op jit(solution)/shard_map/ppermute | solution.py:254
  58.0 0.0 collective-permute-done.6.refs_6_.refs_10_
  58.0 1.4 %gram_partial.1 = f32[64,128]{1,0:T(8,128)S(1)} custom-call(bf16[8,64,256]{2,1,0:T(8,128)(2,1)S(1)} %collective-permute-done.refs_0_.refs_4_, bf16[8,64,256]{2,1,0:T(8,128)(2,1)S(1)} %collective-permute-done.1.refs_1_.refs_5_, bf16[8,64,256]{2,1,0:T(8,128)(2,1)S(1)} %collective-permute-done.2.refs_2_.refs_6_, ...), custom_call_target="tpu_custom_call" | custom-call | flops 134217728 | bytes 2097152 | tf_op jit(solution)/shard_map/gram_partial/pallas_call | solution.py:142
  59.4 0.1 collective-permute-start.7
  59.5 1.5 %collective-permute-start.8 = (f32[64,128]{1,0:T(8,128)S(1)}, f32[64,128]{1,0:T(8,128)S(1)}, u32[]{:S(2)}, u32[]{:S(2)}) collective-permute-start(f32[64,128]{1,0:T(8,128)S(1)} %gram_partial.1), channel_id=1, source_target_pairs={{0,2},{1,3},{2,0},{3,1},{4,6},{5,7},{6,4},{7,5},{8,10},{9,11},{10,... | collective-permute-start | bytes 98312 | tf_op jit(solution)/shard_map/ppermute | solution.py:191
  61.0 0.4 collective-permute-start.9
  61.4 0.0 collective-permute-done.7
  61.4 2.1 %collective-permute-done.8 = f32[64,128]{1,0:T(8,128)S(1)} collective-permute-done((f32[64,128]{1,0:T(8,128)S(1)}, f32[64,128]{1,0:T(8,128)S(1)}, u32[]{:S(2)}, u32[]{:S(2)}) %collective-permute-start.8) | collective-permute-done | bytes 32800 | tf_op jit(solution)/shard_map/ppermute | solution.py:191
  63.5 0.8 %collective-permute-done.9 = f32[64,128]{1,0:T(8,128)S(1)} collective-permute-done((f32[64,128]{1,0:T(8,128)S(1)}, f32[64,128]{1,0:T(8,128)S(1)}, u32[]{:S(2)}, u32[]{:S(2)}) %collective-permute-start.9) | collective-permute-done | bytes 32800 | tf_op jit(solution)/shard_map/ppermute | solution.py:191
  64.3 1.7 %collective-permute-start.10 = (f32[64,128]{1,0:T(8,128)S(1)}, f32[64,128]{1,0:T(8,128)S(1)}, u32[]{:S(2)}, u32[]{:S(2)}) collective-permute-start(f32[64,128]{1,0:T(8,128)S(1)} %add_add_fusion), channel_id=1, source_target_pairs={{0,4},{4,0},{8,12},{12,8},{16,20},{20,16},{24,28},{28,24},{1,5},{5... | collective-permute-start | bytes 98312 | tf_op jit(solution)/shard_map/ppermute | solution.py:191
  66.0 2.3 %collective-permute-done.10 = f32[64,128]{1,0:T(8,128)S(1)} collective-permute-done((f32[64,128]{1,0:T(8,128)S(1)}, f32[64,128]{1,0:T(8,128)S(1)}, u32[]{:S(2)}, u32[]{:S(2)}) %collective-permute-start.10) | collective-permute-done | bytes 32800 | tf_op jit(solution)/shard_map/ppermute | solution.py:191
  68.3 0.0 collective-permute-start.11
  68.3 2.9 %collective-permute-start.12 = (f32[64,128]{1,0:T(8,128)S(1)}, f32[64,128]{1,0:T(8,128)S(1)}, u32[]{:S(2)}, u32[]{:S(2)}) collective-permute-start(f32[64,128]{1,0:T(8,128)S(1)} %add.15.refs_0_), channel_id=1, source_target_pairs={{0,16},{4,20},{8,24},{12,28},{16,0},{20,4},{24,8},{28,12},{1,17},{... | collective-permute-start | bytes 98312 | tf_op jit(solution)/shard_map/ppermute | solution.py:191
  71.2 1.5 %collective-permute-start.13 = (f32[64,128]{1,0:T(8,128)S(1)}, f32[64,128]{1,0:T(8,128)S(1)}, u32[]{:S(2)}, u32[]{:S(2)}) collective-permute-start(f32[64,128]{1,0:T(8,128)S(1)} %add.15.refs_0_), channel_id=1, source_target_pairs={{0,24},{4,28},{8,16},{12,20},{16,8},{20,12},{24,0},{28,4},{1,25},{... | collective-permute-start | bytes 98312 | tf_op jit(solution)/shard_map/ppermute | solution.py:191
  72.7 0.0 collective-permute-done.11.refs_1_
  72.7 0.5 collective-permute-done.12.refs_2_
  73.2 3.7 %collective-permute-done.13.refs_3_ = f32[64,128]{1,0:T(8,128)S(1)} collective-permute-done((f32[64,128]{1,0:T(8,128)S(1)}, f32[64,128]{1,0:T(8,128)S(1)}, u32[]{:S(2)}, u32[]{:S(2)}) %collective-permute-start.13) | collective-permute-done | bytes 32800 | tf_op jit(solution)/shard_map/ppermute | solution.py:191
  76.9 6.8 %solve_and_project.1 = (f32[1,8]{1,0:T(1,128)}, f32[2,32,256]{2,1,0:T(8,128)}) custom-call(f32[64,128]{1,0:T(8,128)S(1)} %add.15.refs_0_, f32[64,128]{1,0:T(8,128)S(1)} %collective-permute-done.11.refs_1_, f32[64,128]{1,0:T(8,128)S(1)} %collective-permute-done.12.refs_2_, f32[64,128]{1,0:T(8,128)S(1)} %collective-permute-done.13.refs_3_, ...), custom_call_target="tpu_custom_call" | custom-call | tf_op jit(solution)/shard_map/solve_and_project/pallas_call | solution.py:235
  (2 shorter events, 0.0 us)
Async XLA Ops:
  0.6 43.2 %copy-start.1 = (f32[8]{0:T(128)S(1)}, f32[8]{0:T(128)}, u32[]{:S(2)}) copy-start(f32[8]{0:T(128)} %param.7) | copy-start | bytes 100
  0.6 43.3 %copy-start = (s32[8,256]{1,0:T(8,128)S(1)}, s32[8,256]{1,0:T(8,128)}, u32[]{:S(2)}) copy-start(s32[8,256]{1,0:T(8,128)} %spins_ref.1) | copy-start | bytes 24580
  4.3 13.6 %collective-permute-start = (bf16[8,64,256]{2,1,0:T(8,128)(2,1)}, bf16[8,64,256]{2,1,0:T(8,128)(2,1)S(1)}, u32[]{:S(2)}, u32[]{:S(2)}) collective-permute-start(bf16[8,64,256]{2,1,0:T(8,128)(2,1)} %get-tuple-element.12), channel_id=1, source_target_pairs={{0,28},{4,24},{8,20},{12,16},{16,12},{20,8},{24,4},{28,0},{1,29},{... | collective-permute-start | bytes 786440 | tf_op jit(solution)/shard_map/ppermute | solution.py:254
  10.4 32.0 %collective-permute-start.1 = (bf16[8,64,256]{2,1,0:T(8,128)(2,1)S(1)}, bf16[8,64,256]{2,1,0:T(8,128)(2,1)S(1)}, u32[]{:S(2)}, u32[]{:S(2)}) collective-permute-start(bf16[8,64,256]{2,1,0:T(8,128)(2,1)S(1)} %get-tuple-element.13), channel_id=1, source_target_pairs={{0,24},{4,28},{8,16},{12,20},{16,8},{20,12},{24,0},{28,4},{1,25},{... | collective-permute-start | bytes 786440 | tf_op jit(solution)/shard_map/ppermute | solution.py:254
  10.6 41.6 %collective-permute-start.2 = (bf16[8,64,256]{2,1,0:T(8,128)(2,1)S(1)}, bf16[8,64,256]{2,1,0:T(8,128)(2,1)S(1)}, u32[]{:S(2)}, u32[]{:S(2)}) collective-permute-start(bf16[8,64,256]{2,1,0:T(8,128)(2,1)S(1)} %get-tuple-element.14), channel_id=1, source_target_pairs={{0,20},{4,16},{8,28},{12,24},{16,4},{20,0},{24,12},{28,8},{1,21},{... | collective-permute-start | bytes 786440 | tf_op jit(solution)/shard_map/ppermute | solution.py:254
  11.3 45.5 %collective-permute-start.3 = (bf16[8,64,256]{2,1,0:T(8,128)(2,1)S(1)}, bf16[8,64,256]{2,1,0:T(8,128)(2,1)S(1)}, u32[]{:S(2)}, u32[]{:S(2)}) collective-permute-start(bf16[8,64,256]{2,1,0:T(8,128)(2,1)S(1)} %get-tuple-element.15), channel_id=1, source_target_pairs={{0,16},{4,20},{8,24},{12,28},{16,0},{20,4},{24,8},{28,12},{1,17},{... | collective-permute-start | bytes 786440 | tf_op jit(solution)/shard_map/ppermute | solution.py:254
  13.4 43.5 %collective-permute-start.4 = (bf16[8,64,256]{2,1,0:T(8,128)(2,1)S(1)}, bf16[8,64,256]{2,1,0:T(8,128)(2,1)S(1)}, u32[]{:S(2)}, u32[]{:S(2)}) collective-permute-start(bf16[8,64,256]{2,1,0:T(8,128)(2,1)S(1)} %get-tuple-element.16), channel_id=1, source_target_pairs={{0,12},{4,8},{8,4},{12,0},{16,28},{20,24},{24,20},{28,16},{1,13},{... | collective-permute-start | bytes 786440 | tf_op jit(solution)/shard_map/ppermute | solution.py:254
  17.9 40.1 %collective-permute-start.5 = (bf16[8,64,256]{2,1,0:T(8,128)(2,1)S(1)}, bf16[8,64,256]{2,1,0:T(8,128)(2,1)S(1)}, u32[]{:S(2)}, u32[]{:S(2)}) collective-permute-start(bf16[8,64,256]{2,1,0:T(8,128)(2,1)S(1)} %get-tuple-element.17), channel_id=1, source_target_pairs={{0,8},{4,12},{8,0},{12,4},{16,24},{20,28},{24,16},{28,20},{1,9},{5... | collective-permute-start | bytes 786440 | tf_op jit(solution)/shard_map/ppermute | solution.py:254
  42.4 15.6 %collective-permute-start.6 = (bf16[8,64,256]{2,1,0:T(8,128)(2,1)S(1)}, bf16[8,64,256]{2,1,0:T(8,128)(2,1)S(1)}, u32[]{:S(2)}, u32[]{:S(2)}) collective-permute-start(bf16[8,64,256]{2,1,0:T(8,128)(2,1)S(1)} %get-tuple-element.18), channel_id=1, source_target_pairs={{0,4},{4,0},{8,12},{12,8},{16,20},{20,16},{24,28},{28,24},{1,5},{5... | collective-permute-start | bytes 786440 | tf_op jit(solution)/shard_map/ppermute | solution.py:254
  59.4 1.9 %collective-permute-start.7 = (f32[64,128]{1,0:T(8,128)S(1)}, f32[64,128]{1,0:T(8,128)S(1)}, u32[]{:S(2)}, u32[]{:S(2)}) collective-permute-start(f32[64,128]{1,0:T(8,128)S(1)} %gram_partial.1), channel_id=1, source_target_pairs={{0,1},{1,0},{2,3},{3,2},{4,5},{5,4},{6,7},{7,6},{8,9},{9,8},{10,11... | collective-permute-start | bytes 98312 | tf_op jit(solution)/shard_map/ppermute | solution.py:191
  59.5 4.0 %collective-permute-start.8 = (f32[64,128]{1,0:T(8,128)S(1)}, f32[64,128]{1,0:T(8,128)S(1)}, u32[]{:S(2)}, u32[]{:S(2)}) collective-permute-start(f32[64,128]{1,0:T(8,128)S(1)} %gram_partial.1), channel_id=1, source_target_pairs={{0,2},{1,3},{2,0},{3,1},{4,6},{5,7},{6,4},{7,5},{8,10},{9,11},{10,... | collective-permute-start | bytes 98312 | tf_op jit(solution)/shard_map/ppermute | solution.py:191
  61.0 3.3 %collective-permute-start.9 = (f32[64,128]{1,0:T(8,128)S(1)}, f32[64,128]{1,0:T(8,128)S(1)}, u32[]{:S(2)}, u32[]{:S(2)}) collective-permute-start(f32[64,128]{1,0:T(8,128)S(1)} %gram_partial.1), channel_id=1, source_target_pairs={{0,3},{1,2},{2,1},{3,0},{4,7},{5,6},{6,5},{7,4},{8,11},{9,10},{10,... | collective-permute-start | bytes 98312 | tf_op jit(solution)/shard_map/ppermute | solution.py:191
  64.3 4.0 %collective-permute-start.10 = (f32[64,128]{1,0:T(8,128)S(1)}, f32[64,128]{1,0:T(8,128)S(1)}, u32[]{:S(2)}, u32[]{:S(2)}) collective-permute-start(f32[64,128]{1,0:T(8,128)S(1)} %add_add_fusion), channel_id=1, source_target_pairs={{0,4},{4,0},{8,12},{12,8},{16,20},{20,16},{24,28},{28,24},{1,5},{5... | collective-permute-start | bytes 98312 | tf_op jit(solution)/shard_map/ppermute | solution.py:191
  68.3 4.4 %collective-permute-start.11 = (f32[64,128]{1,0:T(8,128)S(1)}, f32[64,128]{1,0:T(8,128)S(1)}, u32[]{:S(2)}, u32[]{:S(2)}) collective-permute-start(f32[64,128]{1,0:T(8,128)S(1)} %add.15.refs_0_), channel_id=1, source_target_pairs={{0,8},{4,12},{8,0},{12,4},{16,24},{20,28},{24,16},{28,20},{1,9},{5... | collective-permute-start | bytes 98312 | tf_op jit(solution)/shard_map/ppermute | solution.py:191
  68.3 4.9 %collective-permute-start.12 = (f32[64,128]{1,0:T(8,128)S(1)}, f32[64,128]{1,0:T(8,128)S(1)}, u32[]{:S(2)}, u32[]{:S(2)}) collective-permute-start(f32[64,128]{1,0:T(8,128)S(1)} %add.15.refs_0_), channel_id=1, source_target_pairs={{0,16},{4,20},{8,24},{12,28},{16,0},{20,4},{24,8},{28,12},{1,17},{... | collective-permute-start | bytes 98312 | tf_op jit(solution)/shard_map/ppermute | solution.py:191
  71.2 5.7 %collective-permute-start.13 = (f32[64,128]{1,0:T(8,128)S(1)}, f32[64,128]{1,0:T(8,128)S(1)}, u32[]{:S(2)}, u32[]{:S(2)}) collective-permute-start(f32[64,128]{1,0:T(8,128)S(1)} %add.15.refs_0_), channel_id=1, source_target_pairs={{0,24},{4,28},{8,16},{12,20},{16,8},{20,12},{24,0},{28,4},{1,25},{... | collective-permute-start | bytes 98312 | tf_op jit(solution)/shard_map/ppermute | solution.py:191

commit v11 on v10

--- a/solution.py
+++ b/solution.py
@@ -19,6 +19,24 @@
 
 def iota(shape, dim):
     return lax.broadcasted_iota(jnp.int32, shape, dim)
+
+
+def turns(owners):
+    far, near = list(range(owners // 2, owners)), list(range(owners // 2 - 1, 0, -1))
+    order = [far.pop(0)]
+    while far or near:
+        order += far[:1] + near[:1]
+        far, near = far[1:], near[1:]
+    return order + [0]
+
+
+def in_turn(blocks):
+    return [blocks[k] for k in turns(len(blocks))]
+
+
+def in_place(blocks):
+    order = turns(len(blocks))
+    return [blocks[order.index(k)] for k in range(len(blocks))]
 
 
 def jac_kernel(act_hbm, cot_hbm, *refs):
@@ -111,7 +129,7 @@
 
 def gram_kernel(*refs):
     *block_refs, start_ref, out_ref, flat = refs
-    block_refs = block_refs[::-1]
+    block_refs = in_place(block_refs)
     local, count, d = block_refs[0].shape
     total = local * len(block_refs)
     joined = CHUNK // local
@@ -150,7 +168,7 @@
             transcendentals=0,
         ),
         name="gram_partial",
-    )(*blocks[::-1], start)
+    )(*in_turn(blocks), start)
 
 
 def eliminate(matrix, total):
@@ -194,7 +212,7 @@
 
 def solve_kernel(grams, *refs):
     gram_refs, (*block_refs, weights_ref, update_ref, held) = refs[:grams], refs[grams:]
-    block_refs = block_refs[::-1]
+    block_refs = in_place(block_refs)
     mats, share, d = update_ref.shape
     local = weights_ref.shape[1]
     total, width = gram_refs[0].shape
@@ -241,7 +259,7 @@
         scratch_shapes=[pltpu.VMEM((total, d), F32)],
         compiler_params=pltpu.CompilerParams(vmem_limit_bytes=VMEM_LIMIT),
         name="solve_and_project",
-    )(*grams, *blocks[::-1])
+    )(*grams, *in_turn(blocks))
 
 
 def body(spins, activations, cotangents, offdiag):
@@ -250,7 +268,7 @@
     total = local * owners
     width = (total // LANES + 1) * LANES
     blocks = list(jac_rows(activations, cotangents, owners))
-    for k in range(owners - 1, 0, -1):
+    for k in turns(owners)[:-1]:
         blocks[k] = lax.ppermute(blocks[k], "samp", [(i, i ^ k) for i in range(owners)])
     partial = gram_partial(blocks, energy_column(spins, offdiag, total, width))
     grams = partners(partial, "layer", 1, lax.axis_size("layer"))

time: 83.9 us -> 80.8 us (0.963)
  starting transfers between devices: 45.2 us -> 25.9 us
  waiting for transfers between devices: 25.6 us -> 41.9 us
    ppermute x7, starting transfers between devices: 37.2 us -> 15 us  [body(): lax.ppermute(blocks[k], 'samp', [(i, i ^ k) for i in range(owners)])]
    ppermute x7, waiting for transfers between devices: 16.1 us -> 31.1 us  [body(): lax.ppermute(blocks[k], 'samp', [(i, i ^ k) for i in range(owners)])]
    ppermute x7, starting transfers between devices: 7.97 us -> 10.9 us  [partners(): parts.append(lax.ppermute(value, axis, perm))]
    ppermute x7, waiting for transfers between devices: 9.5 us -> 10.8 us  [partners(): parts.append(lax.ppermute(value, axis, perm))]
where the time goes in v11:
time: 80.8 us; the launch traced here: 80.7 us
  waiting for transfers between devices  41.9 us (52%)
  starting transfers between devices  25.9 us (32%)
  Pallas kernels  12.1 us (15%)
    ppermute x7, waiting for transfers between devices, body(): lax.ppermute(blocks[k], 'samp', [(i, i ^ k) for i in range(owners)])  31.1 us
    ppermute x7, starting transfers between devices, body(): lax.ppermute(blocks[k], 'samp', [(i, i ^ k) for i in range(owners)])  15 us
    ppermute x7, starting transfers between devices, partners(): parts.append(lax.ppermute(value, axis, perm))  10.9 us
    ppermute x7, waiting for transfers between devices, partners(): parts.append(lax.ppermute(value, axis, perm))  10.8 us
    pallas_call x1, Pallas kernels, solve_and_project(): pl.pallas_call(functools.partial(solve_kernel, len(grams)), out_shape=(ja...  6.8 us
    pallas_call x1, Pallas kernels, jac_rows(): pl.pallas_call(jac_kernel, in_specs=[hbm, hbm], out_shape=[jax.ShapeDtype...  3.64 us
  transfers between devices with their start and end apart: 14, of which 9 were waited for; matrix products, arithmetic and copies ran while one was open for 0% of the time, Pallas kernels for 0%

profile of v11, /device:TPU:0, one launch (start us, length us, event | category | flops | bytes accessed | tf_op | source)
XLA Modules:
  0.0 80.7 jit_solution(7672902154371266198)
XLA Ops:
  0.6 0.0 copy-start.1
  0.6 0.0 copy-start
  0.7 3.6 %jac_rows.1 = (bf16[8,64,256]{2,1,0:T(8,128)(2,1)S(1)}, bf16[8,64,256]{2,1,0:T(8,128)(2,1)S(1)}, bf16[8,64,256]{2,1,0:T(8,128)(2,1)S(1)}, bf16[8,64,256]{2,1,0:T...) custom-call(bf16[8,2,256,256]{3,2,1,0:T(8,128)(2,1)} %act_hbm.1, ...), custom_call_target="tpu_custom_call" | custom-call | flops 536870912 | bytes 6291456 | tf_op jit(solution)/shard_map/jac_rows/pallas_call | solution.py:82
  4.3 4.1 %collective-permute-start = (bf16[8,64,256]{2,1,0:T(8,128)(2,1)S(1)}, bf16[8,64,256]{2,1,0:T(8,128)(2,1)S(1)}, u32[]{:S(2)}, u32[]{:S(2)}) collective-permute-start(bf16[8,64,256]{2,1,0:T(8,128)(2,1)S(1)} %get-tuple-element.12), channel_id=1, source_target_pairs={{0,16},{4,20},{8,24},{12,28},{16,0},{20,4},{24,8},{28,12},{1,17},{... | collective-permute-start | bytes 786440 | tf_op jit(solution)/shard_map/ppermute | solution.py:272
  8.4 1.3 %collective-permute-start.1 = (bf16[8,64,256]{2,1,0:T(8,128)(2,1)S(1)}, bf16[8,64,256]{2,1,0:T(8,128)(2,1)S(1)}, u32[]{:S(2)}, u32[]{:S(2)}) collective-permute-start(bf16[8,64,256]{2,1,0:T(8,128)(2,1)S(1)} %get-tuple-element.13), channel_id=1, source_target_pairs={{0,20},{4,16},{8,28},{12,24},{16,4},{20,0},{24,12},{28,8},{1,21},{... | collective-permute-start | bytes 786440 | tf_op jit(solution)/shard_map/ppermute | solution.py:272
  9.7 1.5 %collective-permute-start.2 = (bf16[8,64,256]{2,1,0:T(8,128)(2,1)S(1)}, bf16[8,64,256]{2,1,0:T(8,128)(2,1)S(1)}, u32[]{:S(2)}, u32[]{:S(2)}) collective-permute-start(bf16[8,64,256]{2,1,0:T(8,128)(2,1)S(1)} %get-tuple-element.14), channel_id=1, source_target_pairs={{0,12},{4,8},{8,4},{12,0},{16,28},{20,24},{24,20},{28,16},{1,13},{... | collective-permute-start | bytes 786440 | tf_op jit(solution)/shard_map/ppermute | solution.py:272
  11.2 2.5 %collective-permute-start.3 = (bf16[8,64,256]{2,1,0:T(8,128)(2,1)S(1)}, bf16[8,64,256]{2,1,0:T(8,128)(2,1)S(1)}, u32[]{:S(2)}, u32[]{:S(2)}) collective-permute-start(bf16[8,64,256]{2,1,0:T(8,128)(2,1)S(1)} %get-tuple-element.15), channel_id=1, source_target_pairs={{0,24},{4,28},{8,16},{12,20},{16,8},{20,12},{24,0},{28,4},{1,25},{... | collective-permute-start | bytes 786440 | tf_op jit(solution)/shard_map/ppermute | solution.py:272
  13.7 0.7 collective-permute-start.4
  14.4 12.5 %collective-permute-done.refs_0_.refs_4_ = bf16[8,64,256]{2,1,0:T(8,128)(2,1)S(1)} collective-permute-done((bf16[8,64,256]{2,1,0:T(8,128)(2,1)S(1)}, bf16[8,64,256]{2,1,0:T(8,128)(2,1)S(1)}, u32[]{:S(2)}, u32[]{:S(2)}) %collective-permute-start) | collective-permute-done | bytes 262176 | tf_op jit(solution)/shard_map/ppermute | solution.py:272
  26.9 4.9 %collective-permute-start.5 = (bf16[8,64,256]{2,1,0:T(8,128)(2,1)}, bf16[8,64,256]{2,1,0:T(8,128)(2,1)S(1)}, u32[]{:S(2)}, u32[]{:S(2)}) collective-permute-start(bf16[8,64,256]{2,1,0:T(8,128)(2,1)} %get-tuple-element.17), channel_id=1, source_target_pairs={{0,28},{4,24},{8,20},{12,16},{16,12},{20,8},{24,4},{28,0},{1,29},{... | collective-permute-start | bytes 786440 | tf_op jit(solution)/shard_map/ppermute | solution.py:272
  31.8 7.7 %collective-permute-done.1.refs_1_.refs_5_ = bf16[8,64,256]{2,1,0:T(8,128)(2,1)S(1)} collective-permute-done((bf16[8,64,256]{2,1,0:T(8,128)(2,1)S(1)}, bf16[8,64,256]{2,1,0:T(8,128)(2,1)S(1)}, u32[]{:S(2)}, u32[]{:S(2)}) %collective-permute-start.1) | collective-permute-done | bytes 262176 | tf_op jit(solution)/shard_map/ppermute | solution.py:272
  39.5 0.0 collective-permute-start.6
  39.5 0.0 copy-done.1
  39.5 0.1 copy.6.offdiag_ref
  39.6 0.0 copy-done
  39.6 0.2 energy_column.1.refs_8_
  39.8 0.0 collective-permute-done.2.refs_2_.refs_6_
  39.8 0.0 collective-permute-done.3.refs_3_.refs_7_
  39.9 0.0 collective-permute-done.4.refs_4_.refs_8_
  39.9 6.2 %collective-permute-done.5.refs_5_.refs_9_ = bf16[8,64,256]{2,1,0:T(8,128)(2,1)S(1)} collective-permute-done((bf16[8,64,256]{2,1,0:T(8,128)(2,1)}, bf16[8,64,256]{2,1,0:T(8,128)(2,1)S(1)}, u32[]{:S(2)}, u32[]{:S(2)}) %collective-permute-start.5) | collective-permute-done | bytes 262176 | tf_op jit(solution)/shard_map/ppermute | solution.py:272
  46.1 4.7 %collective-permute-done.6.refs_6_.refs_10_ = bf16[8,64,256]{2,1,0:T(8,128)(2,1)S(1)} collective-permute-done((bf16[8,64,256]{2,1,0:T(8,128)(2,1)S(1)}, bf16[8,64,256]{2,1,0:T(8,128)(2,1)S(1)}, u32[]{:S(2)}, u32[]{:S(2)}) %collective-permute-start.6) | collective-permute-done | bytes 262176 | tf_op jit(solution)/shard_map/ppermute | solution.py:272
  50.7 1.4 %gram_partial.1 = f32[64,128]{1,0:T(8,128)S(1)} custom-call(bf16[8,64,256]{2,1,0:T(8,128)(2,1)S(1)} %collective-permute-done.refs_0_.refs_4_, bf16[8,64,256]{2,1,0:T(8,128)(2,1)S(1)} %collective-permute-done.1.refs_1_.refs_5_, bf16[8,64,256]{2,1,0:T(8,128)(2,1)S(1)} %collective-permute-done.2.refs_2_.refs_6_, ...), custom_call_target="tpu_custom_call" | custom-call | flops 134217728 | bytes 2097152 | tf_op jit(solution)/shard_map/gram_partial/pallas_call | solution.py:160
  52.2 0.1 collective-permute-start.7
  52.3 1.6 %collective-permute-start.8 = (f32[64,128]{1,0:T(8,128)S(1)}, f32[64,128]{1,0:T(8,128)S(1)}, u32[]{:S(2)}, u32[]{:S(2)}) collective-permute-start(f32[64,128]{1,0:T(8,128)S(1)} %gram_partial.1), channel_id=1, source_target_pairs={{0,2},{1,3},{2,0},{3,1},{4,6},{5,7},{6,4},{7,5},{8,10},{9,11},{10,... | collective-permute-start | bytes 98312 | tf_op jit(solution)/shard_map/ppermute | solution.py:209
  53.8 0.3 collective-permute-start.9
  54.1 0.0 collective-permute-done.7
  54.1 2.1 %collective-permute-done.8 = f32[64,128]{1,0:T(8,128)S(1)} collective-permute-done((f32[64,128]{1,0:T(8,128)S(1)}, f32[64,128]{1,0:T(8,128)S(1)}, u32[]{:S(2)}, u32[]{:S(2)}) %collective-permute-start.8) | collective-permute-done | bytes 32800 | tf_op jit(solution)/shard_map/ppermute | solution.py:209
  56.2 0.9 %collective-permute-done.9 = f32[64,128]{1,0:T(8,128)S(1)} collective-permute-done((f32[64,128]{1,0:T(8,128)S(1)}, f32[64,128]{1,0:T(8,128)S(1)}, u32[]{:S(2)}, u32[]{:S(2)}) %collective-permute-start.9) | collective-permute-done | bytes 32800 | tf_op jit(solution)/shard_map/ppermute | solution.py:209
  57.2 0.6 collective-permute-start.10
  57.7 3.4 %collective-permute-done.10 = f32[64,128]{1,0:T(8,128)S(1)} collective-permute-done((f32[64,128]{1,0:T(8,128)S(1)}, f32[64,128]{1,0:T(8,128)S(1)}, u32[]{:S(2)}, u32[]{:S(2)}) %collective-permute-start.10) | collective-permute-done | bytes 32800 | tf_op jit(solution)/shard_map/ppermute | solution.py:209
  61.2 4.9 %collective-permute-start.11 = (f32[64,128]{1,0:T(8,128)S(1)}, f32[64,128]{1,0:T(8,128)S(1)}, u32[]{:S(2)}, u32[]{:S(2)}) collective-permute-start(f32[64,128]{1,0:T(8,128)S(1)} %add.15.refs_0_), channel_id=1, source_target_pairs={{0,8},{4,12},{8,0},{12,4},{16,24},{20,28},{24,16},{28,20},{1,9},{5... | collective-permute-start | bytes 98312 | tf_op jit(solution)/shard_map/ppermute | solution.py:209
  66.1 2.1 %collective-permute-start.12 = (f32[64,128]{1,0:T(8,128)S(1)}, f32[64,128]{1,0:T(8,128)S(1)}, u32[]{:S(2)}, u32[]{:S(2)}) collective-permute-start(f32[64,128]{1,0:T(8,128)S(1)} %add.15.refs_0_), channel_id=1, source_target_pairs={{0,16},{4,20},{8,24},{12,28},{16,0},{20,4},{24,8},{28,12},{1,17},{... | collective-permute-start | bytes 98312 | tf_op jit(solution)/shard_map/ppermute | solution.py:209
  68.2 1.4 %collective-permute-start.13 = (f32[64,128]{1,0:T(8,128)S(1)}, f32[64,128]{1,0:T(8,128)S(1)}, u32[]{:S(2)}, u32[]{:S(2)}) collective-permute-start(f32[64,128]{1,0:T(8,128)S(1)} %add.15.refs_0_), channel_id=1, source_target_pairs={{0,24},{4,28},{8,16},{12,20},{16,8},{20,12},{24,0},{28,4},{1,25},{... | collective-permute-start | bytes 98312 | tf_op jit(solution)/shard_map/ppermute | solution.py:209
  69.6 0.0 collective-permute-done.11.refs_1_
  69.6 1.6 %collective-permute-done.12.refs_2_ = f32[64,128]{1,0:T(8,128)S(1)} collective-permute-done((f32[64,128]{1,0:T(8,128)S(1)}, f32[64,128]{1,0:T(8,128)S(1)}, u32[]{:S(2)}, u32[]{:S(2)}) %collective-permute-start.12) | collective-permute-done | bytes 32800 | tf_op jit(solution)/shard_map/ppermute | solution.py:209
  71.2 2.7 %collective-permute-done.13.refs_3_ = f32[64,128]{1,0:T(8,128)S(1)} collective-permute-done((f32[64,128]{1,0:T(8,128)S(1)}, f32[64,128]{1,0:T(8,128)S(1)}, u32[]{:S(2)}, u32[]{:S(2)}) %collective-permute-start.13) | collective-permute-done | bytes 32800 | tf_op jit(solution)/shard_map/ppermute | solution.py:209
  73.9 6.8 %solve_and_project.1 = (f32[1,8]{1,0:T(1,128)}, f32[2,32,256]{2,1,0:T(8,128)}) custom-call(f32[64,128]{1,0:T(8,128)S(1)} %add.15.refs_0_, f32[64,128]{1,0:T(8,128)S(1)} %collective-permute-done.11.refs_1_, f32[64,128]{1,0:T(8,128)S(1)} %collective-permute-done.12.refs_2_, f32[64,128]{1,0:T(8,128)S(1)} %collective-permute-done.13.refs_3_, ...), custom_call_target="tpu_custom_call" | custom-call | tf_op jit(solution)/shard_map/solve_and_project/pallas_call | solution.py:253
  (2 shorter events, 0.0 us)
Async XLA Ops:
  0.6 38.9 %copy-start.1 = (f32[8]{0:T(128)S(1)}, f32[8]{0:T(128)}, u32[]{:S(2)}) copy-start(f32[8]{0:T(128)} %param.7) | copy-start | bytes 100
  0.6 39.0 %copy-start = (s32[8,256]{1,0:T(8,128)S(1)}, s32[8,256]{1,0:T(8,128)}, u32[]{:S(2)}) copy-start(s32[8,256]{1,0:T(8,128)} %spins_ref.1) | copy-start | bytes 24580
  4.3 22.6 %collective-permute-start = (bf16[8,64,256]{2,1,0:T(8,128)(2,1)S(1)}, bf16[8,64,256]{2,1,0:T(8,128)(2,1)S(1)}, u32[]{:S(2)}, u32[]{:S(2)}) collective-permute-start(bf16[8,64,256]{2,1,0:T(8,128)(2,1)S(1)} %get-tuple-element.12), channel_id=1, source_target_pairs={{0,16},{4,20},{8,24},{12,28},{16,0},{20,4},{24,8},{28,12},{1,17},{... | collective-permute-start | bytes 786440 | tf_op jit(solution)/shard_map/ppermute | solution.py:272
  8.4 31.1 %collective-permute-start.1 = (bf16[8,64,256]{2,1,0:T(8,128)(2,1)S(1)}, bf16[8,64,256]{2,1,0:T(8,128)(2,1)S(1)}, u32[]{:S(2)}, u32[]{:S(2)}) collective-permute-start(bf16[8,64,256]{2,1,0:T(8,128)(2,1)S(1)} %get-tuple-element.13), channel_id=1, source_target_pairs={{0,20},{4,16},{8,28},{12,24},{16,4},{20,0},{24,12},{28,8},{1,21},{... | collective-permute-start | bytes 786440 | tf_op jit(solution)/shard_map/ppermute | solution.py:272
  9.7 30.1 %collective-permute-start.2 = (bf16[8,64,256]{2,1,0:T(8,128)(2,1)S(1)}, bf16[8,64,256]{2,1,0:T(8,128)(2,1)S(1)}, u32[]{:S(2)}, u32[]{:S(2)}) collective-permute-start(bf16[8,64,256]{2,1,0:T(8,128)(2,1)S(1)} %get-tuple-element.14), channel_id=1, source_target_pairs={{0,12},{4,8},{8,4},{12,0},{16,28},{20,24},{24,20},{28,16},{1,13},{... | collective-permute-start | bytes 786440 | tf_op jit(solution)/shard_map/ppermute | solution.py:272
  11.2 28.6 %collective-permute-start.3 = (bf16[8,64,256]{2,1,0:T(8,128)(2,1)S(1)}, bf16[8,64,256]{2,1,0:T(8,128)(2,1)S(1)}, u32[]{:S(2)}, u32[]{:S(2)}) collective-permute-start(bf16[8,64,256]{2,1,0:T(8,128)(2,1)S(1)} %get-tuple-element.15), channel_id=1, source_target_pairs={{0,24},{4,28},{8,16},{12,20},{16,8},{20,12},{24,0},{28,4},{1,25},{... | collective-permute-start | bytes 786440 | tf_op jit(solution)/shard_map/ppermute | solution.py:272
  13.7 26.2 %collective-permute-start.4 = (bf16[8,64,256]{2,1,0:T(8,128)(2,1)S(1)}, bf16[8,64,256]{2,1,0:T(8,128)(2,1)S(1)}, u32[]{:S(2)}, u32[]{:S(2)}) collective-permute-start(bf16[8,64,256]{2,1,0:T(8,128)(2,1)S(1)} %get-tuple-element.16), channel_id=1, source_target_pairs={{0,8},{4,12},{8,0},{12,4},{16,24},{20,28},{24,16},{28,20},{1,9},{5... | collective-permute-start | bytes 786440 | tf_op jit(solution)/shard_map/ppermute | solution.py:272
  26.9 19.2 %collective-permute-start.5 = (bf16[8,64,256]{2,1,0:T(8,128)(2,1)}, bf16[8,64,256]{2,1,0:T(8,128)(2,1)S(1)}, u32[]{:S(2)}, u32[]{:S(2)}) collective-permute-start(bf16[8,64,256]{2,1,0:T(8,128)(2,1)} %get-tuple-element.17), channel_id=1, source_target_pairs={{0,28},{4,24},{8,20},{12,16},{16,12},{20,8},{24,4},{28,0},{1,29},{... | collective-permute-start | bytes 786440 | tf_op jit(solution)/shard_map/ppermute | solution.py:272
  39.5 11.2 %collective-permute-start.6 = (bf16[8,64,256]{2,1,0:T(8,128)(2,1)S(1)}, bf16[8,64,256]{2,1,0:T(8,128)(2,1)S(1)}, u32[]{:S(2)}, u32[]{:S(2)}) collective-permute-start(bf16[8,64,256]{2,1,0:T(8,128)(2,1)S(1)} %get-tuple-element.18), channel_id=1, source_target_pairs={{0,4},{4,0},{8,12},{12,8},{16,20},{20,16},{24,28},{28,24},{1,5},{5... | collective-permute-start | bytes 786440 | tf_op jit(solution)/shard_map/ppermute | solution.py:272
  52.2 1.9 %collective-permute-start.7 = (f32[64,128]{1,0:T(8,128)S(1)}, f32[64,128]{1,0:T(8,128)S(1)}, u32[]{:S(2)}, u32[]{:S(2)}) collective-permute-start(f32[64,128]{1,0:T(8,128)S(1)} %gram_partial.1), channel_id=1, source_target_pairs={{0,1},{1,0},{2,3},{3,2},{4,5},{5,4},{6,7},{7,6},{8,9},{9,8},{10,11... | collective-permute-start | bytes 98312 | tf_op jit(solution)/shard_map/ppermute | solution.py:209
  52.3 4.0 %collective-permute-start.8 = (f32[64,128]{1,0:T(8,128)S(1)}, f32[64,128]{1,0:T(8,128)S(1)}, u32[]{:S(2)}, u32[]{:S(2)}) collective-permute-start(f32[64,128]{1,0:T(8,128)S(1)} %gram_partial.1), channel_id=1, source_target_pairs={{0,2},{1,3},{2,0},{3,1},{4,6},{5,7},{6,4},{7,5},{8,10},{9,11},{10,... | collective-permute-start | bytes 98312 | tf_op jit(solution)/shard_map/ppermute | solution.py:209
  53.8 3.3 %collective-permute-start.9 = (f32[64,128]{1,0:T(8,128)S(1)}, f32[64,128]{1,0:T(8,128)S(1)}, u32[]{:S(2)}, u32[]{:S(2)}) collective-permute-start(f32[64,128]{1,0:T(8,128)S(1)} %gram_partial.1), channel_id=1, source_target_pairs={{0,3},{1,2},{2,1},{3,0},{4,7},{5,6},{6,5},{7,4},{8,11},{9,10},{10,... | collective-permute-start | bytes 98312 | tf_op jit(solution)/shard_map/ppermute | solution.py:209
  57.2 4.0 %collective-permute-start.10 = (f32[64,128]{1,0:T(8,128)S(1)}, f32[64,128]{1,0:T(8,128)S(1)}, u32[]{:S(2)}, u32[]{:S(2)}) collective-permute-start(f32[64,128]{1,0:T(8,128)S(1)} %add_add_fusion), channel_id=1, source_target_pairs={{0,4},{4,0},{8,12},{12,8},{16,20},{20,16},{24,28},{28,24},{1,5},{5... | collective-permute-start | bytes 98312 | tf_op jit(solution)/shard_map/ppermute | solution.py:209
  61.2 8.4 %collective-permute-start.11 = (f32[64,128]{1,0:T(8,128)S(1)}, f32[64,128]{1,0:T(8,128)S(1)}, u32[]{:S(2)}, u32[]{:S(2)}) collective-permute-start(f32[64,128]{1,0:T(8,128)S(1)} %add.15.refs_0_), channel_id=1, source_target_pairs={{0,8},{4,12},{8,0},{12,4},{16,24},{20,28},{24,16},{28,20},{1,9},{5... | collective-permute-start | bytes 98312 | tf_op jit(solution)/shard_map/ppermute | solution.py:209
  66.1 5.1 %collective-permute-start.12 = (f32[64,128]{1,0:T(8,128)S(1)}, f32[64,128]{1,0:T(8,128)S(1)}, u32[]{:S(2)}, u32[]{:S(2)}) collective-permute-start(f32[64,128]{1,0:T(8,128)S(1)} %add.15.refs_0_), channel_id=1, source_target_pairs={{0,16},{4,20},{8,24},{12,28},{16,0},{20,4},{24,8},{28,12},{1,17},{... | collective-permute-start | bytes 98312 | tf_op jit(solution)/shard_map/ppermute | solution.py:209
  68.2 5.7 %collective-permute-start.13 = (f32[64,128]{1,0:T(8,128)S(1)}, f32[64,128]{1,0:T(8,128)S(1)}, u32[]{:S(2)}, u32[]{:S(2)}) collective-permute-start(f32[64,128]{1,0:T(8,128)S(1)} %add.15.refs_0_), channel_id=1, source_target_pairs={{0,24},{4,28},{8,16},{12,20},{16,8},{20,12},{24,0},{28,4},{1,25},{... | collective-permute-start | bytes 98312 | tf_op jit(solution)/shard_map/ppermute | solution.py:209

commit v12 on v11

--- a/solution.py
+++ b/solution.py
@@ -1,5 +1,3 @@
-import functools
-
 import jax
 import jax.numpy as jnp
 from jax import lax
@@ -100,8 +98,7 @@
 
 
 def energy_kernel(spins_ref, offdiag_ref, out_ref):
-    total, width = out_ref.shape
-    local = spins_ref.shape[0]
+    local, width = out_ref.shape
     sites = SIDE * SIDE
     z = (2 * spins_ref[...] - 1).astype(F32)
     column = iota((local, sites), 1) % SIDE
@@ -110,25 +107,21 @@
     )
     below = pltpu.roll(z, sites - SIDE, 1)
     energy = offdiag_ref[...] + jnp.sum(z * (right + below), axis=1, keepdims=True)
-    first = lax.axis_index("samp") * local
-    mine = lax.axis_index("layer") == 0
-    spread = jnp.concatenate([energy] * (total // local), axis=0)
-    row = iota((total, width), 0)
-    here = (row >= first) & (row < first + local) & (iota((total, width), 1) == total) & mine
-    out_ref[...] = jnp.where(here, spread, F32(0.0))
-
-
-def energy_column(spins, offdiag, total, width):
+    here = (iota((local, width), 1) == lax.axis_index("samp")) & (lax.axis_index("layer") == 0)
+    out_ref[...] = jnp.where(here, energy, F32(0.0))
+
+
+def energy_rows(spins, offdiag, width):
     return pl.pallas_call(
         energy_kernel,
-        out_shape=jax.ShapeDtypeStruct((total, width), F32),
+        out_shape=jax.ShapeDtypeStruct((spins.shape[0], width), F32),
         compiler_params=pltpu.CompilerParams(vmem_limit_bytes=VMEM_LIMIT),
-        name="energy_column",
+        name="energy_rows",
     )(spins, offdiag[:, None])
 
 
 def gram_kernel(*refs):
-    *block_refs, start_ref, out_ref, flat = refs
+    *block_refs, energy_ref, out_ref, flat = refs
     block_refs = in_place(block_refs)
     local, count, d = block_refs[0].shape
     total = local * len(block_refs)
@@ -150,16 +143,17 @@
                 flat[row + r, place] = turned[r * CHUNK : (r + 1) * CHUNK]
     lined = jnp.concatenate([flat[r] for r in range(count)], axis=1)
     gram = lax.dot_general(lined, lined, (((1,), (1,)), ((), ())), preferred_element_type=F32)
-    out_ref[...] = start_ref[...]
-    out_ref[:, :total] += gram
-
-
-def gram_partial(blocks, start):
+    top = total // 2
+    out_ref[:top] = jnp.concatenate([gram[:top], gram[top:]], axis=1)
+    out_ref[top:] = energy_ref[...]
+
+
+def gram_partial(blocks, energies):
     local, count, d = blocks[0].shape
-    total, width = start.shape
+    total = local * len(blocks)
     return pl.pallas_call(
         gram_kernel,
-        out_shape=jax.ShapeDtypeStruct((total, width), F32),
+        out_shape=jax.ShapeDtypeStruct((total // 2 + local, 2 * total), F32),
         scratch_shapes=[pltpu.VMEM((count, total, d), BF16)],
         compiler_params=pltpu.CompilerParams(vmem_limit_bytes=VMEM_LIMIT),
         cost_estimate=pl.CostEstimate(
@@ -168,7 +162,7 @@
             transcendentals=0,
         ),
         name="gram_partial",
-    )(*in_turn(blocks), start)
+    )(*in_turn(blocks), energies)
 
 
 def eliminate(matrix, total):
@@ -210,13 +204,35 @@
     return parts
 
 
-def solve_kernel(grams, *refs):
-    gram_refs, (*block_refs, weights_ref, update_ref, held) = refs[:grams], refs[grams:]
+def copies_kernel(*refs):
+    *part_refs, out_ref = refs
+    total = tree_sum([ref[...] for ref in part_refs])
+    for i in range(out_ref.shape[0]):
+        out_ref[i] = total
+
+
+def summed_copies(parts, count):
+    return pl.pallas_call(
+        copies_kernel,
+        out_shape=jax.ShapeDtypeStruct((count, *parts[0].shape), F32),
+        compiler_params=pltpu.CompilerParams(vmem_limit_bytes=VMEM_LIMIT),
+        name="summed_copies",
+    )(*parts)
+
+
+def solve_kernel(*refs):
+    gram_ref, *block_refs, weights_ref, update_ref, held = refs
     block_refs = in_place(block_refs)
     mats, share, d = update_ref.shape
     local = weights_ref.shape[1]
-    total, width = gram_refs[0].shape
-    raw = tree_sum([ref[...] for ref in gram_refs])
+    total = gram_ref.shape[2] // 2
+    top = total // 2
+    width = (total // LANES + 1) * LANES
+    packed = tree_sum([gram_ref[i] for i in range(gram_ref.shape[0])])
+    raw = jnp.concatenate([packed[:top, :total], packed[:top, total:]], axis=0)
+    energy = [packed[top:, i : i + 1] for i in range(total // local)]
+    energy = jnp.concatenate(energy, axis=0)
+    raw = jnp.concatenate([raw, jnp.broadcast_to(energy, (total, width - total))], axis=1)
     row = iota((total, width), 0)
     lane = iota((total, width), 1)
     inside = lane < total
@@ -247,11 +263,11 @@
         update_ref[m] = acc[m * share : (m + 1) * share]
 
 
-def solve_and_project(grams, blocks, mats):
-    total, width = grams[0].shape
+def solve_and_project(gram, blocks, mats):
     local, count, d = blocks[0].shape
-    return pl.pallas_call(
-        functools.partial(solve_kernel, len(grams)),
+    total = local * len(blocks)
+    return pl.pallas_call(
+        solve_kernel,
         out_shape=(
             jax.ShapeDtypeStruct((1, local), F32),
             jax.ShapeDtypeStruct((mats, count // mats, d), F32),
@@ -259,25 +275,22 @@
         scratch_shapes=[pltpu.VMEM((total, d), F32)],
         compiler_params=pltpu.CompilerParams(vmem_limit_bytes=VMEM_LIMIT),
         name="solve_and_project",
-    )(*grams, *in_turn(blocks))
+    )(gram, *in_turn(blocks))
 
 
 def body(spins, activations, cotangents, offdiag):
     local, mats = activations.shape[:2]
     owners = lax.axis_size("samp")
     total = local * owners
-    width = (total // LANES + 1) * LANES
     blocks = list(jac_rows(activations, cotangents, owners))
     for k in turns(owners)[:-1]:
         blocks[k] = lax.ppermute(blocks[k], "samp", [(i, i ^ k) for i in range(owners)])
-    partial = gram_partial(blocks, energy_column(spins, offdiag, total, width))
-    grams = partners(partial, "layer", 1, lax.axis_size("layer"))
-    first = 1
-    while first < owners:
-        count = 2 if first == 1 else min(4, owners // first)
-        grams = partners(tree_sum(grams), "samp", first, count)
-        first *= count
-    weights, update = solve_and_project(grams, blocks, mats)
+    partial = gram_partial(blocks, energy_rows(spins, offdiag, 2 * total))
+    parts = partners(partial, "layer", 1, lax.axis_size("layer"))
+    gram = lax.all_to_all(
+        summed_copies(parts, owners), "samp", split_axis=0, concat_axis=0, tiled=True
+    )
+    weights, update = solve_and_project(gram, blocks, mats)
     return weights.reshape(local), update
 
 

time: 80.8 us -> 80.9 us (level)
  blocking collectives: 0 us -> 16.5 us
  starting transfers between devices: 25.9 us -> 16.9 us
  waiting for transfers between devices: 41.9 us -> 33.2 us
  Pallas kernels: 12.1 us -> 13.3 us
    all_to_all x0 -> x1, blocking collectives: none -> 16.5 us  [body(): lax.all_to_all(summed_copies(parts, owners), 'samp', split_axis=0, concat...]
    ppermute x7 -> x3, starting transfers between devices: 10.9 us -> 1.93 us  [partners(): parts.append(lax.ppermute(value, axis, perm))]
    ppermute x7 -> x3, waiting for transfers between devices: 10.8 us -> 2.12 us  [partners(): parts.append(lax.ppermute(value, axis, perm))]
    pallas_call x3 -> x4, Pallas kernels: 8.46 us -> 9.62 us  [the longest x1 6.93 us: solve_and_project(): pl.pallas_call(solve_kernel, out_shape=(jax.ShapeDtypeStruct((1, local),...]
  transfers between devices with their start and end apart: 14 -> 10, of which waited for: 9 -> 6; matrix products, arithmetic and copies ran while one was open for 0% -> 0% of each run, Pallas kernels for 0% -> 0%
where the time goes in v12:
time: 80.9 us; the launch traced here: 80.7 us
  waiting for transfers between devices  33.2 us (41%)
  starting transfers between devices  16.9 us (21%)
  blocking collectives  16.5 us (20%)
  Pallas kernels  13.3 us (16%)
    ppermute x7, waiting for transfers between devices, body(): lax.ppermute(blocks[k], 'samp', [(i, i ^ k) for i in range(owners)])  31.1 us
    all_to_all x1, blocking collectives, body(): lax.all_to_all(summed_copies(parts, owners), 'samp', split_axis=0, concat...  16.5 us
    ppermute x7, starting transfers between devices, body(): lax.ppermute(blocks[k], 'samp', [(i, i ^ k) for i in range(owners)])  15 us
    pallas_call x1, Pallas kernels, solve_and_project(): pl.pallas_call(solve_kernel, out_shape=(jax.ShapeDtypeStruct((1, local),...  6.93 us
    pallas_call x1, Pallas kernels, jac_rows(): pl.pallas_call(jac_kernel, in_specs=[hbm, hbm], out_shape=[jax.ShapeDtype...  3.64 us
    pallas_call x1, Pallas kernels, gram_partial(): pl.pallas_call(gram_kernel, out_shape=jax.ShapeDtypeStruct((total // 2 +...  2.45 us
    ppermute x3, waiting for transfers between devices, partners(): parts.append(lax.ppermute(value, axis, perm))  2.12 us
    ppermute x3, starting transfers between devices, partners(): parts.append(lax.ppermute(value, axis, perm))  1.93 us
  transfers between devices with their start and end apart: 10, of which 6 were waited for; matrix products, arithmetic and copies ran while one was open for 0% of the time, Pallas kernels for 0%

profile of v12, /device:TPU:0, one launch (start us, length us, event | category | flops | bytes accessed | tf_op | source)
XLA Modules:
  0.0 80.7 jit_solution(11320903667537432032)
XLA Ops:
  0.6 0.0 copy-start.1
  0.6 0.0 copy-start
  0.7 3.6 %jac_rows.1 = (bf16[8,64,256]{2,1,0:T(8,128)(2,1)S(1)}, bf16[8,64,256]{2,1,0:T(8,128)(2,1)S(1)}, bf16[8,64,256]{2,1,0:T(8,128)(2,1)S(1)}, bf16[8,64,256]{2,1,0:T...) custom-call(bf16[8,2,256,256]{3,2,1,0:T(8,128)(2,1)} %act_hbm.1, ...), custom_call_target="tpu_custom_call" | custom-call | flops 536870912 | bytes 6291456 | tf_op jit(solution)/shard_map/jac_rows/pallas_call | solution.py:80
  4.3 4.1 %collective-permute-start = (bf16[8,64,256]{2,1,0:T(8,128)(2,1)S(1)}, bf16[8,64,256]{2,1,0:T(8,128)(2,1)S(1)}, u32[]{:S(2)}, u32[]{:S(2)}) collective-permute-start(bf16[8,64,256]{2,1,0:T(8,128)(2,1)S(1)} %get-tuple-element.12), channel_id=1, source_target_pairs={{0,16},{4,20},{8,24},{12,28},{16,0},{20,4},{24,8},{28,12},{1,17},{... | collective-permute-start | bytes 786440 | tf_op jit(solution)/shard_map/ppermute | solution.py:287
  8.4 1.3 %collective-permute-start.1 = (bf16[8,64,256]{2,1,0:T(8,128)(2,1)S(1)}, bf16[8,64,256]{2,1,0:T(8,128)(2,1)S(1)}, u32[]{:S(2)}, u32[]{:S(2)}) collective-permute-start(bf16[8,64,256]{2,1,0:T(8,128)(2,1)S(1)} %get-tuple-element.13), channel_id=1, source_target_pairs={{0,20},{4,16},{8,28},{12,24},{16,4},{20,0},{24,12},{28,8},{1,21},{... | collective-permute-start | bytes 786440 | tf_op jit(solution)/shard_map/ppermute | solution.py:287
  9.7 1.5 %collective-permute-start.2 = (bf16[8,64,256]{2,1,0:T(8,128)(2,1)S(1)}, bf16[8,64,256]{2,1,0:T(8,128)(2,1)S(1)}, u32[]{:S(2)}, u32[]{:S(2)}) collective-permute-start(bf16[8,64,256]{2,1,0:T(8,128)(2,1)S(1)} %get-tuple-element.14), channel_id=1, source_target_pairs={{0,12},{4,8},{8,4},{12,0},{16,28},{20,24},{24,20},{28,16},{1,13},{... | collective-permute-start | bytes 786440 | tf_op jit(solution)/shard_map/ppermute | solution.py:287
  11.2 2.5 %collective-permute-start.3 = (bf16[8,64,256]{2,1,0:T(8,128)(2,1)S(1)}, bf16[8,64,256]{2,1,0:T(8,128)(2,1)S(1)}, u32[]{:S(2)}, u32[]{:S(2)}) collective-permute-start(bf16[8,64,256]{2,1,0:T(8,128)(2,1)S(1)} %get-tuple-element.15), channel_id=1, source_target_pairs={{0,24},{4,28},{8,16},{12,20},{16,8},{20,12},{24,0},{28,4},{1,25},{... | collective-permute-start | bytes 786440 | tf_op jit(solution)/shard_map/ppermute | solution.py:287
  13.7 0.7 collective-permute-start.4
  14.4 12.5 %collective-permute-done.refs_0_.refs_1_ = bf16[8,64,256]{2,1,0:T(8,128)(2,1)S(1)} collective-permute-done((bf16[8,64,256]{2,1,0:T(8,128)(2,1)S(1)}, bf16[8,64,256]{2,1,0:T(8,128)(2,1)S(1)}, u32[]{:S(2)}, u32[]{:S(2)}) %collective-permute-start) | collective-permute-done | bytes 262176 | tf_op jit(solution)/shard_map/ppermute | solution.py:287
  26.9 4.9 %collective-permute-start.5 = (bf16[8,64,256]{2,1,0:T(8,128)(2,1)}, bf16[8,64,256]{2,1,0:T(8,128)(2,1)S(1)}, u32[]{:S(2)}, u32[]{:S(2)}) collective-permute-start(bf16[8,64,256]{2,1,0:T(8,128)(2,1)} %get-tuple-element.17), channel_id=1, source_target_pairs={{0,28},{4,24},{8,20},{12,16},{16,12},{20,8},{24,4},{28,0},{1,29},{... | collective-permute-start | bytes 786440 | tf_op jit(solution)/shard_map/ppermute | solution.py:287
  31.8 7.7 %collective-permute-done.1.refs_1_.refs_2_ = bf16[8,64,256]{2,1,0:T(8,128)(2,1)S(1)} collective-permute-done((bf16[8,64,256]{2,1,0:T(8,128)(2,1)S(1)}, bf16[8,64,256]{2,1,0:T(8,128)(2,1)S(1)}, u32[]{:S(2)}, u32[]{:S(2)}) %collective-permute-start.1) | collective-permute-done | bytes 262176 | tf_op jit(solution)/shard_map/ppermute | solution.py:287
  39.5 0.0 collective-permute-start.6
  39.5 0.0 copy-done.1
  39.5 0.1 copy.6.offdiag_ref
  39.6 0.0 copy-done
  39.6 0.2 energy_rows.1.refs_8_
  39.8 0.0 collective-permute-done.2.refs_2_.refs_3_
  39.8 0.0 collective-permute-done.3.refs_3_.refs_4_
  39.8 0.0 collective-permute-done.4.refs_4_.refs_5_
  39.8 6.2 %collective-permute-done.5.refs_5_.refs_6_ = bf16[8,64,256]{2,1,0:T(8,128)(2,1)S(1)} collective-permute-done((bf16[8,64,256]{2,1,0:T(8,128)(2,1)}, bf16[8,64,256]{2,1,0:T(8,128)(2,1)S(1)}, u32[]{:S(2)}, u32[]{:S(2)}) %collective-permute-start.5) | collective-permute-done | bytes 262176 | tf_op jit(solution)/shard_map/ppermute | solution.py:287
  46.1 4.7 %collective-permute-done.6.refs_6_.refs_7_ = bf16[8,64,256]{2,1,0:T(8,128)(2,1)S(1)} collective-permute-done((bf16[8,64,256]{2,1,0:T(8,128)(2,1)S(1)}, bf16[8,64,256]{2,1,0:T(8,128)(2,1)S(1)}, u32[]{:S(2)}, u32[]{:S(2)}) %collective-permute-start.6) | collective-permute-done | bytes 262176 | tf_op jit(solution)/shard_map/ppermute | solution.py:287
  50.7 2.5 %gram_partial.1.refs_0_ = f32[40,128]{1,0:T(8,128)S(1)} custom-call(bf16[8,64,256]{2,1,0:T(8,128)(2,1)S(1)} %collective-permute-done.refs_0_.refs_1_, bf16[8,64,256]{2,1,0:T(8,128)(2,1)S(1)} %collective-permute-done.1.refs_1_.refs_2_, bf16[8,64,256]{2,1,0:T(8,128)(2,1)S(1)} %collective-permute-done.2.refs_2_.refs_3_, ...), custom_call_target="tpu_custom_call" | custom-call | flops 134217728 | bytes 2097152 | tf_op jit(solution)/shard_map/gram_partial/pallas_call | solution.py:154
  53.2 0.3 collective-permute-start.9
  53.5 1.4 %collective-permute-start.8 = (f32[40,128]{1,0:T(8,128)S(1)}, f32[40,128]{1,0:T(8,128)S(1)}, u32[]{:S(2)}, u32[]{:S(2)}) collective-permute-start(f32[40,128]{1,0:T(8,128)S(1)} %gram_partial.1.refs_0_), channel_id=1, source_target_pairs={{0,2},{1,3},{2,0},{3,1},{4,6},{5,7},{6,4},{7,5},{8,10},{9,11},{10,... | collective-permute-start | bytes 61448 | tf_op jit(solution)/shard_map/ppermute | solution.py:203
  54.8 0.3 collective-permute-start.7
  55.1 1.5 %collective-permute-done.9.refs_3_ = f32[40,128]{1,0:T(8,128)S(1)} collective-permute-done((f32[40,128]{1,0:T(8,128)S(1)}, f32[40,128]{1,0:T(8,128)S(1)}, u32[]{:S(2)}, u32[]{:S(2)}) %collective-permute-start.9) | collective-permute-done | bytes 20512 | tf_op jit(solution)/shard_map/ppermute | solution.py:203
  56.6 0.6 collective-permute-done.8.refs_2_
  57.2 0.0 collective-permute-done.7.refs_1_
  57.3 16.5 %all_to_all.5.refs_0_ = f32[8,40,128]{2,1,0:T(8,128)S(1)} all-to-all(f32[8,40,128]{2,1,0:T(8,128)S(1)} %summed_copies.1), channel_id=1, replica_groups=mesh['samp'=8,'layer'=4] {'samp'}, dimensions={0} | all-to-all | bytes 327680 | tf_op jit(solution)/shard_map/all_to_all | solution.py:290
  73.8 6.9 %solve_and_project.1 = (f32[1,8]{1,0:T(1,128)}, f32[2,32,256]{2,1,0:T(8,128)}) custom-call(f32[8,40,128]{2,1,0:T(8,128)S(1)} %all_to_all.5.refs_0_, bf16[8,64,256]{2,1,0:T(8,128)(2,1)S(1)} %collective-permute-done.refs_0_.refs_1_, bf16[8,64,256]{2,1,0:T(8,128)(2,1)S(1)} %collective-permute-done.1.refs_1_.refs_2_, ...), custom_call_target="tpu_custom_call" | custom-call | tf_op jit(solution)/shard_map/solve_and_project/pallas_call | solution.py:269
  (1 shorter events, 0.0 us)
Async XLA Ops:
  0.6 38.9 %copy-start.1 = (f32[8]{0:T(128)S(1)}, f32[8]{0:T(128)}, u32[]{:S(2)}) copy-start(f32[8]{0:T(128)} %param.7) | copy-start | bytes 100
  0.6 39.0 %copy-start = (s32[8,256]{1,0:T(8,128)S(1)}, s32[8,256]{1,0:T(8,128)}, u32[]{:S(2)}) copy-start(s32[8,256]{1,0:T(8,128)} %spins_ref.1) | copy-start | bytes 24580
  4.3 22.6 %collective-permute-start = (bf16[8,64,256]{2,1,0:T(8,128)(2,1)S(1)}, bf16[8,64,256]{2,1,0:T(8,128)(2,1)S(1)}, u32[]{:S(2)}, u32[]{:S(2)}) collective-permute-start(bf16[8,64,256]{2,1,0:T(8,128)(2,1)S(1)} %get-tuple-element.12), channel_id=1, source_target_pairs={{0,16},{4,20},{8,24},{12,28},{16,0},{20,4},{24,8},{28,12},{1,17},{... | collective-permute-start | bytes 786440 | tf_op jit(solution)/shard_map/ppermute | solution.py:287
  8.4 31.1 %collective-permute-start.1 = (bf16[8,64,256]{2,1,0:T(8,128)(2,1)S(1)}, bf16[8,64,256]{2,1,0:T(8,128)(2,1)S(1)}, u32[]{:S(2)}, u32[]{:S(2)}) collective-permute-start(bf16[8,64,256]{2,1,0:T(8,128)(2,1)S(1)} %get-tuple-element.13), channel_id=1, source_target_pairs={{0,20},{4,16},{8,28},{12,24},{16,4},{20,0},{24,12},{28,8},{1,21},{... | collective-permute-start | bytes 786440 | tf_op jit(solution)/shard_map/ppermute | solution.py:287
  9.7 30.1 %collective-permute-start.2 = (bf16[8,64,256]{2,1,0:T(8,128)(2,1)S(1)}, bf16[8,64,256]{2,1,0:T(8,128)(2,1)S(1)}, u32[]{:S(2)}, u32[]{:S(2)}) collective-permute-start(bf16[8,64,256]{2,1,0:T(8,128)(2,1)S(1)} %get-tuple-element.14), channel_id=1, source_target_pairs={{0,12},{4,8},{8,4},{12,0},{16,28},{20,24},{24,20},{28,16},{1,13},{... | collective-permute-start | bytes 786440 | tf_op jit(solution)/shard_map/ppermute | solution.py:287
  11.2 28.6 %collective-permute-start.3 = (bf16[8,64,256]{2,1,0:T(8,128)(2,1)S(1)}, bf16[8,64,256]{2,1,0:T(8,128)(2,1)S(1)}, u32[]{:S(2)}, u32[]{:S(2)}) collective-permute-start(bf16[8,64,256]{2,1,0:T(8,128)(2,1)S(1)} %get-tuple-element.15), channel_id=1, source_target_pairs={{0,24},{4,28},{8,16},{12,20},{16,8},{20,12},{24,0},{28,4},{1,25},{... | collective-permute-start | bytes 786440 | tf_op jit(solution)/shard_map/ppermute | solution.py:287
  13.7 26.1 %collective-permute-start.4 = (bf16[8,64,256]{2,1,0:T(8,128)(2,1)S(1)}, bf16[8,64,256]{2,1,0:T(8,128)(2,1)S(1)}, u32[]{:S(2)}, u32[]{:S(2)}) collective-permute-start(bf16[8,64,256]{2,1,0:T(8,128)(2,1)S(1)} %get-tuple-element.16), channel_id=1, source_target_pairs={{0,8},{4,12},{8,0},{12,4},{16,24},{20,28},{24,16},{28,20},{1,9},{5... | collective-permute-start | bytes 786440 | tf_op jit(solution)/shard_map/ppermute | solution.py:287
  26.9 19.2 %collective-permute-start.5 = (bf16[8,64,256]{2,1,0:T(8,128)(2,1)}, bf16[8,64,256]{2,1,0:T(8,128)(2,1)S(1)}, u32[]{:S(2)}, u32[]{:S(2)}) collective-permute-start(bf16[8,64,256]{2,1,0:T(8,128)(2,1)} %get-tuple-element.17), channel_id=1, source_target_pairs={{0,28},{4,24},{8,20},{12,16},{16,12},{20,8},{24,4},{28,0},{1,29},{... | collective-permute-start | bytes 786440 | tf_op jit(solution)/shard_map/ppermute | solution.py:287
  39.5 11.2 %collective-permute-start.6 = (bf16[8,64,256]{2,1,0:T(8,128)(2,1)S(1)}, bf16[8,64,256]{2,1,0:T(8,128)(2,1)S(1)}, u32[]{:S(2)}, u32[]{:S(2)}) collective-permute-start(bf16[8,64,256]{2,1,0:T(8,128)(2,1)S(1)} %get-tuple-element.18), channel_id=1, source_target_pairs={{0,4},{4,0},{8,12},{12,8},{16,20},{20,16},{24,28},{28,24},{1,5},{5... | collective-permute-start | bytes 786440 | tf_op jit(solution)/shard_map/ppermute | solution.py:287
  53.2 3.4 %collective-permute-start.9 = (f32[40,128]{1,0:T(8,128)S(1)}, f32[40,128]{1,0:T(8,128)S(1)}, u32[]{:S(2)}, u32[]{:S(2)}) collective-permute-start(f32[40,128]{1,0:T(8,128)S(1)} %gram_partial.1.refs_0_), channel_id=1, source_target_pairs={{0,3},{1,2},{2,1},{3,0},{4,7},{5,6},{6,5},{7,4},{8,11},{9,10},{10,... | collective-permute-start | bytes 61448 | tf_op jit(solution)/shard_map/ppermute | solution.py:203
  53.5 3.8 %collective-permute-start.8 = (f32[40,128]{1,0:T(8,128)S(1)}, f32[40,128]{1,0:T(8,128)S(1)}, u32[]{:S(2)}, u32[]{:S(2)}) collective-permute-start(f32[40,128]{1,0:T(8,128)S(1)} %gram_partial.1.refs_0_), channel_id=1, source_target_pairs={{0,2},{1,3},{2,0},{3,1},{4,6},{5,7},{6,4},{7,5},{8,10},{9,11},{10,... | collective-permute-start | bytes 61448 | tf_op jit(solution)/shard_map/ppermute | solution.py:203
  54.8 2.4 %collective-permute-start.7 = (f32[40,128]{1,0:T(8,128)S(1)}, f32[40,128]{1,0:T(8,128)S(1)}, u32[]{:S(2)}, u32[]{:S(2)}) collective-permute-start(f32[40,128]{1,0:T(8,128)S(1)} %gram_partial.1.refs_0_), channel_id=1, source_target_pairs={{0,1},{1,0},{2,3},{3,2},{4,5},{5,4},{6,7},{7,6},{8,9},{9,8},{10,11... | collective-permute-start | bytes 61448 | tf_op jit(solution)/shard_map/ppermute | solution.py:203

commit v13 on v11

--- a/solution.py
+++ b/solution.py
@@ -274,7 +274,7 @@
     grams = partners(partial, "layer", 1, lax.axis_size("layer"))
     first = 1
     while first < owners:
-        count = 2 if first == 1 else min(4, owners // first)
+        count = min(4, owners // first)
         grams = partners(tree_sum(grams), "samp", first, count)
         first *= count
     weights, update = solve_and_project(grams, blocks, mats)

time: 80.8 us -> 79.6 us (0.985)
  waiting for transfers between devices: 41.9 us -> 40.9 us
    ppermute x7, waiting for transfers between devices: 10.8 us -> 9.81 us  [partners(): parts.append(lax.ppermute(value, axis, perm))]
where the time goes in v13:
time: 79.6 us; the launch traced here: 79.4 us
  waiting for transfers between devices  40.9 us (51%)
  starting transfers between devices  25.6 us (32%)
  Pallas kernels  12.1 us (15%)
    ppermute x7, waiting for transfers between devices, body(): lax.ppermute(blocks[k], 'samp', [(i, i ^ k) for i in range(owners)])  31.1 us
    ppermute x7, starting transfers between devices, body(): lax.ppermute(blocks[k], 'samp', [(i, i ^ k) for i in range(owners)])  15 us
    ppermute x7, starting transfers between devices, partners(): parts.append(lax.ppermute(value, axis, perm))  10.6 us
    ppermute x7, waiting for transfers between devices, partners(): parts.append(lax.ppermute(value, axis, perm))  9.81 us
    pallas_call x1, Pallas kernels, solve_and_project(): pl.pallas_call(functools.partial(solve_kernel, len(grams)), out_shape=(ja...  6.8 us
    pallas_call x1, Pallas kernels, jac_rows(): pl.pallas_call(jac_kernel, in_specs=[hbm, hbm], out_shape=[jax.ShapeDtype...  3.64 us
  transfers between devices with their start and end apart: 14, of which 9 were waited for; matrix products, arithmetic and copies ran while one was open for 0% of the time, Pallas kernels for 0%

profile of v13, /device:TPU:0, one launch (start us, length us, event | category | flops | bytes accessed | tf_op | source)
XLA Modules:
  0.0 79.4 jit_solution(7421017039845664731)
XLA Ops:
  0.6 0.0 copy-start.1
  0.6 0.0 copy-start
  0.7 3.6 %jac_rows.1 = (bf16[8,64,256]{2,1,0:T(8,128)(2,1)S(1)}, bf16[8,64,256]{2,1,0:T(8,128)(2,1)S(1)}, bf16[8,64,256]{2,1,0:T(8,128)(2,1)S(1)}, bf16[8,64,256]{2,1,0:T...) custom-call(bf16[8,2,256,256]{3,2,1,0:T(8,128)(2,1)} %act_hbm.1, ...), custom_call_target="tpu_custom_call" | custom-call | flops 536870912 | bytes 6291456 | tf_op jit(solution)/shard_map/jac_rows/pallas_call | solution.py:82
  4.3 4.1 %collective-permute-start = (bf16[8,64,256]{2,1,0:T(8,128)(2,1)S(1)}, bf16[8,64,256]{2,1,0:T(8,128)(2,1)S(1)}, u32[]{:S(2)}, u32[]{:S(2)}) collective-permute-start(bf16[8,64,256]{2,1,0:T(8,128)(2,1)S(1)} %get-tuple-element.12), channel_id=1, source_target_pairs={{0,16},{4,20},{8,24},{12,28},{16,0},{20,4},{24,8},{28,12},{1,17},{... | collective-permute-start | bytes 786440 | tf_op jit(solution)/shard_map/ppermute | solution.py:272
  8.4 1.3 %collective-permute-start.1 = (bf16[8,64,256]{2,1,0:T(8,128)(2,1)S(1)}, bf16[8,64,256]{2,1,0:T(8,128)(2,1)S(1)}, u32[]{:S(2)}, u32[]{:S(2)}) collective-permute-start(bf16[8,64,256]{2,1,0:T(8,128)(2,1)S(1)} %get-tuple-element.13), channel_id=1, source_target_pairs={{0,20},{4,16},{8,28},{12,24},{16,4},{20,0},{24,12},{28,8},{1,21},{... | collective-permute-start | bytes 786440 | tf_op jit(solution)/shard_map/ppermute | solution.py:272
  9.7 1.5 %collective-permute-start.2 = (bf16[8,64,256]{2,1,0:T(8,128)(2,1)S(1)}, bf16[8,64,256]{2,1,0:T(8,128)(2,1)S(1)}, u32[]{:S(2)}, u32[]{:S(2)}) collective-permute-start(bf16[8,64,256]{2,1,0:T(8,128)(2,1)S(1)} %get-tuple-element.14), channel_id=1, source_target_pairs={{0,12},{4,8},{8,4},{12,0},{16,28},{20,24},{24,20},{28,16},{1,13},{... | collective-permute-start | bytes 786440 | tf_op jit(solution)/shard_map/ppermute | solution.py:272
  11.2 2.5 %collective-permute-start.3 = (bf16[8,64,256]{2,1,0:T(8,128)(2,1)S(1)}, bf16[8,64,256]{2,1,0:T(8,128)(2,1)S(1)}, u32[]{:S(2)}, u32[]{:S(2)}) collective-permute-start(bf16[8,64,256]{2,1,0:T(8,128)(2,1)S(1)} %get-tuple-element.15), channel_id=1, source_target_pairs={{0,24},{4,28},{8,16},{12,20},{16,8},{20,12},{24,0},{28,4},{1,25},{... | collective-permute-start | bytes 786440 | tf_op jit(solution)/shard_map/ppermute | solution.py:272
  13.7 0.7 collective-permute-start.4
  14.4 12.5 %collective-permute-done.refs_0_.refs_2_ = bf16[8,64,256]{2,1,0:T(8,128)(2,1)S(1)} collective-permute-done((bf16[8,64,256]{2,1,0:T(8,128)(2,1)S(1)}, bf16[8,64,256]{2,1,0:T(8,128)(2,1)S(1)}, u32[]{:S(2)}, u32[]{:S(2)}) %collective-permute-start) | collective-permute-done | bytes 262176 | tf_op jit(solution)/shard_map/ppermute | solution.py:272
  26.9 4.9 %collective-permute-start.5 = (bf16[8,64,256]{2,1,0:T(8,128)(2,1)}, bf16[8,64,256]{2,1,0:T(8,128)(2,1)S(1)}, u32[]{:S(2)}, u32[]{:S(2)}) collective-permute-start(bf16[8,64,256]{2,1,0:T(8,128)(2,1)} %get-tuple-element.17), channel_id=1, source_target_pairs={{0,28},{4,24},{8,20},{12,16},{16,12},{20,8},{24,4},{28,0},{1,29},{... | collective-permute-start | bytes 786440 | tf_op jit(solution)/shard_map/ppermute | solution.py:272
  31.8 7.7 %collective-permute-done.1.refs_1_.refs_3_ = bf16[8,64,256]{2,1,0:T(8,128)(2,1)S(1)} collective-permute-done((bf16[8,64,256]{2,1,0:T(8,128)(2,1)S(1)}, bf16[8,64,256]{2,1,0:T(8,128)(2,1)S(1)}, u32[]{:S(2)}, u32[]{:S(2)}) %collective-permute-start.1) | collective-permute-done | bytes 262176 | tf_op jit(solution)/shard_map/ppermute | solution.py:272
  39.5 0.0 collective-permute-start.6
  39.5 0.0 copy-done.1
  39.5 0.1 copy.6.offdiag_ref
  39.6 0.0 copy-done
  39.6 0.2 energy_column.1.refs_8_
  39.8 0.0 collective-permute-done.2.refs_2_.refs_4_
  39.8 0.0 collective-permute-done.3.refs_3_.refs_5_
  39.9 0.0 collective-permute-done.4.refs_4_.refs_6_
  39.9 6.2 %collective-permute-done.5.refs_5_.refs_7_ = bf16[8,64,256]{2,1,0:T(8,128)(2,1)S(1)} collective-permute-done((bf16[8,64,256]{2,1,0:T(8,128)(2,1)}, bf16[8,64,256]{2,1,0:T(8,128)(2,1)S(1)}, u32[]{:S(2)}, u32[]{:S(2)}) %collective-permute-start.5) | collective-permute-done | bytes 262176 | tf_op jit(solution)/shard_map/ppermute | solution.py:272
  46.1 4.7 %collective-permute-done.6.refs_6_.refs_8_ = bf16[8,64,256]{2,1,0:T(8,128)(2,1)S(1)} collective-permute-done((bf16[8,64,256]{2,1,0:T(8,128)(2,1)S(1)}, bf16[8,64,256]{2,1,0:T(8,128)(2,1)S(1)}, u32[]{:S(2)}, u32[]{:S(2)}) %collective-permute-start.6) | collective-permute-done | bytes 262176 | tf_op jit(solution)/shard_map/ppermute | solution.py:272
  50.7 1.4 %gram_partial.1 = f32[64,128]{1,0:T(8,128)S(1)} custom-call(bf16[8,64,256]{2,1,0:T(8,128)(2,1)S(1)} %collective-permute-done.refs_0_.refs_2_, bf16[8,64,256]{2,1,0:T(8,128)(2,1)S(1)} %collective-permute-done.1.refs_1_.refs_3_, bf16[8,64,256]{2,1,0:T(8,128)(2,1)S(1)} %collective-permute-done.2.refs_2_.refs_4_, ...), custom_call_target="tpu_custom_call" | custom-call | flops 134217728 | bytes 2097152 | tf_op jit(solution)/shard_map/gram_partial/pallas_call | solution.py:160
  52.2 0.1 collective-permute-start.7
  52.3 1.6 %collective-permute-start.8 = (f32[64,128]{1,0:T(8,128)S(1)}, f32[64,128]{1,0:T(8,128)S(1)}, u32[]{:S(2)}, u32[]{:S(2)}) collective-permute-start(f32[64,128]{1,0:T(8,128)S(1)} %gram_partial.1), channel_id=1, source_target_pairs={{0,2},{1,3},{2,0},{3,1},{4,6},{5,7},{6,4},{7,5},{8,10},{9,11},{10,... | collective-permute-start | bytes 98312 | tf_op jit(solution)/shard_map/ppermute | solution.py:209
  53.8 0.3 collective-permute-start.9
  54.1 0.0 collective-permute-done.7
  54.1 2.1 %collective-permute-done.8 = f32[64,128]{1,0:T(8,128)S(1)} collective-permute-done((f32[64,128]{1,0:T(8,128)S(1)}, f32[64,128]{1,0:T(8,128)S(1)}, u32[]{:S(2)}, u32[]{:S(2)}) %collective-permute-start.8) | collective-permute-done | bytes 32800 | tf_op jit(solution)/shard_map/ppermute | solution.py:209
  56.2 0.9 %collective-permute-done.9 = f32[64,128]{1,0:T(8,128)S(1)} collective-permute-done((f32[64,128]{1,0:T(8,128)S(1)}, f32[64,128]{1,0:T(8,128)S(1)}, u32[]{:S(2)}, u32[]{:S(2)}) %collective-permute-start.9) | collective-permute-done | bytes 32800 | tf_op jit(solution)/shard_map/ppermute | solution.py:209
  57.2 0.6 collective-permute-start.10
  57.7 5.2 %collective-permute-start.11 = (f32[64,128]{1,0:T(8,128)S(1)}, f32[64,128]{1,0:T(8,128)S(1)}, u32[]{:S(2)}, u32[]{:S(2)}) collective-permute-start(f32[64,128]{1,0:T(8,128)S(1)} %add_add_fusion.1), channel_id=1, source_target_pairs={{0,8},{4,12},{8,0},{12,4},{16,24},{20,28},{24,16},{28,20},{1,9},{5... | collective-permute-start | bytes 98312 | tf_op jit(solution)/shard_map/ppermute | solution.py:209
  62.9 0.7 collective-permute-start.12
  63.6 0.0 collective-permute-done.10
  63.6 1.2 %collective-permute-done.11 = f32[64,128]{1,0:T(8,128)S(1)} collective-permute-done((f32[64,128]{1,0:T(8,128)S(1)}, f32[64,128]{1,0:T(8,128)S(1)}, u32[]{:S(2)}, u32[]{:S(2)}) %collective-permute-start.11) | collective-permute-done | bytes 32800 | tf_op jit(solution)/shard_map/ppermute | solution.py:209
  64.8 2.9 %collective-permute-done.12 = f32[64,128]{1,0:T(8,128)S(1)} collective-permute-done((f32[64,128]{1,0:T(8,128)S(1)}, f32[64,128]{1,0:T(8,128)S(1)}, u32[]{:S(2)}, u32[]{:S(2)}) %collective-permute-start.12) | collective-permute-done | bytes 32800 | tf_op jit(solution)/shard_map/ppermute | solution.py:209
  67.8 2.2 %collective-permute-start.13 = (f32[64,128]{1,0:T(8,128)S(1)}, f32[64,128]{1,0:T(8,128)S(1)}, u32[]{:S(2)}, u32[]{:S(2)}) collective-permute-start(f32[64,128]{1,0:T(8,128)S(1)} %add_add_fusion.refs_0_), channel_id=1, source_target_pairs={{0,16},{4,20},{8,24},{12,28},{16,0},{20,4},{24,8},{28,12},{1,17},{... | collective-permute-start | bytes 98312 | tf_op jit(solution)/shard_map/ppermute | solution.py:209
  70.0 2.7 %collective-permute-done.13.refs_1_ = f32[64,128]{1,0:T(8,128)S(1)} collective-permute-done((f32[64,128]{1,0:T(8,128)S(1)}, f32[64,128]{1,0:T(8,128)S(1)}, u32[]{:S(2)}, u32[]{:S(2)}) %collective-permute-start.13) | collective-permute-done | bytes 32800 | tf_op jit(solution)/shard_map/ppermute | solution.py:209
  72.6 6.8 %solve_and_project.1 = (f32[1,8]{1,0:T(1,128)}, f32[2,32,256]{2,1,0:T(8,128)}) custom-call(f32[64,128]{1,0:T(8,128)S(1)} %add_add_fusion.refs_0_, f32[64,128]{1,0:T(8,128)S(1)} %collective-permute-done.13.refs_1_, bf16[8,64,256]{2,1,0:T(8,128)(2,1)S(1)} %collective-permute-done.refs_0_.refs_2_, ...), custom_call_target="tpu_custom_call" | custom-call | tf_op jit(solution)/shard_map/solve_and_project/pallas_call | solution.py:253
  (2 shorter events, 0.0 us)
Async XLA Ops:
  0.6 38.9 %copy-start.1 = (f32[8]{0:T(128)S(1)}, f32[8]{0:T(128)}, u32[]{:S(2)}) copy-start(f32[8]{0:T(128)} %param.7) | copy-start | bytes 100
  0.6 39.0 %copy-start = (s32[8,256]{1,0:T(8,128)S(1)}, s32[8,256]{1,0:T(8,128)}, u32[]{:S(2)}) copy-start(s32[8,256]{1,0:T(8,128)} %spins_ref.1) | copy-start | bytes 24580
  4.3 22.6 %collective-permute-start = (bf16[8,64,256]{2,1,0:T(8,128)(2,1)S(1)}, bf16[8,64,256]{2,1,0:T(8,128)(2,1)S(1)}, u32[]{:S(2)}, u32[]{:S(2)}) collective-permute-start(bf16[8,64,256]{2,1,0:T(8,128)(2,1)S(1)} %get-tuple-element.12), channel_id=1, source_target_pairs={{0,16},{4,20},{8,24},{12,28},{16,0},{20,4},{24,8},{28,12},{1,17},{... | collective-permute-start | bytes 786440 | tf_op jit(solution)/shard_map/ppermute | solution.py:272
  8.4 31.1 %collective-permute-start.1 = (bf16[8,64,256]{2,1,0:T(8,128)(2,1)S(1)}, bf16[8,64,256]{2,1,0:T(8,128)(2,1)S(1)}, u32[]{:S(2)}, u32[]{:S(2)}) collective-permute-start(bf16[8,64,256]{2,1,0:T(8,128)(2,1)S(1)} %get-tuple-element.13), channel_id=1, source_target_pairs={{0,20},{4,16},{8,28},{12,24},{16,4},{20,0},{24,12},{28,8},{1,21},{... | collective-permute-start | bytes 786440 | tf_op jit(solution)/shard_map/ppermute | solution.py:272
  9.7 30.1 %collective-permute-start.2 = (bf16[8,64,256]{2,1,0:T(8,128)(2,1)S(1)}, bf16[8,64,256]{2,1,0:T(8,128)(2,1)S(1)}, u32[]{:S(2)}, u32[]{:S(2)}) collective-permute-start(bf16[8,64,256]{2,1,0:T(8,128)(2,1)S(1)} %get-tuple-element.14), channel_id=1, source_target_pairs={{0,12},{4,8},{8,4},{12,0},{16,28},{20,24},{24,20},{28,16},{1,13},{... | collective-permute-start | bytes 786440 | tf_op jit(solution)/shard_map/ppermute | solution.py:272
  11.2 28.6 %collective-permute-start.3 = (bf16[8,64,256]{2,1,0:T(8,128)(2,1)S(1)}, bf16[8,64,256]{2,1,0:T(8,128)(2,1)S(1)}, u32[]{:S(2)}, u32[]{:S(2)}) collective-permute-start(bf16[8,64,256]{2,1,0:T(8,128)(2,1)S(1)} %get-tuple-element.15), channel_id=1, source_target_pairs={{0,24},{4,28},{8,16},{12,20},{16,8},{20,12},{24,0},{28,4},{1,25},{... | collective-permute-start | bytes 786440 | tf_op jit(solution)/shard_map/ppermute | solution.py:272
  13.7 26.2 %collective-permute-start.4 = (bf16[8,64,256]{2,1,0:T(8,128)(2,1)S(1)}, bf16[8,64,256]{2,1,0:T(8,128)(2,1)S(1)}, u32[]{:S(2)}, u32[]{:S(2)}) collective-permute-start(bf16[8,64,256]{2,1,0:T(8,128)(2,1)S(1)} %get-tuple-element.16), channel_id=1, source_target_pairs={{0,8},{4,12},{8,0},{12,4},{16,24},{20,28},{24,16},{28,20},{1,9},{5... | collective-permute-start | bytes 786440 | tf_op jit(solution)/shard_map/ppermute | solution.py:272
  26.9 19.2 %collective-permute-start.5 = (bf16[8,64,256]{2,1,0:T(8,128)(2,1)}, bf16[8,64,256]{2,1,0:T(8,128)(2,1)S(1)}, u32[]{:S(2)}, u32[]{:S(2)}) collective-permute-start(bf16[8,64,256]{2,1,0:T(8,128)(2,1)} %get-tuple-element.17), channel_id=1, source_target_pairs={{0,28},{4,24},{8,20},{12,16},{16,12},{20,8},{24,4},{28,0},{1,29},{... | collective-permute-start | bytes 786440 | tf_op jit(solution)/shard_map/ppermute | solution.py:272
  39.5 11.2 %collective-permute-start.6 = (bf16[8,64,256]{2,1,0:T(8,128)(2,1)S(1)}, bf16[8,64,256]{2,1,0:T(8,128)(2,1)S(1)}, u32[]{:S(2)}, u32[]{:S(2)}) collective-permute-start(bf16[8,64,256]{2,1,0:T(8,128)(2,1)S(1)} %get-tuple-element.18), channel_id=1, source_target_pairs={{0,4},{4,0},{8,12},{12,8},{16,20},{20,16},{24,28},{28,24},{1,5},{5... | collective-permute-start | bytes 786440 | tf_op jit(solution)/shard_map/ppermute | solution.py:272
  52.2 1.9 %collective-permute-start.7 = (f32[64,128]{1,0:T(8,128)S(1)}, f32[64,128]{1,0:T(8,128)S(1)}, u32[]{:S(2)}, u32[]{:S(2)}) collective-permute-start(f32[64,128]{1,0:T(8,128)S(1)} %gram_partial.1), channel_id=1, source_target_pairs={{0,1},{1,0},{2,3},{3,2},{4,5},{5,4},{6,7},{7,6},{8,9},{9,8},{10,11... | collective-permute-start | bytes 98312 | tf_op jit(solution)/shard_map/ppermute | solution.py:209
  52.3 4.0 %collective-permute-start.8 = (f32[64,128]{1,0:T(8,128)S(1)}, f32[64,128]{1,0:T(8,128)S(1)}, u32[]{:S(2)}, u32[]{:S(2)}) collective-permute-start(f32[64,128]{1,0:T(8,128)S(1)} %gram_partial.1), channel_id=1, source_target_pairs={{0,2},{1,3},{2,0},{3,1},{4,6},{5,7},{6,4},{7,5},{8,10},{9,11},{10,... | collective-permute-start | bytes 98312 | tf_op jit(solution)/shard_map/ppermute | solution.py:209
  53.8 3.3 %collective-permute-start.9 = (f32[64,128]{1,0:T(8,128)S(1)}, f32[64,128]{1,0:T(8,128)S(1)}, u32[]{:S(2)}, u32[]{:S(2)}) collective-permute-start(f32[64,128]{1,0:T(8,128)S(1)} %gram_partial.1), channel_id=1, source_target_pairs={{0,3},{1,2},{2,1},{3,0},{4,7},{5,6},{6,5},{7,4},{8,11},{9,10},{10,... | collective-permute-start | bytes 98312 | tf_op jit(solution)/shard_map/ppermute | solution.py:209
  57.2 6.5 %collective-permute-start.10 = (f32[64,128]{1,0:T(8,128)S(1)}, f32[64,128]{1,0:T(8,128)S(1)}, u32[]{:S(2)}, u32[]{:S(2)}) collective-permute-start(f32[64,128]{1,0:T(8,128)S(1)} %add_add_fusion.1), channel_id=1, source_target_pairs={{0,4},{4,0},{8,12},{12,8},{16,20},{20,16},{24,28},{28,24},{1,5},{5... | collective-permute-start | bytes 98312 | tf_op jit(solution)/shard_map/ppermute | solution.py:209
  57.7 7.1 %collective-permute-start.11 = (f32[64,128]{1,0:T(8,128)S(1)}, f32[64,128]{1,0:T(8,128)S(1)}, u32[]{:S(2)}, u32[]{:S(2)}) collective-permute-start(f32[64,128]{1,0:T(8,128)S(1)} %add_add_fusion.1), channel_id=1, source_target_pairs={{0,8},{4,12},{8,0},{12,4},{16,24},{20,28},{24,16},{28,20},{1,9},{5... | collective-permute-start | bytes 98312 | tf_op jit(solution)/shard_map/ppermute | solution.py:209
  62.9 4.8 %collective-permute-start.12 = (f32[64,128]{1,0:T(8,128)S(1)}, f32[64,128]{1,0:T(8,128)S(1)}, u32[]{:S(2)}, u32[]{:S(2)}) collective-permute-start(f32[64,128]{1,0:T(8,128)S(1)} %add_add_fusion.1), channel_id=1, source_target_pairs={{0,12},{4,8},{8,4},{12,0},{16,28},{20,24},{24,20},{28,16},{1,13},{... | collective-permute-start | bytes 98312 | tf_op jit(solution)/shard_map/ppermute | solution.py:209
  67.8 4.9 %collective-permute-start.13 = (f32[64,128]{1,0:T(8,128)S(1)}, f32[64,128]{1,0:T(8,128)S(1)}, u32[]{:S(2)}, u32[]{:S(2)}) collective-permute-start(f32[64,128]{1,0:T(8,128)S(1)} %add_add_fusion.refs_0_), channel_id=1, source_target_pairs={{0,16},{4,20},{8,24},{12,28},{16,0},{20,4},{24,8},{28,12},{1,17},{... | collective-permute-start | bytes 98312 | tf_op jit(solution)/shard_map/ppermute | solution.py:209

commit v14 on v13

--- a/solution.py
+++ b/solution.py
@@ -10,6 +10,7 @@
 SIDE = 16
 LANES = 128
 CHUNK = 16
+PIVOTS = 8
 VMEM_LIMIT = 24 * 2**20
 JAC_VMEM_LIMIT = 52 * 2**20
 shift_ratio = 0.1
@@ -171,34 +172,86 @@
     )(*in_turn(blocks), start)
 
 
+def tree_sum(parts):
+    while len(parts) > 1:
+        odd = parts[len(parts) // 2 * 2 :]
+        parts = [a + b for a, b in zip(parts[::2], parts[1::2])] + odd
+    return parts[0]
+
+
+def pivot_rows(rows, entries):
+    count = len(rows)
+    rows = list(rows)
+    p = [[entries[min(i, l)][max(i, l)] for l in range(count)] for i in range(count)]
+    uppers = {}
+    for j in range(0, count, 2):
+        a, b, c = p[j][j], p[j][j + 1], p[j + 1][j + 1]
+        inverse = F32(1.0) / (a * c - b * b)
+
+        def scaled(x, y):
+            return (c * x - b * y) * inverse, (a * y - b * x) * inverse
+
+        first, second = rows[j], rows[j + 1]
+        rows[j], rows[j + 1] = scaled(first, second)
+        later = range(j + 2, count)
+        for l in later:
+            uppers[j, l], uppers[j + 1, l] = scaled(p[j][l], p[j + 1][l])
+        for i in later:
+            rows[i] = rows[i] - (p[j][i] * rows[j] + p[j + 1][i] * rows[j + 1])
+            for l in range(i, count):
+                change = p[j][i] * uppers[j, l] + p[j + 1][i] * uppers[j + 1, l]
+                p[i][l] = p[l][i] = p[i][l] - change
+    for j in range(count - 4, -1, -2):
+        for i in (j, j + 1):
+            rows[i] = rows[i] - tree_sum([uppers[i, l] * rows[l] for l in range(j + 2, count)])
+    return rows
+
+
 def eliminate(matrix, total):
+    width = matrix.shape[1]
+    if total <= 64:
+        blocks = [matrix[i : i + PIVOTS] for i in range(0, total, PIVOTS)]
+        sub = iota((PIVOTS, width), 0)
+        for b in range(len(blocks)):
+            spread = [
+                [
+                    jnp.broadcast_to(block[:, b * PIVOTS + j : b * PIVOTS + j + 1], (PIVOTS, width))
+                    for block in blocks
+                ]
+                for j in range(PIVOTS)
+            ]
+
+            def line(value, i):
+                return jnp.broadcast_to(value[i : i + 1], (PIVOTS, width))
+
+            entries = [
+                [line(spread[l][b], i) if l >= i else None for l in range(PIVOTS)]
+                for i in range(PIVOTS)
+            ]
+            rows = pivot_rows([line(blocks[b], i) for i in range(PIVOTS)], entries)
+            for i in range(len(blocks)):
+                if i != b:
+                    terms = [spread[j][i] * rows[j] for j in range(PIVOTS)]
+                    blocks[i] = blocks[i] - tree_sum(terms)
+            solved = rows[0]
+            for j in range(1, PIVOTS):
+                solved = jnp.where(sub == j, rows[j], solved)
+            blocks[b] = solved
+        return jnp.concatenate([block[:, total : total + 1] for block in blocks], axis=0)
     row = iota(matrix.shape, 0)
     lane = iota(matrix.shape, 1)
-    if total <= 64:
-        for k in range(total):
-            column = matrix[:, k : k + 1]
-            pivot_row = matrix[k : k + 1, :]
-            scaled = pivot_row * (F32(1.0) / pivot_row[:, k : k + 1])
-            matrix = matrix - jnp.where(row == k, F32(0.0), column) * scaled
-    else:
-
-        def one(k, held):
-            column = jnp.sum(jnp.where(lane == k, held, F32(0.0)), axis=1, keepdims=True)
-            pivot_row = jnp.sum(jnp.where(row == k, held, F32(0.0)), axis=0, keepdims=True)
-            here = lane[:1] == k
-            pivot = jnp.sum(jnp.where(here, pivot_row, F32(0.0)), axis=1, keepdims=True)
-            scaled = pivot_row * (F32(1.0) / pivot)
-            return held - jnp.where(row == k, F32(0.0), column) * scaled
-
-        matrix = lax.fori_loop(0, total, one, matrix)
+
+    def one(k, held):
+        column = jnp.sum(jnp.where(lane == k, held, F32(0.0)), axis=1, keepdims=True)
+        pivot_row = jnp.sum(jnp.where(row == k, held, F32(0.0)), axis=0, keepdims=True)
+        here = lane[:1] == k
+        pivot = jnp.sum(jnp.where(here, pivot_row, F32(0.0)), axis=1, keepdims=True)
+        scaled = pivot_row * (F32(1.0) / pivot)
+        return held - jnp.where(row == k, F32(0.0), column) * scaled
+
+    matrix = lax.fori_loop(0, total, one, matrix)
     diag = jnp.sum(jnp.where(row == lane, matrix, F32(0.0)), axis=1, keepdims=True)
     return matrix[:, total : total + 1] / diag
-
-
-def tree_sum(parts):
-    while len(parts) > 1:
-        parts = [a + b for a, b in zip(parts[::2], parts[1::2])]
-    return parts[0]
 
 
 def partners(value, axis, first, count):

time: 79.6 us -> 76.1 us (0.956)
  Pallas kernels: 12.1 us -> 8.61 us
    pallas_call x1, Pallas kernels: 6.8 us -> 3.31 us  [solve_and_project(): pl.pallas_call(functools.partial(solve_kernel, len(grams)), out_shape=(ja...]
where the time goes in v14:
time: 76.1 us; the launch traced here: 76 us
  waiting for transfers between devices  40.9 us (54%)
  starting transfers between devices  25.6 us (34%)
  Pallas kernels  8.61 us (11%)
    ppermute x7, waiting for transfers between devices, body(): lax.ppermute(blocks[k], 'samp', [(i, i ^ k) for i in range(owners)])  31.1 us
    ppermute x7, starting transfers between devices, body(): lax.ppermute(blocks[k], 'samp', [(i, i ^ k) for i in range(owners)])  15 us
    ppermute x7, starting transfers between devices, partners(): parts.append(lax.ppermute(value, axis, perm))  10.6 us
    ppermute x7, waiting for transfers between devices, partners(): parts.append(lax.ppermute(value, axis, perm))  9.81 us
    pallas_call x1, Pallas kernels, jac_rows(): pl.pallas_call(jac_kernel, in_specs=[hbm, hbm], out_shape=[jax.ShapeDtype...  3.64 us
    pallas_call x1, Pallas kernels, solve_and_project(): pl.pallas_call(functools.partial(solve_kernel, len(grams)), out_shape=(ja...  3.31 us
  transfers between devices with their start and end apart: 14, of which 9 were waited for; matrix products, arithmetic and copies ran while one was open for 0% of the time, Pallas kernels for 0%

profile of v14, /device:TPU:0, one launch (start us, length us, event | category | flops | bytes accessed | tf_op | source)
XLA Modules:
  0.0 76.0 jit_solution(18434197499005527258)
XLA Ops:
  0.6 0.0 copy-start.1
  0.6 0.0 copy-start
  0.7 3.6 %jac_rows.1 = (bf16[8,64,256]{2,1,0:T(8,128)(2,1)S(1)}, bf16[8,64,256]{2,1,0:T(8,128)(2,1)S(1)}, bf16[8,64,256]{2,1,0:T(8,128)(2,1)S(1)}, bf16[8,64,256]{2,1,0:T...) custom-call(bf16[8,2,256,256]{3,2,1,0:T(8,128)(2,1)} %act_hbm.1, ...), custom_call_target="tpu_custom_call" | custom-call | flops 536870912 | bytes 6291456 | tf_op jit(solution)/shard_map/jac_rows/pallas_call | solution.py:83
  4.3 4.1 %collective-permute-start = (bf16[8,64,256]{2,1,0:T(8,128)(2,1)S(1)}, bf16[8,64,256]{2,1,0:T(8,128)(2,1)S(1)}, u32[]{:S(2)}, u32[]{:S(2)}) collective-permute-start(bf16[8,64,256]{2,1,0:T(8,128)(2,1)S(1)} %get-tuple-element.12), channel_id=1, source_target_pairs={{0,16},{4,20},{8,24},{12,28},{16,0},{20,4},{24,8},{28,12},{1,17},{... | collective-permute-start | bytes 786440 | tf_op jit(solution)/shard_map/ppermute | solution.py:325
  8.4 1.3 %collective-permute-start.1 = (bf16[8,64,256]{2,1,0:T(8,128)(2,1)S(1)}, bf16[8,64,256]{2,1,0:T(8,128)(2,1)S(1)}, u32[]{:S(2)}, u32[]{:S(2)}) collective-permute-start(bf16[8,64,256]{2,1,0:T(8,128)(2,1)S(1)} %get-tuple-element.13), channel_id=1, source_target_pairs={{0,20},{4,16},{8,28},{12,24},{16,4},{20,0},{24,12},{28,8},{1,21},{... | collective-permute-start | bytes 786440 | tf_op jit(solution)/shard_map/ppermute | solution.py:325
  9.7 1.5 %collective-permute-start.2 = (bf16[8,64,256]{2,1,0:T(8,128)(2,1)S(1)}, bf16[8,64,256]{2,1,0:T(8,128)(2,1)S(1)}, u32[]{:S(2)}, u32[]{:S(2)}) collective-permute-start(bf16[8,64,256]{2,1,0:T(8,128)(2,1)S(1)} %get-tuple-element.14), channel_id=1, source_target_pairs={{0,12},{4,8},{8,4},{12,0},{16,28},{20,24},{24,20},{28,16},{1,13},{... | collective-permute-start | bytes 786440 | tf_op jit(solution)/shard_map/ppermute | solution.py:325
  11.2 2.5 %collective-permute-start.3 = (bf16[8,64,256]{2,1,0:T(8,128)(2,1)S(1)}, bf16[8,64,256]{2,1,0:T(8,128)(2,1)S(1)}, u32[]{:S(2)}, u32[]{:S(2)}) collective-permute-start(bf16[8,64,256]{2,1,0:T(8,128)(2,1)S(1)} %get-tuple-element.15), channel_id=1, source_target_pairs={{0,24},{4,28},{8,16},{12,20},{16,8},{20,12},{24,0},{28,4},{1,25},{... | collective-permute-start | bytes 786440 | tf_op jit(solution)/shard_map/ppermute | solution.py:325
  13.7 0.7 collective-permute-start.4
  14.4 12.5 %collective-permute-done.refs_0_.refs_2_ = bf16[8,64,256]{2,1,0:T(8,128)(2,1)S(1)} collective-permute-done((bf16[8,64,256]{2,1,0:T(8,128)(2,1)S(1)}, bf16[8,64,256]{2,1,0:T(8,128)(2,1)S(1)}, u32[]{:S(2)}, u32[]{:S(2)}) %collective-permute-start) | collective-permute-done | bytes 262176 | tf_op jit(solution)/shard_map/ppermute | solution.py:325
  26.9 4.9 %collective-permute-start.5 = (bf16[8,64,256]{2,1,0:T(8,128)(2,1)}, bf16[8,64,256]{2,1,0:T(8,128)(2,1)S(1)}, u32[]{:S(2)}, u32[]{:S(2)}) collective-permute-start(bf16[8,64,256]{2,1,0:T(8,128)(2,1)} %get-tuple-element.17), channel_id=1, source_target_pairs={{0,28},{4,24},{8,20},{12,16},{16,12},{20,8},{24,4},{28,0},{1,29},{... | collective-permute-start | bytes 786440 | tf_op jit(solution)/shard_map/ppermute | solution.py:325
  31.8 7.7 %collective-permute-done.1.refs_1_.refs_3_ = bf16[8,64,256]{2,1,0:T(8,128)(2,1)S(1)} collective-permute-done((bf16[8,64,256]{2,1,0:T(8,128)(2,1)S(1)}, bf16[8,64,256]{2,1,0:T(8,128)(2,1)S(1)}, u32[]{:S(2)}, u32[]{:S(2)}) %collective-permute-start.1) | collective-permute-done | bytes 262176 | tf_op jit(solution)/shard_map/ppermute | solution.py:325
  39.5 0.0 collective-permute-start.6
  39.5 0.0 copy-done.1
  39.5 0.1 copy.6.offdiag_ref
  39.6 0.0 copy-done
  39.6 0.2 energy_column.1.refs_8_
  39.8 0.0 collective-permute-done.2.refs_2_.refs_4_
  39.8 0.0 collective-permute-done.3.refs_3_.refs_5_
  39.9 0.0 collective-permute-done.4.refs_4_.refs_6_
  39.9 6.2 %collective-permute-done.5.refs_5_.refs_7_ = bf16[8,64,256]{2,1,0:T(8,128)(2,1)S(1)} collective-permute-done((bf16[8,64,256]{2,1,0:T(8,128)(2,1)}, bf16[8,64,256]{2,1,0:T(8,128)(2,1)S(1)}, u32[]{:S(2)}, u32[]{:S(2)}) %collective-permute-start.5) | collective-permute-done | bytes 262176 | tf_op jit(solution)/shard_map/ppermute | solution.py:325
  46.1 4.7 %collective-permute-done.6.refs_6_.refs_8_ = bf16[8,64,256]{2,1,0:T(8,128)(2,1)S(1)} collective-permute-done((bf16[8,64,256]{2,1,0:T(8,128)(2,1)S(1)}, bf16[8,64,256]{2,1,0:T(8,128)(2,1)S(1)}, u32[]{:S(2)}, u32[]{:S(2)}) %collective-permute-start.6) | collective-permute-done | bytes 262176 | tf_op jit(solution)/shard_map/ppermute | solution.py:325
  50.7 1.4 %gram_partial.1 = f32[64,128]{1,0:T(8,128)S(1)} custom-call(bf16[8,64,256]{2,1,0:T(8,128)(2,1)S(1)} %collective-permute-done.refs_0_.refs_2_, bf16[8,64,256]{2,1,0:T(8,128)(2,1)S(1)} %collective-permute-done.1.refs_1_.refs_3_, bf16[8,64,256]{2,1,0:T(8,128)(2,1)S(1)} %collective-permute-done.2.refs_2_.refs_4_, ...), custom_call_target="tpu_custom_call" | custom-call | flops 134217728 | bytes 2097152 | tf_op jit(solution)/shard_map/gram_partial/pallas_call | solution.py:161
  52.2 0.1 collective-permute-start.7
  52.3 1.6 %collective-permute-start.8 = (f32[64,128]{1,0:T(8,128)S(1)}, f32[64,128]{1,0:T(8,128)S(1)}, u32[]{:S(2)}, u32[]{:S(2)}) collective-permute-start(f32[64,128]{1,0:T(8,128)S(1)} %gram_partial.1), channel_id=1, source_target_pairs={{0,2},{1,3},{2,0},{3,1},{4,6},{5,7},{6,4},{7,5},{8,10},{9,11},{10,... | collective-permute-start | bytes 98312 | tf_op jit(solution)/shard_map/ppermute | solution.py:262
  53.8 0.3 collective-permute-start.9
  54.1 0.0 collective-permute-done.7
  54.1 2.1 %collective-permute-done.8 = f32[64,128]{1,0:T(8,128)S(1)} collective-permute-done((f32[64,128]{1,0:T(8,128)S(1)}, f32[64,128]{1,0:T(8,128)S(1)}, u32[]{:S(2)}, u32[]{:S(2)}) %collective-permute-start.8) | collective-permute-done | bytes 32800 | tf_op jit(solution)/shard_map/ppermute | solution.py:262
  56.2 0.9 %collective-permute-done.9 = f32[64,128]{1,0:T(8,128)S(1)} collective-permute-done((f32[64,128]{1,0:T(8,128)S(1)}, f32[64,128]{1,0:T(8,128)S(1)}, u32[]{:S(2)}, u32[]{:S(2)}) %collective-permute-start.9) | collective-permute-done | bytes 32800 | tf_op jit(solution)/shard_map/ppermute | solution.py:262
  57.2 0.6 collective-permute-start.10
  57.7 5.2 %collective-permute-start.11 = (f32[64,128]{1,0:T(8,128)S(1)}, f32[64,128]{1,0:T(8,128)S(1)}, u32[]{:S(2)}, u32[]{:S(2)}) collective-permute-start(f32[64,128]{1,0:T(8,128)S(1)} %add_add_fusion.1), channel_id=1, source_target_pairs={{0,8},{4,12},{8,0},{12,4},{16,24},{20,28},{24,16},{28,20},{1,9},{5... | collective-permute-start | bytes 98312 | tf_op jit(solution)/shard_map/ppermute | solution.py:262
  62.9 0.7 collective-permute-start.12
  63.6 0.0 collective-permute-done.10
  63.6 1.2 %collective-permute-done.11 = f32[64,128]{1,0:T(8,128)S(1)} collective-permute-done((f32[64,128]{1,0:T(8,128)S(1)}, f32[64,128]{1,0:T(8,128)S(1)}, u32[]{:S(2)}, u32[]{:S(2)}) %collective-permute-start.11) | collective-permute-done | bytes 32800 | tf_op jit(solution)/shard_map/ppermute | solution.py:262
  64.8 2.9 %collective-permute-done.12 = f32[64,128]{1,0:T(8,128)S(1)} collective-permute-done((f32[64,128]{1,0:T(8,128)S(1)}, f32[64,128]{1,0:T(8,128)S(1)}, u32[]{:S(2)}, u32[]{:S(2)}) %collective-permute-start.12) | collective-permute-done | bytes 32800 | tf_op jit(solution)/shard_map/ppermute | solution.py:262
  67.8 2.2 %collective-permute-start.13 = (f32[64,128]{1,0:T(8,128)S(1)}, f32[64,128]{1,0:T(8,128)S(1)}, u32[]{:S(2)}, u32[]{:S(2)}) collective-permute-start(f32[64,128]{1,0:T(8,128)S(1)} %add_add_fusion.refs_0_), channel_id=1, source_target_pairs={{0,16},{4,20},{8,24},{12,28},{16,0},{20,4},{24,8},{28,12},{1,17},{... | collective-permute-start | bytes 98312 | tf_op jit(solution)/shard_map/ppermute | solution.py:262
  70.0 2.7 %collective-permute-done.13.refs_1_ = f32[64,128]{1,0:T(8,128)S(1)} collective-permute-done((f32[64,128]{1,0:T(8,128)S(1)}, f32[64,128]{1,0:T(8,128)S(1)}, u32[]{:S(2)}, u32[]{:S(2)}) %collective-permute-start.13) | collective-permute-done | bytes 32800 | tf_op jit(solution)/shard_map/ppermute | solution.py:262
  72.6 3.3 %solve_and_project.1 = (f32[1,8]{1,0:T(1,128)}, f32[2,32,256]{2,1,0:T(8,128)}) custom-call(f32[64,128]{1,0:T(8,128)S(1)} %add_add_fusion.refs_0_, f32[64,128]{1,0:T(8,128)S(1)} %collective-permute-done.13.refs_1_, bf16[8,64,256]{2,1,0:T(8,128)(2,1)S(1)} %collective-permute-done.refs_0_.refs_2_, ...), custom_call_target="tpu_custom_call" | custom-call | tf_op jit(solution)/shard_map/solve_and_project/pallas_call | solution.py:306
  (2 shorter events, 0.0 us)
Async XLA Ops:
  0.6 38.9 %copy-start.1 = (f32[8]{0:T(128)S(1)}, f32[8]{0:T(128)}, u32[]{:S(2)}) copy-start(f32[8]{0:T(128)} %param.7) | copy-start | bytes 100
  0.6 39.0 %copy-start = (s32[8,256]{1,0:T(8,128)S(1)}, s32[8,256]{1,0:T(8,128)}, u32[]{:S(2)}) copy-start(s32[8,256]{1,0:T(8,128)} %spins_ref.1) | copy-start | bytes 24580
  4.3 22.6 %collective-permute-start = (bf16[8,64,256]{2,1,0:T(8,128)(2,1)S(1)}, bf16[8,64,256]{2,1,0:T(8,128)(2,1)S(1)}, u32[]{:S(2)}, u32[]{:S(2)}) collective-permute-start(bf16[8,64,256]{2,1,0:T(8,128)(2,1)S(1)} %get-tuple-element.12), channel_id=1, source_target_pairs={{0,16},{4,20},{8,24},{12,28},{16,0},{20,4},{24,8},{28,12},{1,17},{... | collective-permute-start | bytes 786440 | tf_op jit(solution)/shard_map/ppermute | solution.py:325
  8.4 31.1 %collective-permute-start.1 = (bf16[8,64,256]{2,1,0:T(8,128)(2,1)S(1)}, bf16[8,64,256]{2,1,0:T(8,128)(2,1)S(1)}, u32[]{:S(2)}, u32[]{:S(2)}) collective-permute-start(bf16[8,64,256]{2,1,0:T(8,128)(2,1)S(1)} %get-tuple-element.13), channel_id=1, source_target_pairs={{0,20},{4,16},{8,28},{12,24},{16,4},{20,0},{24,12},{28,8},{1,21},{... | collective-permute-start | bytes 786440 | tf_op jit(solution)/shard_map/ppermute | solution.py:325
  9.7 30.1 %collective-permute-start.2 = (bf16[8,64,256]{2,1,0:T(8,128)(2,1)S(1)}, bf16[8,64,256]{2,1,0:T(8,128)(2,1)S(1)}, u32[]{:S(2)}, u32[]{:S(2)}) collective-permute-start(bf16[8,64,256]{2,1,0:T(8,128)(2,1)S(1)} %get-tuple-element.14), channel_id=1, source_target_pairs={{0,12},{4,8},{8,4},{12,0},{16,28},{20,24},{24,20},{28,16},{1,13},{... | collective-permute-start | bytes 786440 | tf_op jit(solution)/shard_map/ppermute | solution.py:325
  11.2 28.6 %collective-permute-start.3 = (bf16[8,64,256]{2,1,0:T(8,128)(2,1)S(1)}, bf16[8,64,256]{2,1,0:T(8,128)(2,1)S(1)}, u32[]{:S(2)}, u32[]{:S(2)}) collective-permute-start(bf16[8,64,256]{2,1,0:T(8,128)(2,1)S(1)} %get-tuple-element.15), channel_id=1, source_target_pairs={{0,24},{4,28},{8,16},{12,20},{16,8},{20,12},{24,0},{28,4},{1,25},{... | collective-permute-start | bytes 786440 | tf_op jit(solution)/shard_map/ppermute | solution.py:325
  13.7 26.2 %collective-permute-start.4 = (bf16[8,64,256]{2,1,0:T(8,128)(2,1)S(1)}, bf16[8,64,256]{2,1,0:T(8,128)(2,1)S(1)}, u32[]{:S(2)}, u32[]{:S(2)}) collective-permute-start(bf16[8,64,256]{2,1,0:T(8,128)(2,1)S(1)} %get-tuple-element.16), channel_id=1, source_target_pairs={{0,8},{4,12},{8,0},{12,4},{16,24},{20,28},{24,16},{28,20},{1,9},{5... | collective-permute-start | bytes 786440 | tf_op jit(solution)/shard_map/ppermute | solution.py:325
  26.9 19.2 %collective-permute-start.5 = (bf16[8,64,256]{2,1,0:T(8,128)(2,1)}, bf16[8,64,256]{2,1,0:T(8,128)(2,1)S(1)}, u32[]{:S(2)}, u32[]{:S(2)}) collective-permute-start(bf16[8,64,256]{2,1,0:T(8,128)(2,1)} %get-tuple-element.17), channel_id=1, source_target_pairs={{0,28},{4,24},{8,20},{12,16},{16,12},{20,8},{24,4},{28,0},{1,29},{... | collective-permute-start | bytes 786440 | tf_op jit(solution)/shard_map/ppermute | solution.py:325
  39.5 11.2 %collective-permute-start.6 = (bf16[8,64,256]{2,1,0:T(8,128)(2,1)S(1)}, bf16[8,64,256]{2,1,0:T(8,128)(2,1)S(1)}, u32[]{:S(2)}, u32[]{:S(2)}) collective-permute-start(bf16[8,64,256]{2,1,0:T(8,128)(2,1)S(1)} %get-tuple-element.18), channel_id=1, source_target_pairs={{0,4},{4,0},{8,12},{12,8},{16,20},{20,16},{24,28},{28,24},{1,5},{5... | collective-permute-start | bytes 786440 | tf_op jit(solution)/shard_map/ppermute | solution.py:325
  52.2 1.9 %collective-permute-start.7 = (f32[64,128]{1,0:T(8,128)S(1)}, f32[64,128]{1,0:T(8,128)S(1)}, u32[]{:S(2)}, u32[]{:S(2)}) collective-permute-start(f32[64,128]{1,0:T(8,128)S(1)} %gram_partial.1), channel_id=1, source_target_pairs={{0,1},{1,0},{2,3},{3,2},{4,5},{5,4},{6,7},{7,6},{8,9},{9,8},{10,11... | collective-permute-start | bytes 98312 | tf_op jit(solution)/shard_map/ppermute | solution.py:262
  52.3 4.0 %collective-permute-start.8 = (f32[64,128]{1,0:T(8,128)S(1)}, f32[64,128]{1,0:T(8,128)S(1)}, u32[]{:S(2)}, u32[]{:S(2)}) collective-permute-start(f32[64,128]{1,0:T(8,128)S(1)} %gram_partial.1), channel_id=1, source_target_pairs={{0,2},{1,3},{2,0},{3,1},{4,6},{5,7},{6,4},{7,5},{8,10},{9,11},{10,... | collective-permute-start | bytes 98312 | tf_op jit(solution)/shard_map/ppermute | solution.py:262
  53.8 3.3 %collective-permute-start.9 = (f32[64,128]{1,0:T(8,128)S(1)}, f32[64,128]{1,0:T(8,128)S(1)}, u32[]{:S(2)}, u32[]{:S(2)}) collective-permute-start(f32[64,128]{1,0:T(8,128)S(1)} %gram_partial.1), channel_id=1, source_target_pairs={{0,3},{1,2},{2,1},{3,0},{4,7},{5,6},{6,5},{7,4},{8,11},{9,10},{10,... | collective-permute-start | bytes 98312 | tf_op jit(solution)/shard_map/ppermute | solution.py:262
  57.2 6.5 %collective-permute-start.10 = (f32[64,128]{1,0:T(8,128)S(1)}, f32[64,128]{1,0:T(8,128)S(1)}, u32[]{:S(2)}, u32[]{:S(2)}) collective-permute-start(f32[64,128]{1,0:T(8,128)S(1)} %add_add_fusion.1), channel_id=1, source_target_pairs={{0,4},{4,0},{8,12},{12,8},{16,20},{20,16},{24,28},{28,24},{1,5},{5... | collective-permute-start | bytes 98312 | tf_op jit(solution)/shard_map/ppermute | solution.py:262
  57.7 7.1 %collective-permute-start.11 = (f32[64,128]{1,0:T(8,128)S(1)}, f32[64,128]{1,0:T(8,128)S(1)}, u32[]{:S(2)}, u32[]{:S(2)}) collective-permute-start(f32[64,128]{1,0:T(8,128)S(1)} %add_add_fusion.1), channel_id=1, source_target_pairs={{0,8},{4,12},{8,0},{12,4},{16,24},{20,28},{24,16},{28,20},{1,9},{5... | collective-permute-start | bytes 98312 | tf_op jit(solution)/shard_map/ppermute | solution.py:262
  62.9 4.8 %collective-permute-start.12 = (f32[64,128]{1,0:T(8,128)S(1)}, f32[64,128]{1,0:T(8,128)S(1)}, u32[]{:S(2)}, u32[]{:S(2)}) collective-permute-start(f32[64,128]{1,0:T(8,128)S(1)} %add_add_fusion.1), channel_id=1, source_target_pairs={{0,12},{4,8},{8,4},{12,0},{16,28},{20,24},{24,20},{28,16},{1,13},{... | collective-permute-start | bytes 98312 | tf_op jit(solution)/shard_map/ppermute | solution.py:262
  67.8 4.9 %collective-permute-start.13 = (f32[64,128]{1,0:T(8,128)S(1)}, f32[64,128]{1,0:T(8,128)S(1)}, u32[]{:S(2)}, u32[]{:S(2)}) collective-permute-start(f32[64,128]{1,0:T(8,128)S(1)} %add_add_fusion.refs_0_), channel_id=1, source_target_pairs={{0,16},{4,20},{8,24},{12,28},{16,0},{20,4},{24,8},{28,12},{1,17},{... | collective-permute-start | bytes 98312 | tf_op jit(solution)/shard_map/ppermute | solution.py:262

commit v15 on v14

--- a/solution.py
+++ b/solution.py
@@ -100,8 +100,13 @@
     )(activations, cotangents)
 
 
-def energy_kernel(spins_ref, offdiag_ref, out_ref):
-    total, width = out_ref.shape
+def packed_shape(total):
+    half = total // 2
+    return half, -(-(3 * half + 2) // LANES) * LANES
+
+
+def energy_kernel(total, spins_ref, offdiag_ref, out_ref):
+    shape = out_ref.shape
     local = spins_ref.shape[0]
     sites = SIDE * SIDE
     z = (2 * spins_ref[...] - 1).astype(F32)
@@ -111,25 +116,28 @@
     )
     below = pltpu.roll(z, sites - SIDE, 1)
     energy = offdiag_ref[...] + jnp.sum(z * (right + below), axis=1, keepdims=True)
+    half = total // 2
     first = lax.axis_index("samp") * local
-    mine = lax.axis_index("layer") == 0
-    spread = jnp.concatenate([energy] * (total // local), axis=0)
-    row = iota((total, width), 0)
-    here = (row >= first) & (row < first + local) & (iota((total, width), 1) == total) & mine
+    lower = first // half
+    first = first - lower * half
+    spread = jnp.concatenate([energy] * (half // local), axis=0)
+    row = iota(shape, 0)
+    here = (row >= first) & (row < first + local) & (iota(shape, 1) == 3 * half + lower)
+    here = here & (lax.axis_index("layer") == 0)
     out_ref[...] = jnp.where(here, spread, F32(0.0))
 
 
-def energy_column(spins, offdiag, total, width):
+def packed_energy(spins, offdiag, total):
     return pl.pallas_call(
-        energy_kernel,
-        out_shape=jax.ShapeDtypeStruct((total, width), F32),
+        functools.partial(energy_kernel, total),
+        out_shape=jax.ShapeDtypeStruct(packed_shape(total), F32),
         compiler_params=pltpu.CompilerParams(vmem_limit_bytes=VMEM_LIMIT),
-        name="energy_column",
+        name="packed_energy",
     )(spins, offdiag[:, None])
 
 
 def gram_kernel(*refs):
-    *block_refs, start_ref, out_ref, flat = refs
+    *block_refs, energy_ref, out_ref, flat = refs
     block_refs = in_place(block_refs)
     local, count, d = block_refs[0].shape
     total = local * len(block_refs)
@@ -151,16 +159,20 @@
                 flat[row + r, place] = turned[r * CHUNK : (r + 1) * CHUNK]
     lined = jnp.concatenate([flat[r] for r in range(count)], axis=1)
     gram = lax.dot_general(lined, lined, (((1,), (1,)), ((), ())), preferred_element_type=F32)
-    out_ref[...] = start_ref[...]
-    out_ref[:, :total] += gram
-
-
-def gram_partial(blocks, start):
+    half, width = out_ref.shape
+    gram = jnp.concatenate([gram, jnp.zeros((total, width - total), F32)], axis=1)
+    lane = iota((half, width), 1)
+    lower = pltpu.roll(gram[half:], half, 1)
+    packed = jnp.where(lane < 3 * half, lower, energy_ref[...])
+    out_ref[...] = jnp.where(lane < half, gram[:half], packed)
+
+
+def gram_partial(blocks, energies):
     local, count, d = blocks[0].shape
-    total, width = start.shape
+    total = local * len(blocks)
     return pl.pallas_call(
         gram_kernel,
-        out_shape=jax.ShapeDtypeStruct((total, width), F32),
+        out_shape=jax.ShapeDtypeStruct(packed_shape(total), F32),
         scratch_shapes=[pltpu.VMEM((count, total, d), BF16)],
         compiler_params=pltpu.CompilerParams(vmem_limit_bytes=VMEM_LIMIT),
         cost_estimate=pl.CostEstimate(
@@ -169,7 +181,7 @@
             transcendentals=0,
         ),
         name="gram_partial",
-    )(*in_turn(blocks), start)
+    )(*in_turn(blocks), energies)
 
 
 def tree_sum(parts):
@@ -268,8 +280,16 @@
     block_refs = in_place(block_refs)
     mats, share, d = update_ref.shape
     local = weights_ref.shape[1]
-    total, width = gram_refs[0].shape
-    raw = tree_sum([ref[...] for ref in gram_refs])
+    packed = tree_sum([ref[...] for ref in gram_refs])
+    half, packed_width = packed.shape
+    total = 2 * half
+    width = (total // LANES + 1) * LANES
+    turned = jnp.swapaxes(packed[:, half:total], 0, 1)
+    energy = [packed[:, 3 * half + i : 3 * half + i + 1] for i in range(2)]
+    energy = [jnp.broadcast_to(e, (half, width - total)) for e in energy]
+    upper = jnp.concatenate([packed[:, :half], turned, energy[0]], axis=1)
+    lower = jnp.concatenate([packed[:, half : 3 * half], energy[1]], axis=1)
+    raw = jnp.concatenate([upper, lower], axis=0)
     row = iota((total, width), 0)
     lane = iota((total, width), 1)
     inside = lane < total
@@ -301,8 +321,8 @@
 
 
 def solve_and_project(grams, blocks, mats):
-    total, width = grams[0].shape
     local, count, d = blocks[0].shape
+    total = local * len(blocks)
     return pl.pallas_call(
         functools.partial(solve_kernel, len(grams)),
         out_shape=(
@@ -319,11 +339,10 @@
     local, mats = activations.shape[:2]
     owners = lax.axis_size("samp")
     total = local * owners
-    width = (total // LANES + 1) * LANES
     blocks = list(jac_rows(activations, cotangents, owners))
     for k in turns(owners)[:-1]:
         blocks[k] = lax.ppermute(blocks[k], "samp", [(i, i ^ k) for i in range(owners)])
-    partial = gram_partial(blocks, energy_column(spins, offdiag, total, width))
+    partial = gram_partial(blocks, packed_energy(spins, offdiag, total))
     grams = partners(partial, "layer", 1, lax.axis_size("layer"))
     first = 1
     while first < owners:

time: 76.1 us -> 76.8 us (level)
  Pallas kernels: 8.61 us -> 9.87 us
    pallas_call x2, Pallas kernels: 1.66 us -> 2.71 us  [the longest x1 2.49 us: gram_partial(): pl.pallas_call(gram_kernel, out_shape=jax.ShapeDtypeStruct(packed_shape(t...]
where the time goes in v15:
time: 76.8 us; the launch traced here: 76.6 us
  waiting for transfers between devices  40.6 us (53%)
  starting transfers between devices  25.4 us (33%)
  Pallas kernels  9.87 us (13%)
    ppermute x7, waiting for transfers between devices, body(): lax.ppermute(blocks[k], 'samp', [(i, i ^ k) for i in range(owners)])  31.1 us
    ppermute x7, starting transfers between devices, body(): lax.ppermute(blocks[k], 'samp', [(i, i ^ k) for i in range(owners)])  15 us
    ppermute x7, starting transfers between devices, partners(): parts.append(lax.ppermute(value, axis, perm))  10.4 us
    ppermute x7, waiting for transfers between devices, partners(): parts.append(lax.ppermute(value, axis, perm))  9.45 us
    pallas_call x1, Pallas kernels, jac_rows(): pl.pallas_call(jac_kernel, in_specs=[hbm, hbm], out_shape=[jax.ShapeDtype...  3.64 us
    pallas_call x1, Pallas kernels, solve_and_project(): pl.pallas_call(functools.partial(solve_kernel, len(grams)), out_shape=(ja...  3.52 us
    pallas_call x1, Pallas kernels, gram_partial(): pl.pallas_call(gram_kernel, out_shape=jax.ShapeDtypeStruct(packed_shape(t...  2.49 us
  transfers between devices with their start and end apart: 14, of which 9 were waited for; matrix products, arithmetic and copies ran while one was open for 0% of the time, Pallas kernels for 0%

profile of v15, /device:TPU:0, one launch (start us, length us, event | category | flops | bytes accessed | tf_op | source)
XLA Modules:
  0.0 76.6 jit_solution(4279032951101829758)
XLA Ops:
  0.6 0.0 copy-start.1
  0.6 0.0 copy-start
  0.7 3.6 %jac_rows.1 = (bf16[8,64,256]{2,1,0:T(8,128)(2,1)S(1)}, bf16[8,64,256]{2,1,0:T(8,128)(2,1)S(1)}, bf16[8,64,256]{2,1,0:T(8,128)(2,1)S(1)}, bf16[8,64,256]{2,1,0:T...) custom-call(bf16[8,2,256,256]{3,2,1,0:T(8,128)(2,1)} %act_hbm.1, ...), custom_call_target="tpu_custom_call" | custom-call | flops 536870912 | bytes 6291456 | tf_op jit(solution)/shard_map/jac_rows/pallas_call | solution.py:83
  4.3 4.1 %collective-permute-start = (bf16[8,64,256]{2,1,0:T(8,128)(2,1)S(1)}, bf16[8,64,256]{2,1,0:T(8,128)(2,1)S(1)}, u32[]{:S(2)}, u32[]{:S(2)}) collective-permute-start(bf16[8,64,256]{2,1,0:T(8,128)(2,1)S(1)} %get-tuple-element.12), channel_id=1, source_target_pairs={{0,16},{4,20},{8,24},{12,28},{16,0},{20,4},{24,8},{28,12},{1,17},{... | collective-permute-start | bytes 786440 | tf_op jit(solution)/shard_map/ppermute | solution.py:344
  8.4 1.3 %collective-permute-start.1 = (bf16[8,64,256]{2,1,0:T(8,128)(2,1)S(1)}, bf16[8,64,256]{2,1,0:T(8,128)(2,1)S(1)}, u32[]{:S(2)}, u32[]{:S(2)}) collective-permute-start(bf16[8,64,256]{2,1,0:T(8,128)(2,1)S(1)} %get-tuple-element.13), channel_id=1, source_target_pairs={{0,20},{4,16},{8,28},{12,24},{16,4},{20,0},{24,12},{28,8},{1,21},{... | collective-permute-start | bytes 786440 | tf_op jit(solution)/shard_map/ppermute | solution.py:344
  9.7 1.5 %collective-permute-start.2 = (bf16[8,64,256]{2,1,0:T(8,128)(2,1)S(1)}, bf16[8,64,256]{2,1,0:T(8,128)(2,1)S(1)}, u32[]{:S(2)}, u32[]{:S(2)}) collective-permute-start(bf16[8,64,256]{2,1,0:T(8,128)(2,1)S(1)} %get-tuple-element.14), channel_id=1, source_target_pairs={{0,12},{4,8},{8,4},{12,0},{16,28},{20,24},{24,20},{28,16},{1,13},{... | collective-permute-start | bytes 786440 | tf_op jit(solution)/shard_map/ppermute | solution.py:344
  11.2 2.5 %collective-permute-start.3 = (bf16[8,64,256]{2,1,0:T(8,128)(2,1)S(1)}, bf16[8,64,256]{2,1,0:T(8,128)(2,1)S(1)}, u32[]{:S(2)}, u32[]{:S(2)}) collective-permute-start(bf16[8,64,256]{2,1,0:T(8,128)(2,1)S(1)} %get-tuple-element.15), channel_id=1, source_target_pairs={{0,24},{4,28},{8,16},{12,20},{16,8},{20,12},{24,0},{28,4},{1,25},{... | collective-permute-start | bytes 786440 | tf_op jit(solution)/shard_map/ppermute | solution.py:344
  13.7 0.7 collective-permute-start.4
  14.4 12.5 %collective-permute-done.refs_0_.refs_2_ = bf16[8,64,256]{2,1,0:T(8,128)(2,1)S(1)} collective-permute-done((bf16[8,64,256]{2,1,0:T(8,128)(2,1)S(1)}, bf16[8,64,256]{2,1,0:T(8,128)(2,1)S(1)}, u32[]{:S(2)}, u32[]{:S(2)}) %collective-permute-start) | collective-permute-done | bytes 262176 | tf_op jit(solution)/shard_map/ppermute | solution.py:344
  26.9 4.9 %collective-permute-start.5 = (bf16[8,64,256]{2,1,0:T(8,128)(2,1)}, bf16[8,64,256]{2,1,0:T(8,128)(2,1)S(1)}, u32[]{:S(2)}, u32[]{:S(2)}) collective-permute-start(bf16[8,64,256]{2,1,0:T(8,128)(2,1)} %get-tuple-element.17), channel_id=1, source_target_pairs={{0,28},{4,24},{8,20},{12,16},{16,12},{20,8},{24,4},{28,0},{1,29},{... | collective-permute-start | bytes 786440 | tf_op jit(solution)/shard_map/ppermute | solution.py:344
  31.8 7.7 %collective-permute-done.1.refs_1_.refs_3_ = bf16[8,64,256]{2,1,0:T(8,128)(2,1)S(1)} collective-permute-done((bf16[8,64,256]{2,1,0:T(8,128)(2,1)S(1)}, bf16[8,64,256]{2,1,0:T(8,128)(2,1)S(1)}, u32[]{:S(2)}, u32[]{:S(2)}) %collective-permute-start.1) | collective-permute-done | bytes 262176 | tf_op jit(solution)/shard_map/ppermute | solution.py:344
  39.5 0.0 collective-permute-start.6
  39.5 0.0 copy-done.1
  39.5 0.1 copy.6.offdiag_ref
  39.6 0.0 copy-done
  39.6 0.2 packed_energy.1.refs_8_
  39.8 0.0 collective-permute-done.2.refs_2_.refs_4_
  39.8 0.0 collective-permute-done.3.refs_3_.refs_5_
  39.8 0.0 collective-permute-done.4.refs_4_.refs_6_
  39.9 6.2 %collective-permute-done.5.refs_5_.refs_7_ = bf16[8,64,256]{2,1,0:T(8,128)(2,1)S(1)} collective-permute-done((bf16[8,64,256]{2,1,0:T(8,128)(2,1)}, bf16[8,64,256]{2,1,0:T(8,128)(2,1)S(1)}, u32[]{:S(2)}, u32[]{:S(2)}) %collective-permute-start.5) | collective-permute-done | bytes 262176 | tf_op jit(solution)/shard_map/ppermute | solution.py:344
  46.1 4.7 %collective-permute-done.6.refs_6_.refs_8_ = bf16[8,64,256]{2,1,0:T(8,128)(2,1)S(1)} collective-permute-done((bf16[8,64,256]{2,1,0:T(8,128)(2,1)S(1)}, bf16[8,64,256]{2,1,0:T(8,128)(2,1)S(1)}, u32[]{:S(2)}, u32[]{:S(2)}) %collective-permute-start.6) | collective-permute-done | bytes 262176 | tf_op jit(solution)/shard_map/ppermute | solution.py:344
  50.7 2.5 %gram_partial.1 = f32[32,128]{1,0:T(8,128)S(1)} custom-call(bf16[8,64,256]{2,1,0:T(8,128)(2,1)S(1)} %collective-permute-done.refs_0_.refs_2_, bf16[8,64,256]{2,1,0:T(8,128)(2,1)S(1)} %collective-permute-done.1.refs_1_.refs_3_, bf16[8,64,256]{2,1,0:T(8,128)(2,1)S(1)} %collective-permute-done.2.refs_2_.refs_4_, ...), custom_call_target="tpu_custom_call" | custom-call | flops 134217728 | bytes 2097152 | tf_op jit(solution)/shard_map/gram_partial/pallas_call | solution.py:173
  53.2 0.1 collective-permute-start.7
  53.3 1.6 %collective-permute-start.8 = (f32[32,128]{1,0:T(8,128)S(1)}, f32[32,128]{1,0:T(8,128)S(1)}, u32[]{:S(2)}, u32[]{:S(2)}) collective-permute-start(f32[32,128]{1,0:T(8,128)S(1)} %gram_partial.1), channel_id=1, source_target_pairs={{0,2},{1,3},{2,0},{3,1},{4,6},{5,7},{6,4},{7,5},{8,10},{9,11},{10,... | collective-permute-start | bytes 49160 | tf_op jit(solution)/shard_map/ppermute | solution.py:274
  54.9 0.3 collective-permute-start.9
  55.2 0.0 collective-permute-done.7
  55.2 1.9 %collective-permute-done.8 = f32[32,128]{1,0:T(8,128)S(1)} collective-permute-done((f32[32,128]{1,0:T(8,128)S(1)}, f32[32,128]{1,0:T(8,128)S(1)}, u32[]{:S(2)}, u32[]{:S(2)}) %collective-permute-start.8) | collective-permute-done | bytes 16416 | tf_op jit(solution)/shard_map/ppermute | solution.py:274
  57.1 0.9 %collective-permute-done.9 = f32[32,128]{1,0:T(8,128)S(1)} collective-permute-done((f32[32,128]{1,0:T(8,128)S(1)}, f32[32,128]{1,0:T(8,128)S(1)}, u32[]{:S(2)}, u32[]{:S(2)}) %collective-permute-start.9) | collective-permute-done | bytes 16416 | tf_op jit(solution)/shard_map/ppermute | solution.py:274
  58.0 0.6 collective-permute-start.10
  58.6 5.2 %collective-permute-start.11 = (f32[32,128]{1,0:T(8,128)S(1)}, f32[32,128]{1,0:T(8,128)S(1)}, u32[]{:S(2)}, u32[]{:S(2)}) collective-permute-start(f32[32,128]{1,0:T(8,128)S(1)} %add_add_fusion.1), channel_id=1, source_target_pairs={{0,8},{4,12},{8,0},{12,4},{16,24},{20,28},{24,16},{28,20},{1,9},{5... | collective-permute-start | bytes 49160 | tf_op jit(solution)/shard_map/ppermute | solution.py:274
  63.8 0.7 collective-permute-start.12
  64.5 0.0 collective-permute-done.10
  64.5 1.0 %collective-permute-done.11 = f32[32,128]{1,0:T(8,128)S(1)} collective-permute-done((f32[32,128]{1,0:T(8,128)S(1)}, f32[32,128]{1,0:T(8,128)S(1)}, u32[]{:S(2)}, u32[]{:S(2)}) %collective-permute-start.11) | collective-permute-done | bytes 16416 | tf_op jit(solution)/shard_map/ppermute | solution.py:274
  65.5 2.9 %collective-permute-done.12 = f32[32,128]{1,0:T(8,128)S(1)} collective-permute-done((f32[32,128]{1,0:T(8,128)S(1)}, f32[32,128]{1,0:T(8,128)S(1)}, u32[]{:S(2)}, u32[]{:S(2)}) %collective-permute-start.12) | collective-permute-done | bytes 16416 | tf_op jit(solution)/shard_map/ppermute | solution.py:274
  68.4 2.0 %collective-permute-start.13 = (f32[32,128]{1,0:T(8,128)S(1)}, f32[32,128]{1,0:T(8,128)S(1)}, u32[]{:S(2)}, u32[]{:S(2)}) collective-permute-start(f32[32,128]{1,0:T(8,128)S(1)} %add_add_fusion.refs_0_), channel_id=1, source_target_pairs={{0,16},{4,20},{8,24},{12,28},{16,0},{20,4},{24,8},{28,12},{1,17},{... | collective-permute-start | bytes 49160 | tf_op jit(solution)/shard_map/ppermute | solution.py:274
  70.5 2.6 %collective-permute-done.13.refs_1_ = f32[32,128]{1,0:T(8,128)S(1)} collective-permute-done((f32[32,128]{1,0:T(8,128)S(1)}, f32[32,128]{1,0:T(8,128)S(1)}, u32[]{:S(2)}, u32[]{:S(2)}) %collective-permute-start.13) | collective-permute-done | bytes 16416 | tf_op jit(solution)/shard_map/ppermute | solution.py:274
  73.1 3.5 %solve_and_project.1 = (f32[1,8]{1,0:T(1,128)}, f32[2,32,256]{2,1,0:T(8,128)}) custom-call(f32[32,128]{1,0:T(8,128)S(1)} %add_add_fusion.refs_0_, f32[32,128]{1,0:T(8,128)S(1)} %collective-permute-done.13.refs_1_, bf16[8,64,256]{2,1,0:T(8,128)(2,1)S(1)} %collective-permute-done.refs_0_.refs_2_, ...), custom_call_target="tpu_custom_call" | custom-call | tf_op jit(solution)/shard_map/solve_and_project/pallas_call | solution.py:326
  (2 shorter events, 0.0 us)
Async XLA Ops:
  0.6 38.9 %copy-start.1 = (f32[8]{0:T(128)S(1)}, f32[8]{0:T(128)}, u32[]{:S(2)}) copy-start(f32[8]{0:T(128)} %param.7) | copy-start | bytes 100
  0.6 39.0 %copy-start = (s32[8,256]{1,0:T(8,128)S(1)}, s32[8,256]{1,0:T(8,128)}, u32[]{:S(2)}) copy-start(s32[8,256]{1,0:T(8,128)} %spins_ref.1) | copy-start | bytes 24580
  4.3 22.6 %collective-permute-start = (bf16[8,64,256]{2,1,0:T(8,128)(2,1)S(1)}, bf16[8,64,256]{2,1,0:T(8,128)(2,1)S(1)}, u32[]{:S(2)}, u32[]{:S(2)}) collective-permute-start(bf16[8,64,256]{2,1,0:T(8,128)(2,1)S(1)} %get-tuple-element.12), channel_id=1, source_target_pairs={{0,16},{4,20},{8,24},{12,28},{16,0},{20,4},{24,8},{28,12},{1,17},{... | collective-permute-start | bytes 786440 | tf_op jit(solution)/shard_map/ppermute | solution.py:344
  8.4 31.1 %collective-permute-start.1 = (bf16[8,64,256]{2,1,0:T(8,128)(2,1)S(1)}, bf16[8,64,256]{2,1,0:T(8,128)(2,1)S(1)}, u32[]{:S(2)}, u32[]{:S(2)}) collective-permute-start(bf16[8,64,256]{2,1,0:T(8,128)(2,1)S(1)} %get-tuple-element.13), channel_id=1, source_target_pairs={{0,20},{4,16},{8,28},{12,24},{16,4},{20,0},{24,12},{28,8},{1,21},{... | collective-permute-start | bytes 786440 | tf_op jit(solution)/shard_map/ppermute | solution.py:344
  9.7 30.1 %collective-permute-start.2 = (bf16[8,64,256]{2,1,0:T(8,128)(2,1)S(1)}, bf16[8,64,256]{2,1,0:T(8,128)(2,1)S(1)}, u32[]{:S(2)}, u32[]{:S(2)}) collective-permute-start(bf16[8,64,256]{2,1,0:T(8,128)(2,1)S(1)} %get-tuple-element.14), channel_id=1, source_target_pairs={{0,12},{4,8},{8,4},{12,0},{16,28},{20,24},{24,20},{28,16},{1,13},{... | collective-permute-start | bytes 786440 | tf_op jit(solution)/shard_map/ppermute | solution.py:344
  11.2 28.6 %collective-permute-start.3 = (bf16[8,64,256]{2,1,0:T(8,128)(2,1)S(1)}, bf16[8,64,256]{2,1,0:T(8,128)(2,1)S(1)}, u32[]{:S(2)}, u32[]{:S(2)}) collective-permute-start(bf16[8,64,256]{2,1,0:T(8,128)(2,1)S(1)} %get-tuple-element.15), channel_id=1, source_target_pairs={{0,24},{4,28},{8,16},{12,20},{16,8},{20,12},{24,0},{28,4},{1,25},{... | collective-permute-start | bytes 786440 | tf_op jit(solution)/shard_map/ppermute | solution.py:344
  13.7 26.2 %collective-permute-start.4 = (bf16[8,64,256]{2,1,0:T(8,128)(2,1)S(1)}, bf16[8,64,256]{2,1,0:T(8,128)(2,1)S(1)}, u32[]{:S(2)}, u32[]{:S(2)}) collective-permute-start(bf16[8,64,256]{2,1,0:T(8,128)(2,1)S(1)} %get-tuple-element.16), channel_id=1, source_target_pairs={{0,8},{4,12},{8,0},{12,4},{16,24},{20,28},{24,16},{28,20},{1,9},{5... | collective-permute-start | bytes 786440 | tf_op jit(solution)/shard_map/ppermute | solution.py:344
  26.9 19.2 %collective-permute-start.5 = (bf16[8,64,256]{2,1,0:T(8,128)(2,1)}, bf16[8,64,256]{2,1,0:T(8,128)(2,1)S(1)}, u32[]{:S(2)}, u32[]{:S(2)}) collective-permute-start(bf16[8,64,256]{2,1,0:T(8,128)(2,1)} %get-tuple-element.17), channel_id=1, source_target_pairs={{0,28},{4,24},{8,20},{12,16},{16,12},{20,8},{24,4},{28,0},{1,29},{... | collective-permute-start | bytes 786440 | tf_op jit(solution)/shard_map/ppermute | solution.py:344
  39.5 11.2 %collective-permute-start.6 = (bf16[8,64,256]{2,1,0:T(8,128)(2,1)S(1)}, bf16[8,64,256]{2,1,0:T(8,128)(2,1)S(1)}, u32[]{:S(2)}, u32[]{:S(2)}) collective-permute-start(bf16[8,64,256]{2,1,0:T(8,128)(2,1)S(1)} %get-tuple-element.18), channel_id=1, source_target_pairs={{0,4},{4,0},{8,12},{12,8},{16,20},{20,16},{24,28},{28,24},{1,5},{5... | collective-permute-start | bytes 786440 | tf_op jit(solution)/shard_map/ppermute | solution.py:344
  53.2 1.9 %collective-permute-start.7 = (f32[32,128]{1,0:T(8,128)S(1)}, f32[32,128]{1,0:T(8,128)S(1)}, u32[]{:S(2)}, u32[]{:S(2)}) collective-permute-start(f32[32,128]{1,0:T(8,128)S(1)} %gram_partial.1), channel_id=1, source_target_pairs={{0,1},{1,0},{2,3},{3,2},{4,5},{5,4},{6,7},{7,6},{8,9},{9,8},{10,11... | collective-permute-start | bytes 49160 | tf_op jit(solution)/shard_map/ppermute | solution.py:274
  53.3 3.8 %collective-permute-start.8 = (f32[32,128]{1,0:T(8,128)S(1)}, f32[32,128]{1,0:T(8,128)S(1)}, u32[]{:S(2)}, u32[]{:S(2)}) collective-permute-start(f32[32,128]{1,0:T(8,128)S(1)} %gram_partial.1), channel_id=1, source_target_pairs={{0,2},{1,3},{2,0},{3,1},{4,6},{5,7},{6,4},{7,5},{8,10},{9,11},{10,... | collective-permute-start | bytes 49160 | tf_op jit(solution)/shard_map/ppermute | solution.py:274
  54.9 3.2 %collective-permute-start.9 = (f32[32,128]{1,0:T(8,128)S(1)}, f32[32,128]{1,0:T(8,128)S(1)}, u32[]{:S(2)}, u32[]{:S(2)}) collective-permute-start(f32[32,128]{1,0:T(8,128)S(1)} %gram_partial.1), channel_id=1, source_target_pairs={{0,3},{1,2},{2,1},{3,0},{4,7},{5,6},{6,5},{7,4},{8,11},{9,10},{10,... | collective-permute-start | bytes 49160 | tf_op jit(solution)/shard_map/ppermute | solution.py:274
  58.0 6.4 %collective-permute-start.10 = (f32[32,128]{1,0:T(8,128)S(1)}, f32[32,128]{1,0:T(8,128)S(1)}, u32[]{:S(2)}, u32[]{:S(2)}) collective-permute-start(f32[32,128]{1,0:T(8,128)S(1)} %add_add_fusion.1), channel_id=1, source_target_pairs={{0,4},{4,0},{8,12},{12,8},{16,20},{20,16},{24,28},{28,24},{1,5},{5... | collective-permute-start | bytes 49160 | tf_op jit(solution)/shard_map/ppermute | solution.py:274
  58.6 6.9 %collective-permute-start.11 = (f32[32,128]{1,0:T(8,128)S(1)}, f32[32,128]{1,0:T(8,128)S(1)}, u32[]{:S(2)}, u32[]{:S(2)}) collective-permute-start(f32[32,128]{1,0:T(8,128)S(1)} %add_add_fusion.1), channel_id=1, source_target_pairs={{0,8},{4,12},{8,0},{12,4},{16,24},{20,28},{24,16},{28,20},{1,9},{5... | collective-permute-start | bytes 49160 | tf_op jit(solution)/shard_map/ppermute | solution.py:274
  63.8 4.6 %collective-permute-start.12 = (f32[32,128]{1,0:T(8,128)S(1)}, f32[32,128]{1,0:T(8,128)S(1)}, u32[]{:S(2)}, u32[]{:S(2)}) collective-permute-start(f32[32,128]{1,0:T(8,128)S(1)} %add_add_fusion.1), channel_id=1, source_target_pairs={{0,12},{4,8},{8,4},{12,0},{16,28},{20,24},{24,20},{28,16},{1,13},{... | collective-permute-start | bytes 49160 | tf_op jit(solution)/shard_map/ppermute | solution.py:274
  68.4 4.7 %collective-permute-start.13 = (f32[32,128]{1,0:T(8,128)S(1)}, f32[32,128]{1,0:T(8,128)S(1)}, u32[]{:S(2)}, u32[]{:S(2)}) collective-permute-start(f32[32,128]{1,0:T(8,128)S(1)} %add_add_fusion.refs_0_), channel_id=1, source_target_pairs={{0,16},{4,20},{8,24},{12,28},{16,0},{20,4},{24,8},{28,12},{1,17},{... | collective-permute-start | bytes 49160 | tf_op jit(solution)/shard_map/ppermute | solution.py:274

commit v16 on v15

--- a/solution.py
+++ b/solution.py
@@ -137,7 +137,7 @@
 
 
 def gram_kernel(*refs):
-    *block_refs, energy_ref, out_ref, flat = refs
+    *block_refs, energy_ref, out_ref, flat, whole = refs
     block_refs = in_place(block_refs)
     local, count, d = block_refs[0].shape
     total = local * len(block_refs)
@@ -158,13 +158,14 @@
             for r in range(CHUNK):
                 flat[row + r, place] = turned[r * CHUNK : (r + 1) * CHUNK]
     lined = jnp.concatenate([flat[r] for r in range(count)], axis=1)
-    gram = lax.dot_general(lined, lined, (((1,), (1,)), ((), ())), preferred_element_type=F32)
+    whole[:, :total] = lax.dot_general(
+        lined, lined, (((1,), (1,)), ((), ())), preferred_element_type=F32
+    )
     half, width = out_ref.shape
-    gram = jnp.concatenate([gram, jnp.zeros((total, width - total), F32)], axis=1)
     lane = iota((half, width), 1)
-    lower = pltpu.roll(gram[half:], half, 1)
+    lower = pltpu.roll(whole[half:], half, 1)
     packed = jnp.where(lane < 3 * half, lower, energy_ref[...])
-    out_ref[...] = jnp.where(lane < half, gram[:half], packed)
+    out_ref[...] = jnp.where(lane < half, whole[:half], packed)
 
 
 def gram_partial(blocks, energies):
@@ -173,7 +174,10 @@
     return pl.pallas_call(
         gram_kernel,
         out_shape=jax.ShapeDtypeStruct(packed_shape(total), F32),
-        scratch_shapes=[pltpu.VMEM((count, total, d), BF16)],
+        scratch_shapes=[
+            pltpu.VMEM((count, total, d), BF16),
+            pltpu.VMEM((total, packed_shape(total)[1]), F32),
+        ],
         compiler_params=pltpu.CompilerParams(vmem_limit_bytes=VMEM_LIMIT),
         cost_estimate=pl.CostEstimate(
             flops=2 * total * total * count * d,
@@ -266,13 +270,27 @@
     return matrix[:, total : total + 1] / diag
 
 
+def sum_kernel(*refs):
+    *part_refs, out_ref = refs
+    out_ref[...] = tree_sum([ref[...] for ref in part_refs[::-1]])
+
+
 def partners(value, axis, first, count):
     size = lax.axis_size(axis)
-    parts = [value]
-    for k in range(1, count):
+    parts = []
+    for k in range(count - 1, 0, -1):
         perm = [(i, i ^ (k * first)) for i in range(size)]
         parts.append(lax.ppermute(value, axis, perm))
-    return parts
+    return parts + [value]
+
+
+def sum_over(value, axis, first, count):
+    return pl.pallas_call(
+        sum_kernel,
+        out_shape=jax.ShapeDtypeStruct(value.shape, F32),
+        compiler_params=pltpu.CompilerParams(vmem_limit_bytes=VMEM_LIMIT),
+        name="sum_over",
+    )(*partners(value, axis, first, count))
 
 
 def solve_kernel(grams, *refs):
@@ -280,7 +298,7 @@
     block_refs = in_place(block_refs)
     mats, share, d = update_ref.shape
     local = weights_ref.shape[1]
-    packed = tree_sum([ref[...] for ref in gram_refs])
+    packed = tree_sum([ref[...] for ref in gram_refs[::-1]])
     half, packed_width = packed.shape
     total = 2 * half
     width = (total // LANES + 1) * LANES
@@ -343,12 +361,12 @@
     for k in turns(owners)[:-1]:
         blocks[k] = lax.ppermute(blocks[k], "samp", [(i, i ^ k) for i in range(owners)])
     partial = gram_partial(blocks, packed_energy(spins, offdiag, total))
-    grams = partners(partial, "layer", 1, lax.axis_size("layer"))
+    gram = sum_over(partial, "layer", 1, lax.axis_size("layer"))
     first = 1
-    while first < owners:
-        count = min(4, owners // first)
-        grams = partners(tree_sum(grams), "samp", first, count)
-        first *= count
+    while 4 * first < owners:
+        gram = sum_over(gram, "samp", first, 4)
+        first *= 4
+    grams = partners(gram, "samp", first, owners // first)
     weights, update = solve_and_project(grams, blocks, mats)
     return weights.reshape(local), update
 

time: 76.8 us -> 76.3 us (level)
  waiting for transfers between devices: 40.6 us -> 38 us
  starting transfers between devices: 25.4 us -> 27.5 us
    ppermute x7, waiting for transfers between devices: 9.45 us -> 6.89 us  [partners(): parts.append(lax.ppermute(value, axis, perm))]
    ppermute x7, starting transfers between devices: 10.4 us -> 12.5 us  [partners(): parts.append(lax.ppermute(value, axis, perm))]
where the time goes in v16:
time: 76.3 us; the launch traced here: 76.2 us
  waiting for transfers between devices  38 us (50%)
  starting transfers between devices  27.5 us (36%)
  Pallas kernels  9.9 us (13%)
    ppermute x7, waiting for transfers between devices, body(): lax.ppermute(blocks[k], 'samp', [(i, i ^ k) for i in range(owners)])  31.1 us
    ppermute x7, starting transfers between devices, body(): lax.ppermute(blocks[k], 'samp', [(i, i ^ k) for i in range(owners)])  15 us
    ppermute x7, starting transfers between devices, partners(): parts.append(lax.ppermute(value, axis, perm))  12.5 us
    ppermute x7, waiting for transfers between devices, partners(): parts.append(lax.ppermute(value, axis, perm))  6.89 us
    pallas_call x1, Pallas kernels, jac_rows(): pl.pallas_call(jac_kernel, in_specs=[hbm, hbm], out_shape=[jax.ShapeDtype...  3.64 us
    pallas_call x1, Pallas kernels, solve_and_project(): pl.pallas_call(functools.partial(solve_kernel, len(grams)), out_shape=(ja...  3.52 us
    pallas_call x1, Pallas kernels, gram_partial(): pl.pallas_call(gram_kernel, out_shape=jax.ShapeDtypeStruct(packed_shape(t...  2.51 us
  transfers between devices with their start and end apart: 14, of which 9 were waited for; matrix products, arithmetic and copies ran while one was open for 0% of the time, Pallas kernels for 0%

profile of v16, /device:TPU:0, one launch (start us, length us, event | category | flops | bytes accessed | tf_op | source)
XLA Modules:
  0.0 76.2 jit_solution(7352881348442361629)
XLA Ops:
  0.6 0.0 copy-start.1
  0.6 0.0 copy-start
  0.7 3.6 %jac_rows.1 = (bf16[8,64,256]{2,1,0:T(8,128)(2,1)S(1)}, bf16[8,64,256]{2,1,0:T(8,128)(2,1)S(1)}, bf16[8,64,256]{2,1,0:T(8,128)(2,1)S(1)}, bf16[8,64,256]{2,1,0:T...) custom-call(bf16[8,2,256,256]{3,2,1,0:T(8,128)(2,1)} %act_hbm.1, ...), custom_call_target="tpu_custom_call" | custom-call | flops 536870912 | bytes 6291456 | tf_op jit(solution)/shard_map/jac_rows/pallas_call | solution.py:83
  4.3 4.1 %collective-permute-start = (bf16[8,64,256]{2,1,0:T(8,128)(2,1)S(1)}, bf16[8,64,256]{2,1,0:T(8,128)(2,1)S(1)}, u32[]{:S(2)}, u32[]{:S(2)}) collective-permute-start(bf16[8,64,256]{2,1,0:T(8,128)(2,1)S(1)} %get-tuple-element.12), channel_id=1, source_target_pairs={{0,16},{4,20},{8,24},{12,28},{16,0},{20,4},{24,8},{28,12},{1,17},{... | collective-permute-start | bytes 786440 | tf_op jit(solution)/shard_map/ppermute | solution.py:362
  8.4 1.3 %collective-permute-start.1 = (bf16[8,64,256]{2,1,0:T(8,128)(2,1)S(1)}, bf16[8,64,256]{2,1,0:T(8,128)(2,1)S(1)}, u32[]{:S(2)}, u32[]{:S(2)}) collective-permute-start(bf16[8,64,256]{2,1,0:T(8,128)(2,1)S(1)} %get-tuple-element.13), channel_id=1, source_target_pairs={{0,20},{4,16},{8,28},{12,24},{16,4},{20,0},{24,12},{28,8},{1,21},{... | collective-permute-start | bytes 786440 | tf_op jit(solution)/shard_map/ppermute | solution.py:362
  9.7 1.5 %collective-permute-start.2 = (bf16[8,64,256]{2,1,0:T(8,128)(2,1)S(1)}, bf16[8,64,256]{2,1,0:T(8,128)(2,1)S(1)}, u32[]{:S(2)}, u32[]{:S(2)}) collective-permute-start(bf16[8,64,256]{2,1,0:T(8,128)(2,1)S(1)} %get-tuple-element.14), channel_id=1, source_target_pairs={{0,12},{4,8},{8,4},{12,0},{16,28},{20,24},{24,20},{28,16},{1,13},{... | collective-permute-start | bytes 786440 | tf_op jit(solution)/shard_map/ppermute | solution.py:362
  11.2 2.5 %collective-permute-start.3 = (bf16[8,64,256]{2,1,0:T(8,128)(2,1)S(1)}, bf16[8,64,256]{2,1,0:T(8,128)(2,1)S(1)}, u32[]{:S(2)}, u32[]{:S(2)}) collective-permute-start(bf16[8,64,256]{2,1,0:T(8,128)(2,1)S(1)} %get-tuple-element.15), channel_id=1, source_target_pairs={{0,24},{4,28},{8,16},{12,20},{16,8},{20,12},{24,0},{28,4},{1,25},{... | collective-permute-start | bytes 786440 | tf_op jit(solution)/shard_map/ppermute | solution.py:362
  13.7 0.7 collective-permute-start.4
  14.4 12.5 %collective-permute-done.refs_0_.refs_2_ = bf16[8,64,256]{2,1,0:T(8,128)(2,1)S(1)} collective-permute-done((bf16[8,64,256]{2,1,0:T(8,128)(2,1)S(1)}, bf16[8,64,256]{2,1,0:T(8,128)(2,1)S(1)}, u32[]{:S(2)}, u32[]{:S(2)}) %collective-permute-start) | collective-permute-done | bytes 262176 | tf_op jit(solution)/shard_map/ppermute | solution.py:362
  26.9 4.9 %collective-permute-start.5 = (bf16[8,64,256]{2,1,0:T(8,128)(2,1)}, bf16[8,64,256]{2,1,0:T(8,128)(2,1)S(1)}, u32[]{:S(2)}, u32[]{:S(2)}) collective-permute-start(bf16[8,64,256]{2,1,0:T(8,128)(2,1)} %get-tuple-element.17), channel_id=1, source_target_pairs={{0,28},{4,24},{8,20},{12,16},{16,12},{20,8},{24,4},{28,0},{1,29},{... | collective-permute-start | bytes 786440 | tf_op jit(solution)/shard_map/ppermute | solution.py:362
  31.8 7.7 %collective-permute-done.1.refs_1_.refs_3_ = bf16[8,64,256]{2,1,0:T(8,128)(2,1)S(1)} collective-permute-done((bf16[8,64,256]{2,1,0:T(8,128)(2,1)S(1)}, bf16[8,64,256]{2,1,0:T(8,128)(2,1)S(1)}, u32[]{:S(2)}, u32[]{:S(2)}) %collective-permute-start.1) | collective-permute-done | bytes 262176 | tf_op jit(solution)/shard_map/ppermute | solution.py:362
  39.5 0.0 collective-permute-start.6
  39.5 0.0 copy-done.1
  39.5 0.1 copy.6.offdiag_ref
  39.6 0.0 copy-done
  39.6 0.2 packed_energy.1.refs_8_
  39.8 0.0 collective-permute-done.2.refs_2_.refs_4_
  39.8 0.0 collective-permute-done.3.refs_3_.refs_5_
  39.8 0.0 collective-permute-done.4.refs_4_.refs_6_
  39.9 6.2 %collective-permute-done.5.refs_5_.refs_7_ = bf16[8,64,256]{2,1,0:T(8,128)(2,1)S(1)} collective-permute-done((bf16[8,64,256]{2,1,0:T(8,128)(2,1)}, bf16[8,64,256]{2,1,0:T(8,128)(2,1)S(1)}, u32[]{:S(2)}, u32[]{:S(2)}) %collective-permute-start.5) | collective-permute-done | bytes 262176 | tf_op jit(solution)/shard_map/ppermute | solution.py:362
  46.1 4.7 %collective-permute-done.6.refs_6_.refs_8_ = bf16[8,64,256]{2,1,0:T(8,128)(2,1)S(1)} collective-permute-done((bf16[8,64,256]{2,1,0:T(8,128)(2,1)S(1)}, bf16[8,64,256]{2,1,0:T(8,128)(2,1)S(1)}, u32[]{:S(2)}, u32[]{:S(2)}) %collective-permute-start.6) | collective-permute-done | bytes 262176 | tf_op jit(solution)/shard_map/ppermute | solution.py:362
  50.7 2.5 %gram_partial.1.refs_3_ = f32[32,128]{1,0:T(8,128)S(1)} custom-call(bf16[8,64,256]{2,1,0:T(8,128)(2,1)S(1)} %collective-permute-done.refs_0_.refs_2_, bf16[8,64,256]{2,1,0:T(8,128)(2,1)S(1)} %collective-permute-done.1.refs_1_.refs_3_, bf16[8,64,256]{2,1,0:T(8,128)(2,1)S(1)} %collective-permute-done.2.refs_2_.refs_4_, ...), custom_call_target="tpu_custom_call" | custom-call | flops 134217728 | bytes 2097152 | tf_op jit(solution)/shard_map/gram_partial/pallas_call | solution.py:174
  53.2 0.2 collective-permute-start.7
  53.5 1.4 %collective-permute-start.8 = (f32[32,128]{1,0:T(8,128)S(1)}, f32[32,128]{1,0:T(8,128)S(1)}, u32[]{:S(2)}, u32[]{:S(2)}) collective-permute-start(f32[32,128]{1,0:T(8,128)S(1)} %gram_partial.1.refs_3_), channel_id=1, source_target_pairs={{0,2},{1,3},{2,0},{3,1},{4,6},{5,7},{6,4},{7,5},{8,10},{9,11},{10,... | collective-permute-start | bytes 49160 | tf_op jit(solution)/shard_map/ppermute | solution.py:283
  54.9 0.3 collective-permute-start.9
  55.2 1.4 %collective-permute-done.7.refs_0_ = f32[32,128]{1,0:T(8,128)S(1)} collective-permute-done((f32[32,128]{1,0:T(8,128)S(1)}, f32[32,128]{1,0:T(8,128)S(1)}, u32[]{:S(2)}, u32[]{:S(2)}) %collective-permute-start.7) | collective-permute-done | bytes 16416 | tf_op jit(solution)/shard_map/ppermute | solution.py:283
  56.6 0.6 collective-permute-done.8.refs_1_
  57.2 0.0 collective-permute-done.9.refs_2_
  57.2 6.1 %collective-permute-start.10 = (f32[32,128]{1,0:T(8,128)S(1)}, f32[32,128]{1,0:T(8,128)S(1)}, u32[]{:S(2)}, u32[]{:S(2)}) collective-permute-start(f32[32,128]{1,0:T(8,128)S(1)} %sum_over.2.refs_3_), channel_id=1, source_target_pairs={{0,12},{4,8},{8,4},{12,0},{16,28},{20,24},{24,20},{28,16},{1,13},{... | collective-permute-start | bytes 49160 | tf_op jit(solution)/shard_map/ppermute | solution.py:283
  63.4 0.0 collective-permute-start.11
  63.4 0.6 collective-permute-start.12
  64.0 1.1 %collective-permute-done.10.refs_0_ = f32[32,128]{1,0:T(8,128)S(1)} collective-permute-done((f32[32,128]{1,0:T(8,128)S(1)}, f32[32,128]{1,0:T(8,128)S(1)}, u32[]{:S(2)}, u32[]{:S(2)}) %collective-permute-start.10) | collective-permute-done | bytes 16416 | tf_op jit(solution)/shard_map/ppermute | solution.py:283
  65.1 2.0 %collective-permute-done.11.refs_1_ = f32[32,128]{1,0:T(8,128)S(1)} collective-permute-done((f32[32,128]{1,0:T(8,128)S(1)}, f32[32,128]{1,0:T(8,128)S(1)}, u32[]{:S(2)}, u32[]{:S(2)}) %collective-permute-start.11) | collective-permute-done | bytes 16416 | tf_op jit(solution)/shard_map/ppermute | solution.py:283
  67.1 0.0 collective-permute-done.12.refs_2_
  67.1 3.8 %collective-permute-start.13 = (f32[32,128]{1,0:T(8,128)S(1)}, f32[32,128]{1,0:T(8,128)S(1)}, u32[]{:S(2)}, u32[]{:S(2)}) collective-permute-start(f32[32,128]{1,0:T(8,128)S(1)} %sum_over.3.refs_1_), channel_id=1, source_target_pairs={{0,16},{4,20},{8,24},{12,28},{16,0},{20,4},{24,8},{28,12},{1,17},{... | collective-permute-start | bytes 49160 | tf_op jit(solution)/shard_map/ppermute | solution.py:283
  70.9 1.7 %collective-permute-done.13.refs_0_ = f32[32,128]{1,0:T(8,128)S(1)} collective-permute-done((f32[32,128]{1,0:T(8,128)S(1)}, f32[32,128]{1,0:T(8,128)S(1)}, u32[]{:S(2)}, u32[]{:S(2)}) %collective-permute-start.13) | collective-permute-done | bytes 16416 | tf_op jit(solution)/shard_map/ppermute | solution.py:283
  72.7 3.5 %solve_and_project.1 = (f32[1,8]{1,0:T(1,128)}, f32[2,32,256]{2,1,0:T(8,128)}) custom-call(f32[32,128]{1,0:T(8,128)S(1)} %collective-permute-done.13.refs_0_, f32[32,128]{1,0:T(8,128)S(1)} %sum_over.3.refs_1_, bf16[8,64,256]{2,1,0:T(8,128)(2,1)S(1)} %collective-permute-done.refs_0_.refs_2_, bf16[8,64,256]{2,1,0:T(8,128)(2,1)S(1)} %collective-permute-done.1.refs_1_.refs_3_, ...), custom_call_target="tpu_custom_call" | custom-call | tf_op jit(solution)/shard_map/solve_and_project/pallas_call | solution.py:344
  (2 shorter events, 0.0 us)
Async XLA Ops:
  0.6 38.9 %copy-start.1 = (f32[8]{0:T(128)S(1)}, f32[8]{0:T(128)}, u32[]{:S(2)}) copy-start(f32[8]{0:T(128)} %param.7) | copy-start | bytes 100
  0.6 39.0 %copy-start = (s32[8,256]{1,0:T(8,128)S(1)}, s32[8,256]{1,0:T(8,128)}, u32[]{:S(2)}) copy-start(s32[8,256]{1,0:T(8,128)} %spins_ref.1) | copy-start | bytes 24580
  4.3 22.6 %collective-permute-start = (bf16[8,64,256]{2,1,0:T(8,128)(2,1)S(1)}, bf16[8,64,256]{2,1,0:T(8,128)(2,1)S(1)}, u32[]{:S(2)}, u32[]{:S(2)}) collective-permute-start(bf16[8,64,256]{2,1,0:T(8,128)(2,1)S(1)} %get-tuple-element.12), channel_id=1, source_target_pairs={{0,16},{4,20},{8,24},{12,28},{16,0},{20,4},{24,8},{28,12},{1,17},{... | collective-permute-start | bytes 786440 | tf_op jit(solution)/shard_map/ppermute | solution.py:362
  8.4 31.1 %collective-permute-start.1 = (bf16[8,64,256]{2,1,0:T(8,128)(2,1)S(1)}, bf16[8,64,256]{2,1,0:T(8,128)(2,1)S(1)}, u32[]{:S(2)}, u32[]{:S(2)}) collective-permute-start(bf16[8,64,256]{2,1,0:T(8,128)(2,1)S(1)} %get-tuple-element.13), channel_id=1, source_target_pairs={{0,20},{4,16},{8,28},{12,24},{16,4},{20,0},{24,12},{28,8},{1,21},{... | collective-permute-start | bytes 786440 | tf_op jit(solution)/shard_map/ppermute | solution.py:362
  9.7 30.1 %collective-permute-start.2 = (bf16[8,64,256]{2,1,0:T(8,128)(2,1)S(1)}, bf16[8,64,256]{2,1,0:T(8,128)(2,1)S(1)}, u32[]{:S(2)}, u32[]{:S(2)}) collective-permute-start(bf16[8,64,256]{2,1,0:T(8,128)(2,1)S(1)} %get-tuple-element.14), channel_id=1, source_target_pairs={{0,12},{4,8},{8,4},{12,0},{16,28},{20,24},{24,20},{28,16},{1,13},{... | collective-permute-start | bytes 786440 | tf_op jit(solution)/shard_map/ppermute | solution.py:362
  11.2 28.6 %collective-permute-start.3 = (bf16[8,64,256]{2,1,0:T(8,128)(2,1)S(1)}, bf16[8,64,256]{2,1,0:T(8,128)(2,1)S(1)}, u32[]{:S(2)}, u32[]{:S(2)}) collective-permute-start(bf16[8,64,256]{2,1,0:T(8,128)(2,1)S(1)} %get-tuple-element.15), channel_id=1, source_target_pairs={{0,24},{4,28},{8,16},{12,20},{16,8},{20,12},{24,0},{28,4},{1,25},{... | collective-permute-start | bytes 786440 | tf_op jit(solution)/shard_map/ppermute | solution.py:362
  13.7 26.2 %collective-permute-start.4 = (bf16[8,64,256]{2,1,0:T(8,128)(2,1)S(1)}, bf16[8,64,256]{2,1,0:T(8,128)(2,1)S(1)}, u32[]{:S(2)}, u32[]{:S(2)}) collective-permute-start(bf16[8,64,256]{2,1,0:T(8,128)(2,1)S(1)} %get-tuple-element.16), channel_id=1, source_target_pairs={{0,8},{4,12},{8,0},{12,4},{16,24},{20,28},{24,16},{28,20},{1,9},{5... | collective-permute-start | bytes 786440 | tf_op jit(solution)/shard_map/ppermute | solution.py:362
  26.9 19.2 %collective-permute-start.5 = (bf16[8,64,256]{2,1,0:T(8,128)(2,1)}, bf16[8,64,256]{2,1,0:T(8,128)(2,1)S(1)}, u32[]{:S(2)}, u32[]{:S(2)}) collective-permute-start(bf16[8,64,256]{2,1,0:T(8,128)(2,1)} %get-tuple-element.17), channel_id=1, source_target_pairs={{0,28},{4,24},{8,20},{12,16},{16,12},{20,8},{24,4},{28,0},{1,29},{... | collective-permute-start | bytes 786440 | tf_op jit(solution)/shard_map/ppermute | solution.py:362
  39.5 11.2 %collective-permute-start.6 = (bf16[8,64,256]{2,1,0:T(8,128)(2,1)S(1)}, bf16[8,64,256]{2,1,0:T(8,128)(2,1)S(1)}, u32[]{:S(2)}, u32[]{:S(2)}) collective-permute-start(bf16[8,64,256]{2,1,0:T(8,128)(2,1)S(1)} %get-tuple-element.18), channel_id=1, source_target_pairs={{0,4},{4,0},{8,12},{12,8},{16,20},{20,16},{24,28},{28,24},{1,5},{5... | collective-permute-start | bytes 786440 | tf_op jit(solution)/shard_map/ppermute | solution.py:362
  53.2 3.3 %collective-permute-start.7 = (f32[32,128]{1,0:T(8,128)S(1)}, f32[32,128]{1,0:T(8,128)S(1)}, u32[]{:S(2)}, u32[]{:S(2)}) collective-permute-start(f32[32,128]{1,0:T(8,128)S(1)} %gram_partial.1.refs_3_), channel_id=1, source_target_pairs={{0,3},{1,2},{2,1},{3,0},{4,7},{5,6},{6,5},{7,4},{8,11},{9,10},{10,... | collective-permute-start | bytes 49160 | tf_op jit(solution)/shard_map/ppermute | solution.py:283
  53.5 3.7 %collective-permute-start.8 = (f32[32,128]{1,0:T(8,128)S(1)}, f32[32,128]{1,0:T(8,128)S(1)}, u32[]{:S(2)}, u32[]{:S(2)}) collective-permute-start(f32[32,128]{1,0:T(8,128)S(1)} %gram_partial.1.refs_3_), channel_id=1, source_target_pairs={{0,2},{1,3},{2,0},{3,1},{4,6},{5,7},{6,4},{7,5},{8,10},{9,11},{10,... | collective-permute-start | bytes 49160 | tf_op jit(solution)/shard_map/ppermute | solution.py:283
  54.9 2.4 %collective-permute-start.9 = (f32[32,128]{1,0:T(8,128)S(1)}, f32[32,128]{1,0:T(8,128)S(1)}, u32[]{:S(2)}, u32[]{:S(2)}) collective-permute-start(f32[32,128]{1,0:T(8,128)S(1)} %gram_partial.1.refs_3_), channel_id=1, source_target_pairs={{0,1},{1,0},{2,3},{3,2},{4,5},{5,4},{6,7},{7,6},{8,9},{9,8},{10,11... | collective-permute-start | bytes 49160 | tf_op jit(solution)/shard_map/ppermute | solution.py:283
  57.2 7.8 %collective-permute-start.10 = (f32[32,128]{1,0:T(8,128)S(1)}, f32[32,128]{1,0:T(8,128)S(1)}, u32[]{:S(2)}, u32[]{:S(2)}) collective-permute-start(f32[32,128]{1,0:T(8,128)S(1)} %sum_over.2.refs_3_), channel_id=1, source_target_pairs={{0,12},{4,8},{8,4},{12,0},{16,28},{20,24},{24,20},{28,16},{1,13},{... | collective-permute-start | bytes 49160 | tf_op jit(solution)/shard_map/ppermute | solution.py:283
  63.4 3.7 %collective-permute-start.11 = (f32[32,128]{1,0:T(8,128)S(1)}, f32[32,128]{1,0:T(8,128)S(1)}, u32[]{:S(2)}, u32[]{:S(2)}) collective-permute-start(f32[32,128]{1,0:T(8,128)S(1)} %sum_over.2.refs_3_), channel_id=1, source_target_pairs={{0,8},{4,12},{8,0},{12,4},{16,24},{20,28},{24,16},{28,20},{1,9},{5... | collective-permute-start | bytes 49160 | tf_op jit(solution)/shard_map/ppermute | solution.py:283
  63.4 3.7 %collective-permute-start.12 = (f32[32,128]{1,0:T(8,128)S(1)}, f32[32,128]{1,0:T(8,128)S(1)}, u32[]{:S(2)}, u32[]{:S(2)}) collective-permute-start(f32[32,128]{1,0:T(8,128)S(1)} %sum_over.2.refs_3_), channel_id=1, source_target_pairs={{0,4},{4,0},{8,12},{12,8},{16,20},{20,16},{24,28},{28,24},{1,5},{5... | collective-permute-start | bytes 49160 | tf_op jit(solution)/shard_map/ppermute | solution.py:283
  67.1 5.6 %collective-permute-start.13 = (f32[32,128]{1,0:T(8,128)S(1)}, f32[32,128]{1,0:T(8,128)S(1)}, u32[]{:S(2)}, u32[]{:S(2)}) collective-permute-start(f32[32,128]{1,0:T(8,128)S(1)} %sum_over.3.refs_1_), channel_id=1, source_target_pairs={{0,16},{4,20},{8,24},{12,28},{16,0},{20,4},{24,8},{28,12},{1,17},{... | collective-permute-start | bytes 49160 | tf_op jit(solution)/shard_map/ppermute | solution.py:283

commit v17 on v16

--- a/solution.py
+++ b/solution.py
@@ -56,24 +56,31 @@
     for pair in copies:
         for copy in pair:
             copy.start()
+
+    def share_out(samples):
+        for k, out_ref in enumerate(out_refs):
+            owned = pl.ds(pl.multiple_of((me ^ k) * share, share), share)
+            for s in samples:
+                rows = [held[s, m, owned] for m in range(mats)]
+                out_ref[s] = jnp.concatenate(rows, axis=0).astype(BF16)
+
     group = 2
     for first in range(0, samples, group):
-        for s in range(first, first + group):
+        here = range(first, first + group)
+        for s in here:
             for copy in copies[s]:
                 copy.wait()
-        for s in range(first, first + group):
+        for s in here:
             for m in range(mats):
                 held[s, m] = lax.dot_general(
                     act_buf[s, m],
                     cot_buf[s, m],
                     (((0,), (0,)), ((), ())),
                     preferred_element_type=F32,
-                )
-    for k, out_ref in enumerate(out_refs):
-        owned = pl.ds(pl.multiple_of((me ^ k) * share, share), share)
-        for s in range(samples):
-            rows = [held[s, m, owned] for m in range(mats)]
-            out_ref[s] = jnp.concatenate(rows, axis=0).astype(BF16)
+                ).astype(held.dtype)
+        if first > 0:
+            share_out(range(first - group, first))
+    share_out(range(samples - group, samples))
 
 
 def jac_rows(activations, cotangents, owners):
@@ -87,7 +94,7 @@
         scratch_shapes=[
             pltpu.VMEM((samples, mats, sites, d), BF16),
             pltpu.VMEM((samples, mats, sites, d), BF16),
-            pltpu.VMEM((samples, mats, d, d), F32),
+            pltpu.VMEM((samples, mats, d, d), BF16 if d // owners % CHUNK == 0 else F32),
             pltpu.SemaphoreType.DMA((2, samples)),
         ],
         compiler_params=pltpu.CompilerParams(vmem_limit_bytes=JAC_VMEM_LIMIT),
@@ -158,9 +165,9 @@
             for r in range(CHUNK):
                 flat[row + r, place] = turned[r * CHUNK : (r + 1) * CHUNK]
     lined = jnp.concatenate([flat[r] for r in range(count)], axis=1)
-    whole[:, :total] = lax.dot_general(
-        lined, lined, (((1,), (1,)), ((), ())), preferred_element_type=F32
-    )
+    gram = lax.dot_general(lined, lined, (((1,), (1,)), ((), ())), preferred_element_type=F32)
+    whole[...] = jnp.zeros_like(whole)
+    whole[:, :total] += gram
     half, width = out_ref.shape
     lane = iota((half, width), 1)
     lower = pltpu.roll(whole[half:], half, 1)

time: 76.3 us -> 75.2 us (0.986)
  Pallas kernels: 9.9 us -> 8.84 us
    pallas_call x1, Pallas kernels: 2.51 us -> 1.52 us  [gram_partial(): pl.pallas_call(gram_kernel, out_shape=jax.ShapeDtypeStruct(packed_shape(t...]
where the time goes in v17:
time: 75.2 us; the launch traced here: 75.1 us
  waiting for transfers between devices  38 us (51%)
  starting transfers between devices  27.5 us (37%)
  Pallas kernels  8.84 us (12%)
    ppermute x7, waiting for transfers between devices, body(): lax.ppermute(blocks[k], 'samp', [(i, i ^ k) for i in range(owners)])  31.1 us
    ppermute x7, starting transfers between devices, body(): lax.ppermute(blocks[k], 'samp', [(i, i ^ k) for i in range(owners)])  15 us
    ppermute x7, starting transfers between devices, partners(): parts.append(lax.ppermute(value, axis, perm))  12.5 us
    ppermute x7, waiting for transfers between devices, partners(): parts.append(lax.ppermute(value, axis, perm))  6.87 us
    pallas_call x1, Pallas kernels, jac_rows(): pl.pallas_call(jac_kernel, in_specs=[hbm, hbm], out_shape=[jax.ShapeDtype...  3.57 us
    pallas_call x1, Pallas kernels, solve_and_project(): pl.pallas_call(functools.partial(solve_kernel, len(grams)), out_shape=(ja...  3.52 us
    pallas_call x1, Pallas kernels, gram_partial(): pl.pallas_call(gram_kernel, out_shape=jax.ShapeDtypeStruct(packed_shape(t...  1.52 us
  transfers between devices with their start and end apart: 14, of which 9 were waited for; matrix products, arithmetic and copies ran while one was open for 0% of the time, Pallas kernels for 0%

profile of v17, /device:TPU:0, one launch (start us, length us, event | category | flops | bytes accessed | tf_op | source)
XLA Modules:
  0.0 75.1 jit_solution(12482727513435648673)
XLA Ops:
  0.6 0.0 copy-start.1
  0.6 0.0 copy-start
  0.7 3.6 %jac_rows.1 = (bf16[8,64,256]{2,1,0:T(8,128)(2,1)S(1)}, bf16[8,64,256]{2,1,0:T(8,128)(2,1)S(1)}, bf16[8,64,256]{2,1,0:T(8,128)(2,1)S(1)}, bf16[8,64,256]{2,1,0:T...) custom-call(bf16[8,2,256,256]{3,2,1,0:T(8,128)(2,1)} %act_hbm.1, ...), custom_call_target="tpu_custom_call" | custom-call | flops 536870912 | bytes 6291456 | tf_op jit(solution)/shard_map/jac_rows/pallas_call | solution.py:90
  4.2 4.1 %collective-permute-start = (bf16[8,64,256]{2,1,0:T(8,128)(2,1)S(1)}, bf16[8,64,256]{2,1,0:T(8,128)(2,1)S(1)}, u32[]{:S(2)}, u32[]{:S(2)}) collective-permute-start(bf16[8,64,256]{2,1,0:T(8,128)(2,1)S(1)} %get-tuple-element.12), channel_id=1, source_target_pairs={{0,16},{4,20},{8,24},{12,28},{16,0},{20,4},{24,8},{28,12},{1,17},{... | collective-permute-start | bytes 786440 | tf_op jit(solution)/shard_map/ppermute | solution.py:369
  8.3 1.3 %collective-permute-start.1 = (bf16[8,64,256]{2,1,0:T(8,128)(2,1)S(1)}, bf16[8,64,256]{2,1,0:T(8,128)(2,1)S(1)}, u32[]{:S(2)}, u32[]{:S(2)}) collective-permute-start(bf16[8,64,256]{2,1,0:T(8,128)(2,1)S(1)} %get-tuple-element.13), channel_id=1, source_target_pairs={{0,20},{4,16},{8,28},{12,24},{16,4},{20,0},{24,12},{28,8},{1,21},{... | collective-permute-start | bytes 786440 | tf_op jit(solution)/shard_map/ppermute | solution.py:369
  9.6 1.5 %collective-permute-start.2 = (bf16[8,64,256]{2,1,0:T(8,128)(2,1)S(1)}, bf16[8,64,256]{2,1,0:T(8,128)(2,1)S(1)}, u32[]{:S(2)}, u32[]{:S(2)}) collective-permute-start(bf16[8,64,256]{2,1,0:T(8,128)(2,1)S(1)} %get-tuple-element.14), channel_id=1, source_target_pairs={{0,12},{4,8},{8,4},{12,0},{16,28},{20,24},{24,20},{28,16},{1,13},{... | collective-permute-start | bytes 786440 | tf_op jit(solution)/shard_map/ppermute | solution.py:369
  11.1 2.5 %collective-permute-start.3 = (bf16[8,64,256]{2,1,0:T(8,128)(2,1)S(1)}, bf16[8,64,256]{2,1,0:T(8,128)(2,1)S(1)}, u32[]{:S(2)}, u32[]{:S(2)}) collective-permute-start(bf16[8,64,256]{2,1,0:T(8,128)(2,1)S(1)} %get-tuple-element.15), channel_id=1, source_target_pairs={{0,24},{4,28},{8,16},{12,20},{16,8},{20,12},{24,0},{28,4},{1,25},{... | collective-permute-start | bytes 786440 | tf_op jit(solution)/shard_map/ppermute | solution.py:369
  13.6 0.7 collective-permute-start.4
  14.3 12.5 %collective-permute-done.refs_0_.refs_2_ = bf16[8,64,256]{2,1,0:T(8,128)(2,1)S(1)} collective-permute-done((bf16[8,64,256]{2,1,0:T(8,128)(2,1)S(1)}, bf16[8,64,256]{2,1,0:T(8,128)(2,1)S(1)}, u32[]{:S(2)}, u32[]{:S(2)}) %collective-permute-start) | collective-permute-done | bytes 262176 | tf_op jit(solution)/shard_map/ppermute | solution.py:369
  26.8 4.9 %collective-permute-start.5 = (bf16[8,64,256]{2,1,0:T(8,128)(2,1)}, bf16[8,64,256]{2,1,0:T(8,128)(2,1)S(1)}, u32[]{:S(2)}, u32[]{:S(2)}) collective-permute-start(bf16[8,64,256]{2,1,0:T(8,128)(2,1)} %get-tuple-element.17), channel_id=1, source_target_pairs={{0,28},{4,24},{8,20},{12,16},{16,12},{20,8},{24,4},{28,0},{1,29},{... | collective-permute-start | bytes 786440 | tf_op jit(solution)/shard_map/ppermute | solution.py:369
  31.7 7.7 %collective-permute-done.1.refs_1_.refs_3_ = bf16[8,64,256]{2,1,0:T(8,128)(2,1)S(1)} collective-permute-done((bf16[8,64,256]{2,1,0:T(8,128)(2,1)S(1)}, bf16[8,64,256]{2,1,0:T(8,128)(2,1)S(1)}, u32[]{:S(2)}, u32[]{:S(2)}) %collective-permute-start.1) | collective-permute-done | bytes 262176 | tf_op jit(solution)/shard_map/ppermute | solution.py:369
  39.4 0.0 collective-permute-start.6
  39.5 0.0 copy-done.1
  39.5 0.1 copy.6.offdiag_ref
  39.5 0.0 copy-done
  39.5 0.2 packed_energy.1.refs_8_
  39.8 0.0 collective-permute-done.2.refs_2_.refs_4_
  39.8 0.0 collective-permute-done.3.refs_3_.refs_5_
  39.8 0.0 collective-permute-done.4.refs_4_.refs_6_
  39.8 6.2 %collective-permute-done.5.refs_5_.refs_7_ = bf16[8,64,256]{2,1,0:T(8,128)(2,1)S(1)} collective-permute-done((bf16[8,64,256]{2,1,0:T(8,128)(2,1)}, bf16[8,64,256]{2,1,0:T(8,128)(2,1)S(1)}, u32[]{:S(2)}, u32[]{:S(2)}) %collective-permute-start.5) | collective-permute-done | bytes 262176 | tf_op jit(solution)/shard_map/ppermute | solution.py:369
  46.0 4.7 %collective-permute-done.6.refs_6_.refs_8_ = bf16[8,64,256]{2,1,0:T(8,128)(2,1)S(1)} collective-permute-done((bf16[8,64,256]{2,1,0:T(8,128)(2,1)S(1)}, bf16[8,64,256]{2,1,0:T(8,128)(2,1)S(1)}, u32[]{:S(2)}, u32[]{:S(2)}) %collective-permute-start.6) | collective-permute-done | bytes 262176 | tf_op jit(solution)/shard_map/ppermute | solution.py:369
  50.7 1.5 %gram_partial.1.refs_3_ = f32[32,128]{1,0:T(8,128)S(1)} custom-call(bf16[8,64,256]{2,1,0:T(8,128)(2,1)S(1)} %collective-permute-done.refs_0_.refs_2_, bf16[8,64,256]{2,1,0:T(8,128)(2,1)S(1)} %collective-permute-done.1.refs_1_.refs_3_, bf16[8,64,256]{2,1,0:T(8,128)(2,1)S(1)} %collective-permute-done.2.refs_2_.refs_4_, ...), custom_call_target="tpu_custom_call" | custom-call | flops 134217728 | bytes 2097152 | tf_op jit(solution)/shard_map/gram_partial/pallas_call | solution.py:181
  52.2 0.2 collective-permute-start.7
  52.4 1.4 %collective-permute-start.8 = (f32[32,128]{1,0:T(8,128)S(1)}, f32[32,128]{1,0:T(8,128)S(1)}, u32[]{:S(2)}, u32[]{:S(2)}) collective-permute-start(f32[32,128]{1,0:T(8,128)S(1)} %gram_partial.1.refs_3_), channel_id=1, source_target_pairs={{0,2},{1,3},{2,0},{3,1},{4,6},{5,7},{6,4},{7,5},{8,10},{9,11},{10,... | collective-permute-start | bytes 49160 | tf_op jit(solution)/shard_map/ppermute | solution.py:290
  53.8 0.3 collective-permute-start.9
  54.1 1.4 %collective-permute-done.7.refs_0_ = f32[32,128]{1,0:T(8,128)S(1)} collective-permute-done((f32[32,128]{1,0:T(8,128)S(1)}, f32[32,128]{1,0:T(8,128)S(1)}, u32[]{:S(2)}, u32[]{:S(2)}) %collective-permute-start.7) | collective-permute-done | bytes 16416 | tf_op jit(solution)/shard_map/ppermute | solution.py:290
  55.5 0.6 collective-permute-done.8.refs_1_
  56.2 0.0 collective-permute-done.9.refs_2_
  56.2 6.1 %collective-permute-start.10 = (f32[32,128]{1,0:T(8,128)S(1)}, f32[32,128]{1,0:T(8,128)S(1)}, u32[]{:S(2)}, u32[]{:S(2)}) collective-permute-start(f32[32,128]{1,0:T(8,128)S(1)} %sum_over.2.refs_3_), channel_id=1, source_target_pairs={{0,12},{4,8},{8,4},{12,0},{16,28},{20,24},{24,20},{28,16},{1,13},{... | collective-permute-start | bytes 49160 | tf_op jit(solution)/shard_map/ppermute | solution.py:290
  62.3 0.0 collective-permute-start.11
  62.3 0.6 collective-permute-start.12
  62.9 1.1 %collective-permute-done.10.refs_0_ = f32[32,128]{1,0:T(8,128)S(1)} collective-permute-done((f32[32,128]{1,0:T(8,128)S(1)}, f32[32,128]{1,0:T(8,128)S(1)}, u32[]{:S(2)}, u32[]{:S(2)}) %collective-permute-start.10) | collective-permute-done | bytes 16416 | tf_op jit(solution)/shard_map/ppermute | solution.py:290
  64.0 2.0 %collective-permute-done.11.refs_1_ = f32[32,128]{1,0:T(8,128)S(1)} collective-permute-done((f32[32,128]{1,0:T(8,128)S(1)}, f32[32,128]{1,0:T(8,128)S(1)}, u32[]{:S(2)}, u32[]{:S(2)}) %collective-permute-start.11) | collective-permute-done | bytes 16416 | tf_op jit(solution)/shard_map/ppermute | solution.py:290
  66.0 0.0 collective-permute-done.12.refs_2_
  66.0 3.8 %collective-permute-start.13 = (f32[32,128]{1,0:T(8,128)S(1)}, f32[32,128]{1,0:T(8,128)S(1)}, u32[]{:S(2)}, u32[]{:S(2)}) collective-permute-start(f32[32,128]{1,0:T(8,128)S(1)} %sum_over.3.refs_1_), channel_id=1, source_target_pairs={{0,16},{4,20},{8,24},{12,28},{16,0},{20,4},{24,8},{28,12},{1,17},{... | collective-permute-start | bytes 49160 | tf_op jit(solution)/shard_map/ppermute | solution.py:290
  69.9 1.7 %collective-permute-done.13.refs_0_ = f32[32,128]{1,0:T(8,128)S(1)} collective-permute-done((f32[32,128]{1,0:T(8,128)S(1)}, f32[32,128]{1,0:T(8,128)S(1)}, u32[]{:S(2)}, u32[]{:S(2)}) %collective-permute-start.13) | collective-permute-done | bytes 16416 | tf_op jit(solution)/shard_map/ppermute | solution.py:290
  71.6 3.5 %solve_and_project.1 = (f32[1,8]{1,0:T(1,128)}, f32[2,32,256]{2,1,0:T(8,128)}) custom-call(f32[32,128]{1,0:T(8,128)S(1)} %collective-permute-done.13.refs_0_, f32[32,128]{1,0:T(8,128)S(1)} %sum_over.3.refs_1_, bf16[8,64,256]{2,1,0:T(8,128)(2,1)S(1)} %collective-permute-done.refs_0_.refs_2_, bf16[8,64,256]{2,1,0:T(8,128)(2,1)S(1)} %collective-permute-done.1.refs_1_.refs_3_, ...), custom_call_target="tpu_custom_call" | custom-call | tf_op jit(solution)/shard_map/solve_and_project/pallas_call | solution.py:351
  (2 shorter events, 0.0 us)
Async XLA Ops:
  0.6 38.8 %copy-start.1 = (f32[8]{0:T(128)S(1)}, f32[8]{0:T(128)}, u32[]{:S(2)}) copy-start(f32[8]{0:T(128)} %param.7) | copy-start | bytes 100
  0.6 38.9 %copy-start = (s32[8,256]{1,0:T(8,128)S(1)}, s32[8,256]{1,0:T(8,128)}, u32[]{:S(2)}) copy-start(s32[8,256]{1,0:T(8,128)} %spins_ref.1) | copy-start | bytes 24580
  4.2 22.6 %collective-permute-start = (bf16[8,64,256]{2,1,0:T(8,128)(2,1)S(1)}, bf16[8,64,256]{2,1,0:T(8,128)(2,1)S(1)}, u32[]{:S(2)}, u32[]{:S(2)}) collective-permute-start(bf16[8,64,256]{2,1,0:T(8,128)(2,1)S(1)} %get-tuple-element.12), channel_id=1, source_target_pairs={{0,16},{4,20},{8,24},{12,28},{16,0},{20,4},{24,8},{28,12},{1,17},{... | collective-permute-start | bytes 786440 | tf_op jit(solution)/shard_map/ppermute | solution.py:369
  8.3 31.1 %collective-permute-start.1 = (bf16[8,64,256]{2,1,0:T(8,128)(2,1)S(1)}, bf16[8,64,256]{2,1,0:T(8,128)(2,1)S(1)}, u32[]{:S(2)}, u32[]{:S(2)}) collective-permute-start(bf16[8,64,256]{2,1,0:T(8,128)(2,1)S(1)} %get-tuple-element.13), channel_id=1, source_target_pairs={{0,20},{4,16},{8,28},{12,24},{16,4},{20,0},{24,12},{28,8},{1,21},{... | collective-permute-start | bytes 786440 | tf_op jit(solution)/shard_map/ppermute | solution.py:369
  9.6 30.1 %collective-permute-start.2 = (bf16[8,64,256]{2,1,0:T(8,128)(2,1)S(1)}, bf16[8,64,256]{2,1,0:T(8,128)(2,1)S(1)}, u32[]{:S(2)}, u32[]{:S(2)}) collective-permute-start(bf16[8,64,256]{2,1,0:T(8,128)(2,1)S(1)} %get-tuple-element.14), channel_id=1, source_target_pairs={{0,12},{4,8},{8,4},{12,0},{16,28},{20,24},{24,20},{28,16},{1,13},{... | collective-permute-start | bytes 786440 | tf_op jit(solution)/shard_map/ppermute | solution.py:369
  11.1 28.6 %collective-permute-start.3 = (bf16[8,64,256]{2,1,0:T(8,128)(2,1)S(1)}, bf16[8,64,256]{2,1,0:T(8,128)(2,1)S(1)}, u32[]{:S(2)}, u32[]{:S(2)}) collective-permute-start(bf16[8,64,256]{2,1,0:T(8,128)(2,1)S(1)} %get-tuple-element.15), channel_id=1, source_target_pairs={{0,24},{4,28},{8,16},{12,20},{16,8},{20,12},{24,0},{28,4},{1,25},{... | collective-permute-start | bytes 786440 | tf_op jit(solution)/shard_map/ppermute | solution.py:369
  13.6 26.2 %collective-permute-start.4 = (bf16[8,64,256]{2,1,0:T(8,128)(2,1)S(1)}, bf16[8,64,256]{2,1,0:T(8,128)(2,1)S(1)}, u32[]{:S(2)}, u32[]{:S(2)}) collective-permute-start(bf16[8,64,256]{2,1,0:T(8,128)(2,1)S(1)} %get-tuple-element.16), channel_id=1, source_target_pairs={{0,8},{4,12},{8,0},{12,4},{16,24},{20,28},{24,16},{28,20},{1,9},{5... | collective-permute-start | bytes 786440 | tf_op jit(solution)/shard_map/ppermute | solution.py:369
  26.8 19.2 %collective-permute-start.5 = (bf16[8,64,256]{2,1,0:T(8,128)(2,1)}, bf16[8,64,256]{2,1,0:T(8,128)(2,1)S(1)}, u32[]{:S(2)}, u32[]{:S(2)}) collective-permute-start(bf16[8,64,256]{2,1,0:T(8,128)(2,1)} %get-tuple-element.17), channel_id=1, source_target_pairs={{0,28},{4,24},{8,20},{12,16},{16,12},{20,8},{24,4},{28,0},{1,29},{... | collective-permute-start | bytes 786440 | tf_op jit(solution)/shard_map/ppermute | solution.py:369
  39.4 11.2 %collective-permute-start.6 = (bf16[8,64,256]{2,1,0:T(8,128)(2,1)S(1)}, bf16[8,64,256]{2,1,0:T(8,128)(2,1)S(1)}, u32[]{:S(2)}, u32[]{:S(2)}) collective-permute-start(bf16[8,64,256]{2,1,0:T(8,128)(2,1)S(1)} %get-tuple-element.18), channel_id=1, source_target_pairs={{0,4},{4,0},{8,12},{12,8},{16,20},{20,16},{24,28},{28,24},{1,5},{5... | collective-permute-start | bytes 786440 | tf_op jit(solution)/shard_map/ppermute | solution.py:369
  52.2 3.3 %collective-permute-start.7 = (f32[32,128]{1,0:T(8,128)S(1)}, f32[32,128]{1,0:T(8,128)S(1)}, u32[]{:S(2)}, u32[]{:S(2)}) collective-permute-start(f32[32,128]{1,0:T(8,128)S(1)} %gram_partial.1.refs_3_), channel_id=1, source_target_pairs={{0,3},{1,2},{2,1},{3,0},{4,7},{5,6},{6,5},{7,4},{8,11},{9,10},{10,... | collective-permute-start | bytes 49160 | tf_op jit(solution)/shard_map/ppermute | solution.py:290
  52.4 3.7 %collective-permute-start.8 = (f32[32,128]{1,0:T(8,128)S(1)}, f32[32,128]{1,0:T(8,128)S(1)}, u32[]{:S(2)}, u32[]{:S(2)}) collective-permute-start(f32[32,128]{1,0:T(8,128)S(1)} %gram_partial.1.refs_3_), channel_id=1, source_target_pairs={{0,2},{1,3},{2,0},{3,1},{4,6},{5,7},{6,4},{7,5},{8,10},{9,11},{10,... | collective-permute-start | bytes 49160 | tf_op jit(solution)/shard_map/ppermute | solution.py:290
  53.8 2.4 %collective-permute-start.9 = (f32[32,128]{1,0:T(8,128)S(1)}, f32[32,128]{1,0:T(8,128)S(1)}, u32[]{:S(2)}, u32[]{:S(2)}) collective-permute-start(f32[32,128]{1,0:T(8,128)S(1)} %gram_partial.1.refs_3_), channel_id=1, source_target_pairs={{0,1},{1,0},{2,3},{3,2},{4,5},{5,4},{6,7},{7,6},{8,9},{9,8},{10,11... | collective-permute-start | bytes 49160 | tf_op jit(solution)/shard_map/ppermute | solution.py:290
  56.2 7.8 %collective-permute-start.10 = (f32[32,128]{1,0:T(8,128)S(1)}, f32[32,128]{1,0:T(8,128)S(1)}, u32[]{:S(2)}, u32[]{:S(2)}) collective-permute-start(f32[32,128]{1,0:T(8,128)S(1)} %sum_over.2.refs_3_), channel_id=1, source_target_pairs={{0,12},{4,8},{8,4},{12,0},{16,28},{20,24},{24,20},{28,16},{1,13},{... | collective-permute-start | bytes 49160 | tf_op jit(solution)/shard_map/ppermute | solution.py:290
  62.3 3.7 %collective-permute-start.11 = (f32[32,128]{1,0:T(8,128)S(1)}, f32[32,128]{1,0:T(8,128)S(1)}, u32[]{:S(2)}, u32[]{:S(2)}) collective-permute-start(f32[32,128]{1,0:T(8,128)S(1)} %sum_over.2.refs_3_), channel_id=1, source_target_pairs={{0,8},{4,12},{8,0},{12,4},{16,24},{20,28},{24,16},{28,20},{1,9},{5... | collective-permute-start | bytes 49160 | tf_op jit(solution)/shard_map/ppermute | solution.py:290
  62.3 3.7 %collective-permute-start.12 = (f32[32,128]{1,0:T(8,128)S(1)}, f32[32,128]{1,0:T(8,128)S(1)}, u32[]{:S(2)}, u32[]{:S(2)}) collective-permute-start(f32[32,128]{1,0:T(8,128)S(1)} %sum_over.2.refs_3_), channel_id=1, source_target_pairs={{0,4},{4,0},{8,12},{12,8},{16,20},{20,16},{24,28},{28,24},{1,5},{5... | collective-permute-start | bytes 49160 | tf_op jit(solution)/shard_map/ppermute | solution.py:290
  66.0 5.6 %collective-permute-start.13 = (f32[32,128]{1,0:T(8,128)S(1)}, f32[32,128]{1,0:T(8,128)S(1)}, u32[]{:S(2)}, u32[]{:S(2)}) collective-permute-start(f32[32,128]{1,0:T(8,128)S(1)} %sum_over.3.refs_1_), channel_id=1, source_target_pairs={{0,16},{4,20},{8,24},{12,28},{16,0},{20,4},{24,8},{28,12},{1,17},{... | collective-permute-start | bytes 49160 | tf_op jit(solution)/shard_map/ppermute | solution.py:290

commit v18 on v17

--- a/solution.py
+++ b/solution.py
@@ -282,22 +282,28 @@
     out_ref[...] = tree_sum([ref[...] for ref in part_refs[::-1]])
 
 
-def partners(value, axis, first, count):
+def partners(value, axis, masks):
     size = lax.axis_size(axis)
     parts = []
-    for k in range(count - 1, 0, -1):
-        perm = [(i, i ^ (k * first)) for i in range(size)]
-        parts.append(lax.ppermute(value, axis, perm))
+    for mask in masks[::-1]:
+        parts.append(lax.ppermute(value, axis, [(i, i ^ mask) for i in range(size)]))
     return parts + [value]
 
 
-def sum_over(value, axis, first, count):
+def sum_over(value, axis, masks):
     return pl.pallas_call(
         sum_kernel,
         out_shape=jax.ShapeDtypeStruct(value.shape, F32),
         compiler_params=pltpu.CompilerParams(vmem_limit_bytes=VMEM_LIMIT),
         name="sum_over",
-    )(*partners(value, axis, first, count))
+    )(*partners(value, axis, masks))
+
+
+def rounds(size):
+    masks = [1, size - 2] + [1 << bit for bit in range(1, size.bit_length() - 2)]
+    return [
+        [a, b, a ^ b] if b else [a] for a, b in zip(masks[::2], masks[1::2] + [0] * (len(masks) % 2))
+    ]
 
 
 def solve_kernel(grams, *refs):
@@ -368,12 +374,11 @@
     for k in turns(owners)[:-1]:
         blocks[k] = lax.ppermute(blocks[k], "samp", [(i, i ^ k) for i in range(owners)])
     partial = gram_partial(blocks, packed_energy(spins, offdiag, total))
-    gram = sum_over(partial, "layer", 1, lax.axis_size("layer"))
-    first = 1
-    while 4 * first < owners:
-        gram = sum_over(gram, "samp", first, 4)
-        first *= 4
-    grams = partners(gram, "samp", first, owners // first)
+    gram = sum_over(partial, "layer", list(range(1, lax.axis_size("layer"))))
+    *early, last = rounds(owners)
+    for masks in early:
+        gram = sum_over(gram, "samp", masks)
+    grams = partners(gram, "samp", last)
     weights, update = solve_and_project(grams, blocks, mats)
     return weights.reshape(local), update
 

time: 75.2 us -> 73.9 us (0.983)
  starting transfers between devices: 27.5 us -> 25.7 us
    ppermute x7, starting transfers between devices: 12.5 us -> 10.7 us  [partners(): lax.ppermute(value, axis, [(i, i ^ mask) for i in range(size)])]
where the time goes in v18:
time: 73.9 us; the launch traced here: 73.8 us
  waiting for transfers between devices  38.4 us (52%)
  starting transfers between devices  25.7 us (35%)
  Pallas kernels  8.84 us (12%)
    ppermute x7, waiting for transfers between devices, body(): lax.ppermute(blocks[k], 'samp', [(i, i ^ k) for i in range(owners)])  31.1 us
    ppermute x7, starting transfers between devices, body(): lax.ppermute(blocks[k], 'samp', [(i, i ^ k) for i in range(owners)])  15 us
    ppermute x7, starting transfers between devices, partners(): lax.ppermute(value, axis, [(i, i ^ mask) for i in range(size)])  10.7 us
    ppermute x7, waiting for transfers between devices, partners(): lax.ppermute(value, axis, [(i, i ^ mask) for i in range(size)])  7.31 us
    pallas_call x1, Pallas kernels, jac_rows(): pl.pallas_call(jac_kernel, in_specs=[hbm, hbm], out_shape=[jax.ShapeDtype...  3.57 us
    pallas_call x1, Pallas kernels, solve_and_project(): pl.pallas_call(functools.partial(solve_kernel, len(grams)), out_shape=(ja...  3.52 us
    pallas_call x1, Pallas kernels, gram_partial(): pl.pallas_call(gram_kernel, out_shape=jax.ShapeDtypeStruct(packed_shape(t...  1.52 us
  transfers between devices with their start and end apart: 14, of which 9 were waited for; matrix products, arithmetic and copies ran while one was open for 0% of the time, Pallas kernels for 0%

profile of v18, /device:TPU:0, one launch (start us, length us, event | category | flops | bytes accessed | tf_op | source)
XLA Modules:
  0.0 73.8 jit_solution(16286419282032133052)
XLA Ops:
  0.6 0.0 copy-start.1
  0.6 0.0 copy-start
  0.7 3.6 %jac_rows.1 = (bf16[8,64,256]{2,1,0:T(8,128)(2,1)S(1)}, bf16[8,64,256]{2,1,0:T(8,128)(2,1)S(1)}, bf16[8,64,256]{2,1,0:T(8,128)(2,1)S(1)}, bf16[8,64,256]{2,1,0:T...) custom-call(bf16[8,2,256,256]{3,2,1,0:T(8,128)(2,1)} %act_hbm.1, ...), custom_call_target="tpu_custom_call" | custom-call | flops 536870912 | bytes 6291456 | tf_op jit(solution)/shard_map/jac_rows/pallas_call | solution.py:90
  4.2 4.1 %collective-permute-start = (bf16[8,64,256]{2,1,0:T(8,128)(2,1)S(1)}, bf16[8,64,256]{2,1,0:T(8,128)(2,1)S(1)}, u32[]{:S(2)}, u32[]{:S(2)}) collective-permute-start(bf16[8,64,256]{2,1,0:T(8,128)(2,1)S(1)} %get-tuple-element.12), channel_id=1, source_target_pairs={{0,16},{4,20},{8,24},{12,28},{16,0},{20,4},{24,8},{28,12},{1,17},{... | collective-permute-start | bytes 786440 | tf_op jit(solution)/shard_map/ppermute | solution.py:375
  8.3 1.3 %collective-permute-start.1 = (bf16[8,64,256]{2,1,0:T(8,128)(2,1)S(1)}, bf16[8,64,256]{2,1,0:T(8,128)(2,1)S(1)}, u32[]{:S(2)}, u32[]{:S(2)}) collective-permute-start(bf16[8,64,256]{2,1,0:T(8,128)(2,1)S(1)} %get-tuple-element.13), channel_id=1, source_target_pairs={{0,20},{4,16},{8,28},{12,24},{16,4},{20,0},{24,12},{28,8},{1,21},{... | collective-permute-start | bytes 786440 | tf_op jit(solution)/shard_map/ppermute | solution.py:375
  9.6 1.5 %collective-permute-start.2 = (bf16[8,64,256]{2,1,0:T(8,128)(2,1)S(1)}, bf16[8,64,256]{2,1,0:T(8,128)(2,1)S(1)}, u32[]{:S(2)}, u32[]{:S(2)}) collective-permute-start(bf16[8,64,256]{2,1,0:T(8,128)(2,1)S(1)} %get-tuple-element.14), channel_id=1, source_target_pairs={{0,12},{4,8},{8,4},{12,0},{16,28},{20,24},{24,20},{28,16},{1,13},{... | collective-permute-start | bytes 786440 | tf_op jit(solution)/shard_map/ppermute | solution.py:375
  11.1 2.5 %collective-permute-start.3 = (bf16[8,64,256]{2,1,0:T(8,128)(2,1)S(1)}, bf16[8,64,256]{2,1,0:T(8,128)(2,1)S(1)}, u32[]{:S(2)}, u32[]{:S(2)}) collective-permute-start(bf16[8,64,256]{2,1,0:T(8,128)(2,1)S(1)} %get-tuple-element.15), channel_id=1, source_target_pairs={{0,24},{4,28},{8,16},{12,20},{16,8},{20,12},{24,0},{28,4},{1,25},{... | collective-permute-start | bytes 786440 | tf_op jit(solution)/shard_map/ppermute | solution.py:375
  13.6 0.7 collective-permute-start.4
  14.3 12.5 %collective-permute-done.refs_0_.refs_2_ = bf16[8,64,256]{2,1,0:T(8,128)(2,1)S(1)} collective-permute-done((bf16[8,64,256]{2,1,0:T(8,128)(2,1)S(1)}, bf16[8,64,256]{2,1,0:T(8,128)(2,1)S(1)}, u32[]{:S(2)}, u32[]{:S(2)}) %collective-permute-start) | collective-permute-done | bytes 262176 | tf_op jit(solution)/shard_map/ppermute | solution.py:375
  26.8 4.9 %collective-permute-start.5 = (bf16[8,64,256]{2,1,0:T(8,128)(2,1)}, bf16[8,64,256]{2,1,0:T(8,128)(2,1)S(1)}, u32[]{:S(2)}, u32[]{:S(2)}) collective-permute-start(bf16[8,64,256]{2,1,0:T(8,128)(2,1)} %get-tuple-element.17), channel_id=1, source_target_pairs={{0,28},{4,24},{8,20},{12,16},{16,12},{20,8},{24,4},{28,0},{1,29},{... | collective-permute-start | bytes 786440 | tf_op jit(solution)/shard_map/ppermute | solution.py:375
  31.7 7.7 %collective-permute-done.1.refs_1_.refs_3_ = bf16[8,64,256]{2,1,0:T(8,128)(2,1)S(1)} collective-permute-done((bf16[8,64,256]{2,1,0:T(8,128)(2,1)S(1)}, bf16[8,64,256]{2,1,0:T(8,128)(2,1)S(1)}, u32[]{:S(2)}, u32[]{:S(2)}) %collective-permute-start.1) | collective-permute-done | bytes 262176 | tf_op jit(solution)/shard_map/ppermute | solution.py:375
  39.4 0.0 collective-permute-start.6
  39.5 0.0 copy-done.1
  39.5 0.1 copy.6.offdiag_ref
  39.5 0.0 copy-done
  39.5 0.2 packed_energy.1.refs_8_
  39.8 0.0 collective-permute-done.2.refs_2_.refs_4_
  39.8 0.0 collective-permute-done.3.refs_3_.refs_5_
  39.8 0.0 collective-permute-done.4.refs_4_.refs_6_
  39.8 6.2 %collective-permute-done.5.refs_5_.refs_7_ = bf16[8,64,256]{2,1,0:T(8,128)(2,1)S(1)} collective-permute-done((bf16[8,64,256]{2,1,0:T(8,128)(2,1)}, bf16[8,64,256]{2,1,0:T(8,128)(2,1)S(1)}, u32[]{:S(2)}, u32[]{:S(2)}) %collective-permute-start.5) | collective-permute-done | bytes 262176 | tf_op jit(solution)/shard_map/ppermute | solution.py:375
  46.0 4.7 %collective-permute-done.6.refs_6_.refs_8_ = bf16[8,64,256]{2,1,0:T(8,128)(2,1)S(1)} collective-permute-done((bf16[8,64,256]{2,1,0:T(8,128)(2,1)S(1)}, bf16[8,64,256]{2,1,0:T(8,128)(2,1)S(1)}, u32[]{:S(2)}, u32[]{:S(2)}) %collective-permute-start.6) | collective-permute-done | bytes 262176 | tf_op jit(solution)/shard_map/ppermute | solution.py:375
  50.7 1.5 %gram_partial.1.refs_3_ = f32[32,128]{1,0:T(8,128)S(1)} custom-call(bf16[8,64,256]{2,1,0:T(8,128)(2,1)S(1)} %collective-permute-done.refs_0_.refs_2_, bf16[8,64,256]{2,1,0:T(8,128)(2,1)S(1)} %collective-permute-done.1.refs_1_.refs_3_, bf16[8,64,256]{2,1,0:T(8,128)(2,1)S(1)} %collective-permute-done.2.refs_2_.refs_4_, ...), custom_call_target="tpu_custom_call" | custom-call | flops 134217728 | bytes 2097152 | tf_op jit(solution)/shard_map/gram_partial/pallas_call | solution.py:181
  52.2 0.2 collective-permute-start.7
  52.4 1.4 %collective-permute-start.8 = (f32[32,128]{1,0:T(8,128)S(1)}, f32[32,128]{1,0:T(8,128)S(1)}, u32[]{:S(2)}, u32[]{:S(2)}) collective-permute-start(f32[32,128]{1,0:T(8,128)S(1)} %gram_partial.1.refs_3_), channel_id=1, source_target_pairs={{0,2},{1,3},{2,0},{3,1},{4,6},{5,7},{6,4},{7,5},{8,10},{9,11},{10,... | collective-permute-start | bytes 49160 | tf_op jit(solution)/shard_map/ppermute | solution.py:289
  53.8 0.3 collective-permute-start.9
  54.1 1.4 %collective-permute-done.7.refs_0_ = f32[32,128]{1,0:T(8,128)S(1)} collective-permute-done((f32[32,128]{1,0:T(8,128)S(1)}, f32[32,128]{1,0:T(8,128)S(1)}, u32[]{:S(2)}, u32[]{:S(2)}) %collective-permute-start.7) | collective-permute-done | bytes 16416 | tf_op jit(solution)/shard_map/ppermute | solution.py:289
  55.5 0.6 collective-permute-done.8.refs_1_
  56.2 0.0 collective-permute-done.9.refs_2_
  56.2 3.3 %collective-permute-start.10 = (f32[32,128]{1,0:T(8,128)S(1)}, f32[32,128]{1,0:T(8,128)S(1)}, u32[]{:S(2)}, u32[]{:S(2)}) collective-permute-start(f32[32,128]{1,0:T(8,128)S(1)} %sum_over.2.refs_3_), channel_id=1, source_target_pairs={{0,28},{4,24},{8,20},{12,16},{16,12},{20,8},{24,4},{28,0},{1,29},{... | collective-permute-start | bytes 49160 | tf_op jit(solution)/shard_map/ppermute | solution.py:289
  59.5 0.5 collective-permute-start.11
  60.0 1.5 %collective-permute-start.12 = (f32[32,128]{1,0:T(8,128)S(1)}, f32[32,128]{1,0:T(8,128)S(1)}, u32[]{:S(2)}, u32[]{:S(2)}) collective-permute-start(f32[32,128]{1,0:T(8,128)S(1)} %sum_over.2.refs_3_), channel_id=1, source_target_pairs={{0,4},{4,0},{8,12},{12,8},{16,20},{20,16},{24,28},{28,24},{1,5},{5... | collective-permute-start | bytes 49160 | tf_op jit(solution)/shard_map/ppermute | solution.py:289
  61.5 1.1 %collective-permute-done.10.refs_0_ = f32[32,128]{1,0:T(8,128)S(1)} collective-permute-done((f32[32,128]{1,0:T(8,128)S(1)}, f32[32,128]{1,0:T(8,128)S(1)}, u32[]{:S(2)}, u32[]{:S(2)}) %collective-permute-start.10) | collective-permute-done | bytes 16416 | tf_op jit(solution)/shard_map/ppermute | solution.py:289
  62.7 2.4 %collective-permute-done.11.refs_1_ = f32[32,128]{1,0:T(8,128)S(1)} collective-permute-done((f32[32,128]{1,0:T(8,128)S(1)}, f32[32,128]{1,0:T(8,128)S(1)}, u32[]{:S(2)}, u32[]{:S(2)}) %collective-permute-start.11) | collective-permute-done | bytes 16416 | tf_op jit(solution)/shard_map/ppermute | solution.py:289
  65.0 0.0 collective-permute-done.12.refs_2_
  65.1 3.5 %collective-permute-start.13 = (f32[32,128]{1,0:T(8,128)S(1)}, f32[32,128]{1,0:T(8,128)S(1)}, u32[]{:S(2)}, u32[]{:S(2)}) collective-permute-start(f32[32,128]{1,0:T(8,128)S(1)} %sum_over.3.refs_1_), channel_id=1, source_target_pairs={{0,8},{4,12},{8,0},{12,4},{16,24},{20,28},{24,16},{28,20},{1,9},{5... | collective-permute-start | bytes 49160 | tf_op jit(solution)/shard_map/ppermute | solution.py:289
  68.5 1.7 %collective-permute-done.13.refs_0_ = f32[32,128]{1,0:T(8,128)S(1)} collective-permute-done((f32[32,128]{1,0:T(8,128)S(1)}, f32[32,128]{1,0:T(8,128)S(1)}, u32[]{:S(2)}, u32[]{:S(2)}) %collective-permute-start.13) | collective-permute-done | bytes 16416 | tf_op jit(solution)/shard_map/ppermute | solution.py:289
  70.3 3.5 %solve_and_project.1 = (f32[1,8]{1,0:T(1,128)}, f32[2,32,256]{2,1,0:T(8,128)}) custom-call(f32[32,128]{1,0:T(8,128)S(1)} %collective-permute-done.13.refs_0_, f32[32,128]{1,0:T(8,128)S(1)} %sum_over.3.refs_1_, bf16[8,64,256]{2,1,0:T(8,128)(2,1)S(1)} %collective-permute-done.refs_0_.refs_2_, bf16[8,64,256]{2,1,0:T(8,128)(2,1)S(1)} %collective-permute-done.1.refs_1_.refs_3_, ...), custom_call_target="tpu_custom_call" | custom-call | tf_op jit(solution)/shard_map/solve_and_project/pallas_call | solution.py:357
  (2 shorter events, 0.0 us)
Async XLA Ops:
  0.6 38.8 %copy-start.1 = (f32[8]{0:T(128)S(1)}, f32[8]{0:T(128)}, u32[]{:S(2)}) copy-start(f32[8]{0:T(128)} %param.7) | copy-start | bytes 100
  0.6 38.9 %copy-start = (s32[8,256]{1,0:T(8,128)S(1)}, s32[8,256]{1,0:T(8,128)}, u32[]{:S(2)}) copy-start(s32[8,256]{1,0:T(8,128)} %spins_ref.1) | copy-start | bytes 24580
  4.2 22.6 %collective-permute-start = (bf16[8,64,256]{2,1,0:T(8,128)(2,1)S(1)}, bf16[8,64,256]{2,1,0:T(8,128)(2,1)S(1)}, u32[]{:S(2)}, u32[]{:S(2)}) collective-permute-start(bf16[8,64,256]{2,1,0:T(8,128)(2,1)S(1)} %get-tuple-element.12), channel_id=1, source_target_pairs={{0,16},{4,20},{8,24},{12,28},{16,0},{20,4},{24,8},{28,12},{1,17},{... | collective-permute-start | bytes 786440 | tf_op jit(solution)/shard_map/ppermute | solution.py:375
  8.3 31.1 %collective-permute-start.1 = (bf16[8,64,256]{2,1,0:T(8,128)(2,1)S(1)}, bf16[8,64,256]{2,1,0:T(8,128)(2,1)S(1)}, u32[]{:S(2)}, u32[]{:S(2)}) collective-permute-start(bf16[8,64,256]{2,1,0:T(8,128)(2,1)S(1)} %get-tuple-element.13), channel_id=1, source_target_pairs={{0,20},{4,16},{8,28},{12,24},{16,4},{20,0},{24,12},{28,8},{1,21},{... | collective-permute-start | bytes 786440 | tf_op jit(solution)/shard_map/ppermute | solution.py:375
  9.6 30.1 %collective-permute-start.2 = (bf16[8,64,256]{2,1,0:T(8,128)(2,1)S(1)}, bf16[8,64,256]{2,1,0:T(8,128)(2,1)S(1)}, u32[]{:S(2)}, u32[]{:S(2)}) collective-permute-start(bf16[8,64,256]{2,1,0:T(8,128)(2,1)S(1)} %get-tuple-element.14), channel_id=1, source_target_pairs={{0,12},{4,8},{8,4},{12,0},{16,28},{20,24},{24,20},{28,16},{1,13},{... | collective-permute-start | bytes 786440 | tf_op jit(solution)/shard_map/ppermute | solution.py:375
  11.1 28.6 %collective-permute-start.3 = (bf16[8,64,256]{2,1,0:T(8,128)(2,1)S(1)}, bf16[8,64,256]{2,1,0:T(8,128)(2,1)S(1)}, u32[]{:S(2)}, u32[]{:S(2)}) collective-permute-start(bf16[8,64,256]{2,1,0:T(8,128)(2,1)S(1)} %get-tuple-element.15), channel_id=1, source_target_pairs={{0,24},{4,28},{8,16},{12,20},{16,8},{20,12},{24,0},{28,4},{1,25},{... | collective-permute-start | bytes 786440 | tf_op jit(solution)/shard_map/ppermute | solution.py:375
  13.6 26.2 %collective-permute-start.4 = (bf16[8,64,256]{2,1,0:T(8,128)(2,1)S(1)}, bf16[8,64,256]{2,1,0:T(8,128)(2,1)S(1)}, u32[]{:S(2)}, u32[]{:S(2)}) collective-permute-start(bf16[8,64,256]{2,1,0:T(8,128)(2,1)S(1)} %get-tuple-element.16), channel_id=1, source_target_pairs={{0,8},{4,12},{8,0},{12,4},{16,24},{20,28},{24,16},{28,20},{1,9},{5... | collective-permute-start | bytes 786440 | tf_op jit(solution)/shard_map/ppermute | solution.py:375
  26.8 19.2 %collective-permute-start.5 = (bf16[8,64,256]{2,1,0:T(8,128)(2,1)}, bf16[8,64,256]{2,1,0:T(8,128)(2,1)S(1)}, u32[]{:S(2)}, u32[]{:S(2)}) collective-permute-start(bf16[8,64,256]{2,1,0:T(8,128)(2,1)} %get-tuple-element.17), channel_id=1, source_target_pairs={{0,28},{4,24},{8,20},{12,16},{16,12},{20,8},{24,4},{28,0},{1,29},{... | collective-permute-start | bytes 786440 | tf_op jit(solution)/shard_map/ppermute | solution.py:375
  39.4 11.2 %collective-permute-start.6 = (bf16[8,64,256]{2,1,0:T(8,128)(2,1)S(1)}, bf16[8,64,256]{2,1,0:T(8,128)(2,1)S(1)}, u32[]{:S(2)}, u32[]{:S(2)}) collective-permute-start(bf16[8,64,256]{2,1,0:T(8,128)(2,1)S(1)} %get-tuple-element.18), channel_id=1, source_target_pairs={{0,4},{4,0},{8,12},{12,8},{16,20},{20,16},{24,28},{28,24},{1,5},{5... | collective-permute-start | bytes 786440 | tf_op jit(solution)/shard_map/ppermute | solution.py:375
  52.2 3.3 %collective-permute-start.7 = (f32[32,128]{1,0:T(8,128)S(1)}, f32[32,128]{1,0:T(8,128)S(1)}, u32[]{:S(2)}, u32[]{:S(2)}) collective-permute-start(f32[32,128]{1,0:T(8,128)S(1)} %gram_partial.1.refs_3_), channel_id=1, source_target_pairs={{0,3},{1,2},{2,1},{3,0},{4,7},{5,6},{6,5},{7,4},{8,11},{9,10},{10,... | collective-permute-start | bytes 49160 | tf_op jit(solution)/shard_map/ppermute | solution.py:289
  52.4 3.7 %collective-permute-start.8 = (f32[32,128]{1,0:T(8,128)S(1)}, f32[32,128]{1,0:T(8,128)S(1)}, u32[]{:S(2)}, u32[]{:S(2)}) collective-permute-start(f32[32,128]{1,0:T(8,128)S(1)} %gram_partial.1.refs_3_), channel_id=1, source_target_pairs={{0,2},{1,3},{2,0},{3,1},{4,6},{5,7},{6,4},{7,5},{8,10},{9,11},{10,... | collective-permute-start | bytes 49160 | tf_op jit(solution)/shard_map/ppermute | solution.py:289
  53.8 2.4 %collective-permute-start.9 = (f32[32,128]{1,0:T(8,128)S(1)}, f32[32,128]{1,0:T(8,128)S(1)}, u32[]{:S(2)}, u32[]{:S(2)}) collective-permute-start(f32[32,128]{1,0:T(8,128)S(1)} %gram_partial.1.refs_3_), channel_id=1, source_target_pairs={{0,1},{1,0},{2,3},{3,2},{4,5},{5,4},{6,7},{7,6},{8,9},{9,8},{10,11... | collective-permute-start | bytes 49160 | tf_op jit(solution)/shard_map/ppermute | solution.py:289
  56.2 6.5 %collective-permute-start.10 = (f32[32,128]{1,0:T(8,128)S(1)}, f32[32,128]{1,0:T(8,128)S(1)}, u32[]{:S(2)}, u32[]{:S(2)}) collective-permute-start(f32[32,128]{1,0:T(8,128)S(1)} %sum_over.2.refs_3_), channel_id=1, source_target_pairs={{0,28},{4,24},{8,20},{12,16},{16,12},{20,8},{24,4},{28,0},{1,29},{... | collective-permute-start | bytes 49160 | tf_op jit(solution)/shard_map/ppermute | solution.py:289
  59.5 5.5 %collective-permute-start.11 = (f32[32,128]{1,0:T(8,128)S(1)}, f32[32,128]{1,0:T(8,128)S(1)}, u32[]{:S(2)}, u32[]{:S(2)}) collective-permute-start(f32[32,128]{1,0:T(8,128)S(1)} %sum_over.2.refs_3_), channel_id=1, source_target_pairs={{0,24},{4,28},{8,16},{12,20},{16,8},{20,12},{24,0},{28,4},{1,25},{... | collective-permute-start | bytes 49160 | tf_op jit(solution)/shard_map/ppermute | solution.py:289
  60.0 5.0 %collective-permute-start.12 = (f32[32,128]{1,0:T(8,128)S(1)}, f32[32,128]{1,0:T(8,128)S(1)}, u32[]{:S(2)}, u32[]{:S(2)}) collective-permute-start(f32[32,128]{1,0:T(8,128)S(1)} %sum_over.2.refs_3_), channel_id=1, source_target_pairs={{0,4},{4,0},{8,12},{12,8},{16,20},{20,16},{24,28},{28,24},{1,5},{5... | collective-permute-start | bytes 49160 | tf_op jit(solution)/shard_map/ppermute | solution.py:289
  65.1 5.2 %collective-permute-start.13 = (f32[32,128]{1,0:T(8,128)S(1)}, f32[32,128]{1,0:T(8,128)S(1)}, u32[]{:S(2)}, u32[]{:S(2)}) collective-permute-start(f32[32,128]{1,0:T(8,128)S(1)} %sum_over.3.refs_1_), channel_id=1, source_target_pairs={{0,8},{4,12},{8,0},{12,4},{16,24},{20,28},{24,16},{28,20},{1,9},{5... | collective-permute-start | bytes 49160 | tf_op jit(solution)/shard_map/ppermute | solution.py:289

commit v19 on v18

--- a/solution.py
+++ b/solution.py
@@ -311,7 +311,7 @@
     block_refs = in_place(block_refs)
     mats, share, d = update_ref.shape
     local = weights_ref.shape[1]
-    packed = tree_sum([ref[...] for ref in gram_refs[::-1]])
+    packed = tree_sum([gram_refs[0][i] for i in range(gram_refs[0].shape[0])])
     half, packed_width = packed.shape
     total = 2 * half
     width = (total // LANES + 1) * LANES
@@ -375,10 +375,8 @@
         blocks[k] = lax.ppermute(blocks[k], "samp", [(i, i ^ k) for i in range(owners)])
     partial = gram_partial(blocks, packed_energy(spins, offdiag, total))
     gram = sum_over(partial, "layer", list(range(1, lax.axis_size("layer"))))
-    *early, last = rounds(owners)
-    for masks in early:
-        gram = sum_over(gram, "samp", masks)
-    grams = partners(gram, "samp", last)
+    gathered = lax.all_gather(gram, "samp", axis=0)
+    grams = [gathered]
     weights, update = solve_and_project(grams, blocks, mats)
     return weights.reshape(local), update
 

time: 73.9 us -> 93.2 us (1.26)
  blocking collectives: 0 us -> 33.3 us
  starting transfers between devices: 25.7 us -> 16.9 us
  waiting for transfers between devices: 38.4 us -> 33.2 us
    all_gather x0 -> x1, blocking collectives: none -> 33.3 us  [body(): gathered = lax.all_gather(gram, 'samp', axis=0)]
    ppermute x7 -> x3, starting transfers between devices: 10.7 us -> 1.9 us  [partners(): lax.ppermute(value, axis, [(i, i ^ mask) for i in range(size)])]
    ppermute x7 -> x3, waiting for transfers between devices: 7.31 us -> 2.08 us  [partners(): lax.ppermute(value, axis, [(i, i ^ mask) for i in range(size)])]
  transfers between devices with their start and end apart: 14 -> 10, of which waited for: 9 -> 6; matrix products, arithmetic and copies ran while one was open for 0% -> 0% of each run, Pallas kernels for 0% -> 0%
where the time goes in v19:
time: 93.2 us; the launch traced here: 93 us
  blocking collectives  33.3 us (36%)
  waiting for transfers between devices  33.2 us (36%)
  starting transfers between devices  16.9 us (18%)
  Pallas kernels  8.84 us (9%)
    all_gather x1, blocking collectives, body(): gathered = lax.all_gather(gram, 'samp', axis=0)  33.3 us
    ppermute x7, waiting for transfers between devices, body(): lax.ppermute(blocks[k], 'samp', [(i, i ^ k) for i in range(owners)])  31.1 us
    ppermute x7, starting transfers between devices, body(): lax.ppermute(blocks[k], 'samp', [(i, i ^ k) for i in range(owners)])  15 us
    pallas_call x1, Pallas kernels, jac_rows(): pl.pallas_call(jac_kernel, in_specs=[hbm, hbm], out_shape=[jax.ShapeDtype...  3.58 us
    pallas_call x1, Pallas kernels, solve_and_project(): pl.pallas_call(functools.partial(solve_kernel, len(grams)), out_shape=(ja...  3.52 us
    ppermute x3, waiting for transfers between devices, partners(): lax.ppermute(value, axis, [(i, i ^ mask) for i in range(size)])  2.08 us
    ppermute x3, starting transfers between devices, partners(): lax.ppermute(value, axis, [(i, i ^ mask) for i in range(size)])  1.9 us
  transfers between devices with their start and end apart: 10, of which 6 were waited for; matrix products, arithmetic and copies ran while one was open for 0% of the time, Pallas kernels for 0%

profile of v19, /device:TPU:0, one launch (start us, length us, event | category | flops | bytes accessed | tf_op | source)
XLA Modules:
  0.0 93.0 jit_solution(2290407023642089434)
XLA Ops:
  0.6 0.0 copy-start.1
  0.6 0.0 copy-start
  0.7 3.6 %jac_rows.1 = (bf16[8,64,256]{2,1,0:T(8,128)(2,1)S(1)}, bf16[8,64,256]{2,1,0:T(8,128)(2,1)S(1)}, bf16[8,64,256]{2,1,0:T(8,128)(2,1)S(1)}, bf16[8,64,256]{2,1,0:T...) custom-call(bf16[8,2,256,256]{3,2,1,0:T(8,128)(2,1)} %act_hbm.1, ...), custom_call_target="tpu_custom_call" | custom-call | flops 536870912 | bytes 6291456 | tf_op jit(solution)/shard_map/jac_rows/pallas_call | solution.py:90
  4.2 4.1 %collective-permute-start = (bf16[8,64,256]{2,1,0:T(8,128)(2,1)S(1)}, bf16[8,64,256]{2,1,0:T(8,128)(2,1)S(1)}, u32[]{:S(2)}, u32[]{:S(2)}) collective-permute-start(bf16[8,64,256]{2,1,0:T(8,128)(2,1)S(1)} %get-tuple-element.12), channel_id=1, source_target_pairs={{0,16},{4,20},{8,24},{12,28},{16,0},{20,4},{24,8},{28,12},{1,17},{... | collective-permute-start | bytes 786440 | tf_op jit(solution)/shard_map/ppermute | solution.py:375
  8.3 1.3 %collective-permute-start.1 = (bf16[8,64,256]{2,1,0:T(8,128)(2,1)S(1)}, bf16[8,64,256]{2,1,0:T(8,128)(2,1)S(1)}, u32[]{:S(2)}, u32[]{:S(2)}) collective-permute-start(bf16[8,64,256]{2,1,0:T(8,128)(2,1)S(1)} %get-tuple-element.13), channel_id=1, source_target_pairs={{0,20},{4,16},{8,28},{12,24},{16,4},{20,0},{24,12},{28,8},{1,21},{... | collective-permute-start | bytes 786440 | tf_op jit(solution)/shard_map/ppermute | solution.py:375
  9.6 1.5 %collective-permute-start.2 = (bf16[8,64,256]{2,1,0:T(8,128)(2,1)S(1)}, bf16[8,64,256]{2,1,0:T(8,128)(2,1)S(1)}, u32[]{:S(2)}, u32[]{:S(2)}) collective-permute-start(bf16[8,64,256]{2,1,0:T(8,128)(2,1)S(1)} %get-tuple-element.14), channel_id=1, source_target_pairs={{0,12},{4,8},{8,4},{12,0},{16,28},{20,24},{24,20},{28,16},{1,13},{... | collective-permute-start | bytes 786440 | tf_op jit(solution)/shard_map/ppermute | solution.py:375
  11.2 2.5 %collective-permute-start.3 = (bf16[8,64,256]{2,1,0:T(8,128)(2,1)S(1)}, bf16[8,64,256]{2,1,0:T(8,128)(2,1)S(1)}, u32[]{:S(2)}, u32[]{:S(2)}) collective-permute-start(bf16[8,64,256]{2,1,0:T(8,128)(2,1)S(1)} %get-tuple-element.15), channel_id=1, source_target_pairs={{0,24},{4,28},{8,16},{12,20},{16,8},{20,12},{24,0},{28,4},{1,25},{... | collective-permute-start | bytes 786440 | tf_op jit(solution)/shard_map/ppermute | solution.py:375
  13.6 0.7 collective-permute-start.4
  14.3 12.5 %collective-permute-done.refs_0_.refs_1_ = bf16[8,64,256]{2,1,0:T(8,128)(2,1)S(1)} collective-permute-done((bf16[8,64,256]{2,1,0:T(8,128)(2,1)S(1)}, bf16[8,64,256]{2,1,0:T(8,128)(2,1)S(1)}, u32[]{:S(2)}, u32[]{:S(2)}) %collective-permute-start) | collective-permute-done | bytes 262176 | tf_op jit(solution)/shard_map/ppermute | solution.py:375
  26.8 4.9 %collective-permute-start.5 = (bf16[8,64,256]{2,1,0:T(8,128)(2,1)}, bf16[8,64,256]{2,1,0:T(8,128)(2,1)S(1)}, u32[]{:S(2)}, u32[]{:S(2)}) collective-permute-start(bf16[8,64,256]{2,1,0:T(8,128)(2,1)} %get-tuple-element.17), channel_id=1, source_target_pairs={{0,28},{4,24},{8,20},{12,16},{16,12},{20,8},{24,4},{28,0},{1,29},{... | collective-permute-start | bytes 786440 | tf_op jit(solution)/shard_map/ppermute | solution.py:375
  31.7 7.7 %collective-permute-done.1.refs_1_.refs_2_ = bf16[8,64,256]{2,1,0:T(8,128)(2,1)S(1)} collective-permute-done((bf16[8,64,256]{2,1,0:T(8,128)(2,1)S(1)}, bf16[8,64,256]{2,1,0:T(8,128)(2,1)S(1)}, u32[]{:S(2)}, u32[]{:S(2)}) %collective-permute-start.1) | collective-permute-done | bytes 262176 | tf_op jit(solution)/shard_map/ppermute | solution.py:375
  39.5 0.0 collective-permute-start.6
  39.5 0.0 copy-done.1
  39.5 0.1 copy.6.offdiag_ref
  39.5 0.0 copy-done
  39.5 0.2 packed_energy.1.refs_8_
  39.8 0.0 collective-permute-done.2.refs_2_.refs_3_
  39.8 0.0 collective-permute-done.3.refs_3_.refs_4_
  39.8 0.0 collective-permute-done.4.refs_4_.refs_5_
  39.8 6.2 %collective-permute-done.5.refs_5_.refs_6_ = bf16[8,64,256]{2,1,0:T(8,128)(2,1)S(1)} collective-permute-done((bf16[8,64,256]{2,1,0:T(8,128)(2,1)}, bf16[8,64,256]{2,1,0:T(8,128)(2,1)S(1)}, u32[]{:S(2)}, u32[]{:S(2)}) %collective-permute-start.5) | collective-permute-done | bytes 262176 | tf_op jit(solution)/shard_map/ppermute | solution.py:375
  46.0 4.7 %collective-permute-done.6.refs_6_.refs_7_ = bf16[8,64,256]{2,1,0:T(8,128)(2,1)S(1)} collective-permute-done((bf16[8,64,256]{2,1,0:T(8,128)(2,1)S(1)}, bf16[8,64,256]{2,1,0:T(8,128)(2,1)S(1)}, u32[]{:S(2)}, u32[]{:S(2)}) %collective-permute-start.6) | collective-permute-done | bytes 262176 | tf_op jit(solution)/shard_map/ppermute | solution.py:375
  50.7 1.5 %gram_partial.1.refs_3_ = f32[32,128]{1,0:T(8,128)S(1)} custom-call(bf16[8,64,256]{2,1,0:T(8,128)(2,1)S(1)} %collective-permute-done.refs_0_.refs_1_, bf16[8,64,256]{2,1,0:T(8,128)(2,1)S(1)} %collective-permute-done.1.refs_1_.refs_2_, bf16[8,64,256]{2,1,0:T(8,128)(2,1)S(1)} %collective-permute-done.2.refs_2_.refs_3_, ...), custom_call_target="tpu_custom_call" | custom-call | flops 134217728 | bytes 2097152 | tf_op jit(solution)/shard_map/gram_partial/pallas_call | solution.py:181
  52.2 0.2 collective-permute-start.7
  52.4 1.4 %collective-permute-start.8 = (f32[32,128]{1,0:T(8,128)S(1)}, f32[32,128]{1,0:T(8,128)S(1)}, u32[]{:S(2)}, u32[]{:S(2)}) collective-permute-start(f32[32,128]{1,0:T(8,128)S(1)} %gram_partial.1.refs_3_), channel_id=1, source_target_pairs={{0,2},{1,3},{2,0},{3,1},{4,6},{5,7},{6,4},{7,5},{8,10},{9,11},{10,... | collective-permute-start | bytes 49160 | tf_op jit(solution)/shard_map/ppermute | solution.py:289
  53.8 0.3 collective-permute-start.9
  54.1 1.4 %collective-permute-done.7.refs_0_ = f32[32,128]{1,0:T(8,128)S(1)} collective-permute-done((f32[32,128]{1,0:T(8,128)S(1)}, f32[32,128]{1,0:T(8,128)S(1)}, u32[]{:S(2)}, u32[]{:S(2)}) %collective-permute-start.7) | collective-permute-done | bytes 16416 | tf_op jit(solution)/shard_map/ppermute | solution.py:289
  55.5 0.6 collective-permute-done.8.refs_1_
  56.2 0.0 collective-permute-done.9.refs_2_
  56.2 33.3 %all-gather = f32[256,128]{1,0:T(8,128)S(1)} all-gather(f32[32,128]{1,0:T(8,128)S(1)} %sum_over.1), channel_id=2, replica_groups=mesh['samp'=8,'layer'=4] {'samp'}, dimensions={0}, use_global_device_ids=true | all-gather | bytes 147456 | tf_op jit(solution)/shard_map/all_gather | solution.py:378
  89.5 3.5 %solve_and_project.1 = (f32[1,8]{1,0:T(1,128)}, f32[2,32,256]{2,1,0:T(8,128)}) custom-call(f32[8,32,128]{2,1,0:T(8,128)S(1)} %bitcast.3, bf16[8,64,256]{2,1,0:T(8,128)(2,1)S(1)} %collective-permute-done.refs_0_.refs_1_, bf16[8,64,256]{2,1,0:T(8,128)(2,1)S(1)} %collective-permute-done.1.refs_1_.refs_2_, ...), custom_call_target="tpu_custom_call" | custom-call | tf_op jit(solution)/shard_map/solve_and_project/pallas_call | solution.py:357
  (1 shorter events, 0.0 us)
Async XLA Ops:
  0.6 38.8 %copy-start.1 = (f32[8]{0:T(128)S(1)}, f32[8]{0:T(128)}, u32[]{:S(2)}) copy-start(f32[8]{0:T(128)} %param.7) | copy-start | bytes 100
  0.6 38.9 %copy-start = (s32[8,256]{1,0:T(8,128)S(1)}, s32[8,256]{1,0:T(8,128)}, u32[]{:S(2)}) copy-start(s32[8,256]{1,0:T(8,128)} %spins_ref.1) | copy-start | bytes 24580
  4.2 22.6 %collective-permute-start = (bf16[8,64,256]{2,1,0:T(8,128)(2,1)S(1)}, bf16[8,64,256]{2,1,0:T(8,128)(2,1)S(1)}, u32[]{:S(2)}, u32[]{:S(2)}) collective-permute-start(bf16[8,64,256]{2,1,0:T(8,128)(2,1)S(1)} %get-tuple-element.12), channel_id=1, source_target_pairs={{0,16},{4,20},{8,24},{12,28},{16,0},{20,4},{24,8},{28,12},{1,17},{... | collective-permute-start | bytes 786440 | tf_op jit(solution)/shard_map/ppermute | solution.py:375
  8.3 31.1 %collective-permute-start.1 = (bf16[8,64,256]{2,1,0:T(8,128)(2,1)S(1)}, bf16[8,64,256]{2,1,0:T(8,128)(2,1)S(1)}, u32[]{:S(2)}, u32[]{:S(2)}) collective-permute-start(bf16[8,64,256]{2,1,0:T(8,128)(2,1)S(1)} %get-tuple-element.13), channel_id=1, source_target_pairs={{0,20},{4,16},{8,28},{12,24},{16,4},{20,0},{24,12},{28,8},{1,21},{... | collective-permute-start | bytes 786440 | tf_op jit(solution)/shard_map/ppermute | solution.py:375
  9.6 30.1 %collective-permute-start.2 = (bf16[8,64,256]{2,1,0:T(8,128)(2,1)S(1)}, bf16[8,64,256]{2,1,0:T(8,128)(2,1)S(1)}, u32[]{:S(2)}, u32[]{:S(2)}) collective-permute-start(bf16[8,64,256]{2,1,0:T(8,128)(2,1)S(1)} %get-tuple-element.14), channel_id=1, source_target_pairs={{0,12},{4,8},{8,4},{12,0},{16,28},{20,24},{24,20},{28,16},{1,13},{... | collective-permute-start | bytes 786440 | tf_op jit(solution)/shard_map/ppermute | solution.py:375
  11.2 28.6 %collective-permute-start.3 = (bf16[8,64,256]{2,1,0:T(8,128)(2,1)S(1)}, bf16[8,64,256]{2,1,0:T(8,128)(2,1)S(1)}, u32[]{:S(2)}, u32[]{:S(2)}) collective-permute-start(bf16[8,64,256]{2,1,0:T(8,128)(2,1)S(1)} %get-tuple-element.15), channel_id=1, source_target_pairs={{0,24},{4,28},{8,16},{12,20},{16,8},{20,12},{24,0},{28,4},{1,25},{... | collective-permute-start | bytes 786440 | tf_op jit(solution)/shard_map/ppermute | solution.py:375
  13.6 26.2 %collective-permute-start.4 = (bf16[8,64,256]{2,1,0:T(8,128)(2,1)S(1)}, bf16[8,64,256]{2,1,0:T(8,128)(2,1)S(1)}, u32[]{:S(2)}, u32[]{:S(2)}) collective-permute-start(bf16[8,64,256]{2,1,0:T(8,128)(2,1)S(1)} %get-tuple-element.16), channel_id=1, source_target_pairs={{0,8},{4,12},{8,0},{12,4},{16,24},{20,28},{24,16},{28,20},{1,9},{5... | collective-permute-start | bytes 786440 | tf_op jit(solution)/shard_map/ppermute | solution.py:375
  26.8 19.2 %collective-permute-start.5 = (bf16[8,64,256]{2,1,0:T(8,128)(2,1)}, bf16[8,64,256]{2,1,0:T(8,128)(2,1)S(1)}, u32[]{:S(2)}, u32[]{:S(2)}) collective-permute-start(bf16[8,64,256]{2,1,0:T(8,128)(2,1)} %get-tuple-element.17), channel_id=1, source_target_pairs={{0,28},{4,24},{8,20},{12,16},{16,12},{20,8},{24,4},{28,0},{1,29},{... | collective-permute-start | bytes 786440 | tf_op jit(solution)/shard_map/ppermute | solution.py:375
  39.5 11.2 %collective-permute-start.6 = (bf16[8,64,256]{2,1,0:T(8,128)(2,1)S(1)}, bf16[8,64,256]{2,1,0:T(8,128)(2,1)S(1)}, u32[]{:S(2)}, u32[]{:S(2)}) collective-permute-start(bf16[8,64,256]{2,1,0:T(8,128)(2,1)S(1)} %get-tuple-element.18), channel_id=1, source_target_pairs={{0,4},{4,0},{8,12},{12,8},{16,20},{20,16},{24,28},{28,24},{1,5},{5... | collective-permute-start | bytes 786440 | tf_op jit(solution)/shard_map/ppermute | solution.py:375
  52.2 3.3 %collective-permute-start.7 = (f32[32,128]{1,0:T(8,128)S(1)}, f32[32,128]{1,0:T(8,128)S(1)}, u32[]{:S(2)}, u32[]{:S(2)}) collective-permute-start(f32[32,128]{1,0:T(8,128)S(1)} %gram_partial.1.refs_3_), channel_id=1, source_target_pairs={{0,3},{1,2},{2,1},{3,0},{4,7},{5,6},{6,5},{7,4},{8,11},{9,10},{10,... | collective-permute-start | bytes 49160 | tf_op jit(solution)/shard_map/ppermute | solution.py:289
  52.4 3.7 %collective-permute-start.8 = (f32[32,128]{1,0:T(8,128)S(1)}, f32[32,128]{1,0:T(8,128)S(1)}, u32[]{:S(2)}, u32[]{:S(2)}) collective-permute-start(f32[32,128]{1,0:T(8,128)S(1)} %gram_partial.1.refs_3_), channel_id=1, source_target_pairs={{0,2},{1,3},{2,0},{3,1},{4,6},{5,7},{6,4},{7,5},{8,10},{9,11},{10,... | collective-permute-start | bytes 49160 | tf_op jit(solution)/shard_map/ppermute | solution.py:289
  53.8 2.4 %collective-permute-start.9 = (f32[32,128]{1,0:T(8,128)S(1)}, f32[32,128]{1,0:T(8,128)S(1)}, u32[]{:S(2)}, u32[]{:S(2)}) collective-permute-start(f32[32,128]{1,0:T(8,128)S(1)} %gram_partial.1.refs_3_), channel_id=1, source_target_pairs={{0,1},{1,0},{2,3},{3,2},{4,5},{5,4},{6,7},{7,6},{8,9},{9,8},{10,11... | collective-permute-start | bytes 49160 | tf_op jit(solution)/shard_map/ppermute | solution.py:289

commit v20 on v18

--- a/solution.py
+++ b/solution.py
@@ -22,47 +22,61 @@
     return lax.broadcasted_iota(jnp.int32, shape, dim)
 
 
-def turns(owners):
+def turns(owners, split):
     far, near = list(range(owners // 2, owners)), list(range(owners // 2 - 1, 0, -1))
-    order = [far.pop(0)]
+    cut = split_partners(owners, split)
+    order = [(k, part) for part in range(split) for k in cut]
+    far = [k for k in far if k not in cut]
     while far or near:
-        order += far[:1] + near[:1]
+        order += [(k, 0) for k in near[:1] + far[:1]]
         far, near = far[1:], near[1:]
-    return order + [0]
-
-
-def in_turn(blocks):
-    return [blocks[k] for k in turns(len(blocks))]
-
-
-def in_place(blocks):
-    order = turns(len(blocks))
-    return [blocks[order.index(k)] for k in range(len(blocks))]
-
-
-def jac_kernel(act_hbm, cot_hbm, *refs):
+    return order + [(0, 0)]
+
+
+def split_partners(owners, split):
+    return [owners // 2, owners // 2 + 1] if split > 1 else []
+
+
+def in_turn(blocks, split):
+    return [blocks[k][part] for k, part in turns(len(blocks), split)]
+
+
+def in_place(refs, owners):
+    split = 1 + (len(refs) > owners)
+    blocks = [[] for _ in range(owners)]
+    for (k, _), ref in zip(turns(owners, split), refs):
+        blocks[k].append(ref)
+    return blocks
+
+
+def jac_kernel(first_mat, joined, act_hbm, cot_hbm, *refs):
+    before, refs = refs[: len(joined)], refs[len(joined) :]
     *out_refs, act_buf, cot_buf, held, sems = refs
-    samples, mats = act_buf.shape[:2]
-    share = out_refs[0].shape[1] // mats
+    samples, mats, _, d = held.shape
+    share = d // len(out_refs)
     me = lax.axis_index("samp")
     copies = []
     for s in range(samples):
+        here = (s, pl.ds(first_mat, mats))
         copies.append(
             (
-                pltpu.make_async_copy(act_hbm.at[s], act_buf.at[s], sems.at[0, s]),
-                pltpu.make_async_copy(cot_hbm.at[s], cot_buf.at[s], sems.at[1, s]),
+                pltpu.make_async_copy(act_hbm.at[here], act_buf.at[s], sems.at[0, s]),
+                pltpu.make_async_copy(cot_hbm.at[here], cot_buf.at[s], sems.at[1, s]),
             )
         )
     for pair in copies:
         for copy in pair:
             copy.start()
+    for k, ref in zip(joined, before):
+        out_refs[k][:, : ref.shape[1]] = ref[...]
 
     def share_out(samples):
         for k, out_ref in enumerate(out_refs):
             owned = pl.ds(pl.multiple_of((me ^ k) * share, share), share)
             for s in samples:
                 rows = [held[s, m, owned] for m in range(mats)]
-                out_ref[s] = jnp.concatenate(rows, axis=0).astype(BF16)
+                rows = jnp.concatenate(rows, axis=0).astype(BF16)
+                out_ref[s, out_ref.shape[1] - mats * share :] = rows
 
     group = 2
     for first in range(0, samples, group):
@@ -83,14 +97,18 @@
     share_out(range(samples - group, samples))
 
 
-def jac_rows(activations, cotangents, owners):
+def jac_rows(activations, cotangents, owners, part, split, before=()):
     samples, mats, sites, d = activations.shape
+    mats //= split
     rows = mats * d // owners
+    joined = [k for k, block in enumerate(before) if block is not None]
+    out_rows = [rows + (before[k].shape[1] if k in joined else 0) for k in range(owners)]
     hbm = pl.BlockSpec(memory_space=pltpu.HBM)
+    vmem = pl.BlockSpec(memory_space=pltpu.VMEM)
     return pl.pallas_call(
-        jac_kernel,
-        in_specs=[hbm, hbm],
-        out_shape=[jax.ShapeDtypeStruct((samples, rows, d), BF16)] * owners,
+        functools.partial(jac_kernel, part * mats, joined),
+        in_specs=[hbm, hbm] + [vmem] * len(joined),
+        out_shape=[jax.ShapeDtypeStruct((samples, count, d), BF16) for count in out_rows],
         scratch_shapes=[
             pltpu.VMEM((samples, mats, sites, d), BF16),
             pltpu.VMEM((samples, mats, sites, d), BF16),
@@ -104,7 +122,19 @@
             transcendentals=0,
         ),
         name="jac_rows",
-    )(activations, cotangents)
+    )(activations, cotangents, *[before[k] for k in joined])
+
+
+def jac_blocks(activations, cotangents, owners):
+    mats, d = activations.shape[1], activations.shape[3]
+    split = mats if mats == 2 and d // owners % CHUNK == 0 else 1
+    blocks = [[block] for block in jac_rows(activations, cotangents, owners, 0, split)]
+    if split > 1:
+        cut = split_partners(owners, split)
+        before = [None if k in cut else block[0] for k, block in enumerate(blocks)]
+        later = jac_rows(activations, cotangents, owners, 1, split, before)
+        blocks = [b + [new] if k in cut else [new] for k, (b, new) in enumerate(zip(blocks, later))]
+    return blocks, split
 
 
 def packed_shape(total):
@@ -143,11 +173,18 @@
     )(spins, offdiag[:, None])
 
 
-def gram_kernel(*refs):
+def rows_of(parts, row, rows):
+    for ref in parts:
+        if row < ref.shape[1]:
+            return ref[:, row : row + rows]
+        row -= ref.shape[1]
+
+
+def gram_kernel(owners, *refs):
     *block_refs, energy_ref, out_ref, flat, whole = refs
-    block_refs = in_place(block_refs)
-    local, count, d = block_refs[0].shape
-    total = local * len(block_refs)
+    blocks = in_place(block_refs, owners)
+    local, count, d = blocks[0][0].shape
+    total = local * owners
     joined = CHUNK // local
     me = lax.axis_index("samp")
     block = CHUNK * CHUNK
@@ -157,8 +194,8 @@
     source = sample * CHUNK + dest // CHUNK
     swap = (iota((block, block), 1) == source).astype(F32).astype(BF16)
     for row in range(0, count, CHUNK):
-        for j in range(len(block_refs) // joined):
-            pieces = [ref[:, row : row + CHUNK] for ref in block_refs[j * joined : (j + 1) * joined]]
+        for j in range(owners // joined):
+            pieces = [rows_of(p, row, CHUNK) for p in blocks[j * joined : (j + 1) * joined]]
             piece = jnp.concatenate(pieces, axis=0).reshape(block, d)
             turned = jnp.dot(swap, piece, preferred_element_type=F32).astype(BF16)
             place = pl.ds(pl.multiple_of((me // joined ^ j) * CHUNK, CHUNK), CHUNK)
@@ -175,11 +212,11 @@
     out_ref[...] = jnp.where(lane < half, whole[:half], packed)
 
 
-def gram_partial(blocks, energies):
-    local, count, d = blocks[0].shape
+def gram_partial(blocks, split, energies):
+    local, count, d = blocks[0][0].shape
     total = local * len(blocks)
     return pl.pallas_call(
-        gram_kernel,
+        functools.partial(gram_kernel, len(blocks)),
         out_shape=jax.ShapeDtypeStruct(packed_shape(total), F32),
         scratch_shapes=[
             pltpu.VMEM((count, total, d), BF16),
@@ -192,7 +229,7 @@
             transcendentals=0,
         ),
         name="gram_partial",
-    )(*in_turn(blocks), energies)
+    )(*in_turn(blocks, split), energies)
 
 
 def tree_sum(parts):
@@ -306,9 +343,9 @@
     ]
 
 
-def solve_kernel(grams, *refs):
+def solve_kernel(grams, owners, *refs):
     gram_refs, (*block_refs, weights_ref, update_ref, held) = refs[:grams], refs[grams:]
-    block_refs = in_place(block_refs)
+    blocks = in_place(block_refs, owners)
     mats, share, d = update_ref.shape
     local = weights_ref.shape[1]
     packed = tree_sum([ref[...] for ref in gram_refs[::-1]])
@@ -343,19 +380,20 @@
     coeffs = weights - jnp.sum(weights, axis=0, keepdims=True) * scale
     held[...] = jnp.broadcast_to(coeffs, (total, d))
     acc = jnp.zeros((mats * share, d), F32)
-    for k, block_ref in enumerate(block_refs):
+    for k, parts in enumerate(blocks):
         mine = held[pl.ds(pl.multiple_of((me ^ k) * local, local), local)]
         for s in range(local):
-            acc = acc + mine[s : s + 1] * block_ref[s].astype(F32)
+            rows = jnp.concatenate([ref[s].astype(F32) for ref in parts], axis=0)
+            acc = acc + mine[s : s + 1] * rows
     for m in range(mats):
         update_ref[m] = acc[m * share : (m + 1) * share]
 
 
-def solve_and_project(grams, blocks, mats):
-    local, count, d = blocks[0].shape
+def solve_and_project(grams, blocks, split, mats):
+    local, count, d = blocks[0][0].shape
     total = local * len(blocks)
     return pl.pallas_call(
-        functools.partial(solve_kernel, len(grams)),
+        functools.partial(solve_kernel, len(grams), len(blocks)),
         out_shape=(
             jax.ShapeDtypeStruct((1, local), F32),
             jax.ShapeDtypeStruct((mats, count // mats, d), F32),
@@ -363,23 +401,24 @@
         scratch_shapes=[pltpu.VMEM((total, d), F32)],
         compiler_params=pltpu.CompilerParams(vmem_limit_bytes=VMEM_LIMIT),
         name="solve_and_project",
-    )(*grams, *in_turn(blocks))
+    )(*grams, *in_turn(blocks, split))
 
 
 def body(spins, activations, cotangents, offdiag):
     local, mats = activations.shape[:2]
     owners = lax.axis_size("samp")
     total = local * owners
-    blocks = list(jac_rows(activations, cotangents, owners))
-    for k in turns(owners)[:-1]:
-        blocks[k] = lax.ppermute(blocks[k], "samp", [(i, i ^ k) for i in range(owners)])
-    partial = gram_partial(blocks, packed_energy(spins, offdiag, total))
+    blocks, split = jac_blocks(activations, cotangents, owners)
+    for k, part in turns(owners, split)[:-1]:
+        perm = [(i, i ^ k) for i in range(owners)]
+        blocks[k][part] = lax.ppermute(blocks[k][part], "samp", perm)
+    partial = gram_partial(blocks, split, packed_energy(spins, offdiag, total))
     gram = sum_over(partial, "layer", list(range(1, lax.axis_size("layer"))))
     *early, last = rounds(owners)
     for masks in early:
         gram = sum_over(gram, "samp", masks)
     grams = partners(gram, "samp", last)
-    weights, update = solve_and_project(grams, blocks, mats)
+    weights, update = solve_and_project(grams, blocks, split, mats)
     return weights.reshape(local), update
 
 

time: 73.9 us -> 74.7 us (1.011)
  Pallas kernels: 8.84 us -> 11 us
  waiting for transfers between devices: 38.4 us -> 36.4 us
    ppermute x7 -> x9, waiting for transfers between devices: 31.1 us -> 25.4 us  [body(): blocks[k][part] = lax.ppermute(blocks[k][part], 'samp', perm)]
    ppermute x7, waiting for transfers between devices: 7.31 us -> 10.9 us  [partners(): lax.ppermute(value, axis, [(i, i ^ mask) for i in range(size)])]
    ppermute x7 -> x9, starting transfers between devices: 15 us -> 18.3 us  [body(): blocks[k][part] = lax.ppermute(blocks[k][part], 'samp', perm)]
    ppermute x7, starting transfers between devices: 10.7 us -> 8 us  [partners(): lax.ppermute(value, axis, [(i, i ^ mask) for i in range(size)])]
    pallas_call x3 -> x4, Pallas kernels: 8.61 us -> 10.8 us  [the longest x2 5.74 us: jac_rows(): pl.pallas_call(functools.partial(jac_kernel, part * mats, joined), in_spe...]
  transfers between devices with their start and end apart: 14 -> 16, of which waited for: 9 -> 12; matrix products, arithmetic and copies ran while one was open for 0% -> 0% of each run, Pallas kernels for 0% -> 5%
where the time goes in v20:
time: 74.7 us; the launch traced here: 74.5 us
  waiting for transfers between devices  36.4 us (49%)
  starting transfers between devices  26.3 us (35%)
  Pallas kernels  11 us (15%)
    ppermute x9, waiting for transfers between devices, body(): blocks[k][part] = lax.ppermute(blocks[k][part], 'samp', perm)  25.4 us
    ppermute x9, starting transfers between devices, body(): blocks[k][part] = lax.ppermute(blocks[k][part], 'samp', perm)  18.3 us
    ppermute x7, waiting for transfers between devices, partners(): lax.ppermute(value, axis, [(i, i ^ mask) for i in range(size)])  10.9 us
    ppermute x7, starting transfers between devices, partners(): lax.ppermute(value, axis, [(i, i ^ mask) for i in range(size)])  8 us
    pallas_call x2, Pallas kernels, jac_rows(): pl.pallas_call(functools.partial(jac_kernel, part * mats, joined), in_spe...  5.74 us
    pallas_call x1, Pallas kernels, solve_and_project(): pl.pallas_call(functools.partial(solve_kernel, len(grams), len(blocks)),...  3.52 us
    pallas_call x1, Pallas kernels, gram_partial(): pl.pallas_call(functools.partial(gram_kernel, len(blocks)), out_shape=jax...  1.51 us
  transfers between devices with their start and end apart: 16, of which 12 were waited for; matrix products, arithmetic and copies ran while one was open for 0% of the time, Pallas kernels for 5%

profile of v20, /device:TPU:0, one launch (start us, length us, event | category | flops | bytes accessed | tf_op | source)
XLA Modules:
  0.0 74.5 jit_solution(11979336994604517310)
XLA Ops:
  0.6 2.4 %jac_rows.2 = (bf16[8,32,256]{2,1,0:T(8,128)(2,1)S(1)}, bf16[8,32,256]{2,1,0:T(8,128)(2,1)S(1)}, bf16[8,32,256]{2,1,0:T(8,128)(2,1)S(1)}, bf16[8,32,256]{2,1,0:T...) custom-call(bf16[8,2,256,256]{3,2,1,0:T(8,128)(2,1)} %act_hbm.3, ...), custom_call_target="tpu_custom_call" | custom-call | flops 268435456 | bytes 3145728 | tf_op jit(solution)/shard_map/jac_rows/pallas_call | solution.py:108
  3.1 4.1 %collective-permute-start = (bf16[8,32,256]{2,1,0:T(8,128)(2,1)S(1)}, bf16[8,32,256]{2,1,0:T(8,128)(2,1)S(1)}, u32[]{:S(2)}, u32[]{:S(2)}) collective-permute-start(bf16[8,32,256]{2,1,0:T(8,128)(2,1)S(1)} %get-tuple-element.20), channel_id=1, source_target_pairs={{0,16},{4,20},{8,24},{12,28},{16,0},{20,4},{24,8},{28,12},{1,17},{... | collective-permute-start | bytes 393224 | tf_op jit(solution)/shard_map/ppermute | solution.py:414
  7.2 1.3 %collective-permute-start.1 = (bf16[8,32,256]{2,1,0:T(8,128)(2,1)S(1)}, bf16[8,32,256]{2,1,0:T(8,128)(2,1)S(1)}, u32[]{:S(2)}, u32[]{:S(2)}) collective-permute-start(bf16[8,32,256]{2,1,0:T(8,128)(2,1)S(1)} %get-tuple-element.21), channel_id=1, source_target_pairs={{0,20},{4,16},{8,28},{12,24},{16,4},{20,0},{24,12},{28,8},{1,21},{... | collective-permute-start | bytes 393224 | tf_op jit(solution)/shard_map/ppermute | solution.py:414
  8.4 0.0 copy-start.1
  8.4 0.0 copy-start
  8.5 3.3 %jac_rows.3 = (bf16[8,64,256]{2,1,0:T(8,128)(2,1)S(1)}, bf16[8,64,256]{2,1,0:T(8,128)(2,1)S(1)}, bf16[8,64,256]{2,1,0:T(8,128)(2,1)S(1)}, bf16[8,64,256]{2,1,0:T...) custom-call(bf16[8,2,256,256]{3,2,1,0:T(8,128)(2,1)} %act_hbm.3, ...), custom_call_target="tpu_custom_call" | custom-call | flops 268435456 | bytes 3145728 | tf_op jit(solution)/shard_map/jac_rows/pallas_call | solution.py:108
  11.8 2.7 %collective-permute-start.2 = (bf16[8,32,256]{2,1,0:T(8,128)(2,1)S(1)}, bf16[8,32,256]{2,1,0:T(8,128)(2,1)S(1)}, u32[]{:S(2)}, u32[]{:S(2)}) collective-permute-start(bf16[8,32,256]{2,1,0:T(8,128)(2,1)S(1)} %get-tuple-element.28), channel_id=1, source_target_pairs={{0,16},{4,20},{8,24},{12,28},{16,0},{20,4},{24,8},{28,12},{1,17},{... | collective-permute-start | bytes 393224 | tf_op jit(solution)/shard_map/ppermute | solution.py:414
  14.4 0.0 collective-permute-start.3
  14.5 2.8 %collective-permute-start.4 = (bf16[8,64,256]{2,1,0:T(8,128)(2,1)}, bf16[8,64,256]{2,1,0:T(8,128)(2,1)S(1)}, u32[]{:S(2)}, u32[]{:S(2)}) collective-permute-start(bf16[8,64,256]{2,1,0:T(8,128)(2,1)} %get-tuple-element.30), channel_id=1, source_target_pairs={{0,12},{4,8},{8,4},{12,0},{16,28},{20,24},{24,20},{28,16},{1,13},{... | collective-permute-start | bytes 786440 | tf_op jit(solution)/shard_map/ppermute | solution.py:414
  17.3 5.4 %collective-permute-done.refs_0_.refs_2_ = bf16[8,32,256]{2,1,0:T(8,128)(2,1)S(1)} collective-permute-done((bf16[8,32,256]{2,1,0:T(8,128)(2,1)S(1)}, bf16[8,32,256]{2,1,0:T(8,128)(2,1)S(1)}, u32[]{:S(2)}, u32[]{:S(2)}) %collective-permute-start) | collective-permute-done | bytes 131104 | tf_op jit(solution)/shard_map/ppermute | solution.py:414
  22.7 2.9 %collective-permute-start.5 = (bf16[8,64,256]{2,1,0:T(8,128)(2,1)}, bf16[8,64,256]{2,1,0:T(8,128)(2,1)S(1)}, u32[]{:S(2)}, u32[]{:S(2)}) collective-permute-start(bf16[8,64,256]{2,1,0:T(8,128)(2,1)} %get-tuple-element.31), channel_id=1, source_target_pairs={{0,24},{4,28},{8,16},{12,20},{16,8},{20,12},{24,0},{28,4},{1,25},{... | collective-permute-start | bytes 786440 | tf_op jit(solution)/shard_map/ppermute | solution.py:414
  25.6 1.2 %collective-permute-done.1.refs_1_.refs_3_ = bf16[8,32,256]{2,1,0:T(8,128)(2,1)S(1)} collective-permute-done((bf16[8,32,256]{2,1,0:T(8,128)(2,1)S(1)}, bf16[8,32,256]{2,1,0:T(8,128)(2,1)S(1)}, u32[]{:S(2)}, u32[]{:S(2)}) %collective-permute-start.1) | collective-permute-done | bytes 131104 | tf_op jit(solution)/shard_map/ppermute | solution.py:414
  26.8 0.0 collective-permute-start.6
  26.8 6.6 %collective-permute-done.2.refs_2_.refs_4_ = bf16[8,32,256]{2,1,0:T(8,128)(2,1)S(1)} collective-permute-done((bf16[8,32,256]{2,1,0:T(8,128)(2,1)S(1)}, bf16[8,32,256]{2,1,0:T(8,128)(2,1)S(1)}, u32[]{:S(2)}, u32[]{:S(2)}) %collective-permute-start.2) | collective-permute-done | bytes 131104 | tf_op jit(solution)/shard_map/ppermute | solution.py:414
  33.4 4.3 %collective-permute-start.7 = (bf16[8,64,256]{2,1,0:T(8,128)(2,1)}, bf16[8,64,256]{2,1,0:T(8,128)(2,1)S(1)}, u32[]{:S(2)}, u32[]{:S(2)}) collective-permute-start(bf16[8,64,256]{2,1,0:T(8,128)(2,1)} %get-tuple-element.33), channel_id=1, source_target_pairs={{0,28},{4,24},{8,20},{12,16},{16,12},{20,8},{24,4},{28,0},{1,29},{... | collective-permute-start | bytes 786440 | tf_op jit(solution)/shard_map/ppermute | solution.py:414
  37.8 0.3 collective-permute-done.3.refs_3_.refs_5_
  38.1 0.2 collective-permute-start.8
  38.3 0.0 copy-done.1
  38.3 0.1 copy.6.offdiag_ref
  38.4 0.0 copy-done
  38.4 0.2 packed_energy.1.refs_10_
  38.6 6.8 %collective-permute-done.4.refs_4_.refs_6_ = bf16[8,64,256]{2,1,0:T(8,128)(2,1)S(1)} collective-permute-done((bf16[8,64,256]{2,1,0:T(8,128)(2,1)}, bf16[8,64,256]{2,1,0:T(8,128)(2,1)S(1)}, u32[]{:S(2)}, u32[]{:S(2)}) %collective-permute-start.4) | collective-permute-done | bytes 262176 | tf_op jit(solution)/shard_map/ppermute | solution.py:414
  45.3 0.0 collective-permute-done.5.refs_5_.refs_7_
  45.3 3.2 %collective-permute-done.6.refs_6_.refs_8_ = bf16[8,64,256]{2,1,0:T(8,128)(2,1)S(1)} collective-permute-done((bf16[8,64,256]{2,1,0:T(8,128)(2,1)S(1)}, bf16[8,64,256]{2,1,0:T(8,128)(2,1)S(1)}, u32[]{:S(2)}, u32[]{:S(2)}) %collective-permute-start.6) | collective-permute-done | bytes 262176 | tf_op jit(solution)/shard_map/ppermute | solution.py:414
  48.6 0.0 collective-permute-done.7.refs_7_.refs_9_
  48.6 1.9 %collective-permute-done.8.refs_8_.refs_10_ = bf16[8,64,256]{2,1,0:T(8,128)(2,1)S(1)} collective-permute-done((bf16[8,64,256]{2,1,0:T(8,128)(2,1)S(1)}, bf16[8,64,256]{2,1,0:T(8,128)(2,1)S(1)}, u32[]{:S(2)}, u32[]{:S(2)}) %collective-permute-start.8) | collective-permute-done | bytes 262176 | tf_op jit(solution)/shard_map/ppermute | solution.py:414
  50.5 1.5 %gram_partial.1.refs_3_ = f32[32,128]{1,0:T(8,128)S(1)} custom-call(bf16[8,32,256]{2,1,0:T(8,128)(2,1)S(1)} %collective-permute-done.refs_0_.refs_2_, bf16[8,32,256]{2,1,0:T(8,128)(2,1)S(1)} %collective-permute-done.1.refs_1_.refs_3_, bf16[8,32,256]{2,1,0:T(8,128)(2,1)S(1)} %collective-permute-done.2.refs_2_.refs_4_, ...), custom_call_target="tpu_custom_call" | custom-call | flops 134217728 | bytes 2097152 | tf_op jit(solution)/shard_map/gram_partial/pallas_call | solution.py:218
  52.0 1.1 %collective-permute-start.9 = (f32[32,128]{1,0:T(8,128)S(1)}, f32[32,128]{1,0:T(8,128)S(1)}, u32[]{:S(2)}, u32[]{:S(2)}) collective-permute-start(f32[32,128]{1,0:T(8,128)S(1)} %gram_partial.1.refs_3_), channel_id=1, source_target_pairs={{0,3},{1,2},{2,1},{3,0},{4,7},{5,6},{6,5},{7,4},{8,11},{9,10},{10,... | collective-permute-start | bytes 49160 | tf_op jit(solution)/shard_map/ppermute | solution.py:326
  53.2 0.5 collective-permute-start.10
  53.7 0.2 collective-permute-start.11
  53.9 1.3 %collective-permute-done.9.refs_0_ = f32[32,128]{1,0:T(8,128)S(1)} collective-permute-done((f32[32,128]{1,0:T(8,128)S(1)}, f32[32,128]{1,0:T(8,128)S(1)}, u32[]{:S(2)}, u32[]{:S(2)}) %collective-permute-start.9) | collective-permute-done | bytes 16416 | tf_op jit(solution)/shard_map/ppermute | solution.py:326
  55.2 1.7 %collective-permute-done.10.refs_1_ = f32[32,128]{1,0:T(8,128)S(1)} collective-permute-done((f32[32,128]{1,0:T(8,128)S(1)}, f32[32,128]{1,0:T(8,128)S(1)}, u32[]{:S(2)}, u32[]{:S(2)}) %collective-permute-start.10) | collective-permute-done | bytes 16416 | tf_op jit(solution)/shard_map/ppermute | solution.py:326
  56.9 0.0 collective-permute-done.11.refs_2_
  56.9 4.7 %collective-permute-start.12 = (f32[32,128]{1,0:T(8,128)S(1)}, f32[32,128]{1,0:T(8,128)S(1)}, u32[]{:S(2)}, u32[]{:S(2)}) collective-permute-start(f32[32,128]{1,0:T(8,128)S(1)} %sum_over.2.refs_3_), channel_id=1, source_target_pairs={{0,28},{4,24},{8,20},{12,16},{16,12},{20,8},{24,4},{28,0},{1,29},{... | collective-permute-start | bytes 49160 | tf_op jit(solution)/shard_map/ppermute | solution.py:326
  61.6 0.0 collective-permute-start.13
  61.6 1.2 %collective-permute-start.14 = (f32[32,128]{1,0:T(8,128)S(1)}, f32[32,128]{1,0:T(8,128)S(1)}, u32[]{:S(2)}, u32[]{:S(2)}) collective-permute-start(f32[32,128]{1,0:T(8,128)S(1)} %sum_over.2.refs_3_), channel_id=1, source_target_pairs={{0,4},{4,0},{8,12},{12,8},{16,20},{20,16},{24,28},{28,24},{1,5},{5... | collective-permute-start | bytes 49160 | tf_op jit(solution)/shard_map/ppermute | solution.py:326
  62.8 0.8 %collective-permute-done.12.refs_0_ = f32[32,128]{1,0:T(8,128)S(1)} collective-permute-done((f32[32,128]{1,0:T(8,128)S(1)}, f32[32,128]{1,0:T(8,128)S(1)}, u32[]{:S(2)}, u32[]{:S(2)}) %collective-permute-start.12) | collective-permute-done | bytes 16416 | tf_op jit(solution)/shard_map/ppermute | solution.py:326
  63.6 3.5 %collective-permute-done.13.refs_1_ = f32[32,128]{1,0:T(8,128)S(1)} collective-permute-done((f32[32,128]{1,0:T(8,128)S(1)}, f32[32,128]{1,0:T(8,128)S(1)}, u32[]{:S(2)}, u32[]{:S(2)}) %collective-permute-start.13) | collective-permute-done | bytes 16416 | tf_op jit(solution)/shard_map/ppermute | solution.py:326
  67.2 0.0 collective-permute-done.14.refs_2_
  67.2 0.2 collective-permute-start.15
  67.4 3.6 %collective-permute-done.15.refs_0_ = f32[32,128]{1,0:T(8,128)S(1)} collective-permute-done((f32[32,128]{1,0:T(8,128)S(1)}, f32[32,128]{1,0:T(8,128)S(1)}, u32[]{:S(2)}, u32[]{:S(2)}) %collective-permute-start.15) | collective-permute-done | bytes 16416 | tf_op jit(solution)/shard_map/ppermute | solution.py:326
  71.0 3.5 %solve_and_project.1 = (f32[1,8]{1,0:T(1,128)}, f32[2,32,256]{2,1,0:T(8,128)}) custom-call(f32[32,128]{1,0:T(8,128)S(1)} %collective-permute-done.15.refs_0_, f32[32,128]{1,0:T(8,128)S(1)} %sum_over.3.refs_1_, bf16[8,32,256]{2,1,0:T(8,128)(2,1)S(1)} %collective-permute-done.refs_0_.refs_2_, bf16[8,32,256]{2,1,0:T(8,128)(2,1)S(1)} %collective-permute-done.1.refs_1_.refs_3_, ...), custom_call_target="tpu_custom_call" | custom-call | tf_op jit(solution)/shard_map/solve_and_project/pallas_call | solution.py:395
  (2 shorter events, 0.0 us)
Async XLA Ops:
  3.1 19.6 %collective-permute-start = (bf16[8,32,256]{2,1,0:T(8,128)(2,1)S(1)}, bf16[8,32,256]{2,1,0:T(8,128)(2,1)S(1)}, u32[]{:S(2)}, u32[]{:S(2)}) collective-permute-start(bf16[8,32,256]{2,1,0:T(8,128)(2,1)S(1)} %get-tuple-element.20), channel_id=1, source_target_pairs={{0,16},{4,20},{8,24},{12,28},{16,0},{20,4},{24,8},{28,12},{1,17},{... | collective-permute-start | bytes 393224 | tf_op jit(solution)/shard_map/ppermute | solution.py:414
  7.2 19.7 %collective-permute-start.1 = (bf16[8,32,256]{2,1,0:T(8,128)(2,1)S(1)}, bf16[8,32,256]{2,1,0:T(8,128)(2,1)S(1)}, u32[]{:S(2)}, u32[]{:S(2)}) collective-permute-start(bf16[8,32,256]{2,1,0:T(8,128)(2,1)S(1)} %get-tuple-element.21), channel_id=1, source_target_pairs={{0,20},{4,16},{8,28},{12,24},{16,4},{20,0},{24,12},{28,8},{1,21},{... | collective-permute-start | bytes 393224 | tf_op jit(solution)/shard_map/ppermute | solution.py:414
  8.4 29.8 %copy-start.1 = (f32[8]{0:T(128)S(1)}, f32[8]{0:T(128)}, u32[]{:S(2)}) copy-start(f32[8]{0:T(128)} %param.7) | copy-start | bytes 100
  8.4 29.9 %copy-start = (s32[8,256]{1,0:T(8,128)S(1)}, s32[8,256]{1,0:T(8,128)}, u32[]{:S(2)}) copy-start(s32[8,256]{1,0:T(8,128)} %spins_ref.1) | copy-start | bytes 24580
  11.8 21.7 %collective-permute-start.2 = (bf16[8,32,256]{2,1,0:T(8,128)(2,1)S(1)}, bf16[8,32,256]{2,1,0:T(8,128)(2,1)S(1)}, u32[]{:S(2)}, u32[]{:S(2)}) collective-permute-start(bf16[8,32,256]{2,1,0:T(8,128)(2,1)S(1)} %get-tuple-element.28), channel_id=1, source_target_pairs={{0,16},{4,20},{8,24},{12,28},{16,0},{20,4},{24,8},{28,12},{1,17},{... | collective-permute-start | bytes 393224 | tf_op jit(solution)/shard_map/ppermute | solution.py:414
  14.4 23.6 %collective-permute-start.3 = (bf16[8,32,256]{2,1,0:T(8,128)(2,1)S(1)}, bf16[8,32,256]{2,1,0:T(8,128)(2,1)S(1)}, u32[]{:S(2)}, u32[]{:S(2)}) collective-permute-start(bf16[8,32,256]{2,1,0:T(8,128)(2,1)S(1)} %get-tuple-element.29), channel_id=1, source_target_pairs={{0,20},{4,16},{8,28},{12,24},{16,4},{20,0},{24,12},{28,8},{1,21},{... | collective-permute-start | bytes 393224 | tf_op jit(solution)/shard_map/ppermute | solution.py:414
  14.5 30.9 %collective-permute-start.4 = (bf16[8,64,256]{2,1,0:T(8,128)(2,1)}, bf16[8,64,256]{2,1,0:T(8,128)(2,1)S(1)}, u32[]{:S(2)}, u32[]{:S(2)}) collective-permute-start(bf16[8,64,256]{2,1,0:T(8,128)(2,1)} %get-tuple-element.30), channel_id=1, source_target_pairs={{0,12},{4,8},{8,4},{12,0},{16,28},{20,24},{24,20},{28,16},{1,13},{... | collective-permute-start | bytes 786440 | tf_op jit(solution)/shard_map/ppermute | solution.py:414
  22.7 22.7 %collective-permute-start.5 = (bf16[8,64,256]{2,1,0:T(8,128)(2,1)}, bf16[8,64,256]{2,1,0:T(8,128)(2,1)S(1)}, u32[]{:S(2)}, u32[]{:S(2)}) collective-permute-start(bf16[8,64,256]{2,1,0:T(8,128)(2,1)} %get-tuple-element.31), channel_id=1, source_target_pairs={{0,24},{4,28},{8,16},{12,20},{16,8},{20,12},{24,0},{28,4},{1,25},{... | collective-permute-start | bytes 786440 | tf_op jit(solution)/shard_map/ppermute | solution.py:414
  26.8 21.7 %collective-permute-start.6 = (bf16[8,64,256]{2,1,0:T(8,128)(2,1)S(1)}, bf16[8,64,256]{2,1,0:T(8,128)(2,1)S(1)}, u32[]{:S(2)}, u32[]{:S(2)}) collective-permute-start(bf16[8,64,256]{2,1,0:T(8,128)(2,1)S(1)} %get-tuple-element.32), channel_id=1, source_target_pairs={{0,8},{4,12},{8,0},{12,4},{16,24},{20,28},{24,16},{28,20},{1,9},{5... | collective-permute-start | bytes 786440 | tf_op jit(solution)/shard_map/ppermute | solution.py:414
  33.4 15.1 %collective-permute-start.7 = (bf16[8,64,256]{2,1,0:T(8,128)(2,1)}, bf16[8,64,256]{2,1,0:T(8,128)(2,1)S(1)}, u32[]{:S(2)}, u32[]{:S(2)}) collective-permute-start(bf16[8,64,256]{2,1,0:T(8,128)(2,1)} %get-tuple-element.33), channel_id=1, source_target_pairs={{0,28},{4,24},{8,20},{12,16},{16,12},{20,8},{24,4},{28,0},{1,29},{... | collective-permute-start | bytes 786440 | tf_op jit(solution)/shard_map/ppermute | solution.py:414
  38.1 12.4 %collective-permute-start.8 = (bf16[8,64,256]{2,1,0:T(8,128)(2,1)S(1)}, bf16[8,64,256]{2,1,0:T(8,128)(2,1)S(1)}, u32[]{:S(2)}, u32[]{:S(2)}) collective-permute-start(bf16[8,64,256]{2,1,0:T(8,128)(2,1)S(1)} %get-tuple-element.34), channel_id=1, source_target_pairs={{0,4},{4,0},{8,12},{12,8},{16,20},{20,16},{24,28},{28,24},{1,5},{5... | collective-permute-start | bytes 786440 | tf_op jit(solution)/shard_map/ppermute | solution.py:414
  52.0 3.2 %collective-permute-start.9 = (f32[32,128]{1,0:T(8,128)S(1)}, f32[32,128]{1,0:T(8,128)S(1)}, u32[]{:S(2)}, u32[]{:S(2)}) collective-permute-start(f32[32,128]{1,0:T(8,128)S(1)} %gram_partial.1.refs_3_), channel_id=1, source_target_pairs={{0,3},{1,2},{2,1},{3,0},{4,7},{5,6},{6,5},{7,4},{8,11},{9,10},{10,... | collective-permute-start | bytes 49160 | tf_op jit(solution)/shard_map/ppermute | solution.py:326
  53.2 3.7 %collective-permute-start.10 = (f32[32,128]{1,0:T(8,128)S(1)}, f32[32,128]{1,0:T(8,128)S(1)}, u32[]{:S(2)}, u32[]{:S(2)}) collective-permute-start(f32[32,128]{1,0:T(8,128)S(1)} %gram_partial.1.refs_3_), channel_id=1, source_target_pairs={{0,2},{1,3},{2,0},{3,1},{4,6},{5,7},{6,4},{7,5},{8,10},{9,11},{10,... | collective-permute-start | bytes 49160 | tf_op jit(solution)/shard_map/ppermute | solution.py:326
  53.7 3.2 %collective-permute-start.11 = (f32[32,128]{1,0:T(8,128)S(1)}, f32[32,128]{1,0:T(8,128)S(1)}, u32[]{:S(2)}, u32[]{:S(2)}) collective-permute-start(f32[32,128]{1,0:T(8,128)S(1)} %gram_partial.1.refs_3_), channel_id=1, source_target_pairs={{0,1},{1,0},{2,3},{3,2},{4,5},{5,4},{6,7},{7,6},{8,9},{9,8},{10,11... | collective-permute-start | bytes 49160 | tf_op jit(solution)/shard_map/ppermute | solution.py:326
  56.9 6.7 %collective-permute-start.12 = (f32[32,128]{1,0:T(8,128)S(1)}, f32[32,128]{1,0:T(8,128)S(1)}, u32[]{:S(2)}, u32[]{:S(2)}) collective-permute-start(f32[32,128]{1,0:T(8,128)S(1)} %sum_over.2.refs_3_), channel_id=1, source_target_pairs={{0,28},{4,24},{8,20},{12,16},{16,12},{20,8},{24,4},{28,0},{1,29},{... | collective-permute-start | bytes 49160 | tf_op jit(solution)/shard_map/ppermute | solution.py:326
  61.6 5.5 %collective-permute-start.13 = (f32[32,128]{1,0:T(8,128)S(1)}, f32[32,128]{1,0:T(8,128)S(1)}, u32[]{:S(2)}, u32[]{:S(2)}) collective-permute-start(f32[32,128]{1,0:T(8,128)S(1)} %sum_over.2.refs_3_), channel_id=1, source_target_pairs={{0,24},{4,28},{8,16},{12,20},{16,8},{20,12},{24,0},{28,4},{1,25},{... | collective-permute-start | bytes 49160 | tf_op jit(solution)/shard_map/ppermute | solution.py:326
  61.6 5.5 %collective-permute-start.14 = (f32[32,128]{1,0:T(8,128)S(1)}, f32[32,128]{1,0:T(8,128)S(1)}, u32[]{:S(2)}, u32[]{:S(2)}) collective-permute-start(f32[32,128]{1,0:T(8,128)S(1)} %sum_over.2.refs_3_), channel_id=1, source_target_pairs={{0,4},{4,0},{8,12},{12,8},{16,20},{20,16},{24,28},{28,24},{1,5},{5... | collective-permute-start | bytes 49160 | tf_op jit(solution)/shard_map/ppermute | solution.py:326
  67.2 3.8 %collective-permute-start.15 = (f32[32,128]{1,0:T(8,128)S(1)}, f32[32,128]{1,0:T(8,128)S(1)}, u32[]{:S(2)}, u32[]{:S(2)}) collective-permute-start(f32[32,128]{1,0:T(8,128)S(1)} %sum_over.3.refs_1_), channel_id=1, source_target_pairs={{0,8},{4,12},{8,0},{12,4},{16,24},{20,28},{24,16},{28,20},{1,9},{5... | collective-permute-start | bytes 49160 | tf_op jit(solution)/shard_map/ppermute | solution.py:326

commit v21 on v20

--- a/solution.py
+++ b/solution.py
@@ -319,36 +319,50 @@
     out_ref[...] = tree_sum([ref[...] for ref in part_refs[::-1]])
 
 
-def partners(value, axis, masks):
-    size = lax.axis_size(axis)
+def partners(value, masks):
+    axes = ("samp", "layer")
+    places = lax.axis_size("samp") * lax.axis_size("layer")
     parts = []
     for mask in masks[::-1]:
-        parts.append(lax.ppermute(value, axis, [(i, i ^ mask) for i in range(size)]))
+        perm = [(i, i ^ mask) for i in range(places) if i % 2 == 1]
+        parts.append(lax.ppermute(value, axes, perm))
     return parts + [value]
 
 
-def sum_over(value, axis, masks):
+def sum_over(parts):
     return pl.pallas_call(
         sum_kernel,
-        out_shape=jax.ShapeDtypeStruct(value.shape, F32),
+        out_shape=jax.ShapeDtypeStruct(parts[0].shape, F32),
         compiler_params=pltpu.CompilerParams(vmem_limit_bytes=VMEM_LIMIT),
         name="sum_over",
-    )(*partners(value, axis, masks))
-
-
-def rounds(size):
-    masks = [1, size - 2] + [1 << bit for bit in range(1, size.bit_length() - 2)]
+    )(*parts)
+
+
+def rounds(samp, layer):
+    masks = [1 << bit for bit in range(1, layer.bit_length() - 1)]
+    masks += [layer, layer * (samp - 2)]
+    masks += [layer << bit for bit in range(1, samp.bit_length() - 2)]
     return [
         [a, b, a ^ b] if b else [a] for a, b in zip(masks[::2], masks[1::2] + [0] * (len(masks) % 2))
     ]
 
 
-def solve_kernel(grams, owners, *refs):
-    gram_refs, (*block_refs, weights_ref, update_ref, held) = refs[:grams], refs[grams:]
+def total_sum(value):
+    layer = lax.axis_size("layer")
+    lower = lax.ppermute(value, "layer", [(i, i + 1) for i in range(0, layer, 2)])
+    value = sum_over([lower, value])
+    for masks in rounds(lax.axis_size("samp"), layer):
+        value = sum_over(partners(value, masks))
+    return value, lax.ppermute(value, "layer", [(i + 1, i) for i in range(0, layer, 2)])
+
+
+def solve_kernel(owners, odd_ref, even_ref, *refs):
+    *block_refs, weights_ref, update_ref, held = refs
     blocks = in_place(block_refs, owners)
     mats, share, d = update_ref.shape
     local = weights_ref.shape[1]
-    packed = tree_sum([ref[...] for ref in gram_refs[::-1]])
+    odd = lax.axis_index("layer") % 2 == 1
+    packed = jnp.where(odd, odd_ref[...], even_ref[...])
     half, packed_width = packed.shape
     total = 2 * half
     width = (total // LANES + 1) * LANES
@@ -389,11 +403,11 @@
         update_ref[m] = acc[m * share : (m + 1) * share]
 
 
-def solve_and_project(grams, blocks, split, mats):
+def solve_and_project(sums, blocks, split, mats):
     local, count, d = blocks[0][0].shape
     total = local * len(blocks)
     return pl.pallas_call(
-        functools.partial(solve_kernel, len(grams), len(blocks)),
+        functools.partial(solve_kernel, len(blocks)),
         out_shape=(
             jax.ShapeDtypeStruct((1, local), F32),
             jax.ShapeDtypeStruct((mats, count // mats, d), F32),
@@ -401,7 +415,7 @@
         scratch_shapes=[pltpu.VMEM((total, d), F32)],
         compiler_params=pltpu.CompilerParams(vmem_limit_bytes=VMEM_LIMIT),
         name="solve_and_project",
-    )(*grams, *in_turn(blocks, split))
+    )(*sums, *in_turn(blocks, split))
 
 
 def body(spins, activations, cotangents, offdiag):
@@ -413,12 +427,7 @@
         perm = [(i, i ^ k) for i in range(owners)]
         blocks[k][part] = lax.ppermute(blocks[k][part], "samp", perm)
     partial = gram_partial(blocks, split, packed_energy(spins, offdiag, total))
-    gram = sum_over(partial, "layer", list(range(1, lax.axis_size("layer"))))
-    *early, last = rounds(owners)
-    for masks in early:
-        gram = sum_over(gram, "samp", masks)
-    grams = partners(gram, "samp", last)
-    weights, update = solve_and_project(grams, blocks, split, mats)
+    weights, update = solve_and_project(total_sum(partial), blocks, split, mats)
     return weights.reshape(local), update
 
 

time: 74.7 us -> 87.4 us (1.17)
  waiting for transfers between devices: 36.4 us -> 49.7 us
    ppermute x7 -> x8, waiting for transfers between devices: 10.9 us -> 24.2 us  [the longest x1 23.4 us: total_sum(): lax.ppermute(value, 'layer', [(i + 1, i) for i in range(0, layer, 2)])]
    ppermute x7 -> x8, starting transfers between devices: 8 us -> 7.17 us  [the longest x6 3.96 us: partners(): parts.append(lax.ppermute(value, axes, perm))]
    pallas_call x3 -> x4, Pallas kernels: 3.53 us -> 3.54 us  [the longest x1 3.52 us: solve_and_project(): pl.pallas_call(functools.partial(solve_kernel, len(blocks)), out_shape=(j...]
  transfers between devices with their start and end apart: 16 -> 17, of which waited for: 12 -> 9; matrix products, arithmetic and copies ran while one was open for 0% -> 0% of each run, Pallas kernels for 5% -> 4%
where the time goes in v21:
time: 87.4 us; the launch traced here: 87.1 us
  waiting for transfers between devices  49.7 us (57%)
  starting transfers between devices  25.5 us (29%)
  Pallas kernels  11 us (13%)
    ppermute x9, waiting for transfers between devices, body(): blocks[k][part] = lax.ppermute(blocks[k][part], 'samp', perm)  25.5 us
    ppermute x1, waiting for transfers between devices, total_sum(): lax.ppermute(value, 'layer', [(i + 1, i) for i in range(0, layer, 2)])  23.4 us
    ppermute x9, starting transfers between devices, body(): blocks[k][part] = lax.ppermute(blocks[k][part], 'samp', perm)  18.3 us
    pallas_call x2, Pallas kernels, jac_rows(): pl.pallas_call(functools.partial(jac_kernel, part * mats, joined), in_spe...  5.74 us
    ppermute x6, starting transfers between devices, partners(): parts.append(lax.ppermute(value, axes, perm))  3.96 us
    pallas_call x1, Pallas kernels, solve_and_project(): pl.pallas_call(functools.partial(solve_kernel, len(blocks)), out_shape=(j...  3.52 us
    ppermute x1, starting transfers between devices, total_sum(): lax.ppermute(value, 'layer', [(i, i + 1) for i in range(0, layer, 2)])  1.92 us
  transfers between devices with their start and end apart: 17, of which 9 were waited for; matrix products, arithmetic and copies ran while one was open for 0% of the time, Pallas kernels for 4%

profile of v21, /device:TPU:0, one launch (start us, length us, event | category | flops | bytes accessed | tf_op | source)
XLA Modules:
  0.0 87.1 jit_solution(7192907899714249439)
XLA Ops:
  0.6 2.4 %jac_rows.2 = (bf16[8,32,256]{2,1,0:T(8,128)(2,1)S(1)}, bf16[8,32,256]{2,1,0:T(8,128)(2,1)S(1)}, bf16[8,32,256]{2,1,0:T(8,128)(2,1)S(1)}, bf16[8,32,256]{2,1,0:T...) custom-call(bf16[8,2,256,256]{3,2,1,0:T(8,128)(2,1)} %act_hbm.3, ...), custom_call_target="tpu_custom_call" | custom-call | flops 268435456 | bytes 3145728 | tf_op jit(solution)/shard_map/jac_rows/pallas_call | solution.py:108
  3.1 4.1 %collective-permute-start = (bf16[8,32,256]{2,1,0:T(8,128)(2,1)S(1)}, bf16[8,32,256]{2,1,0:T(8,128)(2,1)S(1)}, u32[]{:S(2)}, u32[]{:S(2)}) collective-permute-start(bf16[8,32,256]{2,1,0:T(8,128)(2,1)S(1)} %get-tuple-element.20), channel_id=1, source_target_pairs={{0,16},{4,20},{8,24},{12,28},{16,0},{20,4},{24,8},{28,12},{1,17},{... | collective-permute-start | bytes 393224 | tf_op jit(solution)/shard_map/ppermute | solution.py:428
  7.2 1.3 %collective-permute-start.1 = (bf16[8,32,256]{2,1,0:T(8,128)(2,1)S(1)}, bf16[8,32,256]{2,1,0:T(8,128)(2,1)S(1)}, u32[]{:S(2)}, u32[]{:S(2)}) collective-permute-start(bf16[8,32,256]{2,1,0:T(8,128)(2,1)S(1)} %get-tuple-element.21), channel_id=1, source_target_pairs={{0,20},{4,16},{8,28},{12,24},{16,4},{20,0},{24,12},{28,8},{1,21},{... | collective-permute-start | bytes 393224 | tf_op jit(solution)/shard_map/ppermute | solution.py:428
  8.4 0.0 copy-start.1
  8.4 0.0 copy-start
  8.5 3.3 %jac_rows.3 = (bf16[8,64,256]{2,1,0:T(8,128)(2,1)S(1)}, bf16[8,64,256]{2,1,0:T(8,128)(2,1)S(1)}, bf16[8,64,256]{2,1,0:T(8,128)(2,1)S(1)}, bf16[8,64,256]{2,1,0:T...) custom-call(bf16[8,2,256,256]{3,2,1,0:T(8,128)(2,1)} %act_hbm.3, ...), custom_call_target="tpu_custom_call" | custom-call | flops 268435456 | bytes 3145728 | tf_op jit(solution)/shard_map/jac_rows/pallas_call | solution.py:108
  11.8 2.7 %collective-permute-start.2 = (bf16[8,32,256]{2,1,0:T(8,128)(2,1)S(1)}, bf16[8,32,256]{2,1,0:T(8,128)(2,1)S(1)}, u32[]{:S(2)}, u32[]{:S(2)}) collective-permute-start(bf16[8,32,256]{2,1,0:T(8,128)(2,1)S(1)} %get-tuple-element.28), channel_id=1, source_target_pairs={{0,16},{4,20},{8,24},{12,28},{16,0},{20,4},{24,8},{28,12},{1,17},{... | collective-permute-start | bytes 393224 | tf_op jit(solution)/shard_map/ppermute | solution.py:428
  14.4 0.0 collective-permute-start.3
  14.5 2.8 %collective-permute-start.4 = (bf16[8,64,256]{2,1,0:T(8,128)(2,1)}, bf16[8,64,256]{2,1,0:T(8,128)(2,1)S(1)}, u32[]{:S(2)}, u32[]{:S(2)}) collective-permute-start(bf16[8,64,256]{2,1,0:T(8,128)(2,1)} %get-tuple-element.30), channel_id=1, source_target_pairs={{0,12},{4,8},{8,4},{12,0},{16,28},{20,24},{24,20},{28,16},{1,13},{... | collective-permute-start | bytes 786440 | tf_op jit(solution)/shard_map/ppermute | solution.py:428
  17.2 5.4 %collective-permute-done.refs_0_ = bf16[8,32,256]{2,1,0:T(8,128)(2,1)S(1)} collective-permute-done((bf16[8,32,256]{2,1,0:T(8,128)(2,1)S(1)}, bf16[8,32,256]{2,1,0:T(8,128)(2,1)S(1)}, u32[]{:S(2)}, u32[]{:S(2)}) %collective-permute-start) | collective-permute-done | bytes 131104 | tf_op jit(solution)/shard_map/ppermute | solution.py:428
  22.7 2.9 %collective-permute-start.5 = (bf16[8,64,256]{2,1,0:T(8,128)(2,1)}, bf16[8,64,256]{2,1,0:T(8,128)(2,1)S(1)}, u32[]{:S(2)}, u32[]{:S(2)}) collective-permute-start(bf16[8,64,256]{2,1,0:T(8,128)(2,1)} %get-tuple-element.31), channel_id=1, source_target_pairs={{0,24},{4,28},{8,16},{12,20},{16,8},{20,12},{24,0},{28,4},{1,25},{... | collective-permute-start | bytes 786440 | tf_op jit(solution)/shard_map/ppermute | solution.py:428
  25.6 1.2 %collective-permute-done.1.refs_1_ = bf16[8,32,256]{2,1,0:T(8,128)(2,1)S(1)} collective-permute-done((bf16[8,32,256]{2,1,0:T(8,128)(2,1)S(1)}, bf16[8,32,256]{2,1,0:T(8,128)(2,1)S(1)}, u32[]{:S(2)}, u32[]{:S(2)}) %collective-permute-start.1) | collective-permute-done | bytes 131104 | tf_op jit(solution)/shard_map/ppermute | solution.py:428
  26.8 0.0 collective-permute-start.6
  26.8 6.6 %collective-permute-done.2.refs_2_ = bf16[8,32,256]{2,1,0:T(8,128)(2,1)S(1)} collective-permute-done((bf16[8,32,256]{2,1,0:T(8,128)(2,1)S(1)}, bf16[8,32,256]{2,1,0:T(8,128)(2,1)S(1)}, u32[]{:S(2)}, u32[]{:S(2)}) %collective-permute-start.2) | collective-permute-done | bytes 131104 | tf_op jit(solution)/shard_map/ppermute | solution.py:428
  33.4 4.3 %collective-permute-start.7 = (bf16[8,64,256]{2,1,0:T(8,128)(2,1)}, bf16[8,64,256]{2,1,0:T(8,128)(2,1)S(1)}, u32[]{:S(2)}, u32[]{:S(2)}) collective-permute-start(bf16[8,64,256]{2,1,0:T(8,128)(2,1)} %get-tuple-element.33), channel_id=1, source_target_pairs={{0,28},{4,24},{8,20},{12,16},{16,12},{20,8},{24,4},{28,0},{1,29},{... | collective-permute-start | bytes 786440 | tf_op jit(solution)/shard_map/ppermute | solution.py:428
  37.8 0.3 collective-permute-done.3.refs_3_
  38.1 0.2 collective-permute-start.8
  38.3 0.0 copy-done.1
  38.3 0.1 copy.6.offdiag_ref
  38.4 0.0 copy-done
  38.4 0.2 packed_energy.1.refs_10_
  38.6 6.8 %collective-permute-done.4.refs_4_ = bf16[8,64,256]{2,1,0:T(8,128)(2,1)S(1)} collective-permute-done((bf16[8,64,256]{2,1,0:T(8,128)(2,1)}, bf16[8,64,256]{2,1,0:T(8,128)(2,1)S(1)}, u32[]{:S(2)}, u32[]{:S(2)}) %collective-permute-start.4) | collective-permute-done | bytes 262176 | tf_op jit(solution)/shard_map/ppermute | solution.py:428
  45.3 0.0 collective-permute-done.5.refs_5_
  45.3 3.2 %collective-permute-done.6.refs_6_ = bf16[8,64,256]{2,1,0:T(8,128)(2,1)S(1)} collective-permute-done((bf16[8,64,256]{2,1,0:T(8,128)(2,1)S(1)}, bf16[8,64,256]{2,1,0:T(8,128)(2,1)S(1)}, u32[]{:S(2)}, u32[]{:S(2)}) %collective-permute-start.6) | collective-permute-done | bytes 262176 | tf_op jit(solution)/shard_map/ppermute | solution.py:428
  48.6 0.0 collective-permute-done.7.refs_7_
  48.6 1.9 %collective-permute-done.8.refs_8_ = bf16[8,64,256]{2,1,0:T(8,128)(2,1)S(1)} collective-permute-done((bf16[8,64,256]{2,1,0:T(8,128)(2,1)S(1)}, bf16[8,64,256]{2,1,0:T(8,128)(2,1)S(1)}, u32[]{:S(2)}, u32[]{:S(2)}) %collective-permute-start.8) | collective-permute-done | bytes 262176 | tf_op jit(solution)/shard_map/ppermute | solution.py:428
  50.5 1.5 %gram_partial.1.refs_1_ = f32[32,128]{1,0:T(8,128)S(1)} custom-call(bf16[8,32,256]{2,1,0:T(8,128)(2,1)S(1)} %collective-permute-done.refs_0_, bf16[8,32,256]{2,1,0:T(8,128)(2,1)S(1)} %collective-permute-done.1.refs_1_, bf16[8,32,256]{2,1,0:T(8,128)(2,1)S(1)} %collective-permute-done.2.refs_2_, bf16[8,32,256]{2,1,0:T(8,128)(2,1)S(1)} %collective-permute-done.3.refs_3_, ...), custom_call_target="tpu_custom_call" | custom-call | flops 134217728 | bytes 2097152 | tf_op jit(solution)/shard_map/gram_partial/pallas_call | solution.py:218
  52.0 1.9 %collective-permute-start.9 = (f32[32,128]{1,0:T(8,128)S(1)}, f32[32,128]{1,0:T(8,128)S(1)}, u32[]{:S(2)}, u32[]{:S(2)}) collective-permute-start(f32[32,128]{1,0:T(8,128)S(1)} %gram_partial.1.refs_1_), channel_id=1, source_target_pairs={{0,1},{2,3},{4,5},{6,7},{8,9},{10,11},{12,13},{14,15},{16,17},{18,... | collective-permute-start | bytes 49160 | tf_op jit(solution)/shard_map/ppermute | solution.py:352
  53.9 0.8 collective-permute-done.9.refs_0_
  54.8 0.7 collective-permute-start.10
  55.4 0.7 collective-permute-start.11
  56.1 0.7 collective-permute-start.12
  56.8 0.0 collective-permute-done.10.refs_0_
  56.8 0.0 collective-permute-done.11.refs_1_
  56.8 0.0 collective-permute-done.12.refs_2_
  56.8 0.7 collective-permute-start.13
  57.5 0.7 collective-permute-start.14
  58.2 0.7 collective-permute-start.15
  58.8 0.0 collective-permute-done.13.refs_0_
  58.8 0.0 collective-permute-done.14.refs_1_
  58.8 0.0 collective-permute-done.15.refs_2_
  58.9 1.3 %collective-permute-start.16 = (f32[32,128]{1,0:T(8,128)S(1)}, f32[32,128]{1,0:T(8,128)S(1)}, u32[]{:S(2)}, u32[]{:S(2)}) collective-permute-start(f32[32,128]{1,0:T(8,128)S(1)} %sum_over.5.odd_ref), channel_id=1, source_target_pairs={{1,0},{3,2},{5,4},{7,6},{9,8},{11,10},{13,12},{15,14},{17,16},{19,... | collective-permute-start | bytes 49160 | tf_op jit(solution)/shard_map/ppermute | solution.py:356
  60.2 23.4 %collective-permute-done.16.even_ref = f32[32,128]{1,0:T(8,128)S(1)} collective-permute-done((f32[32,128]{1,0:T(8,128)S(1)}, f32[32,128]{1,0:T(8,128)S(1)}, u32[]{:S(2)}, u32[]{:S(2)}) %collective-permute-start.16) | collective-permute-done | bytes 16416 | tf_op jit(solution)/shard_map/ppermute | solution.py:356
  83.6 3.5 %solve_and_project.1 = (f32[1,8]{1,0:T(1,128)}, f32[2,32,256]{2,1,0:T(8,128)}) custom-call(f32[32,128]{1,0:T(8,128)S(1)} %sum_over.5.odd_ref, f32[32,128]{1,0:T(8,128)S(1)} %collective-permute-done.16.even_ref, bf16[8,32,256]{2,1,0:T(8,128)(2,1)S(1)} %collective-permute-done.refs_0_, bf16[8,32,256]{2,1,0:T(8,128)(2,1)S(1)} %collective-permute-done.1.refs_1_, ...), custom_call_target="tpu_custom_call" | custom-call | tf_op jit(solution)/shard_map/solve_and_project/pallas_call | solution.py:409
  (3 shorter events, 0.0 us)
Async XLA Ops:
  3.1 19.6 %collective-permute-start = (bf16[8,32,256]{2,1,0:T(8,128)(2,1)S(1)}, bf16[8,32,256]{2,1,0:T(8,128)(2,1)S(1)}, u32[]{:S(2)}, u32[]{:S(2)}) collective-permute-start(bf16[8,32,256]{2,1,0:T(8,128)(2,1)S(1)} %get-tuple-element.20), channel_id=1, source_target_pairs={{0,16},{4,20},{8,24},{12,28},{16,0},{20,4},{24,8},{28,12},{1,17},{... | collective-permute-start | bytes 393224 | tf_op jit(solution)/shard_map/ppermute | solution.py:428
  7.2 19.7 %collective-permute-start.1 = (bf16[8,32,256]{2,1,0:T(8,128)(2,1)S(1)}, bf16[8,32,256]{2,1,0:T(8,128)(2,1)S(1)}, u32[]{:S(2)}, u32[]{:S(2)}) collective-permute-start(bf16[8,32,256]{2,1,0:T(8,128)(2,1)S(1)} %get-tuple-element.21), channel_id=1, source_target_pairs={{0,20},{4,16},{8,28},{12,24},{16,4},{20,0},{24,12},{28,8},{1,21},{... | collective-permute-start | bytes 393224 | tf_op jit(solution)/shard_map/ppermute | solution.py:428
  8.4 29.8 %copy-start.1 = (f32[8]{0:T(128)S(1)}, f32[8]{0:T(128)}, u32[]{:S(2)}) copy-start(f32[8]{0:T(128)} %param.7) | copy-start | bytes 100
  8.4 29.9 %copy-start = (s32[8,256]{1,0:T(8,128)S(1)}, s32[8,256]{1,0:T(8,128)}, u32[]{:S(2)}) copy-start(s32[8,256]{1,0:T(8,128)} %spins_ref.1) | copy-start | bytes 24580
  11.8 21.7 %collective-permute-start.2 = (bf16[8,32,256]{2,1,0:T(8,128)(2,1)S(1)}, bf16[8,32,256]{2,1,0:T(8,128)(2,1)S(1)}, u32[]{:S(2)}, u32[]{:S(2)}) collective-permute-start(bf16[8,32,256]{2,1,0:T(8,128)(2,1)S(1)} %get-tuple-element.28), channel_id=1, source_target_pairs={{0,16},{4,20},{8,24},{12,28},{16,0},{20,4},{24,8},{28,12},{1,17},{... | collective-permute-start | bytes 393224 | tf_op jit(solution)/shard_map/ppermute | solution.py:428
  14.4 23.6 %collective-permute-start.3 = (bf16[8,32,256]{2,1,0:T(8,128)(2,1)S(1)}, bf16[8,32,256]{2,1,0:T(8,128)(2,1)S(1)}, u32[]{:S(2)}, u32[]{:S(2)}) collective-permute-start(bf16[8,32,256]{2,1,0:T(8,128)(2,1)S(1)} %get-tuple-element.29), channel_id=1, source_target_pairs={{0,20},{4,16},{8,28},{12,24},{16,4},{20,0},{24,12},{28,8},{1,21},{... | collective-permute-start | bytes 393224 | tf_op jit(solution)/shard_map/ppermute | solution.py:428
  14.5 30.9 %collective-permute-start.4 = (bf16[8,64,256]{2,1,0:T(8,128)(2,1)}, bf16[8,64,256]{2,1,0:T(8,128)(2,1)S(1)}, u32[]{:S(2)}, u32[]{:S(2)}) collective-permute-start(bf16[8,64,256]{2,1,0:T(8,128)(2,1)} %get-tuple-element.30), channel_id=1, source_target_pairs={{0,12},{4,8},{8,4},{12,0},{16,28},{20,24},{24,20},{28,16},{1,13},{... | collective-permute-start | bytes 786440 | tf_op jit(solution)/shard_map/ppermute | solution.py:428
  22.7 22.6 %collective-permute-start.5 = (bf16[8,64,256]{2,1,0:T(8,128)(2,1)}, bf16[8,64,256]{2,1,0:T(8,128)(2,1)S(1)}, u32[]{:S(2)}, u32[]{:S(2)}) collective-permute-start(bf16[8,64,256]{2,1,0:T(8,128)(2,1)} %get-tuple-element.31), channel_id=1, source_target_pairs={{0,24},{4,28},{8,16},{12,20},{16,8},{20,12},{24,0},{28,4},{1,25},{... | collective-permute-start | bytes 786440 | tf_op jit(solution)/shard_map/ppermute | solution.py:428
  26.8 21.7 %collective-permute-start.6 = (bf16[8,64,256]{2,1,0:T(8,128)(2,1)S(1)}, bf16[8,64,256]{2,1,0:T(8,128)(2,1)S(1)}, u32[]{:S(2)}, u32[]{:S(2)}) collective-permute-start(bf16[8,64,256]{2,1,0:T(8,128)(2,1)S(1)} %get-tuple-element.32), channel_id=1, source_target_pairs={{0,8},{4,12},{8,0},{12,4},{16,24},{20,28},{24,16},{28,20},{1,9},{5... | collective-permute-start | bytes 786440 | tf_op jit(solution)/shard_map/ppermute | solution.py:428
  33.4 15.1 %collective-permute-start.7 = (bf16[8,64,256]{2,1,0:T(8,128)(2,1)}, bf16[8,64,256]{2,1,0:T(8,128)(2,1)S(1)}, u32[]{:S(2)}, u32[]{:S(2)}) collective-permute-start(bf16[8,64,256]{2,1,0:T(8,128)(2,1)} %get-tuple-element.33), channel_id=1, source_target_pairs={{0,28},{4,24},{8,20},{12,16},{16,12},{20,8},{24,4},{28,0},{1,29},{... | collective-permute-start | bytes 786440 | tf_op jit(solution)/shard_map/ppermute | solution.py:428
  38.1 12.4 %collective-permute-start.8 = (bf16[8,64,256]{2,1,0:T(8,128)(2,1)S(1)}, bf16[8,64,256]{2,1,0:T(8,128)(2,1)S(1)}, u32[]{:S(2)}, u32[]{:S(2)}) collective-permute-start(bf16[8,64,256]{2,1,0:T(8,128)(2,1)S(1)} %get-tuple-element.34), channel_id=1, source_target_pairs={{0,4},{4,0},{8,12},{12,8},{16,20},{20,16},{24,28},{28,24},{1,5},{5... | collective-permute-start | bytes 786440 | tf_op jit(solution)/shard_map/ppermute | solution.py:428
  52.0 2.7 %collective-permute-start.9 = (f32[32,128]{1,0:T(8,128)S(1)}, f32[32,128]{1,0:T(8,128)S(1)}, u32[]{:S(2)}, u32[]{:S(2)}) collective-permute-start(f32[32,128]{1,0:T(8,128)S(1)} %gram_partial.1.refs_1_), channel_id=1, source_target_pairs={{0,1},{2,3},{4,5},{6,7},{8,9},{10,11},{12,13},{14,15},{16,17},{18,... | collective-permute-start | bytes 49160 | tf_op jit(solution)/shard_map/ppermute | solution.py:352
  54.8 2.0 %collective-permute-start.10 = (f32[32,128]{1,0:T(8,128)S(1)}, f32[32,128]{1,0:T(8,128)S(1)}, u32[]{:S(2)}, u32[]{:S(2)}) collective-permute-start(f32[32,128]{1,0:T(8,128)S(1)} %sum_over.3.refs_3_), channel_id=1, source_target_pairs={{1,7},{3,5},{5,3},{7,1},{9,15},{11,13},{13,11},{15,9},{17,23},{19,... | collective-permute-start | bytes 49160 | tf_op jit(solution)/shard_map/ppermute | solution.py:328
  55.4 1.4 %collective-permute-start.11 = (f32[32,128]{1,0:T(8,128)S(1)}, f32[32,128]{1,0:T(8,128)S(1)}, u32[]{:S(2)}, u32[]{:S(2)}) collective-permute-start(f32[32,128]{1,0:T(8,128)S(1)} %sum_over.3.refs_3_), channel_id=1, source_target_pairs={{1,5},{3,7},{5,1},{7,3},{9,13},{11,15},{13,9},{15,11},{17,21},{19,... | collective-permute-start | bytes 49160 | tf_op jit(solution)/shard_map/ppermute | solution.py:328
  56.1 0.7 collective-permute-start.12
  56.8 2.0 %collective-permute-start.13 = (f32[32,128]{1,0:T(8,128)S(1)}, f32[32,128]{1,0:T(8,128)S(1)}, u32[]{:S(2)}, u32[]{:S(2)}) collective-permute-start(f32[32,128]{1,0:T(8,128)S(1)} %sum_over.4.refs_3_), channel_id=1, source_target_pairs={{1,17},{3,19},{5,21},{7,23},{9,25},{11,27},{13,29},{15,31},{17,1},... | collective-permute-start | bytes 49160 | tf_op jit(solution)/shard_map/ppermute | solution.py:328
  57.5 1.4 %collective-permute-start.14 = (f32[32,128]{1,0:T(8,128)S(1)}, f32[32,128]{1,0:T(8,128)S(1)}, u32[]{:S(2)}, u32[]{:S(2)}) collective-permute-start(f32[32,128]{1,0:T(8,128)S(1)} %sum_over.4.refs_3_), channel_id=1, source_target_pairs={{1,9},{3,11},{5,13},{7,15},{9,1},{11,3},{13,5},{15,7},{17,25},{19,... | collective-permute-start | bytes 49160 | tf_op jit(solution)/shard_map/ppermute | solution.py:328
  58.2 0.7 collective-permute-start.15
  58.9 24.7 %collective-permute-start.16 = (f32[32,128]{1,0:T(8,128)S(1)}, f32[32,128]{1,0:T(8,128)S(1)}, u32[]{:S(2)}, u32[]{:S(2)}) collective-permute-start(f32[32,128]{1,0:T(8,128)S(1)} %sum_over.5.odd_ref), channel_id=1, source_target_pairs={{1,0},{3,2},{5,4},{7,6},{9,8},{11,10},{13,12},{15,14},{17,16},{19,... | collective-permute-start | bytes 49160 | tf_op jit(solution)/shard_map/ppermute | solution.py:356

commit v22 on v21

--- a/solution.py
+++ b/solution.py
@@ -324,7 +324,7 @@
     places = lax.axis_size("samp") * lax.axis_size("layer")
     parts = []
     for mask in masks[::-1]:
-        perm = [(i, i ^ mask) for i in range(places) if i % 2 == 1]
+        perm = [(i, i ^ mask if i % 2 == 1 else i) for i in range(places)]
         parts.append(lax.ppermute(value, axes, perm))
     return parts + [value]
 
@@ -349,11 +349,11 @@
 
 def total_sum(value):
     layer = lax.axis_size("layer")
-    lower = lax.ppermute(value, "layer", [(i, i + 1) for i in range(0, layer, 2)])
-    value = sum_over([lower, value])
+    pairs = [(i, i ^ 1) for i in range(layer)]
+    value = sum_over([lax.ppermute(value, "layer", pairs), value])
     for masks in rounds(lax.axis_size("samp"), layer):
         value = sum_over(partners(value, masks))
-    return value, lax.ppermute(value, "layer", [(i + 1, i) for i in range(0, layer, 2)])
+    return value, lax.ppermute(value, "layer", pairs)
 
 
 def solve_kernel(owners, odd_ref, even_ref, *refs):

time: 87.4 us -> 84.6 us (0.968)
  waiting for transfers between devices: 49.7 us -> 27.5 us
  starting transfers between devices: 25.5 us -> 45 us
    ppermute x2, waiting for transfers between devices: 24.2 us -> 2 us  [the longest x1 1.16 us: total_sum(): value = sum_over([lax.ppermute(value, 'layer', pairs), value])]
    ppermute x2, starting transfers between devices: 3.21 us -> 22.7 us  [the longest x1 22.6 us: total_sum(): return (value, lax.ppermute(value, 'layer', pairs))]
where the time goes in v22:
time: 84.6 us; the launch traced here: 84.3 us
  starting transfers between devices  45 us (53%)
  waiting for transfers between devices  27.5 us (33%)
  Pallas kernels  11 us (13%)
    ppermute x9, waiting for transfers between devices, body(): blocks[k][part] = lax.ppermute(blocks[k][part], 'samp', perm)  25.5 us
    ppermute x1, starting transfers between devices, total_sum(): return (value, lax.ppermute(value, 'layer', pairs))  22.6 us
    ppermute x9, starting transfers between devices, body(): blocks[k][part] = lax.ppermute(blocks[k][part], 'samp', perm)  18.3 us
    pallas_call x2, Pallas kernels, jac_rows(): pl.pallas_call(functools.partial(jac_kernel, part * mats, joined), in_spe...  5.74 us
    ppermute x6, starting transfers between devices, partners(): parts.append(lax.ppermute(value, axes, perm))  3.96 us
    pallas_call x1, Pallas kernels, solve_and_project(): pl.pallas_call(functools.partial(solve_kernel, len(blocks)), out_shape=(j...  3.52 us
  transfers between devices with their start and end apart: 17, of which 9 were waited for; matrix products, arithmetic and copies ran while one was open for 0% of the time, Pallas kernels for 4%

profile of v22, /device:TPU:0, one launch (start us, length us, event | category | flops | bytes accessed | tf_op | source)
XLA Modules:
  0.0 84.3 jit_solution(7306355359445876843)
XLA Ops:
  0.6 2.4 %jac_rows.2 = (bf16[8,32,256]{2,1,0:T(8,128)(2,1)S(1)}, bf16[8,32,256]{2,1,0:T(8,128)(2,1)S(1)}, bf16[8,32,256]{2,1,0:T(8,128)(2,1)S(1)}, bf16[8,32,256]{2,1,0:T...) custom-call(bf16[8,2,256,256]{3,2,1,0:T(8,128)(2,1)} %act_hbm.3, ...), custom_call_target="tpu_custom_call" | custom-call | flops 268435456 | bytes 3145728 | tf_op jit(solution)/shard_map/jac_rows/pallas_call | solution.py:108
  3.1 4.1 %collective-permute-start = (bf16[8,32,256]{2,1,0:T(8,128)(2,1)S(1)}, bf16[8,32,256]{2,1,0:T(8,128)(2,1)S(1)}, u32[]{:S(2)}, u32[]{:S(2)}) collective-permute-start(bf16[8,32,256]{2,1,0:T(8,128)(2,1)S(1)} %get-tuple-element.20), channel_id=1, source_target_pairs={{0,16},{4,20},{8,24},{12,28},{16,0},{20,4},{24,8},{28,12},{1,17},{... | collective-permute-start | bytes 393224 | tf_op jit(solution)/shard_map/ppermute | solution.py:428
  7.2 1.3 %collective-permute-start.1 = (bf16[8,32,256]{2,1,0:T(8,128)(2,1)S(1)}, bf16[8,32,256]{2,1,0:T(8,128)(2,1)S(1)}, u32[]{:S(2)}, u32[]{:S(2)}) collective-permute-start(bf16[8,32,256]{2,1,0:T(8,128)(2,1)S(1)} %get-tuple-element.21), channel_id=1, source_target_pairs={{0,20},{4,16},{8,28},{12,24},{16,4},{20,0},{24,12},{28,8},{1,21},{... | collective-permute-start | bytes 393224 | tf_op jit(solution)/shard_map/ppermute | solution.py:428
  8.4 0.0 copy-start.1
  8.4 0.0 copy-start
  8.5 3.3 %jac_rows.3 = (bf16[8,64,256]{2,1,0:T(8,128)(2,1)S(1)}, bf16[8,64,256]{2,1,0:T(8,128)(2,1)S(1)}, bf16[8,64,256]{2,1,0:T(8,128)(2,1)S(1)}, bf16[8,64,256]{2,1,0:T...) custom-call(bf16[8,2,256,256]{3,2,1,0:T(8,128)(2,1)} %act_hbm.3, ...), custom_call_target="tpu_custom_call" | custom-call | flops 268435456 | bytes 3145728 | tf_op jit(solution)/shard_map/jac_rows/pallas_call | solution.py:108
  11.8 2.7 %collective-permute-start.2 = (bf16[8,32,256]{2,1,0:T(8,128)(2,1)S(1)}, bf16[8,32,256]{2,1,0:T(8,128)(2,1)S(1)}, u32[]{:S(2)}, u32[]{:S(2)}) collective-permute-start(bf16[8,32,256]{2,1,0:T(8,128)(2,1)S(1)} %get-tuple-element.28), channel_id=1, source_target_pairs={{0,16},{4,20},{8,24},{12,28},{16,0},{20,4},{24,8},{28,12},{1,17},{... | collective-permute-start | bytes 393224 | tf_op jit(solution)/shard_map/ppermute | solution.py:428
  14.4 0.0 collective-permute-start.3
  14.5 2.8 %collective-permute-start.4 = (bf16[8,64,256]{2,1,0:T(8,128)(2,1)}, bf16[8,64,256]{2,1,0:T(8,128)(2,1)S(1)}, u32[]{:S(2)}, u32[]{:S(2)}) collective-permute-start(bf16[8,64,256]{2,1,0:T(8,128)(2,1)} %get-tuple-element.30), channel_id=1, source_target_pairs={{0,12},{4,8},{8,4},{12,0},{16,28},{20,24},{24,20},{28,16},{1,13},{... | collective-permute-start | bytes 786440 | tf_op jit(solution)/shard_map/ppermute | solution.py:428
  17.2 5.4 %collective-permute-done.refs_0_ = bf16[8,32,256]{2,1,0:T(8,128)(2,1)S(1)} collective-permute-done((bf16[8,32,256]{2,1,0:T(8,128)(2,1)S(1)}, bf16[8,32,256]{2,1,0:T(8,128)(2,1)S(1)}, u32[]{:S(2)}, u32[]{:S(2)}) %collective-permute-start) | collective-permute-done | bytes 131104 | tf_op jit(solution)/shard_map/ppermute | solution.py:428
  22.7 2.9 %collective-permute-start.5 = (bf16[8,64,256]{2,1,0:T(8,128)(2,1)}, bf16[8,64,256]{2,1,0:T(8,128)(2,1)S(1)}, u32[]{:S(2)}, u32[]{:S(2)}) collective-permute-start(bf16[8,64,256]{2,1,0:T(8,128)(2,1)} %get-tuple-element.31), channel_id=1, source_target_pairs={{0,24},{4,28},{8,16},{12,20},{16,8},{20,12},{24,0},{28,4},{1,25},{... | collective-permute-start | bytes 786440 | tf_op jit(solution)/shard_map/ppermute | solution.py:428
  25.6 1.2 %collective-permute-done.1.refs_1_ = bf16[8,32,256]{2,1,0:T(8,128)(2,1)S(1)} collective-permute-done((bf16[8,32,256]{2,1,0:T(8,128)(2,1)S(1)}, bf16[8,32,256]{2,1,0:T(8,128)(2,1)S(1)}, u32[]{:S(2)}, u32[]{:S(2)}) %collective-permute-start.1) | collective-permute-done | bytes 131104 | tf_op jit(solution)/shard_map/ppermute | solution.py:428
  26.8 0.0 collective-permute-start.6
  26.8 6.6 %collective-permute-done.2.refs_2_ = bf16[8,32,256]{2,1,0:T(8,128)(2,1)S(1)} collective-permute-done((bf16[8,32,256]{2,1,0:T(8,128)(2,1)S(1)}, bf16[8,32,256]{2,1,0:T(8,128)(2,1)S(1)}, u32[]{:S(2)}, u32[]{:S(2)}) %collective-permute-start.2) | collective-permute-done | bytes 131104 | tf_op jit(solution)/shard_map/ppermute | solution.py:428
  33.4 4.3 %collective-permute-start.7 = (bf16[8,64,256]{2,1,0:T(8,128)(2,1)}, bf16[8,64,256]{2,1,0:T(8,128)(2,1)S(1)}, u32[]{:S(2)}, u32[]{:S(2)}) collective-permute-start(bf16[8,64,256]{2,1,0:T(8,128)(2,1)} %get-tuple-element.33), channel_id=1, source_target_pairs={{0,28},{4,24},{8,20},{12,16},{16,12},{20,8},{24,4},{28,0},{1,29},{... | collective-permute-start | bytes 786440 | tf_op jit(solution)/shard_map/ppermute | solution.py:428
  37.8 0.3 collective-permute-done.3.refs_3_
  38.1 0.2 collective-permute-start.8
  38.3 0.0 copy-done.1
  38.3 0.1 copy.6.offdiag_ref
  38.4 0.0 copy-done
  38.4 0.2 packed_energy.1.refs_10_
  38.6 6.8 %collective-permute-done.4.refs_4_ = bf16[8,64,256]{2,1,0:T(8,128)(2,1)S(1)} collective-permute-done((bf16[8,64,256]{2,1,0:T(8,128)(2,1)}, bf16[8,64,256]{2,1,0:T(8,128)(2,1)S(1)}, u32[]{:S(2)}, u32[]{:S(2)}) %collective-permute-start.4) | collective-permute-done | bytes 262176 | tf_op jit(solution)/shard_map/ppermute | solution.py:428
  45.3 0.0 collective-permute-done.5.refs_5_
  45.3 3.2 %collective-permute-done.6.refs_6_ = bf16[8,64,256]{2,1,0:T(8,128)(2,1)S(1)} collective-permute-done((bf16[8,64,256]{2,1,0:T(8,128)(2,1)S(1)}, bf16[8,64,256]{2,1,0:T(8,128)(2,1)S(1)}, u32[]{:S(2)}, u32[]{:S(2)}) %collective-permute-start.6) | collective-permute-done | bytes 262176 | tf_op jit(solution)/shard_map/ppermute | solution.py:428
  48.6 0.0 collective-permute-done.7.refs_7_
  48.6 1.9 %collective-permute-done.8.refs_8_ = bf16[8,64,256]{2,1,0:T(8,128)(2,1)S(1)} collective-permute-done((bf16[8,64,256]{2,1,0:T(8,128)(2,1)S(1)}, bf16[8,64,256]{2,1,0:T(8,128)(2,1)S(1)}, u32[]{:S(2)}, u32[]{:S(2)}) %collective-permute-start.8) | collective-permute-done | bytes 262176 | tf_op jit(solution)/shard_map/ppermute | solution.py:428
  50.5 1.5 %gram_partial.1.refs_1_ = f32[32,128]{1,0:T(8,128)S(1)} custom-call(bf16[8,32,256]{2,1,0:T(8,128)(2,1)S(1)} %collective-permute-done.refs_0_, bf16[8,32,256]{2,1,0:T(8,128)(2,1)S(1)} %collective-permute-done.1.refs_1_, bf16[8,32,256]{2,1,0:T(8,128)(2,1)S(1)} %collective-permute-done.2.refs_2_, bf16[8,32,256]{2,1,0:T(8,128)(2,1)S(1)} %collective-permute-done.3.refs_3_, ...), custom_call_target="tpu_custom_call" | custom-call | flops 134217728 | bytes 2097152 | tf_op jit(solution)/shard_map/gram_partial/pallas_call | solution.py:218
  52.0 0.1 collective-permute-start.9
  52.1 1.2 %collective-permute-done.9.refs_0_ = f32[32,128]{1,0:T(8,128)S(1)} collective-permute-done((f32[32,128]{1,0:T(8,128)S(1)}, f32[32,128]{1,0:T(8,128)S(1)}, u32[]{:S(2)}, u32[]{:S(2)}) %collective-permute-start.9) | collective-permute-done | bytes 16416 | tf_op jit(solution)/shard_map/ppermute | solution.py:353
  53.2 0.7 collective-permute-start.10
  53.9 0.7 collective-permute-start.11
  54.6 0.7 collective-permute-start.12
  55.2 0.0 collective-permute-done.10.refs_0_
  55.3 0.0 collective-permute-done.11.refs_1_
  55.3 0.0 collective-permute-done.12.refs_2_
  55.3 0.7 collective-permute-start.13
  56.0 0.7 collective-permute-start.14
  56.6 0.7 collective-permute-start.15
  57.3 0.0 collective-permute-done.13.refs_0_
  57.3 0.0 collective-permute-done.14.refs_1_
  57.3 0.0 collective-permute-done.15.refs_2_
  57.4 22.6 %collective-permute-start.16 = (f32[32,128]{1,0:T(8,128)S(1)}, f32[32,128]{1,0:T(8,128)S(1)}, u32[]{:S(2)}, u32[]{:S(2)}) collective-permute-start(f32[32,128]{1,0:T(8,128)S(1)} %sum_over.5.odd_ref), channel_id=1, source_target_pairs={{0,1},{1,0},{2,3},{3,2},{4,5},{5,4},{6,7},{7,6},{8,9},{9,8},{10,11... | collective-permute-start | bytes 49160 | tf_op jit(solution)/shard_map/ppermute | solution.py:356
  79.9 0.8 collective-permute-done.16.even_ref
  80.8 3.5 %solve_and_project.1 = (f32[1,8]{1,0:T(1,128)}, f32[2,32,256]{2,1,0:T(8,128)}) custom-call(f32[32,128]{1,0:T(8,128)S(1)} %sum_over.5.odd_ref, f32[32,128]{1,0:T(8,128)S(1)} %collective-permute-done.16.even_ref, bf16[8,32,256]{2,1,0:T(8,128)(2,1)S(1)} %collective-permute-done.refs_0_, bf16[8,32,256]{2,1,0:T(8,128)(2,1)S(1)} %collective-permute-done.1.refs_1_, ...), custom_call_target="tpu_custom_call" | custom-call | tf_op jit(solution)/shard_map/solve_and_project/pallas_call | solution.py:409
  (3 shorter events, 0.0 us)
Async XLA Ops:
  3.1 19.6 %collective-permute-start = (bf16[8,32,256]{2,1,0:T(8,128)(2,1)S(1)}, bf16[8,32,256]{2,1,0:T(8,128)(2,1)S(1)}, u32[]{:S(2)}, u32[]{:S(2)}) collective-permute-start(bf16[8,32,256]{2,1,0:T(8,128)(2,1)S(1)} %get-tuple-element.20), channel_id=1, source_target_pairs={{0,16},{4,20},{8,24},{12,28},{16,0},{20,4},{24,8},{28,12},{1,17},{... | collective-permute-start | bytes 393224 | tf_op jit(solution)/shard_map/ppermute | solution.py:428
  7.2 19.7 %collective-permute-start.1 = (bf16[8,32,256]{2,1,0:T(8,128)(2,1)S(1)}, bf16[8,32,256]{2,1,0:T(8,128)(2,1)S(1)}, u32[]{:S(2)}, u32[]{:S(2)}) collective-permute-start(bf16[8,32,256]{2,1,0:T(8,128)(2,1)S(1)} %get-tuple-element.21), channel_id=1, source_target_pairs={{0,20},{4,16},{8,28},{12,24},{16,4},{20,0},{24,12},{28,8},{1,21},{... | collective-permute-start | bytes 393224 | tf_op jit(solution)/shard_map/ppermute | solution.py:428
  8.4 29.8 %copy-start.1 = (f32[8]{0:T(128)S(1)}, f32[8]{0:T(128)}, u32[]{:S(2)}) copy-start(f32[8]{0:T(128)} %param.7) | copy-start | bytes 100
  8.4 29.9 %copy-start = (s32[8,256]{1,0:T(8,128)S(1)}, s32[8,256]{1,0:T(8,128)}, u32[]{:S(2)}) copy-start(s32[8,256]{1,0:T(8,128)} %spins_ref.1) | copy-start | bytes 24580
  11.8 21.7 %collective-permute-start.2 = (bf16[8,32,256]{2,1,0:T(8,128)(2,1)S(1)}, bf16[8,32,256]{2,1,0:T(8,128)(2,1)S(1)}, u32[]{:S(2)}, u32[]{:S(2)}) collective-permute-start(bf16[8,32,256]{2,1,0:T(8,128)(2,1)S(1)} %get-tuple-element.28), channel_id=1, source_target_pairs={{0,16},{4,20},{8,24},{12,28},{16,0},{20,4},{24,8},{28,12},{1,17},{... | collective-permute-start | bytes 393224 | tf_op jit(solution)/shard_map/ppermute | solution.py:428
  14.4 23.6 %collective-permute-start.3 = (bf16[8,32,256]{2,1,0:T(8,128)(2,1)S(1)}, bf16[8,32,256]{2,1,0:T(8,128)(2,1)S(1)}, u32[]{:S(2)}, u32[]{:S(2)}) collective-permute-start(bf16[8,32,256]{2,1,0:T(8,128)(2,1)S(1)} %get-tuple-element.29), channel_id=1, source_target_pairs={{0,20},{4,16},{8,28},{12,24},{16,4},{20,0},{24,12},{28,8},{1,21},{... | collective-permute-start | bytes 393224 | tf_op jit(solution)/shard_map/ppermute | solution.py:428
  14.5 30.9 %collective-permute-start.4 = (bf16[8,64,256]{2,1,0:T(8,128)(2,1)}, bf16[8,64,256]{2,1,0:T(8,128)(2,1)S(1)}, u32[]{:S(2)}, u32[]{:S(2)}) collective-permute-start(bf16[8,64,256]{2,1,0:T(8,128)(2,1)} %get-tuple-element.30), channel_id=1, source_target_pairs={{0,12},{4,8},{8,4},{12,0},{16,28},{20,24},{24,20},{28,16},{1,13},{... | collective-permute-start | bytes 786440 | tf_op jit(solution)/shard_map/ppermute | solution.py:428
  22.7 22.6 %collective-permute-start.5 = (bf16[8,64,256]{2,1,0:T(8,128)(2,1)}, bf16[8,64,256]{2,1,0:T(8,128)(2,1)S(1)}, u32[]{:S(2)}, u32[]{:S(2)}) collective-permute-start(bf16[8,64,256]{2,1,0:T(8,128)(2,1)} %get-tuple-element.31), channel_id=1, source_target_pairs={{0,24},{4,28},{8,16},{12,20},{16,8},{20,12},{24,0},{28,4},{1,25},{... | collective-permute-start | bytes 786440 | tf_op jit(solution)/shard_map/ppermute | solution.py:428
  26.8 21.7 %collective-permute-start.6 = (bf16[8,64,256]{2,1,0:T(8,128)(2,1)S(1)}, bf16[8,64,256]{2,1,0:T(8,128)(2,1)S(1)}, u32[]{:S(2)}, u32[]{:S(2)}) collective-permute-start(bf16[8,64,256]{2,1,0:T(8,128)(2,1)S(1)} %get-tuple-element.32), channel_id=1, source_target_pairs={{0,8},{4,12},{8,0},{12,4},{16,24},{20,28},{24,16},{28,20},{1,9},{5... | collective-permute-start | bytes 786440 | tf_op jit(solution)/shard_map/ppermute | solution.py:428
  33.4 15.1 %collective-permute-start.7 = (bf16[8,64,256]{2,1,0:T(8,128)(2,1)}, bf16[8,64,256]{2,1,0:T(8,128)(2,1)S(1)}, u32[]{:S(2)}, u32[]{:S(2)}) collective-permute-start(bf16[8,64,256]{2,1,0:T(8,128)(2,1)} %get-tuple-element.33), channel_id=1, source_target_pairs={{0,28},{4,24},{8,20},{12,16},{16,12},{20,8},{24,4},{28,0},{1,29},{... | collective-permute-start | bytes 786440 | tf_op jit(solution)/shard_map/ppermute | solution.py:428
  38.1 12.4 %collective-permute-start.8 = (bf16[8,64,256]{2,1,0:T(8,128)(2,1)S(1)}, bf16[8,64,256]{2,1,0:T(8,128)(2,1)S(1)}, u32[]{:S(2)}, u32[]{:S(2)}) collective-permute-start(bf16[8,64,256]{2,1,0:T(8,128)(2,1)S(1)} %get-tuple-element.34), channel_id=1, source_target_pairs={{0,4},{4,0},{8,12},{12,8},{16,20},{20,16},{24,28},{28,24},{1,5},{5... | collective-permute-start | bytes 786440 | tf_op jit(solution)/shard_map/ppermute | solution.py:428
  52.0 1.2 %collective-permute-start.9 = (f32[32,128]{1,0:T(8,128)S(1)}, f32[32,128]{1,0:T(8,128)S(1)}, u32[]{:S(2)}, u32[]{:S(2)}) collective-permute-start(f32[32,128]{1,0:T(8,128)S(1)} %gram_partial.1.refs_1_), channel_id=1, source_target_pairs={{0,1},{1,0},{2,3},{3,2},{4,5},{5,4},{6,7},{7,6},{8,9},{9,8},{10,11... | collective-permute-start | bytes 49160 | tf_op jit(solution)/shard_map/ppermute | solution.py:353
  53.2 2.0 %collective-permute-start.10 = (f32[32,128]{1,0:T(8,128)S(1)}, f32[32,128]{1,0:T(8,128)S(1)}, u32[]{:S(2)}, u32[]{:S(2)}) collective-permute-start(f32[32,128]{1,0:T(8,128)S(1)} %sum_over.3.refs_3_), channel_id=1, source_target_pairs={{0,0},{1,7},{2,2},{3,5},{4,4},{5,3},{6,6},{7,1},{8,8},{9,15},{10,1... | collective-permute-start | bytes 49160 | tf_op jit(solution)/shard_map/ppermute | solution.py:328
  53.9 1.4 %collective-permute-start.11 = (f32[32,128]{1,0:T(8,128)S(1)}, f32[32,128]{1,0:T(8,128)S(1)}, u32[]{:S(2)}, u32[]{:S(2)}) collective-permute-start(f32[32,128]{1,0:T(8,128)S(1)} %sum_over.3.refs_3_), channel_id=1, source_target_pairs={{0,0},{1,5},{2,2},{3,7},{4,4},{5,1},{6,6},{7,3},{8,8},{9,13},{10,1... | collective-permute-start | bytes 49160 | tf_op jit(solution)/shard_map/ppermute | solution.py:328
  54.6 0.7 collective-permute-start.12
  55.3 2.0 %collective-permute-start.13 = (f32[32,128]{1,0:T(8,128)S(1)}, f32[32,128]{1,0:T(8,128)S(1)}, u32[]{:S(2)}, u32[]{:S(2)}) collective-permute-start(f32[32,128]{1,0:T(8,128)S(1)} %sum_over.4.refs_3_), channel_id=1, source_target_pairs={{0,0},{1,17},{2,2},{3,19},{4,4},{5,21},{6,6},{7,23},{8,8},{9,25},{... | collective-permute-start | bytes 49160 | tf_op jit(solution)/shard_map/ppermute | solution.py:328
  56.0 1.4 %collective-permute-start.14 = (f32[32,128]{1,0:T(8,128)S(1)}, f32[32,128]{1,0:T(8,128)S(1)}, u32[]{:S(2)}, u32[]{:S(2)}) collective-permute-start(f32[32,128]{1,0:T(8,128)S(1)} %sum_over.4.refs_3_), channel_id=1, source_target_pairs={{0,0},{1,9},{2,2},{3,11},{4,4},{5,13},{6,6},{7,15},{8,8},{9,1},{10... | collective-permute-start | bytes 49160 | tf_op jit(solution)/shard_map/ppermute | solution.py:328
  56.6 0.7 collective-permute-start.15
  57.4 23.4 %collective-permute-start.16 = (f32[32,128]{1,0:T(8,128)S(1)}, f32[32,128]{1,0:T(8,128)S(1)}, u32[]{:S(2)}, u32[]{:S(2)}) collective-permute-start(f32[32,128]{1,0:T(8,128)S(1)} %sum_over.5.odd_ref), channel_id=1, source_target_pairs={{0,1},{1,0},{2,3},{3,2},{4,5},{5,4},{6,7},{7,6},{8,9},{9,8},{10,11... | collective-permute-start | bytes 49160 | tf_op jit(solution)/shard_map/ppermute | solution.py:356

commit v23 on v22

--- a/solution.py
+++ b/solution.py
@@ -322,11 +322,8 @@
 def partners(value, masks):
     axes = ("samp", "layer")
     places = lax.axis_size("samp") * lax.axis_size("layer")
-    parts = []
-    for mask in masks[::-1]:
-        perm = [(i, i ^ mask if i % 2 == 1 else i) for i in range(places)]
-        parts.append(lax.ppermute(value, axes, perm))
-    return parts + [value]
+    perms = [[(i, i ^ mask) for i in range(places)] for mask in masks[::-1]]
+    return [lax.ppermute(value, axes, perm) for perm in perms] + [value]
 
 
 def sum_over(parts):
@@ -342,27 +339,16 @@
     masks = [1 << bit for bit in range(1, layer.bit_length() - 1)]
     masks += [layer, layer * (samp - 2)]
     masks += [layer << bit for bit in range(1, samp.bit_length() - 2)]
-    return [
-        [a, b, a ^ b] if b else [a] for a, b in zip(masks[::2], masks[1::2] + [0] * (len(masks) % 2))
-    ]
-
-
-def total_sum(value):
-    layer = lax.axis_size("layer")
-    pairs = [(i, i ^ 1) for i in range(layer)]
-    value = sum_over([lax.ppermute(value, "layer", pairs), value])
-    for masks in rounds(lax.axis_size("samp"), layer):
-        value = sum_over(partners(value, masks))
-    return value, lax.ppermute(value, "layer", pairs)
-
-
-def solve_kernel(owners, odd_ref, even_ref, *refs):
-    *block_refs, weights_ref, update_ref, held = refs
+    later = zip(masks[::2], masks[1::2] + [0] * (len(masks) % 2))
+    return [[1]] + [[a, b, a ^ b] if b else [a] for a, b in later]
+
+
+def solve_kernel(sums, owners, *refs):
+    sum_refs, (*block_refs, weights_ref, update_ref, held) = refs[:sums], refs[sums:]
     blocks = in_place(block_refs, owners)
     mats, share, d = update_ref.shape
     local = weights_ref.shape[1]
-    odd = lax.axis_index("layer") % 2 == 1
-    packed = jnp.where(odd, odd_ref[...], even_ref[...])
+    packed = tree_sum([ref[...] for ref in sum_refs[::-1]])
     half, packed_width = packed.shape
     total = 2 * half
     width = (total // LANES + 1) * LANES
@@ -407,7 +393,7 @@
     local, count, d = blocks[0][0].shape
     total = local * len(blocks)
     return pl.pallas_call(
-        functools.partial(solve_kernel, len(blocks)),
+        functools.partial(solve_kernel, len(sums), len(blocks)),
         out_shape=(
             jax.ShapeDtypeStruct((1, local), F32),
             jax.ShapeDtypeStruct((mats, count // mats, d), F32),
@@ -427,7 +413,10 @@
         perm = [(i, i ^ k) for i in range(owners)]
         blocks[k][part] = lax.ppermute(blocks[k][part], "samp", perm)
     partial = gram_partial(blocks, split, packed_energy(spins, offdiag, total))
-    weights, update = solve_and_project(total_sum(partial), blocks, split, mats)
+    *early, last = rounds(owners, lax.axis_size("layer"))
+    for masks in early:
+        partial = sum_over(partners(partial, masks))
+    weights, update = solve_and_project(partners(partial, last), blocks, split, mats)
     return weights.reshape(local), update
 
 

time: 84.6 us -> 75.2 us (0.89)
  starting transfers between devices: 45 us -> 29.4 us
  waiting for transfers between devices: 27.5 us -> 33.8 us
    ppermute x8 -> x7, starting transfers between devices: 26.6 us -> 11.1 us  [partners(): return [lax.ppermute(value, axes, perm) for perm in perms] + [value]]
    ppermute x8 -> x7, waiting for transfers between devices: 2.02 us -> 8.37 us  [partners(): return [lax.ppermute(value, axes, perm) for perm in perms] + [value]]
  transfers between devices with their start and end apart: 17 -> 16, of which waited for: 9 -> 14; matrix products, arithmetic and copies ran while one was open for 0% -> 0% of each run, Pallas kernels for 4% -> 5%
where the time goes in v23:
time: 75.2 us; the launch traced here: 75 us
  waiting for transfers between devices  33.8 us (45%)
  starting transfers between devices  29.4 us (39%)
  Pallas kernels  11 us (15%)
    ppermute x9, waiting for transfers between devices, body(): blocks[k][part] = lax.ppermute(blocks[k][part], 'samp', perm)  25.4 us
    ppermute x9, starting transfers between devices, body(): blocks[k][part] = lax.ppermute(blocks[k][part], 'samp', perm)  18.3 us
    ppermute x7, starting transfers between devices, partners(): return [lax.ppermute(value, axes, perm) for perm in perms] + [value]  11.1 us
    ppermute x7, waiting for transfers between devices, partners(): return [lax.ppermute(value, axes, perm) for perm in perms] + [value]  8.37 us
    pallas_call x2, Pallas kernels, jac_rows(): pl.pallas_call(functools.partial(jac_kernel, part * mats, joined), in_spe...  5.74 us
    pallas_call x1, Pallas kernels, solve_and_project(): pl.pallas_call(functools.partial(solve_kernel, len(sums), len(blocks)), o...  3.52 us
    pallas_call x1, Pallas kernels, gram_partial(): pl.pallas_call(functools.partial(gram_kernel, len(blocks)), out_shape=jax...  1.51 us
  transfers between devices with their start and end apart: 16, of which 14 were waited for; matrix products, arithmetic and copies ran while one was open for 0% of the time, Pallas kernels for 5%

profile of v23, /device:TPU:0, one launch (start us, length us, event | category | flops | bytes accessed | tf_op | source)
XLA Modules:
  0.0 75.0 jit_solution(7485906781427522868)
XLA Ops:
  0.6 2.4 %jac_rows.2 = (bf16[8,32,256]{2,1,0:T(8,128)(2,1)S(1)}, bf16[8,32,256]{2,1,0:T(8,128)(2,1)S(1)}, bf16[8,32,256]{2,1,0:T(8,128)(2,1)S(1)}, bf16[8,32,256]{2,1,0:T...) custom-call(bf16[8,2,256,256]{3,2,1,0:T(8,128)(2,1)} %act_hbm.3, ...), custom_call_target="tpu_custom_call" | custom-call | flops 268435456 | bytes 3145728 | tf_op jit(solution)/shard_map/jac_rows/pallas_call | solution.py:108
  3.1 4.1 %collective-permute-start = (bf16[8,32,256]{2,1,0:T(8,128)(2,1)S(1)}, bf16[8,32,256]{2,1,0:T(8,128)(2,1)S(1)}, u32[]{:S(2)}, u32[]{:S(2)}) collective-permute-start(bf16[8,32,256]{2,1,0:T(8,128)(2,1)S(1)} %get-tuple-element.20), channel_id=1, source_target_pairs={{0,16},{4,20},{8,24},{12,28},{16,0},{20,4},{24,8},{28,12},{1,17},{... | collective-permute-start | bytes 393224 | tf_op jit(solution)/shard_map/ppermute | solution.py:414
  7.2 1.3 %collective-permute-start.1 = (bf16[8,32,256]{2,1,0:T(8,128)(2,1)S(1)}, bf16[8,32,256]{2,1,0:T(8,128)(2,1)S(1)}, u32[]{:S(2)}, u32[]{:S(2)}) collective-permute-start(bf16[8,32,256]{2,1,0:T(8,128)(2,1)S(1)} %get-tuple-element.21), channel_id=1, source_target_pairs={{0,20},{4,16},{8,28},{12,24},{16,4},{20,0},{24,12},{28,8},{1,21},{... | collective-permute-start | bytes 393224 | tf_op jit(solution)/shard_map/ppermute | solution.py:414
  8.4 0.0 copy-start.1
  8.4 0.0 copy-start
  8.5 3.3 %jac_rows.3 = (bf16[8,64,256]{2,1,0:T(8,128)(2,1)S(1)}, bf16[8,64,256]{2,1,0:T(8,128)(2,1)S(1)}, bf16[8,64,256]{2,1,0:T(8,128)(2,1)S(1)}, bf16[8,64,256]{2,1,0:T...) custom-call(bf16[8,2,256,256]{3,2,1,0:T(8,128)(2,1)} %act_hbm.3, ...), custom_call_target="tpu_custom_call" | custom-call | flops 268435456 | bytes 3145728 | tf_op jit(solution)/shard_map/jac_rows/pallas_call | solution.py:108
  11.8 2.7 %collective-permute-start.2 = (bf16[8,32,256]{2,1,0:T(8,128)(2,1)S(1)}, bf16[8,32,256]{2,1,0:T(8,128)(2,1)S(1)}, u32[]{:S(2)}, u32[]{:S(2)}) collective-permute-start(bf16[8,32,256]{2,1,0:T(8,128)(2,1)S(1)} %get-tuple-element.28), channel_id=1, source_target_pairs={{0,16},{4,20},{8,24},{12,28},{16,0},{20,4},{24,8},{28,12},{1,17},{... | collective-permute-start | bytes 393224 | tf_op jit(solution)/shard_map/ppermute | solution.py:414
  14.4 0.0 collective-permute-start.3
  14.5 2.8 %collective-permute-start.4 = (bf16[8,64,256]{2,1,0:T(8,128)(2,1)}, bf16[8,64,256]{2,1,0:T(8,128)(2,1)S(1)}, u32[]{:S(2)}, u32[]{:S(2)}) collective-permute-start(bf16[8,64,256]{2,1,0:T(8,128)(2,1)} %get-tuple-element.30), channel_id=1, source_target_pairs={{0,12},{4,8},{8,4},{12,0},{16,28},{20,24},{24,20},{28,16},{1,13},{... | collective-permute-start | bytes 786440 | tf_op jit(solution)/shard_map/ppermute | solution.py:414
  17.3 5.4 %collective-permute-done.refs_0_.refs_4_ = bf16[8,32,256]{2,1,0:T(8,128)(2,1)S(1)} collective-permute-done((bf16[8,32,256]{2,1,0:T(8,128)(2,1)S(1)}, bf16[8,32,256]{2,1,0:T(8,128)(2,1)S(1)}, u32[]{:S(2)}, u32[]{:S(2)}) %collective-permute-start) | collective-permute-done | bytes 131104 | tf_op jit(solution)/shard_map/ppermute | solution.py:414
  22.7 2.9 %collective-permute-start.5 = (bf16[8,64,256]{2,1,0:T(8,128)(2,1)}, bf16[8,64,256]{2,1,0:T(8,128)(2,1)S(1)}, u32[]{:S(2)}, u32[]{:S(2)}) collective-permute-start(bf16[8,64,256]{2,1,0:T(8,128)(2,1)} %get-tuple-element.31), channel_id=1, source_target_pairs={{0,24},{4,28},{8,16},{12,20},{16,8},{20,12},{24,0},{28,4},{1,25},{... | collective-permute-start | bytes 786440 | tf_op jit(solution)/shard_map/ppermute | solution.py:414
  25.6 1.2 %collective-permute-done.1.refs_1_.refs_5_ = bf16[8,32,256]{2,1,0:T(8,128)(2,1)S(1)} collective-permute-done((bf16[8,32,256]{2,1,0:T(8,128)(2,1)S(1)}, bf16[8,32,256]{2,1,0:T(8,128)(2,1)S(1)}, u32[]{:S(2)}, u32[]{:S(2)}) %collective-permute-start.1) | collective-permute-done | bytes 131104 | tf_op jit(solution)/shard_map/ppermute | solution.py:414
  26.8 0.0 collective-permute-start.6
  26.8 6.6 %collective-permute-done.2.refs_2_.refs_6_ = bf16[8,32,256]{2,1,0:T(8,128)(2,1)S(1)} collective-permute-done((bf16[8,32,256]{2,1,0:T(8,128)(2,1)S(1)}, bf16[8,32,256]{2,1,0:T(8,128)(2,1)S(1)}, u32[]{:S(2)}, u32[]{:S(2)}) %collective-permute-start.2) | collective-permute-done | bytes 131104 | tf_op jit(solution)/shard_map/ppermute | solution.py:414
  33.4 4.3 %collective-permute-start.7 = (bf16[8,64,256]{2,1,0:T(8,128)(2,1)}, bf16[8,64,256]{2,1,0:T(8,128)(2,1)S(1)}, u32[]{:S(2)}, u32[]{:S(2)}) collective-permute-start(bf16[8,64,256]{2,1,0:T(8,128)(2,1)} %get-tuple-element.33), channel_id=1, source_target_pairs={{0,28},{4,24},{8,20},{12,16},{16,12},{20,8},{24,4},{28,0},{1,29},{... | collective-permute-start | bytes 786440 | tf_op jit(solution)/shard_map/ppermute | solution.py:414
  37.8 0.3 collective-permute-done.3.refs_3_.refs_7_
  38.1 0.2 collective-permute-start.8
  38.3 0.0 copy-done.1
  38.3 0.1 copy.6.offdiag_ref
  38.4 0.0 copy-done
  38.4 0.2 packed_energy.1.refs_10_
  38.6 6.8 %collective-permute-done.4.refs_4_.refs_8_ = bf16[8,64,256]{2,1,0:T(8,128)(2,1)S(1)} collective-permute-done((bf16[8,64,256]{2,1,0:T(8,128)(2,1)}, bf16[8,64,256]{2,1,0:T(8,128)(2,1)S(1)}, u32[]{:S(2)}, u32[]{:S(2)}) %collective-permute-start.4) | collective-permute-done | bytes 262176 | tf_op jit(solution)/shard_map/ppermute | solution.py:414
  45.3 0.0 collective-permute-done.5.refs_5_.refs_9_
  45.3 3.2 %collective-permute-done.6.refs_6_.refs_10_ = bf16[8,64,256]{2,1,0:T(8,128)(2,1)S(1)} collective-permute-done((bf16[8,64,256]{2,1,0:T(8,128)(2,1)S(1)}, bf16[8,64,256]{2,1,0:T(8,128)(2,1)S(1)}, u32[]{:S(2)}, u32[]{:S(2)}) %collective-permute-start.6) | collective-permute-done | bytes 262176 | tf_op jit(solution)/shard_map/ppermute | solution.py:414
  48.6 0.0 collective-permute-done.7.refs_7_.refs_11_
  48.6 1.9 %collective-permute-done.8.refs_8_.refs_12_ = bf16[8,64,256]{2,1,0:T(8,128)(2,1)S(1)} collective-permute-done((bf16[8,64,256]{2,1,0:T(8,128)(2,1)S(1)}, bf16[8,64,256]{2,1,0:T(8,128)(2,1)S(1)}, u32[]{:S(2)}, u32[]{:S(2)}) %collective-permute-start.8) | collective-permute-done | bytes 262176 | tf_op jit(solution)/shard_map/ppermute | solution.py:414
  50.5 1.5 %gram_partial.1.refs_1_ = f32[32,128]{1,0:T(8,128)S(1)} custom-call(bf16[8,32,256]{2,1,0:T(8,128)(2,1)S(1)} %collective-permute-done.refs_0_.refs_4_, bf16[8,32,256]{2,1,0:T(8,128)(2,1)S(1)} %collective-permute-done.1.refs_1_.refs_5_, bf16[8,32,256]{2,1,0:T(8,128)(2,1)S(1)} %collective-permute-done.2.refs_2_.refs_6_, ...), custom_call_target="tpu_custom_call" | custom-call | flops 134217728 | bytes 2097152 | tf_op jit(solution)/shard_map/gram_partial/pallas_call | solution.py:218
  52.0 0.1 collective-permute-start.9
  52.1 1.2 %collective-permute-done.9.refs_0_ = f32[32,128]{1,0:T(8,128)S(1)} collective-permute-done((f32[32,128]{1,0:T(8,128)S(1)}, f32[32,128]{1,0:T(8,128)S(1)}, u32[]{:S(2)}, u32[]{:S(2)}) %collective-permute-start.9) | collective-permute-done | bytes 16416 | tf_op jit(solution)/shard_map/ppermute | solution.py:326
  53.2 1.6 %collective-permute-start.10 = (f32[32,128]{1,0:T(8,128)S(1)}, f32[32,128]{1,0:T(8,128)S(1)}, u32[]{:S(2)}, u32[]{:S(2)}) collective-permute-start(f32[32,128]{1,0:T(8,128)S(1)} %sum_over.2.refs_3_), channel_id=1, source_target_pairs={{0,6},{1,7},{2,4},{3,5},{4,2},{5,3},{6,0},{7,1},{8,14},{9,15},{10,... | collective-permute-start | bytes 49160 | tf_op jit(solution)/shard_map/ppermute | solution.py:326
  54.9 1.3 %collective-permute-start.11 = (f32[32,128]{1,0:T(8,128)S(1)}, f32[32,128]{1,0:T(8,128)S(1)}, u32[]{:S(2)}, u32[]{:S(2)}) collective-permute-start(f32[32,128]{1,0:T(8,128)S(1)} %sum_over.2.refs_3_), channel_id=1, source_target_pairs={{0,4},{1,5},{2,6},{3,7},{4,0},{5,1},{6,2},{7,3},{8,12},{9,13},{10,... | collective-permute-start | bytes 49160 | tf_op jit(solution)/shard_map/ppermute | solution.py:326
  56.2 0.5 collective-permute-start.12
  56.7 1.1 %collective-permute-done.10.refs_0_ = f32[32,128]{1,0:T(8,128)S(1)} collective-permute-done((f32[32,128]{1,0:T(8,128)S(1)}, f32[32,128]{1,0:T(8,128)S(1)}, u32[]{:S(2)}, u32[]{:S(2)}) %collective-permute-start.10) | collective-permute-done | bytes 16416 | tf_op jit(solution)/shard_map/ppermute | solution.py:326
  57.9 0.7 collective-permute-done.11.refs_1_
  58.6 1.3 %collective-permute-done.12.refs_2_ = f32[32,128]{1,0:T(8,128)S(1)} collective-permute-done((f32[32,128]{1,0:T(8,128)S(1)}, f32[32,128]{1,0:T(8,128)S(1)}, u32[]{:S(2)}, u32[]{:S(2)}) %collective-permute-start.12) | collective-permute-done | bytes 16416 | tf_op jit(solution)/shard_map/ppermute | solution.py:326
  60.0 6.0 %collective-permute-start.13 = (f32[32,128]{1,0:T(8,128)S(1)}, f32[32,128]{1,0:T(8,128)S(1)}, u32[]{:S(2)}, u32[]{:S(2)}) collective-permute-start(f32[32,128]{1,0:T(8,128)S(1)} %sum_over.3.refs_3_), channel_id=1, source_target_pairs={{0,16},{1,17},{2,18},{3,19},{4,20},{5,21},{6,22},{7,23},{8,24},{9,... | collective-permute-start | bytes 49160 | tf_op jit(solution)/shard_map/ppermute | solution.py:326
  65.9 0.0 collective-permute-start.14
  65.9 1.5 %collective-permute-start.15 = (f32[32,128]{1,0:T(8,128)S(1)}, f32[32,128]{1,0:T(8,128)S(1)}, u32[]{:S(2)}, u32[]{:S(2)}) collective-permute-start(f32[32,128]{1,0:T(8,128)S(1)} %sum_over.3.refs_3_), channel_id=1, source_target_pairs={{0,24},{1,25},{2,26},{3,27},{4,28},{5,29},{6,30},{7,31},{8,16},{9,... | collective-permute-start | bytes 49160 | tf_op jit(solution)/shard_map/ppermute | solution.py:326
  67.5 0.2 collective-permute-done.13.refs_0_
  67.6 2.0 %collective-permute-done.14.refs_1_ = f32[32,128]{1,0:T(8,128)S(1)} collective-permute-done((f32[32,128]{1,0:T(8,128)S(1)}, f32[32,128]{1,0:T(8,128)S(1)}, u32[]{:S(2)}, u32[]{:S(2)}) %collective-permute-start.14) | collective-permute-done | bytes 16416 | tf_op jit(solution)/shard_map/ppermute | solution.py:326
  69.7 1.8 %collective-permute-done.15.refs_2_ = f32[32,128]{1,0:T(8,128)S(1)} collective-permute-done((f32[32,128]{1,0:T(8,128)S(1)}, f32[32,128]{1,0:T(8,128)S(1)}, u32[]{:S(2)}, u32[]{:S(2)}) %collective-permute-start.15) | collective-permute-done | bytes 16416 | tf_op jit(solution)/shard_map/ppermute | solution.py:326
  71.5 3.5 %solve_and_project.1 = (f32[1,8]{1,0:T(1,128)}, f32[2,32,256]{2,1,0:T(8,128)}) custom-call(f32[32,128]{1,0:T(8,128)S(1)} %collective-permute-done.13.refs_0_, f32[32,128]{1,0:T(8,128)S(1)} %collective-permute-done.14.refs_1_, f32[32,128]{1,0:T(8,128)S(1)} %collective-permute-done.15.refs_2_, f32[32,128]{1,0:T(8,128)S(1)} %sum_over.3.refs_3_, ...), custom_call_target="tpu_custom_call" | custom-call | tf_op jit(solution)/shard_map/solve_and_project/pallas_call | solution.py:395
  (2 shorter events, 0.0 us)
Async XLA Ops:
  3.1 19.6 %collective-permute-start = (bf16[8,32,256]{2,1,0:T(8,128)(2,1)S(1)}, bf16[8,32,256]{2,1,0:T(8,128)(2,1)S(1)}, u32[]{:S(2)}, u32[]{:S(2)}) collective-permute-start(bf16[8,32,256]{2,1,0:T(8,128)(2,1)S(1)} %get-tuple-element.20), channel_id=1, source_target_pairs={{0,16},{4,20},{8,24},{12,28},{16,0},{20,4},{24,8},{28,12},{1,17},{... | collective-permute-start | bytes 393224 | tf_op jit(solution)/shard_map/ppermute | solution.py:414
  7.2 19.7 %collective-permute-start.1 = (bf16[8,32,256]{2,1,0:T(8,128)(2,1)S(1)}, bf16[8,32,256]{2,1,0:T(8,128)(2,1)S(1)}, u32[]{:S(2)}, u32[]{:S(2)}) collective-permute-start(bf16[8,32,256]{2,1,0:T(8,128)(2,1)S(1)} %get-tuple-element.21), channel_id=1, source_target_pairs={{0,20},{4,16},{8,28},{12,24},{16,4},{20,0},{24,12},{28,8},{1,21},{... | collective-permute-start | bytes 393224 | tf_op jit(solution)/shard_map/ppermute | solution.py:414
  8.4 29.8 %copy-start.1 = (f32[8]{0:T(128)S(1)}, f32[8]{0:T(128)}, u32[]{:S(2)}) copy-start(f32[8]{0:T(128)} %param.7) | copy-start | bytes 100
  8.4 29.9 %copy-start = (s32[8,256]{1,0:T(8,128)S(1)}, s32[8,256]{1,0:T(8,128)}, u32[]{:S(2)}) copy-start(s32[8,256]{1,0:T(8,128)} %spins_ref.1) | copy-start | bytes 24580
  11.8 21.7 %collective-permute-start.2 = (bf16[8,32,256]{2,1,0:T(8,128)(2,1)S(1)}, bf16[8,32,256]{2,1,0:T(8,128)(2,1)S(1)}, u32[]{:S(2)}, u32[]{:S(2)}) collective-permute-start(bf16[8,32,256]{2,1,0:T(8,128)(2,1)S(1)} %get-tuple-element.28), channel_id=1, source_target_pairs={{0,16},{4,20},{8,24},{12,28},{16,0},{20,4},{24,8},{28,12},{1,17},{... | collective-permute-start | bytes 393224 | tf_op jit(solution)/shard_map/ppermute | solution.py:414
  14.4 23.6 %collective-permute-start.3 = (bf16[8,32,256]{2,1,0:T(8,128)(2,1)S(1)}, bf16[8,32,256]{2,1,0:T(8,128)(2,1)S(1)}, u32[]{:S(2)}, u32[]{:S(2)}) collective-permute-start(bf16[8,32,256]{2,1,0:T(8,128)(2,1)S(1)} %get-tuple-element.29), channel_id=1, source_target_pairs={{0,20},{4,16},{8,28},{12,24},{16,4},{20,0},{24,12},{28,8},{1,21},{... | collective-permute-start | bytes 393224 | tf_op jit(solution)/shard_map/ppermute | solution.py:414
  14.5 30.9 %collective-permute-start.4 = (bf16[8,64,256]{2,1,0:T(8,128)(2,1)}, bf16[8,64,256]{2,1,0:T(8,128)(2,1)S(1)}, u32[]{:S(2)}, u32[]{:S(2)}) collective-permute-start(bf16[8,64,256]{2,1,0:T(8,128)(2,1)} %get-tuple-element.30), channel_id=1, source_target_pairs={{0,12},{4,8},{8,4},{12,0},{16,28},{20,24},{24,20},{28,16},{1,13},{... | collective-permute-start | bytes 786440 | tf_op jit(solution)/shard_map/ppermute | solution.py:414
  22.7 22.7 %collective-permute-start.5 = (bf16[8,64,256]{2,1,0:T(8,128)(2,1)}, bf16[8,64,256]{2,1,0:T(8,128)(2,1)S(1)}, u32[]{:S(2)}, u32[]{:S(2)}) collective-permute-start(bf16[8,64,256]{2,1,0:T(8,128)(2,1)} %get-tuple-element.31), channel_id=1, source_target_pairs={{0,24},{4,28},{8,16},{12,20},{16,8},{20,12},{24,0},{28,4},{1,25},{... | collective-permute-start | bytes 786440 | tf_op jit(solution)/shard_map/ppermute | solution.py:414
  26.8 21.7 %collective-permute-start.6 = (bf16[8,64,256]{2,1,0:T(8,128)(2,1)S(1)}, bf16[8,64,256]{2,1,0:T(8,128)(2,1)S(1)}, u32[]{:S(2)}, u32[]{:S(2)}) collective-permute-start(bf16[8,64,256]{2,1,0:T(8,128)(2,1)S(1)} %get-tuple-element.32), channel_id=1, source_target_pairs={{0,8},{4,12},{8,0},{12,4},{16,24},{20,28},{24,16},{28,20},{1,9},{5... | collective-permute-start | bytes 786440 | tf_op jit(solution)/shard_map/ppermute | solution.py:414
  33.4 15.1 %collective-permute-start.7 = (bf16[8,64,256]{2,1,0:T(8,128)(2,1)}, bf16[8,64,256]{2,1,0:T(8,128)(2,1)S(1)}, u32[]{:S(2)}, u32[]{:S(2)}) collective-permute-start(bf16[8,64,256]{2,1,0:T(8,128)(2,1)} %get-tuple-element.33), channel_id=1, source_target_pairs={{0,28},{4,24},{8,20},{12,16},{16,12},{20,8},{24,4},{28,0},{1,29},{... | collective-permute-start | bytes 786440 | tf_op jit(solution)/shard_map/ppermute | solution.py:414
  38.1 12.4 %collective-permute-start.8 = (bf16[8,64,256]{2,1,0:T(8,128)(2,1)S(1)}, bf16[8,64,256]{2,1,0:T(8,128)(2,1)S(1)}, u32[]{:S(2)}, u32[]{:S(2)}) collective-permute-start(bf16[8,64,256]{2,1,0:T(8,128)(2,1)S(1)} %get-tuple-element.34), channel_id=1, source_target_pairs={{0,4},{4,0},{8,12},{12,8},{16,20},{20,16},{24,28},{28,24},{1,5},{5... | collective-permute-start | bytes 786440 | tf_op jit(solution)/shard_map/ppermute | solution.py:414
  52.0 1.2 %collective-permute-start.9 = (f32[32,128]{1,0:T(8,128)S(1)}, f32[32,128]{1,0:T(8,128)S(1)}, u32[]{:S(2)}, u32[]{:S(2)}) collective-permute-start(f32[32,128]{1,0:T(8,128)S(1)} %gram_partial.1.refs_1_), channel_id=1, source_target_pairs={{0,1},{1,0},{2,3},{3,2},{4,5},{5,4},{6,7},{7,6},{8,9},{9,8},{10,11... | collective-permute-start | bytes 49160 | tf_op jit(solution)/shard_map/ppermute | solution.py:326
  53.2 4.6 %collective-permute-start.10 = (f32[32,128]{1,0:T(8,128)S(1)}, f32[32,128]{1,0:T(8,128)S(1)}, u32[]{:S(2)}, u32[]{:S(2)}) collective-permute-start(f32[32,128]{1,0:T(8,128)S(1)} %sum_over.2.refs_3_), channel_id=1, source_target_pairs={{0,6},{1,7},{2,4},{3,5},{4,2},{5,3},{6,0},{7,1},{8,14},{9,15},{10,... | collective-permute-start | bytes 49160 | tf_op jit(solution)/shard_map/ppermute | solution.py:326
  54.9 3.7 %collective-permute-start.11 = (f32[32,128]{1,0:T(8,128)S(1)}, f32[32,128]{1,0:T(8,128)S(1)}, u32[]{:S(2)}, u32[]{:S(2)}) collective-permute-start(f32[32,128]{1,0:T(8,128)S(1)} %sum_over.2.refs_3_), channel_id=1, source_target_pairs={{0,4},{1,5},{2,6},{3,7},{4,0},{5,1},{6,2},{7,3},{8,12},{9,13},{10,... | collective-permute-start | bytes 49160 | tf_op jit(solution)/shard_map/ppermute | solution.py:326
  56.2 3.7 %collective-permute-start.12 = (f32[32,128]{1,0:T(8,128)S(1)}, f32[32,128]{1,0:T(8,128)S(1)}, u32[]{:S(2)}, u32[]{:S(2)}) collective-permute-start(f32[32,128]{1,0:T(8,128)S(1)} %sum_over.2.refs_3_), channel_id=1, source_target_pairs={{0,2},{1,3},{2,0},{3,1},{4,6},{5,7},{6,4},{7,5},{8,10},{9,11},{10,... | collective-permute-start | bytes 49160 | tf_op jit(solution)/shard_map/ppermute | solution.py:326
  60.0 7.7 %collective-permute-start.13 = (f32[32,128]{1,0:T(8,128)S(1)}, f32[32,128]{1,0:T(8,128)S(1)}, u32[]{:S(2)}, u32[]{:S(2)}) collective-permute-start(f32[32,128]{1,0:T(8,128)S(1)} %sum_over.3.refs_3_), channel_id=1, source_target_pairs={{0,16},{1,17},{2,18},{3,19},{4,20},{5,21},{6,22},{7,23},{8,24},{9,... | collective-permute-start | bytes 49160 | tf_op jit(solution)/shard_map/ppermute | solution.py:326
  65.9 3.7 %collective-permute-start.14 = (f32[32,128]{1,0:T(8,128)S(1)}, f32[32,128]{1,0:T(8,128)S(1)}, u32[]{:S(2)}, u32[]{:S(2)}) collective-permute-start(f32[32,128]{1,0:T(8,128)S(1)} %sum_over.3.refs_3_), channel_id=1, source_target_pairs={{0,8},{1,9},{2,10},{3,11},{4,12},{5,13},{6,14},{7,15},{8,0},{9,1},... | collective-permute-start | bytes 49160 | tf_op jit(solution)/shard_map/ppermute | solution.py:326
  65.9 5.5 %collective-permute-start.15 = (f32[32,128]{1,0:T(8,128)S(1)}, f32[32,128]{1,0:T(8,128)S(1)}, u32[]{:S(2)}, u32[]{:S(2)}) collective-permute-start(f32[32,128]{1,0:T(8,128)S(1)} %sum_over.3.refs_3_), channel_id=1, source_target_pairs={{0,24},{1,25},{2,26},{3,27},{4,28},{5,29},{6,30},{7,31},{8,16},{9,... | collective-permute-start | bytes 49160 | tf_op jit(solution)/shard_map/ppermute | solution.py:326

commit v24 on v23

--- a/solution.py
+++ b/solution.py
@@ -337,7 +337,7 @@
 
 def rounds(samp, layer):
     masks = [1 << bit for bit in range(1, layer.bit_length() - 1)]
-    masks += [layer, layer * (samp - 2)]
+    masks += [layer * (samp - 2), layer]
     masks += [layer << bit for bit in range(1, samp.bit_length() - 2)]
     later = zip(masks[::2], masks[1::2] + [0] * (len(masks) % 2))
     return [[1]] + [[a, b, a ^ b] if b else [a] for a, b in later]

time: 75.2 us -> 73.9 us (0.983)
  starting transfers between devices: 29.4 us -> 27.9 us
    ppermute x7, starting transfers between devices: 11.1 us -> 9.54 us  [partners(): return [lax.ppermute(value, axes, perm) for perm in perms] + [value]]
  transfers between devices with their start and end apart: 16 -> 16, of which waited for: 14 -> 12; matrix products, arithmetic and copies ran while one was open for 0% -> 0% of each run, Pallas kernels for 5% -> 5%
where the time goes in v24:
time: 73.9 us; the launch traced here: 73.7 us
  waiting for transfers between devices  34.1 us (46%)
  starting transfers between devices  27.9 us (38%)
  Pallas kernels  11 us (15%)
    ppermute x9, waiting for transfers between devices, body(): blocks[k][part] = lax.ppermute(blocks[k][part], 'samp', perm)  25.4 us
    ppermute x9, starting transfers between devices, body(): blocks[k][part] = lax.ppermute(blocks[k][part], 'samp', perm)  18.3 us
    ppermute x7, starting transfers between devices, partners(): return [lax.ppermute(value, axes, perm) for perm in perms] + [value]  9.54 us
    ppermute x7, waiting for transfers between devices, partners(): return [lax.ppermute(value, axes, perm) for perm in perms] + [value]  8.63 us
    pallas_call x2, Pallas kernels, jac_rows(): pl.pallas_call(functools.partial(jac_kernel, part * mats, joined), in_spe...  5.74 us
    pallas_call x1, Pallas kernels, solve_and_project(): pl.pallas_call(functools.partial(solve_kernel, len(sums), len(blocks)), o...  3.52 us
    pallas_call x1, Pallas kernels, gram_partial(): pl.pallas_call(functools.partial(gram_kernel, len(blocks)), out_shape=jax...  1.51 us
  transfers between devices with their start and end apart: 16, of which 12 were waited for; matrix products, arithmetic and copies ran while one was open for 0% of the time, Pallas kernels for 5%

profile of v24, /device:TPU:0, one launch (start us, length us, event | category | flops | bytes accessed | tf_op | source)
XLA Modules:
  0.0 73.7 jit_solution(13290023133854103827)
XLA Ops:
  0.6 2.4 %jac_rows.2 = (bf16[8,32,256]{2,1,0:T(8,128)(2,1)S(1)}, bf16[8,32,256]{2,1,0:T(8,128)(2,1)S(1)}, bf16[8,32,256]{2,1,0:T(8,128)(2,1)S(1)}, bf16[8,32,256]{2,1,0:T...) custom-call(bf16[8,2,256,256]{3,2,1,0:T(8,128)(2,1)} %act_hbm.3, ...), custom_call_target="tpu_custom_call" | custom-call | flops 268435456 | bytes 3145728 | tf_op jit(solution)/shard_map/jac_rows/pallas_call | solution.py:108
  3.1 4.1 %collective-permute-start = (bf16[8,32,256]{2,1,0:T(8,128)(2,1)S(1)}, bf16[8,32,256]{2,1,0:T(8,128)(2,1)S(1)}, u32[]{:S(2)}, u32[]{:S(2)}) collective-permute-start(bf16[8,32,256]{2,1,0:T(8,128)(2,1)S(1)} %get-tuple-element.20), channel_id=1, source_target_pairs={{0,16},{4,20},{8,24},{12,28},{16,0},{20,4},{24,8},{28,12},{1,17},{... | collective-permute-start | bytes 393224 | tf_op jit(solution)/shard_map/ppermute | solution.py:414
  7.2 1.3 %collective-permute-start.1 = (bf16[8,32,256]{2,1,0:T(8,128)(2,1)S(1)}, bf16[8,32,256]{2,1,0:T(8,128)(2,1)S(1)}, u32[]{:S(2)}, u32[]{:S(2)}) collective-permute-start(bf16[8,32,256]{2,1,0:T(8,128)(2,1)S(1)} %get-tuple-element.21), channel_id=1, source_target_pairs={{0,20},{4,16},{8,28},{12,24},{16,4},{20,0},{24,12},{28,8},{1,21},{... | collective-permute-start | bytes 393224 | tf_op jit(solution)/shard_map/ppermute | solution.py:414
  8.4 0.0 copy-start.1
  8.4 0.0 copy-start
  8.5 3.3 %jac_rows.3 = (bf16[8,64,256]{2,1,0:T(8,128)(2,1)S(1)}, bf16[8,64,256]{2,1,0:T(8,128)(2,1)S(1)}, bf16[8,64,256]{2,1,0:T(8,128)(2,1)S(1)}, bf16[8,64,256]{2,1,0:T...) custom-call(bf16[8,2,256,256]{3,2,1,0:T(8,128)(2,1)} %act_hbm.3, ...), custom_call_target="tpu_custom_call" | custom-call | flops 268435456 | bytes 3145728 | tf_op jit(solution)/shard_map/jac_rows/pallas_call | solution.py:108
  11.8 2.7 %collective-permute-start.2 = (bf16[8,32,256]{2,1,0:T(8,128)(2,1)S(1)}, bf16[8,32,256]{2,1,0:T(8,128)(2,1)S(1)}, u32[]{:S(2)}, u32[]{:S(2)}) collective-permute-start(bf16[8,32,256]{2,1,0:T(8,128)(2,1)S(1)} %get-tuple-element.28), channel_id=1, source_target_pairs={{0,16},{4,20},{8,24},{12,28},{16,0},{20,4},{24,8},{28,12},{1,17},{... | collective-permute-start | bytes 393224 | tf_op jit(solution)/shard_map/ppermute | solution.py:414
  14.4 0.0 collective-permute-start.3
  14.5 2.8 %collective-permute-start.4 = (bf16[8,64,256]{2,1,0:T(8,128)(2,1)}, bf16[8,64,256]{2,1,0:T(8,128)(2,1)S(1)}, u32[]{:S(2)}, u32[]{:S(2)}) collective-permute-start(bf16[8,64,256]{2,1,0:T(8,128)(2,1)} %get-tuple-element.30), channel_id=1, source_target_pairs={{0,12},{4,8},{8,4},{12,0},{16,28},{20,24},{24,20},{28,16},{1,13},{... | collective-permute-start | bytes 786440 | tf_op jit(solution)/shard_map/ppermute | solution.py:414
  17.3 5.4 %collective-permute-done.refs_0_.refs_4_ = bf16[8,32,256]{2,1,0:T(8,128)(2,1)S(1)} collective-permute-done((bf16[8,32,256]{2,1,0:T(8,128)(2,1)S(1)}, bf16[8,32,256]{2,1,0:T(8,128)(2,1)S(1)}, u32[]{:S(2)}, u32[]{:S(2)}) %collective-permute-start) | collective-permute-done | bytes 131104 | tf_op jit(solution)/shard_map/ppermute | solution.py:414
  22.7 2.9 %collective-permute-start.5 = (bf16[8,64,256]{2,1,0:T(8,128)(2,1)}, bf16[8,64,256]{2,1,0:T(8,128)(2,1)S(1)}, u32[]{:S(2)}, u32[]{:S(2)}) collective-permute-start(bf16[8,64,256]{2,1,0:T(8,128)(2,1)} %get-tuple-element.31), channel_id=1, source_target_pairs={{0,24},{4,28},{8,16},{12,20},{16,8},{20,12},{24,0},{28,4},{1,25},{... | collective-permute-start | bytes 786440 | tf_op jit(solution)/shard_map/ppermute | solution.py:414
  25.6 1.2 %collective-permute-done.1.refs_1_.refs_5_ = bf16[8,32,256]{2,1,0:T(8,128)(2,1)S(1)} collective-permute-done((bf16[8,32,256]{2,1,0:T(8,128)(2,1)S(1)}, bf16[8,32,256]{2,1,0:T(8,128)(2,1)S(1)}, u32[]{:S(2)}, u32[]{:S(2)}) %collective-permute-start.1) | collective-permute-done | bytes 131104 | tf_op jit(solution)/shard_map/ppermute | solution.py:414
  26.8 0.0 collective-permute-start.6
  26.8 6.6 %collective-permute-done.2.refs_2_.refs_6_ = bf16[8,32,256]{2,1,0:T(8,128)(2,1)S(1)} collective-permute-done((bf16[8,32,256]{2,1,0:T(8,128)(2,1)S(1)}, bf16[8,32,256]{2,1,0:T(8,128)(2,1)S(1)}, u32[]{:S(2)}, u32[]{:S(2)}) %collective-permute-start.2) | collective-permute-done | bytes 131104 | tf_op jit(solution)/shard_map/ppermute | solution.py:414
  33.4 4.3 %collective-permute-start.7 = (bf16[8,64,256]{2,1,0:T(8,128)(2,1)}, bf16[8,64,256]{2,1,0:T(8,128)(2,1)S(1)}, u32[]{:S(2)}, u32[]{:S(2)}) collective-permute-start(bf16[8,64,256]{2,1,0:T(8,128)(2,1)} %get-tuple-element.33), channel_id=1, source_target_pairs={{0,28},{4,24},{8,20},{12,16},{16,12},{20,8},{24,4},{28,0},{1,29},{... | collective-permute-start | bytes 786440 | tf_op jit(solution)/shard_map/ppermute | solution.py:414
  37.8 0.3 collective-permute-done.3.refs_3_.refs_7_
  38.1 0.2 collective-permute-start.8
  38.3 0.0 copy-done.1
  38.3 0.1 copy.6.offdiag_ref
  38.4 0.0 copy-done
  38.4 0.2 packed_energy.1.refs_10_
  38.6 6.8 %collective-permute-done.4.refs_4_.refs_8_ = bf16[8,64,256]{2,1,0:T(8,128)(2,1)S(1)} collective-permute-done((bf16[8,64,256]{2,1,0:T(8,128)(2,1)}, bf16[8,64,256]{2,1,0:T(8,128)(2,1)S(1)}, u32[]{:S(2)}, u32[]{:S(2)}) %collective-permute-start.4) | collective-permute-done | bytes 262176 | tf_op jit(solution)/shard_map/ppermute | solution.py:414
  45.3 0.0 collective-permute-done.5.refs_5_.refs_9_
  45.3 3.2 %collective-permute-done.6.refs_6_.refs_10_ = bf16[8,64,256]{2,1,0:T(8,128)(2,1)S(1)} collective-permute-done((bf16[8,64,256]{2,1,0:T(8,128)(2,1)S(1)}, bf16[8,64,256]{2,1,0:T(8,128)(2,1)S(1)}, u32[]{:S(2)}, u32[]{:S(2)}) %collective-permute-start.6) | collective-permute-done | bytes 262176 | tf_op jit(solution)/shard_map/ppermute | solution.py:414
  48.6 0.0 collective-permute-done.7.refs_7_.refs_11_
  48.6 1.9 %collective-permute-done.8.refs_8_.refs_12_ = bf16[8,64,256]{2,1,0:T(8,128)(2,1)S(1)} collective-permute-done((bf16[8,64,256]{2,1,0:T(8,128)(2,1)S(1)}, bf16[8,64,256]{2,1,0:T(8,128)(2,1)S(1)}, u32[]{:S(2)}, u32[]{:S(2)}) %collective-permute-start.8) | collective-permute-done | bytes 262176 | tf_op jit(solution)/shard_map/ppermute | solution.py:414
  50.5 1.5 %gram_partial.1.refs_1_ = f32[32,128]{1,0:T(8,128)S(1)} custom-call(bf16[8,32,256]{2,1,0:T(8,128)(2,1)S(1)} %collective-permute-done.refs_0_.refs_4_, bf16[8,32,256]{2,1,0:T(8,128)(2,1)S(1)} %collective-permute-done.1.refs_1_.refs_5_, bf16[8,32,256]{2,1,0:T(8,128)(2,1)S(1)} %collective-permute-done.2.refs_2_.refs_6_, ...), custom_call_target="tpu_custom_call" | custom-call | flops 134217728 | bytes 2097152 | tf_op jit(solution)/shard_map/gram_partial/pallas_call | solution.py:218
  52.0 0.1 collective-permute-start.9
  52.1 1.2 %collective-permute-done.9.refs_0_ = f32[32,128]{1,0:T(8,128)S(1)} collective-permute-done((f32[32,128]{1,0:T(8,128)S(1)}, f32[32,128]{1,0:T(8,128)S(1)}, u32[]{:S(2)}, u32[]{:S(2)}) %collective-permute-start.9) | collective-permute-done | bytes 16416 | tf_op jit(solution)/shard_map/ppermute | solution.py:326
  53.2 5.3 %collective-permute-start.10 = (f32[32,128]{1,0:T(8,128)S(1)}, f32[32,128]{1,0:T(8,128)S(1)}, u32[]{:S(2)}, u32[]{:S(2)}) collective-permute-start(f32[32,128]{1,0:T(8,128)S(1)} %sum_over.2.refs_3_), channel_id=1, source_target_pairs={{0,26},{1,27},{2,24},{3,25},{4,30},{5,31},{6,28},{7,29},{8,18},{9,... | collective-permute-start | bytes 49160 | tf_op jit(solution)/shard_map/ppermute | solution.py:326
  58.5 0.0 collective-permute-start.11
  58.5 0.6 collective-permute-start.12
  59.2 1.1 %collective-permute-done.10.refs_0_ = f32[32,128]{1,0:T(8,128)S(1)} collective-permute-done((f32[32,128]{1,0:T(8,128)S(1)}, f32[32,128]{1,0:T(8,128)S(1)}, u32[]{:S(2)}, u32[]{:S(2)}) %collective-permute-start.10) | collective-permute-done | bytes 16416 | tf_op jit(solution)/shard_map/ppermute | solution.py:326
  60.3 3.8 %collective-permute-done.11.refs_1_ = f32[32,128]{1,0:T(8,128)S(1)} collective-permute-done((f32[32,128]{1,0:T(8,128)S(1)}, f32[32,128]{1,0:T(8,128)S(1)}, u32[]{:S(2)}, u32[]{:S(2)}) %collective-permute-start.11) | collective-permute-done | bytes 16416 | tf_op jit(solution)/shard_map/ppermute | solution.py:326
  64.1 0.0 collective-permute-done.12.refs_2_
  64.1 0.3 collective-permute-start.13
  64.4 2.0 %collective-permute-start.14 = (f32[32,128]{1,0:T(8,128)S(1)}, f32[32,128]{1,0:T(8,128)S(1)}, u32[]{:S(2)}, u32[]{:S(2)}) collective-permute-start(f32[32,128]{1,0:T(8,128)S(1)} %sum_over.3.refs_3_), channel_id=1, source_target_pairs={{0,8},{1,9},{2,10},{3,11},{4,12},{5,13},{6,14},{7,15},{8,0},{9,1},... | collective-permute-start | bytes 49160 | tf_op jit(solution)/shard_map/ppermute | solution.py:326
  66.5 1.2 %collective-permute-start.15 = (f32[32,128]{1,0:T(8,128)S(1)}, f32[32,128]{1,0:T(8,128)S(1)}, u32[]{:S(2)}, u32[]{:S(2)}) collective-permute-start(f32[32,128]{1,0:T(8,128)S(1)} %sum_over.3.refs_3_), channel_id=1, source_target_pairs={{0,4},{1,5},{2,6},{3,7},{4,0},{5,1},{6,2},{7,3},{8,12},{9,13},{10,... | collective-permute-start | bytes 49160 | tf_op jit(solution)/shard_map/ppermute | solution.py:326
  67.6 1.1 %collective-permute-done.13.refs_0_ = f32[32,128]{1,0:T(8,128)S(1)} collective-permute-done((f32[32,128]{1,0:T(8,128)S(1)}, f32[32,128]{1,0:T(8,128)S(1)}, u32[]{:S(2)}, u32[]{:S(2)}) %collective-permute-start.13) | collective-permute-done | bytes 16416 | tf_op jit(solution)/shard_map/ppermute | solution.py:326
  68.8 0.0 collective-permute-done.14.refs_1_
  68.8 1.4 %collective-permute-done.15.refs_2_ = f32[32,128]{1,0:T(8,128)S(1)} collective-permute-done((f32[32,128]{1,0:T(8,128)S(1)}, f32[32,128]{1,0:T(8,128)S(1)}, u32[]{:S(2)}, u32[]{:S(2)}) %collective-permute-start.15) | collective-permute-done | bytes 16416 | tf_op jit(solution)/shard_map/ppermute | solution.py:326
  70.2 3.5 %solve_and_project.1 = (f32[1,8]{1,0:T(1,128)}, f32[2,32,256]{2,1,0:T(8,128)}) custom-call(f32[32,128]{1,0:T(8,128)S(1)} %collective-permute-done.13.refs_0_, f32[32,128]{1,0:T(8,128)S(1)} %collective-permute-done.14.refs_1_, f32[32,128]{1,0:T(8,128)S(1)} %collective-permute-done.15.refs_2_, f32[32,128]{1,0:T(8,128)S(1)} %sum_over.3.refs_3_, ...), custom_call_target="tpu_custom_call" | custom-call | tf_op jit(solution)/shard_map/solve_and_project/pallas_call | solution.py:395
  (2 shorter events, 0.0 us)
Async XLA Ops:
  3.1 19.6 %collective-permute-start = (bf16[8,32,256]{2,1,0:T(8,128)(2,1)S(1)}, bf16[8,32,256]{2,1,0:T(8,128)(2,1)S(1)}, u32[]{:S(2)}, u32[]{:S(2)}) collective-permute-start(bf16[8,32,256]{2,1,0:T(8,128)(2,1)S(1)} %get-tuple-element.20), channel_id=1, source_target_pairs={{0,16},{4,20},{8,24},{12,28},{16,0},{20,4},{24,8},{28,12},{1,17},{... | collective-permute-start | bytes 393224 | tf_op jit(solution)/shard_map/ppermute | solution.py:414
  7.2 19.7 %collective-permute-start.1 = (bf16[8,32,256]{2,1,0:T(8,128)(2,1)S(1)}, bf16[8,32,256]{2,1,0:T(8,128)(2,1)S(1)}, u32[]{:S(2)}, u32[]{:S(2)}) collective-permute-start(bf16[8,32,256]{2,1,0:T(8,128)(2,1)S(1)} %get-tuple-element.21), channel_id=1, source_target_pairs={{0,20},{4,16},{8,28},{12,24},{16,4},{20,0},{24,12},{28,8},{1,21},{... | collective-permute-start | bytes 393224 | tf_op jit(solution)/shard_map/ppermute | solution.py:414
  8.4 29.8 %copy-start.1 = (f32[8]{0:T(128)S(1)}, f32[8]{0:T(128)}, u32[]{:S(2)}) copy-start(f32[8]{0:T(128)} %param.7) | copy-start | bytes 100
  8.4 29.9 %copy-start = (s32[8,256]{1,0:T(8,128)S(1)}, s32[8,256]{1,0:T(8,128)}, u32[]{:S(2)}) copy-start(s32[8,256]{1,0:T(8,128)} %spins_ref.1) | copy-start | bytes 24580
  11.8 21.7 %collective-permute-start.2 = (bf16[8,32,256]{2,1,0:T(8,128)(2,1)S(1)}, bf16[8,32,256]{2,1,0:T(8,128)(2,1)S(1)}, u32[]{:S(2)}, u32[]{:S(2)}) collective-permute-start(bf16[8,32,256]{2,1,0:T(8,128)(2,1)S(1)} %get-tuple-element.28), channel_id=1, source_target_pairs={{0,16},{4,20},{8,24},{12,28},{16,0},{20,4},{24,8},{28,12},{1,17},{... | collective-permute-start | bytes 393224 | tf_op jit(solution)/shard_map/ppermute | solution.py:414
  14.4 23.6 %collective-permute-start.3 = (bf16[8,32,256]{2,1,0:T(8,128)(2,1)S(1)}, bf16[8,32,256]{2,1,0:T(8,128)(2,1)S(1)}, u32[]{:S(2)}, u32[]{:S(2)}) collective-permute-start(bf16[8,32,256]{2,1,0:T(8,128)(2,1)S(1)} %get-tuple-element.29), channel_id=1, source_target_pairs={{0,20},{4,16},{8,28},{12,24},{16,4},{20,0},{24,12},{28,8},{1,21},{... | collective-permute-start | bytes 393224 | tf_op jit(solution)/shard_map/ppermute | solution.py:414
  14.5 30.9 %collective-permute-start.4 = (bf16[8,64,256]{2,1,0:T(8,128)(2,1)}, bf16[8,64,256]{2,1,0:T(8,128)(2,1)S(1)}, u32[]{:S(2)}, u32[]{:S(2)}) collective-permute-start(bf16[8,64,256]{2,1,0:T(8,128)(2,1)} %get-tuple-element.30), channel_id=1, source_target_pairs={{0,12},{4,8},{8,4},{12,0},{16,28},{20,24},{24,20},{28,16},{1,13},{... | collective-permute-start | bytes 786440 | tf_op jit(solution)/shard_map/ppermute | solution.py:414
  22.7 22.7 %collective-permute-start.5 = (bf16[8,64,256]{2,1,0:T(8,128)(2,1)}, bf16[8,64,256]{2,1,0:T(8,128)(2,1)S(1)}, u32[]{:S(2)}, u32[]{:S(2)}) collective-permute-start(bf16[8,64,256]{2,1,0:T(8,128)(2,1)} %get-tuple-element.31), channel_id=1, source_target_pairs={{0,24},{4,28},{8,16},{12,20},{16,8},{20,12},{24,0},{28,4},{1,25},{... | collective-permute-start | bytes 786440 | tf_op jit(solution)/shard_map/ppermute | solution.py:414
  26.8 21.7 %collective-permute-start.6 = (bf16[8,64,256]{2,1,0:T(8,128)(2,1)S(1)}, bf16[8,64,256]{2,1,0:T(8,128)(2,1)S(1)}, u32[]{:S(2)}, u32[]{:S(2)}) collective-permute-start(bf16[8,64,256]{2,1,0:T(8,128)(2,1)S(1)} %get-tuple-element.32), channel_id=1, source_target_pairs={{0,8},{4,12},{8,0},{12,4},{16,24},{20,28},{24,16},{28,20},{1,9},{5... | collective-permute-start | bytes 786440 | tf_op jit(solution)/shard_map/ppermute | solution.py:414
  33.4 15.1 %collective-permute-start.7 = (bf16[8,64,256]{2,1,0:T(8,128)(2,1)}, bf16[8,64,256]{2,1,0:T(8,128)(2,1)S(1)}, u32[]{:S(2)}, u32[]{:S(2)}) collective-permute-start(bf16[8,64,256]{2,1,0:T(8,128)(2,1)} %get-tuple-element.33), channel_id=1, source_target_pairs={{0,28},{4,24},{8,20},{12,16},{16,12},{20,8},{24,4},{28,0},{1,29},{... | collective-permute-start | bytes 786440 | tf_op jit(solution)/shard_map/ppermute | solution.py:414
  38.1 12.4 %collective-permute-start.8 = (bf16[8,64,256]{2,1,0:T(8,128)(2,1)S(1)}, bf16[8,64,256]{2,1,0:T(8,128)(2,1)S(1)}, u32[]{:S(2)}, u32[]{:S(2)}) collective-permute-start(bf16[8,64,256]{2,1,0:T(8,128)(2,1)S(1)} %get-tuple-element.34), channel_id=1, source_target_pairs={{0,4},{4,0},{8,12},{12,8},{16,20},{20,16},{24,28},{28,24},{1,5},{5... | collective-permute-start | bytes 786440 | tf_op jit(solution)/shard_map/ppermute | solution.py:414
  52.0 1.2 %collective-permute-start.9 = (f32[32,128]{1,0:T(8,128)S(1)}, f32[32,128]{1,0:T(8,128)S(1)}, u32[]{:S(2)}, u32[]{:S(2)}) collective-permute-start(f32[32,128]{1,0:T(8,128)S(1)} %gram_partial.1.refs_1_), channel_id=1, source_target_pairs={{0,1},{1,0},{2,3},{3,2},{4,5},{5,4},{6,7},{7,6},{8,9},{9,8},{10,11... | collective-permute-start | bytes 49160 | tf_op jit(solution)/shard_map/ppermute | solution.py:326
  53.2 7.0 %collective-permute-start.10 = (f32[32,128]{1,0:T(8,128)S(1)}, f32[32,128]{1,0:T(8,128)S(1)}, u32[]{:S(2)}, u32[]{:S(2)}) collective-permute-start(f32[32,128]{1,0:T(8,128)S(1)} %sum_over.2.refs_3_), channel_id=1, source_target_pairs={{0,26},{1,27},{2,24},{3,25},{4,30},{5,31},{6,28},{7,29},{8,18},{9,... | collective-permute-start | bytes 49160 | tf_op jit(solution)/shard_map/ppermute | solution.py:326
  58.5 5.5 %collective-permute-start.11 = (f32[32,128]{1,0:T(8,128)S(1)}, f32[32,128]{1,0:T(8,128)S(1)}, u32[]{:S(2)}, u32[]{:S(2)}) collective-permute-start(f32[32,128]{1,0:T(8,128)S(1)} %sum_over.2.refs_3_), channel_id=1, source_target_pairs={{0,24},{1,25},{2,26},{3,27},{4,28},{5,29},{6,30},{7,31},{8,16},{9,... | collective-permute-start | bytes 49160 | tf_op jit(solution)/shard_map/ppermute | solution.py:326
  58.5 5.5 %collective-permute-start.12 = (f32[32,128]{1,0:T(8,128)S(1)}, f32[32,128]{1,0:T(8,128)S(1)}, u32[]{:S(2)}, u32[]{:S(2)}) collective-permute-start(f32[32,128]{1,0:T(8,128)S(1)} %sum_over.2.refs_3_), channel_id=1, source_target_pairs={{0,2},{1,3},{2,0},{3,1},{4,6},{5,7},{6,4},{7,5},{8,10},{9,11},{10,... | collective-permute-start | bytes 49160 | tf_op jit(solution)/shard_map/ppermute | solution.py:326
  64.1 4.7 %collective-permute-start.13 = (f32[32,128]{1,0:T(8,128)S(1)}, f32[32,128]{1,0:T(8,128)S(1)}, u32[]{:S(2)}, u32[]{:S(2)}) collective-permute-start(f32[32,128]{1,0:T(8,128)S(1)} %sum_over.3.refs_3_), channel_id=1, source_target_pairs={{0,12},{1,13},{2,14},{3,15},{4,8},{5,9},{6,10},{7,11},{8,4},{9,5},... | collective-permute-start | bytes 49160 | tf_op jit(solution)/shard_map/ppermute | solution.py:326
  64.4 4.4 %collective-permute-start.14 = (f32[32,128]{1,0:T(8,128)S(1)}, f32[32,128]{1,0:T(8,128)S(1)}, u32[]{:S(2)}, u32[]{:S(2)}) collective-permute-start(f32[32,128]{1,0:T(8,128)S(1)} %sum_over.3.refs_3_), channel_id=1, source_target_pairs={{0,8},{1,9},{2,10},{3,11},{4,12},{5,13},{6,14},{7,15},{8,0},{9,1},... | collective-permute-start | bytes 49160 | tf_op jit(solution)/shard_map/ppermute | solution.py:326
  66.5 3.7 %collective-permute-start.15 = (f32[32,128]{1,0:T(8,128)S(1)}, f32[32,128]{1,0:T(8,128)S(1)}, u32[]{:S(2)}, u32[]{:S(2)}) collective-permute-start(f32[32,128]{1,0:T(8,128)S(1)} %sum_over.3.refs_3_), channel_id=1, source_target_pairs={{0,4},{1,5},{2,6},{3,7},{4,0},{5,1},{6,2},{7,3},{8,12},{9,13},{10,... | collective-permute-start | bytes 49160 | tf_op jit(solution)/shard_map/ppermute | solution.py:326

commit v25 on v24

--- a/solution.py
+++ b/solution.py
@@ -55,18 +55,16 @@
     samples, mats, _, d = held.shape
     share = d // len(out_refs)
     me = lax.axis_index("samp")
+    group = 2
     copies = []
-    for s in range(samples):
-        here = (s, pl.ds(first_mat, mats))
-        copies.append(
-            (
-                pltpu.make_async_copy(act_hbm.at[here], act_buf.at[s], sems.at[0, s]),
-                pltpu.make_async_copy(cot_hbm.at[here], cot_buf.at[s], sems.at[1, s]),
-            )
-        )
-    for pair in copies:
-        for copy in pair:
-            copy.start()
+    for first in range(0, samples, group):
+        here = pl.ds(first, group)
+        mine = (here, pl.ds(first_mat, mats))
+        sem = first // group
+        copies.append(pltpu.make_async_copy(act_hbm.at[mine], act_buf.at[here], sems.at[0, sem]))
+        copies.append(pltpu.make_async_copy(cot_hbm.at[mine], cot_buf.at[here], sems.at[1, sem]))
+    for copy in copies:
+        copy.start()
     for k, ref in zip(joined, before):
         out_refs[k][:, : ref.shape[1]] = ref[...]
 
@@ -78,12 +76,10 @@
                 rows = jnp.concatenate(rows, axis=0).astype(BF16)
                 out_ref[s, out_ref.shape[1] - mats * share :] = rows
 
-    group = 2
     for first in range(0, samples, group):
         here = range(first, first + group)
-        for s in here:
-            for copy in copies[s]:
-                copy.wait()
+        copies[first].wait()
+        copies[first + 1].wait()
         for s in here:
             for m in range(mats):
                 held[s, m] = lax.dot_general(
@@ -368,9 +364,8 @@
     gram = (raw - col_mean - row_mean + mean) * scale
     eps = (raw - col_mean) * F32(1.0 / total**0.5)
     on_diag = row == lane
-    trace = jnp.sum(
-        jnp.sum(jnp.where(on_diag, gram, F32(0.0)), axis=1, keepdims=True), axis=0, keepdims=True
-    )
+    diag = jnp.where(on_diag, raw, F32(0.0))
+    trace = jnp.sum(jnp.sum(diag, axis=0, keepdims=True), axis=1, keepdims=True) * scale - mean
     shift = F32(shift_ratio) * trace * scale
     system = jnp.where(inside, gram + jnp.where(on_diag, shift, F32(0.0)), eps)
     weights = eliminate(system, total)

time: 73.9 us -> 73.7 us (level)
  no operation moved by 1% of the time
where the time goes in v25:
time: 73.7 us; the launch traced here: 73.6 us
  waiting for transfers between devices  34.3 us (47%)
  starting transfers between devices  27.7 us (38%)
  Pallas kernels  10.8 us (15%)
    ppermute x9, waiting for transfers between devices, body(): blocks[k][part] = lax.ppermute(blocks[k][part], 'samp', perm)  25.7 us
    ppermute x9, starting transfers between devices, body(): blocks[k][part] = lax.ppermute(blocks[k][part], 'samp', perm)  18.1 us
    ppermute x7, starting transfers between devices, partners(): return [lax.ppermute(value, axes, perm) for perm in perms] + [value]  9.56 us
    ppermute x7, waiting for transfers between devices, partners(): return [lax.ppermute(value, axes, perm) for perm in perms] + [value]  8.62 us
    pallas_call x2, Pallas kernels, jac_rows(): pl.pallas_call(functools.partial(jac_kernel, part * mats, joined), in_spe...  5.6 us
    pallas_call x1, Pallas kernels, solve_and_project(): pl.pallas_call(functools.partial(solve_kernel, len(sums), len(blocks)), o...  3.45 us
    pallas_call x1, Pallas kernels, gram_partial(): pl.pallas_call(functools.partial(gram_kernel, len(blocks)), out_shape=jax...  1.51 us
  transfers between devices with their start and end apart: 16, of which 12 were waited for; matrix products, arithmetic and copies ran while one was open for 0% of the time, Pallas kernels for 5%

profile of v25, /device:TPU:0, one launch (start us, length us, event | category | flops | bytes accessed | tf_op | source)
XLA Modules:
  0.0 73.6 jit_solution(6030448705131262489)
XLA Ops:
  0.6 2.3 %jac_rows.2 = (bf16[8,32,256]{2,1,0:T(8,128)(2,1)S(1)}, bf16[8,32,256]{2,1,0:T(8,128)(2,1)S(1)}, bf16[8,32,256]{2,1,0:T(8,128)(2,1)S(1)}, bf16[8,32,256]{2,1,0:T...) custom-call(bf16[8,2,256,256]{3,2,1,0:T(8,128)(2,1)} %act_hbm.3, ...), custom_call_target="tpu_custom_call" | custom-call | flops 268435456 | bytes 3145728 | tf_op jit(solution)/shard_map/jac_rows/pallas_call | solution.py:104
  3.0 4.1 %collective-permute-start = (bf16[8,32,256]{2,1,0:T(8,128)(2,1)S(1)}, bf16[8,32,256]{2,1,0:T(8,128)(2,1)S(1)}, u32[]{:S(2)}, u32[]{:S(2)}) collective-permute-start(bf16[8,32,256]{2,1,0:T(8,128)(2,1)S(1)} %get-tuple-element.20), channel_id=1, source_target_pairs={{0,16},{4,20},{8,24},{12,28},{16,0},{20,4},{24,8},{28,12},{1,17},{... | collective-permute-start | bytes 393224 | tf_op jit(solution)/shard_map/ppermute | solution.py:409
  7.1 1.3 %collective-permute-start.1 = (bf16[8,32,256]{2,1,0:T(8,128)(2,1)S(1)}, bf16[8,32,256]{2,1,0:T(8,128)(2,1)S(1)}, u32[]{:S(2)}, u32[]{:S(2)}) collective-permute-start(bf16[8,32,256]{2,1,0:T(8,128)(2,1)S(1)} %get-tuple-element.21), channel_id=1, source_target_pairs={{0,20},{4,16},{8,28},{12,24},{16,4},{20,0},{24,12},{28,8},{1,21},{... | collective-permute-start | bytes 393224 | tf_op jit(solution)/shard_map/ppermute | solution.py:409
  8.4 0.0 copy-start.1
  8.4 0.0 copy-start
  8.4 3.3 %jac_rows.3 = (bf16[8,64,256]{2,1,0:T(8,128)(2,1)S(1)}, bf16[8,64,256]{2,1,0:T(8,128)(2,1)S(1)}, bf16[8,64,256]{2,1,0:T(8,128)(2,1)S(1)}, bf16[8,64,256]{2,1,0:T...) custom-call(bf16[8,2,256,256]{3,2,1,0:T(8,128)(2,1)} %act_hbm.3, ...), custom_call_target="tpu_custom_call" | custom-call | flops 268435456 | bytes 3145728 | tf_op jit(solution)/shard_map/jac_rows/pallas_call | solution.py:104
  11.6 2.7 %collective-permute-start.2 = (bf16[8,32,256]{2,1,0:T(8,128)(2,1)S(1)}, bf16[8,32,256]{2,1,0:T(8,128)(2,1)S(1)}, u32[]{:S(2)}, u32[]{:S(2)}) collective-permute-start(bf16[8,32,256]{2,1,0:T(8,128)(2,1)S(1)} %get-tuple-element.28), channel_id=1, source_target_pairs={{0,16},{4,20},{8,24},{12,28},{16,0},{20,4},{24,8},{28,12},{1,17},{... | collective-permute-start | bytes 393224 | tf_op jit(solution)/shard_map/ppermute | solution.py:409
  14.3 0.0 collective-permute-start.3
  14.3 2.8 %collective-permute-start.4 = (bf16[8,64,256]{2,1,0:T(8,128)(2,1)}, bf16[8,64,256]{2,1,0:T(8,128)(2,1)S(1)}, u32[]{:S(2)}, u32[]{:S(2)}) collective-permute-start(bf16[8,64,256]{2,1,0:T(8,128)(2,1)} %get-tuple-element.30), channel_id=1, source_target_pairs={{0,12},{4,8},{8,4},{12,0},{16,28},{20,24},{24,20},{28,16},{1,13},{... | collective-permute-start | bytes 786440 | tf_op jit(solution)/shard_map/ppermute | solution.py:409
  17.1 5.6 %collective-permute-done.refs_0_.refs_4_ = bf16[8,32,256]{2,1,0:T(8,128)(2,1)S(1)} collective-permute-done((bf16[8,32,256]{2,1,0:T(8,128)(2,1)S(1)}, bf16[8,32,256]{2,1,0:T(8,128)(2,1)S(1)}, u32[]{:S(2)}, u32[]{:S(2)}) %collective-permute-start) | collective-permute-done | bytes 131104 | tf_op jit(solution)/shard_map/ppermute | solution.py:409
  22.7 2.8 %collective-permute-start.5 = (bf16[8,64,256]{2,1,0:T(8,128)(2,1)}, bf16[8,64,256]{2,1,0:T(8,128)(2,1)S(1)}, u32[]{:S(2)}, u32[]{:S(2)}) collective-permute-start(bf16[8,64,256]{2,1,0:T(8,128)(2,1)} %get-tuple-element.31), channel_id=1, source_target_pairs={{0,24},{4,28},{8,16},{12,20},{16,8},{20,12},{24,0},{28,4},{1,25},{... | collective-permute-start | bytes 786440 | tf_op jit(solution)/shard_map/ppermute | solution.py:409
  25.5 1.2 %collective-permute-done.1.refs_1_.refs_5_ = bf16[8,32,256]{2,1,0:T(8,128)(2,1)S(1)} collective-permute-done((bf16[8,32,256]{2,1,0:T(8,128)(2,1)S(1)}, bf16[8,32,256]{2,1,0:T(8,128)(2,1)S(1)}, u32[]{:S(2)}, u32[]{:S(2)}) %collective-permute-start.1) | collective-permute-done | bytes 131104 | tf_op jit(solution)/shard_map/ppermute | solution.py:409
  26.8 0.0 collective-permute-start.6
  26.8 6.7 %collective-permute-done.2.refs_2_.refs_6_ = bf16[8,32,256]{2,1,0:T(8,128)(2,1)S(1)} collective-permute-done((bf16[8,32,256]{2,1,0:T(8,128)(2,1)S(1)}, bf16[8,32,256]{2,1,0:T(8,128)(2,1)S(1)}, u32[]{:S(2)}, u32[]{:S(2)}) %collective-permute-start.2) | collective-permute-done | bytes 131104 | tf_op jit(solution)/shard_map/ppermute | solution.py:409
  33.4 4.3 %collective-permute-start.7 = (bf16[8,64,256]{2,1,0:T(8,128)(2,1)}, bf16[8,64,256]{2,1,0:T(8,128)(2,1)S(1)}, u32[]{:S(2)}, u32[]{:S(2)}) collective-permute-start(bf16[8,64,256]{2,1,0:T(8,128)(2,1)} %get-tuple-element.33), channel_id=1, source_target_pairs={{0,28},{4,24},{8,20},{12,16},{16,12},{20,8},{24,4},{28,0},{1,29},{... | collective-permute-start | bytes 786440 | tf_op jit(solution)/shard_map/ppermute | solution.py:409
  37.7 0.3 collective-permute-done.3.refs_3_.refs_7_
  38.0 0.2 collective-permute-start.8
  38.2 0.0 copy-done.1
  38.2 0.1 copy.6.offdiag_ref
  38.3 0.0 copy-done
  38.3 0.2 packed_energy.1.refs_10_
  38.5 6.8 %collective-permute-done.4.refs_4_.refs_8_ = bf16[8,64,256]{2,1,0:T(8,128)(2,1)S(1)} collective-permute-done((bf16[8,64,256]{2,1,0:T(8,128)(2,1)}, bf16[8,64,256]{2,1,0:T(8,128)(2,1)S(1)}, u32[]{:S(2)}, u32[]{:S(2)}) %collective-permute-start.4) | collective-permute-done | bytes 262176 | tf_op jit(solution)/shard_map/ppermute | solution.py:409
  45.3 0.0 collective-permute-done.5.refs_5_.refs_9_
  45.3 3.2 %collective-permute-done.6.refs_6_.refs_10_ = bf16[8,64,256]{2,1,0:T(8,128)(2,1)S(1)} collective-permute-done((bf16[8,64,256]{2,1,0:T(8,128)(2,1)S(1)}, bf16[8,64,256]{2,1,0:T(8,128)(2,1)S(1)}, u32[]{:S(2)}, u32[]{:S(2)}) %collective-permute-start.6) | collective-permute-done | bytes 262176 | tf_op jit(solution)/shard_map/ppermute | solution.py:409
  48.5 0.0 collective-permute-done.7.refs_7_.refs_11_
  48.5 1.9 %collective-permute-done.8.refs_8_.refs_12_ = bf16[8,64,256]{2,1,0:T(8,128)(2,1)S(1)} collective-permute-done((bf16[8,64,256]{2,1,0:T(8,128)(2,1)S(1)}, bf16[8,64,256]{2,1,0:T(8,128)(2,1)S(1)}, u32[]{:S(2)}, u32[]{:S(2)}) %collective-permute-start.8) | collective-permute-done | bytes 262176 | tf_op jit(solution)/shard_map/ppermute | solution.py:409
  50.4 1.5 %gram_partial.1.refs_1_ = f32[32,128]{1,0:T(8,128)S(1)} custom-call(bf16[8,32,256]{2,1,0:T(8,128)(2,1)S(1)} %collective-permute-done.refs_0_.refs_4_, bf16[8,32,256]{2,1,0:T(8,128)(2,1)S(1)} %collective-permute-done.1.refs_1_.refs_5_, bf16[8,32,256]{2,1,0:T(8,128)(2,1)S(1)} %collective-permute-done.2.refs_2_.refs_6_, ...), custom_call_target="tpu_custom_call" | custom-call | flops 134217728 | bytes 2097152 | tf_op jit(solution)/shard_map/gram_partial/pallas_call | solution.py:214
  51.9 0.1 collective-permute-start.9
  52.0 1.2 %collective-permute-done.9.refs_0_ = f32[32,128]{1,0:T(8,128)S(1)} collective-permute-done((f32[32,128]{1,0:T(8,128)S(1)}, f32[32,128]{1,0:T(8,128)S(1)}, u32[]{:S(2)}, u32[]{:S(2)}) %collective-permute-start.9) | collective-permute-done | bytes 16416 | tf_op jit(solution)/shard_map/ppermute | solution.py:322
  53.2 5.3 %collective-permute-start.10 = (f32[32,128]{1,0:T(8,128)S(1)}, f32[32,128]{1,0:T(8,128)S(1)}, u32[]{:S(2)}, u32[]{:S(2)}) collective-permute-start(f32[32,128]{1,0:T(8,128)S(1)} %sum_over.2.refs_3_), channel_id=1, source_target_pairs={{0,26},{1,27},{2,24},{3,25},{4,30},{5,31},{6,28},{7,29},{8,18},{9,... | collective-permute-start | bytes 49160 | tf_op jit(solution)/shard_map/ppermute | solution.py:322
  58.5 0.0 collective-permute-start.11
  58.5 0.6 collective-permute-start.12
  59.1 1.1 %collective-permute-done.10.refs_0_ = f32[32,128]{1,0:T(8,128)S(1)} collective-permute-done((f32[32,128]{1,0:T(8,128)S(1)}, f32[32,128]{1,0:T(8,128)S(1)}, u32[]{:S(2)}, u32[]{:S(2)}) %collective-permute-start.10) | collective-permute-done | bytes 16416 | tf_op jit(solution)/shard_map/ppermute | solution.py:322
  60.2 3.8 %collective-permute-done.11.refs_1_ = f32[32,128]{1,0:T(8,128)S(1)} collective-permute-done((f32[32,128]{1,0:T(8,128)S(1)}, f32[32,128]{1,0:T(8,128)S(1)}, u32[]{:S(2)}, u32[]{:S(2)}) %collective-permute-start.11) | collective-permute-done | bytes 16416 | tf_op jit(solution)/shard_map/ppermute | solution.py:322
  64.0 0.0 collective-permute-done.12.refs_2_
  64.0 0.3 collective-permute-start.13
  64.4 2.0 %collective-permute-start.14 = (f32[32,128]{1,0:T(8,128)S(1)}, f32[32,128]{1,0:T(8,128)S(1)}, u32[]{:S(2)}, u32[]{:S(2)}) collective-permute-start(f32[32,128]{1,0:T(8,128)S(1)} %sum_over.3.refs_3_), channel_id=1, source_target_pairs={{0,8},{1,9},{2,10},{3,11},{4,12},{5,13},{6,14},{7,15},{8,0},{9,1},... | collective-permute-start | bytes 49160 | tf_op jit(solution)/shard_map/ppermute | solution.py:322
  66.4 1.2 %collective-permute-start.15 = (f32[32,128]{1,0:T(8,128)S(1)}, f32[32,128]{1,0:T(8,128)S(1)}, u32[]{:S(2)}, u32[]{:S(2)}) collective-permute-start(f32[32,128]{1,0:T(8,128)S(1)} %sum_over.3.refs_3_), channel_id=1, source_target_pairs={{0,4},{1,5},{2,6},{3,7},{4,0},{5,1},{6,2},{7,3},{8,12},{9,13},{10,... | collective-permute-start | bytes 49160 | tf_op jit(solution)/shard_map/ppermute | solution.py:322
  67.6 1.1 %collective-permute-done.13.refs_0_ = f32[32,128]{1,0:T(8,128)S(1)} collective-permute-done((f32[32,128]{1,0:T(8,128)S(1)}, f32[32,128]{1,0:T(8,128)S(1)}, u32[]{:S(2)}, u32[]{:S(2)}) %collective-permute-start.13) | collective-permute-done | bytes 16416 | tf_op jit(solution)/shard_map/ppermute | solution.py:322
  68.7 0.0 collective-permute-done.14.refs_1_
  68.7 1.4 %collective-permute-done.15.refs_2_ = f32[32,128]{1,0:T(8,128)S(1)} collective-permute-done((f32[32,128]{1,0:T(8,128)S(1)}, f32[32,128]{1,0:T(8,128)S(1)}, u32[]{:S(2)}, u32[]{:S(2)}) %collective-permute-start.15) | collective-permute-done | bytes 16416 | tf_op jit(solution)/shard_map/ppermute | solution.py:322
  70.1 3.5 %solve_and_project.1 = (f32[1,8]{1,0:T(1,128)}, f32[2,32,256]{2,1,0:T(8,128)}) custom-call(f32[32,128]{1,0:T(8,128)S(1)} %collective-permute-done.13.refs_0_, f32[32,128]{1,0:T(8,128)S(1)} %collective-permute-done.14.refs_1_, f32[32,128]{1,0:T(8,128)S(1)} %collective-permute-done.15.refs_2_, f32[32,128]{1,0:T(8,128)S(1)} %sum_over.3.refs_3_, ...), custom_call_target="tpu_custom_call" | custom-call | tf_op jit(solution)/shard_map/solve_and_project/pallas_call | solution.py:390
  (2 shorter events, 0.0 us)
Async XLA Ops:
  3.0 19.8 %collective-permute-start = (bf16[8,32,256]{2,1,0:T(8,128)(2,1)S(1)}, bf16[8,32,256]{2,1,0:T(8,128)(2,1)S(1)}, u32[]{:S(2)}, u32[]{:S(2)}) collective-permute-start(bf16[8,32,256]{2,1,0:T(8,128)(2,1)S(1)} %get-tuple-element.20), channel_id=1, source_target_pairs={{0,16},{4,20},{8,24},{12,28},{16,0},{20,4},{24,8},{28,12},{1,17},{... | collective-permute-start | bytes 393224 | tf_op jit(solution)/shard_map/ppermute | solution.py:409
  7.1 19.7 %collective-permute-start.1 = (bf16[8,32,256]{2,1,0:T(8,128)(2,1)S(1)}, bf16[8,32,256]{2,1,0:T(8,128)(2,1)S(1)}, u32[]{:S(2)}, u32[]{:S(2)}) collective-permute-start(bf16[8,32,256]{2,1,0:T(8,128)(2,1)S(1)} %get-tuple-element.21), channel_id=1, source_target_pairs={{0,20},{4,16},{8,28},{12,24},{16,4},{20,0},{24,12},{28,8},{1,21},{... | collective-permute-start | bytes 393224 | tf_op jit(solution)/shard_map/ppermute | solution.py:409
  8.4 29.8 %copy-start.1 = (f32[8]{0:T(128)S(1)}, f32[8]{0:T(128)}, u32[]{:S(2)}) copy-start(f32[8]{0:T(128)} %param.7) | copy-start | bytes 100
  8.4 29.9 %copy-start = (s32[8,256]{1,0:T(8,128)S(1)}, s32[8,256]{1,0:T(8,128)}, u32[]{:S(2)}) copy-start(s32[8,256]{1,0:T(8,128)} %spins_ref.1) | copy-start | bytes 24580
  11.6 21.8 %collective-permute-start.2 = (bf16[8,32,256]{2,1,0:T(8,128)(2,1)S(1)}, bf16[8,32,256]{2,1,0:T(8,128)(2,1)S(1)}, u32[]{:S(2)}, u32[]{:S(2)}) collective-permute-start(bf16[8,32,256]{2,1,0:T(8,128)(2,1)S(1)} %get-tuple-element.28), channel_id=1, source_target_pairs={{0,16},{4,20},{8,24},{12,28},{16,0},{20,4},{24,8},{28,12},{1,17},{... | collective-permute-start | bytes 393224 | tf_op jit(solution)/shard_map/ppermute | solution.py:409
  14.3 23.7 %collective-permute-start.3 = (bf16[8,32,256]{2,1,0:T(8,128)(2,1)S(1)}, bf16[8,32,256]{2,1,0:T(8,128)(2,1)S(1)}, u32[]{:S(2)}, u32[]{:S(2)}) collective-permute-start(bf16[8,32,256]{2,1,0:T(8,128)(2,1)S(1)} %get-tuple-element.29), channel_id=1, source_target_pairs={{0,20},{4,16},{8,28},{12,24},{16,4},{20,0},{24,12},{28,8},{1,21},{... | collective-permute-start | bytes 393224 | tf_op jit(solution)/shard_map/ppermute | solution.py:409
  14.3 30.9 %collective-permute-start.4 = (bf16[8,64,256]{2,1,0:T(8,128)(2,1)}, bf16[8,64,256]{2,1,0:T(8,128)(2,1)S(1)}, u32[]{:S(2)}, u32[]{:S(2)}) collective-permute-start(bf16[8,64,256]{2,1,0:T(8,128)(2,1)} %get-tuple-element.30), channel_id=1, source_target_pairs={{0,12},{4,8},{8,4},{12,0},{16,28},{20,24},{24,20},{28,16},{1,13},{... | collective-permute-start | bytes 786440 | tf_op jit(solution)/shard_map/ppermute | solution.py:409
  22.7 22.5 %collective-permute-start.5 = (bf16[8,64,256]{2,1,0:T(8,128)(2,1)}, bf16[8,64,256]{2,1,0:T(8,128)(2,1)S(1)}, u32[]{:S(2)}, u32[]{:S(2)}) collective-permute-start(bf16[8,64,256]{2,1,0:T(8,128)(2,1)} %get-tuple-element.31), channel_id=1, source_target_pairs={{0,24},{4,28},{8,16},{12,20},{16,8},{20,12},{24,0},{28,4},{1,25},{... | collective-permute-start | bytes 786440 | tf_op jit(solution)/shard_map/ppermute | solution.py:409
  26.8 21.7 %collective-permute-start.6 = (bf16[8,64,256]{2,1,0:T(8,128)(2,1)S(1)}, bf16[8,64,256]{2,1,0:T(8,128)(2,1)S(1)}, u32[]{:S(2)}, u32[]{:S(2)}) collective-permute-start(bf16[8,64,256]{2,1,0:T(8,128)(2,1)S(1)} %get-tuple-element.32), channel_id=1, source_target_pairs={{0,8},{4,12},{8,0},{12,4},{16,24},{20,28},{24,16},{28,20},{1,9},{5... | collective-permute-start | bytes 786440 | tf_op jit(solution)/shard_map/ppermute | solution.py:409
  33.4 15.1 %collective-permute-start.7 = (bf16[8,64,256]{2,1,0:T(8,128)(2,1)}, bf16[8,64,256]{2,1,0:T(8,128)(2,1)S(1)}, u32[]{:S(2)}, u32[]{:S(2)}) collective-permute-start(bf16[8,64,256]{2,1,0:T(8,128)(2,1)} %get-tuple-element.33), channel_id=1, source_target_pairs={{0,28},{4,24},{8,20},{12,16},{16,12},{20,8},{24,4},{28,0},{1,29},{... | collective-permute-start | bytes 786440 | tf_op jit(solution)/shard_map/ppermute | solution.py:409
  38.0 12.4 %collective-permute-start.8 = (bf16[8,64,256]{2,1,0:T(8,128)(2,1)S(1)}, bf16[8,64,256]{2,1,0:T(8,128)(2,1)S(1)}, u32[]{:S(2)}, u32[]{:S(2)}) collective-permute-start(bf16[8,64,256]{2,1,0:T(8,128)(2,1)S(1)} %get-tuple-element.34), channel_id=1, source_target_pairs={{0,4},{4,0},{8,12},{12,8},{16,20},{20,16},{24,28},{28,24},{1,5},{5... | collective-permute-start | bytes 786440 | tf_op jit(solution)/shard_map/ppermute | solution.py:409
  51.9 1.2 %collective-permute-start.9 = (f32[32,128]{1,0:T(8,128)S(1)}, f32[32,128]{1,0:T(8,128)S(1)}, u32[]{:S(2)}, u32[]{:S(2)}) collective-permute-start(f32[32,128]{1,0:T(8,128)S(1)} %gram_partial.1.refs_1_), channel_id=1, source_target_pairs={{0,1},{1,0},{2,3},{3,2},{4,5},{5,4},{6,7},{7,6},{8,9},{9,8},{10,11... | collective-permute-start | bytes 49160 | tf_op jit(solution)/shard_map/ppermute | solution.py:322
  53.2 7.0 %collective-permute-start.10 = (f32[32,128]{1,0:T(8,128)S(1)}, f32[32,128]{1,0:T(8,128)S(1)}, u32[]{:S(2)}, u32[]{:S(2)}) collective-permute-start(f32[32,128]{1,0:T(8,128)S(1)} %sum_over.2.refs_3_), channel_id=1, source_target_pairs={{0,26},{1,27},{2,24},{3,25},{4,30},{5,31},{6,28},{7,29},{8,18},{9,... | collective-permute-start | bytes 49160 | tf_op jit(solution)/shard_map/ppermute | solution.py:322
  58.5 5.5 %collective-permute-start.11 = (f32[32,128]{1,0:T(8,128)S(1)}, f32[32,128]{1,0:T(8,128)S(1)}, u32[]{:S(2)}, u32[]{:S(2)}) collective-permute-start(f32[32,128]{1,0:T(8,128)S(1)} %sum_over.2.refs_3_), channel_id=1, source_target_pairs={{0,24},{1,25},{2,26},{3,27},{4,28},{5,29},{6,30},{7,31},{8,16},{9,... | collective-permute-start | bytes 49160 | tf_op jit(solution)/shard_map/ppermute | solution.py:322
  58.5 5.5 %collective-permute-start.12 = (f32[32,128]{1,0:T(8,128)S(1)}, f32[32,128]{1,0:T(8,128)S(1)}, u32[]{:S(2)}, u32[]{:S(2)}) collective-permute-start(f32[32,128]{1,0:T(8,128)S(1)} %sum_over.2.refs_3_), channel_id=1, source_target_pairs={{0,2},{1,3},{2,0},{3,1},{4,6},{5,7},{6,4},{7,5},{8,10},{9,11},{10,... | collective-permute-start | bytes 49160 | tf_op jit(solution)/shard_map/ppermute | solution.py:322
  64.0 4.7 %collective-permute-start.13 = (f32[32,128]{1,0:T(8,128)S(1)}, f32[32,128]{1,0:T(8,128)S(1)}, u32[]{:S(2)}, u32[]{:S(2)}) collective-permute-start(f32[32,128]{1,0:T(8,128)S(1)} %sum_over.3.refs_3_), channel_id=1, source_target_pairs={{0,12},{1,13},{2,14},{3,15},{4,8},{5,9},{6,10},{7,11},{8,4},{9,5},... | collective-permute-start | bytes 49160 | tf_op jit(solution)/shard_map/ppermute | solution.py:322
  64.4 4.4 %collective-permute-start.14 = (f32[32,128]{1,0:T(8,128)S(1)}, f32[32,128]{1,0:T(8,128)S(1)}, u32[]{:S(2)}, u32[]{:S(2)}) collective-permute-start(f32[32,128]{1,0:T(8,128)S(1)} %sum_over.3.refs_3_), channel_id=1, source_target_pairs={{0,8},{1,9},{2,10},{3,11},{4,12},{5,13},{6,14},{7,15},{8,0},{9,1},... | collective-permute-start | bytes 49160 | tf_op jit(solution)/shard_map/ppermute | solution.py:322
  66.4 3.7 %collective-permute-start.15 = (f32[32,128]{1,0:T(8,128)S(1)}, f32[32,128]{1,0:T(8,128)S(1)}, u32[]{:S(2)}, u32[]{:S(2)}) collective-permute-start(f32[32,128]{1,0:T(8,128)S(1)} %sum_over.3.refs_3_), channel_id=1, source_target_pairs={{0,4},{1,5},{2,6},{3,7},{4,0},{5,1},{6,2},{7,3},{8,12},{9,13},{10,... | collective-permute-start | bytes 49160 | tf_op jit(solution)/shard_map/ppermute | solution.py:322

commit v26 on v25

--- a/solution.py
+++ b/solution.py
@@ -27,10 +27,11 @@
     cut = split_partners(owners, split)
     order = [(k, part) for part in range(split) for k in cut]
     far = [k for k in far if k not in cut]
+    last = far.pop()
     while far or near:
         order += [(k, 0) for k in near[:1] + far[:1]]
         far, near = far[1:], near[1:]
-    return order + [(0, 0)]
+    return order + [(last, 0), (0, 0)]
 
 
 def split_partners(owners, split):
@@ -176,31 +177,73 @@
         row -= ref.shape[1]
 
 
-def gram_kernel(owners, *refs):
-    *block_refs, energy_ref, out_ref, flat, whole = refs
-    blocks = in_place(block_refs, owners)
-    local, count, d = blocks[0][0].shape
-    total = local * owners
+def swap_matrix(local, me):
     joined = CHUNK // local
-    me = lax.axis_index("samp")
     block = CHUNK * CHUNK
     dest = iota((block, block), 0)
     sample = dest % CHUNK
     sample = (sample // local ^ me % joined) * local + sample % local
     source = sample * CHUNK + dest // CHUNK
-    swap = (iota((block, block), 1) == source).astype(F32).astype(BF16)
+    return (iota((block, block), 1) == source).astype(F32).astype(BF16)
+
+
+def turned(swap, group, row, d):
+    pieces = [rows_of(parts, row, CHUNK) for parts in group]
+    piece = jnp.concatenate(pieces, axis=0).reshape(CHUNK * CHUNK, d)
+    return jnp.dot(swap, piece, preferred_element_type=F32).astype(BF16)
+
+
+def products(left, right):
+    return lax.dot_general(left, right, (((1,), (1,)), ((), ())), preferred_element_type=F32)
+
+
+def early_kernel(order, joined, *refs):
+    *block_refs, flat, gram_ref = refs
+    blocks = {k: [] for k, _ in order}
+    for (k, _), ref in zip(order, block_refs):
+        blocks[k].append(ref)
+    count, total, d = flat.shape
+    owners = len(blocks) + joined
+    me = lax.axis_index("samp")
+    swap = swap_matrix(CHUNK // joined, me)
+    for j in range(owners // joined):
+        place = pl.ds(pl.multiple_of((me // joined ^ j) * CHUNK, CHUNK), CHUNK)
+        group = [blocks.get(k) for k in range(j * joined, (j + 1) * joined)]
+        for row in range(0, count, CHUNK):
+            if group[0] is None:
+                flat[row : row + CHUNK, place] = jnp.zeros((CHUNK, CHUNK, d), BF16)
+                continue
+            rows = turned(swap, group, row, d)
+            for r in range(CHUNK):
+                flat[row + r, place] = rows[r * CHUNK : (r + 1) * CHUNK]
+    lined = jnp.concatenate([flat[r] for r in range(count)], axis=1)
+    gram = products(lined, lined)
+    gram_ref[...] = jnp.zeros_like(gram_ref)
+    gram_ref[:, :total] += gram
+
+
+def late_kernel(owners, *refs):
+    *block_refs, flat, gram_ref, energy_ref, out_ref, whole, edge = refs
+    count, total, d = flat.shape
+    joined = len(block_refs)
+    me = lax.axis_index("samp")
+    swap = swap_matrix(CHUNK // joined, me)
+    group = [[ref] for ref in block_refs]
+    late = []
     for row in range(0, count, CHUNK):
-        for j in range(owners // joined):
-            pieces = [rows_of(p, row, CHUNK) for p in blocks[j * joined : (j + 1) * joined]]
-            piece = jnp.concatenate(pieces, axis=0).reshape(block, d)
-            turned = jnp.dot(swap, piece, preferred_element_type=F32).astype(BF16)
-            place = pl.ds(pl.multiple_of((me // joined ^ j) * CHUNK, CHUNK), CHUNK)
-            for r in range(CHUNK):
-                flat[row + r, place] = turned[r * CHUNK : (r + 1) * CHUNK]
+        rows = turned(swap, group, row, d)
+        late += [rows[r * CHUNK : (r + 1) * CHUNK] for r in range(CHUNK)]
+    late = jnp.concatenate(late, axis=1)
     lined = jnp.concatenate([flat[r] for r in range(count)], axis=1)
-    gram = lax.dot_general(lined, lined, (((1,), (1,)), ((), ())), preferred_element_type=F32)
-    whole[...] = jnp.zeros_like(whole)
-    whole[:, :total] += gram
+    edge[...] = jnp.zeros_like(edge)
+    edge[:total, :CHUNK] += products(lined, late)
+    edge[total:, :CHUNK] += products(late, late)
+    first = (me // joined ^ (owners // joined - 1)) * CHUNK
+    moved = pltpu.roll(edge[...], first, 1)
+    columns = moved[:total]
+    whole[...] = gram_ref[...] + columns
+    whole[:, :total] += jnp.swapaxes(columns[:, :total], 0, 1)
+    whole[pl.ds(pl.multiple_of(first, CHUNK), CHUNK)] += moved[total:]
     half, width = out_ref.shape
     lane = iota((half, width), 1)
     lower = pltpu.roll(whole[half:], half, 1)
@@ -209,23 +252,42 @@
 
 
 def gram_partial(blocks, split, energies):
+    owners = len(blocks)
     local, count, d = blocks[0][0].shape
-    total = local * len(blocks)
-    return pl.pallas_call(
-        functools.partial(gram_kernel, len(blocks)),
-        out_shape=jax.ShapeDtypeStruct(packed_shape(total), F32),
-        scratch_shapes=[
-            pltpu.VMEM((count, total, d), BF16),
-            pltpu.VMEM((total, packed_shape(total)[1]), F32),
-        ],
-        compiler_params=pltpu.CompilerParams(vmem_limit_bytes=VMEM_LIMIT),
+    total = local * owners
+    joined = CHUNK // local
+    order = [(k, part) for k, part in turns(owners, split) if k < owners - joined]
+    width = packed_shape(total)[1]
+    params = pltpu.CompilerParams(vmem_limit_bytes=VMEM_LIMIT)
+    flat, gram = pl.pallas_call(
+        functools.partial(early_kernel, order, joined),
+        out_shape=(
+            jax.ShapeDtypeStruct((count, total, d), BF16),
+            jax.ShapeDtypeStruct((total, width), F32),
+        ),
+        compiler_params=params,
         cost_estimate=pl.CostEstimate(
             flops=2 * total * total * count * d,
             bytes_accessed=2 * total * count * d,
             transcendentals=0,
         ),
-        name="gram_partial",
-    )(*in_turn(blocks, split), energies)
+        name="gram_early",
+    )(*[blocks[k][part] for k, part in order])
+    return pl.pallas_call(
+        functools.partial(late_kernel, owners),
+        out_shape=jax.ShapeDtypeStruct(packed_shape(total), F32),
+        scratch_shapes=[
+            pltpu.VMEM((total, width), F32),
+            pltpu.VMEM((total + CHUNK, width), F32),
+        ],
+        compiler_params=params,
+        cost_estimate=pl.CostEstimate(
+            flops=2 * total * CHUNK * count * d,
+            bytes_accessed=2 * total * count * d,
+            transcendentals=0,
+        ),
+        name="gram_late",
+    )(*[blocks[k][0] for k in range(owners - joined, owners)], flat, gram, energies)
 
 
 def tree_sum(parts):

time: 73.7 us -> 74.8 us (1.015)
  Pallas kernels: 10.8 us -> 11.8 us
    ppermute x7, waiting for transfers between devices: 8.62 us -> 10.3 us  [partners(): return [lax.ppermute(value, axes, perm) for perm in perms] + [value]]
    ppermute x9, waiting for transfers between devices: 25.7 us -> 24.5 us  [body(): blocks[k][part] = lax.ppermute(blocks[k][part], 'samp', perm)]
    pallas_call x1 -> x2, Pallas kernels: 1.51 us -> 2.5 us  [the longest x1 1.32 us: gram_partial(): pl.pallas_call(functools.partial(early_kernel, order, joined), out_shape=...]
  transfers between devices with their start and end apart: 16 -> 16, of which waited for: 12 -> 12; matrix products, arithmetic and copies ran while one was open for 0% -> 0% of each run, Pallas kernels for 5% -> 6%
where the time goes in v26:
time: 74.8 us; the launch traced here: 74.7 us
  waiting for transfers between devices  34.8 us (47%)
  starting transfers between devices  27.3 us (36%)
  Pallas kernels  11.8 us (16%)
    ppermute x9, waiting for transfers between devices, body(): blocks[k][part] = lax.ppermute(blocks[k][part], 'samp', perm)  24.5 us
    ppermute x9, starting transfers between devices, body(): blocks[k][part] = lax.ppermute(blocks[k][part], 'samp', perm)  17.5 us
    ppermute x7, waiting for transfers between devices, partners(): return [lax.ppermute(value, axes, perm) for perm in perms] + [value]  10.3 us
    ppermute x7, starting transfers between devices, partners(): return [lax.ppermute(value, axes, perm) for perm in perms] + [value]  9.8 us
    pallas_call x2, Pallas kernels, jac_rows(): pl.pallas_call(functools.partial(jac_kernel, part * mats, joined), in_spe...  5.59 us
    pallas_call x1, Pallas kernels, solve_and_project(): pl.pallas_call(functools.partial(solve_kernel, len(sums), len(blocks)), o...  3.45 us
  transfers between devices with their start and end apart: 16, of which 12 were waited for; matrix products, arithmetic and copies ran while one was open for 0% of the time, Pallas kernels for 6%

profile of v26, /device:TPU:0, one launch (start us, length us, event | category | flops | bytes accessed | tf_op | source)
XLA Modules:
  0.0 74.7 jit_solution(13285295726784256500)
XLA Ops:
  0.6 2.3 %jac_rows.2 = (bf16[8,32,256]{2,1,0:T(8,128)(2,1)S(1)}, bf16[8,32,256]{2,1,0:T(8,128)(2,1)S(1)}, bf16[8,32,256]{2,1,0:T(8,128)(2,1)S(1)}, bf16[8,32,256]{2,1,0:T...) custom-call(bf16[8,2,256,256]{3,2,1,0:T(8,128)(2,1)} %act_hbm.3, ...), custom_call_target="tpu_custom_call" | custom-call | flops 268435456 | bytes 3145728 | tf_op jit(solution)/shard_map/jac_rows/pallas_call | solution.py:105
  3.0 4.1 %collective-permute-start.2 = (bf16[8,32,256]{2,1,0:T(8,128)(2,1)S(1)}, bf16[8,32,256]{2,1,0:T(8,128)(2,1)S(1)}, u32[]{:S(2)}, u32[]{:S(2)}) collective-permute-start(bf16[8,32,256]{2,1,0:T(8,128)(2,1)S(1)} %get-tuple-element.30), channel_id=1, source_target_pairs={{0,16},{4,20},{8,24},{12,28},{16,0},{20,4},{24,8},{28,12},{1,17},{... | collective-permute-start | bytes 393224 | tf_op jit(solution)/shard_map/ppermute | solution.py:471
  7.1 1.3 %collective-permute-start.3 = (bf16[8,32,256]{2,1,0:T(8,128)(2,1)S(1)}, bf16[8,32,256]{2,1,0:T(8,128)(2,1)S(1)}, u32[]{:S(2)}, u32[]{:S(2)}) collective-permute-start(bf16[8,32,256]{2,1,0:T(8,128)(2,1)S(1)} %get-tuple-element.31), channel_id=1, source_target_pairs={{0,20},{4,16},{8,28},{12,24},{16,4},{20,0},{24,12},{28,8},{1,21},{... | collective-permute-start | bytes 393224 | tf_op jit(solution)/shard_map/ppermute | solution.py:471
  8.4 0.0 copy-start.1
  8.4 0.0 copy-start
  8.4 3.2 %jac_rows.3 = (bf16[8,64,256]{2,1,0:T(8,128)(2,1)S(1)}, bf16[8,64,256]{2,1,0:T(8,128)(2,1)S(1)}, bf16[8,64,256]{2,1,0:T(8,128)(2,1)S(1)}, bf16[8,64,256]{2,1,0:T...) custom-call(bf16[8,2,256,256]{3,2,1,0:T(8,128)(2,1)} %act_hbm.3, ...), custom_call_target="tpu_custom_call" | custom-call | flops 268435456 | bytes 3145728 | tf_op jit(solution)/shard_map/jac_rows/pallas_call | solution.py:105
  11.6 2.7 %collective-permute-start.4 = (bf16[8,32,256]{2,1,0:T(8,128)(2,1)S(1)}, bf16[8,32,256]{2,1,0:T(8,128)(2,1)S(1)}, u32[]{:S(2)}, u32[]{:S(2)}) collective-permute-start(bf16[8,32,256]{2,1,0:T(8,128)(2,1)S(1)} %get-tuple-element.32), channel_id=1, source_target_pairs={{0,16},{4,20},{8,24},{12,28},{16,0},{20,4},{24,8},{28,12},{1,17},{... | collective-permute-start | bytes 393224 | tf_op jit(solution)/shard_map/ppermute | solution.py:471
  14.3 0.0 collective-permute-start.5
  14.3 2.8 %collective-permute-start.6 = (bf16[8,64,256]{2,1,0:T(8,128)(2,1)}, bf16[8,64,256]{2,1,0:T(8,128)(2,1)S(1)}, u32[]{:S(2)}, u32[]{:S(2)}) collective-permute-start(bf16[8,64,256]{2,1,0:T(8,128)(2,1)} %get-tuple-element.34), channel_id=1, source_target_pairs={{0,12},{4,8},{8,4},{12,0},{16,28},{20,24},{24,20},{28,16},{1,13},{... | collective-permute-start | bytes 786440 | tf_op jit(solution)/shard_map/ppermute | solution.py:471
  17.1 5.6 %collective-permute-done.2.refs_0_.refs_4_ = bf16[8,32,256]{2,1,0:T(8,128)(2,1)S(1)} collective-permute-done((bf16[8,32,256]{2,1,0:T(8,128)(2,1)S(1)}, bf16[8,32,256]{2,1,0:T(8,128)(2,1)S(1)}, u32[]{:S(2)}, u32[]{:S(2)}) %collective-permute-start.2) | collective-permute-done | bytes 131104 | tf_op jit(solution)/shard_map/ppermute | solution.py:471
  22.7 0.0 collective-permute-start.7
  22.7 4.0 %collective-permute-done.3.refs_1_.refs_5_ = bf16[8,32,256]{2,1,0:T(8,128)(2,1)S(1)} collective-permute-done((bf16[8,32,256]{2,1,0:T(8,128)(2,1)S(1)}, bf16[8,32,256]{2,1,0:T(8,128)(2,1)S(1)}, u32[]{:S(2)}, u32[]{:S(2)}) %collective-permute-start.3) | collective-permute-done | bytes 131104 | tf_op jit(solution)/shard_map/ppermute | solution.py:471
  26.8 0.3 collective-permute-start.8
  27.0 1.3 %collective-permute-done.4.refs_2_.refs_6_ = bf16[8,32,256]{2,1,0:T(8,128)(2,1)S(1)} collective-permute-done((bf16[8,32,256]{2,1,0:T(8,128)(2,1)S(1)}, bf16[8,32,256]{2,1,0:T(8,128)(2,1)S(1)}, u32[]{:S(2)}, u32[]{:S(2)}) %collective-permute-start.4) | collective-permute-done | bytes 131104 | tf_op jit(solution)/shard_map/ppermute | solution.py:471
  28.4 2.8 %collective-permute-start = (bf16[8,64,256]{2,1,0:T(8,128)(2,1)}, bf16[8,64,256]{2,1,0:T(8,128)(2,1)S(1)}, u32[]{:S(2)}, u32[]{:S(2)}) collective-permute-start(bf16[8,64,256]{2,1,0:T(8,128)(2,1)} %get-tuple-element.28), channel_id=1, source_target_pairs={{0,24},{4,28},{8,16},{12,20},{16,8},{20,12},{24,0},{28,4},{1,25},{... | collective-permute-start | bytes 786440 | tf_op jit(solution)/shard_map/ppermute | solution.py:471
  31.2 0.2 collective-permute-done.5.refs_3_.refs_7_
  31.4 3.6 %collective-permute-start.1 = (bf16[8,64,256]{2,1,0:T(8,128)(2,1)}, bf16[8,64,256]{2,1,0:T(8,128)(2,1)S(1)}, u32[]{:S(2)}, u32[]{:S(2)}) collective-permute-start(bf16[8,64,256]{2,1,0:T(8,128)(2,1)} %get-tuple-element.29), channel_id=1, source_target_pairs={{0,28},{4,24},{8,20},{12,16},{16,12},{20,8},{24,4},{28,0},{1,29},{... | collective-permute-start | bytes 786440 | tf_op jit(solution)/shard_map/ppermute | solution.py:471
  34.9 0.0 copy-done.1
  34.9 0.1 copy.6.offdiag_ref
  35.0 0.0 copy-done
  35.0 0.2 packed_energy.1.refs_4_
  35.2 10.0 %collective-permute-done.6.refs_4_.refs_8_ = bf16[8,64,256]{2,1,0:T(8,128)(2,1)S(1)} collective-permute-done((bf16[8,64,256]{2,1,0:T(8,128)(2,1)}, bf16[8,64,256]{2,1,0:T(8,128)(2,1)S(1)}, u32[]{:S(2)}, u32[]{:S(2)}) %collective-permute-start.6) | collective-permute-done | bytes 262176 | tf_op jit(solution)/shard_map/ppermute | solution.py:471
  45.3 3.3 %collective-permute-done.7.refs_5_.refs_10_ = bf16[8,64,256]{2,1,0:T(8,128)(2,1)S(1)} collective-permute-done((bf16[8,64,256]{2,1,0:T(8,128)(2,1)S(1)}, bf16[8,64,256]{2,1,0:T(8,128)(2,1)S(1)}, u32[]{:S(2)}, u32[]{:S(2)}) %collective-permute-start.7) | collective-permute-done | bytes 262176 | tf_op jit(solution)/shard_map/ppermute | solution.py:471
  48.5 0.0 collective-permute-done.8.refs_6_.refs_11_
  48.6 1.3 %gram_early.1 = (bf16[64,64,256]{2,1,0:T(8,128)(2,1)S(1)}, f32[64,128]{1,0:T(8,128)S(1)}) custom-call(bf16[8,32,256]{2,1,0:T(8,128)(2,1)S(1)} %collective-permute-done.2.refs_0_.refs_4_, bf16[8,32,256]{2,1,0:T(8,128)(2,1)S(1)} %collective-permute-done.3.refs_1_.refs_5_, bf16[8,32,256]{2,1,0:T(8,128)(2,1)S(1)} %collective-permute-done.4.refs_2_.refs_6_, ...), custom_call_target="tpu_custom_call" | custom-call | flops 134217728 | bytes 2097152 | tf_op jit(solution)/shard_map/gram_early/pallas_call | solution.py:262
  49.9 0.0 collective-permute-done.refs_0_.refs_9_
  49.9 0.0 collective-permute-done.1.refs_1_.refs_12_
  49.9 1.2 %gram_late.1.refs_1_ = f32[32,128]{1,0:T(8,128)S(1)} custom-call(bf16[8,64,256]{2,1,0:T(8,128)(2,1)S(1)} %collective-permute-done.refs_0_.refs_9_, bf16[8,64,256]{2,1,0:T(8,128)(2,1)S(1)} %collective-permute-done.1.refs_1_.refs_12_, bf16[64,64,256]{2,1,0:T(8,128)(2,1)S(1)} %get-tuple-element.38.refs_2_, f32[64,128]{1,0:T(8,128)S(1)} %get-tuple-element.39.refs_3_, ...), custom_call_target="tpu_custom_call" | custom-call | flops 33554432 | bytes 2097152 | tf_op jit(solution)/shard_map/gram_late/pallas_call | solution.py:276
  51.1 0.0 collective-permute-start.9
  51.1 1.2 %collective-permute-done.9.refs_0_ = f32[32,128]{1,0:T(8,128)S(1)} collective-permute-done((f32[32,128]{1,0:T(8,128)S(1)}, f32[32,128]{1,0:T(8,128)S(1)}, u32[]{:S(2)}, u32[]{:S(2)}) %collective-permute-start.9) | collective-permute-done | bytes 16416 | tf_op jit(solution)/shard_map/ppermute | solution.py:384
  52.3 1.5 %collective-permute-start.12 = (f32[32,128]{1,0:T(8,128)S(1)}, f32[32,128]{1,0:T(8,128)S(1)}, u32[]{:S(2)}, u32[]{:S(2)}) collective-permute-start(f32[32,128]{1,0:T(8,128)S(1)} %sum_over.2.refs_3_), channel_id=1, source_target_pairs={{0,2},{1,3},{2,0},{3,1},{4,6},{5,7},{6,4},{7,5},{8,10},{9,11},{10,... | collective-permute-start | bytes 49160 | tf_op jit(solution)/shard_map/ppermute | solution.py:384
  53.9 4.7 %collective-permute-start.11 = (f32[32,128]{1,0:T(8,128)S(1)}, f32[32,128]{1,0:T(8,128)S(1)}, u32[]{:S(2)}, u32[]{:S(2)}) collective-permute-start(f32[32,128]{1,0:T(8,128)S(1)} %sum_over.2.refs_3_), channel_id=1, source_target_pairs={{0,24},{1,25},{2,26},{3,27},{4,28},{5,29},{6,30},{7,31},{8,16},{9,... | collective-permute-start | bytes 49160 | tf_op jit(solution)/shard_map/ppermute | solution.py:384
  58.5 0.0 collective-permute-start.10
  58.5 0.0 collective-permute-done.12.refs_2_
  58.5 1.7 %collective-permute-done.11.refs_1_ = f32[32,128]{1,0:T(8,128)S(1)} collective-permute-done((f32[32,128]{1,0:T(8,128)S(1)}, f32[32,128]{1,0:T(8,128)S(1)}, u32[]{:S(2)}, u32[]{:S(2)}) %collective-permute-start.11) | collective-permute-done | bytes 16416 | tf_op jit(solution)/shard_map/ppermute | solution.py:384
  60.2 4.8 %collective-permute-done.10.refs_0_ = f32[32,128]{1,0:T(8,128)S(1)} collective-permute-done((f32[32,128]{1,0:T(8,128)S(1)}, f32[32,128]{1,0:T(8,128)S(1)}, u32[]{:S(2)}, u32[]{:S(2)}) %collective-permute-start.10) | collective-permute-done | bytes 16416 | tf_op jit(solution)/shard_map/ppermute | solution.py:384
  65.1 1.5 %collective-permute-start.15 = (f32[32,128]{1,0:T(8,128)S(1)}, f32[32,128]{1,0:T(8,128)S(1)}, u32[]{:S(2)}, u32[]{:S(2)}) collective-permute-start(f32[32,128]{1,0:T(8,128)S(1)} %sum_over.3.refs_3_), channel_id=1, source_target_pairs={{0,4},{1,5},{2,6},{3,7},{4,0},{5,1},{6,2},{7,3},{8,12},{9,13},{10,... | collective-permute-start | bytes 49160 | tf_op jit(solution)/shard_map/ppermute | solution.py:384
  66.6 0.0 collective-permute-start.14
  66.6 2.1 %collective-permute-start.13 = (f32[32,128]{1,0:T(8,128)S(1)}, f32[32,128]{1,0:T(8,128)S(1)}, u32[]{:S(2)}, u32[]{:S(2)}) collective-permute-start(f32[32,128]{1,0:T(8,128)S(1)} %sum_over.3.refs_3_), channel_id=1, source_target_pairs={{0,12},{1,13},{2,14},{3,15},{4,8},{5,9},{6,10},{7,11},{8,4},{9,5},... | collective-permute-start | bytes 49160 | tf_op jit(solution)/shard_map/ppermute | solution.py:384
  68.6 0.2 collective-permute-done.15.refs_2_
  68.9 1.4 %collective-permute-done.14.refs_1_ = f32[32,128]{1,0:T(8,128)S(1)} collective-permute-done((f32[32,128]{1,0:T(8,128)S(1)}, f32[32,128]{1,0:T(8,128)S(1)}, u32[]{:S(2)}, u32[]{:S(2)}) %collective-permute-start.14) | collective-permute-done | bytes 16416 | tf_op jit(solution)/shard_map/ppermute | solution.py:384
  70.3 0.9 %collective-permute-done.13.refs_0_ = f32[32,128]{1,0:T(8,128)S(1)} collective-permute-done((f32[32,128]{1,0:T(8,128)S(1)}, f32[32,128]{1,0:T(8,128)S(1)}, u32[]{:S(2)}, u32[]{:S(2)}) %collective-permute-start.13) | collective-permute-done | bytes 16416 | tf_op jit(solution)/shard_map/ppermute | solution.py:384
  71.2 3.5 %solve_and_project.1 = (f32[1,8]{1,0:T(1,128)}, f32[2,32,256]{2,1,0:T(8,128)}) custom-call(f32[32,128]{1,0:T(8,128)S(1)} %collective-permute-done.13.refs_0_, f32[32,128]{1,0:T(8,128)S(1)} %collective-permute-done.14.refs_1_, f32[32,128]{1,0:T(8,128)S(1)} %collective-permute-done.15.refs_2_, f32[32,128]{1,0:T(8,128)S(1)} %sum_over.3.refs_3_, ...), custom_call_target="tpu_custom_call" | custom-call | tf_op jit(solution)/shard_map/solve_and_project/pallas_call | solution.py:452
  (2 shorter events, 0.0 us)
Async XLA Ops:
  3.0 19.8 %collective-permute-start.2 = (bf16[8,32,256]{2,1,0:T(8,128)(2,1)S(1)}, bf16[8,32,256]{2,1,0:T(8,128)(2,1)S(1)}, u32[]{:S(2)}, u32[]{:S(2)}) collective-permute-start(bf16[8,32,256]{2,1,0:T(8,128)(2,1)S(1)} %get-tuple-element.30), channel_id=1, source_target_pairs={{0,16},{4,20},{8,24},{12,28},{16,0},{20,4},{24,8},{28,12},{1,17},{... | collective-permute-start | bytes 393224 | tf_op jit(solution)/shard_map/ppermute | solution.py:471
  7.1 19.7 %collective-permute-start.3 = (bf16[8,32,256]{2,1,0:T(8,128)(2,1)S(1)}, bf16[8,32,256]{2,1,0:T(8,128)(2,1)S(1)}, u32[]{:S(2)}, u32[]{:S(2)}) collective-permute-start(bf16[8,32,256]{2,1,0:T(8,128)(2,1)S(1)} %get-tuple-element.31), channel_id=1, source_target_pairs={{0,20},{4,16},{8,28},{12,24},{16,4},{20,0},{24,12},{28,8},{1,21},{... | collective-permute-start | bytes 393224 | tf_op jit(solution)/shard_map/ppermute | solution.py:471
  8.4 26.5 %copy-start.1 = (f32[8]{0:T(128)S(1)}, f32[8]{0:T(128)}, u32[]{:S(2)}) copy-start(f32[8]{0:T(128)} %param.7) | copy-start | bytes 100
  8.4 26.6 %copy-start = (s32[8,256]{1,0:T(8,128)S(1)}, s32[8,256]{1,0:T(8,128)}, u32[]{:S(2)}) copy-start(s32[8,256]{1,0:T(8,128)} %spins_ref.1) | copy-start | bytes 24580
  11.6 16.7 %collective-permute-start.4 = (bf16[8,32,256]{2,1,0:T(8,128)(2,1)S(1)}, bf16[8,32,256]{2,1,0:T(8,128)(2,1)S(1)}, u32[]{:S(2)}, u32[]{:S(2)}) collective-permute-start(bf16[8,32,256]{2,1,0:T(8,128)(2,1)S(1)} %get-tuple-element.32), channel_id=1, source_target_pairs={{0,16},{4,20},{8,24},{12,28},{16,0},{20,4},{24,8},{28,12},{1,17},{... | collective-permute-start | bytes 393224 | tf_op jit(solution)/shard_map/ppermute | solution.py:471
  14.3 17.1 %collective-permute-start.5 = (bf16[8,32,256]{2,1,0:T(8,128)(2,1)S(1)}, bf16[8,32,256]{2,1,0:T(8,128)(2,1)S(1)}, u32[]{:S(2)}, u32[]{:S(2)}) collective-permute-start(bf16[8,32,256]{2,1,0:T(8,128)(2,1)S(1)} %get-tuple-element.33), channel_id=1, source_target_pairs={{0,20},{4,16},{8,28},{12,24},{16,4},{20,0},{24,12},{28,8},{1,21},{... | collective-permute-start | bytes 393224 | tf_op jit(solution)/shard_map/ppermute | solution.py:471
  14.3 31.0 %collective-permute-start.6 = (bf16[8,64,256]{2,1,0:T(8,128)(2,1)}, bf16[8,64,256]{2,1,0:T(8,128)(2,1)S(1)}, u32[]{:S(2)}, u32[]{:S(2)}) collective-permute-start(bf16[8,64,256]{2,1,0:T(8,128)(2,1)} %get-tuple-element.34), channel_id=1, source_target_pairs={{0,12},{4,8},{8,4},{12,0},{16,28},{20,24},{24,20},{28,16},{1,13},{... | collective-permute-start | bytes 786440 | tf_op jit(solution)/shard_map/ppermute | solution.py:471
  22.7 25.8 %collective-permute-start.7 = (bf16[8,64,256]{2,1,0:T(8,128)(2,1)S(1)}, bf16[8,64,256]{2,1,0:T(8,128)(2,1)S(1)}, u32[]{:S(2)}, u32[]{:S(2)}) collective-permute-start(bf16[8,64,256]{2,1,0:T(8,128)(2,1)S(1)} %get-tuple-element.35), channel_id=1, source_target_pairs={{0,8},{4,12},{8,0},{12,4},{16,24},{20,28},{24,16},{28,20},{1,9},{5... | collective-permute-start | bytes 786440 | tf_op jit(solution)/shard_map/ppermute | solution.py:471
  26.8 21.8 %collective-permute-start.8 = (bf16[8,64,256]{2,1,0:T(8,128)(2,1)S(1)}, bf16[8,64,256]{2,1,0:T(8,128)(2,1)S(1)}, u32[]{:S(2)}, u32[]{:S(2)}) collective-permute-start(bf16[8,64,256]{2,1,0:T(8,128)(2,1)S(1)} %get-tuple-element.36), channel_id=1, source_target_pairs={{0,4},{4,0},{8,12},{12,8},{16,20},{20,16},{24,28},{28,24},{1,5},{5... | collective-permute-start | bytes 786440 | tf_op jit(solution)/shard_map/ppermute | solution.py:471
  28.4 21.5 %collective-permute-start = (bf16[8,64,256]{2,1,0:T(8,128)(2,1)}, bf16[8,64,256]{2,1,0:T(8,128)(2,1)S(1)}, u32[]{:S(2)}, u32[]{:S(2)}) collective-permute-start(bf16[8,64,256]{2,1,0:T(8,128)(2,1)} %get-tuple-element.28), channel_id=1, source_target_pairs={{0,24},{4,28},{8,16},{12,20},{16,8},{20,12},{24,0},{28,4},{1,25},{... | collective-permute-start | bytes 786440 | tf_op jit(solution)/shard_map/ppermute | solution.py:471
  31.4 18.5 %collective-permute-start.1 = (bf16[8,64,256]{2,1,0:T(8,128)(2,1)}, bf16[8,64,256]{2,1,0:T(8,128)(2,1)S(1)}, u32[]{:S(2)}, u32[]{:S(2)}) collective-permute-start(bf16[8,64,256]{2,1,0:T(8,128)(2,1)} %get-tuple-element.29), channel_id=1, source_target_pairs={{0,28},{4,24},{8,20},{12,16},{16,12},{20,8},{24,4},{28,0},{1,29},{... | collective-permute-start | bytes 786440 | tf_op jit(solution)/shard_map/ppermute | solution.py:471
  51.1 1.2 %collective-permute-start.9 = (f32[32,128]{1,0:T(8,128)S(1)}, f32[32,128]{1,0:T(8,128)S(1)}, u32[]{:S(2)}, u32[]{:S(2)}) collective-permute-start(f32[32,128]{1,0:T(8,128)S(1)} %gram_late.1.refs_1_), channel_id=1, source_target_pairs={{0,1},{1,0},{2,3},{3,2},{4,5},{5,4},{6,7},{7,6},{8,9},{9,8},{10,11... | collective-permute-start | bytes 49160 | tf_op jit(solution)/shard_map/ppermute | solution.py:384
  52.3 6.2 %collective-permute-start.12 = (f32[32,128]{1,0:T(8,128)S(1)}, f32[32,128]{1,0:T(8,128)S(1)}, u32[]{:S(2)}, u32[]{:S(2)}) collective-permute-start(f32[32,128]{1,0:T(8,128)S(1)} %sum_over.2.refs_3_), channel_id=1, source_target_pairs={{0,2},{1,3},{2,0},{3,1},{4,6},{5,7},{6,4},{7,5},{8,10},{9,11},{10,... | collective-permute-start | bytes 49160 | tf_op jit(solution)/shard_map/ppermute | solution.py:384
  53.9 6.4 %collective-permute-start.11 = (f32[32,128]{1,0:T(8,128)S(1)}, f32[32,128]{1,0:T(8,128)S(1)}, u32[]{:S(2)}, u32[]{:S(2)}) collective-permute-start(f32[32,128]{1,0:T(8,128)S(1)} %sum_over.2.refs_3_), channel_id=1, source_target_pairs={{0,24},{1,25},{2,26},{3,27},{4,28},{5,29},{6,30},{7,31},{8,16},{9,... | collective-permute-start | bytes 49160 | tf_op jit(solution)/shard_map/ppermute | solution.py:384
  58.5 6.5 %collective-permute-start.10 = (f32[32,128]{1,0:T(8,128)S(1)}, f32[32,128]{1,0:T(8,128)S(1)}, u32[]{:S(2)}, u32[]{:S(2)}) collective-permute-start(f32[32,128]{1,0:T(8,128)S(1)} %sum_over.2.refs_3_), channel_id=1, source_target_pairs={{0,26},{1,27},{2,24},{3,25},{4,30},{5,31},{6,28},{7,29},{8,18},{9,... | collective-permute-start | bytes 49160 | tf_op jit(solution)/shard_map/ppermute | solution.py:384
  65.1 3.8 %collective-permute-start.15 = (f32[32,128]{1,0:T(8,128)S(1)}, f32[32,128]{1,0:T(8,128)S(1)}, u32[]{:S(2)}, u32[]{:S(2)}) collective-permute-start(f32[32,128]{1,0:T(8,128)S(1)} %sum_over.3.refs_3_), channel_id=1, source_target_pairs={{0,4},{1,5},{2,6},{3,7},{4,0},{5,1},{6,2},{7,3},{8,12},{9,13},{10,... | collective-permute-start | bytes 49160 | tf_op jit(solution)/shard_map/ppermute | solution.py:384
  66.6 3.7 %collective-permute-start.14 = (f32[32,128]{1,0:T(8,128)S(1)}, f32[32,128]{1,0:T(8,128)S(1)}, u32[]{:S(2)}, u32[]{:S(2)}) collective-permute-start(f32[32,128]{1,0:T(8,128)S(1)} %sum_over.3.refs_3_), channel_id=1, source_target_pairs={{0,8},{1,9},{2,10},{3,11},{4,12},{5,13},{6,14},{7,15},{8,0},{9,1},... | collective-permute-start | bytes 49160 | tf_op jit(solution)/shard_map/ppermute | solution.py:384
  66.6 4.6 %collective-permute-start.13 = (f32[32,128]{1,0:T(8,128)S(1)}, f32[32,128]{1,0:T(8,128)S(1)}, u32[]{:S(2)}, u32[]{:S(2)}) collective-permute-start(f32[32,128]{1,0:T(8,128)S(1)} %sum_over.3.refs_3_), channel_id=1, source_target_pairs={{0,12},{1,13},{2,14},{3,15},{4,8},{5,9},{6,10},{7,11},{8,4},{9,5},... | collective-permute-start | bytes 49160 | tf_op jit(solution)/shard_map/ppermute | solution.py:384

commit v27 on v25

--- a/solution.py
+++ b/solution.py
@@ -336,7 +336,8 @@
     masks += [layer * (samp - 2), layer]
     masks += [layer << bit for bit in range(1, samp.bit_length() - 2)]
     later = zip(masks[::2], masks[1::2] + [0] * (len(masks) % 2))
-    return [[1]] + [[a, b, a ^ b] if b else [a] for a, b in later]
+    later = [[a, b, a ^ b] if b else [a] for a, b in later]
+    return [[1]] + [[mask ^ 1 for mask in masks] for masks in later]
 
 
 def solve_kernel(sums, owners, *refs):

time: 73.7 us -> 72.2 us (0.980)
  waiting for transfers between devices: 34.3 us -> 33.4 us
    ppermute x7, waiting for transfers between devices: 8.62 us -> 7.67 us  [partners(): return [lax.ppermute(value, axes, perm) for perm in perms] + [value]]
where the time goes in v27:
time: 72.2 us; the launch traced here: 72 us
  waiting for transfers between devices  33.4 us (46%)
  starting transfers between devices  27.1 us (38%)
  Pallas kernels  10.8 us (15%)
    ppermute x9, waiting for transfers between devices, body(): blocks[k][part] = lax.ppermute(blocks[k][part], 'samp', perm)  25.7 us
    ppermute x9, starting transfers between devices, body(): blocks[k][part] = lax.ppermute(blocks[k][part], 'samp', perm)  18.1 us
    ppermute x7, starting transfers between devices, partners(): return [lax.ppermute(value, axes, perm) for perm in perms] + [value]  8.95 us
    ppermute x7, waiting for transfers between devices, partners(): return [lax.ppermute(value, axes, perm) for perm in perms] + [value]  7.67 us
    pallas_call x2, Pallas kernels, jac_rows(): pl.pallas_call(functools.partial(jac_kernel, part * mats, joined), in_spe...  5.6 us
    pallas_call x1, Pallas kernels, solve_and_project(): pl.pallas_call(functools.partial(solve_kernel, len(sums), len(blocks)), o...  3.45 us
    pallas_call x1, Pallas kernels, gram_partial(): pl.pallas_call(functools.partial(gram_kernel, len(blocks)), out_shape=jax...  1.51 us
  transfers between devices with their start and end apart: 16, of which 12 were waited for; matrix products, arithmetic and copies ran while one was open for 0% of the time, Pallas kernels for 5%

profile of v27, /device:TPU:0, one launch (start us, length us, event | category | flops | bytes accessed | tf_op | source)
XLA Modules:
  0.0 72.0 jit_solution(4075088698006536097)
XLA Ops:
  0.6 2.3 %jac_rows.2 = (bf16[8,32,256]{2,1,0:T(8,128)(2,1)S(1)}, bf16[8,32,256]{2,1,0:T(8,128)(2,1)S(1)}, bf16[8,32,256]{2,1,0:T(8,128)(2,1)S(1)}, bf16[8,32,256]{2,1,0:T...) custom-call(bf16[8,2,256,256]{3,2,1,0:T(8,128)(2,1)} %act_hbm.3, ...), custom_call_target="tpu_custom_call" | custom-call | flops 268435456 | bytes 3145728 | tf_op jit(solution)/shard_map/jac_rows/pallas_call | solution.py:104
  3.0 4.1 %collective-permute-start = (bf16[8,32,256]{2,1,0:T(8,128)(2,1)S(1)}, bf16[8,32,256]{2,1,0:T(8,128)(2,1)S(1)}, u32[]{:S(2)}, u32[]{:S(2)}) collective-permute-start(bf16[8,32,256]{2,1,0:T(8,128)(2,1)S(1)} %get-tuple-element.20), channel_id=1, source_target_pairs={{0,16},{4,20},{8,24},{12,28},{16,0},{20,4},{24,8},{28,12},{1,17},{... | collective-permute-start | bytes 393224 | tf_op jit(solution)/shard_map/ppermute | solution.py:410
  7.1 1.3 %collective-permute-start.1 = (bf16[8,32,256]{2,1,0:T(8,128)(2,1)S(1)}, bf16[8,32,256]{2,1,0:T(8,128)(2,1)S(1)}, u32[]{:S(2)}, u32[]{:S(2)}) collective-permute-start(bf16[8,32,256]{2,1,0:T(8,128)(2,1)S(1)} %get-tuple-element.21), channel_id=1, source_target_pairs={{0,20},{4,16},{8,28},{12,24},{16,4},{20,0},{24,12},{28,8},{1,21},{... | collective-permute-start | bytes 393224 | tf_op jit(solution)/shard_map/ppermute | solution.py:410
  8.4 0.0 copy-start.1
  8.4 0.0 copy-start
  8.4 3.3 %jac_rows.3 = (bf16[8,64,256]{2,1,0:T(8,128)(2,1)S(1)}, bf16[8,64,256]{2,1,0:T(8,128)(2,1)S(1)}, bf16[8,64,256]{2,1,0:T(8,128)(2,1)S(1)}, bf16[8,64,256]{2,1,0:T...) custom-call(bf16[8,2,256,256]{3,2,1,0:T(8,128)(2,1)} %act_hbm.3, ...), custom_call_target="tpu_custom_call" | custom-call | flops 268435456 | bytes 3145728 | tf_op jit(solution)/shard_map/jac_rows/pallas_call | solution.py:104
  11.6 2.7 %collective-permute-start.2 = (bf16[8,32,256]{2,1,0:T(8,128)(2,1)S(1)}, bf16[8,32,256]{2,1,0:T(8,128)(2,1)S(1)}, u32[]{:S(2)}, u32[]{:S(2)}) collective-permute-start(bf16[8,32,256]{2,1,0:T(8,128)(2,1)S(1)} %get-tuple-element.28), channel_id=1, source_target_pairs={{0,16},{4,20},{8,24},{12,28},{16,0},{20,4},{24,8},{28,12},{1,17},{... | collective-permute-start | bytes 393224 | tf_op jit(solution)/shard_map/ppermute | solution.py:410
  14.3 0.0 collective-permute-start.3
  14.3 2.8 %collective-permute-start.4 = (bf16[8,64,256]{2,1,0:T(8,128)(2,1)}, bf16[8,64,256]{2,1,0:T(8,128)(2,1)S(1)}, u32[]{:S(2)}, u32[]{:S(2)}) collective-permute-start(bf16[8,64,256]{2,1,0:T(8,128)(2,1)} %get-tuple-element.30), channel_id=1, source_target_pairs={{0,12},{4,8},{8,4},{12,0},{16,28},{20,24},{24,20},{28,16},{1,13},{... | collective-permute-start | bytes 786440 | tf_op jit(solution)/shard_map/ppermute | solution.py:410
  17.1 5.6 %collective-permute-done.refs_0_.refs_4_ = bf16[8,32,256]{2,1,0:T(8,128)(2,1)S(1)} collective-permute-done((bf16[8,32,256]{2,1,0:T(8,128)(2,1)S(1)}, bf16[8,32,256]{2,1,0:T(8,128)(2,1)S(1)}, u32[]{:S(2)}, u32[]{:S(2)}) %collective-permute-start) | collective-permute-done | bytes 131104 | tf_op jit(solution)/shard_map/ppermute | solution.py:410
  22.7 2.8 %collective-permute-start.5 = (bf16[8,64,256]{2,1,0:T(8,128)(2,1)}, bf16[8,64,256]{2,1,0:T(8,128)(2,1)S(1)}, u32[]{:S(2)}, u32[]{:S(2)}) collective-permute-start(bf16[8,64,256]{2,1,0:T(8,128)(2,1)} %get-tuple-element.31), channel_id=1, source_target_pairs={{0,24},{4,28},{8,16},{12,20},{16,8},{20,12},{24,0},{28,4},{1,25},{... | collective-permute-start | bytes 786440 | tf_op jit(solution)/shard_map/ppermute | solution.py:410
  25.5 1.2 %collective-permute-done.1.refs_1_.refs_5_ = bf16[8,32,256]{2,1,0:T(8,128)(2,1)S(1)} collective-permute-done((bf16[8,32,256]{2,1,0:T(8,128)(2,1)S(1)}, bf16[8,32,256]{2,1,0:T(8,128)(2,1)S(1)}, u32[]{:S(2)}, u32[]{:S(2)}) %collective-permute-start.1) | collective-permute-done | bytes 131104 | tf_op jit(solution)/shard_map/ppermute | solution.py:410
  26.8 0.0 collective-permute-start.6
  26.8 6.7 %collective-permute-done.2.refs_2_.refs_6_ = bf16[8,32,256]{2,1,0:T(8,128)(2,1)S(1)} collective-permute-done((bf16[8,32,256]{2,1,0:T(8,128)(2,1)S(1)}, bf16[8,32,256]{2,1,0:T(8,128)(2,1)S(1)}, u32[]{:S(2)}, u32[]{:S(2)}) %collective-permute-start.2) | collective-permute-done | bytes 131104 | tf_op jit(solution)/shard_map/ppermute | solution.py:410
  33.4 4.3 %collective-permute-start.7 = (bf16[8,64,256]{2,1,0:T(8,128)(2,1)}, bf16[8,64,256]{2,1,0:T(8,128)(2,1)S(1)}, u32[]{:S(2)}, u32[]{:S(2)}) collective-permute-start(bf16[8,64,256]{2,1,0:T(8,128)(2,1)} %get-tuple-element.33), channel_id=1, source_target_pairs={{0,28},{4,24},{8,20},{12,16},{16,12},{20,8},{24,4},{28,0},{1,29},{... | collective-permute-start | bytes 786440 | tf_op jit(solution)/shard_map/ppermute | solution.py:410
  37.7 0.3 collective-permute-done.3.refs_3_.refs_7_
  38.0 0.2 collective-permute-start.8
  38.2 0.0 copy-done.1
  38.2 0.1 copy.6.offdiag_ref
  38.3 0.0 copy-done
  38.3 0.2 packed_energy.1.refs_10_
  38.5 6.8 %collective-permute-done.4.refs_4_.refs_8_ = bf16[8,64,256]{2,1,0:T(8,128)(2,1)S(1)} collective-permute-done((bf16[8,64,256]{2,1,0:T(8,128)(2,1)}, bf16[8,64,256]{2,1,0:T(8,128)(2,1)S(1)}, u32[]{:S(2)}, u32[]{:S(2)}) %collective-permute-start.4) | collective-permute-done | bytes 262176 | tf_op jit(solution)/shard_map/ppermute | solution.py:410
  45.3 0.0 collective-permute-done.5.refs_5_.refs_9_
  45.3 3.2 %collective-permute-done.6.refs_6_.refs_10_ = bf16[8,64,256]{2,1,0:T(8,128)(2,1)S(1)} collective-permute-done((bf16[8,64,256]{2,1,0:T(8,128)(2,1)S(1)}, bf16[8,64,256]{2,1,0:T(8,128)(2,1)S(1)}, u32[]{:S(2)}, u32[]{:S(2)}) %collective-permute-start.6) | collective-permute-done | bytes 262176 | tf_op jit(solution)/shard_map/ppermute | solution.py:410
  48.5 0.0 collective-permute-done.7.refs_7_.refs_11_
  48.5 1.9 %collective-permute-done.8.refs_8_.refs_12_ = bf16[8,64,256]{2,1,0:T(8,128)(2,1)S(1)} collective-permute-done((bf16[8,64,256]{2,1,0:T(8,128)(2,1)S(1)}, bf16[8,64,256]{2,1,0:T(8,128)(2,1)S(1)}, u32[]{:S(2)}, u32[]{:S(2)}) %collective-permute-start.8) | collective-permute-done | bytes 262176 | tf_op jit(solution)/shard_map/ppermute | solution.py:410
  50.4 1.5 %gram_partial.1.refs_1_ = f32[32,128]{1,0:T(8,128)S(1)} custom-call(bf16[8,32,256]{2,1,0:T(8,128)(2,1)S(1)} %collective-permute-done.refs_0_.refs_4_, bf16[8,32,256]{2,1,0:T(8,128)(2,1)S(1)} %collective-permute-done.1.refs_1_.refs_5_, bf16[8,32,256]{2,1,0:T(8,128)(2,1)S(1)} %collective-permute-done.2.refs_2_.refs_6_, ...), custom_call_target="tpu_custom_call" | custom-call | flops 134217728 | bytes 2097152 | tf_op jit(solution)/shard_map/gram_partial/pallas_call | solution.py:214
  51.9 0.1 collective-permute-start.9
  52.0 1.2 %collective-permute-done.9.refs_0_ = f32[32,128]{1,0:T(8,128)S(1)} collective-permute-done((f32[32,128]{1,0:T(8,128)S(1)}, f32[32,128]{1,0:T(8,128)S(1)}, u32[]{:S(2)}, u32[]{:S(2)}) %collective-permute-start.9) | collective-permute-done | bytes 16416 | tf_op jit(solution)/shard_map/ppermute | solution.py:322
  53.2 5.1 %collective-permute-start.10 = (f32[32,128]{1,0:T(8,128)S(1)}, f32[32,128]{1,0:T(8,128)S(1)}, u32[]{:S(2)}, u32[]{:S(2)}) collective-permute-start(f32[32,128]{1,0:T(8,128)S(1)} %sum_over.2.refs_3_), channel_id=1, source_target_pairs={{0,27},{1,26},{2,25},{3,24},{4,31},{5,30},{6,29},{7,28},{8,19},{9,... | collective-permute-start | bytes 49160 | tf_op jit(solution)/shard_map/ppermute | solution.py:322
  58.2 0.0 collective-permute-start.11
  58.2 0.6 collective-permute-start.12
  58.8 0.9 %collective-permute-done.10.refs_0_ = f32[32,128]{1,0:T(8,128)S(1)} collective-permute-done((f32[32,128]{1,0:T(8,128)S(1)}, f32[32,128]{1,0:T(8,128)S(1)}, u32[]{:S(2)}, u32[]{:S(2)}) %collective-permute-start.10) | collective-permute-done | bytes 16416 | tf_op jit(solution)/shard_map/ppermute | solution.py:322
  59.7 3.5 %collective-permute-done.11.refs_1_ = f32[32,128]{1,0:T(8,128)S(1)} collective-permute-done((f32[32,128]{1,0:T(8,128)S(1)}, f32[32,128]{1,0:T(8,128)S(1)}, u32[]{:S(2)}, u32[]{:S(2)}) %collective-permute-start.11) | collective-permute-done | bytes 16416 | tf_op jit(solution)/shard_map/ppermute | solution.py:322
  63.2 0.0 collective-permute-done.12.refs_2_
  63.2 0.5 collective-permute-start.13
  63.7 1.7 %collective-permute-start.14 = (f32[32,128]{1,0:T(8,128)S(1)}, f32[32,128]{1,0:T(8,128)S(1)}, u32[]{:S(2)}, u32[]{:S(2)}) collective-permute-start(f32[32,128]{1,0:T(8,128)S(1)} %sum_over.3.refs_3_), channel_id=1, source_target_pairs={{0,9},{1,8},{2,11},{3,10},{4,13},{5,12},{6,15},{7,14},{8,1},{9,0},... | collective-permute-start | bytes 49160 | tf_op jit(solution)/shard_map/ppermute | solution.py:322
  65.4 1.0 %collective-permute-start.15 = (f32[32,128]{1,0:T(8,128)S(1)}, f32[32,128]{1,0:T(8,128)S(1)}, u32[]{:S(2)}, u32[]{:S(2)}) collective-permute-start(f32[32,128]{1,0:T(8,128)S(1)} %sum_over.3.refs_3_), channel_id=1, source_target_pairs={{0,5},{1,4},{2,7},{3,6},{4,1},{5,0},{6,3},{7,2},{8,13},{9,12},{10,... | collective-permute-start | bytes 49160 | tf_op jit(solution)/shard_map/ppermute | solution.py:322
  66.4 0.9 %collective-permute-done.13.refs_0_ = f32[32,128]{1,0:T(8,128)S(1)} collective-permute-done((f32[32,128]{1,0:T(8,128)S(1)}, f32[32,128]{1,0:T(8,128)S(1)}, u32[]{:S(2)}, u32[]{:S(2)}) %collective-permute-start.13) | collective-permute-done | bytes 16416 | tf_op jit(solution)/shard_map/ppermute | solution.py:322
  67.3 0.0 collective-permute-done.14.refs_1_
  67.4 1.2 %collective-permute-done.15.refs_2_ = f32[32,128]{1,0:T(8,128)S(1)} collective-permute-done((f32[32,128]{1,0:T(8,128)S(1)}, f32[32,128]{1,0:T(8,128)S(1)}, u32[]{:S(2)}, u32[]{:S(2)}) %collective-permute-start.15) | collective-permute-done | bytes 16416 | tf_op jit(solution)/shard_map/ppermute | solution.py:322
  68.6 3.5 %solve_and_project.1 = (f32[1,8]{1,0:T(1,128)}, f32[2,32,256]{2,1,0:T(8,128)}) custom-call(f32[32,128]{1,0:T(8,128)S(1)} %collective-permute-done.13.refs_0_, f32[32,128]{1,0:T(8,128)S(1)} %collective-permute-done.14.refs_1_, f32[32,128]{1,0:T(8,128)S(1)} %collective-permute-done.15.refs_2_, f32[32,128]{1,0:T(8,128)S(1)} %sum_over.3.refs_3_, ...), custom_call_target="tpu_custom_call" | custom-call | tf_op jit(solution)/shard_map/solve_and_project/pallas_call | solution.py:391
  (2 shorter events, 0.0 us)
Async XLA Ops:
  3.0 19.8 %collective-permute-start = (bf16[8,32,256]{2,1,0:T(8,128)(2,1)S(1)}, bf16[8,32,256]{2,1,0:T(8,128)(2,1)S(1)}, u32[]{:S(2)}, u32[]{:S(2)}) collective-permute-start(bf16[8,32,256]{2,1,0:T(8,128)(2,1)S(1)} %get-tuple-element.20), channel_id=1, source_target_pairs={{0,16},{4,20},{8,24},{12,28},{16,0},{20,4},{24,8},{28,12},{1,17},{... | collective-permute-start | bytes 393224 | tf_op jit(solution)/shard_map/ppermute | solution.py:410
  7.1 19.7 %collective-permute-start.1 = (bf16[8,32,256]{2,1,0:T(8,128)(2,1)S(1)}, bf16[8,32,256]{2,1,0:T(8,128)(2,1)S(1)}, u32[]{:S(2)}, u32[]{:S(2)}) collective-permute-start(bf16[8,32,256]{2,1,0:T(8,128)(2,1)S(1)} %get-tuple-element.21), channel_id=1, source_target_pairs={{0,20},{4,16},{8,28},{12,24},{16,4},{20,0},{24,12},{28,8},{1,21},{... | collective-permute-start | bytes 393224 | tf_op jit(solution)/shard_map/ppermute | solution.py:410
  8.4 29.8 %copy-start.1 = (f32[8]{0:T(128)S(1)}, f32[8]{0:T(128)}, u32[]{:S(2)}) copy-start(f32[8]{0:T(128)} %param.7) | copy-start | bytes 100
  8.4 29.9 %copy-start = (s32[8,256]{1,0:T(8,128)S(1)}, s32[8,256]{1,0:T(8,128)}, u32[]{:S(2)}) copy-start(s32[8,256]{1,0:T(8,128)} %spins_ref.1) | copy-start | bytes 24580
  11.6 21.8 %collective-permute-start.2 = (bf16[8,32,256]{2,1,0:T(8,128)(2,1)S(1)}, bf16[8,32,256]{2,1,0:T(8,128)(2,1)S(1)}, u32[]{:S(2)}, u32[]{:S(2)}) collective-permute-start(bf16[8,32,256]{2,1,0:T(8,128)(2,1)S(1)} %get-tuple-element.28), channel_id=1, source_target_pairs={{0,16},{4,20},{8,24},{12,28},{16,0},{20,4},{24,8},{28,12},{1,17},{... | collective-permute-start | bytes 393224 | tf_op jit(solution)/shard_map/ppermute | solution.py:410
  14.3 23.7 %collective-permute-start.3 = (bf16[8,32,256]{2,1,0:T(8,128)(2,1)S(1)}, bf16[8,32,256]{2,1,0:T(8,128)(2,1)S(1)}, u32[]{:S(2)}, u32[]{:S(2)}) collective-permute-start(bf16[8,32,256]{2,1,0:T(8,128)(2,1)S(1)} %get-tuple-element.29), channel_id=1, source_target_pairs={{0,20},{4,16},{8,28},{12,24},{16,4},{20,0},{24,12},{28,8},{1,21},{... | collective-permute-start | bytes 393224 | tf_op jit(solution)/shard_map/ppermute | solution.py:410
  14.3 30.9 %collective-permute-start.4 = (bf16[8,64,256]{2,1,0:T(8,128)(2,1)}, bf16[8,64,256]{2,1,0:T(8,128)(2,1)S(1)}, u32[]{:S(2)}, u32[]{:S(2)}) collective-permute-start(bf16[8,64,256]{2,1,0:T(8,128)(2,1)} %get-tuple-element.30), channel_id=1, source_target_pairs={{0,12},{4,8},{8,4},{12,0},{16,28},{20,24},{24,20},{28,16},{1,13},{... | collective-permute-start | bytes 786440 | tf_op jit(solution)/shard_map/ppermute | solution.py:410
  22.7 22.5 %collective-permute-start.5 = (bf16[8,64,256]{2,1,0:T(8,128)(2,1)}, bf16[8,64,256]{2,1,0:T(8,128)(2,1)S(1)}, u32[]{:S(2)}, u32[]{:S(2)}) collective-permute-start(bf16[8,64,256]{2,1,0:T(8,128)(2,1)} %get-tuple-element.31), channel_id=1, source_target_pairs={{0,24},{4,28},{8,16},{12,20},{16,8},{20,12},{24,0},{28,4},{1,25},{... | collective-permute-start | bytes 786440 | tf_op jit(solution)/shard_map/ppermute | solution.py:410
  26.8 21.7 %collective-permute-start.6 = (bf16[8,64,256]{2,1,0:T(8,128)(2,1)S(1)}, bf16[8,64,256]{2,1,0:T(8,128)(2,1)S(1)}, u32[]{:S(2)}, u32[]{:S(2)}) collective-permute-start(bf16[8,64,256]{2,1,0:T(8,128)(2,1)S(1)} %get-tuple-element.32), channel_id=1, source_target_pairs={{0,8},{4,12},{8,0},{12,4},{16,24},{20,28},{24,16},{28,20},{1,9},{5... | collective-permute-start | bytes 786440 | tf_op jit(solution)/shard_map/ppermute | solution.py:410
  33.4 15.1 %collective-permute-start.7 = (bf16[8,64,256]{2,1,0:T(8,128)(2,1)}, bf16[8,64,256]{2,1,0:T(8,128)(2,1)S(1)}, u32[]{:S(2)}, u32[]{:S(2)}) collective-permute-start(bf16[8,64,256]{2,1,0:T(8,128)(2,1)} %get-tuple-element.33), channel_id=1, source_target_pairs={{0,28},{4,24},{8,20},{12,16},{16,12},{20,8},{24,4},{28,0},{1,29},{... | collective-permute-start | bytes 786440 | tf_op jit(solution)/shard_map/ppermute | solution.py:410
  38.0 12.4 %collective-permute-start.8 = (bf16[8,64,256]{2,1,0:T(8,128)(2,1)S(1)}, bf16[8,64,256]{2,1,0:T(8,128)(2,1)S(1)}, u32[]{:S(2)}, u32[]{:S(2)}) collective-permute-start(bf16[8,64,256]{2,1,0:T(8,128)(2,1)S(1)} %get-tuple-element.34), channel_id=1, source_target_pairs={{0,4},{4,0},{8,12},{12,8},{16,20},{20,16},{24,28},{28,24},{1,5},{5... | collective-permute-start | bytes 786440 | tf_op jit(solution)/shard_map/ppermute | solution.py:410
  51.9 1.2 %collective-permute-start.9 = (f32[32,128]{1,0:T(8,128)S(1)}, f32[32,128]{1,0:T(8,128)S(1)}, u32[]{:S(2)}, u32[]{:S(2)}) collective-permute-start(f32[32,128]{1,0:T(8,128)S(1)} %gram_partial.1.refs_1_), channel_id=1, source_target_pairs={{0,1},{1,0},{2,3},{3,2},{4,5},{5,4},{6,7},{7,6},{8,9},{9,8},{10,11... | collective-permute-start | bytes 49160 | tf_op jit(solution)/shard_map/ppermute | solution.py:322
  53.2 6.5 %collective-permute-start.10 = (f32[32,128]{1,0:T(8,128)S(1)}, f32[32,128]{1,0:T(8,128)S(1)}, u32[]{:S(2)}, u32[]{:S(2)}) collective-permute-start(f32[32,128]{1,0:T(8,128)S(1)} %sum_over.2.refs_3_), channel_id=1, source_target_pairs={{0,27},{1,26},{2,25},{3,24},{4,31},{5,30},{6,29},{7,28},{8,19},{9,... | collective-permute-start | bytes 49160 | tf_op jit(solution)/shard_map/ppermute | solution.py:322
  58.2 5.0 %collective-permute-start.11 = (f32[32,128]{1,0:T(8,128)S(1)}, f32[32,128]{1,0:T(8,128)S(1)}, u32[]{:S(2)}, u32[]{:S(2)}) collective-permute-start(f32[32,128]{1,0:T(8,128)S(1)} %sum_over.2.refs_3_), channel_id=1, source_target_pairs={{0,25},{1,24},{2,27},{3,26},{4,29},{5,28},{6,31},{7,30},{8,17},{9,... | collective-permute-start | bytes 49160 | tf_op jit(solution)/shard_map/ppermute | solution.py:322
  58.2 5.0 %collective-permute-start.12 = (f32[32,128]{1,0:T(8,128)S(1)}, f32[32,128]{1,0:T(8,128)S(1)}, u32[]{:S(2)}, u32[]{:S(2)}) collective-permute-start(f32[32,128]{1,0:T(8,128)S(1)} %sum_over.2.refs_3_), channel_id=1, source_target_pairs={{0,3},{1,2},{2,1},{3,0},{4,7},{5,6},{6,5},{7,4},{8,11},{9,10},{10,... | collective-permute-start | bytes 49160 | tf_op jit(solution)/shard_map/ppermute | solution.py:322
  63.2 4.1 %collective-permute-start.13 = (f32[32,128]{1,0:T(8,128)S(1)}, f32[32,128]{1,0:T(8,128)S(1)}, u32[]{:S(2)}, u32[]{:S(2)}) collective-permute-start(f32[32,128]{1,0:T(8,128)S(1)} %sum_over.3.refs_3_), channel_id=1, source_target_pairs={{0,13},{1,12},{2,15},{3,14},{4,9},{5,8},{6,11},{7,10},{8,5},{9,4},... | collective-permute-start | bytes 49160 | tf_op jit(solution)/shard_map/ppermute | solution.py:322
  63.7 3.7 %collective-permute-start.14 = (f32[32,128]{1,0:T(8,128)S(1)}, f32[32,128]{1,0:T(8,128)S(1)}, u32[]{:S(2)}, u32[]{:S(2)}) collective-permute-start(f32[32,128]{1,0:T(8,128)S(1)} %sum_over.3.refs_3_), channel_id=1, source_target_pairs={{0,9},{1,8},{2,11},{3,10},{4,13},{5,12},{6,15},{7,14},{8,1},{9,0},... | collective-permute-start | bytes 49160 | tf_op jit(solution)/shard_map/ppermute | solution.py:322
  65.4 3.2 %collective-permute-start.15 = (f32[32,128]{1,0:T(8,128)S(1)}, f32[32,128]{1,0:T(8,128)S(1)}, u32[]{:S(2)}, u32[]{:S(2)}) collective-permute-start(f32[32,128]{1,0:T(8,128)S(1)} %sum_over.3.refs_3_), channel_id=1, source_target_pairs={{0,5},{1,4},{2,7},{3,6},{4,1},{5,0},{6,3},{7,2},{8,13},{9,12},{10,... | collective-permute-start | bytes 49160 | tf_op jit(solution)/shard_map/ppermute | solution.py:322

commit v28 on v27

--- a/solution.py
+++ b/solution.py
@@ -34,7 +34,7 @@
 
 
 def split_partners(owners, split):
-    return [owners // 2, owners // 2 + 1] if split > 1 else []
+    return [owners - 2, owners // 2] if split > 1 else []
 
 
 def in_turn(blocks, split):

time: 72.2 us -> 73.1 us (1.012)
  starting transfers between devices: 27.1 us -> 31.6 us
  waiting for transfers between devices: 33.4 us -> 29.7 us
    ppermute x9, starting transfers between devices: 18.1 us -> 23.6 us  [body(): blocks[k][part] = lax.ppermute(blocks[k][part], 'samp', perm)]
    ppermute x9, waiting for transfers between devices: 25.7 us -> 23.5 us  [body(): blocks[k][part] = lax.ppermute(blocks[k][part], 'samp', perm)]
    ppermute x7, waiting for transfers between devices: 7.67 us -> 6.17 us  [partners(): return [lax.ppermute(value, axes, perm) for perm in perms] + [value]]
    ppermute x7, starting transfers between devices: 8.95 us -> 8.04 us  [partners(): return [lax.ppermute(value, axes, perm) for perm in perms] + [value]]
  transfers between devices with their start and end apart: 16 -> 16, of which waited for: 12 -> 9; matrix products, arithmetic and copies ran while one was open for 0% -> 0% of each run, Pallas kernels for 5% -> 5%
where the time goes in v28:
time: 73.1 us; the launch traced here: 72.9 us
  starting transfers between devices  31.6 us (43%)
  waiting for transfers between devices  29.7 us (41%)
  Pallas kernels  10.8 us (15%)
    ppermute x9, starting transfers between devices, body(): blocks[k][part] = lax.ppermute(blocks[k][part], 'samp', perm)  23.6 us
    ppermute x9, waiting for transfers between devices, body(): blocks[k][part] = lax.ppermute(blocks[k][part], 'samp', perm)  23.5 us
    ppermute x7, starting transfers between devices, partners(): return [lax.ppermute(value, axes, perm) for perm in perms] + [value]  8.04 us
    ppermute x7, waiting for transfers between devices, partners(): return [lax.ppermute(value, axes, perm) for perm in perms] + [value]  6.17 us
    pallas_call x2, Pallas kernels, jac_rows(): pl.pallas_call(functools.partial(jac_kernel, part * mats, joined), in_spe...  5.6 us
    pallas_call x1, Pallas kernels, solve_and_project(): pl.pallas_call(functools.partial(solve_kernel, len(sums), len(blocks)), o...  3.45 us
    pallas_call x1, Pallas kernels, gram_partial(): pl.pallas_call(functools.partial(gram_kernel, len(blocks)), out_shape=jax...  1.52 us
  transfers between devices with their start and end apart: 16, of which 9 were waited for; matrix products, arithmetic and copies ran while one was open for 0% of the time, Pallas kernels for 5%

profile of v28, /device:TPU:0, one launch (start us, length us, event | category | flops | bytes accessed | tf_op | source)
XLA Modules:
  0.0 72.9 jit_solution(10993447112843230020)
XLA Ops:
  0.6 2.3 %jac_rows.2 = (bf16[8,32,256]{2,1,0:T(8,128)(2,1)S(1)}, bf16[8,32,256]{2,1,0:T(8,128)(2,1)S(1)}, bf16[8,32,256]{2,1,0:T(8,128)(2,1)S(1)}, bf16[8,32,256]{2,1,0:T...) custom-call(bf16[8,2,256,256]{3,2,1,0:T(8,128)(2,1)} %act_hbm.3, ...), custom_call_target="tpu_custom_call" | custom-call | flops 268435456 | bytes 3145728 | tf_op jit(solution)/shard_map/jac_rows/pallas_call | solution.py:104
  3.0 5.1 %collective-permute-start = (bf16[8,32,256]{2,1,0:T(8,128)(2,1)S(1)}, bf16[8,32,256]{2,1,0:T(8,128)(2,1)S(1)}, u32[]{:S(2)}, u32[]{:S(2)}) collective-permute-start(bf16[8,32,256]{2,1,0:T(8,128)(2,1)S(1)} %get-tuple-element.20), channel_id=1, source_target_pairs={{0,24},{4,28},{8,16},{12,20},{16,8},{20,12},{24,0},{28,4},{1,25},{... | collective-permute-start | bytes 393224 | tf_op jit(solution)/shard_map/ppermute | solution.py:410
  8.1 0.0 collective-permute-start.1
  8.1 0.0 copy-start.1
  8.1 0.0 copy-start
  8.1 3.3 %jac_rows.3 = (bf16[8,64,256]{2,1,0:T(8,128)(2,1)S(1)}, bf16[8,64,256]{2,1,0:T(8,128)(2,1)S(1)}, bf16[8,64,256]{2,1,0:T(8,128)(2,1)S(1)}, bf16[8,64,256]{2,1,0:T...) custom-call(bf16[8,2,256,256]{3,2,1,0:T(8,128)(2,1)} %act_hbm.3, ...), custom_call_target="tpu_custom_call" | custom-call | flops 268435456 | bytes 3145728 | tf_op jit(solution)/shard_map/jac_rows/pallas_call | solution.py:104
  11.4 2.0 %collective-permute-start.2 = (bf16[8,32,256]{2,1,0:T(8,128)(2,1)S(1)}, bf16[8,32,256]{2,1,0:T(8,128)(2,1)S(1)}, u32[]{:S(2)}, u32[]{:S(2)}) collective-permute-start(bf16[8,32,256]{2,1,0:T(8,128)(2,1)S(1)} %get-tuple-element.28), channel_id=1, source_target_pairs={{0,24},{4,28},{8,16},{12,20},{16,8},{20,12},{24,0},{28,4},{1,25},{... | collective-permute-start | bytes 393224 | tf_op jit(solution)/shard_map/ppermute | solution.py:410
  13.3 1.1 %collective-permute-start.3 = (bf16[8,32,256]{2,1,0:T(8,128)(2,1)S(1)}, bf16[8,32,256]{2,1,0:T(8,128)(2,1)S(1)}, u32[]{:S(2)}, u32[]{:S(2)}) collective-permute-start(bf16[8,32,256]{2,1,0:T(8,128)(2,1)S(1)} %get-tuple-element.29), channel_id=1, source_target_pairs={{0,16},{4,20},{8,24},{12,28},{16,0},{20,4},{24,8},{28,12},{1,17},{... | collective-permute-start | bytes 393224 | tf_op jit(solution)/shard_map/ppermute | solution.py:410
  14.4 2.3 %collective-permute-start.4 = (bf16[8,64,256]{2,1,0:T(8,128)(2,1)}, bf16[8,64,256]{2,1,0:T(8,128)(2,1)S(1)}, u32[]{:S(2)}, u32[]{:S(2)}) collective-permute-start(bf16[8,64,256]{2,1,0:T(8,128)(2,1)} %get-tuple-element.30), channel_id=1, source_target_pairs={{0,12},{4,8},{8,4},{12,0},{16,28},{20,24},{24,20},{28,16},{1,13},{... | collective-permute-start | bytes 786440 | tf_op jit(solution)/shard_map/ppermute | solution.py:410
  16.8 0.0 collective-permute-done.refs_0_.refs_4_
  16.8 8.9 %collective-permute-start.5 = (bf16[8,64,256]{2,1,0:T(8,128)(2,1)}, bf16[8,64,256]{2,1,0:T(8,128)(2,1)S(1)}, u32[]{:S(2)}, u32[]{:S(2)}) collective-permute-start(bf16[8,64,256]{2,1,0:T(8,128)(2,1)} %get-tuple-element.31), channel_id=1, source_target_pairs={{0,20},{4,16},{8,28},{12,24},{16,4},{20,0},{24,12},{28,8},{1,21},{... | collective-permute-start | bytes 786440 | tf_op jit(solution)/shard_map/ppermute | solution.py:410
  25.7 0.5 collective-permute-done.1.refs_1_.refs_5_
  26.2 0.0 collective-permute-start.6
  26.2 0.0 collective-permute-done.2.refs_2_.refs_6_
  26.2 3.3 %collective-permute-start.7 = (bf16[8,64,256]{2,1,0:T(8,128)(2,1)}, bf16[8,64,256]{2,1,0:T(8,128)(2,1)S(1)}, u32[]{:S(2)}, u32[]{:S(2)}) collective-permute-start(bf16[8,64,256]{2,1,0:T(8,128)(2,1)} %get-tuple-element.33), channel_id=1, source_target_pairs={{0,28},{4,24},{8,20},{12,16},{16,12},{20,8},{24,4},{28,0},{1,29},{... | collective-permute-start | bytes 786440 | tf_op jit(solution)/shard_map/ppermute | solution.py:410
  29.5 8.4 %collective-permute-done.3.refs_3_.refs_7_ = bf16[8,32,256]{2,1,0:T(8,128)(2,1)S(1)} collective-permute-done((bf16[8,32,256]{2,1,0:T(8,128)(2,1)S(1)}, bf16[8,32,256]{2,1,0:T(8,128)(2,1)S(1)}, u32[]{:S(2)}, u32[]{:S(2)}) %collective-permute-start.3) | collective-permute-done | bytes 131104 | tf_op jit(solution)/shard_map/ppermute | solution.py:410
  38.0 0.9 %collective-permute-start.8 = (bf16[8,64,256]{2,1,0:T(8,128)(2,1)S(1)}, bf16[8,64,256]{2,1,0:T(8,128)(2,1)S(1)}, u32[]{:S(2)}, u32[]{:S(2)}) collective-permute-start(bf16[8,64,256]{2,1,0:T(8,128)(2,1)S(1)} %get-tuple-element.34), channel_id=1, source_target_pairs={{0,4},{4,0},{8,12},{12,8},{16,20},{20,16},{24,28},{28,24},{1,5},{5... | collective-permute-start | bytes 786440 | tf_op jit(solution)/shard_map/ppermute | solution.py:410
  38.8 0.0 copy-done.1
  38.8 0.1 copy.6.offdiag_ref
  38.9 0.0 copy-done
  38.9 0.2 packed_energy.1.refs_10_
  39.2 0.0 collective-permute-done.4.refs_4_.refs_8_
  39.2 10.0 %collective-permute-done.5.refs_5_.refs_9_ = bf16[8,64,256]{2,1,0:T(8,128)(2,1)S(1)} collective-permute-done((bf16[8,64,256]{2,1,0:T(8,128)(2,1)}, bf16[8,64,256]{2,1,0:T(8,128)(2,1)S(1)}, u32[]{:S(2)}, u32[]{:S(2)}) %collective-permute-start.5) | collective-permute-done | bytes 262176 | tf_op jit(solution)/shard_map/ppermute | solution.py:410
  49.2 0.0 collective-permute-done.6.refs_6_.refs_10_
  49.2 0.0 collective-permute-done.7.refs_7_.refs_11_
  49.2 4.5 %collective-permute-done.8.refs_8_.refs_12_ = bf16[8,64,256]{2,1,0:T(8,128)(2,1)S(1)} collective-permute-done((bf16[8,64,256]{2,1,0:T(8,128)(2,1)S(1)}, bf16[8,64,256]{2,1,0:T(8,128)(2,1)S(1)}, u32[]{:S(2)}, u32[]{:S(2)}) %collective-permute-start.8) | collective-permute-done | bytes 262176 | tf_op jit(solution)/shard_map/ppermute | solution.py:410
  53.7 1.5 %gram_partial.1.refs_1_ = f32[32,128]{1,0:T(8,128)S(1)} custom-call(bf16[8,32,256]{2,1,0:T(8,128)(2,1)S(1)} %collective-permute-done.refs_0_.refs_4_, bf16[8,32,256]{2,1,0:T(8,128)(2,1)S(1)} %collective-permute-done.1.refs_1_.refs_5_, bf16[8,32,256]{2,1,0:T(8,128)(2,1)S(1)} %collective-permute-done.2.refs_2_.refs_6_, ...), custom_call_target="tpu_custom_call" | custom-call | flops 134217728 | bytes 2097152 | tf_op jit(solution)/shard_map/gram_partial/pallas_call | solution.py:214
  55.2 0.0 collective-permute-start.9
  55.3 1.2 %collective-permute-done.9.refs_0_ = f32[32,128]{1,0:T(8,128)S(1)} collective-permute-done((f32[32,128]{1,0:T(8,128)S(1)}, f32[32,128]{1,0:T(8,128)S(1)}, u32[]{:S(2)}, u32[]{:S(2)}) %collective-permute-start.9) | collective-permute-done | bytes 16416 | tf_op jit(solution)/shard_map/ppermute | solution.py:322
  56.5 3.0 %collective-permute-start.10 = (f32[32,128]{1,0:T(8,128)S(1)}, f32[32,128]{1,0:T(8,128)S(1)}, u32[]{:S(2)}, u32[]{:S(2)}) collective-permute-start(f32[32,128]{1,0:T(8,128)S(1)} %sum_over.2.refs_3_), channel_id=1, source_target_pairs={{0,27},{1,26},{2,25},{3,24},{4,31},{5,30},{6,29},{7,28},{8,19},{9,... | collective-permute-start | bytes 49160 | tf_op jit(solution)/shard_map/ppermute | solution.py:322
  59.5 1.4 %collective-permute-start.11 = (f32[32,128]{1,0:T(8,128)S(1)}, f32[32,128]{1,0:T(8,128)S(1)}, u32[]{:S(2)}, u32[]{:S(2)}) collective-permute-start(f32[32,128]{1,0:T(8,128)S(1)} %sum_over.2.refs_3_), channel_id=1, source_target_pairs={{0,25},{1,24},{2,27},{3,26},{4,29},{5,28},{6,31},{7,30},{8,17},{9,... | collective-permute-start | bytes 49160 | tf_op jit(solution)/shard_map/ppermute | solution.py:322
  60.9 0.3 collective-permute-start.12
  61.2 1.1 %collective-permute-done.10.refs_0_ = f32[32,128]{1,0:T(8,128)S(1)} collective-permute-done((f32[32,128]{1,0:T(8,128)S(1)}, f32[32,128]{1,0:T(8,128)S(1)}, u32[]{:S(2)}, u32[]{:S(2)}) %collective-permute-start.10) | collective-permute-done | bytes 16416 | tf_op jit(solution)/shard_map/ppermute | solution.py:322
  62.3 2.1 %collective-permute-done.11.refs_1_ = f32[32,128]{1,0:T(8,128)S(1)} collective-permute-done((f32[32,128]{1,0:T(8,128)S(1)}, f32[32,128]{1,0:T(8,128)S(1)}, u32[]{:S(2)}, u32[]{:S(2)}) %collective-permute-start.11) | collective-permute-done | bytes 16416 | tf_op jit(solution)/shard_map/ppermute | solution.py:322
  64.5 0.0 collective-permute-done.12.refs_2_
  64.5 0.1 collective-permute-start.13
  64.6 1.8 %collective-permute-start.14 = (f32[32,128]{1,0:T(8,128)S(1)}, f32[32,128]{1,0:T(8,128)S(1)}, u32[]{:S(2)}, u32[]{:S(2)}) collective-permute-start(f32[32,128]{1,0:T(8,128)S(1)} %sum_over.3.refs_3_), channel_id=1, source_target_pairs={{0,9},{1,8},{2,11},{3,10},{4,13},{5,12},{6,15},{7,14},{8,1},{9,0},... | collective-permute-start | bytes 49160 | tf_op jit(solution)/shard_map/ppermute | solution.py:322
  66.3 1.4 %collective-permute-start.15 = (f32[32,128]{1,0:T(8,128)S(1)}, f32[32,128]{1,0:T(8,128)S(1)}, u32[]{:S(2)}, u32[]{:S(2)}) collective-permute-start(f32[32,128]{1,0:T(8,128)S(1)} %sum_over.3.refs_3_), channel_id=1, source_target_pairs={{0,5},{1,4},{2,7},{3,6},{4,1},{5,0},{6,3},{7,2},{8,13},{9,12},{10,... | collective-permute-start | bytes 49160 | tf_op jit(solution)/shard_map/ppermute | solution.py:322
  67.7 0.9 %collective-permute-done.13.refs_0_ = f32[32,128]{1,0:T(8,128)S(1)} collective-permute-done((f32[32,128]{1,0:T(8,128)S(1)}, f32[32,128]{1,0:T(8,128)S(1)}, u32[]{:S(2)}, u32[]{:S(2)}) %collective-permute-start.13) | collective-permute-done | bytes 16416 | tf_op jit(solution)/shard_map/ppermute | solution.py:322
  68.6 0.0 collective-permute-done.14.refs_1_
  68.6 0.9 %collective-permute-done.15.refs_2_ = f32[32,128]{1,0:T(8,128)S(1)} collective-permute-done((f32[32,128]{1,0:T(8,128)S(1)}, f32[32,128]{1,0:T(8,128)S(1)}, u32[]{:S(2)}, u32[]{:S(2)}) %collective-permute-start.15) | collective-permute-done | bytes 16416 | tf_op jit(solution)/shard_map/ppermute | solution.py:322
  69.5 3.5 %solve_and_project.1 = (f32[1,8]{1,0:T(1,128)}, f32[2,32,256]{2,1,0:T(8,128)}) custom-call(f32[32,128]{1,0:T(8,128)S(1)} %collective-permute-done.13.refs_0_, f32[32,128]{1,0:T(8,128)S(1)} %collective-permute-done.14.refs_1_, f32[32,128]{1,0:T(8,128)S(1)} %collective-permute-done.15.refs_2_, f32[32,128]{1,0:T(8,128)S(1)} %sum_over.3.refs_3_, ...), custom_call_target="tpu_custom_call" | custom-call | tf_op jit(solution)/shard_map/solve_and_project/pallas_call | solution.py:391
  (2 shorter events, 0.0 us)
Async XLA Ops:
  3.0 13.8 %collective-permute-start = (bf16[8,32,256]{2,1,0:T(8,128)(2,1)S(1)}, bf16[8,32,256]{2,1,0:T(8,128)(2,1)S(1)}, u32[]{:S(2)}, u32[]{:S(2)}) collective-permute-start(bf16[8,32,256]{2,1,0:T(8,128)(2,1)S(1)} %get-tuple-element.20), channel_id=1, source_target_pairs={{0,24},{4,28},{8,16},{12,20},{16,8},{20,12},{24,0},{28,4},{1,25},{... | collective-permute-start | bytes 393224 | tf_op jit(solution)/shard_map/ppermute | solution.py:410
  8.1 18.1 %collective-permute-start.1 = (bf16[8,32,256]{2,1,0:T(8,128)(2,1)S(1)}, bf16[8,32,256]{2,1,0:T(8,128)(2,1)S(1)}, u32[]{:S(2)}, u32[]{:S(2)}) collective-permute-start(bf16[8,32,256]{2,1,0:T(8,128)(2,1)S(1)} %get-tuple-element.21), channel_id=1, source_target_pairs={{0,16},{4,20},{8,24},{12,28},{16,0},{20,4},{24,8},{28,12},{1,17},{... | collective-permute-start | bytes 393224 | tf_op jit(solution)/shard_map/ppermute | solution.py:410
  8.1 30.7 %copy-start.1 = (f32[8]{0:T(128)S(1)}, f32[8]{0:T(128)}, u32[]{:S(2)}) copy-start(f32[8]{0:T(128)} %param.7) | copy-start | bytes 100
  8.1 30.8 %copy-start = (s32[8,256]{1,0:T(8,128)S(1)}, s32[8,256]{1,0:T(8,128)}, u32[]{:S(2)}) copy-start(s32[8,256]{1,0:T(8,128)} %spins_ref.1) | copy-start | bytes 24580
  11.4 14.9 %collective-permute-start.2 = (bf16[8,32,256]{2,1,0:T(8,128)(2,1)S(1)}, bf16[8,32,256]{2,1,0:T(8,128)(2,1)S(1)}, u32[]{:S(2)}, u32[]{:S(2)}) collective-permute-start(bf16[8,32,256]{2,1,0:T(8,128)(2,1)S(1)} %get-tuple-element.28), channel_id=1, source_target_pairs={{0,24},{4,28},{8,16},{12,20},{16,8},{20,12},{24,0},{28,4},{1,25},{... | collective-permute-start | bytes 393224 | tf_op jit(solution)/shard_map/ppermute | solution.py:410
  13.3 24.6 %collective-permute-start.3 = (bf16[8,32,256]{2,1,0:T(8,128)(2,1)S(1)}, bf16[8,32,256]{2,1,0:T(8,128)(2,1)S(1)}, u32[]{:S(2)}, u32[]{:S(2)}) collective-permute-start(bf16[8,32,256]{2,1,0:T(8,128)(2,1)S(1)} %get-tuple-element.29), channel_id=1, source_target_pairs={{0,16},{4,20},{8,24},{12,28},{16,0},{20,4},{24,8},{28,12},{1,17},{... | collective-permute-start | bytes 393224 | tf_op jit(solution)/shard_map/ppermute | solution.py:410
  14.4 24.7 %collective-permute-start.4 = (bf16[8,64,256]{2,1,0:T(8,128)(2,1)}, bf16[8,64,256]{2,1,0:T(8,128)(2,1)S(1)}, u32[]{:S(2)}, u32[]{:S(2)}) collective-permute-start(bf16[8,64,256]{2,1,0:T(8,128)(2,1)} %get-tuple-element.30), channel_id=1, source_target_pairs={{0,12},{4,8},{8,4},{12,0},{16,28},{20,24},{24,20},{28,16},{1,13},{... | collective-permute-start | bytes 786440 | tf_op jit(solution)/shard_map/ppermute | solution.py:410
  16.8 32.4 %collective-permute-start.5 = (bf16[8,64,256]{2,1,0:T(8,128)(2,1)}, bf16[8,64,256]{2,1,0:T(8,128)(2,1)S(1)}, u32[]{:S(2)}, u32[]{:S(2)}) collective-permute-start(bf16[8,64,256]{2,1,0:T(8,128)(2,1)} %get-tuple-element.31), channel_id=1, source_target_pairs={{0,20},{4,16},{8,28},{12,24},{16,4},{20,0},{24,12},{28,8},{1,21},{... | collective-permute-start | bytes 786440 | tf_op jit(solution)/shard_map/ppermute | solution.py:410
  26.2 22.9 %collective-permute-start.6 = (bf16[8,64,256]{2,1,0:T(8,128)(2,1)S(1)}, bf16[8,64,256]{2,1,0:T(8,128)(2,1)S(1)}, u32[]{:S(2)}, u32[]{:S(2)}) collective-permute-start(bf16[8,64,256]{2,1,0:T(8,128)(2,1)S(1)} %get-tuple-element.32), channel_id=1, source_target_pairs={{0,8},{4,12},{8,0},{12,4},{16,24},{20,28},{24,16},{28,20},{1,9},{5... | collective-permute-start | bytes 786440 | tf_op jit(solution)/shard_map/ppermute | solution.py:410
  26.2 22.9 %collective-permute-start.7 = (bf16[8,64,256]{2,1,0:T(8,128)(2,1)}, bf16[8,64,256]{2,1,0:T(8,128)(2,1)S(1)}, u32[]{:S(2)}, u32[]{:S(2)}) collective-permute-start(bf16[8,64,256]{2,1,0:T(8,128)(2,1)} %get-tuple-element.33), channel_id=1, source_target_pairs={{0,28},{4,24},{8,20},{12,16},{16,12},{20,8},{24,4},{28,0},{1,29},{... | collective-permute-start | bytes 786440 | tf_op jit(solution)/shard_map/ppermute | solution.py:410
  38.0 15.7 %collective-permute-start.8 = (bf16[8,64,256]{2,1,0:T(8,128)(2,1)S(1)}, bf16[8,64,256]{2,1,0:T(8,128)(2,1)S(1)}, u32[]{:S(2)}, u32[]{:S(2)}) collective-permute-start(bf16[8,64,256]{2,1,0:T(8,128)(2,1)S(1)} %get-tuple-element.34), channel_id=1, source_target_pairs={{0,4},{4,0},{8,12},{12,8},{16,20},{20,16},{24,28},{28,24},{1,5},{5... | collective-permute-start | bytes 786440 | tf_op jit(solution)/shard_map/ppermute | solution.py:410
  55.2 1.2 %collective-permute-start.9 = (f32[32,128]{1,0:T(8,128)S(1)}, f32[32,128]{1,0:T(8,128)S(1)}, u32[]{:S(2)}, u32[]{:S(2)}) collective-permute-start(f32[32,128]{1,0:T(8,128)S(1)} %gram_partial.1.refs_1_), channel_id=1, source_target_pairs={{0,1},{1,0},{2,3},{3,2},{4,5},{5,4},{6,7},{7,6},{8,9},{9,8},{10,11... | collective-permute-start | bytes 49160 | tf_op jit(solution)/shard_map/ppermute | solution.py:322
  56.5 5.9 %collective-permute-start.10 = (f32[32,128]{1,0:T(8,128)S(1)}, f32[32,128]{1,0:T(8,128)S(1)}, u32[]{:S(2)}, u32[]{:S(2)}) collective-permute-start(f32[32,128]{1,0:T(8,128)S(1)} %sum_over.2.refs_3_), channel_id=1, source_target_pairs={{0,27},{1,26},{2,25},{3,24},{4,31},{5,30},{6,29},{7,28},{8,19},{9,... | collective-permute-start | bytes 49160 | tf_op jit(solution)/shard_map/ppermute | solution.py:322
  59.5 5.0 %collective-permute-start.11 = (f32[32,128]{1,0:T(8,128)S(1)}, f32[32,128]{1,0:T(8,128)S(1)}, u32[]{:S(2)}, u32[]{:S(2)}) collective-permute-start(f32[32,128]{1,0:T(8,128)S(1)} %sum_over.2.refs_3_), channel_id=1, source_target_pairs={{0,25},{1,24},{2,27},{3,26},{4,29},{5,28},{6,31},{7,30},{8,17},{9,... | collective-permute-start | bytes 49160 | tf_op jit(solution)/shard_map/ppermute | solution.py:322
  60.9 3.5 %collective-permute-start.12 = (f32[32,128]{1,0:T(8,128)S(1)}, f32[32,128]{1,0:T(8,128)S(1)}, u32[]{:S(2)}, u32[]{:S(2)}) collective-permute-start(f32[32,128]{1,0:T(8,128)S(1)} %sum_over.2.refs_3_), channel_id=1, source_target_pairs={{0,3},{1,2},{2,1},{3,0},{4,7},{5,6},{6,5},{7,4},{8,11},{9,10},{10,... | collective-permute-start | bytes 49160 | tf_op jit(solution)/shard_map/ppermute | solution.py:322
  64.5 4.1 %collective-permute-start.13 = (f32[32,128]{1,0:T(8,128)S(1)}, f32[32,128]{1,0:T(8,128)S(1)}, u32[]{:S(2)}, u32[]{:S(2)}) collective-permute-start(f32[32,128]{1,0:T(8,128)S(1)} %sum_over.3.refs_3_), channel_id=1, source_target_pairs={{0,13},{1,12},{2,15},{3,14},{4,9},{5,8},{6,11},{7,10},{8,5},{9,4},... | collective-permute-start | bytes 49160 | tf_op jit(solution)/shard_map/ppermute | solution.py:322
  64.6 4.1 %collective-permute-start.14 = (f32[32,128]{1,0:T(8,128)S(1)}, f32[32,128]{1,0:T(8,128)S(1)}, u32[]{:S(2)}, u32[]{:S(2)}) collective-permute-start(f32[32,128]{1,0:T(8,128)S(1)} %sum_over.3.refs_3_), channel_id=1, source_target_pairs={{0,9},{1,8},{2,11},{3,10},{4,13},{5,12},{6,15},{7,14},{8,1},{9,0},... | collective-permute-start | bytes 49160 | tf_op jit(solution)/shard_map/ppermute | solution.py:322
  66.3 3.2 %collective-permute-start.15 = (f32[32,128]{1,0:T(8,128)S(1)}, f32[32,128]{1,0:T(8,128)S(1)}, u32[]{:S(2)}, u32[]{:S(2)}) collective-permute-start(f32[32,128]{1,0:T(8,128)S(1)} %sum_over.3.refs_3_), channel_id=1, source_target_pairs={{0,5},{1,4},{2,7},{3,6},{4,1},{5,0},{6,3},{7,2},{8,13},{9,12},{10,... | collective-permute-start | bytes 49160 | tf_op jit(solution)/shard_map/ppermute | solution.py:322

commit v29 on v27

--- a/solution.py
+++ b/solution.py
@@ -362,14 +362,15 @@
     row_mean = jnp.sum(jnp.where(inside, raw, F32(0.0)), axis=1, keepdims=True) * scale
     col_mean = jnp.sum(raw, axis=0, keepdims=True) * scale
     mean = jnp.sum(row_mean, axis=0, keepdims=True) * scale
-    gram = (raw - col_mean - row_mean + mean) * scale
+    centered = raw - col_mean - row_mean + mean
     eps = (raw - col_mean) * F32(1.0 / total**0.5)
     on_diag = row == lane
     diag = jnp.where(on_diag, raw, F32(0.0))
     trace = jnp.sum(jnp.sum(diag, axis=0, keepdims=True), axis=1, keepdims=True) * scale - mean
-    shift = F32(shift_ratio) * trace * scale
-    system = jnp.where(inside, gram + jnp.where(on_diag, shift, F32(0.0)), eps)
-    weights = eliminate(system, total)
+    inverse = F32(1.0) / (trace * scale)
+    shift = jnp.where(on_diag, F32(shift_ratio), F32(0.0))
+    system = jnp.where(inside, centered * (scale * inverse) + shift, eps)
+    weights = eliminate(system, total) * inverse
     me = lax.axis_index("samp")
     own = jnp.where(row - me * local == lane, weights, F32(0.0))
     weights_ref[...] = jnp.sum(own, axis=0, keepdims=True)[:, :local]

time: 72.2 us -> 72.2 us (level)
  no operation moved by 1% of the time
where the time goes in v29:
time: 72.2 us; the launch traced here: 72.1 us
  waiting for transfers between devices  33.4 us (46%)
  starting transfers between devices  27.1 us (38%)
  Pallas kernels  10.8 us (15%)
    ppermute x9, waiting for transfers between devices, body(): blocks[k][part] = lax.ppermute(blocks[k][part], 'samp', perm)  25.7 us
    ppermute x9, starting transfers between devices, body(): blocks[k][part] = lax.ppermute(blocks[k][part], 'samp', perm)  18.1 us
    ppermute x7, starting transfers between devices, partners(): return [lax.ppermute(value, axes, perm) for perm in perms] + [value]  8.95 us
    ppermute x7, waiting for transfers between devices, partners(): return [lax.ppermute(value, axes, perm) for perm in perms] + [value]  7.67 us
    pallas_call x2, Pallas kernels, jac_rows(): pl.pallas_call(functools.partial(jac_kernel, part * mats, joined), in_spe...  5.6 us
    pallas_call x1, Pallas kernels, solve_and_project(): pl.pallas_call(functools.partial(solve_kernel, len(sums), len(blocks)), o...  3.48 us
    pallas_call x1, Pallas kernels, gram_partial(): pl.pallas_call(functools.partial(gram_kernel, len(blocks)), out_shape=jax...  1.51 us
  transfers between devices with their start and end apart: 16, of which 12 were waited for; matrix products, arithmetic and copies ran while one was open for 0% of the time, Pallas kernels for 5%

profile of v29, /device:TPU:0, one launch (start us, length us, event | category | flops | bytes accessed | tf_op | source)
XLA Modules:
  0.0 72.1 jit_solution(11905954132025874672)
XLA Ops:
  0.6 2.3 %jac_rows.2 = (bf16[8,32,256]{2,1,0:T(8,128)(2,1)S(1)}, bf16[8,32,256]{2,1,0:T(8,128)(2,1)S(1)}, bf16[8,32,256]{2,1,0:T(8,128)(2,1)S(1)}, bf16[8,32,256]{2,1,0:T...) custom-call(bf16[8,2,256,256]{3,2,1,0:T(8,128)(2,1)} %act_hbm.3, ...), custom_call_target="tpu_custom_call" | custom-call | flops 268435456 | bytes 3145728 | tf_op jit(solution)/shard_map/jac_rows/pallas_call | solution.py:104
  3.0 4.1 %collective-permute-start = (bf16[8,32,256]{2,1,0:T(8,128)(2,1)S(1)}, bf16[8,32,256]{2,1,0:T(8,128)(2,1)S(1)}, u32[]{:S(2)}, u32[]{:S(2)}) collective-permute-start(bf16[8,32,256]{2,1,0:T(8,128)(2,1)S(1)} %get-tuple-element.20), channel_id=1, source_target_pairs={{0,16},{4,20},{8,24},{12,28},{16,0},{20,4},{24,8},{28,12},{1,17},{... | collective-permute-start | bytes 393224 | tf_op jit(solution)/shard_map/ppermute | solution.py:411
  7.1 1.3 %collective-permute-start.1 = (bf16[8,32,256]{2,1,0:T(8,128)(2,1)S(1)}, bf16[8,32,256]{2,1,0:T(8,128)(2,1)S(1)}, u32[]{:S(2)}, u32[]{:S(2)}) collective-permute-start(bf16[8,32,256]{2,1,0:T(8,128)(2,1)S(1)} %get-tuple-element.21), channel_id=1, source_target_pairs={{0,20},{4,16},{8,28},{12,24},{16,4},{20,0},{24,12},{28,8},{1,21},{... | collective-permute-start | bytes 393224 | tf_op jit(solution)/shard_map/ppermute | solution.py:411
  8.4 0.0 copy-start.1
  8.4 0.0 copy-start
  8.4 3.3 %jac_rows.3 = (bf16[8,64,256]{2,1,0:T(8,128)(2,1)S(1)}, bf16[8,64,256]{2,1,0:T(8,128)(2,1)S(1)}, bf16[8,64,256]{2,1,0:T(8,128)(2,1)S(1)}, bf16[8,64,256]{2,1,0:T...) custom-call(bf16[8,2,256,256]{3,2,1,0:T(8,128)(2,1)} %act_hbm.3, ...), custom_call_target="tpu_custom_call" | custom-call | flops 268435456 | bytes 3145728 | tf_op jit(solution)/shard_map/jac_rows/pallas_call | solution.py:104
  11.6 2.7 %collective-permute-start.2 = (bf16[8,32,256]{2,1,0:T(8,128)(2,1)S(1)}, bf16[8,32,256]{2,1,0:T(8,128)(2,1)S(1)}, u32[]{:S(2)}, u32[]{:S(2)}) collective-permute-start(bf16[8,32,256]{2,1,0:T(8,128)(2,1)S(1)} %get-tuple-element.28), channel_id=1, source_target_pairs={{0,16},{4,20},{8,24},{12,28},{16,0},{20,4},{24,8},{28,12},{1,17},{... | collective-permute-start | bytes 393224 | tf_op jit(solution)/shard_map/ppermute | solution.py:411
  14.3 0.0 collective-permute-start.3
  14.3 2.8 %collective-permute-start.4 = (bf16[8,64,256]{2,1,0:T(8,128)(2,1)}, bf16[8,64,256]{2,1,0:T(8,128)(2,1)S(1)}, u32[]{:S(2)}, u32[]{:S(2)}) collective-permute-start(bf16[8,64,256]{2,1,0:T(8,128)(2,1)} %get-tuple-element.30), channel_id=1, source_target_pairs={{0,12},{4,8},{8,4},{12,0},{16,28},{20,24},{24,20},{28,16},{1,13},{... | collective-permute-start | bytes 786440 | tf_op jit(solution)/shard_map/ppermute | solution.py:411
  17.1 5.6 %collective-permute-done.refs_0_.refs_4_ = bf16[8,32,256]{2,1,0:T(8,128)(2,1)S(1)} collective-permute-done((bf16[8,32,256]{2,1,0:T(8,128)(2,1)S(1)}, bf16[8,32,256]{2,1,0:T(8,128)(2,1)S(1)}, u32[]{:S(2)}, u32[]{:S(2)}) %collective-permute-start) | collective-permute-done | bytes 131104 | tf_op jit(solution)/shard_map/ppermute | solution.py:411
  22.7 2.8 %collective-permute-start.5 = (bf16[8,64,256]{2,1,0:T(8,128)(2,1)}, bf16[8,64,256]{2,1,0:T(8,128)(2,1)S(1)}, u32[]{:S(2)}, u32[]{:S(2)}) collective-permute-start(bf16[8,64,256]{2,1,0:T(8,128)(2,1)} %get-tuple-element.31), channel_id=1, source_target_pairs={{0,24},{4,28},{8,16},{12,20},{16,8},{20,12},{24,0},{28,4},{1,25},{... | collective-permute-start | bytes 786440 | tf_op jit(solution)/shard_map/ppermute | solution.py:411
  25.5 1.2 %collective-permute-done.1.refs_1_.refs_5_ = bf16[8,32,256]{2,1,0:T(8,128)(2,1)S(1)} collective-permute-done((bf16[8,32,256]{2,1,0:T(8,128)(2,1)S(1)}, bf16[8,32,256]{2,1,0:T(8,128)(2,1)S(1)}, u32[]{:S(2)}, u32[]{:S(2)}) %collective-permute-start.1) | collective-permute-done | bytes 131104 | tf_op jit(solution)/shard_map/ppermute | solution.py:411
  26.8 0.0 collective-permute-start.6
  26.8 6.7 %collective-permute-done.2.refs_2_.refs_6_ = bf16[8,32,256]{2,1,0:T(8,128)(2,1)S(1)} collective-permute-done((bf16[8,32,256]{2,1,0:T(8,128)(2,1)S(1)}, bf16[8,32,256]{2,1,0:T(8,128)(2,1)S(1)}, u32[]{:S(2)}, u32[]{:S(2)}) %collective-permute-start.2) | collective-permute-done | bytes 131104 | tf_op jit(solution)/shard_map/ppermute | solution.py:411
  33.4 4.3 %collective-permute-start.7 = (bf16[8,64,256]{2,1,0:T(8,128)(2,1)}, bf16[8,64,256]{2,1,0:T(8,128)(2,1)S(1)}, u32[]{:S(2)}, u32[]{:S(2)}) collective-permute-start(bf16[8,64,256]{2,1,0:T(8,128)(2,1)} %get-tuple-element.33), channel_id=1, source_target_pairs={{0,28},{4,24},{8,20},{12,16},{16,12},{20,8},{24,4},{28,0},{1,29},{... | collective-permute-start | bytes 786440 | tf_op jit(solution)/shard_map/ppermute | solution.py:411
  37.7 0.3 collective-permute-done.3.refs_3_.refs_7_
  38.0 0.2 collective-permute-start.8
  38.2 0.0 copy-done.1
  38.2 0.1 copy.6.offdiag_ref
  38.3 0.0 copy-done
  38.3 0.2 packed_energy.1.refs_10_
  38.5 6.8 %collective-permute-done.4.refs_4_.refs_8_ = bf16[8,64,256]{2,1,0:T(8,128)(2,1)S(1)} collective-permute-done((bf16[8,64,256]{2,1,0:T(8,128)(2,1)}, bf16[8,64,256]{2,1,0:T(8,128)(2,1)S(1)}, u32[]{:S(2)}, u32[]{:S(2)}) %collective-permute-start.4) | collective-permute-done | bytes 262176 | tf_op jit(solution)/shard_map/ppermute | solution.py:411
  45.3 0.0 collective-permute-done.5.refs_5_.refs_9_
  45.3 3.2 %collective-permute-done.6.refs_6_.refs_10_ = bf16[8,64,256]{2,1,0:T(8,128)(2,1)S(1)} collective-permute-done((bf16[8,64,256]{2,1,0:T(8,128)(2,1)S(1)}, bf16[8,64,256]{2,1,0:T(8,128)(2,1)S(1)}, u32[]{:S(2)}, u32[]{:S(2)}) %collective-permute-start.6) | collective-permute-done | bytes 262176 | tf_op jit(solution)/shard_map/ppermute | solution.py:411
  48.5 0.0 collective-permute-done.7.refs_7_.refs_11_
  48.5 1.9 %collective-permute-done.8.refs_8_.refs_12_ = bf16[8,64,256]{2,1,0:T(8,128)(2,1)S(1)} collective-permute-done((bf16[8,64,256]{2,1,0:T(8,128)(2,1)S(1)}, bf16[8,64,256]{2,1,0:T(8,128)(2,1)S(1)}, u32[]{:S(2)}, u32[]{:S(2)}) %collective-permute-start.8) | collective-permute-done | bytes 262176 | tf_op jit(solution)/shard_map/ppermute | solution.py:411
  50.4 1.5 %gram_partial.1.refs_1_ = f32[32,128]{1,0:T(8,128)S(1)} custom-call(bf16[8,32,256]{2,1,0:T(8,128)(2,1)S(1)} %collective-permute-done.refs_0_.refs_4_, bf16[8,32,256]{2,1,0:T(8,128)(2,1)S(1)} %collective-permute-done.1.refs_1_.refs_5_, bf16[8,32,256]{2,1,0:T(8,128)(2,1)S(1)} %collective-permute-done.2.refs_2_.refs_6_, ...), custom_call_target="tpu_custom_call" | custom-call | flops 134217728 | bytes 2097152 | tf_op jit(solution)/shard_map/gram_partial/pallas_call | solution.py:214
  51.9 0.1 collective-permute-start.9
  52.0 1.2 %collective-permute-done.9.refs_0_ = f32[32,128]{1,0:T(8,128)S(1)} collective-permute-done((f32[32,128]{1,0:T(8,128)S(1)}, f32[32,128]{1,0:T(8,128)S(1)}, u32[]{:S(2)}, u32[]{:S(2)}) %collective-permute-start.9) | collective-permute-done | bytes 16416 | tf_op jit(solution)/shard_map/ppermute | solution.py:322
  53.2 5.1 %collective-permute-start.10 = (f32[32,128]{1,0:T(8,128)S(1)}, f32[32,128]{1,0:T(8,128)S(1)}, u32[]{:S(2)}, u32[]{:S(2)}) collective-permute-start(f32[32,128]{1,0:T(8,128)S(1)} %sum_over.2.refs_3_), channel_id=1, source_target_pairs={{0,27},{1,26},{2,25},{3,24},{4,31},{5,30},{6,29},{7,28},{8,19},{9,... | collective-permute-start | bytes 49160 | tf_op jit(solution)/shard_map/ppermute | solution.py:322
  58.2 0.0 collective-permute-start.11
  58.2 0.6 collective-permute-start.12
  58.8 0.9 %collective-permute-done.10.refs_0_ = f32[32,128]{1,0:T(8,128)S(1)} collective-permute-done((f32[32,128]{1,0:T(8,128)S(1)}, f32[32,128]{1,0:T(8,128)S(1)}, u32[]{:S(2)}, u32[]{:S(2)}) %collective-permute-start.10) | collective-permute-done | bytes 16416 | tf_op jit(solution)/shard_map/ppermute | solution.py:322
  59.7 3.5 %collective-permute-done.11.refs_1_ = f32[32,128]{1,0:T(8,128)S(1)} collective-permute-done((f32[32,128]{1,0:T(8,128)S(1)}, f32[32,128]{1,0:T(8,128)S(1)}, u32[]{:S(2)}, u32[]{:S(2)}) %collective-permute-start.11) | collective-permute-done | bytes 16416 | tf_op jit(solution)/shard_map/ppermute | solution.py:322
  63.2 0.0 collective-permute-done.12.refs_2_
  63.2 0.5 collective-permute-start.13
  63.7 1.7 %collective-permute-start.14 = (f32[32,128]{1,0:T(8,128)S(1)}, f32[32,128]{1,0:T(8,128)S(1)}, u32[]{:S(2)}, u32[]{:S(2)}) collective-permute-start(f32[32,128]{1,0:T(8,128)S(1)} %sum_over.3.refs_3_), channel_id=1, source_target_pairs={{0,9},{1,8},{2,11},{3,10},{4,13},{5,12},{6,15},{7,14},{8,1},{9,0},... | collective-permute-start | bytes 49160 | tf_op jit(solution)/shard_map/ppermute | solution.py:322
  65.4 1.0 %collective-permute-start.15 = (f32[32,128]{1,0:T(8,128)S(1)}, f32[32,128]{1,0:T(8,128)S(1)}, u32[]{:S(2)}, u32[]{:S(2)}) collective-permute-start(f32[32,128]{1,0:T(8,128)S(1)} %sum_over.3.refs_3_), channel_id=1, source_target_pairs={{0,5},{1,4},{2,7},{3,6},{4,1},{5,0},{6,3},{7,2},{8,13},{9,12},{10,... | collective-permute-start | bytes 49160 | tf_op jit(solution)/shard_map/ppermute | solution.py:322
  66.4 0.9 %collective-permute-done.13.refs_0_ = f32[32,128]{1,0:T(8,128)S(1)} collective-permute-done((f32[32,128]{1,0:T(8,128)S(1)}, f32[32,128]{1,0:T(8,128)S(1)}, u32[]{:S(2)}, u32[]{:S(2)}) %collective-permute-start.13) | collective-permute-done | bytes 16416 | tf_op jit(solution)/shard_map/ppermute | solution.py:322
  67.3 0.0 collective-permute-done.14.refs_1_
  67.4 1.2 %collective-permute-done.15.refs_2_ = f32[32,128]{1,0:T(8,128)S(1)} collective-permute-done((f32[32,128]{1,0:T(8,128)S(1)}, f32[32,128]{1,0:T(8,128)S(1)}, u32[]{:S(2)}, u32[]{:S(2)}) %collective-permute-start.15) | collective-permute-done | bytes 16416 | tf_op jit(solution)/shard_map/ppermute | solution.py:322
  68.6 3.5 %solve_and_project.1 = (f32[1,8]{1,0:T(1,128)}, f32[2,32,256]{2,1,0:T(8,128)}) custom-call(f32[32,128]{1,0:T(8,128)S(1)} %collective-permute-done.13.refs_0_, f32[32,128]{1,0:T(8,128)S(1)} %collective-permute-done.14.refs_1_, f32[32,128]{1,0:T(8,128)S(1)} %collective-permute-done.15.refs_2_, f32[32,128]{1,0:T(8,128)S(1)} %sum_over.3.refs_3_, ...), custom_call_target="tpu_custom_call" | custom-call | tf_op jit(solution)/shard_map/solve_and_project/pallas_call | solution.py:392
  (2 shorter events, 0.0 us)
Async XLA Ops:
  3.0 19.8 %collective-permute-start = (bf16[8,32,256]{2,1,0:T(8,128)(2,1)S(1)}, bf16[8,32,256]{2,1,0:T(8,128)(2,1)S(1)}, u32[]{:S(2)}, u32[]{:S(2)}) collective-permute-start(bf16[8,32,256]{2,1,0:T(8,128)(2,1)S(1)} %get-tuple-element.20), channel_id=1, source_target_pairs={{0,16},{4,20},{8,24},{12,28},{16,0},{20,4},{24,8},{28,12},{1,17},{... | collective-permute-start | bytes 393224 | tf_op jit(solution)/shard_map/ppermute | solution.py:411
  7.1 19.7 %collective-permute-start.1 = (bf16[8,32,256]{2,1,0:T(8,128)(2,1)S(1)}, bf16[8,32,256]{2,1,0:T(8,128)(2,1)S(1)}, u32[]{:S(2)}, u32[]{:S(2)}) collective-permute-start(bf16[8,32,256]{2,1,0:T(8,128)(2,1)S(1)} %get-tuple-element.21), channel_id=1, source_target_pairs={{0,20},{4,16},{8,28},{12,24},{16,4},{20,0},{24,12},{28,8},{1,21},{... | collective-permute-start | bytes 393224 | tf_op jit(solution)/shard_map/ppermute | solution.py:411
  8.4 29.8 %copy-start.1 = (f32[8]{0:T(128)S(1)}, f32[8]{0:T(128)}, u32[]{:S(2)}) copy-start(f32[8]{0:T(128)} %param.7) | copy-start | bytes 100
  8.4 29.9 %copy-start = (s32[8,256]{1,0:T(8,128)S(1)}, s32[8,256]{1,0:T(8,128)}, u32[]{:S(2)}) copy-start(s32[8,256]{1,0:T(8,128)} %spins_ref.1) | copy-start | bytes 24580
  11.6 21.8 %collective-permute-start.2 = (bf16[8,32,256]{2,1,0:T(8,128)(2,1)S(1)}, bf16[8,32,256]{2,1,0:T(8,128)(2,1)S(1)}, u32[]{:S(2)}, u32[]{:S(2)}) collective-permute-start(bf16[8,32,256]{2,1,0:T(8,128)(2,1)S(1)} %get-tuple-element.28), channel_id=1, source_target_pairs={{0,16},{4,20},{8,24},{12,28},{16,0},{20,4},{24,8},{28,12},{1,17},{... | collective-permute-start | bytes 393224 | tf_op jit(solution)/shard_map/ppermute | solution.py:411
  14.3 23.7 %collective-permute-start.3 = (bf16[8,32,256]{2,1,0:T(8,128)(2,1)S(1)}, bf16[8,32,256]{2,1,0:T(8,128)(2,1)S(1)}, u32[]{:S(2)}, u32[]{:S(2)}) collective-permute-start(bf16[8,32,256]{2,1,0:T(8,128)(2,1)S(1)} %get-tuple-element.29), channel_id=1, source_target_pairs={{0,20},{4,16},{8,28},{12,24},{16,4},{20,0},{24,12},{28,8},{1,21},{... | collective-permute-start | bytes 393224 | tf_op jit(solution)/shard_map/ppermute | solution.py:411
  14.3 30.9 %collective-permute-start.4 = (bf16[8,64,256]{2,1,0:T(8,128)(2,1)}, bf16[8,64,256]{2,1,0:T(8,128)(2,1)S(1)}, u32[]{:S(2)}, u32[]{:S(2)}) collective-permute-start(bf16[8,64,256]{2,1,0:T(8,128)(2,1)} %get-tuple-element.30), channel_id=1, source_target_pairs={{0,12},{4,8},{8,4},{12,0},{16,28},{20,24},{24,20},{28,16},{1,13},{... | collective-permute-start | bytes 786440 | tf_op jit(solution)/shard_map/ppermute | solution.py:411
  22.7 22.5 %collective-permute-start.5 = (bf16[8,64,256]{2,1,0:T(8,128)(2,1)}, bf16[8,64,256]{2,1,0:T(8,128)(2,1)S(1)}, u32[]{:S(2)}, u32[]{:S(2)}) collective-permute-start(bf16[8,64,256]{2,1,0:T(8,128)(2,1)} %get-tuple-element.31), channel_id=1, source_target_pairs={{0,24},{4,28},{8,16},{12,20},{16,8},{20,12},{24,0},{28,4},{1,25},{... | collective-permute-start | bytes 786440 | tf_op jit(solution)/shard_map/ppermute | solution.py:411
  26.8 21.7 %collective-permute-start.6 = (bf16[8,64,256]{2,1,0:T(8,128)(2,1)S(1)}, bf16[8,64,256]{2,1,0:T(8,128)(2,1)S(1)}, u32[]{:S(2)}, u32[]{:S(2)}) collective-permute-start(bf16[8,64,256]{2,1,0:T(8,128)(2,1)S(1)} %get-tuple-element.32), channel_id=1, source_target_pairs={{0,8},{4,12},{8,0},{12,4},{16,24},{20,28},{24,16},{28,20},{1,9},{5... | collective-permute-start | bytes 786440 | tf_op jit(solution)/shard_map/ppermute | solution.py:411
  33.4 15.1 %collective-permute-start.7 = (bf16[8,64,256]{2,1,0:T(8,128)(2,1)}, bf16[8,64,256]{2,1,0:T(8,128)(2,1)S(1)}, u32[]{:S(2)}, u32[]{:S(2)}) collective-permute-start(bf16[8,64,256]{2,1,0:T(8,128)(2,1)} %get-tuple-element.33), channel_id=1, source_target_pairs={{0,28},{4,24},{8,20},{12,16},{16,12},{20,8},{24,4},{28,0},{1,29},{... | collective-permute-start | bytes 786440 | tf_op jit(solution)/shard_map/ppermute | solution.py:411
  38.0 12.4 %collective-permute-start.8 = (bf16[8,64,256]{2,1,0:T(8,128)(2,1)S(1)}, bf16[8,64,256]{2,1,0:T(8,128)(2,1)S(1)}, u32[]{:S(2)}, u32[]{:S(2)}) collective-permute-start(bf16[8,64,256]{2,1,0:T(8,128)(2,1)S(1)} %get-tuple-element.34), channel_id=1, source_target_pairs={{0,4},{4,0},{8,12},{12,8},{16,20},{20,16},{24,28},{28,24},{1,5},{5... | collective-permute-start | bytes 786440 | tf_op jit(solution)/shard_map/ppermute | solution.py:411
  51.9 1.2 %collective-permute-start.9 = (f32[32,128]{1,0:T(8,128)S(1)}, f32[32,128]{1,0:T(8,128)S(1)}, u32[]{:S(2)}, u32[]{:S(2)}) collective-permute-start(f32[32,128]{1,0:T(8,128)S(1)} %gram_partial.1.refs_1_), channel_id=1, source_target_pairs={{0,1},{1,0},{2,3},{3,2},{4,5},{5,4},{6,7},{7,6},{8,9},{9,8},{10,11... | collective-permute-start | bytes 49160 | tf_op jit(solution)/shard_map/ppermute | solution.py:322
  53.2 6.5 %collective-permute-start.10 = (f32[32,128]{1,0:T(8,128)S(1)}, f32[32,128]{1,0:T(8,128)S(1)}, u32[]{:S(2)}, u32[]{:S(2)}) collective-permute-start(f32[32,128]{1,0:T(8,128)S(1)} %sum_over.2.refs_3_), channel_id=1, source_target_pairs={{0,27},{1,26},{2,25},{3,24},{4,31},{5,30},{6,29},{7,28},{8,19},{9,... | collective-permute-start | bytes 49160 | tf_op jit(solution)/shard_map/ppermute | solution.py:322
  58.2 5.0 %collective-permute-start.11 = (f32[32,128]{1,0:T(8,128)S(1)}, f32[32,128]{1,0:T(8,128)S(1)}, u32[]{:S(2)}, u32[]{:S(2)}) collective-permute-start(f32[32,128]{1,0:T(8,128)S(1)} %sum_over.2.refs_3_), channel_id=1, source_target_pairs={{0,25},{1,24},{2,27},{3,26},{4,29},{5,28},{6,31},{7,30},{8,17},{9,... | collective-permute-start | bytes 49160 | tf_op jit(solution)/shard_map/ppermute | solution.py:322
  58.2 5.0 %collective-permute-start.12 = (f32[32,128]{1,0:T(8,128)S(1)}, f32[32,128]{1,0:T(8,128)S(1)}, u32[]{:S(2)}, u32[]{:S(2)}) collective-permute-start(f32[32,128]{1,0:T(8,128)S(1)} %sum_over.2.refs_3_), channel_id=1, source_target_pairs={{0,3},{1,2},{2,1},{3,0},{4,7},{5,6},{6,5},{7,4},{8,11},{9,10},{10,... | collective-permute-start | bytes 49160 | tf_op jit(solution)/shard_map/ppermute | solution.py:322
  63.2 4.1 %collective-permute-start.13 = (f32[32,128]{1,0:T(8,128)S(1)}, f32[32,128]{1,0:T(8,128)S(1)}, u32[]{:S(2)}, u32[]{:S(2)}) collective-permute-start(f32[32,128]{1,0:T(8,128)S(1)} %sum_over.3.refs_3_), channel_id=1, source_target_pairs={{0,13},{1,12},{2,15},{3,14},{4,9},{5,8},{6,11},{7,10},{8,5},{9,4},... | collective-permute-start | bytes 49160 | tf_op jit(solution)/shard_map/ppermute | solution.py:322
  63.7 3.7 %collective-permute-start.14 = (f32[32,128]{1,0:T(8,128)S(1)}, f32[32,128]{1,0:T(8,128)S(1)}, u32[]{:S(2)}, u32[]{:S(2)}) collective-permute-start(f32[32,128]{1,0:T(8,128)S(1)} %sum_over.3.refs_3_), channel_id=1, source_target_pairs={{0,9},{1,8},{2,11},{3,10},{4,13},{5,12},{6,15},{7,14},{8,1},{9,0},... | collective-permute-start | bytes 49160 | tf_op jit(solution)/shard_map/ppermute | solution.py:322
  65.4 3.2 %collective-permute-start.15 = (f32[32,128]{1,0:T(8,128)S(1)}, f32[32,128]{1,0:T(8,128)S(1)}, u32[]{:S(2)}, u32[]{:S(2)}) collective-permute-start(f32[32,128]{1,0:T(8,128)S(1)} %sum_over.3.refs_3_), channel_id=1, source_target_pairs={{0,5},{1,4},{2,7},{3,6},{4,1},{5,0},{6,3},{7,2},{8,13},{9,12},{10,... | collective-permute-start | bytes 49160 | tf_op jit(solution)/shard_map/ppermute | solution.py:322

commit v30 on v29

--- a/solution.py
+++ b/solution.py
@@ -27,9 +27,7 @@
     cut = split_partners(owners, split)
     order = [(k, part) for part in range(split) for k in cut]
     far = [k for k in far if k not in cut]
-    while far or near:
-        order += [(k, 0) for k in near[:1] + far[:1]]
-        far, near = far[1:], near[1:]
+    order += [(k, 0) for k in near[:1] + far + near[1:]]
     return order + [(0, 0)]
 
 

time: 72.2 us -> 72.3 us (level)
  starting transfers between devices: 27.1 us -> 25.7 us
  waiting for transfers between devices: 33.4 us -> 34.8 us
    ppermute x9, starting transfers between devices: 18.1 us -> 16.4 us  [body(): blocks[k][part] = lax.ppermute(blocks[k][part], 'samp', perm)]
    ppermute x9, waiting for transfers between devices: 25.7 us -> 27.3 us  [body(): blocks[k][part] = lax.ppermute(blocks[k][part], 'samp', perm)]
where the time goes in v30:
time: 72.3 us; the launch traced here: 72.1 us
  waiting for transfers between devices  34.8 us (48%)
  starting transfers between devices  25.7 us (36%)
  Pallas kernels  10.8 us (15%)
    ppermute x9, waiting for transfers between devices, body(): blocks[k][part] = lax.ppermute(blocks[k][part], 'samp', perm)  27.3 us
    ppermute x9, starting transfers between devices, body(): blocks[k][part] = lax.ppermute(blocks[k][part], 'samp', perm)  16.4 us
    ppermute x7, starting transfers between devices, partners(): return [lax.ppermute(value, axes, perm) for perm in perms] + [value]  9.32 us
    ppermute x7, waiting for transfers between devices, partners(): return [lax.ppermute(value, axes, perm) for perm in perms] + [value]  7.51 us
    pallas_call x2, Pallas kernels, jac_rows(): pl.pallas_call(functools.partial(jac_kernel, part * mats, joined), in_spe...  5.6 us
    pallas_call x1, Pallas kernels, solve_and_project(): pl.pallas_call(functools.partial(solve_kernel, len(sums), len(blocks)), o...  3.48 us
    pallas_call x1, Pallas kernels, gram_partial(): pl.pallas_call(functools.partial(gram_kernel, len(blocks)), out_shape=jax...  1.51 us
  transfers between devices with their start and end apart: 16, of which 12 were waited for; matrix products, arithmetic and copies ran while one was open for 0% of the time, Pallas kernels for 5%

profile of v30, /device:TPU:0, one launch (start us, length us, event | category | flops | bytes accessed | tf_op | source)
XLA Modules:
  0.0 72.1 jit_solution(6237268366929153817)
XLA Ops:
  0.6 2.3 %jac_rows.2 = (bf16[8,32,256]{2,1,0:T(8,128)(2,1)S(1)}, bf16[8,32,256]{2,1,0:T(8,128)(2,1)S(1)}, bf16[8,32,256]{2,1,0:T(8,128)(2,1)S(1)}, bf16[8,32,256]{2,1,0:T...) custom-call(bf16[8,2,256,256]{3,2,1,0:T(8,128)(2,1)} %act_hbm.3, ...), custom_call_target="tpu_custom_call" | custom-call | flops 268435456 | bytes 3145728 | tf_op jit(solution)/shard_map/jac_rows/pallas_call | solution.py:102
  3.0 4.1 %collective-permute-start = (bf16[8,32,256]{2,1,0:T(8,128)(2,1)S(1)}, bf16[8,32,256]{2,1,0:T(8,128)(2,1)S(1)}, u32[]{:S(2)}, u32[]{:S(2)}) collective-permute-start(bf16[8,32,256]{2,1,0:T(8,128)(2,1)S(1)} %get-tuple-element.20), channel_id=1, source_target_pairs={{0,16},{4,20},{8,24},{12,28},{16,0},{20,4},{24,8},{28,12},{1,17},{... | collective-permute-start | bytes 393224 | tf_op jit(solution)/shard_map/ppermute | solution.py:409
  7.1 1.3 %collective-permute-start.1 = (bf16[8,32,256]{2,1,0:T(8,128)(2,1)S(1)}, bf16[8,32,256]{2,1,0:T(8,128)(2,1)S(1)}, u32[]{:S(2)}, u32[]{:S(2)}) collective-permute-start(bf16[8,32,256]{2,1,0:T(8,128)(2,1)S(1)} %get-tuple-element.21), channel_id=1, source_target_pairs={{0,20},{4,16},{8,28},{12,24},{16,4},{20,0},{24,12},{28,8},{1,21},{... | collective-permute-start | bytes 393224 | tf_op jit(solution)/shard_map/ppermute | solution.py:409
  8.4 0.0 copy-start.1
  8.4 0.0 copy-start
  8.4 3.3 %jac_rows.3 = (bf16[8,64,256]{2,1,0:T(8,128)(2,1)S(1)}, bf16[8,64,256]{2,1,0:T(8,128)(2,1)S(1)}, bf16[8,64,256]{2,1,0:T(8,128)(2,1)S(1)}, bf16[8,64,256]{2,1,0:T...) custom-call(bf16[8,2,256,256]{3,2,1,0:T(8,128)(2,1)} %act_hbm.3, ...), custom_call_target="tpu_custom_call" | custom-call | flops 268435456 | bytes 3145728 | tf_op jit(solution)/shard_map/jac_rows/pallas_call | solution.py:102
  11.6 2.7 %collective-permute-start.2 = (bf16[8,32,256]{2,1,0:T(8,128)(2,1)S(1)}, bf16[8,32,256]{2,1,0:T(8,128)(2,1)S(1)}, u32[]{:S(2)}, u32[]{:S(2)}) collective-permute-start(bf16[8,32,256]{2,1,0:T(8,128)(2,1)S(1)} %get-tuple-element.28), channel_id=1, source_target_pairs={{0,16},{4,20},{8,24},{12,28},{16,0},{20,4},{24,8},{28,12},{1,17},{... | collective-permute-start | bytes 393224 | tf_op jit(solution)/shard_map/ppermute | solution.py:409
  14.3 0.0 collective-permute-start.3
  14.3 2.8 %collective-permute-start.4 = (bf16[8,64,256]{2,1,0:T(8,128)(2,1)}, bf16[8,64,256]{2,1,0:T(8,128)(2,1)S(1)}, u32[]{:S(2)}, u32[]{:S(2)}) collective-permute-start(bf16[8,64,256]{2,1,0:T(8,128)(2,1)} %get-tuple-element.30), channel_id=1, source_target_pairs={{0,12},{4,8},{8,4},{12,0},{16,28},{20,24},{24,20},{28,16},{1,13},{... | collective-permute-start | bytes 786440 | tf_op jit(solution)/shard_map/ppermute | solution.py:409
  17.1 5.6 %collective-permute-done.refs_0_.refs_4_ = bf16[8,32,256]{2,1,0:T(8,128)(2,1)S(1)} collective-permute-done((bf16[8,32,256]{2,1,0:T(8,128)(2,1)S(1)}, bf16[8,32,256]{2,1,0:T(8,128)(2,1)S(1)}, u32[]{:S(2)}, u32[]{:S(2)}) %collective-permute-start) | collective-permute-done | bytes 131104 | tf_op jit(solution)/shard_map/ppermute | solution.py:409
  22.7 2.8 %collective-permute-start.5 = (bf16[8,64,256]{2,1,0:T(8,128)(2,1)}, bf16[8,64,256]{2,1,0:T(8,128)(2,1)S(1)}, u32[]{:S(2)}, u32[]{:S(2)}) collective-permute-start(bf16[8,64,256]{2,1,0:T(8,128)(2,1)} %get-tuple-element.31), channel_id=1, source_target_pairs={{0,24},{4,28},{8,16},{12,20},{16,8},{20,12},{24,0},{28,4},{1,25},{... | collective-permute-start | bytes 786440 | tf_op jit(solution)/shard_map/ppermute | solution.py:409
  25.5 1.2 %collective-permute-done.1.refs_1_.refs_5_ = bf16[8,32,256]{2,1,0:T(8,128)(2,1)S(1)} collective-permute-done((bf16[8,32,256]{2,1,0:T(8,128)(2,1)S(1)}, bf16[8,32,256]{2,1,0:T(8,128)(2,1)S(1)}, u32[]{:S(2)}, u32[]{:S(2)}) %collective-permute-start.1) | collective-permute-done | bytes 131104 | tf_op jit(solution)/shard_map/ppermute | solution.py:409
  26.8 2.5 %collective-permute-start.6 = (bf16[8,64,256]{2,1,0:T(8,128)(2,1)}, bf16[8,64,256]{2,1,0:T(8,128)(2,1)S(1)}, u32[]{:S(2)}, u32[]{:S(2)}) collective-permute-start(bf16[8,64,256]{2,1,0:T(8,128)(2,1)} %get-tuple-element.32), channel_id=1, source_target_pairs={{0,28},{4,24},{8,20},{12,16},{16,12},{20,8},{24,4},{28,0},{1,29},{... | collective-permute-start | bytes 786440 | tf_op jit(solution)/shard_map/ppermute | solution.py:409
  29.3 10.3 %collective-permute-done.2.refs_2_.refs_6_ = bf16[8,32,256]{2,1,0:T(8,128)(2,1)S(1)} collective-permute-done((bf16[8,32,256]{2,1,0:T(8,128)(2,1)S(1)}, bf16[8,32,256]{2,1,0:T(8,128)(2,1)S(1)}, u32[]{:S(2)}, u32[]{:S(2)}) %collective-permute-start.2) | collective-permute-done | bytes 131104 | tf_op jit(solution)/shard_map/ppermute | solution.py:409
  39.6 0.0 collective-permute-start.7
  39.6 4.0 %collective-permute-done.3.refs_3_.refs_7_ = bf16[8,32,256]{2,1,0:T(8,128)(2,1)S(1)} collective-permute-done((bf16[8,32,256]{2,1,0:T(8,128)(2,1)S(1)}, bf16[8,32,256]{2,1,0:T(8,128)(2,1)S(1)}, u32[]{:S(2)}, u32[]{:S(2)}) %collective-permute-start.3) | collective-permute-done | bytes 131104 | tf_op jit(solution)/shard_map/ppermute | solution.py:409
  43.6 0.2 collective-permute-start.8
  43.8 0.0 copy-done.1
  43.8 0.1 copy.6.offdiag_ref
  43.9 0.0 copy-done
  43.9 0.2 packed_energy.1.refs_10_
  44.1 1.1 %collective-permute-done.4.refs_4_.refs_8_ = bf16[8,64,256]{2,1,0:T(8,128)(2,1)S(1)} collective-permute-done((bf16[8,64,256]{2,1,0:T(8,128)(2,1)}, bf16[8,64,256]{2,1,0:T(8,128)(2,1)S(1)}, u32[]{:S(2)}, u32[]{:S(2)}) %collective-permute-start.4) | collective-permute-done | bytes 262176 | tf_op jit(solution)/shard_map/ppermute | solution.py:409
  45.2 0.0 collective-permute-done.5.refs_5_.refs_9_
  45.2 0.0 collective-permute-done.6.refs_6_.refs_10_
  45.2 3.3 %collective-permute-done.7.refs_7_.refs_11_ = bf16[8,64,256]{2,1,0:T(8,128)(2,1)S(1)} collective-permute-done((bf16[8,64,256]{2,1,0:T(8,128)(2,1)S(1)}, bf16[8,64,256]{2,1,0:T(8,128)(2,1)S(1)}, u32[]{:S(2)}, u32[]{:S(2)}) %collective-permute-start.7) | collective-permute-done | bytes 262176 | tf_op jit(solution)/shard_map/ppermute | solution.py:409
  48.5 1.8 %collective-permute-done.8.refs_8_.refs_12_ = bf16[8,64,256]{2,1,0:T(8,128)(2,1)S(1)} collective-permute-done((bf16[8,64,256]{2,1,0:T(8,128)(2,1)S(1)}, bf16[8,64,256]{2,1,0:T(8,128)(2,1)S(1)}, u32[]{:S(2)}, u32[]{:S(2)}) %collective-permute-start.8) | collective-permute-done | bytes 262176 | tf_op jit(solution)/shard_map/ppermute | solution.py:409
  50.3 1.5 %gram_partial.1.refs_1_ = f32[32,128]{1,0:T(8,128)S(1)} custom-call(bf16[8,32,256]{2,1,0:T(8,128)(2,1)S(1)} %collective-permute-done.refs_0_.refs_4_, bf16[8,32,256]{2,1,0:T(8,128)(2,1)S(1)} %collective-permute-done.1.refs_1_.refs_5_, bf16[8,32,256]{2,1,0:T(8,128)(2,1)S(1)} %collective-permute-done.2.refs_2_.refs_6_, ...), custom_call_target="tpu_custom_call" | custom-call | flops 134217728 | bytes 2097152 | tf_op jit(solution)/shard_map/gram_partial/pallas_call | solution.py:212
  51.8 0.0 collective-permute-start.9
  51.8 1.2 %collective-permute-done.9.refs_0_ = f32[32,128]{1,0:T(8,128)S(1)} collective-permute-done((f32[32,128]{1,0:T(8,128)S(1)}, f32[32,128]{1,0:T(8,128)S(1)}, u32[]{:S(2)}, u32[]{:S(2)}) %collective-permute-start.9) | collective-permute-done | bytes 16416 | tf_op jit(solution)/shard_map/ppermute | solution.py:320
  53.0 5.6 %collective-permute-start.10 = (f32[32,128]{1,0:T(8,128)S(1)}, f32[32,128]{1,0:T(8,128)S(1)}, u32[]{:S(2)}, u32[]{:S(2)}) collective-permute-start(f32[32,128]{1,0:T(8,128)S(1)} %sum_over.2.refs_3_), channel_id=1, source_target_pairs={{0,27},{1,26},{2,25},{3,24},{4,31},{5,30},{6,29},{7,28},{8,19},{9,... | collective-permute-start | bytes 49160 | tf_op jit(solution)/shard_map/ppermute | solution.py:320
  58.6 0.0 collective-permute-start.11
  58.6 0.6 collective-permute-start.12
  59.2 0.9 %collective-permute-done.10.refs_0_ = f32[32,128]{1,0:T(8,128)S(1)} collective-permute-done((f32[32,128]{1,0:T(8,128)S(1)}, f32[32,128]{1,0:T(8,128)S(1)}, u32[]{:S(2)}, u32[]{:S(2)}) %collective-permute-start.10) | collective-permute-done | bytes 16416 | tf_op jit(solution)/shard_map/ppermute | solution.py:320
  60.0 3.6 %collective-permute-done.11.refs_1_ = f32[32,128]{1,0:T(8,128)S(1)} collective-permute-done((f32[32,128]{1,0:T(8,128)S(1)}, f32[32,128]{1,0:T(8,128)S(1)}, u32[]{:S(2)}, u32[]{:S(2)}) %collective-permute-start.11) | collective-permute-done | bytes 16416 | tf_op jit(solution)/shard_map/ppermute | solution.py:320
  63.7 0.0 collective-permute-done.12.refs_2_
  63.7 1.8 %collective-permute-start.13 = (f32[32,128]{1,0:T(8,128)S(1)}, f32[32,128]{1,0:T(8,128)S(1)}, u32[]{:S(2)}, u32[]{:S(2)}) collective-permute-start(f32[32,128]{1,0:T(8,128)S(1)} %sum_over.3.refs_3_), channel_id=1, source_target_pairs={{0,13},{1,12},{2,15},{3,14},{4,9},{5,8},{6,11},{7,10},{8,5},{9,4},... | collective-permute-start | bytes 49160 | tf_op jit(solution)/shard_map/ppermute | solution.py:320
  65.5 0.0 collective-permute-start.14
  65.5 1.3 %collective-permute-start.15 = (f32[32,128]{1,0:T(8,128)S(1)}, f32[32,128]{1,0:T(8,128)S(1)}, u32[]{:S(2)}, u32[]{:S(2)}) collective-permute-start(f32[32,128]{1,0:T(8,128)S(1)} %sum_over.3.refs_3_), channel_id=1, source_target_pairs={{0,5},{1,4},{2,7},{3,6},{4,1},{5,0},{6,3},{7,2},{8,13},{9,12},{10,... | collective-permute-start | bytes 49160 | tf_op jit(solution)/shard_map/ppermute | solution.py:320
  66.8 1.0 %collective-permute-done.13.refs_0_ = f32[32,128]{1,0:T(8,128)S(1)} collective-permute-done((f32[32,128]{1,0:T(8,128)S(1)}, f32[32,128]{1,0:T(8,128)S(1)}, u32[]{:S(2)}, u32[]{:S(2)}) %collective-permute-start.13) | collective-permute-done | bytes 16416 | tf_op jit(solution)/shard_map/ppermute | solution.py:320
  67.8 0.8 %collective-permute-done.14.refs_1_ = f32[32,128]{1,0:T(8,128)S(1)} collective-permute-done((f32[32,128]{1,0:T(8,128)S(1)}, f32[32,128]{1,0:T(8,128)S(1)}, u32[]{:S(2)}, u32[]{:S(2)}) %collective-permute-start.14) | collective-permute-done | bytes 16416 | tf_op jit(solution)/shard_map/ppermute | solution.py:320
  68.6 0.0 collective-permute-done.15.refs_2_
  68.6 3.5 %solve_and_project.1 = (f32[1,8]{1,0:T(1,128)}, f32[2,32,256]{2,1,0:T(8,128)}) custom-call(f32[32,128]{1,0:T(8,128)S(1)} %collective-permute-done.13.refs_0_, f32[32,128]{1,0:T(8,128)S(1)} %collective-permute-done.14.refs_1_, f32[32,128]{1,0:T(8,128)S(1)} %collective-permute-done.15.refs_2_, f32[32,128]{1,0:T(8,128)S(1)} %sum_over.3.refs_3_, ...), custom_call_target="tpu_custom_call" | custom-call | tf_op jit(solution)/shard_map/solve_and_project/pallas_call | solution.py:390
  (2 shorter events, 0.0 us)
Async XLA Ops:
  3.0 19.8 %collective-permute-start = (bf16[8,32,256]{2,1,0:T(8,128)(2,1)S(1)}, bf16[8,32,256]{2,1,0:T(8,128)(2,1)S(1)}, u32[]{:S(2)}, u32[]{:S(2)}) collective-permute-start(bf16[8,32,256]{2,1,0:T(8,128)(2,1)S(1)} %get-tuple-element.20), channel_id=1, source_target_pairs={{0,16},{4,20},{8,24},{12,28},{16,0},{20,4},{24,8},{28,12},{1,17},{... | collective-permute-start | bytes 393224 | tf_op jit(solution)/shard_map/ppermute | solution.py:409
  7.1 19.7 %collective-permute-start.1 = (bf16[8,32,256]{2,1,0:T(8,128)(2,1)S(1)}, bf16[8,32,256]{2,1,0:T(8,128)(2,1)S(1)}, u32[]{:S(2)}, u32[]{:S(2)}) collective-permute-start(bf16[8,32,256]{2,1,0:T(8,128)(2,1)S(1)} %get-tuple-element.21), channel_id=1, source_target_pairs={{0,20},{4,16},{8,28},{12,24},{16,4},{20,0},{24,12},{28,8},{1,21},{... | collective-permute-start | bytes 393224 | tf_op jit(solution)/shard_map/ppermute | solution.py:409
  8.4 35.4 %copy-start.1 = (f32[8]{0:T(128)S(1)}, f32[8]{0:T(128)}, u32[]{:S(2)}) copy-start(f32[8]{0:T(128)} %param.7) | copy-start | bytes 100
  8.4 35.5 %copy-start = (s32[8,256]{1,0:T(8,128)S(1)}, s32[8,256]{1,0:T(8,128)}, u32[]{:S(2)}) copy-start(s32[8,256]{1,0:T(8,128)} %spins_ref.1) | copy-start | bytes 24580
  11.6 28.0 %collective-permute-start.2 = (bf16[8,32,256]{2,1,0:T(8,128)(2,1)S(1)}, bf16[8,32,256]{2,1,0:T(8,128)(2,1)S(1)}, u32[]{:S(2)}, u32[]{:S(2)}) collective-permute-start(bf16[8,32,256]{2,1,0:T(8,128)(2,1)S(1)} %get-tuple-element.28), channel_id=1, source_target_pairs={{0,16},{4,20},{8,24},{12,28},{16,0},{20,4},{24,8},{28,12},{1,17},{... | collective-permute-start | bytes 393224 | tf_op jit(solution)/shard_map/ppermute | solution.py:409
  14.3 29.3 %collective-permute-start.3 = (bf16[8,32,256]{2,1,0:T(8,128)(2,1)S(1)}, bf16[8,32,256]{2,1,0:T(8,128)(2,1)S(1)}, u32[]{:S(2)}, u32[]{:S(2)}) collective-permute-start(bf16[8,32,256]{2,1,0:T(8,128)(2,1)S(1)} %get-tuple-element.29), channel_id=1, source_target_pairs={{0,20},{4,16},{8,28},{12,24},{16,4},{20,0},{24,12},{28,8},{1,21},{... | collective-permute-start | bytes 393224 | tf_op jit(solution)/shard_map/ppermute | solution.py:409
  14.3 30.9 %collective-permute-start.4 = (bf16[8,64,256]{2,1,0:T(8,128)(2,1)}, bf16[8,64,256]{2,1,0:T(8,128)(2,1)S(1)}, u32[]{:S(2)}, u32[]{:S(2)}) collective-permute-start(bf16[8,64,256]{2,1,0:T(8,128)(2,1)} %get-tuple-element.30), channel_id=1, source_target_pairs={{0,12},{4,8},{8,4},{12,0},{16,28},{20,24},{24,20},{28,16},{1,13},{... | collective-permute-start | bytes 786440 | tf_op jit(solution)/shard_map/ppermute | solution.py:409
  22.7 22.5 %collective-permute-start.5 = (bf16[8,64,256]{2,1,0:T(8,128)(2,1)}, bf16[8,64,256]{2,1,0:T(8,128)(2,1)S(1)}, u32[]{:S(2)}, u32[]{:S(2)}) collective-permute-start(bf16[8,64,256]{2,1,0:T(8,128)(2,1)} %get-tuple-element.31), channel_id=1, source_target_pairs={{0,24},{4,28},{8,16},{12,20},{16,8},{20,12},{24,0},{28,4},{1,25},{... | collective-permute-start | bytes 786440 | tf_op jit(solution)/shard_map/ppermute | solution.py:409
  26.8 18.5 %collective-permute-start.6 = (bf16[8,64,256]{2,1,0:T(8,128)(2,1)}, bf16[8,64,256]{2,1,0:T(8,128)(2,1)S(1)}, u32[]{:S(2)}, u32[]{:S(2)}) collective-permute-start(bf16[8,64,256]{2,1,0:T(8,128)(2,1)} %get-tuple-element.32), channel_id=1, source_target_pairs={{0,28},{4,24},{8,20},{12,16},{16,12},{20,8},{24,4},{28,0},{1,29},{... | collective-permute-start | bytes 786440 | tf_op jit(solution)/shard_map/ppermute | solution.py:409
  39.6 8.9 %collective-permute-start.7 = (bf16[8,64,256]{2,1,0:T(8,128)(2,1)S(1)}, bf16[8,64,256]{2,1,0:T(8,128)(2,1)S(1)}, u32[]{:S(2)}, u32[]{:S(2)}) collective-permute-start(bf16[8,64,256]{2,1,0:T(8,128)(2,1)S(1)} %get-tuple-element.33), channel_id=1, source_target_pairs={{0,8},{4,12},{8,0},{12,4},{16,24},{20,28},{24,16},{28,20},{1,9},{5... | collective-permute-start | bytes 786440 | tf_op jit(solution)/shard_map/ppermute | solution.py:409
  43.6 6.7 %collective-permute-start.8 = (bf16[8,64,256]{2,1,0:T(8,128)(2,1)S(1)}, bf16[8,64,256]{2,1,0:T(8,128)(2,1)S(1)}, u32[]{:S(2)}, u32[]{:S(2)}) collective-permute-start(bf16[8,64,256]{2,1,0:T(8,128)(2,1)S(1)} %get-tuple-element.34), channel_id=1, source_target_pairs={{0,4},{4,0},{8,12},{12,8},{16,20},{20,16},{24,28},{28,24},{1,5},{5... | collective-permute-start | bytes 786440 | tf_op jit(solution)/shard_map/ppermute | solution.py:409
  51.8 1.2 %collective-permute-start.9 = (f32[32,128]{1,0:T(8,128)S(1)}, f32[32,128]{1,0:T(8,128)S(1)}, u32[]{:S(2)}, u32[]{:S(2)}) collective-permute-start(f32[32,128]{1,0:T(8,128)S(1)} %gram_partial.1.refs_1_), channel_id=1, source_target_pairs={{0,1},{1,0},{2,3},{3,2},{4,5},{5,4},{6,7},{7,6},{8,9},{9,8},{10,11... | collective-permute-start | bytes 49160 | tf_op jit(solution)/shard_map/ppermute | solution.py:320
  53.0 7.0 %collective-permute-start.10 = (f32[32,128]{1,0:T(8,128)S(1)}, f32[32,128]{1,0:T(8,128)S(1)}, u32[]{:S(2)}, u32[]{:S(2)}) collective-permute-start(f32[32,128]{1,0:T(8,128)S(1)} %sum_over.2.refs_3_), channel_id=1, source_target_pairs={{0,27},{1,26},{2,25},{3,24},{4,31},{5,30},{6,29},{7,28},{8,19},{9,... | collective-permute-start | bytes 49160 | tf_op jit(solution)/shard_map/ppermute | solution.py:320
  58.6 5.1 %collective-permute-start.11 = (f32[32,128]{1,0:T(8,128)S(1)}, f32[32,128]{1,0:T(8,128)S(1)}, u32[]{:S(2)}, u32[]{:S(2)}) collective-permute-start(f32[32,128]{1,0:T(8,128)S(1)} %sum_over.2.refs_3_), channel_id=1, source_target_pairs={{0,25},{1,24},{2,27},{3,26},{4,29},{5,28},{6,31},{7,30},{8,17},{9,... | collective-permute-start | bytes 49160 | tf_op jit(solution)/shard_map/ppermute | solution.py:320
  58.6 5.1 %collective-permute-start.12 = (f32[32,128]{1,0:T(8,128)S(1)}, f32[32,128]{1,0:T(8,128)S(1)}, u32[]{:S(2)}, u32[]{:S(2)}) collective-permute-start(f32[32,128]{1,0:T(8,128)S(1)} %sum_over.2.refs_3_), channel_id=1, source_target_pairs={{0,3},{1,2},{2,1},{3,0},{4,7},{5,6},{6,5},{7,4},{8,11},{9,10},{10,... | collective-permute-start | bytes 49160 | tf_op jit(solution)/shard_map/ppermute | solution.py:320
  63.7 4.1 %collective-permute-start.13 = (f32[32,128]{1,0:T(8,128)S(1)}, f32[32,128]{1,0:T(8,128)S(1)}, u32[]{:S(2)}, u32[]{:S(2)}) collective-permute-start(f32[32,128]{1,0:T(8,128)S(1)} %sum_over.3.refs_3_), channel_id=1, source_target_pairs={{0,13},{1,12},{2,15},{3,14},{4,9},{5,8},{6,11},{7,10},{8,5},{9,4},... | collective-permute-start | bytes 49160 | tf_op jit(solution)/shard_map/ppermute | solution.py:320
  65.5 3.2 %collective-permute-start.14 = (f32[32,128]{1,0:T(8,128)S(1)}, f32[32,128]{1,0:T(8,128)S(1)}, u32[]{:S(2)}, u32[]{:S(2)}) collective-permute-start(f32[32,128]{1,0:T(8,128)S(1)} %sum_over.3.refs_3_), channel_id=1, source_target_pairs={{0,9},{1,8},{2,11},{3,10},{4,13},{5,12},{6,15},{7,14},{8,1},{9,0},... | collective-permute-start | bytes 49160 | tf_op jit(solution)/shard_map/ppermute | solution.py:320
  65.5 3.2 %collective-permute-start.15 = (f32[32,128]{1,0:T(8,128)S(1)}, f32[32,128]{1,0:T(8,128)S(1)}, u32[]{:S(2)}, u32[]{:S(2)}) collective-permute-start(f32[32,128]{1,0:T(8,128)S(1)} %sum_over.3.refs_3_), channel_id=1, source_target_pairs={{0,5},{1,4},{2,7},{3,6},{4,1},{5,0},{6,3},{7,2},{8,13},{9,12},{10,... | collective-permute-start | bytes 49160 | tf_op jit(solution)/shard_map/ppermute | solution.py:320

commit v31 on v29

--- a/solution.py
+++ b/solution.py
@@ -242,7 +242,10 @@
     uppers = {}
     for j in range(0, count, 2):
         a, b, c = p[j][j], p[j][j + 1], p[j + 1][j + 1]
-        inverse = F32(1.0) / (a * c - b * b)
+        determinant = a * c - b * b
+        inverse = pl.reciprocal(determinant, approx=True)
+        for _ in range(2):
+            inverse = inverse * (F32(2.0) - determinant * inverse)
 
         def scaled(x, y):
             return (c * x - b * y) * inverse, (a * y - b * x) * inverse

time: 72.2 us -> 72.4 us (level)
  no operation moved by 1% of the time
where the time goes in v31:
time: 72.4 us; the launch traced here: 72.2 us
  waiting for transfers between devices  33.4 us (46%)
  starting transfers between devices  27.1 us (37%)
  Pallas kernels  11 us (15%)
    ppermute x9, waiting for transfers between devices, body(): blocks[k][part] = lax.ppermute(blocks[k][part], 'samp', perm)  25.7 us
    ppermute x9, starting transfers between devices, body(): blocks[k][part] = lax.ppermute(blocks[k][part], 'samp', perm)  18.1 us
    ppermute x7, starting transfers between devices, partners(): return [lax.ppermute(value, axes, perm) for perm in perms] + [value]  8.95 us
    ppermute x7, waiting for transfers between devices, partners(): return [lax.ppermute(value, axes, perm) for perm in perms] + [value]  7.67 us
    pallas_call x2, Pallas kernels, jac_rows(): pl.pallas_call(functools.partial(jac_kernel, part * mats, joined), in_spe...  5.6 us
    pallas_call x1, Pallas kernels, solve_and_project(): pl.pallas_call(functools.partial(solve_kernel, len(sums), len(blocks)), o...  3.63 us
    pallas_call x1, Pallas kernels, gram_partial(): pl.pallas_call(functools.partial(gram_kernel, len(blocks)), out_shape=jax...  1.51 us
  transfers between devices with their start and end apart: 16, of which 12 were waited for; matrix products, arithmetic and copies ran while one was open for 0% of the time, Pallas kernels for 5%

profile of v31, /device:TPU:0, one launch (start us, length us, event | category | flops | bytes accessed | tf_op | source)
XLA Modules:
  0.0 72.2 jit_solution(6123682369122738855)
XLA Ops:
  0.6 2.3 %jac_rows.2 = (bf16[8,32,256]{2,1,0:T(8,128)(2,1)S(1)}, bf16[8,32,256]{2,1,0:T(8,128)(2,1)S(1)}, bf16[8,32,256]{2,1,0:T(8,128)(2,1)S(1)}, bf16[8,32,256]{2,1,0:T...) custom-call(bf16[8,2,256,256]{3,2,1,0:T(8,128)(2,1)} %act_hbm.3, ...), custom_call_target="tpu_custom_call" | custom-call | flops 268435456 | bytes 3145728 | tf_op jit(solution)/shard_map/jac_rows/pallas_call | solution.py:104
  3.0 4.1 %collective-permute-start = (bf16[8,32,256]{2,1,0:T(8,128)(2,1)S(1)}, bf16[8,32,256]{2,1,0:T(8,128)(2,1)S(1)}, u32[]{:S(2)}, u32[]{:S(2)}) collective-permute-start(bf16[8,32,256]{2,1,0:T(8,128)(2,1)S(1)} %get-tuple-element.20), channel_id=1, source_target_pairs={{0,16},{4,20},{8,24},{12,28},{16,0},{20,4},{24,8},{28,12},{1,17},{... | collective-permute-start | bytes 393224 | tf_op jit(solution)/shard_map/ppermute | solution.py:414
  7.1 1.3 %collective-permute-start.1 = (bf16[8,32,256]{2,1,0:T(8,128)(2,1)S(1)}, bf16[8,32,256]{2,1,0:T(8,128)(2,1)S(1)}, u32[]{:S(2)}, u32[]{:S(2)}) collective-permute-start(bf16[8,32,256]{2,1,0:T(8,128)(2,1)S(1)} %get-tuple-element.21), channel_id=1, source_target_pairs={{0,20},{4,16},{8,28},{12,24},{16,4},{20,0},{24,12},{28,8},{1,21},{... | collective-permute-start | bytes 393224 | tf_op jit(solution)/shard_map/ppermute | solution.py:414
  8.4 0.0 copy-start.1
  8.4 0.0 copy-start
  8.4 3.3 %jac_rows.3 = (bf16[8,64,256]{2,1,0:T(8,128)(2,1)S(1)}, bf16[8,64,256]{2,1,0:T(8,128)(2,1)S(1)}, bf16[8,64,256]{2,1,0:T(8,128)(2,1)S(1)}, bf16[8,64,256]{2,1,0:T...) custom-call(bf16[8,2,256,256]{3,2,1,0:T(8,128)(2,1)} %act_hbm.3, ...), custom_call_target="tpu_custom_call" | custom-call | flops 268435456 | bytes 3145728 | tf_op jit(solution)/shard_map/jac_rows/pallas_call | solution.py:104
  11.6 2.7 %collective-permute-start.2 = (bf16[8,32,256]{2,1,0:T(8,128)(2,1)S(1)}, bf16[8,32,256]{2,1,0:T(8,128)(2,1)S(1)}, u32[]{:S(2)}, u32[]{:S(2)}) collective-permute-start(bf16[8,32,256]{2,1,0:T(8,128)(2,1)S(1)} %get-tuple-element.28), channel_id=1, source_target_pairs={{0,16},{4,20},{8,24},{12,28},{16,0},{20,4},{24,8},{28,12},{1,17},{... | collective-permute-start | bytes 393224 | tf_op jit(solution)/shard_map/ppermute | solution.py:414
  14.3 0.0 collective-permute-start.3
  14.3 2.8 %collective-permute-start.4 = (bf16[8,64,256]{2,1,0:T(8,128)(2,1)}, bf16[8,64,256]{2,1,0:T(8,128)(2,1)S(1)}, u32[]{:S(2)}, u32[]{:S(2)}) collective-permute-start(bf16[8,64,256]{2,1,0:T(8,128)(2,1)} %get-tuple-element.30), channel_id=1, source_target_pairs={{0,12},{4,8},{8,4},{12,0},{16,28},{20,24},{24,20},{28,16},{1,13},{... | collective-permute-start | bytes 786440 | tf_op jit(solution)/shard_map/ppermute | solution.py:414
  17.1 5.6 %collective-permute-done.refs_0_.refs_4_ = bf16[8,32,256]{2,1,0:T(8,128)(2,1)S(1)} collective-permute-done((bf16[8,32,256]{2,1,0:T(8,128)(2,1)S(1)}, bf16[8,32,256]{2,1,0:T(8,128)(2,1)S(1)}, u32[]{:S(2)}, u32[]{:S(2)}) %collective-permute-start) | collective-permute-done | bytes 131104 | tf_op jit(solution)/shard_map/ppermute | solution.py:414
  22.7 2.8 %collective-permute-start.5 = (bf16[8,64,256]{2,1,0:T(8,128)(2,1)}, bf16[8,64,256]{2,1,0:T(8,128)(2,1)S(1)}, u32[]{:S(2)}, u32[]{:S(2)}) collective-permute-start(bf16[8,64,256]{2,1,0:T(8,128)(2,1)} %get-tuple-element.31), channel_id=1, source_target_pairs={{0,24},{4,28},{8,16},{12,20},{16,8},{20,12},{24,0},{28,4},{1,25},{... | collective-permute-start | bytes 786440 | tf_op jit(solution)/shard_map/ppermute | solution.py:414
  25.5 1.2 %collective-permute-done.1.refs_1_.refs_5_ = bf16[8,32,256]{2,1,0:T(8,128)(2,1)S(1)} collective-permute-done((bf16[8,32,256]{2,1,0:T(8,128)(2,1)S(1)}, bf16[8,32,256]{2,1,0:T(8,128)(2,1)S(1)}, u32[]{:S(2)}, u32[]{:S(2)}) %collective-permute-start.1) | collective-permute-done | bytes 131104 | tf_op jit(solution)/shard_map/ppermute | solution.py:414
  26.8 0.0 collective-permute-start.6
  26.8 6.7 %collective-permute-done.2.refs_2_.refs_6_ = bf16[8,32,256]{2,1,0:T(8,128)(2,1)S(1)} collective-permute-done((bf16[8,32,256]{2,1,0:T(8,128)(2,1)S(1)}, bf16[8,32,256]{2,1,0:T(8,128)(2,1)S(1)}, u32[]{:S(2)}, u32[]{:S(2)}) %collective-permute-start.2) | collective-permute-done | bytes 131104 | tf_op jit(solution)/shard_map/ppermute | solution.py:414
  33.4 4.3 %collective-permute-start.7 = (bf16[8,64,256]{2,1,0:T(8,128)(2,1)}, bf16[8,64,256]{2,1,0:T(8,128)(2,1)S(1)}, u32[]{:S(2)}, u32[]{:S(2)}) collective-permute-start(bf16[8,64,256]{2,1,0:T(8,128)(2,1)} %get-tuple-element.33), channel_id=1, source_target_pairs={{0,28},{4,24},{8,20},{12,16},{16,12},{20,8},{24,4},{28,0},{1,29},{... | collective-permute-start | bytes 786440 | tf_op jit(solution)/shard_map/ppermute | solution.py:414
  37.7 0.3 collective-permute-done.3.refs_3_.refs_7_
  38.0 0.2 collective-permute-start.8
  38.2 0.0 copy-done.1
  38.2 0.1 copy.6.offdiag_ref
  38.3 0.0 copy-done
  38.3 0.2 packed_energy.1.refs_10_
  38.5 6.8 %collective-permute-done.4.refs_4_.refs_8_ = bf16[8,64,256]{2,1,0:T(8,128)(2,1)S(1)} collective-permute-done((bf16[8,64,256]{2,1,0:T(8,128)(2,1)}, bf16[8,64,256]{2,1,0:T(8,128)(2,1)S(1)}, u32[]{:S(2)}, u32[]{:S(2)}) %collective-permute-start.4) | collective-permute-done | bytes 262176 | tf_op jit(solution)/shard_map/ppermute | solution.py:414
  45.3 0.0 collective-permute-done.5.refs_5_.refs_9_
  45.3 3.2 %collective-permute-done.6.refs_6_.refs_10_ = bf16[8,64,256]{2,1,0:T(8,128)(2,1)S(1)} collective-permute-done((bf16[8,64,256]{2,1,0:T(8,128)(2,1)S(1)}, bf16[8,64,256]{2,1,0:T(8,128)(2,1)S(1)}, u32[]{:S(2)}, u32[]{:S(2)}) %collective-permute-start.6) | collective-permute-done | bytes 262176 | tf_op jit(solution)/shard_map/ppermute | solution.py:414
  48.5 0.0 collective-permute-done.7.refs_7_.refs_11_
  48.5 1.9 %collective-permute-done.8.refs_8_.refs_12_ = bf16[8,64,256]{2,1,0:T(8,128)(2,1)S(1)} collective-permute-done((bf16[8,64,256]{2,1,0:T(8,128)(2,1)S(1)}, bf16[8,64,256]{2,1,0:T(8,128)(2,1)S(1)}, u32[]{:S(2)}, u32[]{:S(2)}) %collective-permute-start.8) | collective-permute-done | bytes 262176 | tf_op jit(solution)/shard_map/ppermute | solution.py:414
  50.4 1.5 %gram_partial.1.refs_1_ = f32[32,128]{1,0:T(8,128)S(1)} custom-call(bf16[8,32,256]{2,1,0:T(8,128)(2,1)S(1)} %collective-permute-done.refs_0_.refs_4_, bf16[8,32,256]{2,1,0:T(8,128)(2,1)S(1)} %collective-permute-done.1.refs_1_.refs_5_, bf16[8,32,256]{2,1,0:T(8,128)(2,1)S(1)} %collective-permute-done.2.refs_2_.refs_6_, ...), custom_call_target="tpu_custom_call" | custom-call | flops 134217728 | bytes 2097152 | tf_op jit(solution)/shard_map/gram_partial/pallas_call | solution.py:214
  51.9 0.1 collective-permute-start.9
  52.0 1.2 %collective-permute-done.9.refs_0_ = f32[32,128]{1,0:T(8,128)S(1)} collective-permute-done((f32[32,128]{1,0:T(8,128)S(1)}, f32[32,128]{1,0:T(8,128)S(1)}, u32[]{:S(2)}, u32[]{:S(2)}) %collective-permute-start.9) | collective-permute-done | bytes 16416 | tf_op jit(solution)/shard_map/ppermute | solution.py:325
  53.2 5.1 %collective-permute-start.10 = (f32[32,128]{1,0:T(8,128)S(1)}, f32[32,128]{1,0:T(8,128)S(1)}, u32[]{:S(2)}, u32[]{:S(2)}) collective-permute-start(f32[32,128]{1,0:T(8,128)S(1)} %sum_over.2.refs_3_), channel_id=1, source_target_pairs={{0,27},{1,26},{2,25},{3,24},{4,31},{5,30},{6,29},{7,28},{8,19},{9,... | collective-permute-start | bytes 49160 | tf_op jit(solution)/shard_map/ppermute | solution.py:325
  58.2 0.0 collective-permute-start.11
  58.2 0.6 collective-permute-start.12
  58.8 0.9 %collective-permute-done.10.refs_0_ = f32[32,128]{1,0:T(8,128)S(1)} collective-permute-done((f32[32,128]{1,0:T(8,128)S(1)}, f32[32,128]{1,0:T(8,128)S(1)}, u32[]{:S(2)}, u32[]{:S(2)}) %collective-permute-start.10) | collective-permute-done | bytes 16416 | tf_op jit(solution)/shard_map/ppermute | solution.py:325
  59.7 3.5 %collective-permute-done.11.refs_1_ = f32[32,128]{1,0:T(8,128)S(1)} collective-permute-done((f32[32,128]{1,0:T(8,128)S(1)}, f32[32,128]{1,0:T(8,128)S(1)}, u32[]{:S(2)}, u32[]{:S(2)}) %collective-permute-start.11) | collective-permute-done | bytes 16416 | tf_op jit(solution)/shard_map/ppermute | solution.py:325
  63.2 0.0 collective-permute-done.12.refs_2_
  63.2 0.5 collective-permute-start.13
  63.7 1.7 %collective-permute-start.14 = (f32[32,128]{1,0:T(8,128)S(1)}, f32[32,128]{1,0:T(8,128)S(1)}, u32[]{:S(2)}, u32[]{:S(2)}) collective-permute-start(f32[32,128]{1,0:T(8,128)S(1)} %sum_over.3.refs_3_), channel_id=1, source_target_pairs={{0,9},{1,8},{2,11},{3,10},{4,13},{5,12},{6,15},{7,14},{8,1},{9,0},... | collective-permute-start | bytes 49160 | tf_op jit(solution)/shard_map/ppermute | solution.py:325
  65.4 1.0 %collective-permute-start.15 = (f32[32,128]{1,0:T(8,128)S(1)}, f32[32,128]{1,0:T(8,128)S(1)}, u32[]{:S(2)}, u32[]{:S(2)}) collective-permute-start(f32[32,128]{1,0:T(8,128)S(1)} %sum_over.3.refs_3_), channel_id=1, source_target_pairs={{0,5},{1,4},{2,7},{3,6},{4,1},{5,0},{6,3},{7,2},{8,13},{9,12},{10,... | collective-permute-start | bytes 49160 | tf_op jit(solution)/shard_map/ppermute | solution.py:325
  66.4 0.9 %collective-permute-done.13.refs_0_ = f32[32,128]{1,0:T(8,128)S(1)} collective-permute-done((f32[32,128]{1,0:T(8,128)S(1)}, f32[32,128]{1,0:T(8,128)S(1)}, u32[]{:S(2)}, u32[]{:S(2)}) %collective-permute-start.13) | collective-permute-done | bytes 16416 | tf_op jit(solution)/shard_map/ppermute | solution.py:325
  67.3 0.0 collective-permute-done.14.refs_1_
  67.4 1.2 %collective-permute-done.15.refs_2_ = f32[32,128]{1,0:T(8,128)S(1)} collective-permute-done((f32[32,128]{1,0:T(8,128)S(1)}, f32[32,128]{1,0:T(8,128)S(1)}, u32[]{:S(2)}, u32[]{:S(2)}) %collective-permute-start.15) | collective-permute-done | bytes 16416 | tf_op jit(solution)/shard_map/ppermute | solution.py:325
  68.6 3.6 %solve_and_project.1 = (f32[1,8]{1,0:T(1,128)}, f32[2,32,256]{2,1,0:T(8,128)}) custom-call(f32[32,128]{1,0:T(8,128)S(1)} %collective-permute-done.13.refs_0_, f32[32,128]{1,0:T(8,128)S(1)} %collective-permute-done.14.refs_1_, f32[32,128]{1,0:T(8,128)S(1)} %collective-permute-done.15.refs_2_, f32[32,128]{1,0:T(8,128)S(1)} %sum_over.3.refs_3_, ...), custom_call_target="tpu_custom_call" | custom-call | tf_op jit(solution)/shard_map/solve_and_project/pallas_call | solution.py:395
  (2 shorter events, 0.0 us)
Async XLA Ops:
  3.0 19.8 %collective-permute-start = (bf16[8,32,256]{2,1,0:T(8,128)(2,1)S(1)}, bf16[8,32,256]{2,1,0:T(8,128)(2,1)S(1)}, u32[]{:S(2)}, u32[]{:S(2)}) collective-permute-start(bf16[8,32,256]{2,1,0:T(8,128)(2,1)S(1)} %get-tuple-element.20), channel_id=1, source_target_pairs={{0,16},{4,20},{8,24},{12,28},{16,0},{20,4},{24,8},{28,12},{1,17},{... | collective-permute-start | bytes 393224 | tf_op jit(solution)/shard_map/ppermute | solution.py:414
  7.1 19.7 %collective-permute-start.1 = (bf16[8,32,256]{2,1,0:T(8,128)(2,1)S(1)}, bf16[8,32,256]{2,1,0:T(8,128)(2,1)S(1)}, u32[]{:S(2)}, u32[]{:S(2)}) collective-permute-start(bf16[8,32,256]{2,1,0:T(8,128)(2,1)S(1)} %get-tuple-element.21), channel_id=1, source_target_pairs={{0,20},{4,16},{8,28},{12,24},{16,4},{20,0},{24,12},{28,8},{1,21},{... | collective-permute-start | bytes 393224 | tf_op jit(solution)/shard_map/ppermute | solution.py:414
  8.4 29.8 %copy-start.1 = (f32[8]{0:T(128)S(1)}, f32[8]{0:T(128)}, u32[]{:S(2)}) copy-start(f32[8]{0:T(128)} %param.7) | copy-start | bytes 100
  8.4 29.9 %copy-start = (s32[8,256]{1,0:T(8,128)S(1)}, s32[8,256]{1,0:T(8,128)}, u32[]{:S(2)}) copy-start(s32[8,256]{1,0:T(8,128)} %spins_ref.1) | copy-start | bytes 24580
  11.6 21.8 %collective-permute-start.2 = (bf16[8,32,256]{2,1,0:T(8,128)(2,1)S(1)}, bf16[8,32,256]{2,1,0:T(8,128)(2,1)S(1)}, u32[]{:S(2)}, u32[]{:S(2)}) collective-permute-start(bf16[8,32,256]{2,1,0:T(8,128)(2,1)S(1)} %get-tuple-element.28), channel_id=1, source_target_pairs={{0,16},{4,20},{8,24},{12,28},{16,0},{20,4},{24,8},{28,12},{1,17},{... | collective-permute-start | bytes 393224 | tf_op jit(solution)/shard_map/ppermute | solution.py:414
  14.3 23.7 %collective-permute-start.3 = (bf16[8,32,256]{2,1,0:T(8,128)(2,1)S(1)}, bf16[8,32,256]{2,1,0:T(8,128)(2,1)S(1)}, u32[]{:S(2)}, u32[]{:S(2)}) collective-permute-start(bf16[8,32,256]{2,1,0:T(8,128)(2,1)S(1)} %get-tuple-element.29), channel_id=1, source_target_pairs={{0,20},{4,16},{8,28},{12,24},{16,4},{20,0},{24,12},{28,8},{1,21},{... | collective-permute-start | bytes 393224 | tf_op jit(solution)/shard_map/ppermute | solution.py:414
  14.3 30.9 %collective-permute-start.4 = (bf16[8,64,256]{2,1,0:T(8,128)(2,1)}, bf16[8,64,256]{2,1,0:T(8,128)(2,1)S(1)}, u32[]{:S(2)}, u32[]{:S(2)}) collective-permute-start(bf16[8,64,256]{2,1,0:T(8,128)(2,1)} %get-tuple-element.30), channel_id=1, source_target_pairs={{0,12},{4,8},{8,4},{12,0},{16,28},{20,24},{24,20},{28,16},{1,13},{... | collective-permute-start | bytes 786440 | tf_op jit(solution)/shard_map/ppermute | solution.py:414
  22.7 22.5 %collective-permute-start.5 = (bf16[8,64,256]{2,1,0:T(8,128)(2,1)}, bf16[8,64,256]{2,1,0:T(8,128)(2,1)S(1)}, u32[]{:S(2)}, u32[]{:S(2)}) collective-permute-start(bf16[8,64,256]{2,1,0:T(8,128)(2,1)} %get-tuple-element.31), channel_id=1, source_target_pairs={{0,24},{4,28},{8,16},{12,20},{16,8},{20,12},{24,0},{28,4},{1,25},{... | collective-permute-start | bytes 786440 | tf_op jit(solution)/shard_map/ppermute | solution.py:414
  26.8 21.7 %collective-permute-start.6 = (bf16[8,64,256]{2,1,0:T(8,128)(2,1)S(1)}, bf16[8,64,256]{2,1,0:T(8,128)(2,1)S(1)}, u32[]{:S(2)}, u32[]{:S(2)}) collective-permute-start(bf16[8,64,256]{2,1,0:T(8,128)(2,1)S(1)} %get-tuple-element.32), channel_id=1, source_target_pairs={{0,8},{4,12},{8,0},{12,4},{16,24},{20,28},{24,16},{28,20},{1,9},{5... | collective-permute-start | bytes 786440 | tf_op jit(solution)/shard_map/ppermute | solution.py:414
  33.4 15.1 %collective-permute-start.7 = (bf16[8,64,256]{2,1,0:T(8,128)(2,1)}, bf16[8,64,256]{2,1,0:T(8,128)(2,1)S(1)}, u32[]{:S(2)}, u32[]{:S(2)}) collective-permute-start(bf16[8,64,256]{2,1,0:T(8,128)(2,1)} %get-tuple-element.33), channel_id=1, source_target_pairs={{0,28},{4,24},{8,20},{12,16},{16,12},{20,8},{24,4},{28,0},{1,29},{... | collective-permute-start | bytes 786440 | tf_op jit(solution)/shard_map/ppermute | solution.py:414
  38.0 12.4 %collective-permute-start.8 = (bf16[8,64,256]{2,1,0:T(8,128)(2,1)S(1)}, bf16[8,64,256]{2,1,0:T(8,128)(2,1)S(1)}, u32[]{:S(2)}, u32[]{:S(2)}) collective-permute-start(bf16[8,64,256]{2,1,0:T(8,128)(2,1)S(1)} %get-tuple-element.34), channel_id=1, source_target_pairs={{0,4},{4,0},{8,12},{12,8},{16,20},{20,16},{24,28},{28,24},{1,5},{5... | collective-permute-start | bytes 786440 | tf_op jit(solution)/shard_map/ppermute | solution.py:414
  51.9 1.2 %collective-permute-start.9 = (f32[32,128]{1,0:T(8,128)S(1)}, f32[32,128]{1,0:T(8,128)S(1)}, u32[]{:S(2)}, u32[]{:S(2)}) collective-permute-start(f32[32,128]{1,0:T(8,128)S(1)} %gram_partial.1.refs_1_), channel_id=1, source_target_pairs={{0,1},{1,0},{2,3},{3,2},{4,5},{5,4},{6,7},{7,6},{8,9},{9,8},{10,11... | collective-permute-start | bytes 49160 | tf_op jit(solution)/shard_map/ppermute | solution.py:325
  53.2 6.5 %collective-permute-start.10 = (f32[32,128]{1,0:T(8,128)S(1)}, f32[32,128]{1,0:T(8,128)S(1)}, u32[]{:S(2)}, u32[]{:S(2)}) collective-permute-start(f32[32,128]{1,0:T(8,128)S(1)} %sum_over.2.refs_3_), channel_id=1, source_target_pairs={{0,27},{1,26},{2,25},{3,24},{4,31},{5,30},{6,29},{7,28},{8,19},{9,... | collective-permute-start | bytes 49160 | tf_op jit(solution)/shard_map/ppermute | solution.py:325
  58.2 5.0 %collective-permute-start.11 = (f32[32,128]{1,0:T(8,128)S(1)}, f32[32,128]{1,0:T(8,128)S(1)}, u32[]{:S(2)}, u32[]{:S(2)}) collective-permute-start(f32[32,128]{1,0:T(8,128)S(1)} %sum_over.2.refs_3_), channel_id=1, source_target_pairs={{0,25},{1,24},{2,27},{3,26},{4,29},{5,28},{6,31},{7,30},{8,17},{9,... | collective-permute-start | bytes 49160 | tf_op jit(solution)/shard_map/ppermute | solution.py:325
  58.2 5.0 %collective-permute-start.12 = (f32[32,128]{1,0:T(8,128)S(1)}, f32[32,128]{1,0:T(8,128)S(1)}, u32[]{:S(2)}, u32[]{:S(2)}) collective-permute-start(f32[32,128]{1,0:T(8,128)S(1)} %sum_over.2.refs_3_), channel_id=1, source_target_pairs={{0,3},{1,2},{2,1},{3,0},{4,7},{5,6},{6,5},{7,4},{8,11},{9,10},{10,... | collective-permute-start | bytes 49160 | tf_op jit(solution)/shard_map/ppermute | solution.py:325
  63.2 4.1 %collective-permute-start.13 = (f32[32,128]{1,0:T(8,128)S(1)}, f32[32,128]{1,0:T(8,128)S(1)}, u32[]{:S(2)}, u32[]{:S(2)}) collective-permute-start(f32[32,128]{1,0:T(8,128)S(1)} %sum_over.3.refs_3_), channel_id=1, source_target_pairs={{0,13},{1,12},{2,15},{3,14},{4,9},{5,8},{6,11},{7,10},{8,5},{9,4},... | collective-permute-start | bytes 49160 | tf_op jit(solution)/shard_map/ppermute | solution.py:325
  63.7 3.7 %collective-permute-start.14 = (f32[32,128]{1,0:T(8,128)S(1)}, f32[32,128]{1,0:T(8,128)S(1)}, u32[]{:S(2)}, u32[]{:S(2)}) collective-permute-start(f32[32,128]{1,0:T(8,128)S(1)} %sum_over.3.refs_3_), channel_id=1, source_target_pairs={{0,9},{1,8},{2,11},{3,10},{4,13},{5,12},{6,15},{7,14},{8,1},{9,0},... | collective-permute-start | bytes 49160 | tf_op jit(solution)/shard_map/ppermute | solution.py:325
  65.4 3.2 %collective-permute-start.15 = (f32[32,128]{1,0:T(8,128)S(1)}, f32[32,128]{1,0:T(8,128)S(1)}, u32[]{:S(2)}, u32[]{:S(2)}) collective-permute-start(f32[32,128]{1,0:T(8,128)S(1)} %sum_over.3.refs_3_), channel_id=1, source_target_pairs={{0,5},{1,4},{2,7},{3,6},{4,1},{5,0},{6,3},{7,2},{8,13},{9,12},{10,... | collective-permute-start | bytes 49160 | tf_op jit(solution)/shard_map/ppermute | solution.py:325
